TPU v7x, 32 devices: a whole 2x2x4 slice. The times are simulated.
32 devices in a mesh: groups: 2 (over x), blocks: 16 (over z, y, core).
Axes of the slice: x: 2, y: 2, z: 4, core: 2. Of those that a mesh axis runs over, the one named last changes fastest.
Arguments:
- features: bfloat16 [16384, 512], P(('groups', 'blocks')), parts along dimension 0, may hold values from -12 to 12
- conv_weight: bfloat16 [13824, 512], P('blocks'), may hold values from -0.0546875 to 0.0546875
- cpe_weight: bfloat16 [512, 512], replicated, may hold values from -0.25 to 0.25
- cpe_gain: float32 [512], replicated, may hold values from 0.1 to 1.9
- attn_gain: float32 [512], replicated, may hold values from 0.1 to 1.9
- qkv_weight: bfloat16 [512, 1536], replicated, as said below
- proj_weight: bfloat16 [512, 512], replicated, may hold values from -0.25 to 0.25
- mlp_gain: float32 [512], replicated, may hold values from 0.1 to 1.9
- up_weight: bfloat16 [512, 2048], replicated, may hold values from -0.25 to 0.25
- down_weight: bfloat16 [2048, 512], replicated, may hold values from -0.125 to 0.125
- face_rows: int32 [32, 8, 64], P(('groups', 'blocks')), parts along dimension 0, may hold values from 0 to 512, as said below
- neighbours: int32 [16384, 26], P(('groups', 'blocks')), parts along dimension 0, may hold values from 0 to 1024, as said below
- serial_rank: int32 [16384], P(('groups', 'blocks')), parts along dimension 0, may hold values from 0 to 8191, as said below
- serial_order: int32 [16384], P(('groups', 'blocks')), parts along dimension 0, may hold values from 0 to 8191, as said below
Outputs:
- output: bfloat16 [16384, 512], P(('groups', 'blocks')), parts along dimension 0
There are 2 independent parts, one for each index of `groups`. A program takes and returns all parts, laid end to end along the dimension named above; an argument that names none is the same for every part. Nothing has to cross between parts.
Inputs may be any that keep to these rules, and one draw needn't show every extreme that they name: `qkv_weight`: projections for queries, keys and values, columns in that order. face_rows[b, k, f] is a local row of block b sent toward direction k, or 512 for an empty slot; live slots come first in each list; lists toward blocks outside the grid are empty; every block has a full list. `neighbours`: row index into the point's block table: local rows below 512, received face rows from 512 to 1023, and 1024 for a missing neighbour. `serial_rank`: A permutation; serial_order is its inverse. Position r belongs to stretch r // 512. The points of one block fall into any one stretch 0, 32 or 64 at a time, and 64 is reached. `serial_order`: the inverse of serial_rank.
All inputs are finite; a program needn't handle non-finite values.
Results may differ from a plain program's by a relative error of at most 0.011.
The roundings to bfloat16 on the way count: a program that leaves them out, or rounds other values in their place, can miss the bound.
Values may be sent and summed in bfloat16 or wider, within the bound.
No kernel may reach another device: no remote copies, remote signals or barrier semaphores. Data moves between devices by JAX's collectives and lax.ppermute only.
A program may use at most 128 MiB of HBM per device.

v0:
```python
import math

import jax
import jax.numpy as jnp
from jax import lax
from jax.sharding import PartitionSpec as P

HEADS = 32
PATCH = 512
GY = 8
HD = 16


EPSILON = 1e-05
STEPS_X = (-1, -1, -1, 0, 0, 1, 1, 1)
STEPS_Y = (-1, 0, 1, -1, 1, -1, 0, 1)


def shifted(value, axis, steps):
    count = lax.axis_size(axis)
    initial, last = (max(0, -steps), min(count, count - steps))
    return lax.ppermute(value, axis, [(source, source + steps) for source in range(initial, last)])


def layer_norm(inputs, gain_vector):
    row_mean = jnp.mean(inputs, axis=-1, keepdims=True)
    centred = inputs - row_mean
    variance = jnp.mean(centred * centred, axis=-1, keepdims=True)
    return centred * lax.rsqrt(variance + EPSILON) * gain_vector


def exchange_faces(faces):
    arrived = []
    for facing in range(8):
        offset = STEPS_X[facing] * GY + STEPS_Y[facing]
        arrived.append(shifted(faces[facing], "blocks", offset))
    result = jnp.stack(arrived)
    return result


def return_rows(inputs, in_row, out_row, devices, capacity):
    points, width = inputs.shape
    back_index = (
        jnp.full((devices * capacity,), points, jnp.int32)
        .at[in_row]
        .set(jnp.arange(points, dtype=jnp.int32))
    )
    padded_rows = jnp.concatenate([inputs, jnp.zeros((1, width), inputs.dtype)], axis=0)
    outgoing = padded_rows[back_index].reshape(devices, capacity, width)
    arrived = lax.all_to_all(outgoing, "blocks", split_axis=0, concat_axis=0, tiled=True).reshape(
        devices * capacity, width
    )
    return arrived[out_row]


def feed_forward(attended, mlp_gain, up_weight, down_weight):
    hidden_in = layer_norm(attended.astype(jnp.float32), mlp_gain).astype(jnp.bfloat16)
    hidden = jax.nn.gelu(
        jnp.dot(hidden_in, up_weight, preferred_element_type=jnp.float32), approximate=False
    ).astype(jnp.bfloat16)
    finished = attended.astype(jnp.float32) + jnp.dot(
        hidden, down_weight, preferred_element_type=jnp.float32
    )
    return finished.astype(jnp.bfloat16)


def body(
    features,
    conv_weight,
    cpe_weight,
    cpe_gain,
    attn_gain,
    qkv_weight,
    proj_weight,
    mlp_gain,
    up_weight,
    down_weight,
    face_rows,
    neighbours,
    serial_rank,
    serial_order,
):
    points, width = features.shape
    devices = lax.axis_size("blocks")
    capacity = 2 * points // devices
    zero_row = jnp.zeros((1, width), jnp.bfloat16)
    padded_rows = jnp.concatenate([features, zero_row], axis=0)
    faces = padded_rows[face_rows[0]]
    received = exchange_faces(faces).reshape(-1, width)
    lookup = jnp.concatenate([features, received, zero_row], axis=0)
    gathered = lookup[neighbours]
    stacked = jnp.concatenate(
        [gathered[:, :13], features[:, None], gathered[:, 13:]], axis=1
    ).reshape(points, 27 * width)
    whole_kernel = lax.all_gather(conv_weight, "blocks", axis=0, tiled=True)
    convolved = jnp.dot(stacked, whole_kernel, preferred_element_type=jnp.float32)
    convolved = convolved.astype(jnp.bfloat16)
    linear = jnp.dot(convolved, cpe_weight, preferred_element_type=jnp.float32)
    mixed_rows = (features.astype(jnp.float32) + layer_norm(linear, cpe_gain)).astype(jnp.bfloat16)
    positions = jnp.arange(points, dtype=jnp.int32)
    target = serial_rank // points
    earlier = (target[None, :] == target[:, None]) & (serial_rank[None, :] < serial_rank[:, None])
    out_row = target * capacity + jnp.sum(earlier.astype(jnp.int32), axis=1)
    anchor = serial_order // points
    before = (anchor[None, :] == anchor[:, None]) & (positions[None, :] < positions[:, None])
    in_row = anchor * capacity + jnp.sum(before.astype(jnp.int32), axis=1)
    send_index = jnp.full((devices * capacity,), points, jnp.int32).at[out_row].set(positions)
    mixed_padded = jnp.concatenate([mixed_rows, zero_row], axis=0)
    outgoing = mixed_padded[send_index].reshape(devices, capacity, width)
    arrived = lax.all_to_all(outgoing, "blocks", split_axis=0, concat_axis=0, tiled=True).reshape(
        devices * capacity, width
    )
    serial = arrived[in_row]
    normed = layer_norm(serial.astype(jnp.float32), attn_gain).astype(jnp.bfloat16)
    projected_cols = lax.dot_general(
        qkv_weight, normed, (((0,), (1,)), ((), ())), preferred_element_type=jnp.float32
    ).astype(jnp.bfloat16)
    patch_count = points // PATCH
    group_count = HEADS // 4
    scale = 1.0 / math.sqrt(HD)
    shaped = projected_cols.reshape(3, group_count, 4, HD, patch_count, PATCH)

    def attend(group_parts):
        query_part, key_part, value_part = group_parts
        scores = (
            jnp.einsum("hdpq,hdpk->hpqk", query_part, key_part, preferred_element_type=jnp.float32)
            * scale
        )
        row_max = jnp.max(scores, axis=-1, keepdims=True)
        weights = jnp.exp(scores - row_max)
        weights = (weights / jnp.sum(weights, axis=-1, keepdims=True)).astype(jnp.bfloat16)
        return jnp.einsum(
            "hpqk,hdpk->hdpq", weights, value_part, preferred_element_type=jnp.float32
        ).astype(jnp.bfloat16)

    grouped = lax.map(attend, (shaped[0], shaped[1], shaped[2]))
    head_cols = grouped.reshape(width, points)
    update = lax.dot_general(
        head_cols, proj_weight, (((0,), (0,)), ((), ())), preferred_element_type=jnp.float32
    )
    attended = (serial.astype(jnp.float32) + update).astype(jnp.bfloat16)
    output = return_rows(
        feed_forward(attended, mlp_gain, up_weight, down_weight), in_row, out_row, devices, capacity
    )
    return output


def solution(mesh):
    placed = (
        P(("groups", "blocks"), None),
        P("blocks", None),
        P(),
        P(),
        P(),
        P(),
        P(),
        P(),
        P(),
        P(),
        P(("groups", "blocks"), None, None),
        P(("groups", "blocks"), None),
        P(("groups", "blocks")),
        P(("groups", "blocks")),
    )
    return jax.shard_map(
        body, mesh=mesh, in_specs=placed, out_specs=P(("groups", "blocks"), None), check_vma=False
    )
```

profile of v0, /device:TPU:9, one launch (start us, length us, event | category | flops | bytes accessed | tf_op | source)
XLA Modules:
  0.0 365.0 jit_solution(17035427855203211598)
XLA Ops:
  7.3 0.7 compare_select_fusion.3
  8.1 1.1 concatenate.15
  9.2 2.6 gather_fusion
  11.8 1.1 fusion.135
  12.9 1.3 collective-permute-start
  14.2 1.3 collective-permute-start.1
  15.5 1.3 collective-permute-start.2
  16.8 2.6 collective-permute-start.3
  19.4 3.0 collective-permute-start.4
  22.5 0.9 compare_select_fusion
  24.6 2.4 scatter_custom_fusion
  27.4 2.4 scatter_custom_fusion.1
  30.4 1.8 copy.41
  32.2 6.8 %collective-permute-start.5 = (bf16[64,512]{1,0:T(8,128)(2,1)S(1)}, bf16[64,512]{1,0:T(8,128)(2,1)S(1)}, u32[]{:S(2)}, u32[]{:S(2)}) collective-permute-start(bf16[64,512]{1,0:T(8,128)(2,1)S(1)} %get-tuple-element.72), channel_id=1, source_target_pairs={{0,7},{1,8},{2,9},{3,10},{4,11},{5,12},{6,13},{7,14},{8,15},{16,23... | collective-permute-start | bytes 196616 | tf_op jit(solution)/shard_map/ppermute | solution.py:22
  39.0 0.8 bitcast_dynamic-update-slice_fusion.7
  39.9 1.6 collective-permute-start.6
  41.5 0.8 bitcast_dynamic-update-slice_fusion.6
  42.4 1.5 collective-permute-start.7
  43.8 0.8 bitcast_dynamic-update-slice_fusion.5
  44.7 0.8 bitcast_dynamic-update-slice_fusion.4
  45.5 0.8 bitcast_dynamic-update-slice_fusion.3
  46.4 5.7 %collective-permute-done.6 = bf16[64,512]{1,0:T(8,128)(2,1)S(1)} collective-permute-done((bf16[64,512]{1,0:T(8,128)(2,1)S(1)}, bf16[64,512]{1,0:T(8,128)(2,1)S(1)}, u32[]{:S(2)}, u32[]{:S(2)}) %collective-permute-start.6) | collective-permute-done | bytes 65568 | tf_op jit(solution)/shard_map/ppermute | solution.py:22
  52.1 4.5 %collective-permute-done.7 = bf16[64,512]{1,0:T(8,128)(2,1)S(1)} collective-permute-done((bf16[64,512]{1,0:T(8,128)(2,1)S(1)}, bf16[64,512]{1,0:T(8,128)(2,1)S(1)}, u32[]{:S(2)}, u32[]{:S(2)}) %collective-permute-start.7) | collective-permute-done | bytes 65568 | tf_op jit(solution)/shard_map/ppermute | solution.py:22
  56.6 1.3 maximum_maximum_fusion
  57.9 53.9 %gather_fusion.1 = bf16[13312,512]{1,0:T(8,128)(2,1)} fusion(bf16[1025,512]{1,0:T(8,128)(2,1)S(1)} %maximum_maximum_fusion, s32[13312]{0:T(1024)S(1)} %broadcast_clamp_fusion), kind=kCustom, calls=%fused_computation.1 | custom fusion | bytes 27316224 | tf_op jit(solution)/shard_map/gather | solution.py:91
  111.8 20.6 %reshape.151 = bf16[512,26,512]{2,1,0:T(8,128)(2,1)} reshape(bf16[13312,512]{1,0:T(8,128)(2,1)} %gather_fusion.1) | data formatting | bytes 27262976 | tf_op jit(solution)/shard_map/gather | solution.py:91
  132.5 9.2 %fusion.133 = (bf16[512,13,512]{2,1,0:T(8,128)(2,1)S(1)}, bf16[512,13,512]{2,1,0:T(8,128)(2,1)S(1)}) fusion(bf16[512,26,512]{2,1,0:T(8,128)(2,1)} %reshape.151), kind=kLoop, calls=%fused_computation.165 | loop fusion | bytes 27262976 | tf_op jit(solution)/shard_map/slice | solution.py:93
  141.7 11.6 %pad_maximum_fusion = bf16[512,27,512]{2,1,0:T(8,128)(2,1)} fusion(bf16[512,13,512]{2,1,0:T(8,128)(2,1)S(1)} %get-tuple-element.66, bf16[512,1,512]{2,1,0:T(2,128)(2,1)S(1)} %copy-done.4, bf16[512,13,512]{2,1,0:T(8,128)(2,1)S(1)} %get-tuple-element.65), kind=kLoop, calls=%fused_computation.34 | loop fusion | flops 42467328 | bytes 28311552 | tf_op jit(solution)/shard_map/concatenate | solution.py:92
  153.2 25.9 %copy.42 = bf16[512,27,512]{0,2,1:T(8,128)(2,1)} copy(bf16[512,27,512]{2,1,0:T(8,128)(2,1)} %pad_maximum_fusion) | data formatting | bytes 28311552 | tf_op jit(solution)/shard_map/concatenate | solution.py:92
  179.1 14.9 %convolution_convert_fusion.1 = bf16[512,512]{1,0:T(8,128)(2,1)S(1)} fusion(bf16[512,13824]{0,1:T(8,128)(2,1)} %bitcast.90, bf16[13824,512]{1,0:T(8,128)(2,1)} %all-gather.2.cloned.1.call-done), kind=kOutput, calls=%fused_computation.65 | convolution fusion | flops 7248019456 | bytes 28835840 | tf_op jit(solution)/shard_map/dot_general | solution.py:96
  195.2 5.1 %gather_fusion.2 = bf16[1024,512]{1,0:T(8,128)(2,1)} fusion(bf16[513,512]{1,0:T(8,128)(2,1)S(1)} %concatenate.18, s32[1024]{0:T(1024)S(1)} %get-tuple-element.82), kind=kCustom, calls=%fused_computation.2 | custom fusion | bytes 2101248 | tf_op jit(solution)/shard_map/gather | solution.py:109
  200.2 7.3 %all-to-all-start = ((bf16[16,64,512]{2,1,0:T(8,128)(2,1)}), bf16[16,64,512]{2,1,0:T(8,128)(2,1)S(1)}, u32[]{:S(2)}, u32[]{:S(2)}) async-start(bf16[16,64,512]{2,1,0:T(8,128)(2,1)} %bitcast.92), calls=%async_computation | async-start | bytes 2097152 | tf_op jit(solution)/shard_map/all_to_all | solution.py:110
  207.5 24.8 %all-to-all-done = bf16[16,64,512]{2,1,0:T(8,128)(2,1)S(1)} async-done(((bf16[16,64,512]{2,1,0:T(8,128)(2,1)}), bf16[16,64,512]{2,1,0:T(8,128)(2,1)S(1)}, u32[]{:S(2)}, u32[]{:S(2)}) %all-to-all-start) | async-done | bytes 1048608 | tf_op jit(solution)/shard_map/all_to_all | solution.py:110
  232.4 2.6 gather_fusion.3
  235.0 1.2 convert_reduce_fusion.1
  236.2 1.3 fusion.64
  237.5 2.6 fusion.48
  240.2 0.9 fusion.134
  241.1 2.1 copy.43
  243.1 1.0 copy.44
  244.4 60.1 %while.10 = (s32[]{:T(128)}, bf16[8,4,16,1,512]{4,2,1,3,0:T(8,128)(2,1)}, bf16[8,4,16,1,512]{4,2,1,3,0:T(8,128)(2,1)}, bf16[8,4,16,1,512]{4,2,1,3,0:T(8,128)(2,1...) while((s32[]{:T(128)}, bf16[8,4,16,1,512]{4,2,1,3,0:T(8,128)(2,1)}, ...), condition=%wide.region_10.11_spmd, body=%wide.region_7.10_spmd.sunk | while | flops 72385024 | bytes 8669253 | solution.py:136
  244.4 4.3 %fusion.154 = (f32[4,512]{1,0:T(4,128)S(1)}, f32[4,512,512]{1,2,0:T(8,128)}) fusion(bf16[8,4,16,1,512]{4,2,1,3,0:T(8,128)(2,1)S(1)} %get-tuple-element.135, s32[]{:T(128)} %get-tuple-element.125, bf16[8,4,16,1,512]{4,2,1,3,0:T(8,128)(2,1)} %get-tuple-element.134), kind=kOutput, calls=%fused_computation.164.clone.1 | convolution fusion | flops 36700672 | bytes 4334592 | tf_op jit(solution)/shard_map/while/body/eval_jaxpr/sub | solution.py:130
  248.7 3.3 fusion.155
  252.0 4.2 %fusion.154 = (f32[4,512]{1,0:T(4,128)S(1)}, f32[4,512,512]{1,2,0:T(8,128)}) fusion(bf16[8,4,16,1,512]{4,2,1,3,0:T(8,128)(2,1)S(1)} %get-tuple-element.135, s32[]{:T(128)} %get-tuple-element.125, bf16[8,4,16,1,512]{4,2,1,3,0:T(8,128)(2,1)} %get-tuple-element.134), kind=kOutput, calls=%fused_computation.164.clone.1 | convolution fusion | flops 36700672 | bytes 4334592 | tf_op jit(solution)/shard_map/while/body/eval_jaxpr/sub | solution.py:130
  256.2 3.3 fusion.155
  259.5 4.3 %fusion.154 = (f32[4,512]{1,0:T(4,128)S(1)}, f32[4,512,512]{1,2,0:T(8,128)}) fusion(bf16[8,4,16,1,512]{4,2,1,3,0:T(8,128)(2,1)S(1)} %get-tuple-element.135, s32[]{:T(128)} %get-tuple-element.125, bf16[8,4,16,1,512]{4,2,1,3,0:T(8,128)(2,1)} %get-tuple-element.134), kind=kOutput, calls=%fused_computation.164.clone.1 | convolution fusion | flops 36700672 | bytes 4334592 | tf_op jit(solution)/shard_map/while/body/eval_jaxpr/sub | solution.py:130
  263.7 3.3 fusion.155
  267.0 4.2 %fusion.154 = (f32[4,512]{1,0:T(4,128)S(1)}, f32[4,512,512]{1,2,0:T(8,128)}) fusion(bf16[8,4,16,1,512]{4,2,1,3,0:T(8,128)(2,1)S(1)} %get-tuple-element.135, s32[]{:T(128)} %get-tuple-element.125, bf16[8,4,16,1,512]{4,2,1,3,0:T(8,128)(2,1)} %get-tuple-element.134), kind=kOutput, calls=%fused_computation.164.clone.1 | convolution fusion | flops 36700672 | bytes 4334592 | tf_op jit(solution)/shard_map/while/body/eval_jaxpr/sub | solution.py:130
  271.3 3.3 fusion.155
  274.5 4.3 %fusion.154 = (f32[4,512]{1,0:T(4,128)S(1)}, f32[4,512,512]{1,2,0:T(8,128)}) fusion(bf16[8,4,16,1,512]{4,2,1,3,0:T(8,128)(2,1)S(1)} %get-tuple-element.135, s32[]{:T(128)} %get-tuple-element.125, bf16[8,4,16,1,512]{4,2,1,3,0:T(8,128)(2,1)} %get-tuple-element.134), kind=kOutput, calls=%fused_computation.164.clone.1 | convolution fusion | flops 36700672 | bytes 4334592 | tf_op jit(solution)/shard_map/while/body/eval_jaxpr/sub | solution.py:130
  278.8 3.3 fusion.155
  282.0 4.2 %fusion.154 = (f32[4,512]{1,0:T(4,128)S(1)}, f32[4,512,512]{1,2,0:T(8,128)}) fusion(bf16[8,4,16,1,512]{4,2,1,3,0:T(8,128)(2,1)S(1)} %get-tuple-element.135, s32[]{:T(128)} %get-tuple-element.125, bf16[8,4,16,1,512]{4,2,1,3,0:T(8,128)(2,1)} %get-tuple-element.134), kind=kOutput, calls=%fused_computation.164.clone.1 | convolution fusion | flops 36700672 | bytes 4334592 | tf_op jit(solution)/shard_map/while/body/eval_jaxpr/sub | solution.py:130
  286.3 3.3 fusion.155
  289.5 4.3 %fusion.154 = (f32[4,512]{1,0:T(4,128)S(1)}, f32[4,512,512]{1,2,0:T(8,128)}) fusion(bf16[8,4,16,1,512]{4,2,1,3,0:T(8,128)(2,1)S(1)} %get-tuple-element.135, s32[]{:T(128)} %get-tuple-element.125, bf16[8,4,16,1,512]{4,2,1,3,0:T(8,128)(2,1)} %get-tuple-element.134), kind=kOutput, calls=%fused_computation.164.clone.1 | convolution fusion | flops 36700672 | bytes 4334592 | tf_op jit(solution)/shard_map/while/body/eval_jaxpr/sub | solution.py:130
  293.8 3.3 fusion.155
  297.0 4.2 %fusion.154 = (f32[4,512]{1,0:T(4,128)S(1)}, f32[4,512,512]{1,2,0:T(8,128)}) fusion(bf16[8,4,16,1,512]{4,2,1,3,0:T(8,128)(2,1)S(1)} %get-tuple-element.135, s32[]{:T(128)} %get-tuple-element.125, bf16[8,4,16,1,512]{4,2,1,3,0:T(8,128)(2,1)} %get-tuple-element.134), kind=kOutput, calls=%fused_computation.164.clone.1 | convolution fusion | flops 36700672 | bytes 4334592 | tf_op jit(solution)/shard_map/while/body/eval_jaxpr/sub | solution.py:130
  301.3 3.3 fusion.155
  304.5 1.8 convert_reduce_fusion
  306.6 12.9 %fusion.54 = bf16[512,512]{1,0:T(8,128)(2,1)} fusion(bf16[2048,512]{1,0:T(8,128)(2,1)S(1)} %copy-done, bf16[512,512]{1,0:T(8,128)(2,1)S(1)} %get-tuple-element.81, bf16[512,2048]{1,0:T(8,128)(2,1)} %param.24, f32[512]{0:T(512)S(1)} %copy-done.13, f32[512]{0:T(512)S(1)} %add_rsqrt_fusion, f32[512]{0:T(512)S(1)} %broadcast_multiply_fusion), kind=kOutput, calls=%fused_computation.64 | convolution fusion | flops 2217738240 | bytes 5249024 | tf_op jit(solution)/shard_map/dot_general | solution.py:61
  319.5 1.1 concatenate.19
  320.6 5.1 %gather_fusion.4 = bf16[1024,512]{1,0:T(8,128)(2,1)} fusion(bf16[513,512]{1,0:T(8,128)(2,1)S(1)} %concatenate.19, s32[1024]{0:T(1024)S(1)} %copy-done.7), kind=kCustom, calls=%fused_computation.4 | custom fusion | bytes 2101248 | tf_op jit(solution)/shard_map/gather | solution.py:49
  325.7 5.0 %all-to-all-start.1 = ((bf16[16,64,512]{2,1,0:T(8,128)(2,1)}), bf16[16,64,512]{2,1,0:T(8,128)(2,1)S(1)}, u32[]{:S(2)}, u32[]{:S(2)}) async-start(bf16[16,64,512]{2,1,0:T(8,128)(2,1)} %bitcast.93), calls=%async_computation.1 | async-start | bytes 2097152 | tf_op jit(solution)/shard_map/all_to_all | solution.py:50
  330.7 24.8 %all-to-all-done.1 = bf16[16,64,512]{2,1,0:T(8,128)(2,1)S(1)} async-done(((bf16[16,64,512]{2,1,0:T(8,128)(2,1)}), bf16[16,64,512]{2,1,0:T(8,128)(2,1)S(1)}, u32[]{:S(2)}, u32[]{:S(2)}) %all-to-all-start.1) | async-done | bytes 1048608 | tf_op jit(solution)/shard_map/all_to_all | solution.py:50
  355.5 2.6 gather_fusion.5
  (70 shorter events, 4.7 us)
Async XLA Ops:
  6.5 300.1 %copy-start = (bf16[2048,512]{1,0:T(8,128)(2,1)S(1)}, bf16[2048,512]{1,0:T(8,128)(2,1)}, u32[]{:S(2)}) copy-start(bf16[2048,512]{1,0:T(8,128)(2,1)} %param.25) | copy-start | bytes 6291460
  6.5 23.9 %copy-start.1 = (bf16[512,512]{1,0:T(8,128)(2,1)S(1)}, bf16[512,512]{1,0:T(8,128)(2,1)}, u32[]{:S(2)}) copy-start(bf16[512,512]{1,0:T(8,128)(2,1)} %param.16) | copy-start | bytes 1572868
  6.5 17.1 %copy-start.6 = (s32[512]{0:T(512)S(1)}, s32[512]{0:T(512)}, u32[]{:S(2)}) copy-start(s32[512]{0:T(512)} %param.28) | copy-start | bytes 6148
  6.5 20.5 %copy-start.10 = (s32[512]{0:T(512)S(1)}, s32[512]{0:T(512)}, u32[]{:S(2)}) copy-start(s32[512]{0:T(512)} %param.29) | copy-start | bytes 6148
  6.5 172.6 %all-gather.2.cloned.1.call-start = ((), (), s32[]{:S(2)}) async-start(), calls=%async_computation.2 | async-start | bytes 15040512 | tf_op jit(solution)/shard_map/all_gather | solution.py:95
  12.9 19.3 %collective-permute-start = (bf16[64,512]{1,0:T(8,128)(2,1)S(1)}, bf16[64,512]{1,0:T(8,128)(2,1)}, u32[]{:S(2)}, u32[]{:S(2)}) collective-permute-start(bf16[64,512]{1,0:T(8,128)(2,1)S(1)} %get-tuple-element.77), channel_id=1, source_target_pairs={{9,0},{10,1},{11,2},{12,3},{13,4},{14,5},{15,6},{25,16},{26,17},{2... | collective-permute-start | bytes 196616 | tf_op jit(solution)/shard_map/ppermute | solution.py:22
  14.2 25.7 %collective-permute-start.1 = (bf16[64,512]{1,0:T(8,128)(2,1)S(1)}, bf16[64,512]{1,0:T(8,128)(2,1)}, u32[]{:S(2)}, u32[]{:S(2)}) collective-permute-start(bf16[64,512]{1,0:T(8,128)(2,1)S(1)} %get-tuple-element.76), channel_id=1, source_target_pairs={{8,0},{9,1},{10,2},{11,3},{12,4},{13,5},{14,6},{15,7},{24,16},{25,... | collective-permute-start | bytes 196616 | tf_op jit(solution)/shard_map/ppermute | solution.py:22
  15.5 26.9 %collective-permute-start.2 = (bf16[64,512]{1,0:T(8,128)(2,1)S(1)}, bf16[64,512]{1,0:T(8,128)(2,1)}, u32[]{:S(2)}, u32[]{:S(2)}) collective-permute-start(bf16[64,512]{1,0:T(8,128)(2,1)S(1)} %get-tuple-element.75), channel_id=1, source_target_pairs={{7,0},{8,1},{9,2},{10,3},{11,4},{12,5},{13,6},{14,7},{15,8},{23,16... | collective-permute-start | bytes 196616 | tf_op jit(solution)/shard_map/ppermute | solution.py:22
  16.8 27.9 %collective-permute-start.3 = (bf16[64,512]{1,0:T(8,128)(2,1)S(1)}, bf16[64,512]{1,0:T(8,128)(2,1)}, u32[]{:S(2)}, u32[]{:S(2)}) collective-permute-start(bf16[64,512]{1,0:T(8,128)(2,1)S(1)} %get-tuple-element.74), channel_id=1, source_target_pairs={{1,0},{2,1},{3,2},{4,3},{5,4},{6,5},{7,6},{8,7},{9,8},{10,9},{11,1... | collective-permute-start | bytes 196616 | tf_op jit(solution)/shard_map/ppermute | solution.py:22
  19.4 26.1 %collective-permute-start.4 = (bf16[64,512]{1,0:T(8,128)(2,1)S(1)}, bf16[64,512]{1,0:T(8,128)(2,1)}, u32[]{:S(2)}, u32[]{:S(2)}) collective-permute-start(bf16[64,512]{1,0:T(8,128)(2,1)S(1)} %get-tuple-element.73), channel_id=1, source_target_pairs={{0,1},{1,2},{2,3},{3,4},{4,5},{5,6},{6,7},{7,8},{8,9},{9,10},{10,1... | collective-permute-start | bytes 196616 | tf_op jit(solution)/shard_map/ppermute | solution.py:22
  24.0 0.6 copy-start.8
  32.2 14.2 %collective-permute-start.5 = (bf16[64,512]{1,0:T(8,128)(2,1)S(1)}, bf16[64,512]{1,0:T(8,128)(2,1)S(1)}, u32[]{:S(2)}, u32[]{:S(2)}) collective-permute-start(bf16[64,512]{1,0:T(8,128)(2,1)S(1)} %get-tuple-element.72), channel_id=1, source_target_pairs={{0,7},{1,8},{2,9},{3,10},{4,11},{5,12},{6,13},{7,14},{8,15},{16,23... | collective-permute-start | bytes 196616 | tf_op jit(solution)/shard_map/ppermute | solution.py:22
  39.9 12.2 %collective-permute-start.6 = (bf16[64,512]{1,0:T(8,128)(2,1)S(1)}, bf16[64,512]{1,0:T(8,128)(2,1)S(1)}, u32[]{:S(2)}, u32[]{:S(2)}) collective-permute-start(bf16[64,512]{1,0:T(8,128)(2,1)S(1)} %get-tuple-element.71), channel_id=1, source_target_pairs={{0,8},{1,9},{2,10},{3,11},{4,12},{5,13},{6,14},{7,15},{16,24},{17,... | collective-permute-start | bytes 196616 | tf_op jit(solution)/shard_map/ppermute | solution.py:22
  42.4 14.2 %collective-permute-start.7 = (bf16[64,512]{1,0:T(8,128)(2,1)S(1)}, bf16[64,512]{1,0:T(8,128)(2,1)S(1)}, u32[]{:S(2)}, u32[]{:S(2)}) collective-permute-start(bf16[64,512]{1,0:T(8,128)(2,1)S(1)} %get-tuple-element.70), channel_id=1, source_target_pairs={{0,9},{1,10},{2,11},{3,12},{4,13},{5,14},{6,15},{16,25},{17,26},{1... | collective-permute-start | bytes 196616 | tf_op jit(solution)/shard_map/ppermute | solution.py:22
  132.5 9.2 %copy-start.4 = (bf16[512,1,512]{2,1,0:T(2,128)(2,1)S(1)}, bf16[512,1,512]{2,1,0:T(2,128)(2,1)}, u32[]{:S(2)}) copy-start(bf16[512,1,512]{2,1,0:T(2,128)(2,1)} %copy.41) | copy-start | bytes 1572868
  179.1 14.9 %copy-start.5 = (bf16[512,512]{1,0:T(8,128)(2,1)S(1)}, bf16[512,512]{1,0:T(8,128)(2,1)}, u32[]{:S(2)}) copy-start(bf16[512,512]{1,0:T(8,128)(2,1)} %param.18) | copy-start | bytes 1572868
  179.1 15.7 %copy-start.2 = (bf16[512,512]{1,0:T(8,128)(2,1)S(1)}, bf16[512,512]{1,0:T(8,128)(2,1)}, u32[]{:S(2)}) copy-start(bf16[512,512]{1,0:T(8,128)(2,1)} %param.16) | copy-start | bytes 1572868
  179.1 15.7 %copy-start.11 = (f32[512]{0:T(512)S(1)}, f32[512]{0:T(512)}, u32[]{:S(2)}) copy-start(f32[512]{0:T(512)} %param.19) | copy-start | bytes 6148
  200.2 37.3 %copy-start.12 = (f32[512]{0:T(512)S(1)}, f32[512]{0:T(512)}, u32[]{:S(2)}) copy-start(f32[512]{0:T(512)} %param.20) | copy-start | bytes 6148
  200.2 32.1 %all-to-all-start = ((bf16[16,64,512]{2,1,0:T(8,128)(2,1)}), bf16[16,64,512]{2,1,0:T(8,128)(2,1)S(1)}, u32[]{:S(2)}, u32[]{:S(2)}) async-start(bf16[16,64,512]{2,1,0:T(8,128)(2,1)} %bitcast.92), calls=%async_computation | async-start | bytes 2097152 | tf_op jit(solution)/shard_map/all_to_all | solution.py:110
  244.4 60.1 %copy-start.3 = (bf16[512,512]{1,0:T(8,128)(2,1)S(1)}, bf16[512,512]{1,0:T(8,128)(2,1)}, u32[]{:S(2)}) copy-start(bf16[512,512]{1,0:T(8,128)(2,1)} %gather_fusion.3) | copy-start | bytes 1572868
  244.4 62.2 %copy-start.13 = (f32[512]{0:T(512)S(1)}, f32[512]{0:T(512)}, u32[]{:S(2)}) copy-start(f32[512]{0:T(512)} %param.23) | copy-start | bytes 6148
  306.6 14.0 %copy-start.7 = (s32[1024]{0:T(1024)S(1)}, s32[1024]{0:T(1024)}, u32[]{:S(2)}) copy-start(s32[1024]{0:T(1024)} %get-tuple-element.83) | copy-start | bytes 12292
  320.6 10.0 %copy-start.9 = (s32[512]{0:T(512)S(1)}, s32[512]{0:T(512)}, u32[]{:S(2)}) copy-start(s32[512]{0:T(512)} %copy-done.8) | copy-start | bytes 6148
  325.7 29.8 %all-to-all-start.1 = ((bf16[16,64,512]{2,1,0:T(8,128)(2,1)}), bf16[16,64,512]{2,1,0:T(8,128)(2,1)S(1)}, u32[]{:S(2)}, u32[]{:S(2)}) async-start(bf16[16,64,512]{2,1,0:T(8,128)(2,1)} %bitcast.93), calls=%async_computation.1 | async-start | bytes 2097152 | tf_op jit(solution)/shard_map/all_to_all | solution.py:50
Sparse Core Ops, SparseCore 0:
  9.7 118.9 all-gather.1
where the time goes:
time: 368 us; the launch traced here: 365 us
  local copies, waits for them, and re-layouts  147 us (40%)
  matrix products  92.8 us (25%)
  waiting for transfers between devices  60.5 us (16%)
  starting transfers between devices  31.7 us (9%)
  other arithmetic  19.1 us (5%)
  between operations  13.8 us (4%)
    gather x2, local copies, waits for them, and re-layouts, body(): gathered = lookup[neighbours]  74.6 us
    sub x8, matrix products, attend(): weights = jnp.exp(scores - row_max)  34.1 us
    dot_general x8, matrix products, attend(): jnp.einsum('hpqk,hdpk->hdpq', weights, value_part, preferred_element_type...  26 us
    concatenate x1, local copies, waits for them, and re-layouts, body(): jnp.concatenate([gathered[:, :13], features[:, None], gathered[:, 13:]],...  25.9 us
    all_to_all x1, waiting for transfers between devices, body(): lax.all_to_all(outgoing, 'blocks', split_axis=0, concat_axis=0, tiled=True)  24.8 us
    all_to_all x1, waiting for transfers between devices, return_rows(): lax.all_to_all(outgoing, 'blocks', split_axis=0, concat_axis=0, tiled=True)  24.8 us
    ppermute x8, starting transfers between devices, shifted(): lax.ppermute(value, axis, [(source, source + steps) for source in range(i...  19.4 us
    dot_general x1, matrix products, body(): jnp.dot(stacked, whole_kernel, preferred_element_type=jnp.float32)  14.9 us
  transfers between devices with their start and end apart: 11, of which 4 were waited for; matrix products, arithmetic and copies ran while one was open for 39% of the time, Pallas kernels for 0%

commit v1 on v0

v1 whole, which is shorter than its diff:
```python
import functools
import math

import jax
import jax.numpy as jnp
from jax import lax
from jax.experimental import pallas as pl
from jax.experimental.pallas import tpu as pltpu
from jax.sharding import PartitionSpec as P

HEADS = 32
GY = 8
HD = 16
TAPS = 27
EPSILON = 1e-05
STEPS_X = (-1, -1, -1, 0, 0, 1, 1, 1)
STEPS_Y = (-1, 0, 1, -1, 1, -1, 0, 1)
F32 = jnp.float32
BF16 = jnp.bfloat16
MIB = 1 << 20


def dot(left, right):
    return jnp.dot(left, right, preferred_element_type=F32)


def layer_norm(inputs, gain_vector):
    row_mean = jnp.mean(inputs, axis=-1, keepdims=True)
    centred = inputs - row_mean
    variance = jnp.mean(centred * centred, axis=-1, keepdims=True)
    return centred * lax.rsqrt(variance + EPSILON) * gain_vector


def one_hot(mask):
    return jnp.where(mask, 1.0, 0.0).astype(BF16)


def call(kernel, out_shape, limit, flops, moved, **extra):
    return pl.pallas_call(
        kernel,
        out_shape=out_shape,
        compiler_params=pltpu.CompilerParams(vmem_limit_bytes=limit * MIB),
        cost_estimate=pl.CostEstimate(flops=flops, bytes_accessed=moved, transcendentals=0),
        **extra,
    )


def faces_kernel(unit, features_ref, rows_ref, ordered_ref, faces_ref):
    points, width = features_ref.shape
    half = width // 2
    place = lax.broadcasted_iota(jnp.int32, (width, width), 1)
    within = lax.rem(place, half)
    source = (within // unit) * (2 * unit) + (place // half) * unit + lax.rem(place, unit)
    channel = lax.broadcasted_iota(jnp.int32, (width, width), 0)
    ordered = dot(features_ref[...], one_hot(channel == source)).astype(BF16)
    ordered_ref[...] = ordered
    row_ids = lax.broadcasted_iota(jnp.int32, (rows_ref.shape[0], points), 1)
    faces_ref[...] = dot(one_hot(rows_ref[...] == row_ids), ordered).astype(BF16)


def gather_kernel(own_rows, other_rows, own_table, other_table, own_out, other_out):
    tap = pl.program_id(0)
    points, lanes = own_rows.shape
    chosen = lax.broadcasted_iota(jnp.int32, (points, lanes), 1) == tap
    row_ids = lax.broadcasted_iota(jnp.int32, (1, own_table.shape[0]), 1).astype(F32)
    for rows, table, out in ((own_rows, own_table, own_out), (other_rows, other_table, other_out)):
        column = jnp.sum(jnp.where(chosen, rows[...], 0.0), axis=1, keepdims=True)
        out[...] = dot(one_hot(column == row_ids), table[...]).astype(BF16)


def conv_kernel(stacked_ref, weight_ref, out_ref):
    product = dot(stacked_ref[...], weight_ref[...])

    @pl.when(pl.program_id(0) == 0)
    def _():
        out_ref[...] = product

    @pl.when(pl.program_id(0) > 0)
    def _():
        out_ref[...] += product


def conv_part(stacked, weight):
    points, depth = stacked.shape
    width = weight.shape[1]
    step = 3 * (width // 2)
    return call(
        conv_kernel,
        jax.ShapeDtypeStruct((points, width), F32),
        32,
        2 * points * depth * width,
        2 * depth * (points + width),
        grid=(depth // step,),
        in_specs=[
            pl.BlockSpec((points, step), lambda k: (0, k)),
            pl.BlockSpec((step, width), lambda k: (k, 0)),
        ],
        out_specs=pl.BlockSpec((points, width), lambda k: (0, 0)),
    )(stacked, weight)


def mix_kernel(own_ref, got_ref, features_ref, weight_ref, gain_ref, slot_ref, out_ref):
    convolved = (own_ref[...] + got_ref[...]).astype(BF16)
    linear = dot(convolved, weight_ref[...])
    mixed = (features_ref[...].astype(F32) + layer_norm(linear, gain_ref[...])).astype(BF16)
    slots = lax.broadcasted_iota(jnp.int32, (out_ref.shape[0], mixed.shape[0]), 0)
    out_ref[...] = dot(one_hot(slots == slot_ref[...]), mixed).astype(BF16)


def block_kernel(
    arrived_ref,
    slot_col_ref,
    slot_row_ref,
    attn_gain_ref,
    qv_ref,
    key_ref,
    proj_ref,
    mlp_gain_ref,
    up_ref,
    down_ref,
    out_ref,
    serial_ref,
    qv_cols_ref,
    keys_ref,
    heads_ref,
    total_ref,
):
    slots = arrived_ref.shape[0]
    points, width = serial_ref.shape
    slot_ids = lax.broadcasted_iota(jnp.int32, (points, slots), 1)
    serial = dot(one_hot(slot_col_ref[...] == slot_ids), arrived_ref[...])
    serial_ref[...] = serial
    normed = layer_norm(serial, attn_gain_ref[...]).astype(BF16)
    keys_ref[...] = dot(normed, key_ref[...]).astype(BF16)
    factor = math.log2(math.e) / math.sqrt(HD)
    contract_last = (((1,), (1,)), ((), ()))
    qv_cols_ref[:width] = (
        lax.dot_general(qv_ref[:width], normed, contract_last, preferred_element_type=F32) * factor
    ).astype(BF16)
    qv_cols_ref[width:] = lax.dot_general(
        qv_ref[width:], normed, contract_last, preferred_element_type=F32
    ).astype(BF16)
    ones = jnp.ones((HD, points), BF16)
    per_group = 128 // HD
    head_of_row = lax.broadcasted_iota(jnp.int32, (128, points), 0) // HD

    for group in range(HEADS // per_group):
        base = group * 128

        def attend(head, carry):
            group_queries = qv_cols_ref[base : base + 128]
            queries = jnp.where(head_of_row == head, group_queries.astype(F32), 0.0).astype(BF16)
            scores = dot(keys_ref[:, base : base + 128], queries)
            weights = jnp.exp2(scores - jnp.max(scores, axis=0, keepdims=True)).astype(BF16)
            at = pl.multiple_of(base + head * HD, HD)
            values = qv_cols_ref[pl.ds(width + at, HD)]
            sums = dot(jnp.concatenate([values, ones], axis=0), weights)
            heads_ref[pl.ds(at, HD)] = (sums[:HD] / sums[HD : HD + 1]).astype(BF16)
            return carry

        lax.fori_loop(0, per_group, attend, 0, unroll=2)

    update = lax.dot_general(
        heads_ref[...], proj_ref[...], (((0,), (0,)), ((), ())), preferred_element_type=F32
    )
    attended = (serial_ref[...] + update).astype(BF16).astype(F32)
    hidden_in = layer_norm(attended, mlp_gain_ref[...]).astype(BF16)
    total_ref[...] = attended
    chunk = width
    for start in range(0, up_ref.shape[1], chunk):
        raised = dot(hidden_in, up_ref[:, start : start + chunk])
        hidden = (raised * (1.0 + lax.erf(raised * math.sqrt(0.5))) * 0.5).astype(BF16)
        total_ref[...] += dot(hidden, down_ref[start : start + chunk])
    finished = total_ref[...].astype(BF16)
    slot_rows = lax.broadcasted_iota(jnp.int32, (slots, points), 0)
    out_ref[...] = dot(one_hot(slot_rows == slot_row_ref[...]), finished).astype(BF16)


def return_kernel(arrived_ref, slot_ref, out_ref):
    slot_ids = lax.broadcasted_iota(jnp.int32, (out_ref.shape[0], arrived_ref.shape[0]), 1)
    out_ref[...] = dot(one_hot(slot_ref[...] == slot_ids), arrived_ref[...]).astype(BF16)


def exchange_faces(faces, devices, index):
    zero = jnp.zeros_like(faces[0])
    received = [zero] * 8

    def valid(source, dx, dy):
        return 0 <= source // GY + dx < devices // GY and 0 <= source % GY + dy < GY

    if devices == 2 * GY:
        lower = index < GY
        for dy in (-1, 0, 1):
            payload = jnp.where(lower, faces[6 + dy], faces[1 + dy])
            pairs = []
            for source in range(devices):
                dx = 1 if source < GY else -1
                if valid(source, dx, dy):
                    pairs.append((source, source + dx * GY + dy))
            got = lax.ppermute(payload, "blocks", pairs)
            received[1 + dy] = jnp.where(lower, got, zero)
            received[6 + dy] = jnp.where(lower, zero, got)
        rest = (3, 4)
    else:
        rest = range(8)
    for facing in rest:
        dx, dy = STEPS_X[facing], STEPS_Y[facing]
        pairs = [
            (source, source + dx * GY + dy) for source in range(devices) if valid(source, dx, dy)
        ]
        received[facing] = lax.ppermute(faces[facing], "blocks", pairs)
    return received


def padded_taps(neighbours):
    points = neighbours.shape[0]
    own = jnp.arange(points, dtype=jnp.int32)[:, None]
    rest = jnp.zeros((points, 128 - TAPS), jnp.int32)
    middle = TAPS // 2
    return jnp.concatenate(
        [neighbours[:, :middle], own, neighbours[:, middle:], rest], axis=1
    ).astype(F32)


def body(
    features,
    conv_weight,
    cpe_weight,
    cpe_gain,
    attn_gain,
    qkv_weight,
    proj_weight,
    mlp_gain,
    up_weight,
    down_weight,
    face_rows,
    neighbours,
    serial_rank,
    serial_order,
):
    points, width = features.shape
    half = width // 2
    devices = lax.axis_size("blocks")
    index = lax.axis_index("blocks")
    core = lax.rem(index, 2)
    partner = [(source, source ^ 1) for source in range(devices)]
    capacity = 2 * points // devices
    slots = devices * capacity

    unit = conv_weight.shape[0] // TAPS
    units = conv_weight.reshape(TAPS, unit, width)
    kept, sent = units[0::2], units[1::2]
    got = lax.ppermute(sent, "blocks", partner)
    mine = jnp.where(
        core == 0, jnp.concatenate([kept, got]), jnp.concatenate([got, kept])
    ).reshape(TAPS * unit, width)
    same_core = [list(range(first, devices, 2)) for first in range(2)]
    weight = lax.all_gather(mine, "blocks", axis=0, tiled=True, axis_index_groups=same_core)

    face_list = face_rows.reshape(-1, 1)
    ordered, faces = call(
        functools.partial(faces_kernel, unit),
        (
            jax.ShapeDtypeStruct((points, width), BF16),
            jax.ShapeDtypeStruct((face_list.shape[0], width), BF16),
        ),
        32,
        4 * points * width * width,
        8 * points * width,
    )(features, face_list)
    received = exchange_faces(faces.reshape(8, -1, width), devices, index)
    table = jnp.concatenate([ordered] + received, axis=0)
    own_table = lax.dynamic_slice(table, (0, core * half), (table.shape[0], half))
    other_half = lax.dynamic_slice(table, (0, (1 - core) * half), (table.shape[0], half))
    other_table = lax.ppermute(other_half, "blocks", partner)
    other_neighbours = lax.ppermute(neighbours, "blocks", partner)
    whole = lambda tap: (0, 0)
    column = lambda tap: (0, tap)
    own_stacked, other_stacked = call(
        gather_kernel,
        (jax.ShapeDtypeStruct((points, TAPS * half), BF16),) * 2,
        40,
        4 * TAPS * points * table.shape[0] * half,
        4 * TAPS * points * half,
        grid=(TAPS,),
        in_specs=[
            pl.BlockSpec((points, 128), whole),
            pl.BlockSpec((points, 128), whole),
            pl.BlockSpec((table.shape[0], half), whole),
            pl.BlockSpec((table.shape[0], half), whole),
        ],
        out_specs=[pl.BlockSpec((points, half), column)] * 2,
    )(padded_taps(neighbours), padded_taps(other_neighbours), own_table, other_table)

    positions = jnp.arange(points, dtype=jnp.int32)
    target = serial_rank // points
    earlier = (target[None, :] == target[:, None]) & (serial_rank[None, :] < serial_rank[:, None])
    out_slot = target * capacity + jnp.sum(earlier.astype(jnp.int32), axis=1)
    anchor = serial_order // points
    before = (anchor[None, :] == anchor[:, None]) & (positions[None, :] < positions[:, None])
    in_slot = anchor * capacity + jnp.sum(before.astype(jnp.int32), axis=1)

    for_partner = conv_part(other_stacked, weight)
    from_partner = lax.ppermute(for_partner, "blocks", partner)
    own_part = conv_part(own_stacked, weight)

    outgoing = call(
        mix_kernel,
        jax.ShapeDtypeStruct((slots, width), BF16),
        32,
        2 * points * width * (width + slots),
        8 * points * width,
    )(
        own_part,
        from_partner,
        features,
        cpe_weight,
        cpe_gain.reshape(1, width),
        out_slot.reshape(1, points),
    )
    arrived = lax.all_to_all(
        outgoing.reshape(devices, capacity, width), "blocks", split_axis=0, concat_axis=0, tiled=True
    ).reshape(slots, width)

    key_weight = qkv_weight[:, width : 2 * width]
    qv_weight = jnp.concatenate([qkv_weight[:, :width], qkv_weight[:, 2 * width :]], axis=1).T
    back = call(
        block_kernel,
        jax.ShapeDtypeStruct((slots, width), BF16),
        48,
        20 * points * width * width,
        16 * width * width,
        scratch_shapes=[
            pltpu.VMEM((points, width), F32),
            pltpu.VMEM((2 * width, points), BF16),
            pltpu.VMEM((points, width), BF16),
            pltpu.VMEM((width, points), BF16),
            pltpu.VMEM((points, width), F32),
        ],
    )(
        arrived,
        in_slot.reshape(points, 1),
        in_slot.reshape(1, points),
        attn_gain.reshape(1, width),
        qv_weight,
        key_weight,
        proj_weight,
        mlp_gain.reshape(1, width),
        up_weight,
        down_weight,
    )
    returned = lax.all_to_all(
        back.reshape(devices, capacity, width), "blocks", split_axis=0, concat_axis=0, tiled=True
    ).reshape(slots, width)
    return call(
        return_kernel,
        jax.ShapeDtypeStruct((points, width), BF16),
        32,
        2 * points * slots * width,
        6 * points * width,
    )(returned, out_slot.reshape(points, 1))


def solution(mesh):
    placed = (
        P(("groups", "blocks"), None),
        P("blocks", None),
        P(),
        P(),
        P(),
        P(),
        P(),
        P(),
        P(),
        P(),
        P(("groups", "blocks"), None, None),
        P(("groups", "blocks"), None),
        P(("groups", "blocks")),
        P(("groups", "blocks")),
    )
    return jax.shard_map(
        body, mesh=mesh, in_specs=placed, out_specs=P(("groups", "blocks"), None), check_vma=False
    )
```

time: 368 us -> 240 us (0.65)
  local copies, waits for them, and re-layouts: 147 us -> 15.8 us
  matrix products: 92.8 us -> 0 us
  Pallas kernels: 0 us -> 65.3 us
  waiting for transfers between devices: 60.5 us -> 110 us
  other arithmetic: 19.1 us -> 3.39 us
    gather x7 -> x0, local copies, waits for them, and re-layouts: 92.5 us -> none  [the longest x2 74.6 us: body(): gathered = lookup[neighbours]]
    pallas_call x0 -> x7, Pallas kernels: none -> 65.3 us  [the longest x1 25.9 us: body(): call(block_kernel, jax.ShapeDtypeStruct((slots, width), BF16), 48, 20 * p...]
    all_gather x1, waiting for transfers between devices: 0.01 us -> 62.2 us  [body(): lax.all_gather(mine, 'blocks', axis=0, tiled=True, axis_index_groups=same...]
    dot_general x13 -> x0, matrix products: 58.7 us -> none  [the longest x8 26 us: attend(): jnp.einsum('hpqk,hdpk->hdpq', weights, value_part, preferred_element_type...]
    sub x8 -> x0, matrix products: 34.1 us -> none  [attend(): weights = jnp.exp(scores - row_max)]
    concatenate x5 -> x1, local copies, waits for them, and re-layouts: 28.1 us -> 0.07 us  [padded_taps(): jnp.concatenate([neighbours[:, :middle], own, neighbours[:, middle:], res...]
    concatenate x2 -> x1, other arithmetic: 12.9 us -> 0.01 us  [body(): table = jnp.concatenate([ordered] + received, axis=0)]
    slice x6 -> x7, local copies, waits for them, and re-layouts: 14.5 us -> 3.99 us  [the longest x2 2.1 us: body(): kept, sent = (units[0::2], units[1::2])]
  transfers between devices with their start and end apart: 11 -> 12, of which waited for: 4 -> 8; matrix products, arithmetic and copies ran while one was open for 39% -> 3% of each run, Pallas kernels for 0% -> 12%
where the time goes in v1:
time: 240 us; the launch traced here: 239 us
  waiting for transfers between devices  110 us (46%)
  Pallas kernels  65.3 us (27%)
  starting transfers between devices  31.2 us (13%)
  local copies, waits for them, and re-layouts  15.8 us (7%)
  between operations  13.8 us (6%)
  other arithmetic  3.39 us (1%)
    all_gather x1, waiting for transfers between devices, body(): lax.all_gather(mine, 'blocks', axis=0, tiled=True, axis_index_groups=same...  62.2 us
    pallas_call x1, Pallas kernels, body(): call(block_kernel, jax.ShapeDtypeStruct((slots, width), BF16), 48, 20 * p...  25.9 us
    all_to_all x1, waiting for transfers between devices, body(): lax.all_to_all(back.reshape(devices, capacity, width), 'blocks', split_ax...  24.7 us
    pallas_call x1, Pallas kernels, body(): call(gather_kernel, (jax.ShapeDtypeStruct((points, TAPS * half), BF16),)...  21.6 us
    all_to_all x1, waiting for transfers between devices, body(): lax.all_to_all(outgoing.reshape(devices, capacity, width), 'blocks', spli...  19.6 us
    pallas_call x2, Pallas kernels, conv_part(): call(conv_kernel, jax.ShapeDtypeStruct((points, width), F32), 32, 2 * poi...  13.1 us
    unnamed x34, local copies, waits for them, and re-layouts  11.1 us
    ppermute x3, starting transfers between devices, exchange_faces(): got = lax.ppermute(payload, 'blocks', pairs)  10 us
  transfers between devices with their start and end apart: 12, of which 8 were waited for; matrix products, arithmetic and copies ran while one was open for 3% of the time, Pallas kernels for 12%

profile of v1, /device:TPU:9, one launch (start us, length us, event | category | flops | bytes accessed | tf_op | source)
XLA Modules:
  0.0 239.3 jit_solution(1891792753229691083)
XLA Ops:
  6.5 0.0 all-gather.2.cloned.1.call-start
  6.5 1.1 slice.72
  7.6 0.0 copy-start.4
  7.6 0.7 collective-permute-start.7
  8.3 1.1 slice.71
  9.4 0.3 collective-permute-done.7
  9.7 1.1 maximum_select_fusion
  10.8 0.0 all-gather.2.cloned.1.call-update
  10.9 0.0 copy-done.13
  10.9 0.2 reshape.80.rows_ref
  11.1 0.8 shard_map.136
  11.9 4.5 %collective-permute-start.1 = (bf16[64,512]{1,0:T(8,128)(2,1)S(1)}, bf16[64,512]{1,0:T(8,128)(2,1)S(1)}, u32[]{:S(2)}, u32[]{:S(2)}) collective-permute-start(bf16[64,512]{1,0:T(8,128)(2,1)S(1)} %get-tuple-element.21), channel_id=1, source_target_pairs={{1,8},{2,9},{3,10},{4,11},{5,12},{6,13},{7,14},{9,0},{10,1},{11,2}... | collective-permute-start | bytes 196616 | tf_op jit(solution)/shard_map/ppermute | solution.py:200
  16.4 0.1 collective-permute-start.2
  16.5 5.4 %collective-permute-start.3 = (bf16[64,512]{1,0:T(8,128)(2,1)S(1)}, bf16[64,512]{1,0:T(8,128)(2,1)S(1)}, u32[]{:S(2)}, u32[]{:S(2)}) collective-permute-start(bf16[64,512]{1,0:T(8,128)(2,1)S(1)} %get-tuple-element.22), channel_id=1, source_target_pairs={{0,9},{1,10},{2,11},{3,12},{4,13},{5,14},{6,15},{8,1},{9,2},{10,3}... | collective-permute-start | bytes 196616 | tf_op jit(solution)/shard_map/ppermute | solution.py:200
  21.9 1.9 collective-permute-start.4
  23.9 3.6 %collective-permute-start.5 = (bf16[64,512]{1,0:T(8,128)(2,1)S(1)}, bf16[64,512]{1,0:T(8,128)(2,1)S(1)}, u32[]{:S(2)}, u32[]{:S(2)}) collective-permute-start(bf16[64,512]{1,0:T(8,128)(2,1)S(1)} %get-tuple-element.18), channel_id=1, source_target_pairs={{0,1},{1,2},{2,3},{3,4},{4,5},{5,6},{6,7},{8,9},{9,10},{10,11},{11... | collective-permute-start | bytes 196616 | tf_op jit(solution)/shard_map/ppermute | solution.py:211
  27.5 0.1 copy.30
  27.7 0.0 collective-permute-done.1
  27.7 0.1 collective-permute-start
  27.8 0.0 collective-permute-done.2
  27.9 1.3 collective-permute-done.3
  29.2 0.1 collective-permute-done.4
  29.3 0.8 collective-permute-done.5
  30.2 0.1 constant_dynamic-slice_fusion
  30.2 3.2 %collective-permute-start.6 = (bf16[1024,256]{1,0:T(8,128)(2,1)S(1)}, bf16[1024,256]{1,0:T(8,128)(2,1)S(1)}, u32[]{:S(2)}, u32[]{:S(2)}) collective-permute-start(bf16[1024,256]{1,0:T(8,128)(2,1)S(1)} %get-tuple-element.16), channel_id=1, source_target_pairs={{0,1},{1,0},{2,3},{3,2},{4,5},{5,4},{6,7},{7,6},{8,9},{9,8},{10,11... | collective-permute-start | bytes 1572872 | tf_op jit(solution)/shard_map/ppermute | solution.py:275
  33.5 0.1 copy.28
  33.6 0.1 copy.29
  33.8 0.1 pad.13.clone
  33.9 0.0 collective-permute-done
  33.9 0.1 fusion.7
  34.0 0.3 add_convert_fusion.1
  34.3 0.7 collective-permute-done.6.other_table
  35.0 21.6 %shard_map.137 = (bf16[512,6912]{1,0:T(8,128)(2,1)S(1)}, bf16[512,6912]{1,0:T(8,128)(2,1)}) custom-call(f32[512,128]{1,0:T(8,128)S(1)} %get-tuple-element.24.own_rows, f32[512,128]{1,0:T(8,128)S(1)} %get-tuple-element.23.other_rows, bf16[1024,256]{1,0:T(8,128)(2,1)S(1)} %get-tuple-element.17.own_table, bf16[1024,256]{1,0:T(8,128)(2,1)S(1)} %collective-permute-done.6.other_table), custom_call_target="tpu_custom_call" | custom-call | flops 14495514624 | bytes 14155776 | tf_op jit(solution)/shard_map/pallas_call | solution.py:279
  56.6 2.8 %copy-done.1 = bf16[512,6912]{1,0:T(8,128)(2,1)} copy-done((bf16[512,6912]{1,0:T(8,128)(2,1)}, bf16[512,6912]{1,0:T(8,128)(2,1)S(1)}, u32[]{:S(2)}) %copy-start.1) | copy-done | bytes 7077912
  59.5 62.2 %all-gather.2.cloned.1.call-done.weight_ref = bf16[6912,512]{1,0:T(8,128)(2,1)} async-done(((bf16[864,512]{1,0:T(8,128)(2,1)}), bf16[6912,512]{1,0:T(8,128)(2,1)}) %all-gather.2.cloned.1.call-update) | async-done | bytes 7077904 | tf_op jit(solution)/shard_map/all_gather | solution.py:258
  121.7 3.0 %copy-done = bf16[6912,512]{1,0:T(8,128)(2,1)S(1)} copy-done((bf16[6912,512]{1,0:T(8,128)(2,1)S(1)}, bf16[6912,512]{1,0:T(8,128)(2,1)}, u32[]{:S(2)}) %copy-start) | copy-done | bytes 7077912
  124.7 3.0 %copy-done.3 = bf16[512,6912]{1,0:T(8,128)(2,1)S(1)} copy-done((bf16[512,6912]{1,0:T(8,128)(2,1)S(1)}, bf16[512,6912]{1,0:T(8,128)(2,1)}, u32[]{:S(2)}) %copy-start.3) | copy-done | bytes 7077912
  127.7 6.6 %shard_map.139 = f32[512,512]{1,0:T(8,128)S(1)} custom-call(bf16[512,6912]{1,0:T(8,128)(2,1)S(1)} %copy-done.3, bf16[6912,512]{1,0:T(8,128)(2,1)S(1)} %copy-done), custom_call_target="tpu_custom_call" | custom-call | flops 3623878656 | bytes 14155776 | tf_op jit(solution)/shard_map/pallas_call | solution.py:87
  134.2 1.3 collective-permute-start.8
  135.6 0.0 copy-done.11
  135.6 0.3 convert_reduce_fusion.1
  135.9 0.0 copy-done.2
  135.9 0.0 copy-start.5
  136.0 0.0 copy-start.6
  136.0 6.6 %shard_map.138.own_ref = f32[512,512]{1,0:T(8,128)S(1)} custom-call(bf16[512,6912]{1,0:T(8,128)(2,1)S(1)} %copy-done.2, bf16[6912,512]{1,0:T(8,128)(2,1)S(1)} %copy-done), custom_call_target="tpu_custom_call" | custom-call | flops 3623878656 | bytes 14155776 | tf_op jit(solution)/shard_map/pallas_call | solution.py:87
  142.5 0.0 collective-permute-done.8.got_ref
  142.6 2.3 shard_map.140
  144.9 5.4 %all-to-all-start = ((bf16[16,64,512]{2,1,0:T(8,128)(2,1)}), bf16[16,64,512]{2,1,0:T(8,128)(2,1)S(1)}, u32[]{:S(2)}, u32[]{:S(2)}) async-start(bf16[16,64,512]{2,1,0:T(8,128)(2,1)} %bitcast.4), calls=%async_computation | async-start | bytes 2097152 | tf_op jit(solution)/shard_map/all_to_all | solution.py:321
  150.2 1.5 fusion.5
  151.7 0.0 copy-start.7
  151.7 0.0 copy-start.8
  151.7 0.0 copy-start.9
  151.8 1.0 copy.36
  152.8 1.0 copy.37
  153.8 0.2 convert_reduce_fusion
  154.1 0.1 copy.34.slot_col_ref
  154.2 1.3 maximum_bitcast_fusion.qv_ref
  155.5 19.6 %all-to-all-done = bf16[16,64,512]{2,1,0:T(8,128)(2,1)S(1)} async-done(((bf16[16,64,512]{2,1,0:T(8,128)(2,1)}), bf16[16,64,512]{2,1,0:T(8,128)(2,1)S(1)}, u32[]{:S(2)}, u32[]{:S(2)}) %all-to-all-start) | async-done | bytes 1048608 | tf_op jit(solution)/shard_map/all_to_all | solution.py:321
  175.1 0.0 copy-done.8
  175.1 25.9 %shard_map.141 = bf16[1024,512]{1,0:T(8,128)(2,1)} custom-call(bf16[1024,512]{1,0:T(8,128)(2,1)S(1)} %bitcast.15, s32[512,1]{1,0:T(8,128)S(1)} %copy.34.slot_col_ref, s32[1,512]{1,0:T(1,128)S(1)} %bitcast.20, f32[1,512]{1,0:T(1,128)S(1)} %bitcast.22, bf16[1024,512]{1,0:T(8,128)(2,1)S(1)} %maximum_bitcast_fusion.qv_ref, ...), custom_call_target="tpu_custom_call" | custom-call | flops 2684354560 | bytes 4194304 | tf_op jit(solution)/shard_map/pallas_call | solution.py:327
  201.1 4.9 %all-to-all-start.1 = ((bf16[16,64,512]{2,1,0:T(8,128)(2,1)}), bf16[16,64,512]{2,1,0:T(8,128)(2,1)S(1)}, u32[]{:S(2)}, u32[]{:S(2)}) async-start(bf16[16,64,512]{2,1,0:T(8,128)(2,1)} %bitcast.11), calls=%async_computation.1 | async-start | bytes 2097152 | tf_op jit(solution)/shard_map/all_to_all | solution.py:352
  206.0 0.1 copy.35.slot_ref
  206.2 24.7 %all-to-all-done.1 = bf16[16,64,512]{2,1,0:T(8,128)(2,1)S(1)} async-done(((bf16[16,64,512]{2,1,0:T(8,128)(2,1)}), bf16[16,64,512]{2,1,0:T(8,128)(2,1)S(1)}, u32[]{:S(2)}, u32[]{:S(2)}) %all-to-all-start.1) | async-done | bytes 1048608 | tf_op jit(solution)/shard_map/all_to_all | solution.py:352
  230.8 1.6 shard_map.142
  (32 shorter events, 0.3 us)
Async XLA Ops:
  6.5 115.1 %all-gather.2.cloned.1.call-start = ((), (), s32[]{:S(2)}) async-start(), calls=%async_computation.2 | async-start | bytes 7962624 | tf_op jit(solution)/shard_map/all_gather | solution.py:258
  6.5 4.3 %copy-start.13 = (s32[1,8,64]{2,1,0:T(8,128)S(1)}, s32[1,8,64]{2,1,0:T(8,128)}, u32[]{:S(2)}) copy-start(s32[1,8,64]{2,1,0:T(8,128)} %param.24) | copy-start | bytes 6148
  7.6 3.5 %copy-start.4 = (bf16[512,512]{1,0:T(8,128)(2,1)S(1)}, bf16[512,512]{1,0:T(8,128)(2,1)}, u32[]{:S(2)}) copy-start(bf16[512,512]{1,0:T(8,128)(2,1)} %features_ref.3) | copy-start | bytes 1572868
  7.6 2.1 collective-permute-start.7
  10.8 16.7 %copy-start.10 = (s32[512,26]{0,1:T(8,128)S(1)}, s32[512,26]{0,1:T(8,128)}, u32[]{:S(2)}) copy-start(s32[512,26]{0,1:T(8,128)} %param.25) | copy-start | bytes 159748
  11.9 15.8 %collective-permute-start.1 = (bf16[64,512]{1,0:T(8,128)(2,1)S(1)}, bf16[64,512]{1,0:T(8,128)(2,1)S(1)}, u32[]{:S(2)}, u32[]{:S(2)}) collective-permute-start(bf16[64,512]{1,0:T(8,128)(2,1)S(1)} %get-tuple-element.21), channel_id=1, source_target_pairs={{1,8},{2,9},{3,10},{4,11},{5,12},{6,13},{7,14},{9,0},{10,1},{11,2}... | collective-permute-start | bytes 196616 | tf_op jit(solution)/shard_map/ppermute | solution.py:200
  16.4 11.4 %collective-permute-start.2 = (bf16[64,512]{1,0:T(8,128)(2,1)S(1)}, bf16[64,512]{1,0:T(8,128)(2,1)S(1)}, u32[]{:S(2)}, u32[]{:S(2)}) collective-permute-start(bf16[64,512]{1,0:T(8,128)(2,1)S(1)} %get-tuple-element.19), channel_id=1, source_target_pairs={{0,8},{1,9},{2,10},{3,11},{4,12},{5,13},{6,14},{7,15},{8,0},{9,1},... | collective-permute-start | bytes 196616 | tf_op jit(solution)/shard_map/ppermute | solution.py:200
  16.5 12.6 %collective-permute-start.3 = (bf16[64,512]{1,0:T(8,128)(2,1)S(1)}, bf16[64,512]{1,0:T(8,128)(2,1)S(1)}, u32[]{:S(2)}, u32[]{:S(2)}) collective-permute-start(bf16[64,512]{1,0:T(8,128)(2,1)S(1)} %get-tuple-element.22), channel_id=1, source_target_pairs={{0,9},{1,10},{2,11},{3,12},{4,13},{5,14},{6,15},{8,1},{9,2},{10,3}... | collective-permute-start | bytes 196616 | tf_op jit(solution)/shard_map/ppermute | solution.py:200
  21.9 7.4 %collective-permute-start.4 = (bf16[64,512]{1,0:T(8,128)(2,1)S(1)}, bf16[64,512]{1,0:T(8,128)(2,1)S(1)}, u32[]{:S(2)}, u32[]{:S(2)}) collective-permute-start(bf16[64,512]{1,0:T(8,128)(2,1)S(1)} %get-tuple-element.20), channel_id=1, source_target_pairs={{1,0},{2,1},{3,2},{4,3},{5,4},{6,5},{7,6},{9,8},{10,9},{11,10},{12... | collective-permute-start | bytes 196616 | tf_op jit(solution)/shard_map/ppermute | solution.py:211
  23.9 6.2 %collective-permute-start.5 = (bf16[64,512]{1,0:T(8,128)(2,1)S(1)}, bf16[64,512]{1,0:T(8,128)(2,1)S(1)}, u32[]{:S(2)}, u32[]{:S(2)}) collective-permute-start(bf16[64,512]{1,0:T(8,128)(2,1)S(1)} %get-tuple-element.18), channel_id=1, source_target_pairs={{0,1},{1,2},{2,3},{3,4},{4,5},{5,6},{6,7},{8,9},{9,10},{10,11},{11... | collective-permute-start | bytes 196616 | tf_op jit(solution)/shard_map/ppermute | solution.py:211
  27.7 6.1 %collective-permute-start = (s32[512,26]{1,0:T(8,128)S(1)}, s32[512,26]{1,0:T(8,128)S(1)}, u32[]{:S(2)}, u32[]{:S(2)}) collective-permute-start(s32[512,26]{1,0:T(8,128)S(1)} %copy.30), channel_id=1, source_target_pairs={{0,1},{1,0},{2,3},{3,2},{4,5},{5,4},{6,7},{7,6},{8,9},{9,8},{10,11... | collective-permute-start | bytes 159752 | tf_op jit(solution)/shard_map/ppermute | solution.py:276
  30.2 4.8 %collective-permute-start.6 = (bf16[1024,256]{1,0:T(8,128)(2,1)S(1)}, bf16[1024,256]{1,0:T(8,128)(2,1)S(1)}, u32[]{:S(2)}, u32[]{:S(2)}) collective-permute-start(bf16[1024,256]{1,0:T(8,128)(2,1)S(1)} %get-tuple-element.16), channel_id=1, source_target_pairs={{0,1},{1,0},{2,3},{3,2},{4,5},{5,4},{6,7},{7,6},{8,9},{9,8},{10,11... | collective-permute-start | bytes 1572872 | tf_op jit(solution)/shard_map/ppermute | solution.py:275
  56.6 2.8 %copy-start.1 = (bf16[512,6912]{1,0:T(8,128)(2,1)}, bf16[512,6912]{1,0:T(8,128)(2,1)S(1)}, u32[]{:S(2)}) copy-start(bf16[512,6912]{1,0:T(8,128)(2,1)S(1)} %get-tuple-element.11.stacked_ref) | copy-start | bytes 21233668
  121.7 3.0 %copy-start = (bf16[6912,512]{1,0:T(8,128)(2,1)S(1)}, bf16[6912,512]{1,0:T(8,128)(2,1)}, u32[]{:S(2)}) copy-start(bf16[6912,512]{1,0:T(8,128)(2,1)} %all-gather.2.cloned.1.call-done.weight_ref) | copy-start | bytes 21233668
  124.7 3.0 %copy-start.3 = (bf16[512,6912]{1,0:T(8,128)(2,1)S(1)}, bf16[512,6912]{1,0:T(8,128)(2,1)}, u32[]{:S(2)}) copy-start(bf16[512,6912]{1,0:T(8,128)(2,1)} %get-tuple-element.12.stacked_ref) | copy-start | bytes 21233668
  127.7 7.9 %copy-start.11 = (s32[512]{0:T(512)S(1)}, s32[512]{0:T(512)}, u32[]{:S(2)}) copy-start(s32[512]{0:T(512)} %param.26) | copy-start | bytes 6148
  127.7 8.2 %copy-start.2 = (bf16[512,6912]{1,0:T(8,128)(2,1)S(1)}, bf16[512,6912]{1,0:T(8,128)(2,1)}, u32[]{:S(2)}) copy-start(bf16[512,6912]{1,0:T(8,128)(2,1)} %copy-done.1) | copy-start | bytes 21233668
  134.2 8.3 %collective-permute-start.8 = (f32[512,512]{1,0:T(8,128)S(1)}, f32[512,512]{1,0:T(8,128)S(1)}, u32[]{:S(2)}, u32[]{:S(2)}) collective-permute-start(f32[512,512]{1,0:T(8,128)S(1)} %shard_map.139), channel_id=1, source_target_pairs={{0,1},{1,0},{2,3},{3,2},{4,5},{5,4},{6,7},{7,6},{8,9},{9,8},{10,11... | collective-permute-start | bytes 3145736 | tf_op jit(solution)/shard_map/ppermute | solution.py:304
  135.9 6.6 %copy-start.5 = (bf16[512,512]{1,0:T(8,128)(2,1)S(1)}, bf16[512,512]{1,0:T(8,128)(2,1)}, u32[]{:S(2)}) copy-start(bf16[512,512]{1,0:T(8,128)(2,1)} %weight_ref.1) | copy-start | bytes 1572868
  136.0 6.6 %copy-start.6 = (f32[512]{0:T(512)S(1)}, f32[512]{0:T(512)}, u32[]{:S(2)}) copy-start(f32[512]{0:T(512)} %param.17) | copy-start | bytes 6148
  144.9 30.2 %all-to-all-start = ((bf16[16,64,512]{2,1,0:T(8,128)(2,1)}), bf16[16,64,512]{2,1,0:T(8,128)(2,1)S(1)}, u32[]{:S(2)}, u32[]{:S(2)}) async-start(bf16[16,64,512]{2,1,0:T(8,128)(2,1)} %bitcast.4), calls=%async_computation | async-start | bytes 2097152 | tf_op jit(solution)/shard_map/all_to_all | solution.py:321
  150.2 3.5 %copy-start.12 = (s32[512]{0:T(512)S(1)}, s32[512]{0:T(512)}, u32[]{:S(2)}) copy-start(s32[512]{0:T(512)} %param.27) | copy-start | bytes 6148
  151.7 23.4 %copy-start.7 = (bf16[512,512]{1,0:T(8,128)(2,1)S(1)}, bf16[512,512]{1,0:T(8,128)(2,1)}, u32[]{:S(2)}) copy-start(bf16[512,512]{1,0:T(8,128)(2,1)} %proj_ref.1) | copy-start | bytes 1572868
  151.7 23.4 %copy-start.8 = (f32[512]{0:T(512)S(1)}, f32[512]{0:T(512)}, u32[]{:S(2)}) copy-start(f32[512]{0:T(512)} %param.18) | copy-start | bytes 6148
  151.7 23.4 %copy-start.9 = (f32[512]{0:T(512)S(1)}, f32[512]{0:T(512)}, u32[]{:S(2)}) copy-start(f32[512]{0:T(512)} %param.21) | copy-start | bytes 6148
  201.1 29.8 %all-to-all-start.1 = ((bf16[16,64,512]{2,1,0:T(8,128)(2,1)}), bf16[16,64,512]{2,1,0:T(8,128)(2,1)S(1)}, u32[]{:S(2)}, u32[]{:S(2)}) async-start(bf16[16,64,512]{2,1,0:T(8,128)(2,1)} %bitcast.11), calls=%async_computation.1 | async-start | bytes 2097152 | tf_op jit(solution)/shard_map/all_to_all | solution.py:352
Sparse Core Ops, SparseCore 0:
  11.0 110.6 all-gather.1

commit v2 on v1

--- a/solution.py
+++ b/solution.py
@@ -58,49 +58,115 @@
     faces_ref[...] = dot(one_hot(rows_ref[...] == row_ids), ordered).astype(BF16)
 
 
-def gather_kernel(own_rows, other_rows, own_table, other_table, own_out, other_out):
+def gather_kernel(other_rows, own_rows, other_table, own_table, out_ref):
     tap = pl.program_id(0)
     points, lanes = own_rows.shape
     chosen = lax.broadcasted_iota(jnp.int32, (points, lanes), 1) == tap
     row_ids = lax.broadcasted_iota(jnp.int32, (1, own_table.shape[0]), 1).astype(F32)
-    for rows, table, out in ((own_rows, own_table, own_out), (other_rows, other_table, other_out)):
+    for start, rows, table in ((0, other_rows, other_table), (points, own_rows, own_table)):
         column = jnp.sum(jnp.where(chosen, rows[...], 0.0), axis=1, keepdims=True)
-        out[...] = dot(one_hot(column == row_ids), table[...]).astype(BF16)
-
-
-def conv_kernel(stacked_ref, weight_ref, out_ref):
-    product = dot(stacked_ref[...], weight_ref[...])
-
-    @pl.when(pl.program_id(0) == 0)
+        taken = dot(one_hot(column == row_ids), table[...]).astype(BF16)
+        out_ref[start : start + points] = taken
+
+
+def conv_kernel(pieces, needed, flip_ref, stacked_ref, *refs):
+    sources = len(refs) - 4
+    weights, (other_ref, own_ref, held, sems) = refs[:sources], refs[sources:]
+    step = pl.program_id(0)
+    width = held.shape[1] // sources
+    rows = held.shape[0] // pieces
+    depth, points = stacked_ref.shape[1], own_ref.shape[0]
+
+    def copies(piece):
+        place = jnp.where(flip_ref[0] == 1, pieces - 1 - piece, piece)
+        return [
+            pltpu.make_async_copy(
+                weight.at[place],
+                held.at[pl.ds(piece * rows, rows), pl.ds(at * width, width)],
+                sems.at[at, piece],
+            )
+            for at, weight in enumerate(weights)
+        ]
+
+    @pl.when(step == 0)
     def _():
-        out_ref[...] = product
-
-    @pl.when(pl.program_id(0) > 0)
+        for piece in range(pieces):
+            for copy in copies(piece):
+                copy.start()
+
+    for at, wanted in enumerate(needed):
+
+        @pl.when(step == at)
+        def _():
+            for piece in wanted:
+                for copy in copies(piece):
+                    copy.wait()
+
+    rows_here = pl.ds(pl.multiple_of(step * depth, 256), depth)
+    product = dot(stacked_ref[...], held[rows_here])
+
+    @pl.when(step == 0)
     def _():
-        out_ref[...] += product
-
-
-def conv_part(stacked, weight):
+        other_ref[...] = product[:points]
+        own_ref[...] = product[points:]
+
+    @pl.when(step > 0)
+    def _():
+        other_ref[...] += product[:points]
+        own_ref[...] += product[points:]
+
+
+def conv_part(stacked, flip, weights):
     points, depth = stacked.shape
-    width = weight.shape[1]
-    step = 3 * (width // 2)
+    pieces, rows, columns = weights[0].shape
+    width = columns * len(weights)
+    step = depth // 9
+    ends = [-1] + [(step * (at + 1) - 1) // rows for at in range(9)]
+    needed = [range(ends[at] + 1, ends[at + 1] + 1) for at in range(9)]
     return call(
-        conv_kernel,
-        jax.ShapeDtypeStruct((points, width), F32),
-        32,
+        functools.partial(conv_kernel, pieces, needed),
+        (jax.ShapeDtypeStruct((points // 2, width), F32),) * 2,
+        60,
         2 * points * depth * width,
         2 * depth * (points + width),
-        grid=(depth // step,),
+        grid=(9,),
         in_specs=[
+            pl.BlockSpec(memory_space=pltpu.SMEM),
             pl.BlockSpec((points, step), lambda k: (0, k)),
-            pl.BlockSpec((step, width), lambda k: (k, 0)),
+        ]
+        + [pl.BlockSpec(memory_space=pl.ANY)] * len(weights),
+        out_specs=[pl.BlockSpec((points // 2, width), lambda k: (0, 0))] * 2,
+        scratch_shapes=[
+            pltpu.VMEM((depth, width), BF16),
+            pltpu.SemaphoreType.DMA((len(weights), pieces)),
         ],
-        out_specs=pl.BlockSpec((points, width), lambda k: (0, 0)),
-    )(stacked, weight)
-
-
-def mix_kernel(own_ref, got_ref, features_ref, weight_ref, gain_ref, slot_ref, out_ref):
-    convolved = (own_ref[...] + got_ref[...]).astype(BF16)
+    )(flip, stacked, *weights)
+
+
+def mix_kernel(
+    side_ref,
+    own_ref,
+    got_ref,
+    own_late_ref,
+    got_late_ref,
+    features_ref,
+    weight_ref,
+    gain_ref,
+    slot_ref,
+    out_ref,
+):
+    late = (own_late_ref[...] + got_late_ref[...]).astype(BF16)
+    quarter = late.shape[1] // 2
+    first, second = late[:, :quarter], late[:, quarter:]
+    here = side_ref[0] == 0
+    convolved = jnp.concatenate(
+        [
+            jnp.where(here, first, second),
+            jnp.where(here, second, first),
+            (own_ref[...] + got_ref[...]).astype(BF16),
+        ],
+        axis=1,
+    )
     linear = dot(convolved, weight_ref[...])
     mixed = (features_ref[...].astype(F32) + layer_norm(linear, gain_ref[...])).astype(BF16)
     slots = lax.broadcasted_iota(jnp.int32, (out_ref.shape[0], mixed.shape[0]), 0)
@@ -254,8 +320,24 @@
     mine = jnp.where(
         core == 0, jnp.concatenate([kept, got]), jnp.concatenate([got, kept])
     ).reshape(TAPS * unit, width)
-    same_core = [list(range(first, devices, 2)) for first in range(2)]
-    weight = lax.all_gather(mine, "blocks", axis=0, tiled=True, axis_index_groups=same_core)
+    reverse = unit % 16 == 0
+    even, odd = list(range(0, devices, 2)), list(range(1, devices, 2))
+    same_core = [even, odd[::-1] if reverse else odd]
+    flip = (core if reverse else 0 * core).reshape(1)
+    pieces = devices // 2 if reverse else 1
+
+    def spread(columns):
+        gathered = lax.all_gather(
+            columns, "blocks", axis=0, tiled=True, axis_index_groups=same_core
+        )
+        return gathered.reshape(pieces, -1, columns.shape[1])
+
+    side = lax.axis_index("groups")
+    quarter = width // 4
+    mine_late = jnp.where(side == 0, mine[:, :quarter], mine[:, quarter:half])
+    late = spread(mine_late)
+    weight = spread(mine[:, half:])
+    late_got = lax.ppermute(late, "groups", [(0, 1), (1, 0)])
 
     face_list = face_rows.reshape(-1, 1)
     ordered, faces = call(
@@ -276,10 +358,10 @@
     other_neighbours = lax.ppermute(neighbours, "blocks", partner)
     whole = lambda tap: (0, 0)
     column = lambda tap: (0, tap)
-    own_stacked, other_stacked = call(
+    stacked = call(
         gather_kernel,
-        (jax.ShapeDtypeStruct((points, TAPS * half), BF16),) * 2,
-        40,
+        jax.ShapeDtypeStruct((2 * points, TAPS * half), BF16),
+        60,
         4 * TAPS * points * table.shape[0] * half,
         4 * TAPS * points * half,
         grid=(TAPS,),
@@ -289,8 +371,8 @@
             pl.BlockSpec((table.shape[0], half), whole),
             pl.BlockSpec((table.shape[0], half), whole),
         ],
-        out_specs=[pl.BlockSpec((points, half), column)] * 2,
-    )(padded_taps(neighbours), padded_taps(other_neighbours), own_table, other_table)
+        out_specs=pl.BlockSpec((2 * points, half), column),
+    )(padded_taps(other_neighbours), padded_taps(neighbours), other_table, own_table)
 
     positions = jnp.arange(points, dtype=jnp.int32)
     target = serial_rank // points
@@ -300,9 +382,10 @@
     before = (anchor[None, :] == anchor[:, None]) & (positions[None, :] < positions[:, None])
     in_slot = anchor * capacity + jnp.sum(before.astype(jnp.int32), axis=1)
 
-    for_partner = conv_part(other_stacked, weight)
+    for_partner, own_part = conv_part(stacked, flip, [weight])
     from_partner = lax.ppermute(for_partner, "blocks", partner)
-    own_part = conv_part(own_stacked, weight)
+    for_partner_late, own_late = conv_part(stacked, flip, [late, late_got])
+    from_partner_late = lax.ppermute(for_partner_late, "blocks", partner)
 
     outgoing = call(
         mix_kernel,
@@ -310,9 +393,13 @@
         32,
         2 * points * width * (width + slots),
         8 * points * width,
+        in_specs=[pl.BlockSpec(memory_space=pltpu.SMEM)] + [pl.BlockSpec()] * 8,
     )(
+        side.reshape(1),
         own_part,
         from_partner,
+        own_late,
+        from_partner_late,
         features,
         cpe_weight,
         cpe_gain.reshape(1, width),

time: 240 us -> 249 us (1.038)
  Pallas kernels: 65.3 us -> 80.4 us
  local copies, waits for them, and re-layouts: 15.8 us -> 10.8 us
    all_gather x1 -> x2, waiting for transfers between devices: 62.2 us -> 44.8 us  [spread(): lax.all_gather(columns, 'blocks', axis=0, tiled=True, axis_index_groups=s...]
    pallas_call x3, Pallas kernels: 34.7 us -> 49.8 us  [the longest x2 25.8 us: conv_part(): call(functools.partial(conv_kernel, pieces, needed), (jax.ShapeDtypeStruc...]
    ppermute x0 -> x2, waiting for transfers between devices: none -> 14 us  [the longest x1 14 us: body(): late_got = lax.ppermute(late, 'groups', [(0, 1), (1, 0)])]
    unnamed x34 -> x32, local copies, waits for them, and re-layouts: 11.1 us -> 4.51 us
    ppermute x1, starting transfers between devices: 3.24 us -> 0.01 us  [body(): other_table = lax.ppermute(other_half, 'blocks', partner)]
  transfers between devices with their start and end apart: 12 -> 15, of which waited for: 8 -> 9; matrix products, arithmetic and copies ran while one was open for 3% -> 4% of each run, Pallas kernels for 12% -> 20%
where the time goes in v2:
time: 249 us; the launch traced here: 248 us
  waiting for transfers between devices  109 us (44%)
  Pallas kernels  80.4 us (32%)
  starting transfers between devices  29.9 us (12%)
  between operations  13.8 us (6%)
  local copies, waits for them, and re-layouts  10.8 us (4%)
  other arithmetic  3.95 us (2%)
    all_gather x2, waiting for transfers between devices, spread(): lax.all_gather(columns, 'blocks', axis=0, tiled=True, axis_index_groups=s...  44.8 us
    pallas_call x1, Pallas kernels, body(): call(block_kernel, jax.ShapeDtypeStruct((slots, width), BF16), 48, 20 * p...  25.9 us
    pallas_call x2, Pallas kernels, conv_part(): call(functools.partial(conv_kernel, pieces, needed), (jax.ShapeDtypeStruc...  25.8 us
    all_to_all x1, waiting for transfers between devices, body(): lax.all_to_all(back.reshape(devices, capacity, width), 'blocks', split_ax...  24.7 us
    pallas_call x1, Pallas kernels, body(): call(gather_kernel, jax.ShapeDtypeStruct((2 * points, TAPS * half), BF16)...  24 us
    all_to_all x1, waiting for transfers between devices, body(): lax.all_to_all(outgoing.reshape(devices, capacity, width), 'blocks', spli...  19.6 us
    ppermute x1, waiting for transfers between devices, body(): late_got = lax.ppermute(late, 'groups', [(0, 1), (1, 0)])  14 us
    ppermute x3, starting transfers between devices, exchange_faces(): got = lax.ppermute(payload, 'blocks', pairs)  10 us
  transfers between devices with their start and end apart: 15, of which 9 were waited for; matrix products, arithmetic and copies ran while one was open for 4% of the time, Pallas kernels for 20%

profile of v2, /device:TPU:9, one launch (start us, length us, event | category | flops | bytes accessed | tf_op | source)
XLA Modules:
  0.0 247.8 jit_solution(5700564186594803511)
XLA Ops:
  6.5 1.0 slice.81
  7.6 0.7 collective-permute-start.7
  8.3 1.1 slice.80
  9.4 0.0 copy-start.12
  9.4 0.0 copy-start
  9.4 0.3 collective-permute-done.7
  9.7 0.1 maximum_select_fusion
  9.9 0.7 slice_select_fusion
  10.6 0.0 all-gather.5.cloned.1.call-update
  10.6 0.0 copy-start.9
  10.6 0.0 all-gather.3.cloned.1.call-start
  10.7 0.8 slice.90
  11.5 0.0 all-gather.3.cloned.1.call-update
  11.5 0.2 reshape.96.rows_ref
  11.7 0.8 shard_map.136
  12.6 4.5 %collective-permute-start.1 = (bf16[64,512]{1,0:T(8,128)(2,1)S(1)}, bf16[64,512]{1,0:T(8,128)(2,1)S(1)}, u32[]{:S(2)}, u32[]{:S(2)}) collective-permute-start(bf16[64,512]{1,0:T(8,128)(2,1)S(1)} %get-tuple-element.25), channel_id=1, source_target_pairs={{1,8},{2,9},{3,10},{4,11},{5,12},{6,13},{7,14},{9,0},{10,1},{11,2}... | collective-permute-start | bytes 196616 | tf_op jit(solution)/shard_map/ppermute | solution.py:266
  17.1 0.1 collective-permute-start.2
  17.2 5.4 %collective-permute-start.3 = (bf16[64,512]{1,0:T(8,128)(2,1)S(1)}, bf16[64,512]{1,0:T(8,128)(2,1)S(1)}, u32[]{:S(2)}, u32[]{:S(2)}) collective-permute-start(bf16[64,512]{1,0:T(8,128)(2,1)S(1)} %get-tuple-element.26), channel_id=1, source_target_pairs={{0,9},{1,10},{2,11},{3,12},{4,13},{5,14},{6,15},{8,1},{9,2},{10,3}... | collective-permute-start | bytes 196616 | tf_op jit(solution)/shard_map/ppermute | solution.py:266
  22.6 1.9 collective-permute-start.4
  24.5 3.6 %collective-permute-start.5 = (bf16[64,512]{1,0:T(8,128)(2,1)S(1)}, bf16[64,512]{1,0:T(8,128)(2,1)S(1)}, u32[]{:S(2)}, u32[]{:S(2)}) collective-permute-start(bf16[64,512]{1,0:T(8,128)(2,1)S(1)} %get-tuple-element.22), channel_id=1, source_target_pairs={{0,1},{1,2},{2,3},{3,4},{4,5},{5,6},{6,7},{8,9},{9,10},{10,11},{11... | collective-permute-start | bytes 196616 | tf_op jit(solution)/shard_map/ppermute | solution.py:277
  28.2 0.1 copy.28
  28.4 0.0 collective-permute-done.1
  28.4 0.1 collective-permute-start
  28.5 0.0 collective-permute-done.2
  28.5 2.8 %collective-permute-done.3 = bf16[64,512]{1,0:T(8,128)(2,1)S(1)} collective-permute-done((bf16[64,512]{1,0:T(8,128)(2,1)S(1)}, bf16[64,512]{1,0:T(8,128)(2,1)S(1)}, u32[]{:S(2)}, u32[]{:S(2)}) %collective-permute-start.3) | collective-permute-done | bytes 65568 | tf_op jit(solution)/shard_map/ppermute | solution.py:266
  31.4 1.3 collective-permute-done.4
  32.7 0.9 constant_dynamic-slice_fusion
  33.6 0.1 copy.29
  33.8 0.1 copy.30
  33.9 0.1 pad.13.clone
  34.0 22.6 %all-gather.5.cloned.1.call-done = bf16[6912,128]{1,0:T(8,128)(2,1)} async-done(((bf16[864,128]{1,0:T(8,128)(2,1)}), bf16[6912,128]{1,0:T(8,128)(2,1)}) %all-gather.5.cloned.1.call-update) | async-done | bytes 1769488 | tf_op jit(solution)/shard_map/all_gather | solution.py:330
  56.6 0.3 collective-permute-start.9
  56.9 0.1 fusion.7
  57.0 1.1 add_convert_fusion.1
  58.1 0.0 collective-permute-done.6.other_table
  58.1 24.0 %shard_map.137.stacked_ref = bf16[1024,6912]{1,0:T(8,128)(2,1)} custom-call(f32[512,128]{1,0:T(8,128)} %get-tuple-element.28.other_rows, f32[512,128]{1,0:T(8,128)} %get-tuple-element.27.own_rows, bf16[1024,256]{1,0:T(8,128)(2,1)} %collective-permute-done.6.other_table, bf16[1024,256]{1,0:T(8,128)(2,1)} %get-tuple-element.20.own_table), custom_call_target="tpu_custom_call" | custom-call | flops 14495514624 | bytes 14155776 | tf_op jit(solution)/shard_map/pallas_call | solution.py:361
  82.1 14.0 %collective-permute-done.9.refs_1_ = bf16[8,864,128]{2,1,0:T(8,128)(2,1)S(1)} collective-permute-done((bf16[8,864,128]{2,1,0:T(8,128)(2,1)}, bf16[8,864,128]{2,1,0:T(8,128)(2,1)S(1)}, u32[]{:S(2)}, u32[]{:S(2)}) %collective-permute-start.9) | collective-permute-done | bytes 1769504 | tf_op jit(solution)/shard_map/ppermute | solution.py:340
  96.1 1.2 copy-done.8
  97.3 12.9 %shard_map.139 = (f32[512,256]{1,0:T(8,128)}, f32[512,256]{1,0:T(8,128)}) custom-call(s32[1]{0:T(128)} %bitcast.1.flip_ref, bf16[1024,6912]{1,0:T(8,128)(2,1)} %shard_map.137.stacked_ref, bf16[8,864,128]{2,1,0:T(8,128)(2,1)} %bitcast.32, bf16[8,864,128]{2,1,0:T(8,128)(2,1)} %copy-done.8), custom_call_target="tpu_custom_call" | custom-call | flops 3623878656 | bytes 17694720 | tf_op jit(solution)/shard_map/pallas_call | solution.py:126
  110.3 1.8 collective-permute-start.10
  112.0 22.3 %all-gather.3.cloned.1.call-done = bf16[6912,256]{1,0:T(8,128)(2,1)} async-done(((bf16[864,256]{1,0:T(8,128)(2,1)}), bf16[6912,256]{1,0:T(8,128)(2,1)}) %all-gather.3.cloned.1.call-update) | async-done | bytes 3538960 | tf_op jit(solution)/shard_map/all_gather | solution.py:330
  134.3 12.9 %shard_map.138 = (f32[512,256]{1,0:T(8,128)}, f32[512,256]{1,0:T(8,128)}) custom-call(s32[1]{0:T(128)} %bitcast.1.flip_ref, bf16[1024,6912]{1,0:T(8,128)(2,1)} %shard_map.137.stacked_ref, bf16[8,864,256]{2,1,0:T(8,128)(2,1)} %bitcast.28), custom_call_target="tpu_custom_call" | custom-call | flops 3623878656 | bytes 17694720 | tf_op jit(solution)/shard_map/pallas_call | solution.py:126
  147.3 0.6 collective-permute-start.8
  147.9 0.3 convert_reduce_fusion.1
  148.3 0.0 collective-permute-done.10.got_late_ref
  148.3 1.4 collective-permute-done.8.got_ref
  149.6 1.0 copy-done.3
  150.7 2.3 shard_map.140
  153.0 5.8 %all-to-all-start = ((bf16[16,64,512]{2,1,0:T(8,128)(2,1)}), bf16[16,64,512]{2,1,0:T(8,128)(2,1)S(1)}, u32[]{:S(2)}, u32[]{:S(2)}) async-start(bf16[16,64,512]{2,1,0:T(8,128)(2,1)} %bitcast.8), calls=%async_computation | async-start | bytes 2097152 | tf_op jit(solution)/shard_map/all_to_all | solution.py:408
  158.8 1.5 fusion.5
  160.3 0.0 copy-start.5
  160.3 0.0 copy-start.6
  160.3 0.0 copy-start.7
  160.3 1.0 copy.36
  161.3 1.0 copy.37
  162.3 0.2 convert_reduce_fusion
  162.6 0.1 copy.34.slot_col_ref
  162.7 1.3 maximum_bitcast_fusion.qv_ref
  164.0 19.6 %all-to-all-done = bf16[16,64,512]{2,1,0:T(8,128)(2,1)S(1)} async-done(((bf16[16,64,512]{2,1,0:T(8,128)(2,1)}), bf16[16,64,512]{2,1,0:T(8,128)(2,1)S(1)}, u32[]{:S(2)}, u32[]{:S(2)}) %all-to-all-start) | async-done | bytes 1048608 | tf_op jit(solution)/shard_map/all_to_all | solution.py:408
  183.6 25.9 %shard_map.141 = bf16[1024,512]{1,0:T(8,128)(2,1)} custom-call(bf16[1024,512]{1,0:T(8,128)(2,1)S(1)} %bitcast.19, s32[512,1]{1,0:T(8,128)S(1)} %copy.34.slot_col_ref, s32[1,512]{1,0:T(1,128)S(1)} %bitcast.24, f32[1,512]{1,0:T(1,128)S(1)} %bitcast.26, bf16[1024,512]{1,0:T(8,128)(2,1)S(1)} %maximum_bitcast_fusion.qv_ref, ...), custom_call_target="tpu_custom_call" | custom-call | flops 2684354560 | bytes 4194304 | tf_op jit(solution)/shard_map/pallas_call | solution.py:414
  209.6 5.0 %all-to-all-start.1 = ((bf16[16,64,512]{2,1,0:T(8,128)(2,1)}), bf16[16,64,512]{2,1,0:T(8,128)(2,1)S(1)}, u32[]{:S(2)}, u32[]{:S(2)}) async-start(bf16[16,64,512]{2,1,0:T(8,128)(2,1)} %bitcast.15), calls=%async_computation.1 | async-start | bytes 2097152 | tf_op jit(solution)/shard_map/all_to_all | solution.py:439
  214.5 0.1 copy.35.slot_ref
  214.7 24.7 %all-to-all-done.1 = bf16[16,64,512]{2,1,0:T(8,128)(2,1)S(1)} async-done(((bf16[16,64,512]{2,1,0:T(8,128)(2,1)}), bf16[16,64,512]{2,1,0:T(8,128)(2,1)S(1)}, u32[]{:S(2)}, u32[]{:S(2)}) %all-to-all-start.1) | async-done | bytes 1048608 | tf_op jit(solution)/shard_map/all_to_all | solution.py:439
  239.4 1.6 shard_map.142
  (39 shorter events, 0.3 us)
Async XLA Ops:
  6.5 50.0 %all-gather.5.cloned.1.call-start = ((), (), s32[]{:S(2)}) async-start(), calls=%async_computation.3 | async-start | bytes 1990656 | tf_op jit(solution)/shard_map/all_gather | solution.py:330
  7.6 2.1 collective-permute-start.7
  9.4 2.1 copy-start.12
  9.4 2.3 copy-start
  10.6 17.6 %copy-start.9 = (s32[512,26]{0,1:T(8,128)S(1)}, s32[512,26]{0,1:T(8,128)}, u32[]{:S(2)}) copy-start(s32[512,26]{0,1:T(8,128)} %param.25) | copy-start | bytes 159748
  10.6 123.7 %all-gather.3.cloned.1.call-start = ((), (), s32[]{:S(2)}) async-start(), calls=%async_computation.2 | async-start | bytes 3981312 | tf_op jit(solution)/shard_map/all_gather | solution.py:330
  12.6 15.8 %collective-permute-start.1 = (bf16[64,512]{1,0:T(8,128)(2,1)S(1)}, bf16[64,512]{1,0:T(8,128)(2,1)S(1)}, u32[]{:S(2)}, u32[]{:S(2)}) collective-permute-start(bf16[64,512]{1,0:T(8,128)(2,1)S(1)} %get-tuple-element.25), channel_id=1, source_target_pairs={{1,8},{2,9},{3,10},{4,11},{5,12},{6,13},{7,14},{9,0},{10,1},{11,2}... | collective-permute-start | bytes 196616 | tf_op jit(solution)/shard_map/ppermute | solution.py:266
  17.1 11.4 %collective-permute-start.2 = (bf16[64,512]{1,0:T(8,128)(2,1)S(1)}, bf16[64,512]{1,0:T(8,128)(2,1)S(1)}, u32[]{:S(2)}, u32[]{:S(2)}) collective-permute-start(bf16[64,512]{1,0:T(8,128)(2,1)S(1)} %get-tuple-element.23), channel_id=1, source_target_pairs={{0,8},{1,9},{2,10},{3,11},{4,12},{5,13},{6,14},{7,15},{8,0},{9,1},... | collective-permute-start | bytes 196616 | tf_op jit(solution)/shard_map/ppermute | solution.py:266
  17.2 14.2 %collective-permute-start.3 = (bf16[64,512]{1,0:T(8,128)(2,1)S(1)}, bf16[64,512]{1,0:T(8,128)(2,1)S(1)}, u32[]{:S(2)}, u32[]{:S(2)}) collective-permute-start(bf16[64,512]{1,0:T(8,128)(2,1)S(1)} %get-tuple-element.26), channel_id=1, source_target_pairs={{0,9},{1,10},{2,11},{3,12},{4,13},{5,14},{6,15},{8,1},{9,2},{10,3}... | collective-permute-start | bytes 196616 | tf_op jit(solution)/shard_map/ppermute | solution.py:266
  22.6 10.1 %collective-permute-start.4 = (bf16[64,512]{1,0:T(8,128)(2,1)S(1)}, bf16[64,512]{1,0:T(8,128)(2,1)S(1)}, u32[]{:S(2)}, u32[]{:S(2)}) collective-permute-start(bf16[64,512]{1,0:T(8,128)(2,1)S(1)} %get-tuple-element.24), channel_id=1, source_target_pairs={{1,0},{2,1},{3,2},{4,3},{5,4},{6,5},{7,6},{9,8},{10,9},{11,10},{12... | collective-permute-start | bytes 196616 | tf_op jit(solution)/shard_map/ppermute | solution.py:277
  24.5 8.1 %collective-permute-start.5 = (bf16[64,512]{1,0:T(8,128)(2,1)S(1)}, bf16[64,512]{1,0:T(8,128)(2,1)S(1)}, u32[]{:S(2)}, u32[]{:S(2)}) collective-permute-start(bf16[64,512]{1,0:T(8,128)(2,1)S(1)} %get-tuple-element.22), channel_id=1, source_target_pairs={{0,1},{1,2},{2,3},{3,4},{4,5},{5,6},{6,7},{8,9},{9,10},{10,11},{11... | collective-permute-start | bytes 196616 | tf_op jit(solution)/shard_map/ppermute | solution.py:277
  28.4 28.5 %collective-permute-start = (s32[512,26]{1,0:T(8,128)S(1)}, s32[512,26]{1,0:T(8,128)S(1)}, u32[]{:S(2)}, u32[]{:S(2)}) collective-permute-start(s32[512,26]{1,0:T(8,128)S(1)} %copy.28), channel_id=1, source_target_pairs={{0,1},{1,0},{2,3},{3,2},{4,5},{5,4},{6,7},{7,6},{8,9},{9,8},{10,11... | collective-permute-start | bytes 159752 | tf_op jit(solution)/shard_map/ppermute | solution.py:358
  33.6 24.5 %collective-permute-start.6 = (bf16[1024,256]{1,0:T(8,128)(2,1)S(1)}, bf16[1024,256]{1,0:T(8,128)(2,1)}, u32[]{:S(2)}, u32[]{:S(2)}) collective-permute-start(bf16[1024,256]{1,0:T(8,128)(2,1)S(1)} %get-tuple-element.21), channel_id=1, source_target_pairs={{0,1},{1,0},{2,3},{3,2},{4,5},{5,4},{6,7},{7,6},{8,9},{9,8},{10,11... | collective-permute-start | bytes 1572872 | tf_op jit(solution)/shard_map/ppermute | solution.py:357
  56.6 39.5 %collective-permute-start.9 = (bf16[8,864,128]{2,1,0:T(8,128)(2,1)}, bf16[8,864,128]{2,1,0:T(8,128)(2,1)S(1)}, u32[]{:S(2)}, u32[]{:S(2)}) collective-permute-start(bf16[8,864,128]{2,1,0:T(8,128)(2,1)} %bitcast.31), channel_id=1, source_target_pairs={{0,16},{16,0},{1,17},{17,1},{2,18},{18,2},{3,19},{19,3},{4,20},{20... | collective-permute-start | bytes 5308424 | tf_op jit(solution)/shard_map/ppermute | solution.py:340
  96.1 1.2 copy-start.8
  110.3 38.0 %collective-permute-start.10 = (f32[512,256]{1,0:T(8,128)}, f32[512,256]{1,0:T(8,128)S(1)}, u32[]{:S(2)}, u32[]{:S(2)}) collective-permute-start(f32[512,256]{1,0:T(8,128)} %get-tuple-element.16), channel_id=1, source_target_pairs={{0,1},{1,0},{2,3},{3,2},{4,5},{5,4},{6,7},{7,6},{8,9},{9,8},{10,11... | collective-permute-start | bytes 1572872 | tf_op jit(solution)/shard_map/ppermute | solution.py:388
  134.3 13.6 %copy-start.10 = (s32[512]{0:T(512)S(1)}, s32[512]{0:T(512)}, u32[]{:S(2)}) copy-start(s32[512]{0:T(512)} %param.26) | copy-start | bytes 6148
  134.3 15.3 %copy-start.1 = (bf16[512,512]{1,0:T(8,128)(2,1)S(1)}, bf16[512,512]{1,0:T(8,128)(2,1)}, u32[]{:S(2)}) copy-start(bf16[512,512]{1,0:T(8,128)(2,1)} %weight_ref.1) | copy-start | bytes 1572868
  134.3 15.3 %copy-start.2 = (f32[512,256]{1,0:T(8,128)S(1)}, f32[512,256]{1,0:T(8,128)}, u32[]{:S(2)}) copy-start(f32[512,256]{1,0:T(8,128)} %get-tuple-element.15.own_late_ref) | copy-start | bytes 1572868
  134.3 15.3 %copy-start.4 = (f32[512]{0:T(512)S(1)}, f32[512]{0:T(512)}, u32[]{:S(2)}) copy-start(f32[512]{0:T(512)} %param.17) | copy-start | bytes 6148
  147.3 2.4 collective-permute-start.8
  149.6 1.0 copy-start.3
  153.0 30.6 %all-to-all-start = ((bf16[16,64,512]{2,1,0:T(8,128)(2,1)}), bf16[16,64,512]{2,1,0:T(8,128)(2,1)S(1)}, u32[]{:S(2)}, u32[]{:S(2)}) async-start(bf16[16,64,512]{2,1,0:T(8,128)(2,1)} %bitcast.8), calls=%async_computation | async-start | bytes 2097152 | tf_op jit(solution)/shard_map/all_to_all | solution.py:408
  158.8 3.5 %copy-start.11 = (s32[512]{0:T(512)S(1)}, s32[512]{0:T(512)}, u32[]{:S(2)}) copy-start(s32[512]{0:T(512)} %param.27) | copy-start | bytes 6148
  160.3 23.4 %copy-start.5 = (bf16[512,512]{1,0:T(8,128)(2,1)S(1)}, bf16[512,512]{1,0:T(8,128)(2,1)}, u32[]{:S(2)}) copy-start(bf16[512,512]{1,0:T(8,128)(2,1)} %proj_ref.1) | copy-start | bytes 1572868
  160.3 23.4 %copy-start.6 = (f32[512]{0:T(512)S(1)}, f32[512]{0:T(512)}, u32[]{:S(2)}) copy-start(f32[512]{0:T(512)} %param.18) | copy-start | bytes 6148
  160.3 23.3 %copy-start.7 = (f32[512]{0:T(512)S(1)}, f32[512]{0:T(512)}, u32[]{:S(2)}) copy-start(f32[512]{0:T(512)} %param.21) | copy-start | bytes 6148
  209.6 29.8 %all-to-all-start.1 = ((bf16[16,64,512]{2,1,0:T(8,128)(2,1)}), bf16[16,64,512]{2,1,0:T(8,128)(2,1)S(1)}, u32[]{:S(2)}, u32[]{:S(2)}) async-start(bf16[16,64,512]{2,1,0:T(8,128)(2,1)} %bitcast.15), calls=%async_computation.1 | async-start | bytes 2097152 | tf_op jit(solution)/shard_map/all_to_all | solution.py:439
Sparse Core Ops, SparseCore 0:
  10.7 45.8 all-gather.4
  58.1 76.1 all-gather.2

commit v3 on v1

--- a/solution.py
+++ b/solution.py
@@ -58,45 +58,89 @@
     faces_ref[...] = dot(one_hot(rows_ref[...] == row_ids), ordered).astype(BF16)
 
 
-def gather_kernel(own_rows, other_rows, own_table, other_table, own_out, other_out):
-    tap = pl.program_id(0)
+def gather_kernel(first, other_rows, own_rows, other_table, own_table, *refs):
+    out_ref = refs[-1]
+    tap = first + pl.program_id(0)
     points, lanes = own_rows.shape
     chosen = lax.broadcasted_iota(jnp.int32, (points, lanes), 1) == tap
     row_ids = lax.broadcasted_iota(jnp.int32, (1, own_table.shape[0]), 1).astype(F32)
-    for rows, table, out in ((own_rows, own_table, own_out), (other_rows, other_table, other_out)):
+    for start, rows, table in ((0, other_rows, other_table), (points, own_rows, own_table)):
         column = jnp.sum(jnp.where(chosen, rows[...], 0.0), axis=1, keepdims=True)
-        out[...] = dot(one_hot(column == row_ids), table[...]).astype(BF16)
-
-
-def conv_kernel(stacked_ref, weight_ref, out_ref):
-    product = dot(stacked_ref[...], weight_ref[...])
-
-    @pl.when(pl.program_id(0) == 0)
+        taken = dot(one_hot(column == row_ids), table[...]).astype(BF16)
+        out_ref[start : start + points] = taken
+
+
+def gather_part(first, count, tables, stacked):
+    points, lanes = tables[1].shape
+    height, half = tables[3].shape
+    whole = lambda tap: (0, 0)
+    extra = [] if stacked is None else [stacked]
+    return call(
+        functools.partial(gather_kernel, first),
+        jax.ShapeDtypeStruct((2 * points, TAPS * half), BF16),
+        60,
+        4 * count * points * height * half,
+        4 * count * points * half,
+        grid=(count,),
+        in_specs=[pl.BlockSpec((points, lanes), whole)] * 2
+        + [pl.BlockSpec((height, half), whole)] * 2
+        + [pl.BlockSpec(memory_space=pl.ANY)] * len(extra),
+        out_specs=pl.BlockSpec((2 * points, half), lambda tap: (0, first + tap)),
+        input_output_aliases={} if stacked is None else {4: 0},
+    )(*tables, *extra)
+
+
+def conv_kernel(starts_ref, stacked_ref, *refs):
+    count = len(refs) - 4
+    pieces, (other_ref, own_ref, held, sems) = refs[:count], refs[count:]
+    step = pl.program_id(0)
+    depth, points = stacked_ref.shape[1], own_ref.shape[0]
+    copies = []
+    for at, piece in enumerate(pieces):
+        start = pl.multiple_of(starts_ref[at], 32)
+        copies.append(
+            pltpu.make_async_copy(
+                piece, held.at[pl.ds(start, piece.shape[0])], sems.at[at]
+            )
+        )
+
+    @pl.when(step == 0)
     def _():
-        out_ref[...] = product
-
-    @pl.when(pl.program_id(0) > 0)
-    def _():
-        out_ref[...] += product
-
-
-def conv_part(stacked, weight):
+        for copy in copies:
+            copy.start()
+        other_ref[...] = jnp.zeros_like(other_ref)
+        own_ref[...] = jnp.zeros_like(own_ref)
+        for copy in copies:
+            copy.wait()
+
+    weight = held[pl.ds(pl.multiple_of(step * depth, 256), depth)]
+    other_ref[...] += dot(stacked_ref[:points], weight)
+    own_ref[...] += dot(stacked_ref[points:], weight)
+
+
+def conv_part(stacked, starts, pieces):
     points, depth = stacked.shape
-    width = weight.shape[1]
-    step = 3 * (width // 2)
+    width = pieces[0].shape[1]
+    steps = 3
+    step = depth // steps
     return call(
         conv_kernel,
-        jax.ShapeDtypeStruct((points, width), F32),
-        32,
+        (jax.ShapeDtypeStruct((points // 2, width), F32),) * 2,
+        60,
         2 * points * depth * width,
         2 * depth * (points + width),
-        grid=(depth // step,),
+        grid=(steps,),
         in_specs=[
+            pl.BlockSpec(memory_space=pltpu.SMEM),
             pl.BlockSpec((points, step), lambda k: (0, k)),
-            pl.BlockSpec((step, width), lambda k: (k, 0)),
+        ]
+        + [pl.BlockSpec(memory_space=pl.ANY)] * len(pieces),
+        out_specs=[pl.BlockSpec((points // 2, width), lambda k: (0, 0))] * 2,
+        scratch_shapes=[
+            pltpu.VMEM((depth, width), BF16),
+            pltpu.SemaphoreType.DMA((len(pieces),)),
         ],
-        out_specs=pl.BlockSpec((points, width), lambda k: (0, 0)),
-    )(stacked, weight)
+    )(starts, stacked, *pieces)
 
 
 def mix_kernel(own_ref, got_ref, features_ref, weight_ref, gain_ref, slot_ref, out_ref):
@@ -212,6 +256,18 @@
     return received
 
 
+def way_round(devices):
+    chips = devices // 2
+    cycle = list(range(0, chips, 2)) + list(range(chips - 1, 0, -2))
+    pairs, origins = [], [[0] * chips for _ in range(devices)]
+    for place, chip in enumerate(cycle):
+        for core, way in ((0, 1), (1, -1)):
+            pairs.append((2 * chip + core, 2 * cycle[(place + way) % chips] + core))
+            for step in range(chips):
+                origins[2 * chip + core][step] = cycle[(place - way * step) % chips]
+    return pairs, origins
+
+
 def padded_taps(neighbours):
     points = neighbours.shape[0]
     own = jnp.arange(points, dtype=jnp.int32)[:, None]
@@ -254,9 +310,6 @@
     mine = jnp.where(
         core == 0, jnp.concatenate([kept, got]), jnp.concatenate([got, kept])
     ).reshape(TAPS * unit, width)
-    same_core = [list(range(first, devices, 2)) for first in range(2)]
-    weight = lax.all_gather(mine, "blocks", axis=0, tiled=True, axis_index_groups=same_core)
-
     face_list = face_rows.reshape(-1, 1)
     ordered, faces = call(
         functools.partial(faces_kernel, unit),
@@ -268,29 +321,38 @@
         4 * points * width * width,
         8 * points * width,
     )(features, face_list)
+    round_trip = devices == 16
+    pairs, origins = way_round(devices)
+    ring = [mine]
+
+    def pass_on(*beside):
+        if not round_trip:
+            return beside
+        tied = lax.optimization_barrier((ring[-1], *beside))
+        ring[-1] = tied[0]
+        ring.append(lax.ppermute(ring[-1], "blocks", pairs))
+        return tied[1:]
+
+    (faces,) = pass_on(faces)
     received = exchange_faces(faces.reshape(8, -1, width), devices, index)
-    table = jnp.concatenate([ordered] + received, axis=0)
+    pass_on()
+    received = pass_on(*received)
+    table = jnp.concatenate([ordered, *received], axis=0)
     own_table = lax.dynamic_slice(table, (0, core * half), (table.shape[0], half))
     other_half = lax.dynamic_slice(table, (0, (1 - core) * half), (table.shape[0], half))
     other_table = lax.ppermute(other_half, "blocks", partner)
     other_neighbours = lax.ppermute(neighbours, "blocks", partner)
-    whole = lambda tap: (0, 0)
-    column = lambda tap: (0, tap)
-    own_stacked, other_stacked = call(
-        gather_kernel,
-        (jax.ShapeDtypeStruct((points, TAPS * half), BF16),) * 2,
-        40,
-        4 * TAPS * points * table.shape[0] * half,
-        4 * TAPS * points * half,
-        grid=(TAPS,),
-        in_specs=[
-            pl.BlockSpec((points, 128), whole),
-            pl.BlockSpec((points, 128), whole),
-            pl.BlockSpec((table.shape[0], half), whole),
-            pl.BlockSpec((table.shape[0], half), whole),
-        ],
-        out_specs=[pl.BlockSpec((points, half), column)] * 2,
-    )(padded_taps(neighbours), padded_taps(other_neighbours), own_table, other_table)
+    tables = (padded_taps(other_neighbours), padded_taps(neighbours), other_table, own_table)
+    stacked = None
+    for first, count in ((0, 4), (4, 8), (12, 8), (20, 7)):
+        stacked = gather_part(first, count, tables, stacked)
+        (stacked,) = pass_on(stacked)
+    if round_trip:
+        starts = jnp.array(origins, jnp.int32)[index] * mine.shape[0]
+    else:
+        groups = [list(range(first, devices, 2)) for first in range(2)]
+        ring = [lax.all_gather(mine, "blocks", axis=0, tiled=True, axis_index_groups=groups)]
+        starts = jnp.zeros((1,), jnp.int32)
 
     positions = jnp.arange(points, dtype=jnp.int32)
     target = serial_rank // points
@@ -300,9 +362,8 @@
     before = (anchor[None, :] == anchor[:, None]) & (positions[None, :] < positions[:, None])
     in_slot = anchor * capacity + jnp.sum(before.astype(jnp.int32), axis=1)
 
-    for_partner = conv_part(other_stacked, weight)
+    for_partner, own_part = conv_part(stacked, starts, ring)
     from_partner = lax.ppermute(for_partner, "blocks", partner)
-    own_part = conv_part(own_stacked, weight)
 
     outgoing = call(
         mix_kernel,

time: 240 us -> 224 us (0.933)
  waiting for transfers between devices: 110 us -> 86.1 us
  between operations: 13.8 us -> 0.42 us
  Pallas kernels: 65.3 us -> 77 us
  starting transfers between devices: 31.2 us -> 42.7 us
  local copies, waits for them, and re-layouts: 15.8 us -> 12.4 us
    all_gather x1 -> x0, waiting for transfers between devices: 62.2 us -> none  [body(): lax.all_gather(mine, 'blocks', axis=0, tiled=True, axis_index_groups=same...]
    ppermute x0 -> x7, waiting for transfers between devices: none -> 36.4 us  [pass_on(): ring.append(lax.ppermute(ring[-1], 'blocks', pairs))]
    pallas_call x3 -> x5, Pallas kernels: 34.7 us -> 46.3 us  [the longest x4 31.5 us: gather_part(): call(functools.partial(gather_kernel, first), jax.ShapeDtypeStruct((2 * p...]
    ppermute x2, starting transfers between devices: 5.56 us -> 13.8 us  [exchange_faces(): received[facing] = lax.ppermute(faces[facing], 'blocks', pairs)]
    unnamed x34 -> x47, local copies, waits for them, and re-layouts: 11.1 us -> 6.28 us
    ppermute x1, starting transfers between devices: 1.31 us -> 4.34 us  [body(): from_partner = lax.ppermute(for_partner, 'blocks', partner)]
    ppermute x2, waiting for transfers between devices: 0.92 us -> 3.41 us  [exchange_faces(): received[facing] = lax.ppermute(faces[facing], 'blocks', pairs)]
  transfers between devices with their start and end apart: 12 -> 18, of which waited for: 8 -> 11; matrix products, arithmetic and copies ran while one was open for 3% -> 5% of each run, Pallas kernels for 12% -> 14%
where the time goes in v3:
time: 224 us; the launch traced here: 223 us
  waiting for transfers between devices  86.1 us (38%)
  Pallas kernels  77 us (34%)
  starting transfers between devices  42.7 us (19%)
  local copies, waits for them, and re-layouts  12.4 us (6%)
  other arithmetic  4.44 us (2%)
    ppermute x7, waiting for transfers between devices, pass_on(): ring.append(lax.ppermute(ring[-1], 'blocks', pairs))  36.4 us
    pallas_call x4, Pallas kernels, gather_part(): call(functools.partial(gather_kernel, first), jax.ShapeDtypeStruct((2 * p...  31.5 us
    pallas_call x1, Pallas kernels, body(): call(block_kernel, jax.ShapeDtypeStruct((slots, width), BF16), 48, 20 * p...  25.9 us
    all_to_all x1, waiting for transfers between devices, body(): lax.all_to_all(back.reshape(devices, capacity, width), 'blocks', split_ax...  24.7 us
    all_to_all x1, waiting for transfers between devices, body(): lax.all_to_all(outgoing.reshape(devices, capacity, width), 'blocks', spli...  19.2 us
    pallas_call x1, Pallas kernels, conv_part(): call(conv_kernel, (jax.ShapeDtypeStruct((points // 2, width), F32),) * 2,...  14.8 us
    ppermute x2, starting transfers between devices, exchange_faces(): received[facing] = lax.ppermute(faces[facing], 'blocks', pairs)  13.8 us
    ppermute x3, starting transfers between devices, exchange_faces(): got = lax.ppermute(payload, 'blocks', pairs)  9.26 us
  transfers between devices with their start and end apart: 18, of which 11 were waited for; matrix products, arithmetic and copies ran while one was open for 5% of the time, Pallas kernels for 14%

profile of v3, /device:TPU:9, one launch (start us, length us, event | category | flops | bytes accessed | tf_op | source)
XLA Modules:
  0.0 223.0 jit_solution(15806090648839699905)
XLA Ops:
  0.0 1.0 slice.60
  1.0 0.7 collective-permute-start
  1.8 1.1 slice.59
  2.8 0.0 copy-start.10
  2.9 0.9 reshape.82.rows_ref
  3.8 0.0 copy-start.1
  3.8 1.0 copy-done.1
  4.8 0.8 shard_map.145
  5.6 0.1 maximum_select_fusion
  5.8 0.1 collective-permute-start.1
  5.9 0.1 copy.33
  6.0 1.6 collective-permute-start.9
  7.7 10.5 %collective-permute-done.1.refs_1_ = bf16[864,512]{1,0:T(8,128)(2,1)} collective-permute-done((bf16[864,512]{1,0:T(8,128)(2,1)S(1)}, bf16[864,512]{1,0:T(8,128)(2,1)}, u32[]{:S(2)}, u32[]{:S(2)}) %collective-permute-start.1) | collective-permute-done | bytes 884768 | tf_op jit(solution)/shard_map/ppermute | solution.py:333
  18.2 0.0 collective-permute-start.2
  18.2 6.4 %collective-permute-start.5 = (bf16[64,512]{1,0:T(8,128)(2,1)S(1)}, bf16[64,512]{1,0:T(8,128)(2,1)S(1)}, u32[]{:S(2)}, u32[]{:S(2)}) collective-permute-start(bf16[64,512]{1,0:T(8,128)(2,1)S(1)} %get-tuple-element.60), channel_id=1, source_target_pairs={{0,9},{1,10},{2,11},{3,12},{4,13},{5,14},{6,15},{8,1},{9,2},{10,3}... | collective-permute-start | bytes 196616 | tf_op jit(solution)/shard_map/ppermute | solution.py:244
  24.6 0.1 collective-permute-start.4
  24.7 2.8 %collective-permute-start.3 = (bf16[64,512]{1,0:T(8,128)(2,1)S(1)}, bf16[64,512]{1,0:T(8,128)(2,1)S(1)}, u32[]{:S(2)}, u32[]{:S(2)}) collective-permute-start(bf16[64,512]{1,0:T(8,128)(2,1)S(1)} %get-tuple-element.59), channel_id=1, source_target_pairs={{1,8},{2,9},{3,10},{4,11},{5,12},{6,13},{7,14},{9,0},{10,1},{11,2}... | collective-permute-start | bytes 196616 | tf_op jit(solution)/shard_map/ppermute | solution.py:244
  27.5 0.2 collective-permute-done.5
  27.7 11.9 %collective-permute-start.6 = (bf16[64,512]{1,0:T(8,128)(2,1)S(1)}, bf16[64,512]{1,0:T(8,128)(2,1)S(1)}, u32[]{:S(2)}, u32[]{:S(2)}) collective-permute-start(bf16[64,512]{1,0:T(8,128)(2,1)S(1)} %get-tuple-element.58), channel_id=1, source_target_pairs={{1,0},{2,1},{3,2},{4,3},{5,4},{6,5},{7,6},{9,8},{10,9},{11,10},{12... | collective-permute-start | bytes 196616 | tf_op jit(solution)/shard_map/ppermute | solution.py:255
  39.6 1.9 collective-permute-start.7
  41.6 3.4 %collective-permute-done.7 = bf16[64,512]{1,0:T(8,128)(2,1)S(1)} collective-permute-done((bf16[64,512]{1,0:T(8,128)(2,1)S(1)}, bf16[64,512]{1,0:T(8,128)(2,1)S(1)}, u32[]{:S(2)}, u32[]{:S(2)}) %collective-permute-start.7) | collective-permute-done | bytes 65568 | tf_op jit(solution)/shard_map/ppermute | solution.py:255
  45.1 0.9 constant_dynamic-slice_fusion
  46.0 3.8 %collective-permute-start.10 = (bf16[1024,256]{1,0:T(8,128)(2,1)S(1)}, bf16[1024,256]{1,0:T(8,128)(2,1)S(1)}, u32[]{:S(2)}, u32[]{:S(2)}) collective-permute-start(bf16[1024,256]{1,0:T(8,128)(2,1)S(1)} %get-tuple-element.55), channel_id=1, source_target_pairs={{0,1},{1,0},{2,3},{3,2},{4,5},{5,4},{6,7},{7,6},{8,9},{9,8},{10,11... | collective-permute-start | bytes 1572872 | tf_op jit(solution)/shard_map/ppermute | solution.py:343
  49.9 0.1 copy.34
  50.0 0.1 copy.35
  50.2 0.1 pad.9.clone
  50.2 0.1 fusion.9
  50.4 1.1 add_convert_fusion.1
  51.5 0.8 copy-done.8
  52.3 5.4 %shard_map.146.refs_0_ = bf16[1024,6912]{1,0:T(8,128)(2,1)} custom-call(f32[512,128]{1,0:T(8,128)} %get-tuple-element.62.other_rows, f32[512,128]{1,0:T(8,128)} %get-tuple-element.61.own_rows, bf16[1024,256]{1,0:T(8,128)(2,1)} %copy-done.8, bf16[1024,256]{1,0:T(8,128)(2,1)} %get-tuple-element.54.own_table), custom_call_target="tpu_custom_call" | custom-call | flops 2147483648 | bytes 2097152 | tf_op jit(solution)/shard_map/pallas_call | solution.py:78
  57.7 4.6 %collective-permute-done.8.refs_3_ = bf16[864,512]{1,0:T(8,128)(2,1)S(1)} collective-permute-done((bf16[864,512]{1,0:T(8,128)(2,1)}, bf16[864,512]{1,0:T(8,128)(2,1)S(1)}, u32[]{:S(2)}, u32[]{:S(2)}) %collective-permute-start.8) | collective-permute-done | bytes 884768 | tf_op jit(solution)/shard_map/ppermute | solution.py:333
  62.3 8.9 %shard_map.147.refs_0_ = bf16[1024,6912]{1,0:T(8,128)(2,1)} custom-call(f32[512,128]{1,0:T(8,128)} %get-tuple-element.62.other_rows, f32[512,128]{1,0:T(8,128)} %get-tuple-element.61.own_rows, bf16[1024,256]{1,0:T(8,128)(2,1)} %copy-done.8, bf16[1024,256]{1,0:T(8,128)(2,1)} %get-tuple-element.54.own_table, ...), custom_call_target="tpu_custom_call", output_to_operand_aliasing={{}: (4, {})} | custom-call | flops 4294967296 | bytes 4194304 | tf_op jit(solution)/shard_map/pallas_call | solution.py:78
  71.2 3.3 %collective-permute-done.11.refs_4_ = bf16[864,512]{1,0:T(8,128)(2,1)S(1)} collective-permute-done((bf16[864,512]{1,0:T(8,128)(2,1)S(1)}, bf16[864,512]{1,0:T(8,128)(2,1)S(1)}, u32[]{:S(2)}, u32[]{:S(2)}) %collective-permute-start.11) | collective-permute-done | bytes 884768 | tf_op jit(solution)/shard_map/ppermute | solution.py:333
  74.4 0.0 collective-permute-start.12
  74.4 9.0 %shard_map.148.refs_0_ = bf16[1024,6912]{1,0:T(8,128)(2,1)} custom-call(f32[512,128]{1,0:T(8,128)} %get-tuple-element.62.other_rows, f32[512,128]{1,0:T(8,128)} %get-tuple-element.61.own_rows, bf16[1024,256]{1,0:T(8,128)(2,1)} %copy-done.8, bf16[1024,256]{1,0:T(8,128)(2,1)} %get-tuple-element.54.own_table, ...), custom_call_target="tpu_custom_call", output_to_operand_aliasing={{}: (4, {})} | custom-call | flops 4294967296 | bytes 4194304 | tf_op jit(solution)/shard_map/pallas_call | solution.py:78
  83.4 3.2 %collective-permute-done.12.refs_5_ = bf16[864,512]{1,0:T(8,128)(2,1)S(1)} collective-permute-done((bf16[864,512]{1,0:T(8,128)(2,1)S(1)}, bf16[864,512]{1,0:T(8,128)(2,1)S(1)}, u32[]{:S(2)}, u32[]{:S(2)}) %collective-permute-start.12) | collective-permute-done | bytes 884768 | tf_op jit(solution)/shard_map/ppermute | solution.py:333
  86.6 8.2 %shard_map.149.stacked_ref = bf16[1024,6912]{1,0:T(8,128)(2,1)} custom-call(f32[512,128]{1,0:T(8,128)} %get-tuple-element.62.other_rows, f32[512,128]{1,0:T(8,128)} %get-tuple-element.61.own_rows, bf16[1024,256]{1,0:T(8,128)(2,1)} %copy-done.8, bf16[1024,256]{1,0:T(8,128)(2,1)} %get-tuple-element.54.own_table, ...), custom_call_target="tpu_custom_call", output_to_operand_aliasing={{}: (4, {})} | custom-call | flops 3758096384 | bytes 3670016 | tf_op jit(solution)/shard_map/pallas_call | solution.py:78
  94.9 4.0 %collective-permute-done.13.refs_6_ = bf16[864,512]{1,0:T(8,128)(2,1)S(1)} collective-permute-done((bf16[864,512]{1,0:T(8,128)(2,1)S(1)}, bf16[864,512]{1,0:T(8,128)(2,1)S(1)}, u32[]{:S(2)}, u32[]{:S(2)}) %collective-permute-start.13) | collective-permute-done | bytes 884768 | tf_op jit(solution)/shard_map/ppermute | solution.py:333
  98.8 0.0 collective-permute-start.14
  98.8 1.2 fusion.6.starts_ref
  100.1 10.9 %collective-permute-done.14.refs_7_ = bf16[864,512]{1,0:T(8,128)(2,1)S(1)} collective-permute-done((bf16[864,512]{1,0:T(8,128)(2,1)S(1)}, bf16[864,512]{1,0:T(8,128)(2,1)S(1)}, u32[]{:S(2)}, u32[]{:S(2)}) %collective-permute-start.14) | collective-permute-done | bytes 884768 | tf_op jit(solution)/shard_map/ppermute | solution.py:333
  111.0 0.9 copy-done.17
  112.0 14.8 %shard_map.150 = (f32[512,512]{1,0:T(8,128)}, f32[512,512]{1,0:T(8,128)}) custom-call(s32[8]{0:T(128)} %fusion.6.starts_ref, bf16[1024,6912]{1,0:T(8,128)(2,1)} %shard_map.149.stacked_ref, bf16[864,512]{1,0:T(8,128)(2,1)} %bitcast.29, bf16[864,512]{1,0:T(8,128)(2,1)} %collective-permute-done.1.refs_1_, bf16[864,512]{1,0:T(8,128)(2,1)} %collective-permute-done.2.refs_2_, ...), custom_call_target="tpu_custom_call" | custom-call | flops 7247757312 | bytes 21233664 | tf_op jit(solution)/shard_map/pallas_call | solution.py:126
  126.8 4.3 %collective-permute-start.15 = (f32[512,512]{1,0:T(8,128)}, f32[512,512]{1,0:T(8,128)S(1)}, u32[]{:S(2)}, u32[]{:S(2)}) collective-permute-start(f32[512,512]{1,0:T(8,128)} %get-tuple-element.50), channel_id=1, source_target_pairs={{0,1},{1,0},{2,3},{3,2},{4,5},{5,4},{6,7},{7,6},{8,9},{9,8},{10,11... | collective-permute-start | bytes 3145736 | tf_op jit(solution)/shard_map/ppermute | solution.py:366
  131.1 0.3 convert_reduce_fusion.1
  131.5 2.1 collective-permute-done.15.got_ref
  133.6 1.2 copy-done
  134.9 2.3 %shard_map.151 = bf16[1024,512]{1,0:T(8,128)(2,1)} custom-call(f32[512,512]{1,0:T(8,128)S(1)} %copy-done, f32[512,512]{1,0:T(8,128)S(1)} %collective-permute-done.15.got_ref, bf16[512,512]{1,0:T(8,128)(2,1)S(1)} %copy-done.2, bf16[512,512]{1,0:T(8,128)(2,1)S(1)} %copy-done.3, f32[1,512]{1,0:T(1,128)S(1)} %bitcast.23, s32[1,512]{1,0:T(1,128)S(1)} %bitcast.19), custom_call_target="tpu_custom_call" | custom-call | flops 805306368 | bytes 2097152 | tf_op jit(solution)/shard_map/pallas_call | solution.py:368
  137.2 3.7 %all-to-all-start = ((bf16[16,64,512]{2,1,0:T(8,128)(2,1)}), bf16[16,64,512]{2,1,0:T(8,128)(2,1)S(1)}, u32[]{:S(2)}, u32[]{:S(2)}) async-start(bf16[16,64,512]{2,1,0:T(8,128)(2,1)} %bitcast.5), calls=%async_computation | async-start | bytes 2097152 | tf_op jit(solution)/shard_map/all_to_all | solution.py:382
  140.9 0.0 copy-start.12
  141.0 1.5 fusion.7
  142.4 0.0 copy-start.5
  142.4 0.0 copy-start.6
  142.5 1.0 copy.40
  143.5 1.0 copy.41
  144.5 0.2 convert_reduce_fusion
  144.8 0.1 copy.38.slot_col_ref
  144.9 1.3 maximum_bitcast_fusion.qv_ref
  146.2 19.2 %all-to-all-done = bf16[16,64,512]{2,1,0:T(8,128)(2,1)S(1)} async-done(((bf16[16,64,512]{2,1,0:T(8,128)(2,1)}), bf16[16,64,512]{2,1,0:T(8,128)(2,1)S(1)}, u32[]{:S(2)}, u32[]{:S(2)}) %all-to-all-start) | async-done | bytes 1048608 | tf_op jit(solution)/shard_map/all_to_all | solution.py:382
  165.4 25.9 %shard_map.152 = bf16[1024,512]{1,0:T(8,128)(2,1)} custom-call(bf16[1024,512]{1,0:T(8,128)(2,1)S(1)} %bitcast.17, s32[512,1]{1,0:T(8,128)S(1)} %copy.38.slot_col_ref, s32[1,512]{1,0:T(1,128)S(1)} %bitcast.22, f32[1,512]{1,0:T(1,128)S(1)} %bitcast.24, bf16[1024,512]{1,0:T(8,128)(2,1)S(1)} %maximum_bitcast_fusion.qv_ref, ...), custom_call_target="tpu_custom_call" | custom-call | flops 2684354560 | bytes 4194304 | tf_op jit(solution)/shard_map/pallas_call | solution.py:388
  191.4 5.2 %all-to-all-start.1 = ((bf16[16,64,512]{2,1,0:T(8,128)(2,1)}), bf16[16,64,512]{2,1,0:T(8,128)(2,1)S(1)}, u32[]{:S(2)}, u32[]{:S(2)}) async-start(bf16[16,64,512]{2,1,0:T(8,128)(2,1)} %bitcast.12), calls=%async_computation.1 | async-start | bytes 2097152 | tf_op jit(solution)/shard_map/all_to_all | solution.py:413
  196.6 0.1 copy.39.slot_ref
  196.8 24.7 %all-to-all-done.1 = bf16[16,64,512]{2,1,0:T(8,128)(2,1)S(1)} async-done(((bf16[16,64,512]{2,1,0:T(8,128)(2,1)}), bf16[16,64,512]{2,1,0:T(8,128)(2,1)S(1)}, u32[]{:S(2)}, u32[]{:S(2)}) %all-to-all-start.1) | async-done | bytes 1048608 | tf_op jit(solution)/shard_map/all_to_all | solution.py:413
  221.5 1.5 shard_map.153
  (57 shorter events, 0.3 us)
Async XLA Ops:
  1.0 4.6 %collective-permute-start = (bf16[13,32,512]{2,1,0:T(8,128)(2,1)S(1)}, bf16[13,32,512]{2,1,0:T(8,128)(2,1)S(1)}, u32[]{:S(2)}, u32[]{:S(2)}) collective-permute-start(bf16[13,32,512]{2,1,0:T(8,128)(2,1)S(1)} %slice.60), channel_id=1, source_target_pairs={{0,1},{1,0},{2,3},{3,2},{4,5},{5,4},{6,7},{7,6},{8,9},{9,8},{10,11... | collective-permute-start | bytes 1277960 | tf_op jit(solution)/shard_map/ppermute | solution.py:309
  2.8 3.0 %copy-start.10 = (s32[512,26]{0,1:T(8,128)S(1)}, s32[512,26]{0,1:T(8,128)}, u32[]{:S(2)}) copy-start(s32[512,26]{0,1:T(8,128)} %param.26) | copy-start | bytes 159748
  3.8 1.0 copy-start.1
  5.8 40.2 %copy-start.9 = (bf16[27,32,512]{2,1,0:T(8,128)(2,1)}, bf16[27,32,512]{2,1,0:T(8,128)(2,1)S(1)}, u32[]{:S(2)}) copy-start(bf16[27,32,512]{2,1,0:T(8,128)(2,1)S(1)} %maximum_select_fusion) | copy-start | bytes 2654212
  5.8 12.3 %collective-permute-start.1 = (bf16[864,512]{1,0:T(8,128)(2,1)S(1)}, bf16[864,512]{1,0:T(8,128)(2,1)}, u32[]{:S(2)}, u32[]{:S(2)}) collective-permute-start(bf16[864,512]{1,0:T(8,128)(2,1)S(1)} %bitcast.28), channel_id=1, source_target_pairs={{0,4},{1,3},{4,8},{5,1},{8,12},{9,5},{12,14},{13,9},{14,10},{15,13... | collective-permute-start | bytes 2654216 | tf_op jit(solution)/shard_map/ppermute | solution.py:333
  6.0 44.2 %collective-permute-start.9 = (s32[512,26]{1,0:T(8,128)S(1)}, s32[512,26]{1,0:T(8,128)S(1)}, u32[]{:S(2)}, u32[]{:S(2)}) collective-permute-start(s32[512,26]{1,0:T(8,128)S(1)} %copy.33), channel_id=1, source_target_pairs={{0,1},{1,0},{2,3},{3,2},{4,5},{5,4},{6,7},{7,6},{8,9},{9,8},{10,11... | collective-permute-start | bytes 159752 | tf_op jit(solution)/shard_map/ppermute | solution.py:344
  18.2 26.9 %collective-permute-start.2 = (bf16[864,512]{1,0:T(8,128)(2,1)}, bf16[864,512]{1,0:T(8,128)(2,1)}, u32[]{:S(2)}, u32[]{:S(2)}) collective-permute-start(bf16[864,512]{1,0:T(8,128)(2,1)} %collective-permute-done.1.refs_1_), channel_id=1, source_target_pairs={{0,4},{1,3},{4,8},{5,1},{8,12},{9,5},{12,14},{13,9},{14,10},{15,13... | collective-permute-start | bytes 2654216 | tf_op jit(solution)/shard_map/ppermute | solution.py:333
  18.2 9.5 %collective-permute-start.5 = (bf16[64,512]{1,0:T(8,128)(2,1)S(1)}, bf16[64,512]{1,0:T(8,128)(2,1)S(1)}, u32[]{:S(2)}, u32[]{:S(2)}) collective-permute-start(bf16[64,512]{1,0:T(8,128)(2,1)S(1)} %get-tuple-element.60), channel_id=1, source_target_pairs={{0,9},{1,10},{2,11},{3,12},{4,13},{5,14},{6,15},{8,1},{9,2},{10,3}... | collective-permute-start | bytes 196616 | tf_op jit(solution)/shard_map/ppermute | solution.py:244
  24.6 15.0 %collective-permute-start.4 = (bf16[64,512]{1,0:T(8,128)(2,1)S(1)}, bf16[64,512]{1,0:T(8,128)(2,1)S(1)}, u32[]{:S(2)}, u32[]{:S(2)}) collective-permute-start(bf16[64,512]{1,0:T(8,128)(2,1)S(1)} %get-tuple-element.57), channel_id=1, source_target_pairs={{0,8},{1,9},{2,10},{3,11},{4,12},{5,13},{6,14},{7,15},{8,0},{9,1},... | collective-permute-start | bytes 196616 | tf_op jit(solution)/shard_map/ppermute | solution.py:244
  24.7 16.8 %collective-permute-start.3 = (bf16[64,512]{1,0:T(8,128)(2,1)S(1)}, bf16[64,512]{1,0:T(8,128)(2,1)S(1)}, u32[]{:S(2)}, u32[]{:S(2)}) collective-permute-start(bf16[64,512]{1,0:T(8,128)(2,1)S(1)} %get-tuple-element.59), channel_id=1, source_target_pairs={{1,8},{2,9},{3,10},{4,11},{5,12},{6,13},{7,14},{9,0},{10,1},{11,2}... | collective-permute-start | bytes 196616 | tf_op jit(solution)/shard_map/ppermute | solution.py:244
  27.7 13.9 %collective-permute-start.6 = (bf16[64,512]{1,0:T(8,128)(2,1)S(1)}, bf16[64,512]{1,0:T(8,128)(2,1)S(1)}, u32[]{:S(2)}, u32[]{:S(2)}) collective-permute-start(bf16[64,512]{1,0:T(8,128)(2,1)S(1)} %get-tuple-element.58), channel_id=1, source_target_pairs={{1,0},{2,1},{3,2},{4,3},{5,4},{6,5},{7,6},{9,8},{10,9},{11,10},{12... | collective-permute-start | bytes 196616 | tf_op jit(solution)/shard_map/ppermute | solution.py:255
  39.6 5.4 %collective-permute-start.7 = (bf16[64,512]{1,0:T(8,128)(2,1)S(1)}, bf16[64,512]{1,0:T(8,128)(2,1)S(1)}, u32[]{:S(2)}, u32[]{:S(2)}) collective-permute-start(bf16[64,512]{1,0:T(8,128)(2,1)S(1)} %get-tuple-element.56), channel_id=1, source_target_pairs={{0,1},{1,2},{2,3},{3,4},{4,5},{5,6},{6,7},{8,9},{9,10},{10,11},{11... | collective-permute-start | bytes 196616 | tf_op jit(solution)/shard_map/ppermute | solution.py:255
  46.0 5.5 %collective-permute-start.10 = (bf16[1024,256]{1,0:T(8,128)(2,1)S(1)}, bf16[1024,256]{1,0:T(8,128)(2,1)S(1)}, u32[]{:S(2)}, u32[]{:S(2)}) collective-permute-start(bf16[1024,256]{1,0:T(8,128)(2,1)S(1)} %get-tuple-element.55), channel_id=1, source_target_pairs={{0,1},{1,0},{2,3},{3,2},{4,5},{5,4},{6,7},{7,6},{8,9},{9,8},{10,11... | collective-permute-start | bytes 1572872 | tf_op jit(solution)/shard_map/ppermute | solution.py:343
  49.9 12.4 %collective-permute-start.8 = (bf16[864,512]{1,0:T(8,128)(2,1)}, bf16[864,512]{1,0:T(8,128)(2,1)S(1)}, u32[]{:S(2)}, u32[]{:S(2)}) collective-permute-start(bf16[864,512]{1,0:T(8,128)(2,1)} %collective-permute-done.2.refs_2_), channel_id=1, source_target_pairs={{0,4},{1,3},{4,8},{5,1},{8,12},{9,5},{12,14},{13,9},{14,10},{15,13... | collective-permute-start | bytes 2654216 | tf_op jit(solution)/shard_map/ppermute | solution.py:333
  51.5 0.8 copy-start.8
  62.3 8.9 %copy-start.13 = (bf16[864,512]{1,0:T(8,128)(2,1)}, bf16[864,512]{1,0:T(8,128)(2,1)S(1)}, u32[]{:S(2)}) copy-start(bf16[864,512]{1,0:T(8,128)(2,1)S(1)} %collective-permute-done.8.refs_3_) | copy-start | bytes 2654212
  62.3 12.2 %collective-permute-start.11 = (bf16[864,512]{1,0:T(8,128)(2,1)S(1)}, bf16[864,512]{1,0:T(8,128)(2,1)S(1)}, u32[]{:S(2)}, u32[]{:S(2)}) collective-permute-start(bf16[864,512]{1,0:T(8,128)(2,1)S(1)} %collective-permute-done.8.refs_3_), channel_id=1, source_target_pairs={{0,4},{1,3},{4,8},{5,1},{8,12},{9,5},{12,14},{13,9},{14,10},{15,13... | collective-permute-start | bytes 2654216 | tf_op jit(solution)/shard_map/ppermute | solution.py:333
  74.4 9.0 %copy-start.14 = (bf16[864,512]{1,0:T(8,128)(2,1)}, bf16[864,512]{1,0:T(8,128)(2,1)S(1)}, u32[]{:S(2)}) copy-start(bf16[864,512]{1,0:T(8,128)(2,1)S(1)} %collective-permute-done.11.refs_4_) | copy-start | bytes 2654212
  74.4 12.2 %collective-permute-start.12 = (bf16[864,512]{1,0:T(8,128)(2,1)S(1)}, bf16[864,512]{1,0:T(8,128)(2,1)S(1)}, u32[]{:S(2)}, u32[]{:S(2)}) collective-permute-start(bf16[864,512]{1,0:T(8,128)(2,1)S(1)} %collective-permute-done.11.refs_4_), channel_id=1, source_target_pairs={{0,4},{1,3},{4,8},{5,1},{8,12},{9,5},{12,14},{13,9},{14,10},{15,13... | collective-permute-start | bytes 2654216 | tf_op jit(solution)/shard_map/ppermute | solution.py:333
  86.6 8.2 %copy-start.15 = (bf16[864,512]{1,0:T(8,128)(2,1)}, bf16[864,512]{1,0:T(8,128)(2,1)S(1)}, u32[]{:S(2)}) copy-start(bf16[864,512]{1,0:T(8,128)(2,1)S(1)} %collective-permute-done.12.refs_5_) | copy-start | bytes 2654212
  86.6 12.2 %collective-permute-start.13 = (bf16[864,512]{1,0:T(8,128)(2,1)S(1)}, bf16[864,512]{1,0:T(8,128)(2,1)S(1)}, u32[]{:S(2)}, u32[]{:S(2)}) collective-permute-start(bf16[864,512]{1,0:T(8,128)(2,1)S(1)} %collective-permute-done.12.refs_5_), channel_id=1, source_target_pairs={{0,4},{1,3},{4,8},{5,1},{8,12},{9,5},{12,14},{13,9},{14,10},{15,13... | collective-permute-start | bytes 2654216 | tf_op jit(solution)/shard_map/ppermute | solution.py:333
  98.8 12.2 %copy-start.16 = (bf16[864,512]{1,0:T(8,128)(2,1)}, bf16[864,512]{1,0:T(8,128)(2,1)S(1)}, u32[]{:S(2)}) copy-start(bf16[864,512]{1,0:T(8,128)(2,1)S(1)} %collective-permute-done.13.refs_6_) | copy-start | bytes 2654212
  98.8 12.2 %collective-permute-start.14 = (bf16[864,512]{1,0:T(8,128)(2,1)S(1)}, bf16[864,512]{1,0:T(8,128)(2,1)S(1)}, u32[]{:S(2)}, u32[]{:S(2)}) collective-permute-start(bf16[864,512]{1,0:T(8,128)(2,1)S(1)} %collective-permute-done.13.refs_6_), channel_id=1, source_target_pairs={{0,4},{1,3},{4,8},{5,1},{8,12},{9,5},{12,14},{13,9},{14,10},{15,13... | collective-permute-start | bytes 2654216 | tf_op jit(solution)/shard_map/ppermute | solution.py:333
  100.1 31.1 %copy-start.11 = (s32[512]{0:T(512)S(1)}, s32[512]{0:T(512)}, u32[]{:S(2)}) copy-start(s32[512]{0:T(512)} %param.27) | copy-start | bytes 6148
  100.1 33.6 %copy-start.2 = (bf16[512,512]{1,0:T(8,128)(2,1)S(1)}, bf16[512,512]{1,0:T(8,128)(2,1)}, u32[]{:S(2)}) copy-start(bf16[512,512]{1,0:T(8,128)(2,1)} %features_ref.3) | copy-start | bytes 1572868
  100.1 33.6 %copy-start.3 = (bf16[512,512]{1,0:T(8,128)(2,1)S(1)}, bf16[512,512]{1,0:T(8,128)(2,1)}, u32[]{:S(2)}) copy-start(bf16[512,512]{1,0:T(8,128)(2,1)} %weight_ref.1) | copy-start | bytes 1572868
  100.1 33.6 %copy-start.4 = (f32[512]{0:T(512)S(1)}, f32[512]{0:T(512)}, u32[]{:S(2)}) copy-start(f32[512]{0:T(512)} %param.18) | copy-start | bytes 6148
  111.0 0.9 copy-start.17
  126.8 6.8 %collective-permute-start.15 = (f32[512,512]{1,0:T(8,128)}, f32[512,512]{1,0:T(8,128)S(1)}, u32[]{:S(2)}, u32[]{:S(2)}) collective-permute-start(f32[512,512]{1,0:T(8,128)} %get-tuple-element.50), channel_id=1, source_target_pairs={{0,1},{1,0},{2,3},{3,2},{4,5},{5,4},{6,7},{7,6},{8,9},{9,8},{10,11... | collective-permute-start | bytes 3145736 | tf_op jit(solution)/shard_map/ppermute | solution.py:366
  133.6 1.2 copy-start
  137.2 28.2 %all-to-all-start = ((bf16[16,64,512]{2,1,0:T(8,128)(2,1)}), bf16[16,64,512]{2,1,0:T(8,128)(2,1)S(1)}, u32[]{:S(2)}, u32[]{:S(2)}) async-start(bf16[16,64,512]{2,1,0:T(8,128)(2,1)} %bitcast.5), calls=%async_computation | async-start | bytes 2097152 | tf_op jit(solution)/shard_map/all_to_all | solution.py:382
  140.9 3.5 %copy-start.12 = (s32[512]{0:T(512)S(1)}, s32[512]{0:T(512)}, u32[]{:S(2)}) copy-start(s32[512]{0:T(512)} %param.28) | copy-start | bytes 6148
  142.4 23.0 %copy-start.5 = (bf16[512,512]{1,0:T(8,128)(2,1)S(1)}, bf16[512,512]{1,0:T(8,128)(2,1)}, u32[]{:S(2)}) copy-start(bf16[512,512]{1,0:T(8,128)(2,1)} %proj_ref.1) | copy-start | bytes 1572868
  142.4 23.0 %copy-start.6 = (f32[512]{0:T(512)S(1)}, f32[512]{0:T(512)}, u32[]{:S(2)}) copy-start(f32[512]{0:T(512)} %param.19) | copy-start | bytes 6148
  142.5 23.0 %copy-start.7 = (f32[512]{0:T(512)S(1)}, f32[512]{0:T(512)}, u32[]{:S(2)}) copy-start(f32[512]{0:T(512)} %param.22) | copy-start | bytes 6148
  191.4 30.1 %all-to-all-start.1 = ((bf16[16,64,512]{2,1,0:T(8,128)(2,1)}), bf16[16,64,512]{2,1,0:T(8,128)(2,1)S(1)}, u32[]{:S(2)}, u32[]{:S(2)}) async-start(bf16[16,64,512]{2,1,0:T(8,128)(2,1)} %bitcast.12), calls=%async_computation.1 | async-start | bytes 2097152 | tf_op jit(solution)/shard_map/all_to_all | solution.py:413

commit v4 on v3

--- a/solution.py
+++ b/solution.py
@@ -90,57 +90,73 @@
     )(*tables, *extra)
 
 
-def conv_kernel(starts_ref, stacked_ref, *refs):
-    count = len(refs) - 4
-    pieces, (other_ref, own_ref, held, sems) = refs[:count], refs[count:]
-    step = pl.program_id(0)
-    depth, points = stacked_ref.shape[1], own_ref.shape[0]
-    copies = []
-    for at, piece in enumerate(pieces):
-        start = pl.multiple_of(starts_ref[at], 32)
-        copies.append(
-            pltpu.make_async_copy(
-                piece, held.at[pl.ds(start, piece.shape[0])], sems.at[at]
+def conv_kernel(slots, first, places_ref, stacked_ref, *refs):
+    pieces = refs[: sum(slots)]
+    other_ref, own_ref, lhs, held, sems = refs[-5:]
+    points = own_ref.shape[0]
+    length = held.shape[1]
+    copies, taken = [], 0
+    for at, count in enumerate(slots):
+        column = pl.multiple_of(places_ref[2 * at], 128)
+        row = pl.multiple_of(places_ref[2 * at + 1], 16)
+        copy = pltpu.make_async_copy(
+            stacked_ref.at[:, pl.ds(column, length)], lhs.at[at], sems.at[at, 0]
+        )
+        copy.start()
+        copies.append([copy])
+        short = count * pieces[taken].shape[0]
+        edge = length - short
+        if edge:
+            held[at, :edge] = jnp.zeros((edge, held.shape[2]), BF16)
+            held[at, length - edge :] = jnp.zeros((edge, held.shape[2]), BF16)
+        for part in range(count):
+            piece = pieces[taken]
+            size = piece.shape[0]
+            copy = pltpu.make_async_copy(
+                piece, held.at[at, pl.ds(row + part * size, size)], sems.at[at, 1 + part]
             )
-        )
-
-    @pl.when(step == 0)
-    def _():
-        for copy in copies:
             copy.start()
-        other_ref[...] = jnp.zeros_like(other_ref)
-        own_ref[...] = jnp.zeros_like(own_ref)
-        for copy in copies:
+            copies[-1].append(copy)
+            taken += 1
+    for at in range(len(slots)):
+        for copy in copies[at]:
             copy.wait()
-
-    weight = held[pl.ds(pl.multiple_of(step * depth, 256), depth)]
-    other_ref[...] += dot(stacked_ref[:points], weight)
-    own_ref[...] += dot(stacked_ref[points:], weight)
-
-
-def conv_part(stacked, starts, pieces):
+        for half, ref in enumerate((other_ref, own_ref)):
+            product = dot(lhs[at, half * points : (half + 1) * points], held[at])
+            if at > 0:
+                ref[...] += product
+            elif first:
+                ref[...] = product
+            else:
+                ref[...] = refs[half - 7][...] + product
+
+
+def conv_part(stacked, places, pieces, before, length):
     points, depth = stacked.shape
-    width = pieces[0].shape[1]
-    steps = 3
-    step = depth // steps
+    width = pieces[0][0].shape[1]
+    slots = [len(parts) for parts in pieces]
+    flat = [piece for parts in pieces for piece in parts]
     return call(
-        conv_kernel,
+        functools.partial(conv_kernel, slots, before is None),
         (jax.ShapeDtypeStruct((points // 2, width), F32),) * 2,
-        60,
-        2 * points * depth * width,
-        2 * depth * (points + width),
-        grid=(steps,),
+        40,
+        2 * points * length * width * len(slots),
+        2 * length * (points + width) * len(slots),
         in_specs=[
             pl.BlockSpec(memory_space=pltpu.SMEM),
-            pl.BlockSpec((points, step), lambda k: (0, k)),
+            pl.BlockSpec(memory_space=pl.ANY),
         ]
-        + [pl.BlockSpec(memory_space=pl.ANY)] * len(pieces),
-        out_specs=[pl.BlockSpec((points // 2, width), lambda k: (0, 0))] * 2,
+        + [pl.BlockSpec(memory_space=pl.ANY)] * len(flat)
+        + ([] if before is None else [pl.BlockSpec()] * 2),
+        input_output_aliases=(
+            {} if before is None else {2 + len(flat): 0, 3 + len(flat): 1}
+        ),
         scratch_shapes=[
-            pltpu.VMEM((depth, width), BF16),
-            pltpu.SemaphoreType.DMA((len(pieces),)),
+            pltpu.VMEM((len(slots), points, length), BF16),
+            pltpu.VMEM((len(slots), length, width), BF16),
+            pltpu.SemaphoreType.DMA((len(slots), 3)),
         ],
-    )(starts, stacked, *pieces)
+    )(places.reshape(-1), stacked, *flat, *(before or ()))
 
 
 def mix_kernel(own_ref, got_ref, features_ref, weight_ref, gain_ref, slot_ref, out_ref):
@@ -256,16 +272,26 @@
     return received
 
 
-def way_round(devices):
+def way_round(devices, rows, length):
     chips = devices // 2
     cycle = list(range(0, chips, 2)) + list(range(chips - 1, 0, -2))
-    pairs, origins = [], [[0] * chips for _ in range(devices)]
+    back, on = [], []
+    places = [None] * devices
     for place, chip in enumerate(cycle):
-        for core, way in ((0, 1), (1, -1)):
-            pairs.append((2 * chip + core, 2 * cycle[(place + way) % chips] + core))
-            for step in range(chips):
-                origins[2 * chip + core][step] = cycle[(place - way * step) % chips]
-    return pairs, origins
+        for core in range(2):
+            me = 2 * chip + core
+            back.append((me, 2 * cycle[(place + 1) % chips] + core))
+            on.append((me, 2 * cycle[place - 1] + core))
+            order = [0]
+            for step in range(1, chips // 2):
+                order += [-step, step]
+            order.append(chips // 2)
+            places[me] = []
+            for offset in order:
+                start = cycle[(place + offset) % chips] * rows
+                column = min(start // 128 * 128, chips * rows - length)
+                places[me].append((column, start - column))
+    return back, on, places
 
 
 def padded_taps(neighbours):
@@ -322,20 +348,25 @@
         8 * points * width,
     )(features, face_list)
     round_trip = devices == 16
-    pairs, origins = way_round(devices)
-    ring = [mine]
+    rows = mine.shape[0]
+    length = -(-(rows + 127) // 128) * 128 if round_trip else rows * (devices // 2)
+    back_pairs, on_pairs, places = way_round(devices, rows, length)
+    back, on = [mine], [mine]
 
     def pass_on(*beside):
         if not round_trip:
             return beside
-        tied = lax.optimization_barrier((ring[-1], *beside))
-        ring[-1] = tied[0]
-        ring.append(lax.ppermute(ring[-1], "blocks", pairs))
-        return tied[1:]
+        tied = lax.optimization_barrier((back[-1], on[-1], *beside))
+        first, second = tied[:2]
+        back[-1], on[-1] = first, second
+        if len(back) == devices // 4:
+            first, second = first[: rows // 2], second[rows // 2 :]
+        back.append(lax.ppermute(first, "blocks", back_pairs))
+        on.append(lax.ppermute(second, "blocks", on_pairs))
+        return tied[2:]
 
     (faces,) = pass_on(faces)
     received = exchange_faces(faces.reshape(8, -1, width), devices, index)
-    pass_on()
     received = pass_on(*received)
     table = jnp.concatenate([ordered, *received], axis=0)
     own_table = lax.dynamic_slice(table, (0, core * half), (table.shape[0], half))
@@ -343,16 +374,21 @@
     other_table = lax.ppermute(other_half, "blocks", partner)
     other_neighbours = lax.ppermute(neighbours, "blocks", partner)
     tables = (padded_taps(other_neighbours), padded_taps(neighbours), other_table, own_table)
-    stacked = None
-    for first, count in ((0, 4), (4, 8), (12, 8), (20, 7)):
-        stacked = gather_part(first, count, tables, stacked)
-        (stacked,) = pass_on(stacked)
+    stacked = gather_part(0, 16, tables, None)
+    (stacked,) = pass_on(stacked)
+    stacked = gather_part(16, TAPS - 16, tables, stacked)
     if round_trip:
-        starts = jnp.array(origins, jnp.int32)[index] * mine.shape[0]
+        places = jnp.array(places, jnp.int32)[index]
+        early = [[mine], [back[1]], [on[1]], [back[2]], [on[2]]]
+        sums = conv_part(stacked, places[:5], early, None, length)
+        sums = pass_on(*sums)
+        sums = conv_part(stacked, places[5:7], [[back[3]], [on[3]]], sums, length)
+        sums = conv_part(stacked, places[7:], [[back[4], on[4]]], sums, length)
     else:
         groups = [list(range(first, devices, 2)) for first in range(2)]
-        ring = [lax.all_gather(mine, "blocks", axis=0, tiled=True, axis_index_groups=groups)]
-        starts = jnp.zeros((1,), jnp.int32)
+        weight = lax.all_gather(mine, "blocks", axis=0, tiled=True, axis_index_groups=groups)
+        sums = conv_part(stacked, jnp.zeros((1, 2), jnp.int32), [[weight]], None, length)
+    for_partner, own_part = sums
 
     positions = jnp.arange(points, dtype=jnp.int32)
     target = serial_rank // points
@@ -362,7 +398,6 @@
     before = (anchor[None, :] == anchor[:, None]) & (positions[None, :] < positions[:, None])
     in_slot = anchor * capacity + jnp.sum(before.astype(jnp.int32), axis=1)
 
-    for_partner, own_part = conv_part(stacked, starts, ring)
     from_partner = lax.ppermute(for_partner, "blocks", partner)
 
     outgoing = call(

time: 224 us -> 210 us (0.938)
  waiting for transfers between devices: 86.1 us -> 75.8 us
  starting transfers between devices: 42.7 us -> 35.3 us
  local copies, waits for them, and re-layouts: 12.4 us -> 19.5 us
  Pallas kernels: 77 us -> 73.4 us
    ppermute x7 -> x8, waiting for transfers between devices: 36.4 us -> 7.11 us  [the longest x4 5.16 us: pass_on(): back.append(lax.ppermute(first, 'blocks', back_pairs))]
    ppermute x3, waiting for transfers between devices: 0.17 us -> 21.2 us  [exchange_faces(): got = lax.ppermute(payload, 'blocks', pairs)]
    ppermute x2, starting transfers between devices: 13.8 us -> 4.78 us  [exchange_faces(): received[facing] = lax.ppermute(faces[facing], 'blocks', pairs)]
    ppermute x7 -> x8, starting transfers between devices: 0.08 us -> 5.95 us  [the longest x4 4.13 us: pass_on(): on.append(lax.ppermute(second, 'blocks', on_pairs))]
    pallas_call x4 -> x2, Pallas kernels: 31.5 us -> 26.1 us  [gather_part(): call(functools.partial(gather_kernel, first), jax.ShapeDtypeStruct((2 * p...]
    slice x0 -> x3, local copies, waits for them, and re-layouts: none -> 2.6 us  [the longest x2 2.6 us: pass_on(): first, second = (first[:rows // 2], second[rows // 2:])]
    unnamed x47, local copies, waits for them, and re-layouts: 6.28 us -> 8.72 us
    pallas_call x1 -> x3, Pallas kernels: 14.8 us -> 16.5 us  [conv_part(): call(functools.partial(conv_kernel, slots, before is None), (jax.ShapeDty...]
  transfers between devices with their start and end apart: 18 -> 19, of which waited for: 11 -> 9; matrix products, arithmetic and copies ran while one was open for 5% -> 8% of each run, Pallas kernels for 14% -> 19%
where the time goes in v4:
time: 210 us; the launch traced here: 209 us
  waiting for transfers between devices  75.8 us (36%)
  Pallas kernels  73.4 us (35%)
  starting transfers between devices  35.3 us (17%)
  local copies, waits for them, and re-layouts  19.5 us (9%)
  other arithmetic  4.24 us (2%)
    pallas_call x2, Pallas kernels, gather_part(): call(functools.partial(gather_kernel, first), jax.ShapeDtypeStruct((2 * p...  26.1 us
    pallas_call x1, Pallas kernels, body(): call(block_kernel, jax.ShapeDtypeStruct((slots, width), BF16), 48, 20 * p...  26 us
    all_to_all x1, waiting for transfers between devices, body(): lax.all_to_all(back.reshape(devices, capacity, width), 'blocks', split_ax...  24.7 us
    ppermute x3, waiting for transfers between devices, exchange_faces(): got = lax.ppermute(payload, 'blocks', pairs)  21.2 us
    all_to_all x1, waiting for transfers between devices, body(): lax.all_to_all(outgoing.reshape(devices, capacity, width), 'blocks', spli...  19.6 us
    pallas_call x3, Pallas kernels, conv_part(): call(functools.partial(conv_kernel, slots, before is None), (jax.ShapeDty...  16.5 us
    unnamed x47, local copies, waits for them, and re-layouts  8.72 us
    ppermute x3, starting transfers between devices, exchange_faces(): got = lax.ppermute(payload, 'blocks', pairs)  8.13 us
  transfers between devices with their start and end apart: 19, of which 9 were waited for; matrix products, arithmetic and copies ran while one was open for 8% of the time, Pallas kernels for 19%

profile of v4, /device:TPU:9, one launch (start us, length us, event | category | flops | bytes accessed | tf_op | source)
XLA Modules:
  0.0 208.7 jit_solution(17919497965356328399)
XLA Ops:
  0.0 1.1 slice.83
  1.1 0.7 collective-permute-start.1
  1.9 1.0 copy.34
  2.8 0.1 collective-permute-start
  2.9 1.1 slice.82
  4.0 0.2 reshape.98.rows_ref
  4.2 0.8 shard_map.145
  5.1 0.1 maximum_select_fusion
  5.2 1.3 collective-permute-start.2
  6.6 0.2 collective-permute-start.3
  6.8 6.1 %collective-permute-start.6 = (bf16[64,512]{1,0:T(8,128)(2,1)S(1)}, bf16[64,512]{1,0:T(8,128)(2,1)S(1)}, u32[]{:S(2)}, u32[]{:S(2)}) collective-permute-start(bf16[64,512]{1,0:T(8,128)(2,1)S(1)} %get-tuple-element.70), channel_id=1, source_target_pairs={{0,9},{1,10},{2,11},{3,12},{4,13},{5,14},{6,15},{8,1},{9,2},{10,3}... | collective-permute-start | bytes 196616 | tf_op jit(solution)/shard_map/ppermute | solution.py:260
  12.9 0.1 collective-permute-start.5
  13.1 18.1 %collective-permute-done.6 = bf16[64,512]{1,0:T(8,128)(2,1)S(1)} collective-permute-done((bf16[64,512]{1,0:T(8,128)(2,1)S(1)}, bf16[64,512]{1,0:T(8,128)(2,1)S(1)}, u32[]{:S(2)}, u32[]{:S(2)}) %collective-permute-start.6) | collective-permute-done | bytes 65568 | tf_op jit(solution)/shard_map/ppermute | solution.py:260
  31.2 1.9 collective-permute-start.4
  33.1 2.3 %collective-permute-start.7 = (bf16[64,512]{1,0:T(8,128)(2,1)S(1)}, bf16[64,512]{1,0:T(8,128)(2,1)S(1)}, u32[]{:S(2)}, u32[]{:S(2)}) collective-permute-start(bf16[64,512]{1,0:T(8,128)(2,1)S(1)} %get-tuple-element.68), channel_id=1, source_target_pairs={{1,0},{2,1},{3,2},{4,3},{5,4},{6,5},{7,6},{9,8},{10,9},{11,10},{12... | collective-permute-start | bytes 196616 | tf_op jit(solution)/shard_map/ppermute | solution.py:271
  35.5 3.1 %collective-permute-done.4 = bf16[64,512]{1,0:T(8,128)(2,1)S(1)} collective-permute-done((bf16[64,512]{1,0:T(8,128)(2,1)S(1)}, bf16[64,512]{1,0:T(8,128)(2,1)S(1)}, u32[]{:S(2)}, u32[]{:S(2)}) %collective-permute-start.4) | collective-permute-done | bytes 65568 | tf_op jit(solution)/shard_map/ppermute | solution.py:260
  38.6 2.5 %collective-permute-start.8 = (bf16[64,512]{1,0:T(8,128)(2,1)S(1)}, bf16[64,512]{1,0:T(8,128)(2,1)S(1)}, u32[]{:S(2)}, u32[]{:S(2)}) collective-permute-start(bf16[64,512]{1,0:T(8,128)(2,1)S(1)} %get-tuple-element.66), channel_id=1, source_target_pairs={{0,1},{1,2},{2,3},{3,4},{4,5},{5,6},{6,7},{8,9},{9,10},{10,11},{11... | collective-permute-start | bytes 196616 | tf_op jit(solution)/shard_map/ppermute | solution.py:271
  41.1 1.3 collective-permute-done.8
  42.5 1.2 constant_dynamic-slice_fusion
  43.7 3.2 %collective-permute-start.9 = (bf16[1024,256]{1,0:T(8,128)(2,1)}, bf16[1024,256]{1,0:T(8,128)(2,1)}, u32[]{:S(2)}, u32[]{:S(2)}) collective-permute-start(bf16[1024,256]{1,0:T(8,128)(2,1)} %get-tuple-element.65), channel_id=1, source_target_pairs={{0,1},{1,0},{2,3},{3,2},{4,5},{5,4},{6,7},{7,6},{8,9},{9,8},{10,11... | collective-permute-start | bytes 1572872 | tf_op jit(solution)/shard_map/ppermute | solution.py:374
  47.0 0.7 constant_dynamic-slice_fusion.2
  47.6 0.9 copy.35
  48.5 0.8 copy.36
  49.4 0.1 reshape.85.places_ref
  49.5 0.1 fusion.7
  49.7 1.4 collective-permute-start.11
  51.2 2.1 %add_convert_fusion.1 = (f32[512,128]{1,0:T(8,128)}, f32[512,128]{1,0:T(8,128)}) fusion(s32[512,13]{1,0:T(8,128)} %copy.36, s32[512,13]{1,0:T(8,128)} %copy.35, s32[512,1]{1,0:T(8,128)S(1)} %iota.13, s32[128]{0:T(128)S(1)} %pad.13.clone, s32[512,13]{1,0:T(8,128)S(1)} %get-tuple-element.74, s32[512,13]{1,0:T(8,128)S(1)} %get-tuple-element.73), kind=kLoop, calls=%fused_computation.7 | loop fusion | flops 524288 | bytes 633344 | tf_op jit(solution)/shard_map/convert_element_type | solution.py:304
  53.3 15.2 %shard_map.146.refs_0_ = bf16[1024,6912]{1,0:T(8,128)(2,1)} custom-call(f32[512,128]{1,0:T(8,128)} %get-tuple-element.72.other_rows, f32[512,128]{1,0:T(8,128)} %get-tuple-element.71.own_rows, bf16[1024,256]{1,0:T(8,128)(2,1)} %collective-permute-done.9.other_table, bf16[1024,256]{1,0:T(8,128)(2,1)} %get-tuple-element.64.own_table), custom_call_target="tpu_custom_call" | custom-call | flops 8589934592 | bytes 8388608 | tf_op jit(solution)/shard_map/pallas_call | solution.py:78
  68.5 2.6 %collective-permute-done.10.refs_3_ = bf16[864,512]{1,0:T(8,128)(2,1)S(1)} collective-permute-done((bf16[864,512]{1,0:T(8,128)(2,1)S(1)}, bf16[864,512]{1,0:T(8,128)(2,1)S(1)}, u32[]{:S(2)}, u32[]{:S(2)}) %collective-permute-start.10) | collective-permute-done | bytes 884768 | tf_op jit(solution)/shard_map/ppermute | solution.py:364
  71.1 0.9 copy-done.9
  72.0 0.2 collective-permute-start.12
  72.2 1.3 collective-permute-start.13
  73.5 11.0 %shard_map.147.stacked_ref = bf16[1024,6912]{1,0:T(8,128)(2,1)} custom-call(f32[512,128]{1,0:T(8,128)} %get-tuple-element.72.other_rows, f32[512,128]{1,0:T(8,128)} %get-tuple-element.71.own_rows, bf16[1024,256]{1,0:T(8,128)(2,1)} %collective-permute-done.9.other_table, ...), custom_call_target="tpu_custom_call", output_to_operand_aliasing={{}: (4, {})} | custom-call | flops 5905580032 | bytes 5767168 | tf_op jit(solution)/shard_map/pallas_call | solution.py:78
  84.5 1.2 copy-done.1
  85.6 1.2 copy-done.6
  86.8 1.2 copy-done.8
  88.0 1.2 copy-done.10
  89.1 8.1 %shard_map.148 = (f32[512,512]{1,0:T(8,128)S(1)}, f32[512,512]{1,0:T(8,128)S(1)}) custom-call(s32[10]{0:T(128)S(1)} %reshape.85.places_ref, bf16[1024,6912]{1,0:T(8,128)(2,1)} %shard_map.147.stacked_ref, bf16[864,512]{1,0:T(8,128)(2,1)S(1)} %bitcast.22, bf16[864,512]{1,0:T(8,128)(2,1)S(1)} %copy-done.6, bf16[864,512]{1,0:T(8,128)(2,1)S(1)} %copy-done.8, ...), custom_call_target="tpu_custom_call" | custom-call | flops 5368709120 | bytes 15728640 | tf_op jit(solution)/shard_map/pallas_call | solution.py:139
  97.2 0.8 slice.93
  98.0 0.2 collective-permute-start.14
  98.2 1.8 slice.94
  100.0 1.3 collective-permute-start.15
  101.3 0.1 reshape.86.places_ref
  101.4 4.8 %shard_map.149 = (f32[512,512]{1,0:T(8,128)S(1)}, f32[512,512]{1,0:T(8,128)S(1)}) custom-call(s32[4]{0:T(128)S(1)} %reshape.86.places_ref, bf16[1024,6912]{1,0:T(8,128)(2,1)} %shard_map.147.stacked_ref, bf16[864,512]{1,0:T(8,128)(2,1)S(1)} %collective-permute-done.12.refs_0_, ...), custom_call_target="tpu_custom_call", output_to_operand_aliasing={{0}: (4, {}), {1}: (5, {})} | custom-call | flops 2147483648 | bytes 6291456 | tf_op jit(solution)/shard_map/pallas_call | solution.py:139
  106.2 2.5 %collective-permute-done.14.refs_0_ = bf16[432,512]{1,0:T(8,128)(2,1)} collective-permute-done((bf16[432,512]{1,0:T(8,128)(2,1)}, bf16[432,512]{1,0:T(8,128)(2,1)}, u32[]{:S(2)}, u32[]{:S(2)}) %collective-permute-start.14) | collective-permute-done | bytes 442400 | tf_op jit(solution)/shard_map/ppermute | solution.py:364
  108.8 1.9 collective-permute-done.15.refs_1_
  110.7 3.7 %shard_map.150 = (f32[512,512]{1,0:T(8,128)S(1)}, f32[512,512]{1,0:T(8,128)S(1)}) custom-call(s32[2]{0:T(128)S(1)} %slice_bitcast_fusion.places_ref, bf16[1024,6912]{1,0:T(8,128)(2,1)} %shard_map.147.stacked_ref, bf16[432,512]{1,0:T(8,128)(2,1)} %collective-permute-done.14.refs_0_, ...), custom_call_target="tpu_custom_call", output_to_operand_aliasing={{0}: (4, {}), {1}: (5, {})} | custom-call | flops 1073741824 | bytes 3145728 | tf_op jit(solution)/shard_map/pallas_call | solution.py:139
  114.4 2.3 %collective-permute-start.16 = (f32[512,512]{1,0:T(8,128)S(1)}, f32[512,512]{1,0:T(8,128)S(1)}, u32[]{:S(2)}, u32[]{:S(2)}) collective-permute-start(f32[512,512]{1,0:T(8,128)S(1)} %get-tuple-element.60), channel_id=1, source_target_pairs={{0,1},{1,0},{2,3},{3,2},{4,5},{5,4},{6,7},{7,6},{8,9},{9,8},{10,11... | collective-permute-start | bytes 3145736 | tf_op jit(solution)/shard_map/ppermute | solution.py:401
  116.7 0.3 convert_reduce_fusion.1
  117.1 1.9 collective-permute-done.16.got_ref
  119.0 2.4 %shard_map.151 = bf16[1024,512]{1,0:T(8,128)(2,1)} custom-call(f32[512,512]{1,0:T(8,128)S(1)} %get-tuple-element.59.own_ref, f32[512,512]{1,0:T(8,128)S(1)} %collective-permute-done.16.got_ref, bf16[512,512]{1,0:T(8,128)(2,1)S(1)} %copy-done.2, bf16[512,512]{1,0:T(8,128)(2,1)S(1)} %copy-done.3, f32[1,512]{1,0:T(1,128)S(1)} %bitcast.27, s32[1,512]{1,0:T(1,128)S(1)} %bitcast.23), custom_call_target="tpu_custom_call" | custom-call | flops 805306368 | bytes 2097152 | tf_op jit(solution)/shard_map/pallas_call | solution.py:403
  121.3 5.2 %all-to-all-start = ((bf16[16,64,512]{2,1,0:T(8,128)(2,1)}), bf16[16,64,512]{2,1,0:T(8,128)(2,1)S(1)}, u32[]{:S(2)}, u32[]{:S(2)}) async-start(bf16[16,64,512]{2,1,0:T(8,128)(2,1)} %bitcast.5), calls=%async_computation | async-start | bytes 2097152 | tf_op jit(solution)/shard_map/all_to_all | solution.py:417
  126.5 1.5 fusion.5
  128.0 1.0 copy.42
  129.0 1.0 copy.43
  130.1 0.2 convert_reduce_fusion
  130.3 0.1 copy.40.slot_col_ref
  130.5 1.3 maximum_bitcast_fusion.qv_ref
  131.8 19.6 %all-to-all-done = bf16[16,64,512]{2,1,0:T(8,128)(2,1)S(1)} async-done(((bf16[16,64,512]{2,1,0:T(8,128)(2,1)}), bf16[16,64,512]{2,1,0:T(8,128)(2,1)S(1)}, u32[]{:S(2)}, u32[]{:S(2)}) %all-to-all-start) | async-done | bytes 1048608 | tf_op jit(solution)/shard_map/all_to_all | solution.py:417
  151.4 26.0 %shard_map.152 = bf16[1024,512]{1,0:T(8,128)(2,1)} custom-call(bf16[1024,512]{1,0:T(8,128)(2,1)S(1)} %bitcast.18, s32[512,1]{1,0:T(8,128)S(1)} %copy.40.slot_col_ref, s32[1,512]{1,0:T(1,128)S(1)} %bitcast.26, f32[1,512]{1,0:T(1,128)S(1)} %bitcast.28, bf16[1024,512]{1,0:T(8,128)(2,1)S(1)} %maximum_bitcast_fusion.qv_ref, ...), custom_call_target="tpu_custom_call" | custom-call | flops 2684354560 | bytes 4194304 | tf_op jit(solution)/shard_map/pallas_call | solution.py:423
  177.4 4.9 %all-to-all-start.1 = ((bf16[16,64,512]{2,1,0:T(8,128)(2,1)}), bf16[16,64,512]{2,1,0:T(8,128)(2,1)S(1)}, u32[]{:S(2)}, u32[]{:S(2)}) async-start(bf16[16,64,512]{2,1,0:T(8,128)(2,1)} %bitcast.12), calls=%async_computation.1 | async-start | bytes 2097152 | tf_op jit(solution)/shard_map/all_to_all | solution.py:448
  182.3 0.1 copy.41.slot_ref
  182.5 24.7 %all-to-all-done.1 = bf16[16,64,512]{2,1,0:T(8,128)(2,1)S(1)} async-done(((bf16[16,64,512]{2,1,0:T(8,128)(2,1)}), bf16[16,64,512]{2,1,0:T(8,128)(2,1)S(1)}, u32[]{:S(2)}, u32[]{:S(2)}) %all-to-all-start.1) | async-done | bytes 1048608 | tf_op jit(solution)/shard_map/all_to_all | solution.py:448
  207.2 1.6 shard_map.153
  (65 shorter events, 0.5 us)
Async XLA Ops:
  0.0 4.0 %copy-start.17 = (s32[1,8,64]{2,1,0:T(8,128)S(1)}, s32[1,8,64]{2,1,0:T(8,128)}, u32[]{:S(2)}) copy-start(s32[1,8,64]{2,1,0:T(8,128)} %param.25) | copy-start | bytes 6148
  0.0 4.2 %copy-start.2 = (bf16[512,512]{1,0:T(8,128)(2,1)S(1)}, bf16[512,512]{1,0:T(8,128)(2,1)}, u32[]{:S(2)}) copy-start(bf16[512,512]{1,0:T(8,128)(2,1)} %features_ref.3) | copy-start | bytes 1572868
  0.0 5.0 %copy-start.14 = (s32[512,26]{0,1:T(8,128)S(1)}, s32[512,26]{0,1:T(8,128)}, u32[]{:S(2)}) copy-start(s32[512,26]{0,1:T(8,128)} %param.26) | copy-start | bytes 159748
  1.1 4.0 %collective-permute-start.1 = (bf16[13,32,512]{2,1,0:T(8,128)(2,1)S(1)}, bf16[13,32,512]{2,1,0:T(8,128)(2,1)S(1)}, u32[]{:S(2)}, u32[]{:S(2)}) collective-permute-start(bf16[13,32,512]{2,1,0:T(8,128)(2,1)S(1)} %slice.83), channel_id=1, source_target_pairs={{0,1},{1,0},{2,3},{3,2},{4,5},{5,4},{6,7},{7,6},{8,9},{9,8},{10,11... | collective-permute-start | bytes 1277960 | tf_op jit(solution)/shard_map/ppermute | solution.py:335
  2.8 46.7 %collective-permute-start = (s32[512,26]{1,0:T(8,128)S(1)}, s32[512,26]{1,0:T(8,128)S(1)}, u32[]{:S(2)}, u32[]{:S(2)}) collective-permute-start(s32[512,26]{1,0:T(8,128)S(1)} %copy.34), channel_id=1, source_target_pairs={{0,1},{1,0},{2,3},{3,2},{4,5},{5,4},{6,7},{7,6},{8,9},{9,8},{10,11... | collective-permute-start | bytes 159752 | tf_op jit(solution)/shard_map/ppermute | solution.py:375
  5.2 38.5 %copy-start = (bf16[27,32,512]{2,1,0:T(8,128)(2,1)}, bf16[27,32,512]{2,1,0:T(8,128)(2,1)S(1)}, u32[]{:S(2)}) copy-start(bf16[27,32,512]{2,1,0:T(8,128)(2,1)S(1)} %maximum_select_fusion) | copy-start | bytes 2654212
  5.2 37.1 %collective-permute-start.2 = (bf16[864,512]{1,0:T(8,128)(2,1)S(1)}, bf16[864,512]{1,0:T(8,128)(2,1)S(1)}, u32[]{:S(2)}, u32[]{:S(2)}) collective-permute-start(bf16[864,512]{1,0:T(8,128)(2,1)S(1)} %bitcast.20), channel_id=1, source_target_pairs={{0,4},{1,5},{4,8},{5,9},{8,12},{9,13},{12,14},{13,15},{14,10},{15,... | collective-permute-start | bytes 2654216 | tf_op jit(solution)/shard_map/ppermute | solution.py:364
  6.6 35.8 %collective-permute-start.3 = (bf16[864,512]{1,0:T(8,128)(2,1)S(1)}, bf16[864,512]{1,0:T(8,128)(2,1)S(1)}, u32[]{:S(2)}, u32[]{:S(2)}) collective-permute-start(bf16[864,512]{1,0:T(8,128)(2,1)S(1)} %bitcast.21), channel_id=1, source_target_pairs={{0,2},{1,3},{4,0},{5,1},{8,4},{9,5},{12,8},{13,9},{14,12},{15,13},... | collective-permute-start | bytes 2654216 | tf_op jit(solution)/shard_map/ppermute | solution.py:365
  6.8 24.4 %collective-permute-start.6 = (bf16[64,512]{1,0:T(8,128)(2,1)S(1)}, bf16[64,512]{1,0:T(8,128)(2,1)S(1)}, u32[]{:S(2)}, u32[]{:S(2)}) collective-permute-start(bf16[64,512]{1,0:T(8,128)(2,1)S(1)} %get-tuple-element.70), channel_id=1, source_target_pairs={{0,9},{1,10},{2,11},{3,12},{4,13},{5,14},{6,15},{8,1},{9,2},{10,3}... | collective-permute-start | bytes 196616 | tf_op jit(solution)/shard_map/ppermute | solution.py:260
  12.9 20.2 %collective-permute-start.5 = (bf16[64,512]{1,0:T(8,128)(2,1)S(1)}, bf16[64,512]{1,0:T(8,128)(2,1)S(1)}, u32[]{:S(2)}, u32[]{:S(2)}) collective-permute-start(bf16[64,512]{1,0:T(8,128)(2,1)S(1)} %get-tuple-element.67), channel_id=1, source_target_pairs={{0,8},{1,9},{2,10},{3,11},{4,12},{5,13},{6,14},{7,15},{8,0},{9,1},... | collective-permute-start | bytes 196616 | tf_op jit(solution)/shard_map/ppermute | solution.py:260
  31.2 7.4 %collective-permute-start.4 = (bf16[64,512]{1,0:T(8,128)(2,1)S(1)}, bf16[64,512]{1,0:T(8,128)(2,1)S(1)}, u32[]{:S(2)}, u32[]{:S(2)}) collective-permute-start(bf16[64,512]{1,0:T(8,128)(2,1)S(1)} %get-tuple-element.69), channel_id=1, source_target_pairs={{1,8},{2,9},{3,10},{4,11},{5,12},{6,13},{7,14},{9,0},{10,1},{11,2}... | collective-permute-start | bytes 196616 | tf_op jit(solution)/shard_map/ppermute | solution.py:260
  33.1 7.9 %collective-permute-start.7 = (bf16[64,512]{1,0:T(8,128)(2,1)S(1)}, bf16[64,512]{1,0:T(8,128)(2,1)S(1)}, u32[]{:S(2)}, u32[]{:S(2)}) collective-permute-start(bf16[64,512]{1,0:T(8,128)(2,1)S(1)} %get-tuple-element.68), channel_id=1, source_target_pairs={{1,0},{2,1},{3,2},{4,3},{5,4},{6,5},{7,6},{9,8},{10,9},{11,10},{12... | collective-permute-start | bytes 196616 | tf_op jit(solution)/shard_map/ppermute | solution.py:271
  38.6 3.8 %collective-permute-start.8 = (bf16[64,512]{1,0:T(8,128)(2,1)S(1)}, bf16[64,512]{1,0:T(8,128)(2,1)S(1)}, u32[]{:S(2)}, u32[]{:S(2)}) collective-permute-start(bf16[64,512]{1,0:T(8,128)(2,1)S(1)} %get-tuple-element.66), channel_id=1, source_target_pairs={{0,1},{1,2},{2,3},{3,4},{4,5},{5,6},{6,7},{8,9},{9,10},{10,11},{11... | collective-permute-start | bytes 196616 | tf_op jit(solution)/shard_map/ppermute | solution.py:271
  42.4 7.3 %copy-start.5 = (bf16[864,512]{1,0:T(8,128)(2,1)}, bf16[864,512]{1,0:T(8,128)(2,1)S(1)}, u32[]{:S(2)}) copy-start(bf16[864,512]{1,0:T(8,128)(2,1)S(1)} %collective-permute-done.2.refs_1_) | copy-start | bytes 2654212
  42.4 7.4 %copy-start.7 = (bf16[864,512]{1,0:T(8,128)(2,1)}, bf16[864,512]{1,0:T(8,128)(2,1)S(1)}, u32[]{:S(2)}) copy-start(bf16[864,512]{1,0:T(8,128)(2,1)S(1)} %collective-permute-done.3.refs_2_) | copy-start | bytes 2654212
  43.7 9.6 %collective-permute-start.9 = (bf16[1024,256]{1,0:T(8,128)(2,1)}, bf16[1024,256]{1,0:T(8,128)(2,1)}, u32[]{:S(2)}, u32[]{:S(2)}) collective-permute-start(bf16[1024,256]{1,0:T(8,128)(2,1)} %get-tuple-element.65), channel_id=1, source_target_pairs={{0,1},{1,0},{2,3},{3,2},{4,5},{5,4},{6,7},{7,6},{8,9},{9,8},{10,11... | collective-permute-start | bytes 1572872 | tf_op jit(solution)/shard_map/ppermute | solution.py:374
  49.7 21.4 %collective-permute-start.10 = (bf16[864,512]{1,0:T(8,128)(2,1)S(1)}, bf16[864,512]{1,0:T(8,128)(2,1)S(1)}, u32[]{:S(2)}, u32[]{:S(2)}) collective-permute-start(bf16[864,512]{1,0:T(8,128)(2,1)S(1)} %collective-permute-done.2.refs_1_), channel_id=1, source_target_pairs={{0,4},{1,5},{4,8},{5,9},{8,12},{9,13},{12,14},{13,15},{14,10},{15,... | collective-permute-start | bytes 2654216 | tf_op jit(solution)/shard_map/ppermute | solution.py:364
  49.7 22.3 %collective-permute-start.11 = (bf16[864,512]{1,0:T(8,128)(2,1)S(1)}, bf16[864,512]{1,0:T(8,128)(2,1)}, u32[]{:S(2)}, u32[]{:S(2)}) collective-permute-start(bf16[864,512]{1,0:T(8,128)(2,1)S(1)} %collective-permute-done.3.refs_2_), channel_id=1, source_target_pairs={{0,2},{1,3},{4,0},{5,1},{8,4},{9,5},{12,8},{13,9},{14,12},{15,13},... | collective-permute-start | bytes 2654216 | tf_op jit(solution)/shard_map/ppermute | solution.py:365
  71.1 0.9 copy-start.9
  72.0 25.2 %collective-permute-start.12 = (bf16[864,512]{1,0:T(8,128)(2,1)}, bf16[864,512]{1,0:T(8,128)(2,1)S(1)}, u32[]{:S(2)}, u32[]{:S(2)}) collective-permute-start(bf16[864,512]{1,0:T(8,128)(2,1)} %copy-done.9), channel_id=1, source_target_pairs={{0,4},{1,5},{4,8},{5,9},{8,12},{9,13},{12,14},{13,15},{14,10},{15,... | collective-permute-start | bytes 2654216 | tf_op jit(solution)/shard_map/ppermute | solution.py:364
  72.2 25.0 %collective-permute-start.13 = (bf16[864,512]{1,0:T(8,128)(2,1)}, bf16[864,512]{1,0:T(8,128)(2,1)}, u32[]{:S(2)}, u32[]{:S(2)}) collective-permute-start(bf16[864,512]{1,0:T(8,128)(2,1)} %collective-permute-done.11.refs_4_), channel_id=1, source_target_pairs={{0,2},{1,3},{4,0},{5,1},{8,4},{9,5},{12,8},{13,9},{14,12},{15,13},... | collective-permute-start | bytes 2654216 | tf_op jit(solution)/shard_map/ppermute | solution.py:365
  84.5 1.2 copy-start.1
  85.6 1.2 copy-start.6
  86.8 1.2 copy-start.8
  88.0 1.2 copy-start.10
  98.0 10.7 %collective-permute-start.14 = (bf16[432,512]{1,0:T(8,128)(2,1)}, bf16[432,512]{1,0:T(8,128)(2,1)}, u32[]{:S(2)}, u32[]{:S(2)}) collective-permute-start(bf16[432,512]{1,0:T(8,128)(2,1)} %slice.93), channel_id=1, source_target_pairs={{0,4},{1,5},{4,8},{5,9},{8,12},{9,13},{12,14},{13,15},{14,10},{15,... | collective-permute-start | bytes 1327112 | tf_op jit(solution)/shard_map/ppermute | solution.py:364
  100.0 10.7 %collective-permute-start.15 = (bf16[432,512]{1,0:T(8,128)(2,1)}, bf16[432,512]{1,0:T(8,128)(2,1)}, u32[]{:S(2)}, u32[]{:S(2)}) collective-permute-start(bf16[432,512]{1,0:T(8,128)(2,1)} %slice.94), channel_id=1, source_target_pairs={{0,2},{1,3},{4,0},{5,1},{8,4},{9,5},{12,8},{13,9},{14,12},{15,13},... | collective-permute-start | bytes 1327112 | tf_op jit(solution)/shard_map/ppermute | solution.py:365
  110.7 6.0 %copy-start.15 = (s32[512]{0:T(512)S(1)}, s32[512]{0:T(512)}, u32[]{:S(2)}) copy-start(s32[512]{0:T(512)} %param.27) | copy-start | bytes 6148
  110.7 8.3 %copy-start.3 = (bf16[512,512]{1,0:T(8,128)(2,1)S(1)}, bf16[512,512]{1,0:T(8,128)(2,1)}, u32[]{:S(2)}) copy-start(bf16[512,512]{1,0:T(8,128)(2,1)} %weight_ref.1) | copy-start | bytes 1572868
  110.7 8.3 %copy-start.4 = (f32[512]{0:T(512)S(1)}, f32[512]{0:T(512)}, u32[]{:S(2)}) copy-start(f32[512]{0:T(512)} %param.18) | copy-start | bytes 6148
  114.4 4.6 %collective-permute-start.16 = (f32[512,512]{1,0:T(8,128)S(1)}, f32[512,512]{1,0:T(8,128)S(1)}, u32[]{:S(2)}, u32[]{:S(2)}) collective-permute-start(f32[512,512]{1,0:T(8,128)S(1)} %get-tuple-element.60), channel_id=1, source_target_pairs={{0,1},{1,0},{2,3},{3,2},{4,5},{5,4},{6,7},{7,6},{8,9},{9,8},{10,11... | collective-permute-start | bytes 3145736 | tf_op jit(solution)/shard_map/ppermute | solution.py:401
  121.3 30.1 %all-to-all-start = ((bf16[16,64,512]{2,1,0:T(8,128)(2,1)}), bf16[16,64,512]{2,1,0:T(8,128)(2,1)S(1)}, u32[]{:S(2)}, u32[]{:S(2)}) async-start(bf16[16,64,512]{2,1,0:T(8,128)(2,1)} %bitcast.5), calls=%async_computation | async-start | bytes 2097152 | tf_op jit(solution)/shard_map/all_to_all | solution.py:417
  126.5 3.5 %copy-start.16 = (s32[512]{0:T(512)S(1)}, s32[512]{0:T(512)}, u32[]{:S(2)}) copy-start(s32[512]{0:T(512)} %param.28) | copy-start | bytes 6148
  128.0 23.4 %copy-start.11 = (bf16[512,512]{1,0:T(8,128)(2,1)S(1)}, bf16[512,512]{1,0:T(8,128)(2,1)}, u32[]{:S(2)}) copy-start(bf16[512,512]{1,0:T(8,128)(2,1)} %proj_ref.1) | copy-start | bytes 1572868
  128.0 23.4 %copy-start.12 = (f32[512]{0:T(512)S(1)}, f32[512]{0:T(512)}, u32[]{:S(2)}) copy-start(f32[512]{0:T(512)} %param.19) | copy-start | bytes 6148
  128.0 23.4 %copy-start.13 = (f32[512]{0:T(512)S(1)}, f32[512]{0:T(512)}, u32[]{:S(2)}) copy-start(f32[512]{0:T(512)} %param.22) | copy-start | bytes 6148
  177.4 29.8 %all-to-all-start.1 = ((bf16[16,64,512]{2,1,0:T(8,128)(2,1)}), bf16[16,64,512]{2,1,0:T(8,128)(2,1)S(1)}, u32[]{:S(2)}, u32[]{:S(2)}) async-start(bf16[16,64,512]{2,1,0:T(8,128)(2,1)} %bitcast.12), calls=%async_computation.1 | async-start | bytes 2097152 | tf_op jit(solution)/shard_map/all_to_all | solution.py:448

commit v5 on v4

--- a/solution.py
+++ b/solution.py
@@ -58,52 +58,44 @@
     faces_ref[...] = dot(one_hot(rows_ref[...] == row_ids), ordered).astype(BF16)
 
 
-def gather_kernel(first, other_rows, own_rows, other_table, own_table, *refs):
-    out_ref = refs[-1]
-    tap = first + pl.program_id(0)
-    points, lanes = own_rows.shape
-    chosen = lax.broadcasted_iota(jnp.int32, (points, lanes), 1) == tap
-    row_ids = lax.broadcasted_iota(jnp.int32, (1, own_table.shape[0]), 1).astype(F32)
-    for start, rows, table in ((0, other_rows, other_table), (points, own_rows, own_table)):
-        column = jnp.sum(jnp.where(chosen, rows[...], 0.0), axis=1, keepdims=True)
-        taken = dot(one_hot(column == row_ids), table[...]).astype(BF16)
-        out_ref[start : start + points] = taken
-
-
-def gather_part(first, count, tables, stacked):
-    points, lanes = tables[1].shape
-    height, half = tables[3].shape
+def gather_kernel(rows_ref, table_ref, out_ref):
+    chosen = lax.broadcasted_iota(jnp.int32, rows_ref.shape, 1) == pl.program_id(0)
+    row_ids = lax.broadcasted_iota(jnp.int32, (1, table_ref.shape[0]), 1).astype(F32)
+    column = jnp.sum(jnp.where(chosen, rows_ref[...], 0.0), axis=1, keepdims=True)
+    out_ref[...] = dot(one_hot(column == row_ids), table_ref[...]).astype(BF16)
+
+
+def gather_block(rows, table):
+    points, lanes = rows.shape
+    height, half = table.shape
     whole = lambda tap: (0, 0)
-    extra = [] if stacked is None else [stacked]
     return call(
-        functools.partial(gather_kernel, first),
-        jax.ShapeDtypeStruct((2 * points, TAPS * half), BF16),
+        gather_kernel,
+        jax.ShapeDtypeStruct((points, TAPS * half), BF16),
         60,
-        4 * count * points * height * half,
-        4 * count * points * half,
-        grid=(count,),
-        in_specs=[pl.BlockSpec((points, lanes), whole)] * 2
-        + [pl.BlockSpec((height, half), whole)] * 2
-        + [pl.BlockSpec(memory_space=pl.ANY)] * len(extra),
-        out_specs=pl.BlockSpec((2 * points, half), lambda tap: (0, first + tap)),
-        input_output_aliases={} if stacked is None else {4: 0},
-    )(*tables, *extra)
-
-
-def conv_kernel(slots, first, places_ref, stacked_ref, *refs):
+        2 * TAPS * points * height * half,
+        2 * TAPS * points * half,
+        grid=(TAPS,),
+        in_specs=[pl.BlockSpec((points, lanes), whole), pl.BlockSpec((height, half), whole)],
+        out_specs=pl.BlockSpec((points, half), lambda tap: (0, tap)),
+    )(rows, table)
+
+
+def conv_kernel(slots, first, places_ref, other_stacked, own_stacked, *refs):
     pieces = refs[: sum(slots)]
     other_ref, own_ref, lhs, held, sems = refs[-5:]
-    points = own_ref.shape[0]
     length = held.shape[1]
     copies, taken = [], 0
     for at, count in enumerate(slots):
         column = pl.multiple_of(places_ref[2 * at], 128)
         row = pl.multiple_of(places_ref[2 * at + 1], 16)
-        copy = pltpu.make_async_copy(
-            stacked_ref.at[:, pl.ds(column, length)], lhs.at[at], sems.at[at, 0]
-        )
-        copy.start()
-        copies.append([copy])
+        copies.append([])
+        for half, stacked in enumerate((other_stacked, own_stacked)):
+            copy = pltpu.make_async_copy(
+                stacked.at[:, pl.ds(column, length)], lhs.at[at, half], sems.at[at, half]
+            )
+            copy.start()
+            copies[-1].append(copy)
         short = count * pieces[taken].shape[0]
         edge = length - short
         if edge:
@@ -113,7 +105,7 @@
             piece = pieces[taken]
             size = piece.shape[0]
             copy = pltpu.make_async_copy(
-                piece, held.at[at, pl.ds(row + part * size, size)], sems.at[at, 1 + part]
+                piece, held.at[at, pl.ds(row + part * size, size)], sems.at[at, 2 + part]
             )
             copy.start()
             copies[-1].append(copy)
@@ -122,7 +114,7 @@
         for copy in copies[at]:
             copy.wait()
         for half, ref in enumerate((other_ref, own_ref)):
-            product = dot(lhs[at, half * points : (half + 1) * points], held[at])
+            product = dot(lhs[at, half], held[at])
             if at > 0:
                 ref[...] += product
             elif first:
@@ -132,31 +124,28 @@
 
 
 def conv_part(stacked, places, pieces, before, length):
-    points, depth = stacked.shape
+    points, depth = stacked[0].shape
     width = pieces[0][0].shape[1]
     slots = [len(parts) for parts in pieces]
     flat = [piece for parts in pieces for piece in parts]
     return call(
         functools.partial(conv_kernel, slots, before is None),
-        (jax.ShapeDtypeStruct((points // 2, width), F32),) * 2,
-        40,
-        2 * points * length * width * len(slots),
-        2 * length * (points + width) * len(slots),
-        in_specs=[
-            pl.BlockSpec(memory_space=pltpu.SMEM),
-            pl.BlockSpec(memory_space=pl.ANY),
-        ]
-        + [pl.BlockSpec(memory_space=pl.ANY)] * len(flat)
+        (jax.ShapeDtypeStruct((points, width), F32),) * 2,
+        60,
+        4 * points * length * width * len(slots),
+        2 * length * (2 * points + width) * len(slots),
+        in_specs=[pl.BlockSpec(memory_space=pltpu.SMEM)]
+        + [pl.BlockSpec(memory_space=pl.ANY)] * (2 + len(flat))
         + ([] if before is None else [pl.BlockSpec()] * 2),
         input_output_aliases=(
-            {} if before is None else {2 + len(flat): 0, 3 + len(flat): 1}
+            {} if before is None else {3 + len(flat): 0, 4 + len(flat): 1}
         ),
         scratch_shapes=[
-            pltpu.VMEM((len(slots), points, length), BF16),
+            pltpu.VMEM((len(slots), 2, points, length), BF16),
             pltpu.VMEM((len(slots), length, width), BF16),
-            pltpu.SemaphoreType.DMA((len(slots), 3)),
+            pltpu.SemaphoreType.DMA((len(slots), 4)),
         ],
-    )(places.reshape(-1), stacked, *flat, *(before or ()))
+    )(places.reshape(-1), *stacked, *flat, *(before or ()))
 
 
 def mix_kernel(own_ref, got_ref, features_ref, weight_ref, gain_ref, slot_ref, out_ref):
@@ -365,7 +354,6 @@
         on.append(lax.ppermute(second, "blocks", on_pairs))
         return tied[2:]
 
-    (faces,) = pass_on(faces)
     received = exchange_faces(faces.reshape(8, -1, width), devices, index)
     received = pass_on(*received)
     table = jnp.concatenate([ordered, *received], axis=0)
@@ -373,10 +361,10 @@
     other_half = lax.dynamic_slice(table, (0, (1 - core) * half), (table.shape[0], half))
     other_table = lax.ppermute(other_half, "blocks", partner)
     other_neighbours = lax.ppermute(neighbours, "blocks", partner)
-    tables = (padded_taps(other_neighbours), padded_taps(neighbours), other_table, own_table)
-    stacked = gather_part(0, 16, tables, None)
-    (stacked,) = pass_on(stacked)
-    stacked = gather_part(16, TAPS - 16, tables, stacked)
+    own_stacked = gather_block(padded_taps(neighbours), own_table)
+    own_stacked, other_table = pass_on(own_stacked, other_table)
+    other_stacked = gather_block(padded_taps(other_neighbours), other_table)
+    stacked = pass_on(other_stacked, own_stacked)
     if round_trip:
         places = jnp.array(places, jnp.int32)[index]
         early = [[mine], [back[1]], [on[1]], [back[2]], [on[2]]]
@@ -423,7 +411,7 @@
     back = call(
         block_kernel,
         jax.ShapeDtypeStruct((slots, width), BF16),
-        48,
+        28,
         20 * points * width * width,
         16 * width * width,
         scratch_shapes=[

time: 210 us -> 206 us (0.981)
  waiting for transfers between devices: 75.8 us -> 56.5 us
  Pallas kernels: 73.4 us -> 87.4 us
  other arithmetic: 4.24 us -> 7.53 us
  local copies, waits for them, and re-layouts: 19.5 us -> 16.3 us
    ppermute x3, waiting for transfers between devices: 21.2 us -> 0.01 us  [exchange_faces(): got = lax.ppermute(payload, 'blocks', pairs)]
    pallas_call x3, Pallas kernels: 52.1 us -> 60.7 us  [the longest x2 37 us: gather_block(): call(gather_kernel, jax.ShapeDtypeStruct((points, TAPS * half), BF16), 60...]
    pallas_call x3, Pallas kernels: 16.5 us -> 22.1 us  [conv_part(): call(functools.partial(conv_kernel, slots, before is None), (jax.ShapeDty...]
    slice x2, local copies, waits for them, and re-layouts: 2.6 us -> 0.06 us  [pass_on(): first, second = (first[:rows // 2], second[rows // 2:])]
    select_n x3, other arithmetic: 0.05 us -> 2.56 us  [exchange_faces(): received[6 + dy] = jnp.where(lower, zero, got)]
    ppermute x1, starting transfers between devices: 3.22 us -> 0.95 us  [body(): other_table = lax.ppermute(other_half, 'blocks', partner)]
    ppermute x4, waiting for transfers between devices: 5.16 us -> 7.42 us  [pass_on(): back.append(lax.ppermute(first, 'blocks', back_pairs))]
    unnamed x47 -> x55, local copies, waits for them, and re-layouts: 8.72 us -> 8.65 us
  transfers between devices with their start and end apart: 19 -> 19, of which waited for: 9 -> 7; matrix products, arithmetic and copies ran while one was open for 8% -> 8% of each run, Pallas kernels for 19% -> 26%
where the time goes in v5:
time: 206 us; the launch traced here: 205 us
  Pallas kernels  87.4 us (42%)
  waiting for transfers between devices  56.5 us (27%)
  starting transfers between devices  36.9 us (18%)
  local copies, waits for them, and re-layouts  16.3 us (8%)
  other arithmetic  7.53 us (4%)
    pallas_call x2, Pallas kernels, gather_block(): call(gather_kernel, jax.ShapeDtypeStruct((points, TAPS * half), BF16), 60...  37 us
    all_to_all x1, waiting for transfers between devices, body(): lax.all_to_all(back.reshape(devices, capacity, width), 'blocks', split_ax...  24.7 us
    pallas_call x1, Pallas kernels, body(): call(block_kernel, jax.ShapeDtypeStruct((slots, width), BF16), 28, 20 * p...  23.7 us
    pallas_call x3, Pallas kernels, conv_part(): call(functools.partial(conv_kernel, slots, before is None), (jax.ShapeDty...  22.1 us
    all_to_all x1, waiting for transfers between devices, body(): lax.all_to_all(outgoing.reshape(devices, capacity, width), 'blocks', spli...  19.6 us
    ppermute x3, starting transfers between devices, exchange_faces(): got = lax.ppermute(payload, 'blocks', pairs)  9.09 us
    unnamed x55, local copies, waits for them, and re-layouts  8.65 us
    ppermute x4, waiting for transfers between devices, pass_on(): back.append(lax.ppermute(first, 'blocks', back_pairs))  7.42 us
  transfers between devices with their start and end apart: 19, of which 7 were waited for; matrix products, arithmetic and copies ran while one was open for 8% of the time, Pallas kernels for 26%

profile of v5, /device:TPU:9, one launch (start us, length us, event | category | flops | bytes accessed | tf_op | source)
XLA Modules:
  0.0 205.2 jit_solution(15801726318506941797)
XLA Ops:
  0.0 1.1 slice.79
  1.1 0.7 collective-permute-start
  1.8 0.9 reshape.98.rows_ref
  2.7 1.0 copy-done.1
  3.8 0.8 shard_map.145
  4.6 0.7 fusion.6
  5.3 5.1 %collective-permute-start.3 = (bf16[64,512]{1,0:T(8,128)(2,1)}, bf16[64,512]{1,0:T(8,128)(2,1)}, u32[]{:S(2)}, u32[]{:S(2)}) collective-permute-start(bf16[64,512]{1,0:T(8,128)(2,1)} %get-tuple-element.74), channel_id=1, source_target_pairs={{0,9},{1,10},{2,11},{3,12},{4,13},{5,14},{6,15},{8,1},{9,2},{10,3}... | collective-permute-start | bytes 196616 | tf_op jit(solution)/shard_map/ppermute | solution.py:249
  10.5 3.9 %collective-permute-start.1 = (bf16[64,512]{1,0:T(8,128)(2,1)}, bf16[64,512]{1,0:T(8,128)(2,1)}, u32[]{:S(2)}, u32[]{:S(2)}) collective-permute-start(bf16[64,512]{1,0:T(8,128)(2,1)} %get-tuple-element.73), channel_id=1, source_target_pairs={{1,8},{2,9},{3,10},{4,11},{5,12},{6,13},{7,14},{9,0},{10,1},{11,2}... | collective-permute-start | bytes 196616 | tf_op jit(solution)/shard_map/ppermute | solution.py:249
  14.4 0.1 copy.36
  14.5 0.7 collective-permute-start.11
  15.3 0.1 copy.34
  15.5 0.1 copy.35
  15.7 0.7 collective-permute-done.11
  16.4 2.3 %collective-permute-start.4 = (bf16[64,512]{1,0:T(8,128)(2,1)}, bf16[64,512]{1,0:T(8,128)(2,1)S(1)}, u32[]{:S(2)}, u32[]{:S(2)}) collective-permute-start(bf16[64,512]{1,0:T(8,128)(2,1)} %get-tuple-element.72), channel_id=1, source_target_pairs={{1,0},{2,1},{3,2},{4,3},{5,4},{6,5},{7,6},{9,8},{10,9},{11,10},{12... | collective-permute-start | bytes 196616 | tf_op jit(solution)/shard_map/ppermute | solution.py:260
  18.7 0.1 fusion.7
  18.8 1.1 add_convert_fusion.1
  19.9 3.3 %collective-permute-start.5 = (bf16[64,512]{1,0:T(8,128)(2,1)S(1)}, bf16[64,512]{1,0:T(8,128)(2,1)S(1)}, u32[]{:S(2)}, u32[]{:S(2)}) collective-permute-start(bf16[64,512]{1,0:T(8,128)(2,1)S(1)} %get-tuple-element.70), channel_id=1, source_target_pairs={{0,1},{1,2},{2,3},{3,4},{4,5},{5,6},{6,7},{8,9},{9,10},{10,11},{11... | collective-permute-start | bytes 196616 | tf_op jit(solution)/shard_map/ppermute | solution.py:260
  23.2 0.9 broadcast_select_fusion
  24.1 0.9 broadcast_select_fusion.1
  24.9 0.9 broadcast_select_fusion.2
  25.8 1.3 maximum_select_fusion
  27.2 1.5 collective-permute-start.7
  28.7 0.9 constant_dynamic-slice_fusion
  29.6 0.9 collective-permute-start.8
  30.6 18.5 %shard_map.146.own_stacked = bf16[512,6912]{1,0:T(8,128)(2,1)} custom-call(f32[512,128]{1,0:T(8,128)} %get-tuple-element.76.rows_ref, bf16[1024,256]{1,0:T(8,128)(2,1)} %get-tuple-element.69.table_ref), custom_call_target="tpu_custom_call" | custom-call | flops 7247757312 | bytes 7077888 | tf_op jit(solution)/shard_map/pallas_call | solution.py:72
  49.1 0.2 collective-permute-start.10
  49.3 1.3 collective-permute-start.9
  50.6 18.5 %shard_map.147.other_stacked = bf16[512,6912]{1,0:T(8,128)(2,1)} custom-call(f32[512,128]{1,0:T(8,128)} %get-tuple-element.75.rows_ref, bf16[1024,256]{1,0:T(8,128)(2,1)} %copy-done.21), custom_call_target="tpu_custom_call" | custom-call | flops 7247757312 | bytes 7077888 | tf_op jit(solution)/shard_map/pallas_call | solution.py:72
  69.1 1.2 collective-permute-done.10.refs_4_
  70.3 1.1 collective-permute-start.12
  71.4 0.5 collective-permute-start.13
  71.9 0.7 constant_dynamic-slice_fusion.2
  72.6 0.6 reshape.85.places_ref
  73.2 9.4 %shard_map.148 = (f32[512,512]{1,0:T(8,128)}, f32[512,512]{1,0:T(8,128)}) custom-call(s32[10]{0:T(128)} %reshape.85.places_ref, bf16[512,6912]{1,0:T(8,128)(2,1)} %shard_map.147.other_stacked, bf16[512,6912]{1,0:T(8,128)(2,1)} %shard_map.146.own_stacked, bf16[864,512]{1,0:T(8,128)(2,1)} %bitcast.31, bf16[864,512]{1,0:T(8,128)(2,1)} %collective-permute-done.6.refs_1_, ...), custom_call_target="tpu_custom_call" | custom-call | flops 5368709120 | bytes 15728640 | tf_op jit(solution)/shard_map/pallas_call | solution.py:131
  82.6 7.4 %collective-permute-done.12.refs_0_ = bf16[864,512]{1,0:T(8,128)(2,1)S(1)} collective-permute-done((bf16[864,512]{1,0:T(8,128)(2,1)S(1)}, bf16[864,512]{1,0:T(8,128)(2,1)S(1)}, u32[]{:S(2)}, u32[]{:S(2)}) %collective-permute-start.12) | collective-permute-done | bytes 884768 | tf_op jit(solution)/shard_map/ppermute | solution.py:353
  90.0 0.8 collective-permute-done.13.refs_1_
  90.9 0.3 collective-permute-start.14
  91.3 1.2 collective-permute-start.15
  92.5 0.6 reshape.86.places_ref
  93.1 0.6 slice_bitcast_fusion.places_ref
  93.7 6.9 %shard_map.149 = (f32[512,512]{1,0:T(8,128)}, f32[512,512]{1,0:T(8,128)}) custom-call(s32[4]{0:T(128)} %reshape.86.places_ref, bf16[512,6912]{1,0:T(8,128)(2,1)} %shard_map.147.other_stacked, bf16[512,6912]{1,0:T(8,128)(2,1)} %shard_map.146.own_stacked, bf16[864,512]{1,0:T(8,128)(2,1)} %copy-done.10, ...), custom_call_target="tpu_custom_call", output_to_operand_aliasing={{0}: (5, {}), {1}: (6, {})} | custom-call | flops 2147483648 | bytes 6291456 | tf_op jit(solution)/shard_map/pallas_call | solution.py:131
  100.7 0.7 copy-done.14
  101.4 0.2 copy-done.15
  101.6 5.7 %shard_map.150 = (f32[512,512]{1,0:T(8,128)}, f32[512,512]{1,0:T(8,128)}) custom-call(s32[2]{0:T(128)} %slice_bitcast_fusion.places_ref, bf16[512,6912]{1,0:T(8,128)(2,1)} %shard_map.147.other_stacked, bf16[512,6912]{1,0:T(8,128)(2,1)} %shard_map.146.own_stacked, bf16[432,512]{1,0:T(8,128)(2,1)} %copy-done.14, ...), custom_call_target="tpu_custom_call", output_to_operand_aliasing={{0}: (5, {}), {1}: (6, {})} | custom-call | flops 1073741824 | bytes 3145728 | tf_op jit(solution)/shard_map/pallas_call | solution.py:131
  107.3 3.2 %collective-permute-start.16 = (f32[512,512]{1,0:T(8,128)}, f32[512,512]{1,0:T(8,128)S(1)}, u32[]{:S(2)}, u32[]{:S(2)}) collective-permute-start(f32[512,512]{1,0:T(8,128)} %get-tuple-element.64), channel_id=1, source_target_pairs={{0,1},{1,0},{2,3},{3,2},{4,5},{5,4},{6,7},{7,6},{8,9},{9,8},{10,11... | collective-permute-start | bytes 3145736 | tf_op jit(solution)/shard_map/ppermute | solution.py:389
  110.6 0.3 convert_reduce_fusion.1
  110.9 2.1 %collective-permute-done.16.got_ref = f32[512,512]{1,0:T(8,128)S(1)} collective-permute-done((f32[512,512]{1,0:T(8,128)}, f32[512,512]{1,0:T(8,128)S(1)}, u32[]{:S(2)}, u32[]{:S(2)}) %collective-permute-start.16) | collective-permute-done | bytes 1048608 | tf_op jit(solution)/shard_map/ppermute | solution.py:389
  113.1 1.2 copy-done
  114.3 2.3 %shard_map.151 = bf16[1024,512]{1,0:T(8,128)(2,1)} custom-call(f32[512,512]{1,0:T(8,128)S(1)} %copy-done, f32[512,512]{1,0:T(8,128)S(1)} %collective-permute-done.16.got_ref, bf16[512,512]{1,0:T(8,128)(2,1)S(1)} %copy-done.2, bf16[512,512]{1,0:T(8,128)(2,1)S(1)} %copy-done.3, f32[1,512]{1,0:T(1,128)S(1)} %bitcast.24, s32[1,512]{1,0:T(1,128)S(1)} %bitcast.20), custom_call_target="tpu_custom_call" | custom-call | flops 805306368 | bytes 2097152 | tf_op jit(solution)/shard_map/pallas_call | solution.py:391
  116.6 5.5 %all-to-all-start = ((bf16[16,64,512]{2,1,0:T(8,128)(2,1)}), bf16[16,64,512]{2,1,0:T(8,128)(2,1)S(1)}, u32[]{:S(2)}, u32[]{:S(2)}) async-start(bf16[16,64,512]{2,1,0:T(8,128)(2,1)} %bitcast.5), calls=%async_computation | async-start | bytes 2097152 | tf_op jit(solution)/shard_map/all_to_all | solution.py:405
  122.1 1.5 fusion.5
  123.6 1.0 copy.41
  124.7 1.0 copy.42
  125.7 0.2 convert_reduce_fusion
  125.9 0.1 copy.39.slot_col_ref
  126.1 1.3 maximum_bitcast_fusion.qv_ref
  127.4 19.6 %all-to-all-done = bf16[16,64,512]{2,1,0:T(8,128)(2,1)S(1)} async-done(((bf16[16,64,512]{2,1,0:T(8,128)(2,1)}), bf16[16,64,512]{2,1,0:T(8,128)(2,1)S(1)}, u32[]{:S(2)}, u32[]{:S(2)}) %all-to-all-start) | async-done | bytes 1048608 | tf_op jit(solution)/shard_map/all_to_all | solution.py:405
  147.0 1.6 copy-done.5
  148.6 1.6 copy-done.6
  150.1 23.7 %shard_map.152 = bf16[1024,512]{1,0:T(8,128)(2,1)} custom-call(bf16[1024,512]{1,0:T(8,128)(2,1)S(1)} %bitcast.18, s32[512,1]{1,0:T(8,128)S(1)} %copy.39.slot_col_ref, s32[1,512]{1,0:T(1,128)S(1)} %bitcast.23, f32[1,512]{1,0:T(1,128)S(1)} %bitcast.25, bf16[1024,512]{1,0:T(8,128)(2,1)S(1)} %maximum_bitcast_fusion.qv_ref, ...), custom_call_target="tpu_custom_call" | custom-call | flops 2684354560 | bytes 4194304 | tf_op jit(solution)/shard_map/pallas_call | solution.py:411
  173.8 5.0 %all-to-all-start.1 = ((bf16[16,64,512]{2,1,0:T(8,128)(2,1)}), bf16[16,64,512]{2,1,0:T(8,128)(2,1)S(1)}, u32[]{:S(2)}, u32[]{:S(2)}) async-start(bf16[16,64,512]{2,1,0:T(8,128)(2,1)} %bitcast.12), calls=%async_computation.1 | async-start | bytes 2097152 | tf_op jit(solution)/shard_map/all_to_all | solution.py:436
  178.8 0.1 copy.40.slot_ref
  179.0 24.7 %all-to-all-done.1 = bf16[16,64,512]{2,1,0:T(8,128)(2,1)S(1)} async-done(((bf16[16,64,512]{2,1,0:T(8,128)(2,1)}), bf16[16,64,512]{2,1,0:T(8,128)(2,1)S(1)}, u32[]{:S(2)}, u32[]{:S(2)}) %all-to-all-start.1) | async-done | bytes 1048608 | tf_op jit(solution)/shard_map/all_to_all | solution.py:436
  203.7 1.5 shard_map.153
  (73 shorter events, 0.6 us)
Async XLA Ops:
  0.0 14.4 %copy-start.16 = (s32[512,26]{0,1:T(8,128)S(1)}, s32[512,26]{0,1:T(8,128)}, u32[]{:S(2)}) copy-start(s32[512,26]{0,1:T(8,128)} %param.26) | copy-start | bytes 159748
  1.1 24.7 %collective-permute-start = (bf16[13,32,512]{2,1,0:T(8,128)(2,1)S(1)}, bf16[13,32,512]{2,1,0:T(8,128)(2,1)}, u32[]{:S(2)}, u32[]{:S(2)}) collective-permute-start(bf16[13,32,512]{2,1,0:T(8,128)(2,1)S(1)} %slice.79), channel_id=1, source_target_pairs={{0,1},{1,0},{2,3},{3,2},{4,5},{5,4},{6,7},{7,6},{8,9},{9,8},{10,11... | collective-permute-start | bytes 1277960 | tf_op jit(solution)/shard_map/ppermute | solution.py:324
  2.7 1.0 copy-start.1
  3.8 11.5 %copy-start.12 = (bf16[864,512]{1,0:T(8,128)(2,1)S(1)}, bf16[864,512]{1,0:T(8,128)(2,1)}, u32[]{:S(2)}) copy-start(bf16[864,512]{1,0:T(8,128)(2,1)} %param.16) | copy-start | bytes 2654212
  5.3 14.7 %collective-permute-start.3 = (bf16[64,512]{1,0:T(8,128)(2,1)}, bf16[64,512]{1,0:T(8,128)(2,1)}, u32[]{:S(2)}, u32[]{:S(2)}) collective-permute-start(bf16[64,512]{1,0:T(8,128)(2,1)} %get-tuple-element.74), channel_id=1, source_target_pairs={{0,9},{1,10},{2,11},{3,12},{4,13},{5,14},{6,15},{8,1},{9,2},{10,3}... | collective-permute-start | bytes 196616 | tf_op jit(solution)/shard_map/ppermute | solution.py:249
  10.3 13.7 %collective-permute-start.2 = (bf16[64,512]{1,0:T(8,128)(2,1)}, bf16[64,512]{1,0:T(8,128)(2,1)}, u32[]{:S(2)}, u32[]{:S(2)}) collective-permute-start(bf16[64,512]{1,0:T(8,128)(2,1)} %get-tuple-element.71), channel_id=1, source_target_pairs={{0,8},{1,9},{2,10},{3,11},{4,12},{5,13},{6,14},{7,15},{8,0},{9,1},... | collective-permute-start | bytes 196616 | tf_op jit(solution)/shard_map/ppermute | solution.py:249
  10.5 14.5 %collective-permute-start.1 = (bf16[64,512]{1,0:T(8,128)(2,1)}, bf16[64,512]{1,0:T(8,128)(2,1)}, u32[]{:S(2)}, u32[]{:S(2)}) collective-permute-start(bf16[64,512]{1,0:T(8,128)(2,1)} %get-tuple-element.73), channel_id=1, source_target_pairs={{1,8},{2,9},{3,10},{4,11},{5,12},{6,13},{7,14},{9,0},{10,1},{11,2}... | collective-permute-start | bytes 196616 | tf_op jit(solution)/shard_map/ppermute | solution.py:249
  14.5 1.9 collective-permute-start.11
  16.4 10.7 %collective-permute-start.4 = (bf16[64,512]{1,0:T(8,128)(2,1)}, bf16[64,512]{1,0:T(8,128)(2,1)S(1)}, u32[]{:S(2)}, u32[]{:S(2)}) collective-permute-start(bf16[64,512]{1,0:T(8,128)(2,1)} %get-tuple-element.72), channel_id=1, source_target_pairs={{1,0},{2,1},{3,2},{4,3},{5,4},{6,5},{7,6},{9,8},{10,9},{11,10},{12... | collective-permute-start | bytes 196616 | tf_op jit(solution)/shard_map/ppermute | solution.py:260
  19.9 7.2 %collective-permute-start.5 = (bf16[64,512]{1,0:T(8,128)(2,1)S(1)}, bf16[64,512]{1,0:T(8,128)(2,1)S(1)}, u32[]{:S(2)}, u32[]{:S(2)}) collective-permute-start(bf16[64,512]{1,0:T(8,128)(2,1)S(1)} %get-tuple-element.70), channel_id=1, source_target_pairs={{0,1},{1,2},{2,3},{3,4},{4,5},{5,6},{6,7},{8,9},{9,10},{10,11},{11... | collective-permute-start | bytes 196616 | tf_op jit(solution)/shard_map/ppermute | solution.py:260
  27.1 22.0 %copy-start.13 = (bf16[27,32,512]{2,1,0:T(8,128)(2,1)}, bf16[27,32,512]{2,1,0:T(8,128)(2,1)S(1)}, u32[]{:S(2)}) copy-start(bf16[27,32,512]{2,1,0:T(8,128)(2,1)S(1)} %maximum_select_fusion) | copy-start | bytes 2654212
  27.1 21.9 %collective-permute-start.6 = (bf16[864,512]{1,0:T(8,128)(2,1)S(1)}, bf16[864,512]{1,0:T(8,128)(2,1)}, u32[]{:S(2)}, u32[]{:S(2)}) collective-permute-start(bf16[864,512]{1,0:T(8,128)(2,1)S(1)} %bitcast.29), channel_id=1, source_target_pairs={{0,4},{1,5},{4,8},{5,9},{8,12},{9,13},{12,14},{13,15},{14,10},{15,... | collective-permute-start | bytes 2654216 | tf_op jit(solution)/shard_map/ppermute | solution.py:353
  27.2 21.9 %collective-permute-start.7 = (bf16[864,512]{1,0:T(8,128)(2,1)S(1)}, bf16[864,512]{1,0:T(8,128)(2,1)}, u32[]{:S(2)}, u32[]{:S(2)}) collective-permute-start(bf16[864,512]{1,0:T(8,128)(2,1)S(1)} %bitcast.30), channel_id=1, source_target_pairs={{0,2},{1,3},{4,0},{5,1},{8,4},{9,5},{12,8},{13,9},{14,12},{15,13},... | collective-permute-start | bytes 2654216 | tf_op jit(solution)/shard_map/ppermute | solution.py:354
  29.6 19.4 %collective-permute-start.8 = (bf16[1024,256]{1,0:T(8,128)(2,1)S(1)}, bf16[1024,256]{1,0:T(8,128)(2,1)S(1)}, u32[]{:S(2)}, u32[]{:S(2)}) collective-permute-start(bf16[1024,256]{1,0:T(8,128)(2,1)S(1)} %get-tuple-element.68), channel_id=1, source_target_pairs={{0,1},{1,0},{2,3},{3,2},{4,5},{5,4},{6,7},{7,6},{8,9},{9,8},{10,11... | collective-permute-start | bytes 1572872 | tf_op jit(solution)/shard_map/ppermute | solution.py:362
  49.0 1.5 copy-start.21
  49.1 21.2 %collective-permute-start.10 = (bf16[864,512]{1,0:T(8,128)(2,1)}, bf16[864,512]{1,0:T(8,128)(2,1)S(1)}, u32[]{:S(2)}, u32[]{:S(2)}) collective-permute-start(bf16[864,512]{1,0:T(8,128)(2,1)} %collective-permute-done.7.refs_2_), channel_id=1, source_target_pairs={{0,2},{1,3},{4,0},{5,1},{8,4},{9,5},{12,8},{13,9},{14,12},{15,13},... | collective-permute-start | bytes 2654216 | tf_op jit(solution)/shard_map/ppermute | solution.py:354
  49.3 21.0 %collective-permute-start.9 = (bf16[864,512]{1,0:T(8,128)(2,1)}, bf16[864,512]{1,0:T(8,128)(2,1)S(1)}, u32[]{:S(2)}, u32[]{:S(2)}) collective-permute-start(bf16[864,512]{1,0:T(8,128)(2,1)} %collective-permute-done.6.refs_1_), channel_id=1, source_target_pairs={{0,4},{1,5},{4,8},{5,9},{8,12},{9,13},{12,14},{13,15},{14,10},{15,... | collective-permute-start | bytes 2654216 | tf_op jit(solution)/shard_map/ppermute | solution.py:353
  70.3 2.9 %copy-start.19 = (bf16[864,512]{1,0:T(8,128)(2,1)}, bf16[864,512]{1,0:T(8,128)(2,1)S(1)}, u32[]{:S(2)}) copy-start(bf16[864,512]{1,0:T(8,128)(2,1)S(1)} %collective-permute-done.10.refs_4_) | copy-start | bytes 2654212
  70.3 2.9 %copy-start.20 = (bf16[864,512]{1,0:T(8,128)(2,1)}, bf16[864,512]{1,0:T(8,128)(2,1)S(1)}, u32[]{:S(2)}) copy-start(bf16[864,512]{1,0:T(8,128)(2,1)S(1)} %collective-permute-done.9.refs_3_) | copy-start | bytes 2654212
  70.3 19.7 %collective-permute-start.12 = (bf16[864,512]{1,0:T(8,128)(2,1)S(1)}, bf16[864,512]{1,0:T(8,128)(2,1)S(1)}, u32[]{:S(2)}, u32[]{:S(2)}) collective-permute-start(bf16[864,512]{1,0:T(8,128)(2,1)S(1)} %collective-permute-done.9.refs_3_), channel_id=1, source_target_pairs={{0,4},{1,5},{4,8},{5,9},{8,12},{9,13},{12,14},{13,15},{14,10},{15,... | collective-permute-start | bytes 2654216 | tf_op jit(solution)/shard_map/ppermute | solution.py:353
  71.4 19.4 %collective-permute-start.13 = (bf16[864,512]{1,0:T(8,128)(2,1)S(1)}, bf16[864,512]{1,0:T(8,128)(2,1)S(1)}, u32[]{:S(2)}, u32[]{:S(2)}) collective-permute-start(bf16[864,512]{1,0:T(8,128)(2,1)S(1)} %collective-permute-done.10.refs_4_), channel_id=1, source_target_pairs={{0,2},{1,3},{4,0},{5,1},{8,4},{9,5},{12,8},{13,9},{14,12},{15,13},... | collective-permute-start | bytes 2654216 | tf_op jit(solution)/shard_map/ppermute | solution.py:354
  90.0 3.7 %copy-start.10 = (bf16[864,512]{1,0:T(8,128)(2,1)}, bf16[864,512]{1,0:T(8,128)(2,1)S(1)}, u32[]{:S(2)}) copy-start(bf16[864,512]{1,0:T(8,128)(2,1)S(1)} %collective-permute-done.12.refs_0_) | copy-start | bytes 2654212
  90.9 2.8 %copy-start.11 = (bf16[864,512]{1,0:T(8,128)(2,1)}, bf16[864,512]{1,0:T(8,128)(2,1)S(1)}, u32[]{:S(2)}) copy-start(bf16[864,512]{1,0:T(8,128)(2,1)S(1)} %collective-permute-done.13.refs_1_) | copy-start | bytes 2654212
  90.9 9.7 %collective-permute-start.14 = (bf16[432,512]{1,0:T(8,128)(2,1)S(1)}, bf16[432,512]{1,0:T(8,128)(2,1)S(1)}, u32[]{:S(2)}, u32[]{:S(2)}) collective-permute-start(bf16[432,512]{1,0:T(8,128)(2,1)S(1)} %slice.93), channel_id=1, source_target_pairs={{0,4},{1,5},{4,8},{5,9},{8,12},{9,13},{12,14},{13,15},{14,10},{15,... | collective-permute-start | bytes 1327112 | tf_op jit(solution)/shard_map/ppermute | solution.py:353
  91.3 9.4 %collective-permute-start.15 = (bf16[432,512]{1,0:T(8,128)(2,1)S(1)}, bf16[432,512]{1,0:T(8,128)(2,1)S(1)}, u32[]{:S(2)}, u32[]{:S(2)}) collective-permute-start(bf16[432,512]{1,0:T(8,128)(2,1)S(1)} %slice.94), channel_id=1, source_target_pairs={{0,2},{1,3},{4,0},{5,1},{8,4},{9,5},{12,8},{13,9},{14,12},{15,13},... | collective-permute-start | bytes 1327112 | tf_op jit(solution)/shard_map/ppermute | solution.py:354
  100.7 0.8 copy-start.14
  100.7 0.9 copy-start.15
  101.6 9.0 %copy-start.17 = (s32[512]{0:T(512)S(1)}, s32[512]{0:T(512)}, u32[]{:S(2)}) copy-start(s32[512]{0:T(512)} %param.27) | copy-start | bytes 6148
  101.6 11.5 %copy-start.2 = (bf16[512,512]{1,0:T(8,128)(2,1)S(1)}, bf16[512,512]{1,0:T(8,128)(2,1)}, u32[]{:S(2)}) copy-start(bf16[512,512]{1,0:T(8,128)(2,1)} %features_ref.3) | copy-start | bytes 1572868
  101.6 11.5 %copy-start.3 = (bf16[512,512]{1,0:T(8,128)(2,1)S(1)}, bf16[512,512]{1,0:T(8,128)(2,1)}, u32[]{:S(2)}) copy-start(bf16[512,512]{1,0:T(8,128)(2,1)} %weight_ref.1) | copy-start | bytes 1572868
  101.6 11.5 %copy-start.4 = (f32[512]{0:T(512)S(1)}, f32[512]{0:T(512)}, u32[]{:S(2)}) copy-start(f32[512]{0:T(512)} %param.18) | copy-start | bytes 6148
  107.3 5.7 %collective-permute-start.16 = (f32[512,512]{1,0:T(8,128)}, f32[512,512]{1,0:T(8,128)S(1)}, u32[]{:S(2)}, u32[]{:S(2)}) collective-permute-start(f32[512,512]{1,0:T(8,128)} %get-tuple-element.64), channel_id=1, source_target_pairs={{0,1},{1,0},{2,3},{3,2},{4,5},{5,4},{6,7},{7,6},{8,9},{9,8},{10,11... | collective-permute-start | bytes 3145736 | tf_op jit(solution)/shard_map/ppermute | solution.py:389
  113.1 1.2 copy-start
  116.6 30.3 %all-to-all-start = ((bf16[16,64,512]{2,1,0:T(8,128)(2,1)}), bf16[16,64,512]{2,1,0:T(8,128)(2,1)S(1)}, u32[]{:S(2)}, u32[]{:S(2)}) async-start(bf16[16,64,512]{2,1,0:T(8,128)(2,1)} %bitcast.5), calls=%async_computation | async-start | bytes 2097152 | tf_op jit(solution)/shard_map/all_to_all | solution.py:405
  122.1 3.6 %copy-start.18 = (s32[512]{0:T(512)S(1)}, s32[512]{0:T(512)}, u32[]{:S(2)}) copy-start(s32[512]{0:T(512)} %param.28) | copy-start | bytes 6148
  123.6 23.4 %copy-start.7 = (bf16[512,512]{1,0:T(8,128)(2,1)S(1)}, bf16[512,512]{1,0:T(8,128)(2,1)}, u32[]{:S(2)}) copy-start(bf16[512,512]{1,0:T(8,128)(2,1)} %proj_ref.1) | copy-start | bytes 1572868
  123.6 23.4 %copy-start.8 = (f32[512]{0:T(512)S(1)}, f32[512]{0:T(512)}, u32[]{:S(2)}) copy-start(f32[512]{0:T(512)} %param.19) | copy-start | bytes 6148
  123.6 23.3 %copy-start.9 = (f32[512]{0:T(512)S(1)}, f32[512]{0:T(512)}, u32[]{:S(2)}) copy-start(f32[512]{0:T(512)} %param.22) | copy-start | bytes 6148
  147.0 1.6 copy-start.5
  148.6 1.6 copy-start.6
  173.8 29.8 %all-to-all-start.1 = ((bf16[16,64,512]{2,1,0:T(8,128)(2,1)}), bf16[16,64,512]{2,1,0:T(8,128)(2,1)S(1)}, u32[]{:S(2)}, u32[]{:S(2)}) async-start(bf16[16,64,512]{2,1,0:T(8,128)(2,1)} %bitcast.12), calls=%async_computation.1 | async-start | bytes 2097152 | tf_op jit(solution)/shard_map/all_to_all | solution.py:436

commit v6 on v5

--- a/solution.py
+++ b/solution.py
@@ -45,7 +45,7 @@
     )
 
 
-def faces_kernel(unit, features_ref, rows_ref, ordered_ref, faces_ref):
+def faces_kernel(unit, features_ref, rows_ref, ordered_ref, *face_refs):
     points, width = features_ref.shape
     half = width // 2
     place = lax.broadcasted_iota(jnp.int32, (width, width), 1)
@@ -55,44 +55,54 @@
     ordered = dot(features_ref[...], one_hot(channel == source)).astype(BF16)
     ordered_ref[...] = ordered
     row_ids = lax.broadcasted_iota(jnp.int32, (rows_ref.shape[0], points), 1)
-    faces_ref[...] = dot(one_hot(rows_ref[...] == row_ids), ordered).astype(BF16)
-
-
-def gather_kernel(rows_ref, table_ref, out_ref):
-    chosen = lax.broadcasted_iota(jnp.int32, rows_ref.shape, 1) == pl.program_id(0)
+    rows = dot(one_hot(rows_ref[...] == row_ids), ordered).astype(BF16)
+    size = rows.shape[0] // len(face_refs)
+    for at, ref in enumerate(face_refs):
+        ref[...] = rows[at * size : (at + 1) * size]
+
+
+def gather_kernel(taps, rows_ref, table_ref, out_ref):
+    half = table_ref.shape[1]
+    lane = lax.broadcasted_iota(jnp.int32, rows_ref.shape, 1)
     row_ids = lax.broadcasted_iota(jnp.int32, (1, table_ref.shape[0]), 1).astype(F32)
-    column = jnp.sum(jnp.where(chosen, rows_ref[...], 0.0), axis=1, keepdims=True)
-    out_ref[...] = dot(one_hot(column == row_ids), table_ref[...]).astype(BF16)
+    for at in range(taps):
+        chosen = lane == taps * pl.program_id(0) + at
+        column = jnp.sum(jnp.where(chosen, rows_ref[...], 0.0), axis=1, keepdims=True)
+        taken = dot(one_hot(column == row_ids), table_ref[...]).astype(BF16)
+        out_ref[:, at * half : (at + 1) * half] = taken
 
 
 def gather_block(rows, table):
     points, lanes = rows.shape
     height, half = table.shape
-    whole = lambda tap: (0, 0)
+    taps = 3
+    whole = lambda step: (0, 0)
     return call(
-        gather_kernel,
+        functools.partial(gather_kernel, taps),
         jax.ShapeDtypeStruct((points, TAPS * half), BF16),
         60,
         2 * TAPS * points * height * half,
         2 * TAPS * points * half,
-        grid=(TAPS,),
+        grid=(TAPS // taps,),
         in_specs=[pl.BlockSpec((points, lanes), whole), pl.BlockSpec((height, half), whole)],
-        out_specs=pl.BlockSpec((points, half), lambda tap: (0, tap)),
+        out_specs=pl.BlockSpec((points, taps * half), lambda step: (0, step)),
     )(rows, table)
 
 
-def conv_kernel(slots, first, places_ref, other_stacked, own_stacked, *refs):
-    pieces = refs[: sum(slots)]
-    other_ref, own_ref, lhs, held, sems = refs[-5:]
+def conv_kernel(slots, blocks, first, places_ref, *refs):
+    stacked, refs = refs[:blocks], refs[blocks:]
+    pieces, refs = refs[: sum(slots)], refs[sum(slots) :]
+    before = [] if first else refs[:blocks]
+    outs, (lhs, held, sems) = refs[-3 - blocks : -3], refs[-3:]
     length = held.shape[1]
     copies, taken = [], 0
     for at, count in enumerate(slots):
         column = pl.multiple_of(places_ref[2 * at], 128)
         row = pl.multiple_of(places_ref[2 * at + 1], 16)
         copies.append([])
-        for half, stacked in enumerate((other_stacked, own_stacked)):
+        for block in range(blocks):
             copy = pltpu.make_async_copy(
-                stacked.at[:, pl.ds(column, length)], lhs.at[at, half], sems.at[at, half]
+                stacked[block].at[:, pl.ds(column, length)], lhs.at[at, block], sems.at[at, block]
             )
             copy.start()
             copies[-1].append(copy)
@@ -113,14 +123,14 @@
     for at in range(len(slots)):
         for copy in copies[at]:
             copy.wait()
-        for half, ref in enumerate((other_ref, own_ref)):
-            product = dot(lhs[at, half], held[at])
+        for block, ref in enumerate(outs):
+            product = dot(lhs[at, block], held[at])
             if at > 0:
                 ref[...] += product
             elif first:
                 ref[...] = product
             else:
-                ref[...] = refs[half - 7][...] + product
+                ref[...] = before[block][...] + product
 
 
 def conv_part(stacked, places, pieces, before, length):
@@ -128,20 +138,22 @@
     width = pieces[0][0].shape[1]
     slots = [len(parts) for parts in pieces]
     flat = [piece for parts in pieces for piece in parts]
+    blocks = len(stacked)
+    held = 1 + blocks + len(flat)
     return call(
-        functools.partial(conv_kernel, slots, before is None),
-        (jax.ShapeDtypeStruct((points, width), F32),) * 2,
+        functools.partial(conv_kernel, slots, blocks, before is None),
+        [jax.ShapeDtypeStruct((points, width), F32)] * blocks,
         60,
-        4 * points * length * width * len(slots),
-        2 * length * (2 * points + width) * len(slots),
+        2 * blocks * points * length * width * len(slots),
+        2 * length * (blocks * points + width) * len(slots),
         in_specs=[pl.BlockSpec(memory_space=pltpu.SMEM)]
-        + [pl.BlockSpec(memory_space=pl.ANY)] * (2 + len(flat))
-        + ([] if before is None else [pl.BlockSpec()] * 2),
+        + [pl.BlockSpec(memory_space=pl.ANY)] * (held - 1)
+        + ([] if before is None else [pl.BlockSpec()] * blocks),
         input_output_aliases=(
-            {} if before is None else {3 + len(flat): 0, 4 + len(flat): 1}
+            {} if before is None else {held + block: block for block in range(blocks)}
         ),
         scratch_shapes=[
-            pltpu.VMEM((len(slots), 2, points, length), BF16),
+            pltpu.VMEM((len(slots), blocks, points, length), BF16),
             pltpu.VMEM((len(slots), length, width), BF16),
             pltpu.SemaphoreType.DMA((len(slots), 4)),
         ],
@@ -161,26 +173,42 @@
     slot_col_ref,
     slot_row_ref,
     attn_gain_ref,
+    mlp_gain_ref,
+    qv_hbm,
+    key_hbm,
+    proj_hbm,
+    up_hbm,
+    down_hbm,
+    out_ref,
     qv_ref,
     key_ref,
     proj_ref,
-    mlp_gain_ref,
     up_ref,
     down_ref,
-    out_ref,
+    sems,
     serial_ref,
     qv_cols_ref,
     keys_ref,
     heads_ref,
     total_ref,
 ):
+    sources = (key_hbm, qv_hbm, proj_hbm, up_hbm, down_hbm)
+    targets = (key_ref, qv_ref, proj_ref, up_ref, down_ref)
+    copies = [
+        pltpu.make_async_copy(source, target, sems.at[at])
+        for at, (source, target) in enumerate(zip(sources, targets))
+    ]
+    for copy in copies:
+        copy.start()
     slots = arrived_ref.shape[0]
     points, width = serial_ref.shape
     slot_ids = lax.broadcasted_iota(jnp.int32, (points, slots), 1)
     serial = dot(one_hot(slot_col_ref[...] == slot_ids), arrived_ref[...])
     serial_ref[...] = serial
     normed = layer_norm(serial, attn_gain_ref[...]).astype(BF16)
+    copies[0].wait()
     keys_ref[...] = dot(normed, key_ref[...]).astype(BF16)
+    copies[1].wait()
     factor = math.log2(math.e) / math.sqrt(HD)
     contract_last = (((1,), (1,)), ((), ()))
     qv_cols_ref[:width] = (
@@ -207,8 +235,10 @@
             heads_ref[pl.ds(at, HD)] = (sums[:HD] / sums[HD : HD + 1]).astype(BF16)
             return carry
 
-        lax.fori_loop(0, per_group, attend, 0, unroll=2)
-
+        lax.fori_loop(0, per_group, attend, 0, unroll=4)
+
+    for copy in copies[2:]:
+        copy.wait()
     update = lax.dot_general(
         heads_ref[...], proj_ref[...], (((0,), (0,)), ((), ())), preferred_element_type=F32
     )
@@ -230,34 +260,29 @@
     out_ref[...] = dot(one_hot(slot_ref[...] == slot_ids), arrived_ref[...]).astype(BF16)
 
 
-def exchange_faces(faces, devices, index):
-    zero = jnp.zeros_like(faces[0])
-    received = [zero] * 8
-
-    def valid(source, dx, dy):
-        return 0 <= source // GY + dx < devices // GY and 0 <= source % GY + dy < GY
-
-    if devices == 2 * GY:
-        lower = index < GY
-        for dy in (-1, 0, 1):
-            payload = jnp.where(lower, faces[6 + dy], faces[1 + dy])
-            pairs = []
-            for source in range(devices):
-                dx = 1 if source < GY else -1
-                if valid(source, dx, dy):
-                    pairs.append((source, source + dx * GY + dy))
-            got = lax.ppermute(payload, "blocks", pairs)
-            received[1 + dy] = jnp.where(lower, got, zero)
-            received[6 + dy] = jnp.where(lower, zero, got)
-        rest = (3, 4)
-    else:
-        rest = range(8)
-    for facing in rest:
-        dx, dy = STEPS_X[facing], STEPS_Y[facing]
-        pairs = [
-            (source, source + dx * GY + dy) for source in range(devices) if valid(source, dx, dy)
+def face_routes(devices):
+    def pairs(dx, dy):
+        return [
+            (source, source + dx * GY + dy)
+            for source in range(devices)
+            if 0 <= source // GY + dx < devices // GY and 0 <= source % GY + dy < GY
         ]
-        received[facing] = lax.ppermute(faces[facing], "blocks", pairs)
+
+    if devices != 2 * GY:
+        return [(k, k, pairs(STEPS_X[k], STEPS_Y[k])) for k in range(8)]
+    both = [(6 + dy, 1 + dy, pairs(1, dy) + pairs(-1, dy)) for dy in (-1, 0, 1)]
+    return both + [(k, k, pairs(0, STEPS_Y[k])) for k in (3, 4)]
+
+
+def received_faces(routes, got, lower):
+    received = [None] * 8
+    for (first, second, _), rows in zip(routes, got):
+        if first == second:
+            received[first] = rows
+        else:
+            zero = jnp.zeros_like(rows)
+            received[first] = jnp.where(lower, zero, rows)
+            received[second] = jnp.where(lower, rows, zero)
     return received
 
 
@@ -325,17 +350,22 @@
     mine = jnp.where(
         core == 0, jnp.concatenate([kept, got]), jnp.concatenate([got, kept])
     ).reshape(TAPS * unit, width)
-    face_list = face_rows.reshape(-1, 1)
-    ordered, faces = call(
+    lower = index < GY
+    routes = face_routes(devices)
+    lists = [jnp.where(lower, face_rows[0, first], face_rows[0, second]) for first, second, _ in routes]
+    face_list = jnp.concatenate(lists).reshape(-1, 1)
+    ordered, *faces = call(
         functools.partial(faces_kernel, unit),
-        (
-            jax.ShapeDtypeStruct((points, width), BF16),
-            jax.ShapeDtypeStruct((face_list.shape[0], width), BF16),
-        ),
+        [jax.ShapeDtypeStruct((points, width), BF16)]
+        + [jax.ShapeDtypeStruct((face_rows.shape[2], width), BF16)] * len(routes),
         32,
         4 * points * width * width,
         8 * points * width,
     )(features, face_list)
+    faces = [
+        lax.ppermute(rows, "blocks", pairs) for rows, (_, _, pairs) in zip(faces, routes)
+    ]
+
     round_trip = devices == 16
     rows = mine.shape[0]
     length = -(-(rows + 127) // 128) * 128 if round_trip else rows * (devices // 2)
@@ -354,8 +384,8 @@
         on.append(lax.ppermute(second, "blocks", on_pairs))
         return tied[2:]
 
-    received = exchange_faces(faces.reshape(8, -1, width), devices, index)
-    received = pass_on(*received)
+    neighbours, *faces = pass_on(neighbours, *faces)
+    received = received_faces(routes, faces, lower)
     table = jnp.concatenate([ordered, *received], axis=0)
     own_table = lax.dynamic_slice(table, (0, core * half), (table.shape[0], half))
     other_half = lax.dynamic_slice(table, (0, (1 - core) * half), (table.shape[0], half))
@@ -371,12 +401,14 @@
         sums = conv_part(stacked, places[:5], early, None, length)
         sums = pass_on(*sums)
         sums = conv_part(stacked, places[5:7], [[back[3]], [on[3]]], sums, length)
-        sums = conv_part(stacked, places[7:], [[back[4], on[4]]], sums, length)
+        last = [[back[4], on[4]]]
+        (for_partner,) = conv_part(stacked[:1], places[7:], last, sums[:1], length)
+        (own_part,) = conv_part(stacked[1:], places[7:], last, sums[1:], length)
     else:
         groups = [list(range(first, devices, 2)) for first in range(2)]
         weight = lax.all_gather(mine, "blocks", axis=0, tiled=True, axis_index_groups=groups)
-        sums = conv_part(stacked, jnp.zeros((1, 2), jnp.int32), [[weight]], None, length)
-    for_partner, own_part = sums
+        nowhere = jnp.zeros((1, 2), jnp.int32)
+        for_partner, own_part = conv_part(stacked, nowhere, [[weight]], None, length)
 
     positions = jnp.arange(points, dtype=jnp.int32)
     target = serial_rank // points
@@ -408,13 +440,17 @@
 
     key_weight = qkv_weight[:, width : 2 * width]
     qv_weight = jnp.concatenate([qkv_weight[:, :width], qkv_weight[:, 2 * width :]], axis=1).T
+    weights = (qv_weight, key_weight, proj_weight, up_weight, down_weight)
     back = call(
         block_kernel,
         jax.ShapeDtypeStruct((slots, width), BF16),
-        28,
+        60,
         20 * points * width * width,
         16 * width * width,
-        scratch_shapes=[
+        in_specs=[pl.BlockSpec()] * 5 + [pl.BlockSpec(memory_space=pl.ANY)] * len(weights),
+        scratch_shapes=[pltpu.VMEM(weight.shape, BF16) for weight in weights]
+        + [
+            pltpu.SemaphoreType.DMA((len(weights),)),
             pltpu.VMEM((points, width), F32),
             pltpu.VMEM((2 * width, points), BF16),
             pltpu.VMEM((points, width), BF16),
@@ -426,12 +462,8 @@
         in_slot.reshape(points, 1),
         in_slot.reshape(1, points),
         attn_gain.reshape(1, width),
-        qv_weight,
-        key_weight,
-        proj_weight,
         mlp_gain.reshape(1, width),
-        up_weight,
-        down_weight,
+        *weights,
     )
     returned = lax.all_to_all(
         back.reshape(devices, capacity, width), "blocks", split_axis=0, concat_axis=0, tiled=True

time: 206 us -> 207 us (level)
  waiting for transfers between devices: 56.5 us -> 67.5 us
  Pallas kernels: 87.4 us -> 77 us
  local copies, waits for them, and re-layouts: 16.3 us -> 14.2 us
    pallas_call x7 -> x8, Pallas kernels: 83.5 us -> 73.1 us  [the longest x4 25.3 us: conv_part(): call(functools.partial(conv_kernel, slots, blocks, before is None), [jax....]
    ppermute x4, waiting for transfers between devices: 2.03 us -> 8.22 us  [pass_on(): on.append(lax.ppermute(second, 'blocks', on_pairs))]
    ppermute x4, waiting for transfers between devices: 7.42 us -> 13.2 us  [pass_on(): back.append(lax.ppermute(first, 'blocks', back_pairs))]
    unnamed x55 -> x49, local copies, waits for them, and re-layouts: 8.65 us -> 5.24 us
    unnamed x0 -> x5, other arithmetic: none -> 2.63 us
    select_n x3 -> x0, other arithmetic: 2.56 us -> none  [exchange_faces(): received[6 + dy] = jnp.where(lower, zero, got)]
    ppermute x1, waiting for transfers between devices: 2.12 us -> 0.01 us  [body(): from_partner = lax.ppermute(for_partner, 'blocks', partner)]
  transfers between devices with their start and end apart: 19 -> 19, of which waited for: 7 -> 8; matrix products, arithmetic and copies ran while one was open for 8% -> 6% of each run, Pallas kernels for 26% -> 22%
where the time goes in v6:
time: 207 us; the launch traced here: 206 us
  Pallas kernels  77 us (37%)
  waiting for transfers between devices  67.5 us (33%)
  starting transfers between devices  38.9 us (19%)
  local copies, waits for them, and re-layouts  14.2 us (7%)
  other arithmetic  7.68 us (4%)
    pallas_call x4, Pallas kernels, conv_part(): call(functools.partial(conv_kernel, slots, blocks, before is None), [jax....  25.3 us
    all_to_all x1, waiting for transfers between devices, body(): lax.all_to_all(back.reshape(devices, capacity, width), 'blocks', split_ax...  24.7 us
    pallas_call x1, Pallas kernels, body(): call(block_kernel, jax.ShapeDtypeStruct((slots, width), BF16), 60, 20 * p...  24.2 us
    pallas_call x2, Pallas kernels, gather_block(): call(functools.partial(gather_kernel, taps), jax.ShapeDtypeStruct((points...  22.9 us
    all_to_all x1, waiting for transfers between devices, body(): lax.all_to_all(outgoing.reshape(devices, capacity, width), 'blocks', spli...  21.4 us
    ppermute x5, starting transfers between devices, body(): lax.ppermute(rows, 'blocks', pairs)  15.6 us
    ppermute x4, waiting for transfers between devices, pass_on(): back.append(lax.ppermute(first, 'blocks', back_pairs))  13.2 us
    ppermute x4, waiting for transfers between devices, pass_on(): on.append(lax.ppermute(second, 'blocks', on_pairs))  8.22 us
  transfers between devices with their start and end apart: 19, of which 8 were waited for; matrix products, arithmetic and copies ran while one was open for 6% of the time, Pallas kernels for 22%

profile of v6, /device:TPU:9, one launch (start us, length us, event | category | flops | bytes accessed | tf_op | source)
XLA Modules:
  0.0 205.8 jit_solution(16880950279168850939)
XLA Ops:
  0.0 1.1 slice.74
  1.1 0.7 collective-permute-start
  1.9 1.0 slice_bitcast_fusion
  3.0 1.0 copy-done.1
  4.1 0.7 shard_map.145
  4.8 4.1 %collective-permute-start.1 = (bf16[64,512]{1,0:T(8,128)(2,1)S(1)}, bf16[64,512]{1,0:T(8,128)(2,1)S(1)}, u32[]{:S(2)}, u32[]{:S(2)}) collective-permute-start(bf16[64,512]{1,0:T(8,128)(2,1)S(1)} %get-tuple-element.35), channel_id=1, source_target_pairs={{1,8},{2,9},{3,10},{4,11},{5,12},{6,13},{7,14},{9,0},{10,1},{11,2}... | collective-permute-start | bytes 196616 | tf_op jit(solution)/shard_map/ppermute | solution.py:366
  8.9 0.2 collective-permute-start.2
  9.1 5.7 %collective-permute-start.3 = (bf16[64,512]{1,0:T(8,128)(2,1)S(1)}, bf16[64,512]{1,0:T(8,128)(2,1)S(1)}, u32[]{:S(2)}, u32[]{:S(2)}) collective-permute-start(bf16[64,512]{1,0:T(8,128)(2,1)S(1)} %get-tuple-element.37), channel_id=1, source_target_pairs={{0,9},{1,10},{2,11},{3,12},{4,13},{5,14},{6,15},{8,1},{9,2},{10,3}... | collective-permute-start | bytes 196616 | tf_op jit(solution)/shard_map/ppermute | solution.py:366
  14.8 1.9 collective-permute-start.4
  16.9 3.6 %collective-permute-start.5 = (bf16[64,512]{1,0:T(8,128)(2,1)S(1)}, bf16[64,512]{1,0:T(8,128)(2,1)S(1)}, u32[]{:S(2)}, u32[]{:S(2)}) collective-permute-start(bf16[64,512]{1,0:T(8,128)(2,1)S(1)} %get-tuple-element.39), channel_id=1, source_target_pairs={{0,1},{1,2},{2,3},{3,4},{4,5},{5,6},{6,7},{8,9},{9,10},{10,11},{11... | collective-permute-start | bytes 196616 | tf_op jit(solution)/shard_map/ppermute | solution.py:366
  20.6 1.3 maximum_select_fusion
  22.0 0.6 copy-done.12
  22.7 1.0 copy.36
  23.7 0.9 fusion.10
  24.5 0.9 select_dynamic-update-slice_fusion.5
  25.4 0.9 select_dynamic-update-slice_fusion.4
  26.3 0.9 select_dynamic-update-slice_fusion.3
  27.1 0.8 constant_dynamic-update-slice_fusion.1
  28.1 2.3 %collective-permute-start.11 = (s32[512,26]{1,0:T(8,128)S(1)}, s32[512,26]{1,0:T(8,128)S(1)}, u32[]{:S(2)}, u32[]{:S(2)}) collective-permute-start(s32[512,26]{1,0:T(8,128)S(1)} %copy.36), channel_id=1, source_target_pairs={{0,1},{1,0},{2,3},{3,2},{4,5},{5,4},{6,7},{7,6},{8,9},{9,8},{10,11... | collective-permute-start | bytes 159752 | tf_op jit(solution)/shard_map/ppermute | solution.py:393
  30.4 0.9 constant_dynamic-slice_fusion
  31.3 0.1 copy.34
  31.4 0.1 copy.35
  31.7 1.4 collective-permute-start.7
  33.4 1.1 add_convert_fusion.1
  34.4 11.5 %shard_map.146.refs_1_.refs_0_ = bf16[512,6912]{1,0:T(8,128)(2,1)} custom-call(f32[512,128]{1,0:T(8,128)} %get-tuple-element.71.rows_ref, bf16[1024,256]{1,0:T(8,128)(2,1)} %get-tuple-element.69.table_ref), custom_call_target="tpu_custom_call" | custom-call | flops 7247757312 | bytes 7077888 | tf_op jit(solution)/shard_map/pallas_call | solution.py:80
  45.9 6.7 %collective-permute-done.6.refs_3_ = bf16[864,512]{1,0:T(8,128)(2,1)S(1)} collective-permute-done((bf16[864,512]{1,0:T(8,128)(2,1)S(1)}, bf16[864,512]{1,0:T(8,128)(2,1)S(1)}, u32[]{:S(2)}, u32[]{:S(2)}) %collective-permute-start.6) | collective-permute-done | bytes 884768 | tf_op jit(solution)/shard_map/ppermute | solution.py:383
  52.6 0.1 collective-permute-done.7.refs_4_
  52.8 1.0 collective-permute-start.10
  53.7 0.5 collective-permute-start.9
  54.2 11.5 %shard_map.147.refs_0_ = bf16[512,6912]{1,0:T(8,128)(2,1)} custom-call(f32[512,128]{1,0:T(8,128)} %get-tuple-element.70.rows_ref, bf16[1024,256]{1,0:T(8,128)(2,1)} %copy-done.21), custom_call_target="tpu_custom_call" | custom-call | flops 7247757312 | bytes 7077888 | tf_op jit(solution)/shard_map/pallas_call | solution.py:80
  65.7 7.3 %collective-permute-done.10.refs_6_ = bf16[864,512]{1,0:T(8,128)(2,1)S(1)} collective-permute-done((bf16[864,512]{1,0:T(8,128)(2,1)}, bf16[864,512]{1,0:T(8,128)(2,1)S(1)}, u32[]{:S(2)}, u32[]{:S(2)}) %collective-permute-start.10) | collective-permute-done | bytes 884768 | tf_op jit(solution)/shard_map/ppermute | solution.py:384
  73.1 0.9 collective-permute-start.12
  74.0 0.6 collective-permute-start.13
  74.6 0.7 constant_dynamic-slice_fusion.2
  75.3 0.6 reshape.75.places_ref
  75.9 9.4 %shard_map.148 = (f32[512,512]{1,0:T(8,128)}, f32[512,512]{1,0:T(8,128)}) custom-call(s32[10]{0:T(128)} %reshape.75.places_ref, bf16[512,6912]{1,0:T(8,128)(2,1)} %shard_map.147.refs_0_, bf16[512,6912]{1,0:T(8,128)(2,1)} %shard_map.146.refs_1_.refs_0_, bf16[864,512]{1,0:T(8,128)(2,1)} %bitcast.37, bf16[864,512]{1,0:T(8,128)(2,1)} %copy-done.19, ...), custom_call_target="tpu_custom_call" | custom-call | flops 5368709120 | bytes 15728640 | tf_op jit(solution)/shard_map/pallas_call | solution.py:143
  85.3 6.4 %collective-permute-done.12.refs_2_ = bf16[864,512]{1,0:T(8,128)(2,1)S(1)} collective-permute-done((bf16[864,512]{1,0:T(8,128)(2,1)}, bf16[864,512]{1,0:T(8,128)(2,1)S(1)}, u32[]{:S(2)}, u32[]{:S(2)}) %collective-permute-start.12) | collective-permute-done | bytes 884768 | tf_op jit(solution)/shard_map/ppermute | solution.py:383
  91.7 0.8 collective-permute-done.13.refs_3_
  92.5 0.5 collective-permute-start.14
  93.0 1.0 collective-permute-start.15
  94.1 0.6 reshape.76.places_ref
  94.7 0.6 slice_bitcast_fusion.2.places_ref
  95.3 6.9 %shard_map.149 = (f32[512,512]{1,0:T(8,128)}, f32[512,512]{1,0:T(8,128)}) custom-call(s32[4]{0:T(128)} %reshape.76.places_ref, bf16[512,6912]{1,0:T(8,128)(2,1)} %shard_map.147.refs_0_, bf16[512,6912]{1,0:T(8,128)(2,1)} %shard_map.146.refs_1_.refs_0_, bf16[864,512]{1,0:T(8,128)(2,1)} %copy-done.5, ...), custom_call_target="tpu_custom_call", output_to_operand_aliasing={{0}: (5, {}), {1}: (6, {})} | custom-call | flops 2147483648 | bytes 6291456 | tf_op jit(solution)/shard_map/pallas_call | solution.py:143
  102.2 0.7 copy-done.7
  103.0 0.2 copy-done.8
  103.1 4.4 %shard_map.151 = f32[512,512]{1,0:T(8,128)} custom-call(s32[2]{0:T(128)} %slice_bitcast_fusion.2.places_ref, bf16[512,6912]{1,0:T(8,128)(2,1)} %shard_map.147.refs_0_, bf16[432,512]{1,0:T(8,128)(2,1)} %copy-done.7, bf16[432,512]{1,0:T(8,128)(2,1)} %copy-done.8, f32[512,512]{1,0:T(8,128)} %get-tuple-element.64.refs_3_), custom_call_target="tpu_custom_call", output_to_operand_aliasing={{}: (4, {})} | custom-call | flops 536870912 | bytes 2097152 | tf_op jit(solution)/shard_map/pallas_call | solution.py:143
  107.6 4.2 %collective-permute-start.16 = (f32[512,512]{1,0:T(8,128)}, f32[512,512]{1,0:T(8,128)S(1)}, u32[]{:S(2)}, u32[]{:S(2)}) collective-permute-start(f32[512,512]{1,0:T(8,128)} %shard_map.151), channel_id=1, source_target_pairs={{0,1},{1,0},{2,3},{3,2},{4,5},{5,4},{6,7},{7,6},{8,9},{9,8},{10,11... | collective-permute-start | bytes 3145736 | tf_op jit(solution)/shard_map/ppermute | solution.py:421
  111.8 0.3 convert_reduce_fusion.1
  112.2 4.5 %shard_map.150.own_ref = f32[512,512]{1,0:T(8,128)} custom-call(s32[2]{0:T(128)} %slice_bitcast_fusion.2.places_ref, bf16[512,6912]{1,0:T(8,128)(2,1)} %shard_map.146.refs_1_.refs_0_, bf16[432,512]{1,0:T(8,128)(2,1)} %copy-done.7, bf16[432,512]{1,0:T(8,128)(2,1)} %copy-done.8, f32[512,512]{1,0:T(8,128)} %get-tuple-element.63.refs_3_), custom_call_target="tpu_custom_call", output_to_operand_aliasing={{}: (4, {})} | custom-call | flops 536870912 | bytes 2097152 | tf_op jit(solution)/shard_map/pallas_call | solution.py:143
  116.8 1.2 copy-done
  118.0 2.3 %shard_map.152 = bf16[1024,512]{1,0:T(8,128)(2,1)} custom-call(f32[512,512]{1,0:T(8,128)S(1)} %copy-done, f32[512,512]{1,0:T(8,128)S(1)} %collective-permute-done.16.got_ref, bf16[512,512]{1,0:T(8,128)(2,1)S(1)} %copy-done.2, bf16[512,512]{1,0:T(8,128)(2,1)S(1)} %copy-done.3, f32[1,512]{1,0:T(1,128)S(1)} %bitcast.31, s32[1,512]{1,0:T(1,128)S(1)} %bitcast.29), custom_call_target="tpu_custom_call" | custom-call | flops 805306368 | bytes 2097152 | tf_op jit(solution)/shard_map/pallas_call | solution.py:423
  120.3 4.9 %all-to-all-start = ((bf16[16,64,512]{2,1,0:T(8,128)(2,1)}), bf16[16,64,512]{2,1,0:T(8,128)(2,1)}, u32[]{:S(2)}, u32[]{:S(2)}) async-start(bf16[16,64,512]{2,1,0:T(8,128)(2,1)} %bitcast.10), calls=%async_computation | async-start | bytes 2097152 | tf_op jit(solution)/shard_map/all_to_all | solution.py:437
  125.3 0.9 fusion.8
  126.2 0.2 copy.41
  126.4 0.2 copy.42
  126.6 0.2 convert_reduce_fusion
  126.9 0.9 copy.39.slot_col_ref
  127.8 1.0 maximum_bitcast_fusion.qv_hbm
  128.9 21.4 %all-to-all-done = bf16[16,64,512]{2,1,0:T(8,128)(2,1)} async-done(((bf16[16,64,512]{2,1,0:T(8,128)(2,1)}), bf16[16,64,512]{2,1,0:T(8,128)(2,1)}, u32[]{:S(2)}, u32[]{:S(2)}) %all-to-all-start) | async-done | bytes 1048608 | tf_op jit(solution)/shard_map/all_to_all | solution.py:437
  150.3 24.2 %shard_map.153 = bf16[1024,512]{1,0:T(8,128)(2,1)} custom-call(bf16[1024,512]{1,0:T(8,128)(2,1)} %bitcast.11.arrived_ref, s32[512,1]{1,0:T(8,128)} %copy.39.slot_col_ref, s32[1,512]{1,0:T(1,128)} %bitcast.40, f32[1,512]{1,0:T(1,128)} %bitcast.41, f32[1,512]{1,0:T(1,128)} %bitcast.42, bf16[1024,512]{1,0:T(8,128)(2,1)} %maximum_bitcast_fusion.qv_hbm, ...), custom_call_target="tpu_custom_call" | custom-call | flops 2684354560 | bytes 4194304 | tf_op jit(solution)/shard_map/pallas_call | solution.py:444
  174.5 5.0 %all-to-all-start.1 = ((bf16[16,64,512]{2,1,0:T(8,128)(2,1)}), bf16[16,64,512]{2,1,0:T(8,128)(2,1)S(1)}, u32[]{:S(2)}, u32[]{:S(2)}) async-start(bf16[16,64,512]{2,1,0:T(8,128)(2,1)} %bitcast.32), calls=%async_computation.1 | async-start | bytes 2097152 | tf_op jit(solution)/shard_map/all_to_all | solution.py:468
  179.4 0.1 copy.40.slot_ref
  179.6 24.7 %all-to-all-done.1 = bf16[16,64,512]{2,1,0:T(8,128)(2,1)S(1)} async-done(((bf16[16,64,512]{2,1,0:T(8,128)(2,1)}), bf16[16,64,512]{2,1,0:T(8,128)(2,1)S(1)}, u32[]{:S(2)}, u32[]{:S(2)}) %all-to-all-start.1) | async-done | bytes 1048608 | tf_op jit(solution)/shard_map/all_to_all | solution.py:468
  204.3 1.5 shard_map.154
  (72 shorter events, 1.1 us)
Async XLA Ops:
  0.0 16.7 %copy-start.10 = (bf16[864,512]{1,0:T(8,128)(2,1)S(1)}, bf16[864,512]{1,0:T(8,128)(2,1)}, u32[]{:S(2)}) copy-start(bf16[864,512]{1,0:T(8,128)(2,1)} %param.16) | copy-start | bytes 2654212
  1.1 15.8 %collective-permute-start = (bf16[13,32,512]{2,1,0:T(8,128)(2,1)S(1)}, bf16[13,32,512]{2,1,0:T(8,128)(2,1)}, u32[]{:S(2)}, u32[]{:S(2)}) collective-permute-start(bf16[13,32,512]{2,1,0:T(8,128)(2,1)S(1)} %slice.74), channel_id=1, source_target_pairs={{0,1},{1,0},{2,3},{3,2},{4,5},{5,4},{6,7},{7,6},{8,9},{9,8},{10,11... | collective-permute-start | bytes 1277960 | tf_op jit(solution)/shard_map/ppermute | solution.py:349
  3.0 1.0 copy-start.1
  4.8 17.1 %collective-permute-start.1 = (bf16[64,512]{1,0:T(8,128)(2,1)S(1)}, bf16[64,512]{1,0:T(8,128)(2,1)S(1)}, u32[]{:S(2)}, u32[]{:S(2)}) collective-permute-start(bf16[64,512]{1,0:T(8,128)(2,1)S(1)} %get-tuple-element.35), channel_id=1, source_target_pairs={{1,8},{2,9},{3,10},{4,11},{5,12},{6,13},{7,14},{9,0},{10,1},{11,2}... | collective-permute-start | bytes 196616 | tf_op jit(solution)/shard_map/ppermute | solution.py:366
  8.9 13.0 %collective-permute-start.2 = (bf16[64,512]{1,0:T(8,128)(2,1)S(1)}, bf16[64,512]{1,0:T(8,128)(2,1)S(1)}, u32[]{:S(2)}, u32[]{:S(2)}) collective-permute-start(bf16[64,512]{1,0:T(8,128)(2,1)S(1)} %get-tuple-element.36), channel_id=1, source_target_pairs={{0,8},{1,9},{2,10},{3,11},{4,12},{5,13},{6,14},{7,15},{8,0},{9,1},... | collective-permute-start | bytes 196616 | tf_op jit(solution)/shard_map/ppermute | solution.py:366
  9.1 12.8 %collective-permute-start.3 = (bf16[64,512]{1,0:T(8,128)(2,1)S(1)}, bf16[64,512]{1,0:T(8,128)(2,1)S(1)}, u32[]{:S(2)}, u32[]{:S(2)}) collective-permute-start(bf16[64,512]{1,0:T(8,128)(2,1)S(1)} %get-tuple-element.37), channel_id=1, source_target_pairs={{0,9},{1,10},{2,11},{3,12},{4,13},{5,14},{6,15},{8,1},{9,2},{10,3}... | collective-permute-start | bytes 196616 | tf_op jit(solution)/shard_map/ppermute | solution.py:366
  14.8 7.1 %collective-permute-start.4 = (bf16[64,512]{1,0:T(8,128)(2,1)S(1)}, bf16[64,512]{1,0:T(8,128)(2,1)S(1)}, u32[]{:S(2)}, u32[]{:S(2)}) collective-permute-start(bf16[64,512]{1,0:T(8,128)(2,1)S(1)} %get-tuple-element.38), channel_id=1, source_target_pairs={{1,0},{2,1},{3,2},{4,3},{5,4},{6,5},{7,6},{9,8},{10,9},{11,10},{12... | collective-permute-start | bytes 196616 | tf_op jit(solution)/shard_map/ppermute | solution.py:366
  16.9 5.0 %collective-permute-start.5 = (bf16[64,512]{1,0:T(8,128)(2,1)S(1)}, bf16[64,512]{1,0:T(8,128)(2,1)S(1)}, u32[]{:S(2)}, u32[]{:S(2)}) collective-permute-start(bf16[64,512]{1,0:T(8,128)(2,1)S(1)} %get-tuple-element.39), channel_id=1, source_target_pairs={{0,1},{1,2},{2,3},{3,4},{4,5},{5,6},{6,7},{8,9},{9,10},{10,11},{11... | collective-permute-start | bytes 196616 | tf_op jit(solution)/shard_map/ppermute | solution.py:366
  21.9 9.9 %copy-start.11 = (bf16[27,32,512]{2,1,0:T(8,128)(2,1)}, bf16[27,32,512]{2,1,0:T(8,128)(2,1)S(1)}, u32[]{:S(2)}) copy-start(bf16[27,32,512]{2,1,0:T(8,128)(2,1)S(1)} %maximum_select_fusion) | copy-start | bytes 2654212
  21.9 0.7 copy-start.12
  21.9 0.7 copy-start.13
  21.9 0.7 copy-start.14
  22.0 0.7 copy-start.15
  28.1 5.1 %collective-permute-start.11 = (s32[512,26]{1,0:T(8,128)S(1)}, s32[512,26]{1,0:T(8,128)S(1)}, u32[]{:S(2)}, u32[]{:S(2)}) collective-permute-start(s32[512,26]{1,0:T(8,128)S(1)} %copy.36), channel_id=1, source_target_pairs={{0,1},{1,0},{2,3},{3,2},{4,5},{5,4},{6,7},{7,6},{8,9},{9,8},{10,11... | collective-permute-start | bytes 159752 | tf_op jit(solution)/shard_map/ppermute | solution.py:393
  31.6 14.3 %collective-permute-start.8 = (bf16[1024,256]{1,0:T(8,128)(2,1)S(1)}, bf16[1024,256]{1,0:T(8,128)(2,1)S(1)}, u32[]{:S(2)}, u32[]{:S(2)}) collective-permute-start(bf16[1024,256]{1,0:T(8,128)(2,1)S(1)} %get-tuple-element.68), channel_id=1, source_target_pairs={{0,1},{1,0},{2,3},{3,2},{4,5},{5,4},{6,7},{7,6},{8,9},{9,8},{10,11... | collective-permute-start | bytes 1572872 | tf_op jit(solution)/shard_map/ppermute | solution.py:392
  31.7 20.9 %collective-permute-start.6 = (bf16[864,512]{1,0:T(8,128)(2,1)S(1)}, bf16[864,512]{1,0:T(8,128)(2,1)S(1)}, u32[]{:S(2)}, u32[]{:S(2)}) collective-permute-start(bf16[864,512]{1,0:T(8,128)(2,1)S(1)} %bitcast.35), channel_id=1, source_target_pairs={{0,4},{1,5},{4,8},{5,9},{8,12},{9,13},{12,14},{13,15},{14,10},{15,... | collective-permute-start | bytes 2654216 | tf_op jit(solution)/shard_map/ppermute | solution.py:383
  31.7 21.0 %collective-permute-start.7 = (bf16[864,512]{1,0:T(8,128)(2,1)S(1)}, bf16[864,512]{1,0:T(8,128)(2,1)}, u32[]{:S(2)}, u32[]{:S(2)}) collective-permute-start(bf16[864,512]{1,0:T(8,128)(2,1)S(1)} %bitcast.36), channel_id=1, source_target_pairs={{0,2},{1,3},{4,0},{5,1},{8,4},{9,5},{12,8},{13,9},{14,12},{15,13},... | collective-permute-start | bytes 2654216 | tf_op jit(solution)/shard_map/ppermute | solution.py:384
  45.9 8.3 %copy-start.21 = (bf16[1024,256]{1,0:T(8,128)(2,1)}, bf16[1024,256]{1,0:T(8,128)(2,1)S(1)}, u32[]{:S(2)}) copy-start(bf16[1024,256]{1,0:T(8,128)(2,1)S(1)} %collective-permute-done.8.table_ref) | copy-start | bytes 1572868
  52.6 13.1 %copy-start.19 = (bf16[864,512]{1,0:T(8,128)(2,1)}, bf16[864,512]{1,0:T(8,128)(2,1)S(1)}, u32[]{:S(2)}) copy-start(bf16[864,512]{1,0:T(8,128)(2,1)S(1)} %collective-permute-done.6.refs_3_) | copy-start | bytes 2654212
  52.8 20.3 %collective-permute-start.10 = (bf16[864,512]{1,0:T(8,128)(2,1)}, bf16[864,512]{1,0:T(8,128)(2,1)S(1)}, u32[]{:S(2)}, u32[]{:S(2)}) collective-permute-start(bf16[864,512]{1,0:T(8,128)(2,1)} %collective-permute-done.7.refs_4_), channel_id=1, source_target_pairs={{0,2},{1,3},{4,0},{5,1},{8,4},{9,5},{12,8},{13,9},{14,12},{15,13},... | collective-permute-start | bytes 2654216 | tf_op jit(solution)/shard_map/ppermute | solution.py:384
  53.7 19.4 %collective-permute-start.9 = (bf16[864,512]{1,0:T(8,128)(2,1)S(1)}, bf16[864,512]{1,0:T(8,128)(2,1)}, u32[]{:S(2)}, u32[]{:S(2)}) collective-permute-start(bf16[864,512]{1,0:T(8,128)(2,1)S(1)} %collective-permute-done.6.refs_3_), channel_id=1, source_target_pairs={{0,4},{1,5},{4,8},{5,9},{8,12},{9,13},{12,14},{13,15},{14,10},{15,... | collective-permute-start | bytes 2654216 | tf_op jit(solution)/shard_map/ppermute | solution.py:383
  73.0 2.9 %copy-start.20 = (bf16[864,512]{1,0:T(8,128)(2,1)}, bf16[864,512]{1,0:T(8,128)(2,1)S(1)}, u32[]{:S(2)}) copy-start(bf16[864,512]{1,0:T(8,128)(2,1)S(1)} %collective-permute-done.10.refs_6_) | copy-start | bytes 2654212
  73.1 18.5 %collective-permute-start.12 = (bf16[864,512]{1,0:T(8,128)(2,1)}, bf16[864,512]{1,0:T(8,128)(2,1)S(1)}, u32[]{:S(2)}, u32[]{:S(2)}) collective-permute-start(bf16[864,512]{1,0:T(8,128)(2,1)} %collective-permute-done.9.refs_5_), channel_id=1, source_target_pairs={{0,4},{1,5},{4,8},{5,9},{8,12},{9,13},{12,14},{13,15},{14,10},{15,... | collective-permute-start | bytes 2654216 | tf_op jit(solution)/shard_map/ppermute | solution.py:383
  74.0 18.5 %collective-permute-start.13 = (bf16[864,512]{1,0:T(8,128)(2,1)S(1)}, bf16[864,512]{1,0:T(8,128)(2,1)S(1)}, u32[]{:S(2)}, u32[]{:S(2)}) collective-permute-start(bf16[864,512]{1,0:T(8,128)(2,1)S(1)} %collective-permute-done.10.refs_6_), channel_id=1, source_target_pairs={{0,2},{1,3},{4,0},{5,1},{8,4},{9,5},{12,8},{13,9},{14,12},{15,13},... | collective-permute-start | bytes 2654216 | tf_op jit(solution)/shard_map/ppermute | solution.py:384
  91.7 3.6 %copy-start.5 = (bf16[864,512]{1,0:T(8,128)(2,1)}, bf16[864,512]{1,0:T(8,128)(2,1)S(1)}, u32[]{:S(2)}) copy-start(bf16[864,512]{1,0:T(8,128)(2,1)S(1)} %collective-permute-done.12.refs_2_) | copy-start | bytes 2654212
  92.4 2.8 %copy-start.6 = (bf16[864,512]{1,0:T(8,128)(2,1)}, bf16[864,512]{1,0:T(8,128)(2,1)S(1)}, u32[]{:S(2)}) copy-start(bf16[864,512]{1,0:T(8,128)(2,1)S(1)} %collective-permute-done.13.refs_3_) | copy-start | bytes 2654212
  92.5 9.7 %collective-permute-start.14 = (bf16[432,512]{1,0:T(8,128)(2,1)S(1)}, bf16[432,512]{1,0:T(8,128)(2,1)S(1)}, u32[]{:S(2)}, u32[]{:S(2)}) collective-permute-start(bf16[432,512]{1,0:T(8,128)(2,1)S(1)} %slice.88), channel_id=1, source_target_pairs={{0,4},{1,5},{4,8},{5,9},{8,12},{9,13},{12,14},{13,15},{14,10},{15,... | collective-permute-start | bytes 1327112 | tf_op jit(solution)/shard_map/ppermute | solution.py:383
  93.0 9.2 %collective-permute-start.15 = (bf16[432,512]{1,0:T(8,128)(2,1)S(1)}, bf16[432,512]{1,0:T(8,128)(2,1)S(1)}, u32[]{:S(2)}, u32[]{:S(2)}) collective-permute-start(bf16[432,512]{1,0:T(8,128)(2,1)S(1)} %slice.89), channel_id=1, source_target_pairs={{0,2},{1,3},{4,0},{5,1},{8,4},{9,5},{12,8},{13,9},{14,12},{15,13},... | collective-permute-start | bytes 1327112 | tf_op jit(solution)/shard_map/ppermute | solution.py:384
  102.2 0.8 copy-start.7
  102.2 0.9 copy-start.8
  103.1 8.7 %copy-start.16 = (s32[512]{0:T(512)S(1)}, s32[512]{0:T(512)}, u32[]{:S(2)}) copy-start(s32[512]{0:T(512)} %param.27) | copy-start | bytes 6148
  107.6 9.2 %collective-permute-start.16 = (f32[512,512]{1,0:T(8,128)}, f32[512,512]{1,0:T(8,128)S(1)}, u32[]{:S(2)}, u32[]{:S(2)}) collective-permute-start(f32[512,512]{1,0:T(8,128)} %shard_map.151), channel_id=1, source_target_pairs={{0,1},{1,0},{2,3},{3,2},{4,5},{5,4},{6,7},{7,6},{8,9},{9,8},{10,11... | collective-permute-start | bytes 3145736 | tf_op jit(solution)/shard_map/ppermute | solution.py:421
  112.2 4.6 %copy-start.2 = (bf16[512,512]{1,0:T(8,128)(2,1)S(1)}, bf16[512,512]{1,0:T(8,128)(2,1)}, u32[]{:S(2)}) copy-start(bf16[512,512]{1,0:T(8,128)(2,1)} %features_ref.3) | copy-start | bytes 1572868
  112.2 4.6 %copy-start.3 = (bf16[512,512]{1,0:T(8,128)(2,1)S(1)}, bf16[512,512]{1,0:T(8,128)(2,1)}, u32[]{:S(2)}) copy-start(bf16[512,512]{1,0:T(8,128)(2,1)} %weight_ref.1) | copy-start | bytes 1572868
  112.2 4.6 %copy-start.4 = (f32[512]{0:T(512)S(1)}, f32[512]{0:T(512)}, u32[]{:S(2)}) copy-start(f32[512]{0:T(512)} %param.18) | copy-start | bytes 6148
  116.8 1.2 copy-start
  120.3 5.0 %copy-start.9 = (bf16[512,1536]{1,0:T(8,128)(2,1)S(1)}, bf16[512,1536]{1,0:T(8,128)(2,1)}, u32[]{:S(2)}) copy-start(bf16[512,1536]{1,0:T(8,128)(2,1)} %param.20) | copy-start | bytes 4718596
  120.3 29.9 %all-to-all-start = ((bf16[16,64,512]{2,1,0:T(8,128)(2,1)}), bf16[16,64,512]{2,1,0:T(8,128)(2,1)}, u32[]{:S(2)}, u32[]{:S(2)}) async-start(bf16[16,64,512]{2,1,0:T(8,128)(2,1)} %bitcast.10), calls=%async_computation | async-start | bytes 2097152 | tf_op jit(solution)/shard_map/all_to_all | solution.py:437
  125.3 1.3 copy-start.18
  126.9 23.3 %copy-start.17 = (s32[512]{0:T(512)}, s32[512]{0:T(512)S(1)}, u32[]{:S(2)}) copy-start(s32[512]{0:T(512)S(1)} %multiply_add_fusion) | copy-start | bytes 6148
  174.5 29.8 %all-to-all-start.1 = ((bf16[16,64,512]{2,1,0:T(8,128)(2,1)}), bf16[16,64,512]{2,1,0:T(8,128)(2,1)S(1)}, u32[]{:S(2)}, u32[]{:S(2)}) async-start(bf16[16,64,512]{2,1,0:T(8,128)(2,1)} %bitcast.32), calls=%async_computation.1 | async-start | bytes 2097152 | tf_op jit(solution)/shard_map/all_to_all | solution.py:468

commit v7 on v6

--- a/solution.py
+++ b/solution.py
@@ -56,9 +56,30 @@
     ordered_ref[...] = ordered
     row_ids = lax.broadcasted_iota(jnp.int32, (rows_ref.shape[0], points), 1)
     rows = dot(one_hot(rows_ref[...] == row_ids), ordered).astype(BF16)
-    size = rows.shape[0] // len(face_refs)
-    for at, ref in enumerate(face_refs):
-        ref[...] = rows[at * size : (at + 1) * size]
+    taken = 0
+    for ref in face_refs:
+        ref[...] = rows[taken : taken + ref.shape[0]]
+        taken += ref.shape[0]
+
+
+def table_kernel(flags_ref, ordered_ref, side_ref, behind_ref, ahead_ref, own_ref, other_ref, held):
+    size = behind_ref.shape[0] // 2
+    points = ordered_ref.shape[0]
+    half = own_ref.shape[1]
+    lower, even = flags_ref[0] == 1, flags_ref[1] == 0
+    held[:points] = ordered_ref[...]
+    across = (ahead_ref[size:], side_ref[size : 2 * size], behind_ref[size:])
+    zero = jnp.zeros_like(across[0])
+    for at, rows in enumerate(across):
+        start = points + at * size
+        held[start : start + size] = jnp.where(lower, rows, zero)
+        start += 5 * size
+        held[start : start + size] = jnp.where(lower, zero, rows)
+    held[points + 3 * size : points + 4 * size] = ahead_ref[:size]
+    held[points + 4 * size : points + 5 * size] = behind_ref[:size]
+    first, second = held[:, :half], held[:, half:]
+    own_ref[...] = jnp.where(even, first, second)
+    other_ref[...] = jnp.where(even, second, first)
 
 
 def gather_kernel(taps, rows_ref, table_ref, out_ref):
@@ -260,30 +281,12 @@
     out_ref[...] = dot(one_hot(slot_ref[...] == slot_ids), arrived_ref[...]).astype(BF16)
 
 
-def face_routes(devices):
-    def pairs(dx, dy):
-        return [
-            (source, source + dx * GY + dy)
-            for source in range(devices)
-            if 0 <= source // GY + dx < devices // GY and 0 <= source % GY + dy < GY
-        ]
-
-    if devices != 2 * GY:
-        return [(k, k, pairs(STEPS_X[k], STEPS_Y[k])) for k in range(8)]
-    both = [(6 + dy, 1 + dy, pairs(1, dy) + pairs(-1, dy)) for dy in (-1, 0, 1)]
-    return both + [(k, k, pairs(0, STEPS_Y[k])) for k in (3, 4)]
-
-
-def received_faces(routes, got, lower):
-    received = [None] * 8
-    for (first, second, _), rows in zip(routes, got):
-        if first == second:
-            received[first] = rows
-        else:
-            zero = jnp.zeros_like(rows)
-            received[first] = jnp.where(lower, zero, rows)
-            received[second] = jnp.where(lower, rows, zero)
-    return received
+def face_pairs(devices, dx, dy):
+    return [
+        (source, source + dx * GY + dy)
+        for source in range(devices)
+        if 0 <= source // GY + dx < devices // GY and 0 <= source % GY + dy < GY
+    ]
 
 
 def way_round(devices, rows, length):
@@ -350,23 +353,25 @@
     mine = jnp.where(
         core == 0, jnp.concatenate([kept, got]), jnp.concatenate([got, kept])
     ).reshape(TAPS * unit, width)
+    round_trip = devices == 2 * GY
     lower = index < GY
-    routes = face_routes(devices)
-    lists = [jnp.where(lower, face_rows[0, first], face_rows[0, second]) for first, second, _ in routes]
-    face_list = jnp.concatenate(lists).reshape(-1, 1)
+    if round_trip:
+        across = jnp.where(lower, face_rows[0, 5:], face_rows[0, :3])
+        face_list = jnp.concatenate([across, face_rows[0, 3:5]]).reshape(-1, 1)
+        counts = (3, 1, 1)
+    else:
+        face_list = face_rows.reshape(-1, 1)
+        counts = (1,) * 8
+    size = face_rows.shape[2]
     ordered, *faces = call(
         functools.partial(faces_kernel, unit),
         [jax.ShapeDtypeStruct((points, width), BF16)]
-        + [jax.ShapeDtypeStruct((face_rows.shape[2], width), BF16)] * len(routes),
-        32,
+        + [jax.ShapeDtypeStruct((count * size, width), BF16) for count in counts],
+        60,
         4 * points * width * width,
         8 * points * width,
     )(features, face_list)
-    faces = [
-        lax.ppermute(rows, "blocks", pairs) for rows, (_, _, pairs) in zip(faces, routes)
-    ]
-
-    round_trip = devices == 16
+
     rows = mine.shape[0]
     length = -(-(rows + 127) // 128) * 128 if round_trip else rows * (devices // 2)
     back_pairs, on_pairs, places = way_round(devices, rows, length)
@@ -384,17 +389,40 @@
         on.append(lax.ppermute(second, "blocks", on_pairs))
         return tied[2:]
 
-    neighbours, *faces = pass_on(neighbours, *faces)
-    received = received_faces(routes, faces, lower)
-    table = jnp.concatenate([ordered, *received], axis=0)
-    own_table = lax.dynamic_slice(table, (0, core * half), (table.shape[0], half))
-    other_half = lax.dynamic_slice(table, (0, (1 - core) * half), (table.shape[0], half))
+    sent_neighbours = neighbours
+    if round_trip:
+        lists, back_list, on_list = faces
+        side = face_pairs(devices, 1, 0) + face_pairs(devices, -1, 0)
+        (lists,) = pass_on(lax.ppermute(lists, "blocks", side))
+        to_on = jnp.concatenate([on_list, lists[2 * size :]])
+        to_back = jnp.concatenate([back_list, lists[:size]])
+        behind = lax.ppermute(to_on, "blocks", face_pairs(devices, 0, 1))
+        ahead = lax.ppermute(to_back, "blocks", face_pairs(devices, 0, -1))
+        sent_neighbours, lists, behind, ahead = pass_on(neighbours, lists, behind, ahead)
+        height = points + 8 * size
+        own_table, other_half = call(
+            table_kernel,
+            [jax.ShapeDtypeStruct((height, half), BF16)] * 2,
+            32,
+            0,
+            4 * height * width,
+            in_specs=[pl.BlockSpec(memory_space=pltpu.SMEM)] + [pl.BlockSpec()] * 4,
+            scratch_shapes=[pltpu.VMEM((height, width), BF16)],
+        )(jnp.stack([lower.astype(jnp.int32), core]), ordered, lists, behind, ahead)
+    else:
+        got = [
+            lax.ppermute(faces[k], "blocks", face_pairs(devices, STEPS_X[k], STEPS_Y[k]))
+            for k in range(8)
+        ]
+        table = jnp.concatenate([ordered, *got], axis=0)
+        own_table = lax.dynamic_slice(table, (0, core * half), (table.shape[0], half))
+        other_half = lax.dynamic_slice(table, (0, (1 - core) * half), (table.shape[0], half))
     other_table = lax.ppermute(other_half, "blocks", partner)
-    other_neighbours = lax.ppermute(neighbours, "blocks", partner)
+    other_neighbours = lax.ppermute(sent_neighbours, "blocks", partner)
     own_stacked = gather_block(padded_taps(neighbours), own_table)
     own_stacked, other_table = pass_on(own_stacked, other_table)
     other_stacked = gather_block(padded_taps(other_neighbours), other_table)
-    stacked = pass_on(other_stacked, own_stacked)
+    stacked = other_stacked, own_stacked
     if round_trip:
         places = jnp.array(places, jnp.int32)[index]
         early = [[mine], [back[1]], [on[1]], [back[2]], [on[2]]]

time: 207 us -> 206 us (level)
  waiting for transfers between devices: 67.5 us -> 80.9 us
  starting transfers between devices: 38.9 us -> 29.7 us
  other arithmetic: 7.68 us -> 3.81 us
  local copies, waits for them, and re-layouts: 14.2 us -> 10.9 us
  Pallas kernels: 77 us -> 79.5 us
    ppermute x6 -> x4, waiting for transfers between devices: 0.02 us -> 12.9 us  [the longest x1 8.88 us: body(): lists, = pass_on(lax.ppermute(lists, 'blocks', side))]
    ppermute x6 -> x4, starting transfers between devices: 17.9 us -> 10.5 us  [the longest x1 4.03 us: body(): behind = lax.ppermute(to_on, 'blocks', face_pairs(devices, 0, 1))]
    ppermute x4, waiting for transfers between devices: 13.2 us -> 16.1 us  [pass_on(): back.append(lax.ppermute(first, 'blocks', back_pairs))]
    unnamed x5 -> x0, other arithmetic: 2.63 us -> none
    ppermute x4, waiting for transfers between devices: 8.22 us -> 5.87 us  [pass_on(): on.append(lax.ppermute(second, 'blocks', on_pairs))]
    unnamed x49 -> x42, local copies, waits for them, and re-layouts: 5.24 us -> 3.27 us
  transfers between devices with their start and end apart: 19 -> 17, of which waited for: 8 -> 10; matrix products, arithmetic and copies ran while one was open for 6% -> 5% of each run, Pallas kernels for 22% -> 23%
where the time goes in v7:
time: 206 us; the launch traced here: 205 us
  waiting for transfers between devices  80.9 us (39%)
  Pallas kernels  79.5 us (39%)
  starting transfers between devices  29.7 us (14%)
  local copies, waits for them, and re-layouts  10.9 us (5%)
  other arithmetic  3.81 us (2%)
    pallas_call x4, Pallas kernels, conv_part(): call(functools.partial(conv_kernel, slots, blocks, before is None), [jax....  25.3 us
    all_to_all x1, waiting for transfers between devices, body(): lax.all_to_all(back.reshape(devices, capacity, width), 'blocks', split_ax...  24.7 us
    pallas_call x1, Pallas kernels, body(): call(block_kernel, jax.ShapeDtypeStruct((slots, width), BF16), 60, 20 * p...  24.2 us
    pallas_call x2, Pallas kernels, gather_block(): call(functools.partial(gather_kernel, taps), jax.ShapeDtypeStruct((points...  23 us
    all_to_all x1, waiting for transfers between devices, body(): lax.all_to_all(outgoing.reshape(devices, capacity, width), 'blocks', spli...  21.3 us
    ppermute x4, waiting for transfers between devices, pass_on(): back.append(lax.ppermute(first, 'blocks', back_pairs))  16.1 us
    ppermute x1, waiting for transfers between devices, body(): lists, = pass_on(lax.ppermute(lists, 'blocks', side))  8.88 us
    ppermute x4, waiting for transfers between devices, pass_on(): on.append(lax.ppermute(second, 'blocks', on_pairs))  5.87 us
  transfers between devices with their start and end apart: 17, of which 10 were waited for; matrix products, arithmetic and copies ran while one was open for 5% of the time, Pallas kernels for 23%

profile of v7, /device:TPU:9, one launch (start us, length us, event | category | flops | bytes accessed | tf_op | source)
XLA Modules:
  0.0 205.3 jit_solution(2553355751644266652)
XLA Ops:
  0.0 1.1 slice.63
  1.1 0.7 collective-permute-start
  1.9 0.8 select_bitcast_fusion
  2.6 0.7 slice_bitcast_fusion
  3.3 0.8 reshape.85.rows_ref
  4.2 2.5 %shard_map.145 = (bf16[512,512]{1,0:T(8,128)(2,1)}, bf16[192,512]{1,0:T(8,128)(2,1)}, bf16[64,512]{1,0:T(8,128)(2,1)}, bf16[64,512]{1,0:T(8,128)(2,1)}) custom-call(bf16[512,512]{1,0:T(8,128)(2,1)} %features_ref.3, s32[320,1]{1,0:T(8,128)} %reshape.85.rows_ref), custom_call_target="tpu_custom_call" | custom-call | flops 536870912 | bytes 2097152 | tf_op jit(solution)/shard_map/pallas_call | solution.py:366
  6.6 2.4 %collective-permute-start.1 = (bf16[192,512]{1,0:T(8,128)(2,1)}, bf16[192,512]{1,0:T(8,128)(2,1)S(1)}, u32[]{:S(2)}, u32[]{:S(2)}) collective-permute-start(bf16[192,512]{1,0:T(8,128)(2,1)} %get-tuple-element.32), channel_id=1, source_target_pairs={{0,8},{1,9},{2,10},{3,11},{4,12},{5,13},{6,14},{7,15},{8,0},{9,1},... | collective-permute-start | bytes 589832 | tf_op jit(solution)/shard_map/ppermute | solution.py:396
  9.0 0.1 maximum_select_fusion
  9.2 8.9 %collective-permute-done.1.side_ref = bf16[192,512]{1,0:T(8,128)(2,1)S(1)} collective-permute-done((bf16[192,512]{1,0:T(8,128)(2,1)}, bf16[192,512]{1,0:T(8,128)(2,1)S(1)}, u32[]{:S(2)}, u32[]{:S(2)}) %collective-permute-start.1) | collective-permute-done | bytes 196640 | tf_op jit(solution)/shard_map/ppermute | solution.py:396
  18.1 1.5 collective-permute-start.3
  19.6 4.0 %collective-permute-start.4 = (bf16[128,512]{1,0:T(8,128)(2,1)S(1)}, bf16[128,512]{1,0:T(8,128)(2,1)S(1)}, u32[]{:S(2)}, u32[]{:S(2)}) collective-permute-start(bf16[128,512]{1,0:T(8,128)(2,1)S(1)} %pad_maximum_fusion), channel_id=1, source_target_pairs={{0,1},{1,2},{2,3},{3,4},{4,5},{5,6},{6,7},{8,9},{9,10},{10,11},{11... | collective-permute-start | bytes 393224 | tf_op jit(solution)/shard_map/ppermute | solution.py:399
  23.7 1.9 collective-permute-start.5
  25.6 0.7 constant_dynamic-slice_fusion
  26.3 4.0 %collective-permute-done.5.ahead_ref = bf16[128,512]{1,0:T(8,128)(2,1)S(1)} collective-permute-done((bf16[128,512]{1,0:T(8,128)(2,1)S(1)}, bf16[128,512]{1,0:T(8,128)(2,1)S(1)}, u32[]{:S(2)}, u32[]{:S(2)}) %collective-permute-start.5) | collective-permute-done | bytes 131104 | tf_op jit(solution)/shard_map/ppermute | solution.py:400
  30.4 8.6 %collective-permute-done.2.refs_3_ = bf16[864,512]{1,0:T(8,128)(2,1)} collective-permute-done((bf16[864,512]{1,0:T(8,128)(2,1)S(1)}, bf16[864,512]{1,0:T(8,128)(2,1)}, u32[]{:S(2)}, u32[]{:S(2)}) %collective-permute-start.2) | collective-permute-done | bytes 884768 | tf_op jit(solution)/shard_map/ppermute | solution.py:388
  39.0 1.8 collective-permute-done.3.refs_4_
  40.8 0.1 copy.36
  40.9 2.2 %collective-permute-start.11 = (s32[512,26]{1,0:T(8,128)S(1)}, s32[512,26]{1,0:T(8,128)S(1)}, u32[]{:S(2)}, u32[]{:S(2)}) collective-permute-start(s32[512,26]{1,0:T(8,128)S(1)} %copy.36), channel_id=1, source_target_pairs={{0,1},{1,0},{2,3},{3,2},{4,5},{5,4},{6,7},{7,6},{8,9},{9,8},{10,11... | collective-permute-start | bytes 159752 | tf_op jit(solution)/shard_map/ppermute | solution.py:421
  43.1 0.1 pad_add_fusion.1.flags_ref
  43.2 0.1 copy.34
  43.4 0.1 copy.35
  43.5 0.1 pad.11.clone
  43.6 0.6 reshape.71.places_ref
  44.1 0.6 shard_map.146
  44.8 0.8 copy-done.5
  45.6 0.0 collective-permute-start.8
  45.6 0.6 collective-permute-start.6
  46.2 0.9 collective-permute-start.7
  47.1 0.1 fusion.6
  47.2 1.1 add_convert_fusion.1
  48.4 11.5 %shard_map.147.refs_1_.refs_0_ = bf16[512,6912]{1,0:T(8,128)(2,1)} custom-call(f32[512,128]{1,0:T(8,128)} %get-tuple-element.63.rows_ref, bf16[1024,256]{1,0:T(8,128)(2,1)} %copy-done.5), custom_call_target="tpu_custom_call" | custom-call | flops 7247757312 | bytes 7077888 | tf_op jit(solution)/shard_map/pallas_call | solution.py:101
  59.9 6.8 %collective-permute-done.6.refs_5_ = bf16[864,512]{1,0:T(8,128)(2,1)} collective-permute-done((bf16[864,512]{1,0:T(8,128)(2,1)}, bf16[864,512]{1,0:T(8,128)(2,1)}, u32[]{:S(2)}, u32[]{:S(2)}) %collective-permute-start.6) | collective-permute-done | bytes 884768 | tf_op jit(solution)/shard_map/ppermute | solution.py:388
  66.7 3.4 %collective-permute-done.7.refs_6_ = bf16[864,512]{1,0:T(8,128)(2,1)} collective-permute-done((bf16[864,512]{1,0:T(8,128)(2,1)}, bf16[864,512]{1,0:T(8,128)(2,1)}, u32[]{:S(2)}, u32[]{:S(2)}) %collective-permute-start.7) | collective-permute-done | bytes 884768 | tf_op jit(solution)/shard_map/ppermute | solution.py:389
  70.1 1.5 collective-permute-start.9
  71.6 11.5 %shard_map.148.refs_0_ = bf16[512,6912]{1,0:T(8,128)(2,1)} custom-call(f32[512,128]{1,0:T(8,128)} %get-tuple-element.62.rows_ref, bf16[1024,256]{1,0:T(8,128)(2,1)} %copy-done.19), custom_call_target="tpu_custom_call" | custom-call | flops 7247757312 | bytes 7077888 | tf_op jit(solution)/shard_map/pallas_call | solution.py:101
  83.0 9.4 %shard_map.149 = (f32[512,512]{1,0:T(8,128)}, f32[512,512]{1,0:T(8,128)}) custom-call(s32[10]{0:T(128)} %reshape.71.places_ref, bf16[512,6912]{1,0:T(8,128)(2,1)} %shard_map.148.refs_0_, bf16[512,6912]{1,0:T(8,128)(2,1)} %shard_map.147.refs_1_.refs_0_, bf16[864,512]{1,0:T(8,128)(2,1)} %bitcast.33, bf16[864,512]{1,0:T(8,128)(2,1)} %collective-permute-done.2.refs_3_, ...), custom_call_target="tpu_custom_call" | custom-call | flops 5368709120 | bytes 15728640 | tf_op jit(solution)/shard_map/pallas_call | solution.py:164
  92.5 1.2 collective-permute-start.12
  93.8 0.4 collective-permute-start.13
  94.2 0.6 reshape.72.places_ref
  94.7 0.5 slice_bitcast_fusion.1.places_ref
  95.3 6.9 %shard_map.150 = (f32[512,512]{1,0:T(8,128)}, f32[512,512]{1,0:T(8,128)}) custom-call(s32[4]{0:T(128)} %reshape.72.places_ref, bf16[512,6912]{1,0:T(8,128)(2,1)} %shard_map.148.refs_0_, bf16[512,6912]{1,0:T(8,128)(2,1)} %shard_map.147.refs_1_.refs_0_, bf16[864,512]{1,0:T(8,128)(2,1)} %copy-done.7, ...), custom_call_target="tpu_custom_call", output_to_operand_aliasing={{0}: (5, {}), {1}: (6, {})} | custom-call | flops 2147483648 | bytes 6291456 | tf_op jit(solution)/shard_map/pallas_call | solution.py:164
  102.2 0.7 collective-permute-done.12.refs_1_
  102.9 0.6 collective-permute-done.13.refs_2_
  103.5 0.1 copy-done.8
  103.7 0.6 copy-done.9
  104.3 4.4 %shard_map.152 = f32[512,512]{1,0:T(8,128)} custom-call(s32[2]{0:T(128)} %slice_bitcast_fusion.1.places_ref, bf16[512,6912]{1,0:T(8,128)(2,1)} %shard_map.148.refs_0_, bf16[432,512]{1,0:T(8,128)(2,1)} %copy-done.8, bf16[432,512]{1,0:T(8,128)(2,1)} %copy-done.9, f32[512,512]{1,0:T(8,128)} %get-tuple-element.58.refs_3_), custom_call_target="tpu_custom_call", output_to_operand_aliasing={{}: (4, {})} | custom-call | flops 536870912 | bytes 2097152 | tf_op jit(solution)/shard_map/pallas_call | solution.py:164
  108.7 2.9 %collective-permute-start.14 = (f32[512,512]{1,0:T(8,128)}, f32[512,512]{1,0:T(8,128)S(1)}, u32[]{:S(2)}, u32[]{:S(2)}) collective-permute-start(f32[512,512]{1,0:T(8,128)} %shard_map.152), channel_id=1, source_target_pairs={{0,1},{1,0},{2,3},{3,2},{4,5},{5,4},{6,7},{7,6},{8,9},{9,8},{10,11... | collective-permute-start | bytes 3145736 | tf_op jit(solution)/shard_map/ppermute | solution.py:449
  111.7 0.3 convert_reduce_fusion.1
  112.1 4.5 %shard_map.151.own_ref = f32[512,512]{1,0:T(8,128)} custom-call(s32[2]{0:T(128)} %slice_bitcast_fusion.1.places_ref, bf16[512,6912]{1,0:T(8,128)(2,1)} %shard_map.147.refs_1_.refs_0_, bf16[432,512]{1,0:T(8,128)(2,1)} %copy-done.8, bf16[432,512]{1,0:T(8,128)(2,1)} %copy-done.9, f32[512,512]{1,0:T(8,128)} %get-tuple-element.57.refs_3_), custom_call_target="tpu_custom_call", output_to_operand_aliasing={{}: (4, {})} | custom-call | flops 536870912 | bytes 2097152 | tf_op jit(solution)/shard_map/pallas_call | solution.py:164
  116.7 1.2 copy-done
  117.9 2.3 %shard_map.153 = bf16[1024,512]{1,0:T(8,128)(2,1)} custom-call(f32[512,512]{1,0:T(8,128)S(1)} %copy-done, f32[512,512]{1,0:T(8,128)S(1)} %collective-permute-done.14.got_ref, bf16[512,512]{1,0:T(8,128)(2,1)S(1)} %copy-done.1, bf16[512,512]{1,0:T(8,128)(2,1)S(1)} %copy-done.2, f32[1,512]{1,0:T(1,128)S(1)} %bitcast.27, s32[1,512]{1,0:T(1,128)S(1)} %bitcast.25), custom_call_target="tpu_custom_call" | custom-call | flops 805306368 | bytes 2097152 | tf_op jit(solution)/shard_map/pallas_call | solution.py:451
  120.2 4.5 %all-to-all-start = ((bf16[16,64,512]{2,1,0:T(8,128)(2,1)}), bf16[16,64,512]{2,1,0:T(8,128)(2,1)}, u32[]{:S(2)}, u32[]{:S(2)}) async-start(bf16[16,64,512]{2,1,0:T(8,128)(2,1)} %bitcast.9), calls=%async_computation | async-start | bytes 2097152 | tf_op jit(solution)/shard_map/all_to_all | solution.py:465
  124.8 0.9 fusion.5
  125.7 0.2 copy.41
  125.9 0.2 copy.42
  126.2 0.2 convert_reduce_fusion
  126.4 0.9 copy.39.slot_col_ref
  127.3 1.0 maximum_bitcast_fusion.qv_hbm
  128.4 21.3 %all-to-all-done = bf16[16,64,512]{2,1,0:T(8,128)(2,1)} async-done(((bf16[16,64,512]{2,1,0:T(8,128)(2,1)}), bf16[16,64,512]{2,1,0:T(8,128)(2,1)}, u32[]{:S(2)}, u32[]{:S(2)}) %all-to-all-start) | async-done | bytes 1048608 | tf_op jit(solution)/shard_map/all_to_all | solution.py:465
  149.7 24.2 %shard_map.154 = bf16[1024,512]{1,0:T(8,128)(2,1)} custom-call(bf16[1024,512]{1,0:T(8,128)(2,1)} %bitcast.10.arrived_ref, s32[512,1]{1,0:T(8,128)} %copy.39.slot_col_ref, s32[1,512]{1,0:T(1,128)} %bitcast.36, f32[1,512]{1,0:T(1,128)} %bitcast.37, f32[1,512]{1,0:T(1,128)} %bitcast.38, bf16[1024,512]{1,0:T(8,128)(2,1)} %maximum_bitcast_fusion.qv_hbm, ...), custom_call_target="tpu_custom_call" | custom-call | flops 2684354560 | bytes 4194304 | tf_op jit(solution)/shard_map/pallas_call | solution.py:472
  173.9 4.9 %all-to-all-start.1 = ((bf16[16,64,512]{2,1,0:T(8,128)(2,1)}), bf16[16,64,512]{2,1,0:T(8,128)(2,1)S(1)}, u32[]{:S(2)}, u32[]{:S(2)}) async-start(bf16[16,64,512]{2,1,0:T(8,128)(2,1)} %bitcast.28), calls=%async_computation.1 | async-start | bytes 2097152 | tf_op jit(solution)/shard_map/all_to_all | solution.py:496
  178.9 0.1 copy.40.slot_ref
  179.0 24.7 %all-to-all-done.1 = bf16[16,64,512]{2,1,0:T(8,128)(2,1)S(1)} async-done(((bf16[16,64,512]{2,1,0:T(8,128)(2,1)}), bf16[16,64,512]{2,1,0:T(8,128)(2,1)S(1)}, u32[]{:S(2)}, u32[]{:S(2)}) %all-to-all-start.1) | async-done | bytes 1048608 | tf_op jit(solution)/shard_map/all_to_all | solution.py:496
  203.7 1.5 shard_map.155
  (60 shorter events, 0.3 us)
Async XLA Ops:
  0.0 9.0 %copy-start.11 = (bf16[864,512]{1,0:T(8,128)(2,1)S(1)}, bf16[864,512]{1,0:T(8,128)(2,1)}, u32[]{:S(2)}) copy-start(bf16[864,512]{1,0:T(8,128)(2,1)} %param.16) | copy-start | bytes 2654212
  1.1 7.9 %collective-permute-start = (bf16[13,32,512]{2,1,0:T(8,128)(2,1)S(1)}, bf16[13,32,512]{2,1,0:T(8,128)(2,1)S(1)}, u32[]{:S(2)}, u32[]{:S(2)}) collective-permute-start(bf16[13,32,512]{2,1,0:T(8,128)(2,1)S(1)} %slice.63), channel_id=1, source_target_pairs={{0,1},{1,0},{2,3},{3,2},{4,5},{5,4},{6,7},{7,6},{8,9},{9,8},{10,11... | collective-permute-start | bytes 1277960 | tf_op jit(solution)/shard_map/ppermute | solution.py:352
  6.6 13.0 %copy-start.15 = (bf16[64,512]{1,0:T(8,128)(2,1)S(1)}, bf16[64,512]{1,0:T(8,128)(2,1)}, u32[]{:S(2)}) copy-start(bf16[64,512]{1,0:T(8,128)(2,1)} %get-tuple-element.36) | copy-start | bytes 196612
  6.6 17.0 %copy-start.14 = (bf16[64,512]{1,0:T(8,128)(2,1)S(1)}, bf16[64,512]{1,0:T(8,128)(2,1)}, u32[]{:S(2)}) copy-start(bf16[64,512]{1,0:T(8,128)(2,1)} %get-tuple-element.37) | copy-start | bytes 196612
  6.6 19.0 %copy-start.13 = (s32[512,26]{0,1:T(8,128)S(1)}, s32[512,26]{0,1:T(8,128)}, u32[]{:S(2)}) copy-start(s32[512,26]{0,1:T(8,128)} %param.26) | copy-start | bytes 159748
  6.6 11.5 %collective-permute-start.1 = (bf16[192,512]{1,0:T(8,128)(2,1)}, bf16[192,512]{1,0:T(8,128)(2,1)S(1)}, u32[]{:S(2)}, u32[]{:S(2)}) collective-permute-start(bf16[192,512]{1,0:T(8,128)(2,1)} %get-tuple-element.32), channel_id=1, source_target_pairs={{0,8},{1,9},{2,10},{3,11},{4,12},{5,13},{6,14},{7,15},{8,0},{9,1},... | collective-permute-start | bytes 589832 | tf_op jit(solution)/shard_map/ppermute | solution.py:396
  9.0 35.2 %copy-start.3 = (bf16[512,512]{1,0:T(8,128)(2,1)S(1)}, bf16[512,512]{1,0:T(8,128)(2,1)}, u32[]{:S(2)}) copy-start(bf16[512,512]{1,0:T(8,128)(2,1)} %get-tuple-element.40.ordered_ref) | copy-start | bytes 1572868
  9.2 39.2 %copy-start.12 = (bf16[27,32,512]{2,1,0:T(8,128)(2,1)}, bf16[27,32,512]{2,1,0:T(8,128)(2,1)S(1)}, u32[]{:S(2)}) copy-start(bf16[27,32,512]{2,1,0:T(8,128)(2,1)S(1)} %maximum_select_fusion) | copy-start | bytes 2654212
  18.1 20.9 %collective-permute-start.2 = (bf16[864,512]{1,0:T(8,128)(2,1)S(1)}, bf16[864,512]{1,0:T(8,128)(2,1)}, u32[]{:S(2)}, u32[]{:S(2)}) collective-permute-start(bf16[864,512]{1,0:T(8,128)(2,1)S(1)} %bitcast.31), channel_id=1, source_target_pairs={{0,4},{1,5},{4,8},{5,9},{8,12},{9,13},{12,14},{13,15},{14,10},{15,... | collective-permute-start | bytes 2654216 | tf_op jit(solution)/shard_map/ppermute | solution.py:388
  18.1 22.7 %collective-permute-start.3 = (bf16[864,512]{1,0:T(8,128)(2,1)S(1)}, bf16[864,512]{1,0:T(8,128)(2,1)}, u32[]{:S(2)}, u32[]{:S(2)}) collective-permute-start(bf16[864,512]{1,0:T(8,128)(2,1)S(1)} %bitcast.32), channel_id=1, source_target_pairs={{0,2},{1,3},{4,0},{5,1},{8,4},{9,5},{12,8},{13,9},{14,12},{15,13},... | collective-permute-start | bytes 2654216 | tf_op jit(solution)/shard_map/ppermute | solution.py:389
  19.6 6.7 %collective-permute-start.4 = (bf16[128,512]{1,0:T(8,128)(2,1)S(1)}, bf16[128,512]{1,0:T(8,128)(2,1)S(1)}, u32[]{:S(2)}, u32[]{:S(2)}) collective-permute-start(bf16[128,512]{1,0:T(8,128)(2,1)S(1)} %pad_maximum_fusion), channel_id=1, source_target_pairs={{0,1},{1,2},{2,3},{3,4},{4,5},{5,6},{6,7},{8,9},{9,10},{10,11},{11... | collective-permute-start | bytes 393224 | tf_op jit(solution)/shard_map/ppermute | solution.py:399
  23.7 6.7 %collective-permute-start.5 = (bf16[128,512]{1,0:T(8,128)(2,1)S(1)}, bf16[128,512]{1,0:T(8,128)(2,1)S(1)}, u32[]{:S(2)}, u32[]{:S(2)}) collective-permute-start(bf16[128,512]{1,0:T(8,128)(2,1)S(1)} %pad_maximum_fusion.1), channel_id=1, source_target_pairs={{1,0},{2,1},{3,2},{4,3},{5,4},{6,5},{7,6},{9,8},{10,9},{11,10},{12... | collective-permute-start | bytes 393224 | tf_op jit(solution)/shard_map/ppermute | solution.py:400
  40.9 6.1 %collective-permute-start.11 = (s32[512,26]{1,0:T(8,128)S(1)}, s32[512,26]{1,0:T(8,128)S(1)}, u32[]{:S(2)}, u32[]{:S(2)}) collective-permute-start(s32[512,26]{1,0:T(8,128)S(1)} %copy.36), channel_id=1, source_target_pairs={{0,1},{1,0},{2,3},{3,2},{4,5},{5,4},{6,7},{7,6},{8,9},{9,8},{10,11... | collective-permute-start | bytes 159752 | tf_op jit(solution)/shard_map/ppermute | solution.py:421
  44.8 0.8 copy-start.5
  45.6 14.3 %collective-permute-start.8 = (bf16[1024,256]{1,0:T(8,128)(2,1)S(1)}, bf16[1024,256]{1,0:T(8,128)(2,1)S(1)}, u32[]{:S(2)}, u32[]{:S(2)}) collective-permute-start(bf16[1024,256]{1,0:T(8,128)(2,1)S(1)} %get-tuple-element.45), channel_id=1, source_target_pairs={{0,1},{1,0},{2,3},{3,2},{4,5},{5,4},{6,7},{7,6},{8,9},{9,8},{10,11... | collective-permute-start | bytes 1572872 | tf_op jit(solution)/shard_map/ppermute | solution.py:420
  45.6 21.0 %collective-permute-start.6 = (bf16[864,512]{1,0:T(8,128)(2,1)}, bf16[864,512]{1,0:T(8,128)(2,1)}, u32[]{:S(2)}, u32[]{:S(2)}) collective-permute-start(bf16[864,512]{1,0:T(8,128)(2,1)} %collective-permute-done.2.refs_3_), channel_id=1, source_target_pairs={{0,4},{1,5},{4,8},{5,9},{8,12},{9,13},{12,14},{13,15},{14,10},{15,... | collective-permute-start | bytes 2654216 | tf_op jit(solution)/shard_map/ppermute | solution.py:388
  46.2 23.9 %collective-permute-start.7 = (bf16[864,512]{1,0:T(8,128)(2,1)}, bf16[864,512]{1,0:T(8,128)(2,1)}, u32[]{:S(2)}, u32[]{:S(2)}) collective-permute-start(bf16[864,512]{1,0:T(8,128)(2,1)} %collective-permute-done.3.refs_4_), channel_id=1, source_target_pairs={{0,2},{1,3},{4,0},{5,1},{8,4},{9,5},{12,8},{13,9},{14,12},{15,13},... | collective-permute-start | bytes 2654216 | tf_op jit(solution)/shard_map/ppermute | solution.py:389
  59.9 11.7 %copy-start.19 = (bf16[1024,256]{1,0:T(8,128)(2,1)}, bf16[1024,256]{1,0:T(8,128)(2,1)S(1)}, u32[]{:S(2)}) copy-start(bf16[1024,256]{1,0:T(8,128)(2,1)S(1)} %collective-permute-done.8.table_ref) | copy-start | bytes 1572868
  70.1 22.4 %collective-permute-start.10 = (bf16[864,512]{1,0:T(8,128)(2,1)}, bf16[864,512]{1,0:T(8,128)(2,1)S(1)}, u32[]{:S(2)}, u32[]{:S(2)}) collective-permute-start(bf16[864,512]{1,0:T(8,128)(2,1)} %collective-permute-done.7.refs_6_), channel_id=1, source_target_pairs={{0,2},{1,3},{4,0},{5,1},{8,4},{9,5},{12,8},{13,9},{14,12},{15,13},... | collective-permute-start | bytes 2654216 | tf_op jit(solution)/shard_map/ppermute | solution.py:389
  70.1 22.4 %collective-permute-start.9 = (bf16[864,512]{1,0:T(8,128)(2,1)}, bf16[864,512]{1,0:T(8,128)(2,1)S(1)}, u32[]{:S(2)}, u32[]{:S(2)}) collective-permute-start(bf16[864,512]{1,0:T(8,128)(2,1)} %collective-permute-done.6.refs_5_), channel_id=1, source_target_pairs={{0,4},{1,5},{4,8},{5,9},{8,12},{9,13},{12,14},{13,15},{14,10},{15,... | collective-permute-start | bytes 2654216 | tf_op jit(solution)/shard_map/ppermute | solution.py:388
  92.5 2.8 %copy-start.6 = (bf16[864,512]{1,0:T(8,128)(2,1)}, bf16[864,512]{1,0:T(8,128)(2,1)S(1)}, u32[]{:S(2)}) copy-start(bf16[864,512]{1,0:T(8,128)(2,1)S(1)} %collective-permute-done.10.refs_3_) | copy-start | bytes 2654212
  92.5 2.8 %copy-start.7 = (bf16[864,512]{1,0:T(8,128)(2,1)}, bf16[864,512]{1,0:T(8,128)(2,1)S(1)}, u32[]{:S(2)}) copy-start(bf16[864,512]{1,0:T(8,128)(2,1)S(1)} %collective-permute-done.9.refs_2_) | copy-start | bytes 2654212
  92.5 10.4 %collective-permute-start.12 = (bf16[432,512]{1,0:T(8,128)(2,1)S(1)}, bf16[432,512]{1,0:T(8,128)(2,1)S(1)}, u32[]{:S(2)}, u32[]{:S(2)}) collective-permute-start(bf16[432,512]{1,0:T(8,128)(2,1)S(1)} %slice.74), channel_id=1, source_target_pairs={{0,4},{1,5},{4,8},{5,9},{8,12},{9,13},{12,14},{13,15},{14,10},{15,... | collective-permute-start | bytes 1327112 | tf_op jit(solution)/shard_map/ppermute | solution.py:388
  93.8 9.8 %collective-permute-start.13 = (bf16[432,512]{1,0:T(8,128)(2,1)S(1)}, bf16[432,512]{1,0:T(8,128)(2,1)S(1)}, u32[]{:S(2)}, u32[]{:S(2)}) collective-permute-start(bf16[432,512]{1,0:T(8,128)(2,1)S(1)} %slice.75), channel_id=1, source_target_pairs={{0,2},{1,3},{4,0},{5,1},{8,4},{9,5},{12,8},{13,9},{14,12},{15,13},... | collective-permute-start | bytes 1327112 | tf_op jit(solution)/shard_map/ppermute | solution.py:389
  102.9 0.8 copy-start.8
  103.5 0.8 copy-start.9
  104.3 7.4 %copy-start.16 = (s32[512]{0:T(512)S(1)}, s32[512]{0:T(512)}, u32[]{:S(2)}) copy-start(s32[512]{0:T(512)} %param.27) | copy-start | bytes 6148
  108.7 7.9 %collective-permute-start.14 = (f32[512,512]{1,0:T(8,128)}, f32[512,512]{1,0:T(8,128)S(1)}, u32[]{:S(2)}, u32[]{:S(2)}) collective-permute-start(f32[512,512]{1,0:T(8,128)} %shard_map.152), channel_id=1, source_target_pairs={{0,1},{1,0},{2,3},{3,2},{4,5},{5,4},{6,7},{7,6},{8,9},{9,8},{10,11... | collective-permute-start | bytes 3145736 | tf_op jit(solution)/shard_map/ppermute | solution.py:449
  112.1 4.6 %copy-start.1 = (bf16[512,512]{1,0:T(8,128)(2,1)S(1)}, bf16[512,512]{1,0:T(8,128)(2,1)}, u32[]{:S(2)}) copy-start(bf16[512,512]{1,0:T(8,128)(2,1)} %features_ref.3) | copy-start | bytes 1572868
  112.1 4.6 %copy-start.2 = (bf16[512,512]{1,0:T(8,128)(2,1)S(1)}, bf16[512,512]{1,0:T(8,128)(2,1)}, u32[]{:S(2)}) copy-start(bf16[512,512]{1,0:T(8,128)(2,1)} %weight_ref.1) | copy-start | bytes 1572868
  112.1 4.6 %copy-start.4 = (f32[512]{0:T(512)S(1)}, f32[512]{0:T(512)}, u32[]{:S(2)}) copy-start(f32[512]{0:T(512)} %param.18) | copy-start | bytes 6148
  116.7 1.2 copy-start
  120.2 4.6 %copy-start.10 = (bf16[512,1536]{1,0:T(8,128)(2,1)S(1)}, bf16[512,1536]{1,0:T(8,128)(2,1)}, u32[]{:S(2)}) copy-start(bf16[512,1536]{1,0:T(8,128)(2,1)} %param.20) | copy-start | bytes 4718596
  120.2 29.5 %all-to-all-start = ((bf16[16,64,512]{2,1,0:T(8,128)(2,1)}), bf16[16,64,512]{2,1,0:T(8,128)(2,1)}, u32[]{:S(2)}, u32[]{:S(2)}) async-start(bf16[16,64,512]{2,1,0:T(8,128)(2,1)} %bitcast.9), calls=%async_computation | async-start | bytes 2097152 | tf_op jit(solution)/shard_map/all_to_all | solution.py:465
  124.8 1.3 copy-start.18
  126.4 23.3 %copy-start.17 = (s32[512]{0:T(512)}, s32[512]{0:T(512)S(1)}, u32[]{:S(2)}) copy-start(s32[512]{0:T(512)S(1)} %multiply_add_fusion) | copy-start | bytes 6148
  173.9 29.8 %all-to-all-start.1 = ((bf16[16,64,512]{2,1,0:T(8,128)(2,1)}), bf16[16,64,512]{2,1,0:T(8,128)(2,1)S(1)}, u32[]{:S(2)}, u32[]{:S(2)}) async-start(bf16[16,64,512]{2,1,0:T(8,128)(2,1)} %bitcast.28), calls=%async_computation.1 | async-start | bytes 2097152 | tf_op jit(solution)/shard_map/all_to_all | solution.py:496

commit v8 on v7

--- a/solution.py
+++ b/solution.py
@@ -45,7 +45,7 @@
     )
 
 
-def faces_kernel(unit, features_ref, rows_ref, ordered_ref, *face_refs):
+def faces_kernel(unit, core_ref, features_ref, rows_ref, own_ref, other_ref, *face_refs):
     points, width = features_ref.shape
     half = width // 2
     place = lax.broadcasted_iota(jnp.int32, (width, width), 1)
@@ -53,7 +53,10 @@
     source = (within // unit) * (2 * unit) + (place // half) * unit + lax.rem(place, unit)
     channel = lax.broadcasted_iota(jnp.int32, (width, width), 0)
     ordered = dot(features_ref[...], one_hot(channel == source)).astype(BF16)
-    ordered_ref[...] = ordered
+    first, second = ordered[:, :half], ordered[:, half:]
+    even = core_ref[0] == 0
+    own_ref[...] = jnp.where(even, first, second)
+    other_ref[...] = jnp.where(even, second, first)
     row_ids = lax.broadcasted_iota(jnp.int32, (rows_ref.shape[0], points), 1)
     rows = dot(one_hot(rows_ref[...] == row_ids), ordered).astype(BF16)
     taken = 0
@@ -62,52 +65,57 @@
         taken += ref.shape[0]
 
 
-def table_kernel(flags_ref, ordered_ref, side_ref, behind_ref, ahead_ref, own_ref, other_ref, held):
+def received_kernel(flags_ref, side_ref, behind_ref, ahead_ref, own_ref, other_ref):
     size = behind_ref.shape[0] // 2
-    points = ordered_ref.shape[0]
     half = own_ref.shape[1]
     lower, even = flags_ref[0] == 1, flags_ref[1] == 0
-    held[:points] = ordered_ref[...]
-    across = (ahead_ref[size:], side_ref[size : 2 * size], behind_ref[size:])
-    zero = jnp.zeros_like(across[0])
-    for at, rows in enumerate(across):
-        start = points + at * size
-        held[start : start + size] = jnp.where(lower, rows, zero)
-        start += 5 * size
-        held[start : start + size] = jnp.where(lower, zero, rows)
-    held[points + 3 * size : points + 4 * size] = ahead_ref[:size]
-    held[points + 4 * size : points + 5 * size] = behind_ref[:size]
-    first, second = held[:, :half], held[:, half:]
-    own_ref[...] = jnp.where(even, first, second)
-    other_ref[...] = jnp.where(even, second, first)
-
-
-def gather_kernel(taps, rows_ref, table_ref, out_ref):
-    half = table_ref.shape[1]
+    across = [ahead_ref[size:], side_ref[size : 2 * size], behind_ref[size:]]
+    along = [ahead_ref[:size], behind_ref[:size]]
+    for at, (low, high) in enumerate(zip(across + along, along + across)):
+        rows = jnp.where(lower, low, high)
+        first, second = rows[:, :half], rows[:, half:]
+        own_ref[at * size : (at + 1) * size] = jnp.where(even, first, second)
+        other_ref[at * size : (at + 1) * size] = jnp.where(even, second, first)
+
+
+def gather_kernel(taps, start_ref, rows_ref, table_ref, *refs):
+    out_ref = refs[-1]
+    height, half = table_ref.shape
     lane = lax.broadcasted_iota(jnp.int32, rows_ref.shape, 1)
-    row_ids = lax.broadcasted_iota(jnp.int32, (1, table_ref.shape[0]), 1).astype(F32)
+    row_ids = (lax.broadcasted_iota(jnp.int32, (1, height), 1) + start_ref[0]).astype(F32)
     for at in range(taps):
         chosen = lane == taps * pl.program_id(0) + at
         column = jnp.sum(jnp.where(chosen, rows_ref[...], 0.0), axis=1, keepdims=True)
-        taken = dot(one_hot(column == row_ids), table_ref[...]).astype(BF16)
-        out_ref[:, at * half : (at + 1) * half] = taken
-
-
-def gather_block(rows, table):
+        taken = dot(one_hot(column == row_ids), table_ref[...])
+        place = slice(at * half, (at + 1) * half)
+        if len(refs) > 1:
+            taken += refs[0][:, place].astype(F32)
+        out_ref[:, place] = taken.astype(BF16)
+
+
+def gather_part(start, rows, table, before=None):
     points, lanes = rows.shape
     height, half = table.shape
     taps = 3
     whole = lambda step: (0, 0)
+    block = pl.BlockSpec((points, taps * half), lambda step: (0, step))
+    extra = [] if before is None else [before]
     return call(
         functools.partial(gather_kernel, taps),
         jax.ShapeDtypeStruct((points, TAPS * half), BF16),
         60,
         2 * TAPS * points * height * half,
-        2 * TAPS * points * half,
+        2 * TAPS * points * half * (1 + len(extra)),
         grid=(TAPS // taps,),
-        in_specs=[pl.BlockSpec((points, lanes), whole), pl.BlockSpec((height, half), whole)],
-        out_specs=pl.BlockSpec((points, taps * half), lambda step: (0, step)),
-    )(rows, table)
+        in_specs=[
+            pl.BlockSpec(memory_space=pltpu.SMEM),
+            pl.BlockSpec((points, lanes), whole),
+            pl.BlockSpec((height, half), whole),
+        ]
+        + [block] * len(extra),
+        out_specs=block,
+        input_output_aliases={3: 0} if extra else {},
+    )(start, rows, table, *extra)
 
 
 def conv_kernel(slots, blocks, first, places_ref, *refs):
@@ -363,14 +371,17 @@
         face_list = face_rows.reshape(-1, 1)
         counts = (1,) * 8
     size = face_rows.shape[2]
-    ordered, *faces = call(
+    own_local, other_half, *faces = call(
         functools.partial(faces_kernel, unit),
-        [jax.ShapeDtypeStruct((points, width), BF16)]
+        [jax.ShapeDtypeStruct((points, half), BF16)] * 2
         + [jax.ShapeDtypeStruct((count * size, width), BF16) for count in counts],
         60,
         4 * points * width * width,
         8 * points * width,
-    )(features, face_list)
+        in_specs=[pl.BlockSpec(memory_space=pltpu.SMEM)] + [pl.BlockSpec()] * 2,
+    )(core.reshape(1), features, face_list)
+    other_local = lax.ppermute(other_half, "blocks", partner)
+    other_neighbours = lax.ppermute(neighbours, "blocks", partner)
 
     rows = mine.shape[0]
     length = -(-(rows + 127) // 128) * 128 if round_trip else rows * (devices // 2)
@@ -389,40 +400,47 @@
         on.append(lax.ppermute(second, "blocks", on_pairs))
         return tied[2:]
 
-    sent_neighbours = neighbours
     if round_trip:
         lists, back_list, on_list = faces
         side = face_pairs(devices, 1, 0) + face_pairs(devices, -1, 0)
-        (lists,) = pass_on(lax.ppermute(lists, "blocks", side))
+        lists = lax.ppermute(lists, "blocks", side)
+        other_local, other_neighbours = pass_on(other_local, other_neighbours)
+    own_rows, other_rows = padded_taps(neighbours), padded_taps(other_neighbours)
+    nothing = jnp.zeros((1,), jnp.int32)
+    own_stacked = gather_part(nothing, own_rows, own_local)
+    other_stacked = gather_part(nothing, other_rows, other_local)
+    if round_trip:
+        own_stacked, lists = lax.optimization_barrier((own_stacked, lists))
         to_on = jnp.concatenate([on_list, lists[2 * size :]])
         to_back = jnp.concatenate([back_list, lists[:size]])
         behind = lax.ppermute(to_on, "blocks", face_pairs(devices, 0, 1))
         ahead = lax.ppermute(to_back, "blocks", face_pairs(devices, 0, -1))
-        sent_neighbours, lists, behind, ahead = pass_on(neighbours, lists, behind, ahead)
-        height = points + 8 * size
-        own_table, other_half = call(
-            table_kernel,
-            [jax.ShapeDtypeStruct((height, half), BF16)] * 2,
+        own_stacked, other_stacked, lists, behind, ahead = pass_on(
+            own_stacked, other_stacked, lists, behind, ahead
+        )
+        own_remote, other_half = call(
+            received_kernel,
+            [jax.ShapeDtypeStruct((5 * size, half), BF16)] * 2,
             32,
             0,
-            4 * height * width,
-            in_specs=[pl.BlockSpec(memory_space=pltpu.SMEM)] + [pl.BlockSpec()] * 4,
-            scratch_shapes=[pltpu.VMEM((height, width), BF16)],
-        )(jnp.stack([lower.astype(jnp.int32), core]), ordered, lists, behind, ahead)
+            20 * size * width,
+            in_specs=[pl.BlockSpec(memory_space=pltpu.SMEM)] + [pl.BlockSpec()] * 3,
+        )(jnp.stack([lower.astype(jnp.int32), core]), lists, behind, ahead)
+        start = jnp.where(lower, points, points + 3 * size).reshape(1)
     else:
-        got = [
-            lax.ppermute(faces[k], "blocks", face_pairs(devices, STEPS_X[k], STEPS_Y[k]))
-            for k in range(8)
-        ]
-        table = jnp.concatenate([ordered, *got], axis=0)
-        own_table = lax.dynamic_slice(table, (0, core * half), (table.shape[0], half))
-        other_half = lax.dynamic_slice(table, (0, (1 - core) * half), (table.shape[0], half))
-    other_table = lax.ppermute(other_half, "blocks", partner)
-    other_neighbours = lax.ppermute(sent_neighbours, "blocks", partner)
-    own_stacked = gather_block(padded_taps(neighbours), own_table)
-    own_stacked, other_table = pass_on(own_stacked, other_table)
-    other_stacked = gather_block(padded_taps(other_neighbours), other_table)
-    stacked = other_stacked, own_stacked
+        received = jnp.concatenate(
+            [
+                lax.ppermute(faces[k], "blocks", face_pairs(devices, STEPS_X[k], STEPS_Y[k]))
+                for k in range(8)
+            ]
+        )
+        own_remote = lax.dynamic_slice(received, (0, core * half), (8 * size, half))
+        other_half = lax.dynamic_slice(received, (0, (1 - core) * half), (8 * size, half))
+        start = nothing + points
+    other_remote = lax.ppermute(other_half, "blocks", partner)
+    own_stacked = gather_part(start, own_rows, own_remote, own_stacked)
+    other_stacked = gather_part(start, other_rows, other_remote, other_stacked)
+    stacked = pass_on(other_stacked, own_stacked)
     if round_trip:
         places = jnp.array(places, jnp.int32)[index]
         early = [[mine], [back[1]], [on[1]], [back[2]], [on[2]]]
@@ -451,7 +469,7 @@
     outgoing = call(
         mix_kernel,
         jax.ShapeDtypeStruct((slots, width), BF16),
-        32,
+        60,
         2 * points * width * (width + slots),
         8 * points * width,
     )(

time: 206 us -> 204 us (level)
  waiting for transfers between devices: 80.9 us -> 58.4 us
  Pallas kernels: 79.5 us -> 98.2 us
    pallas_call x4 -> x6, Pallas kernels: 26 us -> 44.8 us  [the longest x4 40.1 us: gather_part(): call(functools.partial(gather_kernel, taps), jax.ShapeDtypeStruct((points...]
    ppermute x3 -> x4, waiting for transfers between devices: 8.88 us -> 0.01 us  [the longest x1 0.01 us: body(): other_local = lax.ppermute(other_half, 'blocks', partner)]
    ppermute x4, waiting for transfers between devices: 16.1 us -> 10.5 us  [pass_on(): back.append(lax.ppermute(first, 'blocks', back_pairs))]
    ppermute x1, waiting for transfers between devices: 4.03 us -> 0.01 us  [body(): ahead = lax.ppermute(to_back, 'blocks', face_pairs(devices, 0, -1))]
    ppermute x4, waiting for transfers between devices: 5.87 us -> 1.85 us  [pass_on(): on.append(lax.ppermute(second, 'blocks', on_pairs))]
    ppermute x3 -> x4, starting transfers between devices: 4.59 us -> 3.62 us  [the longest x1 2.32 us: body(): lists = lax.ppermute(lists, 'blocks', side)]
  transfers between devices with their start and end apart: 17 -> 18, of which waited for: 10 -> 7; matrix products, arithmetic and copies ran while one was open for 5% -> 6% of each run, Pallas kernels for 23% -> 31%
where the time goes in v8:
time: 204 us; the launch traced here: 203 us
  Pallas kernels  98.2 us (48%)
  waiting for transfers between devices  58.4 us (29%)
  starting transfers between devices  30.2 us (15%)
  local copies, waits for them, and re-layouts  11.3 us (6%)
  other arithmetic  4.36 us (2%)
    pallas_call x4, Pallas kernels, gather_part(): call(functools.partial(gather_kernel, taps), jax.ShapeDtypeStruct((points...  40.1 us
    pallas_call x4, Pallas kernels, conv_part(): call(functools.partial(conv_kernel, slots, blocks, before is None), [jax....  25.2 us
    all_to_all x1, waiting for transfers between devices, body(): lax.all_to_all(back.reshape(devices, capacity, width), 'blocks', split_ax...  24.7 us
    pallas_call x1, Pallas kernels, body(): call(block_kernel, jax.ShapeDtypeStruct((slots, width), BF16), 60, 20 * p...  24.2 us
    all_to_all x1, waiting for transfers between devices, body(): lax.all_to_all(outgoing.reshape(devices, capacity, width), 'blocks', spli...  21.3 us
    ppermute x4, waiting for transfers between devices, pass_on(): back.append(lax.ppermute(first, 'blocks', back_pairs))  10.5 us
    all_to_all x1, starting transfers between devices, body(): lax.all_to_all(outgoing.reshape(devices, capacity, width), 'blocks', spli...  5.39 us
    all_to_all x1, starting transfers between devices, body(): lax.all_to_all(back.reshape(devices, capacity, width), 'blocks', split_ax...  4.95 us
  transfers between devices with their start and end apart: 18, of which 7 were waited for; matrix products, arithmetic and copies ran while one was open for 6% of the time, Pallas kernels for 31%

profile of v8, /device:TPU:9, one launch (start us, length us, event | category | flops | bytes accessed | tf_op | source)
XLA Modules:
  0.0 202.8 jit_solution(1178985192365669778)
XLA Ops:
  0.0 1.1 slice.63
  1.1 0.7 collective-permute-start
  1.9 0.8 select_bitcast_fusion
  2.6 0.7 slice_bitcast_fusion
  3.3 0.8 reshape.93.rows_ref
  4.2 2.4 %shard_map.145 = (bf16[512,256]{1,0:T(8,128)(2,1)}, bf16[512,256]{1,0:T(8,128)(2,1)}, bf16[192,512]{1,0:T(8,128)(2,1)}, bf16[64,512]{1,0:T(8,128)(2,1)}, bf16[64,512]{1,0:T(8,128)(2,1)}) custom-call(s32[1]{0:T(128)} %bitcast.3.core_ref, bf16[512,512]{1,0:T(8,128)(2,1)} %features_ref.3, s32[320,1]{1,0:T(8,128)} %reshape.93.rows_ref), custom_call_target="tpu_custom_call" | custom-call | flops 536870912 | bytes 2097152 | tf_op jit(solution)/shard_map/pallas_call | solution.py:374
  6.6 0.1 copy.36
  6.8 0.6 collective-permute-start.2
  7.3 2.3 %collective-permute-start.5 = (bf16[192,512]{1,0:T(8,128)(2,1)}, bf16[192,512]{1,0:T(8,128)(2,1)S(1)}, u32[]{:S(2)}, u32[]{:S(2)}) collective-permute-start(bf16[192,512]{1,0:T(8,128)(2,1)} %get-tuple-element.41), channel_id=1, source_target_pairs={{0,8},{1,9},{2,10},{3,11},{4,12},{5,13},{6,14},{7,15},{8,0},{9,1},... | collective-permute-start | bytes 589832 | tf_op jit(solution)/shard_map/ppermute | solution.py:406
  9.7 0.1 copy.37
  9.9 0.1 copy.38
  10.0 0.1 pad.15.clone
  10.1 0.1 maximum_select_fusion
  10.3 0.1 fusion.6
  10.5 1.5 collective-permute-start.4
  11.9 1.1 add_convert_fusion.1
  13.0 8.9 %shard_map.146.refs_0_ = bf16[512,6912]{1,0:T(8,128)(2,1)} custom-call(s32[1]{0:T(128)} %constant.38.clone.1.start_ref, f32[512,128]{1,0:T(8,128)} %get-tuple-element.73.rows_ref, bf16[512,256]{1,0:T(8,128)(2,1)} %get-tuple-element.40.table_ref), custom_call_target="tpu_custom_call" | custom-call | flops 3623878656 | bytes 7077888 | tf_op jit(solution)/shard_map/pallas_call | solution.py:103
  21.9 3.9 %collective-permute-start.6 = (bf16[128,512]{1,0:T(8,128)(2,1)S(1)}, bf16[128,512]{1,0:T(8,128)(2,1)S(1)}, u32[]{:S(2)}, u32[]{:S(2)}) collective-permute-start(bf16[128,512]{1,0:T(8,128)(2,1)S(1)} %pad_maximum_fusion), channel_id=1, source_target_pairs={{0,1},{1,2},{2,3},{3,4},{4,5},{5,6},{6,7},{8,9},{9,10},{10,11},{11... | collective-permute-start | bytes 393224 | tf_op jit(solution)/shard_map/ppermute | solution.py:416
  25.9 1.9 collective-permute-start.7
  27.8 8.9 %shard_map.147.refs_0_ = bf16[512,6912]{1,0:T(8,128)(2,1)} custom-call(s32[1]{0:T(128)} %constant.38.clone.1.start_ref, f32[512,128]{1,0:T(8,128)} %get-tuple-element.72.rows_ref, bf16[512,256]{1,0:T(8,128)(2,1)} %collective-permute-done.1.table_ref), custom_call_target="tpu_custom_call" | custom-call | flops 3623878656 | bytes 7077888 | tf_op jit(solution)/shard_map/pallas_call | solution.py:103
  36.7 0.9 collective-permute-done.3.refs_3_
  37.6 2.2 %collective-permute-start.8 = (bf16[864,512]{1,0:T(8,128)(2,1)S(1)}, bf16[864,512]{1,0:T(8,128)(2,1)S(1)}, u32[]{:S(2)}, u32[]{:S(2)}) collective-permute-start(bf16[864,512]{1,0:T(8,128)(2,1)S(1)} %collective-permute-done.3.refs_3_), channel_id=1, source_target_pairs={{0,4},{1,5},{4,8},{5,9},{8,12},{9,13},{12,14},{13,15},{14,10},{15,... | collective-permute-start | bytes 2654216 | tf_op jit(solution)/shard_map/ppermute | solution.py:399
  39.9 0.1 pad_add_fusion.1.flags_ref
  39.9 0.6 shard_map.148
  40.5 0.6 copy-done
  41.2 0.7 collective-permute-start.10
  41.9 11.1 %shard_map.150.refs_1_.refs_0_ = bf16[512,6912]{1,0:T(8,128)(2,1)} custom-call(s32[1]{0:T(128)} %bitcast.6.start_ref, f32[512,128]{1,0:T(8,128)} %get-tuple-element.73.rows_ref, bf16[320,256]{1,0:T(8,128)(2,1)} %copy-done, bf16[512,6912]{1,0:T(8,128)(2,1)} %shard_map.146.refs_0_), custom_call_target="tpu_custom_call", output_to_operand_aliasing={{}: (3, {})} | custom-call | flops 2264924160 | bytes 14155776 | tf_op jit(solution)/shard_map/pallas_call | solution.py:103
  53.1 0.7 copy-done.10
  53.7 11.1 %shard_map.149.refs_0_ = bf16[512,6912]{1,0:T(8,128)(2,1)} custom-call(s32[1]{0:T(128)} %bitcast.6.start_ref, f32[512,128]{1,0:T(8,128)} %get-tuple-element.72.rows_ref, bf16[320,256]{1,0:T(8,128)(2,1)} %copy-done.10, bf16[512,6912]{1,0:T(8,128)(2,1)} %shard_map.147.refs_0_), custom_call_target="tpu_custom_call", output_to_operand_aliasing={{}: (3, {})} | custom-call | flops 2264924160 | bytes 14155776 | tf_op jit(solution)/shard_map/pallas_call | solution.py:103
  64.9 1.8 collective-permute-start.11
  66.7 0.7 constant_dynamic-slice_fusion
  67.4 0.6 reshape.79.places_ref
  68.0 9.4 %shard_map.151 = (f32[512,512]{1,0:T(8,128)}, f32[512,512]{1,0:T(8,128)}) custom-call(s32[10]{0:T(128)} %reshape.79.places_ref, bf16[512,6912]{1,0:T(8,128)(2,1)} %shard_map.149.refs_0_, bf16[512,6912]{1,0:T(8,128)(2,1)} %shard_map.150.refs_1_.refs_0_, bf16[864,512]{1,0:T(8,128)(2,1)} %bitcast.32, bf16[864,512]{1,0:T(8,128)(2,1)} %copy-done.17, ...), custom_call_target="tpu_custom_call" | custom-call | flops 5368709120 | bytes 15728640 | tf_op jit(solution)/shard_map/pallas_call | solution.py:172
  77.4 8.8 %collective-permute-done.11.refs_2_ = bf16[864,512]{1,0:T(8,128)(2,1)S(1)} collective-permute-done((bf16[864,512]{1,0:T(8,128)(2,1)S(1)}, bf16[864,512]{1,0:T(8,128)(2,1)S(1)}, u32[]{:S(2)}, u32[]{:S(2)}) %collective-permute-start.11) | collective-permute-done | bytes 884768 | tf_op jit(solution)/shard_map/ppermute | solution.py:399
  86.2 1.6 collective-permute-done.12.refs_3_
  87.9 0.3 collective-permute-start.13
  88.2 1.5 collective-permute-start.14
  89.7 0.6 reshape.80.places_ref
  90.3 0.5 slice_bitcast_fusion.1.places_ref
  90.8 6.9 %shard_map.152 = (f32[512,512]{1,0:T(8,128)}, f32[512,512]{1,0:T(8,128)}) custom-call(s32[4]{0:T(128)} %reshape.80.places_ref, bf16[512,6912]{1,0:T(8,128)(2,1)} %shard_map.149.refs_0_, bf16[512,6912]{1,0:T(8,128)(2,1)} %shard_map.150.refs_1_.refs_0_, bf16[864,512]{1,0:T(8,128)(2,1)} %copy-done.1, ...), custom_call_target="tpu_custom_call", output_to_operand_aliasing={{0}: (5, {}), {1}: (6, {})} | custom-call | flops 2147483648 | bytes 6291456 | tf_op jit(solution)/shard_map/pallas_call | solution.py:172
  97.7 0.8 collective-permute-done.13.refs_1_
  98.5 0.2 collective-permute-done.14.refs_2_
  98.7 0.5 copy-done.3
  99.3 0.2 copy-done.4
  99.5 4.4 %shard_map.154 = f32[512,512]{1,0:T(8,128)} custom-call(s32[2]{0:T(128)} %slice_bitcast_fusion.1.places_ref, bf16[512,6912]{1,0:T(8,128)(2,1)} %shard_map.149.refs_0_, bf16[432,512]{1,0:T(8,128)(2,1)} %copy-done.3, bf16[432,512]{1,0:T(8,128)(2,1)} %copy-done.4, f32[512,512]{1,0:T(8,128)} %get-tuple-element.68.refs_3_), custom_call_target="tpu_custom_call", output_to_operand_aliasing={{}: (4, {})} | custom-call | flops 536870912 | bytes 2097152 | tf_op jit(solution)/shard_map/pallas_call | solution.py:172
  103.9 2.4 %collective-permute-start.15 = (f32[512,512]{1,0:T(8,128)}, f32[512,512]{1,0:T(8,128)S(1)}, u32[]{:S(2)}, u32[]{:S(2)}) collective-permute-start(f32[512,512]{1,0:T(8,128)} %shard_map.154), channel_id=1, source_target_pairs={{0,1},{1,0},{2,3},{3,2},{4,5},{5,4},{6,7},{7,6},{8,9},{9,8},{10,11... | collective-permute-start | bytes 3145736 | tf_op jit(solution)/shard_map/ppermute | solution.py:467
  106.3 0.3 convert_reduce_fusion.1
  106.7 0.6 multiply_add_fusion.1
  107.3 4.4 %shard_map.153.own_ref = f32[512,512]{1,0:T(8,128)} custom-call(s32[2]{0:T(128)} %slice_bitcast_fusion.1.places_ref, bf16[512,6912]{1,0:T(8,128)(2,1)} %shard_map.150.refs_1_.refs_0_, bf16[432,512]{1,0:T(8,128)(2,1)} %copy-done.3, bf16[432,512]{1,0:T(8,128)(2,1)} %copy-done.4, f32[512,512]{1,0:T(8,128)} %get-tuple-element.67.refs_3_), custom_call_target="tpu_custom_call", output_to_operand_aliasing={{}: (4, {})} | custom-call | flops 536870912 | bytes 2097152 | tf_op jit(solution)/shard_map/pallas_call | solution.py:172
  111.7 1.0 copy-done.6
  112.7 4.2 %shard_map.155 = bf16[1024,512]{1,0:T(8,128)(2,1)} custom-call(f32[512,512]{1,0:T(8,128)} %shard_map.153.own_ref, f32[512,512]{1,0:T(8,128)} %copy-done.6, bf16[512,512]{1,0:T(8,128)(2,1)} %features_ref.3, bf16[512,512]{1,0:T(8,128)(2,1)} %weight_ref.1, f32[1,512]{1,0:T(1,128)} %bitcast.38, s32[1,512]{1,0:T(1,128)} %bitcast.34), custom_call_target="tpu_custom_call" | custom-call | flops 805306368 | bytes 2097152 | tf_op jit(solution)/shard_map/pallas_call | solution.py:469
  116.9 5.4 %all-to-all-start = ((bf16[16,64,512]{2,1,0:T(8,128)(2,1)}), bf16[16,64,512]{2,1,0:T(8,128)(2,1)}, u32[]{:S(2)}, u32[]{:S(2)}) async-start(bf16[16,64,512]{2,1,0:T(8,128)(2,1)} %bitcast.26), calls=%async_computation | async-start | bytes 2097152 | tf_op jit(solution)/shard_map/all_to_all | solution.py:483
  122.3 1.0 fusion.5
  123.2 0.2 copy.43
  123.4 0.2 copy.44
  123.7 0.2 convert_reduce_fusion
  123.9 0.9 copy.41.slot_col_ref
  124.8 1.1 maximum_bitcast_fusion.qv_hbm
  125.9 21.3 %all-to-all-done = bf16[16,64,512]{2,1,0:T(8,128)(2,1)} async-done(((bf16[16,64,512]{2,1,0:T(8,128)(2,1)}), bf16[16,64,512]{2,1,0:T(8,128)(2,1)}, u32[]{:S(2)}, u32[]{:S(2)}) %all-to-all-start) | async-done | bytes 1048608 | tf_op jit(solution)/shard_map/all_to_all | solution.py:483
  147.2 24.2 %shard_map.156 = bf16[1024,512]{1,0:T(8,128)(2,1)} custom-call(bf16[1024,512]{1,0:T(8,128)(2,1)} %bitcast.11.arrived_ref, s32[512,1]{1,0:T(8,128)} %copy.41.slot_col_ref, s32[1,512]{1,0:T(1,128)} %bitcast.37, f32[1,512]{1,0:T(1,128)} %bitcast.39, f32[1,512]{1,0:T(1,128)} %bitcast.40, bf16[1024,512]{1,0:T(8,128)(2,1)} %maximum_bitcast_fusion.qv_hbm, ...), custom_call_target="tpu_custom_call" | custom-call | flops 2684354560 | bytes 4194304 | tf_op jit(solution)/shard_map/pallas_call | solution.py:490
  171.4 5.0 %all-to-all-start.1 = ((bf16[16,64,512]{2,1,0:T(8,128)(2,1)}), bf16[16,64,512]{2,1,0:T(8,128)(2,1)S(1)}, u32[]{:S(2)}, u32[]{:S(2)}) async-start(bf16[16,64,512]{2,1,0:T(8,128)(2,1)} %bitcast.27), calls=%async_computation.1 | async-start | bytes 2097152 | tf_op jit(solution)/shard_map/all_to_all | solution.py:514
  176.4 0.1 copy.42.slot_ref
  176.6 24.7 %all-to-all-done.1 = bf16[16,64,512]{2,1,0:T(8,128)(2,1)S(1)} async-done(((bf16[16,64,512]{2,1,0:T(8,128)(2,1)}), bf16[16,64,512]{2,1,0:T(8,128)(2,1)S(1)}, u32[]{:S(2)}, u32[]{:S(2)}) %all-to-all-start.1) | async-done | bytes 1048608 | tf_op jit(solution)/shard_map/all_to_all | solution.py:514
  201.2 1.5 shard_map.157
  (62 shorter events, 0.4 us)
Async XLA Ops:
  0.0 9.7 %copy-start.7 = (bf16[864,512]{1,0:T(8,128)(2,1)S(1)}, bf16[864,512]{1,0:T(8,128)(2,1)}, u32[]{:S(2)}) copy-start(bf16[864,512]{1,0:T(8,128)(2,1)} %param.16) | copy-start | bytes 2654212
  0.0 6.6 %copy-start.9 = (s32[512,26]{0,1:T(8,128)S(1)}, s32[512,26]{0,1:T(8,128)}, u32[]{:S(2)}) copy-start(s32[512,26]{0,1:T(8,128)} %param.26) | copy-start | bytes 159748
  1.1 9.0 %collective-permute-start = (bf16[13,32,512]{2,1,0:T(8,128)(2,1)S(1)}, bf16[13,32,512]{2,1,0:T(8,128)(2,1)S(1)}, u32[]{:S(2)}, u32[]{:S(2)}) collective-permute-start(bf16[13,32,512]{2,1,0:T(8,128)(2,1)S(1)} %slice.63), channel_id=1, source_target_pairs={{0,1},{1,0},{2,3},{3,2},{4,5},{5,4},{6,7},{7,6},{8,9},{9,8},{10,11... | collective-permute-start | bytes 1277960 | tf_op jit(solution)/shard_map/ppermute | solution.py:360
  6.6 3.6 %collective-permute-start.1 = (bf16[512,256]{1,0:T(8,128)(2,1)}, bf16[512,256]{1,0:T(8,128)(2,1)}, u32[]{:S(2)}, u32[]{:S(2)}) collective-permute-start(bf16[512,256]{1,0:T(8,128)(2,1)} %get-tuple-element.37), channel_id=1, source_target_pairs={{0,1},{1,0},{2,3},{3,2},{4,5},{5,4},{6,7},{7,6},{8,9},{9,8},{10,11... | collective-permute-start | bytes 786440 | tf_op jit(solution)/shard_map/ppermute | solution.py:383
  6.8 3.5 %collective-permute-start.2 = (s32[512,26]{1,0:T(8,128)S(1)}, s32[512,26]{1,0:T(8,128)S(1)}, u32[]{:S(2)}, u32[]{:S(2)}) collective-permute-start(s32[512,26]{1,0:T(8,128)S(1)} %copy.36), channel_id=1, source_target_pairs={{0,1},{1,0},{2,3},{3,2},{4,5},{5,4},{6,7},{7,6},{8,9},{9,8},{10,11... | collective-permute-start | bytes 159752 | tf_op jit(solution)/shard_map/ppermute | solution.py:384
  7.3 14.6 %collective-permute-start.5 = (bf16[192,512]{1,0:T(8,128)(2,1)}, bf16[192,512]{1,0:T(8,128)(2,1)S(1)}, u32[]{:S(2)}, u32[]{:S(2)}) collective-permute-start(bf16[192,512]{1,0:T(8,128)(2,1)} %get-tuple-element.41), channel_id=1, source_target_pairs={{0,8},{1,9},{2,10},{3,11},{4,12},{5,13},{6,14},{7,15},{8,0},{9,1},... | collective-permute-start | bytes 589832 | tf_op jit(solution)/shard_map/ppermute | solution.py:406
  10.2 11.6 %copy-start.8 = (bf16[27,32,512]{2,1,0:T(8,128)(2,1)}, bf16[27,32,512]{2,1,0:T(8,128)(2,1)S(1)}, u32[]{:S(2)}) copy-start(bf16[27,32,512]{2,1,0:T(8,128)(2,1)S(1)} %maximum_select_fusion) | copy-start | bytes 2654212
  10.4 27.2 %collective-permute-start.3 = (bf16[864,512]{1,0:T(8,128)(2,1)S(1)}, bf16[864,512]{1,0:T(8,128)(2,1)S(1)}, u32[]{:S(2)}, u32[]{:S(2)}) collective-permute-start(bf16[864,512]{1,0:T(8,128)(2,1)S(1)} %bitcast.30), channel_id=1, source_target_pairs={{0,4},{1,5},{4,8},{5,9},{8,12},{9,13},{12,14},{13,15},{14,10},{15,... | collective-permute-start | bytes 2654216 | tf_op jit(solution)/shard_map/ppermute | solution.py:399
  10.5 27.2 %collective-permute-start.4 = (bf16[864,512]{1,0:T(8,128)(2,1)S(1)}, bf16[864,512]{1,0:T(8,128)(2,1)}, u32[]{:S(2)}, u32[]{:S(2)}) collective-permute-start(bf16[864,512]{1,0:T(8,128)(2,1)S(1)} %bitcast.31), channel_id=1, source_target_pairs={{0,2},{1,3},{4,0},{5,1},{8,4},{9,5},{12,8},{13,9},{14,12},{15,13},... | collective-permute-start | bytes 2654216 | tf_op jit(solution)/shard_map/ppermute | solution.py:400
  13.0 8.9 %copy-start.12 = (bf16[64,512]{1,0:T(8,128)(2,1)S(1)}, bf16[64,512]{1,0:T(8,128)(2,1)}, u32[]{:S(2)}) copy-start(bf16[64,512]{1,0:T(8,128)(2,1)} %get-tuple-element.46) | copy-start | bytes 196612
  13.0 12.9 %copy-start.11 = (bf16[64,512]{1,0:T(8,128)(2,1)S(1)}, bf16[64,512]{1,0:T(8,128)(2,1)}, u32[]{:S(2)}) copy-start(bf16[64,512]{1,0:T(8,128)(2,1)} %get-tuple-element.47) | copy-start | bytes 196612
  21.9 14.8 %collective-permute-start.6 = (bf16[128,512]{1,0:T(8,128)(2,1)S(1)}, bf16[128,512]{1,0:T(8,128)(2,1)S(1)}, u32[]{:S(2)}, u32[]{:S(2)}) collective-permute-start(bf16[128,512]{1,0:T(8,128)(2,1)S(1)} %pad_maximum_fusion), channel_id=1, source_target_pairs={{0,1},{1,2},{2,3},{3,4},{4,5},{5,6},{6,7},{8,9},{9,10},{10,11},{11... | collective-permute-start | bytes 393224 | tf_op jit(solution)/shard_map/ppermute | solution.py:416
  25.9 10.8 %collective-permute-start.7 = (bf16[128,512]{1,0:T(8,128)(2,1)S(1)}, bf16[128,512]{1,0:T(8,128)(2,1)S(1)}, u32[]{:S(2)}, u32[]{:S(2)}) collective-permute-start(bf16[128,512]{1,0:T(8,128)(2,1)S(1)} %pad_maximum_fusion.1), channel_id=1, source_target_pairs={{1,0},{2,1},{3,2},{4,3},{5,4},{6,5},{7,6},{9,8},{10,9},{11,10},{12... | collective-permute-start | bytes 393224 | tf_op jit(solution)/shard_map/ppermute | solution.py:417
  37.6 15.4 %copy-start.17 = (bf16[864,512]{1,0:T(8,128)(2,1)}, bf16[864,512]{1,0:T(8,128)(2,1)S(1)}, u32[]{:S(2)}) copy-start(bf16[864,512]{1,0:T(8,128)(2,1)S(1)} %collective-permute-done.3.refs_3_) | copy-start | bytes 2654212
  37.6 27.2 %collective-permute-start.8 = (bf16[864,512]{1,0:T(8,128)(2,1)S(1)}, bf16[864,512]{1,0:T(8,128)(2,1)S(1)}, u32[]{:S(2)}, u32[]{:S(2)}) collective-permute-start(bf16[864,512]{1,0:T(8,128)(2,1)S(1)} %collective-permute-done.3.refs_3_), channel_id=1, source_target_pairs={{0,4},{1,5},{4,8},{5,9},{8,12},{9,13},{12,14},{13,15},{14,10},{15,... | collective-permute-start | bytes 2654216 | tf_op jit(solution)/shard_map/ppermute | solution.py:399
  39.8 25.0 %collective-permute-start.9 = (bf16[864,512]{1,0:T(8,128)(2,1)}, bf16[864,512]{1,0:T(8,128)(2,1)}, u32[]{:S(2)}, u32[]{:S(2)}) collective-permute-start(bf16[864,512]{1,0:T(8,128)(2,1)} %collective-permute-done.4.refs_4_), channel_id=1, source_target_pairs={{0,2},{1,3},{4,0},{5,1},{8,4},{9,5},{12,8},{13,9},{14,12},{15,13},... | collective-permute-start | bytes 2654216 | tf_op jit(solution)/shard_map/ppermute | solution.py:400
  40.5 0.7 copy-start
  41.2 11.9 %collective-permute-start.10 = (bf16[320,256]{1,0:T(8,128)(2,1)S(1)}, bf16[320,256]{1,0:T(8,128)(2,1)S(1)}, u32[]{:S(2)}, u32[]{:S(2)}) collective-permute-start(bf16[320,256]{1,0:T(8,128)(2,1)S(1)} %get-tuple-element.53), channel_id=1, source_target_pairs={{0,1},{1,0},{2,3},{3,2},{4,5},{5,4},{6,7},{7,6},{8,9},{9,8},{10,11... | collective-permute-start | bytes 491528 | tf_op jit(solution)/shard_map/ppermute | solution.py:440
  53.0 0.7 copy-start.10
  64.9 3.1 %copy-start.18 = (bf16[864,512]{1,0:T(8,128)(2,1)}, bf16[864,512]{1,0:T(8,128)(2,1)S(1)}, u32[]{:S(2)}) copy-start(bf16[864,512]{1,0:T(8,128)(2,1)S(1)} %collective-permute-done.8.refs_5_) | copy-start | bytes 2654212
  64.9 21.3 %collective-permute-start.11 = (bf16[864,512]{1,0:T(8,128)(2,1)S(1)}, bf16[864,512]{1,0:T(8,128)(2,1)S(1)}, u32[]{:S(2)}, u32[]{:S(2)}) collective-permute-start(bf16[864,512]{1,0:T(8,128)(2,1)S(1)} %collective-permute-done.8.refs_5_), channel_id=1, source_target_pairs={{0,4},{1,5},{4,8},{5,9},{8,12},{9,13},{12,14},{13,15},{14,10},{15,... | collective-permute-start | bytes 2654216 | tf_op jit(solution)/shard_map/ppermute | solution.py:399
  66.7 21.2 %collective-permute-start.12 = (bf16[864,512]{1,0:T(8,128)(2,1)}, bf16[864,512]{1,0:T(8,128)(2,1)S(1)}, u32[]{:S(2)}, u32[]{:S(2)}) collective-permute-start(bf16[864,512]{1,0:T(8,128)(2,1)} %collective-permute-done.9.refs_6_), channel_id=1, source_target_pairs={{0,2},{1,3},{4,0},{5,1},{8,4},{9,5},{12,8},{13,9},{14,12},{15,13},... | collective-permute-start | bytes 2654216 | tf_op jit(solution)/shard_map/ppermute | solution.py:400
  86.2 4.6 %copy-start.1 = (bf16[864,512]{1,0:T(8,128)(2,1)}, bf16[864,512]{1,0:T(8,128)(2,1)S(1)}, u32[]{:S(2)}) copy-start(bf16[864,512]{1,0:T(8,128)(2,1)S(1)} %collective-permute-done.11.refs_2_) | copy-start | bytes 2654212
  87.9 2.9 %copy-start.2 = (bf16[864,512]{1,0:T(8,128)(2,1)}, bf16[864,512]{1,0:T(8,128)(2,1)S(1)}, u32[]{:S(2)}) copy-start(bf16[864,512]{1,0:T(8,128)(2,1)S(1)} %collective-permute-done.12.refs_3_) | copy-start | bytes 2654212
  87.9 10.6 %collective-permute-start.13 = (bf16[432,512]{1,0:T(8,128)(2,1)S(1)}, bf16[432,512]{1,0:T(8,128)(2,1)S(1)}, u32[]{:S(2)}, u32[]{:S(2)}) collective-permute-start(bf16[432,512]{1,0:T(8,128)(2,1)S(1)} %slice.74), channel_id=1, source_target_pairs={{0,4},{1,5},{4,8},{5,9},{8,12},{9,13},{12,14},{13,15},{14,10},{15,... | collective-permute-start | bytes 1327112 | tf_op jit(solution)/shard_map/ppermute | solution.py:399
  88.2 10.5 %collective-permute-start.14 = (bf16[432,512]{1,0:T(8,128)(2,1)S(1)}, bf16[432,512]{1,0:T(8,128)(2,1)S(1)}, u32[]{:S(2)}, u32[]{:S(2)}) collective-permute-start(bf16[432,512]{1,0:T(8,128)(2,1)S(1)} %slice.75), channel_id=1, source_target_pairs={{0,2},{1,3},{4,0},{5,1},{8,4},{9,5},{12,8},{13,9},{14,12},{15,13},... | collective-permute-start | bytes 1327112 | tf_op jit(solution)/shard_map/ppermute | solution.py:400
  98.5 0.8 copy-start.3
  98.7 0.8 copy-start.4
  99.5 6.8 %copy-start.13 = (s32[512]{0:T(512)S(1)}, s32[512]{0:T(512)}, u32[]{:S(2)}) copy-start(s32[512]{0:T(512)} %param.27) | copy-start | bytes 6148
  103.9 7.8 %collective-permute-start.15 = (f32[512,512]{1,0:T(8,128)}, f32[512,512]{1,0:T(8,128)S(1)}, u32[]{:S(2)}, u32[]{:S(2)}) collective-permute-start(f32[512,512]{1,0:T(8,128)} %shard_map.154), channel_id=1, source_target_pairs={{0,1},{1,0},{2,3},{3,2},{4,5},{5,4},{6,7},{7,6},{8,9},{9,8},{10,11... | collective-permute-start | bytes 3145736 | tf_op jit(solution)/shard_map/ppermute | solution.py:467
  111.7 1.0 copy-start.6
  116.8 5.4 %copy-start.5 = (bf16[512,1536]{1,0:T(8,128)(2,1)S(1)}, bf16[512,1536]{1,0:T(8,128)(2,1)}, u32[]{:S(2)}) copy-start(bf16[512,1536]{1,0:T(8,128)(2,1)} %param.20) | copy-start | bytes 4718596
  116.9 30.4 %all-to-all-start = ((bf16[16,64,512]{2,1,0:T(8,128)(2,1)}), bf16[16,64,512]{2,1,0:T(8,128)(2,1)}, u32[]{:S(2)}, u32[]{:S(2)}) async-start(bf16[16,64,512]{2,1,0:T(8,128)(2,1)} %bitcast.26), calls=%async_computation | async-start | bytes 2097152 | tf_op jit(solution)/shard_map/all_to_all | solution.py:483
  122.2 1.4 copy-start.16
  123.9 23.3 %copy-start.15 = (s32[512]{0:T(512)}, s32[512]{0:T(512)S(1)}, u32[]{:S(2)}) copy-start(s32[512]{0:T(512)S(1)} %multiply_add_fusion) | copy-start | bytes 6148
  171.4 5.0 %copy-start.14 = (s32[512]{0:T(512)S(1)}, s32[512]{0:T(512)}, u32[]{:S(2)}) copy-start(s32[512]{0:T(512)} %multiply_add_fusion.1) | copy-start | bytes 6148
  171.4 29.8 %all-to-all-start.1 = ((bf16[16,64,512]{2,1,0:T(8,128)(2,1)}), bf16[16,64,512]{2,1,0:T(8,128)(2,1)S(1)}, u32[]{:S(2)}, u32[]{:S(2)}) async-start(bf16[16,64,512]{2,1,0:T(8,128)(2,1)} %bitcast.27), calls=%async_computation.1 | async-start | bytes 2097152 | tf_op jit(solution)/shard_map/all_to_all | solution.py:514

commit v9 on v8

--- a/solution.py
+++ b/solution.py
@@ -76,46 +76,50 @@
         first, second = rows[:, :half], rows[:, half:]
         own_ref[at * size : (at + 1) * size] = jnp.where(even, first, second)
         other_ref[at * size : (at + 1) * size] = jnp.where(even, second, first)
-
-
-def gather_kernel(taps, start_ref, rows_ref, table_ref, *refs):
-    out_ref = refs[-1]
-    height, half = table_ref.shape
-    lane = lax.broadcasted_iota(jnp.int32, rows_ref.shape, 1)
-    row_ids = (lax.broadcasted_iota(jnp.int32, (1, height), 1) + start_ref[0]).astype(F32)
+    rest = jnp.zeros((size, half), BF16)
+    own_ref[5 * size :] = rest
+    other_ref[5 * size :] = rest
+
+
+def gather_kernel(taps, start_ref, rows_ref, own_ref, got_ref, out_ref):
+    half = own_ref.shape[1]
+    part = lax.rem(lax.broadcasted_iota(jnp.int32, (rows_ref.shape[1], 128), 0), 128)
+    lane = lax.broadcasted_iota(jnp.int32, (1, 128), 1)
     for at in range(taps):
-        chosen = lane == taps * pl.program_id(0) + at
-        column = jnp.sum(jnp.where(chosen, rows_ref[...], 0.0), axis=1, keepdims=True)
-        taken = dot(one_hot(column == row_ids), table_ref[...])
-        place = slice(at * half, (at + 1) * half)
-        if len(refs) > 1:
-            taken += refs[0][:, place].astype(F32)
-        out_ref[:, place] = taken.astype(BF16)
-
-
-def gather_part(start, rows, table, before=None):
+        chosen = one_hot(part == taps * pl.program_id(0) + at)
+        index = dot(rows_ref[...], chosen)
+        taken = None
+        for table, start in ((own_ref, 0), (got_ref, start_ref[0])):
+            hits = [
+                one_hot(index == (lane + (start + first)).astype(F32))
+                for first in range(0, table.shape[0], 128)
+            ]
+            product = dot(jnp.concatenate(hits, axis=1), table[...])
+            taken = product if taken is None else taken + product
+        out_ref[:, at * half : (at + 1) * half] = taken.astype(BF16)
+
+
+def gather_block(start, rows, own, got):
     points, lanes = rows.shape
-    height, half = table.shape
+    half = own.shape[1]
+    height = own.shape[0] + got.shape[0]
     taps = 3
     whole = lambda step: (0, 0)
-    block = pl.BlockSpec((points, taps * half), lambda step: (0, step))
-    extra = [] if before is None else [before]
     return call(
         functools.partial(gather_kernel, taps),
         jax.ShapeDtypeStruct((points, TAPS * half), BF16),
         60,
         2 * TAPS * points * height * half,
-        2 * TAPS * points * half * (1 + len(extra)),
+        2 * TAPS * points * half,
         grid=(TAPS // taps,),
         in_specs=[
             pl.BlockSpec(memory_space=pltpu.SMEM),
             pl.BlockSpec((points, lanes), whole),
-            pl.BlockSpec((height, half), whole),
-        ]
-        + [block] * len(extra),
-        out_specs=block,
-        input_output_aliases={3: 0} if extra else {},
-    )(start, rows, table, *extra)
+            pl.BlockSpec(own.shape, whole),
+            pl.BlockSpec(got.shape, whole),
+        ],
+        out_specs=pl.BlockSpec((points, taps * half), lambda step: (0, step)),
+    )(start, rows, own, got)
 
 
 def conv_kernel(slots, blocks, first, places_ref, *refs):
@@ -324,9 +328,9 @@
     own = jnp.arange(points, dtype=jnp.int32)[:, None]
     rest = jnp.zeros((points, 128 - TAPS), jnp.int32)
     middle = TAPS // 2
-    return jnp.concatenate(
-        [neighbours[:, :middle], own, neighbours[:, middle:], rest], axis=1
-    ).astype(F32)
+    rows = jnp.concatenate([neighbours[:, :middle], own, neighbours[:, middle:], rest], axis=1)
+    fine = rows % 32
+    return jnp.concatenate([rows - fine, fine], axis=1).astype(BF16)
 
 
 def body(
@@ -403,24 +407,18 @@
     if round_trip:
         lists, back_list, on_list = faces
         side = face_pairs(devices, 1, 0) + face_pairs(devices, -1, 0)
+        lists, other_local, other_neighbours = pass_on(lists, other_local, other_neighbours)
         lists = lax.ppermute(lists, "blocks", side)
-        other_local, other_neighbours = pass_on(other_local, other_neighbours)
     own_rows, other_rows = padded_taps(neighbours), padded_taps(other_neighbours)
-    nothing = jnp.zeros((1,), jnp.int32)
-    own_stacked = gather_part(nothing, own_rows, own_local)
-    other_stacked = gather_part(nothing, other_rows, other_local)
     if round_trip:
-        own_stacked, lists = lax.optimization_barrier((own_stacked, lists))
         to_on = jnp.concatenate([on_list, lists[2 * size :]])
         to_back = jnp.concatenate([back_list, lists[:size]])
         behind = lax.ppermute(to_on, "blocks", face_pairs(devices, 0, 1))
         ahead = lax.ppermute(to_back, "blocks", face_pairs(devices, 0, -1))
-        own_stacked, other_stacked, lists, behind, ahead = pass_on(
-            own_stacked, other_stacked, lists, behind, ahead
-        )
+        lists, behind, ahead = pass_on(lists, behind, ahead)
         own_remote, other_half = call(
             received_kernel,
-            [jax.ShapeDtypeStruct((5 * size, half), BF16)] * 2,
+            [jax.ShapeDtypeStruct((6 * size, half), BF16)] * 2,
             32,
             0,
             20 * size * width,
@@ -436,10 +434,10 @@
         )
         own_remote = lax.dynamic_slice(received, (0, core * half), (8 * size, half))
         other_half = lax.dynamic_slice(received, (0, (1 - core) * half), (8 * size, half))
-        start = nothing + points
+        start = jnp.full((1,), points, jnp.int32)
     other_remote = lax.ppermute(other_half, "blocks", partner)
-    own_stacked = gather_part(start, own_rows, own_remote, own_stacked)
-    other_stacked = gather_part(start, other_rows, other_remote, other_stacked)
+    own_stacked = gather_block(start, own_rows, own_local, own_remote)
+    other_stacked = gather_block(start, other_rows, other_local, other_remote)
     stacked = pass_on(other_stacked, own_stacked)
     if round_trip:
         places = jnp.array(places, jnp.int32)[index]
@@ -469,7 +467,7 @@
     outgoing = call(
         mix_kernel,
         jax.ShapeDtypeStruct((slots, width), BF16),
-        60,
+        32,
         2 * points * width * (width + slots),
         8 * points * width,
     )(

time: 204 us -> 208 us (1.020)
  waiting for transfers between devices: 58.4 us -> 76.4 us
  Pallas kernels: 98.2 us -> 85.3 us
    pallas_call x6 -> x4, Pallas kernels: 44.8 us -> 31.8 us  [the longest x2 28.9 us: gather_block(): call(functools.partial(gather_kernel, taps), jax.ShapeDtypeStruct((points...]
    ppermute x1, waiting for transfers between devices: 0.01 us -> 6.94 us  [body(): lists = lax.ppermute(lists, 'blocks', side)]
    ppermute x4, waiting for transfers between devices: 10.5 us -> 17.3 us  [pass_on(): back.append(lax.ppermute(first, 'blocks', back_pairs))]
    ppermute x1, waiting for transfers between devices: 0.01 us -> 3.78 us  [body(): ahead = lax.ppermute(to_back, 'blocks', face_pairs(devices, 0, -1))]
  transfers between devices with their start and end apart: 18 -> 18, of which waited for: 7 -> 9; matrix products, arithmetic and copies ran while one was open for 6% -> 5% of each run, Pallas kernels for 31% -> 25%
where the time goes in v9:
time: 208 us; the launch traced here: 207 us
  Pallas kernels  85.3 us (41%)
  waiting for transfers between devices  76.4 us (37%)
  starting transfers between devices  29.5 us (14%)
  local copies, waits for them, and re-layouts  11.6 us (6%)
  other arithmetic  4.18 us (2%)
    pallas_call x2, Pallas kernels, gather_block(): call(functools.partial(gather_kernel, taps), jax.ShapeDtypeStruct((points...  28.9 us
    pallas_call x4, Pallas kernels, conv_part(): call(functools.partial(conv_kernel, slots, blocks, before is None), [jax....  25.3 us
    all_to_all x1, waiting for transfers between devices, body(): lax.all_to_all(back.reshape(devices, capacity, width), 'blocks', split_ax...  24.7 us
    pallas_call x1, Pallas kernels, body(): call(block_kernel, jax.ShapeDtypeStruct((slots, width), BF16), 60, 20 * p...  24.2 us
    all_to_all x1, waiting for transfers between devices, body(): lax.all_to_all(outgoing.reshape(devices, capacity, width), 'blocks', spli...  21.4 us
    ppermute x4, waiting for transfers between devices, pass_on(): back.append(lax.ppermute(first, 'blocks', back_pairs))  17.3 us
    ppermute x1, waiting for transfers between devices, body(): lists = lax.ppermute(lists, 'blocks', side)  6.94 us
    all_to_all x1, starting transfers between devices, body(): lax.all_to_all(outgoing.reshape(devices, capacity, width), 'blocks', spli...  5.24 us
  transfers between devices with their start and end apart: 18, of which 9 were waited for; matrix products, arithmetic and copies ran while one was open for 5% of the time, Pallas kernels for 25%

profile of v9, /device:TPU:9, one launch (start us, length us, event | category | flops | bytes accessed | tf_op | source)
XLA Modules:
  0.0 207.2 jit_solution(6016704117623750772)
XLA Ops:
  0.0 1.1 slice.63
  1.1 0.7 collective-permute-start
  1.9 0.7 slice_bitcast_fusion
  2.6 0.8 select_bitcast_fusion
  3.3 0.8 reshape.93.rows_ref
  4.2 2.5 %shard_map.145 = (bf16[512,256]{1,0:T(8,128)(2,1)}, bf16[512,256]{1,0:T(8,128)(2,1)}, bf16[192,512]{1,0:T(8,128)(2,1)}, bf16[64,512]{1,0:T(8,128)(2,1)}, bf16[64,512]{1,0:T(8,128)(2,1)}) custom-call(s32[1]{0:T(128)} %bitcast.3.core_ref, bf16[512,512]{1,0:T(8,128)(2,1)} %features_ref.3, s32[320,1]{1,0:T(8,128)} %reshape.93.rows_ref), custom_call_target="tpu_custom_call" | custom-call | flops 536870912 | bytes 2097152 | tf_op jit(solution)/shard_map/pallas_call | solution.py:378
  6.6 0.1 copy.34
  6.8 0.6 collective-permute-start.2
  7.4 0.1 copy.35
  7.5 0.1 copy.36
  7.7 0.1 pad.15.clone
  7.8 0.1 maximum_select_fusion
  8.0 0.5 collective-permute-done.2
  8.5 2.3 %collective-permute-start.5 = (bf16[192,512]{1,0:T(8,128)(2,1)}, bf16[192,512]{1,0:T(8,128)(2,1)S(1)}, u32[]{:S(2)}, u32[]{:S(2)}) collective-permute-start(bf16[192,512]{1,0:T(8,128)(2,1)} %get-tuple-element.38), channel_id=1, source_target_pairs={{0,8},{1,9},{2,10},{3,11},{4,12},{5,13},{6,14},{7,15},{8,0},{9,1},... | collective-permute-start | bytes 589832 | tf_op jit(solution)/shard_map/ppermute | solution.py:411
  10.8 1.5 collective-permute-start.4
  12.3 0.1 fusion.10
  12.5 0.4 subtract_convert_fusion
  12.9 0.1 fusion.3
  13.0 6.9 %collective-permute-done.5.side_ref = bf16[192,512]{1,0:T(8,128)(2,1)S(1)} collective-permute-done((bf16[192,512]{1,0:T(8,128)(2,1)}, bf16[192,512]{1,0:T(8,128)(2,1)S(1)}, u32[]{:S(2)}, u32[]{:S(2)}) %collective-permute-start.5) | collective-permute-done | bytes 196640 | tf_op jit(solution)/shard_map/ppermute | solution.py:411
  20.0 3.6 %collective-permute-start.6 = (bf16[128,512]{1,0:T(8,128)(2,1)S(1)}, bf16[128,512]{1,0:T(8,128)(2,1)S(1)}, u32[]{:S(2)}, u32[]{:S(2)}) collective-permute-start(bf16[128,512]{1,0:T(8,128)(2,1)S(1)} %pad_maximum_fusion.2), channel_id=1, source_target_pairs={{0,1},{1,2},{2,3},{3,4},{4,5},{5,6},{6,7},{8,9},{9,10},{10,11},{11... | collective-permute-start | bytes 393224 | tf_op jit(solution)/shard_map/ppermute | solution.py:416
  23.6 1.9 collective-permute-start.7
  25.5 0.1 fusion.4
  25.7 0.9 pad_maximum_fusion
  26.5 3.8 %collective-permute-done.7.ahead_ref = bf16[128,512]{1,0:T(8,128)(2,1)S(1)} collective-permute-done((bf16[128,512]{1,0:T(8,128)(2,1)S(1)}, bf16[128,512]{1,0:T(8,128)(2,1)S(1)}, u32[]{:S(2)}, u32[]{:S(2)}) %collective-permute-start.7) | collective-permute-done | bytes 131104 | tf_op jit(solution)/shard_map/ppermute | solution.py:417
  30.3 8.5 %collective-permute-done.3.refs_3_ = bf16[864,512]{1,0:T(8,128)(2,1)S(1)} collective-permute-done((bf16[864,512]{1,0:T(8,128)(2,1)S(1)}, bf16[864,512]{1,0:T(8,128)(2,1)S(1)}, u32[]{:S(2)}, u32[]{:S(2)}) %collective-permute-start.3) | collective-permute-done | bytes 884768 | tf_op jit(solution)/shard_map/ppermute | solution.py:403
  38.8 0.6 shard_map.146
  39.4 0.7 copy-done.4
  40.1 0.5 collective-permute-start.10
  40.5 2.2 %collective-permute-start.8 = (bf16[864,512]{1,0:T(8,128)(2,1)S(1)}, bf16[864,512]{1,0:T(8,128)(2,1)S(1)}, u32[]{:S(2)}, u32[]{:S(2)}) collective-permute-start(bf16[864,512]{1,0:T(8,128)(2,1)S(1)} %collective-permute-done.3.refs_3_), channel_id=1, source_target_pairs={{0,4},{1,5},{4,8},{5,9},{8,12},{9,13},{12,14},{13,15},{14,10},{15,... | collective-permute-start | bytes 2654216 | tf_op jit(solution)/shard_map/ppermute | solution.py:403
  42.7 14.4 %shard_map.148.refs_1_.refs_0_ = bf16[512,6912]{1,0:T(8,128)(2,1)} custom-call(s32[1]{0:T(128)} %bitcast.6.start_ref, bf16[512,256]{1,0:T(8,128)(2,1)} %get-tuple-element.79.rows_ref, bf16[512,256]{1,0:T(8,128)(2,1)} %get-tuple-element.49.own_ref, bf16[384,256]{1,0:T(8,128)(2,1)} %copy-done.4), custom_call_target="tpu_custom_call" | custom-call | flops 6341787648 | bytes 7077888 | tf_op jit(solution)/shard_map/pallas_call | solution.py:108
  57.2 0.7 copy-done.20
  57.9 14.4 %shard_map.147.refs_0_ = bf16[512,6912]{1,0:T(8,128)(2,1)} custom-call(s32[1]{0:T(128)} %bitcast.6.start_ref, bf16[512,256]{1,0:T(8,128)(2,1)} %get-tuple-element.78.rows_ref, bf16[512,256]{1,0:T(8,128)(2,1)} %collective-permute-done.1.own_ref, bf16[384,256]{1,0:T(8,128)(2,1)} %copy-done.20), custom_call_target="tpu_custom_call" | custom-call | flops 6341787648 | bytes 7077888 | tf_op jit(solution)/shard_map/pallas_call | solution.py:108
  72.3 1.5 collective-permute-start.11
  73.8 0.7 constant_dynamic-slice_fusion
  74.5 0.6 reshape.79.places_ref
  75.1 9.4 %shard_map.149 = (f32[512,512]{1,0:T(8,128)}, f32[512,512]{1,0:T(8,128)}) custom-call(s32[10]{0:T(128)} %reshape.79.places_ref, bf16[512,6912]{1,0:T(8,128)(2,1)} %shard_map.147.refs_0_, bf16[512,6912]{1,0:T(8,128)(2,1)} %shard_map.148.refs_1_.refs_0_, bf16[864,512]{1,0:T(8,128)(2,1)} %bitcast.34, bf16[864,512]{1,0:T(8,128)(2,1)} %copy-done.18, ...), custom_call_target="tpu_custom_call" | custom-call | flops 5368709120 | bytes 15728640 | tf_op jit(solution)/shard_map/pallas_call | solution.py:176
  84.5 8.7 %collective-permute-done.11.refs_2_ = bf16[864,512]{1,0:T(8,128)(2,1)S(1)} collective-permute-done((bf16[864,512]{1,0:T(8,128)(2,1)S(1)}, bf16[864,512]{1,0:T(8,128)(2,1)S(1)}, u32[]{:S(2)}, u32[]{:S(2)}) %collective-permute-start.11) | collective-permute-done | bytes 884768 | tf_op jit(solution)/shard_map/ppermute | solution.py:403
  93.3 1.0 collective-permute-done.12.refs_3_
  94.4 0.4 collective-permute-start.13
  94.8 1.3 collective-permute-start.14
  96.1 0.6 reshape.80.places_ref
  96.7 0.6 slice_bitcast_fusion.1.places_ref
  97.3 6.9 %shard_map.150 = (f32[512,512]{1,0:T(8,128)}, f32[512,512]{1,0:T(8,128)}) custom-call(s32[4]{0:T(128)} %reshape.80.places_ref, bf16[512,6912]{1,0:T(8,128)(2,1)} %shard_map.147.refs_0_, bf16[512,6912]{1,0:T(8,128)(2,1)} %shard_map.148.refs_1_.refs_0_, bf16[864,512]{1,0:T(8,128)(2,1)} %copy-done.5, ...), custom_call_target="tpu_custom_call", output_to_operand_aliasing={{0}: (5, {}), {1}: (6, {})} | custom-call | flops 2147483648 | bytes 6291456 | tf_op jit(solution)/shard_map/pallas_call | solution.py:176
  104.3 0.7 collective-permute-done.14.refs_2_
  105.1 0.7 copy-done.8
  105.8 4.4 %shard_map.152 = f32[512,512]{1,0:T(8,128)} custom-call(s32[2]{0:T(128)} %slice_bitcast_fusion.1.places_ref, bf16[512,6912]{1,0:T(8,128)(2,1)} %shard_map.147.refs_0_, bf16[432,512]{1,0:T(8,128)(2,1)} %copy-done.7, bf16[432,512]{1,0:T(8,128)(2,1)} %copy-done.8, f32[512,512]{1,0:T(8,128)} %get-tuple-element.62.refs_3_), custom_call_target="tpu_custom_call", output_to_operand_aliasing={{}: (4, {})} | custom-call | flops 536870912 | bytes 2097152 | tf_op jit(solution)/shard_map/pallas_call | solution.py:176
  110.2 2.7 %collective-permute-start.15 = (f32[512,512]{1,0:T(8,128)}, f32[512,512]{1,0:T(8,128)S(1)}, u32[]{:S(2)}, u32[]{:S(2)}) collective-permute-start(f32[512,512]{1,0:T(8,128)} %shard_map.152), channel_id=1, source_target_pairs={{0,1},{1,0},{2,3},{3,2},{4,5},{5,4},{6,7},{7,6},{8,9},{9,8},{10,11... | collective-permute-start | bytes 3145736 | tf_op jit(solution)/shard_map/ppermute | solution.py:465
  113.0 0.3 convert_reduce_fusion.1
  113.4 4.5 %shard_map.151.own_ref = f32[512,512]{1,0:T(8,128)} custom-call(s32[2]{0:T(128)} %slice_bitcast_fusion.1.places_ref, bf16[512,6912]{1,0:T(8,128)(2,1)} %shard_map.148.refs_1_.refs_0_, bf16[432,512]{1,0:T(8,128)(2,1)} %copy-done.7, bf16[432,512]{1,0:T(8,128)(2,1)} %copy-done.8, f32[512,512]{1,0:T(8,128)} %get-tuple-element.61.refs_3_), custom_call_target="tpu_custom_call", output_to_operand_aliasing={{}: (4, {})} | custom-call | flops 536870912 | bytes 2097152 | tf_op jit(solution)/shard_map/pallas_call | solution.py:176
  117.9 1.2 copy-done
  119.1 2.3 %shard_map.153 = bf16[1024,512]{1,0:T(8,128)(2,1)} custom-call(f32[512,512]{1,0:T(8,128)S(1)} %copy-done, f32[512,512]{1,0:T(8,128)S(1)} %collective-permute-done.15.got_ref, bf16[512,512]{1,0:T(8,128)(2,1)S(1)} %copy-done.1, bf16[512,512]{1,0:T(8,128)(2,1)S(1)} %copy-done.2, f32[1,512]{1,0:T(1,128)S(1)} %bitcast.28, s32[1,512]{1,0:T(1,128)S(1)} %bitcast.26), custom_call_target="tpu_custom_call" | custom-call | flops 805306368 | bytes 2097152 | tf_op jit(solution)/shard_map/pallas_call | solution.py:467
  121.5 5.2 %all-to-all-start = ((bf16[16,64,512]{2,1,0:T(8,128)(2,1)}), bf16[16,64,512]{2,1,0:T(8,128)(2,1)}, u32[]{:S(2)}, u32[]{:S(2)}) async-start(bf16[16,64,512]{2,1,0:T(8,128)(2,1)} %bitcast.10), calls=%async_computation | async-start | bytes 2097152 | tf_op jit(solution)/shard_map/all_to_all | solution.py:481
  126.7 0.9 fusion.9
  127.6 0.2 copy.41
  127.8 0.2 copy.42
  128.1 0.2 convert_reduce_fusion
  128.3 0.9 copy.39.slot_col_ref
  129.2 1.0 maximum_bitcast_fusion.qv_hbm
  130.3 21.4 %all-to-all-done = bf16[16,64,512]{2,1,0:T(8,128)(2,1)} async-done(((bf16[16,64,512]{2,1,0:T(8,128)(2,1)}), bf16[16,64,512]{2,1,0:T(8,128)(2,1)}, u32[]{:S(2)}, u32[]{:S(2)}) %all-to-all-start) | async-done | bytes 1048608 | tf_op jit(solution)/shard_map/all_to_all | solution.py:481
  151.7 24.2 %shard_map.154 = bf16[1024,512]{1,0:T(8,128)(2,1)} custom-call(bf16[1024,512]{1,0:T(8,128)(2,1)} %bitcast.11.arrived_ref, s32[512,1]{1,0:T(8,128)} %copy.39.slot_col_ref, s32[1,512]{1,0:T(1,128)} %bitcast.37, f32[1,512]{1,0:T(1,128)} %bitcast.38, f32[1,512]{1,0:T(1,128)} %bitcast.39, bf16[1024,512]{1,0:T(8,128)(2,1)} %maximum_bitcast_fusion.qv_hbm, ...), custom_call_target="tpu_custom_call" | custom-call | flops 2684354560 | bytes 4194304 | tf_op jit(solution)/shard_map/pallas_call | solution.py:488
  175.9 5.0 %all-to-all-start.1 = ((bf16[16,64,512]{2,1,0:T(8,128)(2,1)}), bf16[16,64,512]{2,1,0:T(8,128)(2,1)S(1)}, u32[]{:S(2)}, u32[]{:S(2)}) async-start(bf16[16,64,512]{2,1,0:T(8,128)(2,1)} %bitcast.29), calls=%async_computation.1 | async-start | bytes 2097152 | tf_op jit(solution)/shard_map/all_to_all | solution.py:512
  180.8 0.1 copy.40.slot_ref
  181.0 24.7 %all-to-all-done.1 = bf16[16,64,512]{2,1,0:T(8,128)(2,1)S(1)} async-done(((bf16[16,64,512]{2,1,0:T(8,128)(2,1)}), bf16[16,64,512]{2,1,0:T(8,128)(2,1)S(1)}, u32[]{:S(2)}, u32[]{:S(2)}) %all-to-all-start.1) | async-done | bytes 1048608 | tf_op jit(solution)/shard_map/all_to_all | solution.py:512
  205.7 1.5 shard_map.155
  (67 shorter events, 0.5 us)
Async XLA Ops:
  0.0 7.3 %copy-start.10 = (bf16[864,512]{1,0:T(8,128)(2,1)S(1)}, bf16[864,512]{1,0:T(8,128)(2,1)}, u32[]{:S(2)}) copy-start(bf16[864,512]{1,0:T(8,128)(2,1)} %param.16) | copy-start | bytes 2654212
  0.0 6.6 %copy-start.12 = (s32[512,26]{0,1:T(8,128)S(1)}, s32[512,26]{0,1:T(8,128)}, u32[]{:S(2)}) copy-start(s32[512,26]{0,1:T(8,128)} %param.26) | copy-start | bytes 159748
  1.1 6.7 %collective-permute-start = (bf16[13,32,512]{2,1,0:T(8,128)(2,1)S(1)}, bf16[13,32,512]{2,1,0:T(8,128)(2,1)S(1)}, u32[]{:S(2)}, u32[]{:S(2)}) collective-permute-start(bf16[13,32,512]{2,1,0:T(8,128)(2,1)S(1)} %slice.63), channel_id=1, source_target_pairs={{0,1},{1,0},{2,3},{3,2},{4,5},{5,4},{6,7},{7,6},{8,9},{9,8},{10,11... | collective-permute-start | bytes 1277960 | tf_op jit(solution)/shard_map/ppermute | solution.py:364
  6.6 1.9 collective-permute-start.1
  6.8 1.7 collective-permute-start.2
  8.0 12.0 %copy-start.11 = (bf16[27,32,512]{2,1,0:T(8,128)(2,1)}, bf16[27,32,512]{2,1,0:T(8,128)(2,1)S(1)}, u32[]{:S(2)}) copy-start(bf16[27,32,512]{2,1,0:T(8,128)(2,1)S(1)} %maximum_select_fusion) | copy-start | bytes 2654212
  8.0 12.0 %copy-start.14 = (bf16[64,512]{1,0:T(8,128)(2,1)S(1)}, bf16[64,512]{1,0:T(8,128)(2,1)}, u32[]{:S(2)}) copy-start(bf16[64,512]{1,0:T(8,128)(2,1)} %get-tuple-element.39) | copy-start | bytes 196612
  8.5 15.1 %copy-start.13 = (bf16[64,512]{1,0:T(8,128)(2,1)S(1)}, bf16[64,512]{1,0:T(8,128)(2,1)}, u32[]{:S(2)}) copy-start(bf16[64,512]{1,0:T(8,128)(2,1)} %get-tuple-element.40) | copy-start | bytes 196612
  8.5 11.4 %collective-permute-start.5 = (bf16[192,512]{1,0:T(8,128)(2,1)}, bf16[192,512]{1,0:T(8,128)(2,1)S(1)}, u32[]{:S(2)}, u32[]{:S(2)}) collective-permute-start(bf16[192,512]{1,0:T(8,128)(2,1)} %get-tuple-element.38), channel_id=1, source_target_pairs={{0,8},{1,9},{2,10},{3,11},{4,12},{5,13},{6,14},{7,15},{8,0},{9,1},... | collective-permute-start | bytes 589832 | tf_op jit(solution)/shard_map/ppermute | solution.py:411
  10.8 28.0 %collective-permute-start.3 = (bf16[864,512]{1,0:T(8,128)(2,1)S(1)}, bf16[864,512]{1,0:T(8,128)(2,1)S(1)}, u32[]{:S(2)}, u32[]{:S(2)}) collective-permute-start(bf16[864,512]{1,0:T(8,128)(2,1)S(1)} %bitcast.32), channel_id=1, source_target_pairs={{0,4},{1,5},{4,8},{5,9},{8,12},{9,13},{12,14},{13,15},{14,10},{15,... | collective-permute-start | bytes 2654216 | tf_op jit(solution)/shard_map/ppermute | solution.py:403
  10.8 28.0 %collective-permute-start.4 = (bf16[864,512]{1,0:T(8,128)(2,1)S(1)}, bf16[864,512]{1,0:T(8,128)(2,1)}, u32[]{:S(2)}, u32[]{:S(2)}) collective-permute-start(bf16[864,512]{1,0:T(8,128)(2,1)S(1)} %bitcast.33), channel_id=1, source_target_pairs={{0,2},{1,3},{4,0},{5,1},{8,4},{9,5},{12,8},{13,9},{14,12},{15,13},... | collective-permute-start | bytes 2654216 | tf_op jit(solution)/shard_map/ppermute | solution.py:404
  20.0 6.5 %collective-permute-start.6 = (bf16[128,512]{1,0:T(8,128)(2,1)S(1)}, bf16[128,512]{1,0:T(8,128)(2,1)S(1)}, u32[]{:S(2)}, u32[]{:S(2)}) collective-permute-start(bf16[128,512]{1,0:T(8,128)(2,1)S(1)} %pad_maximum_fusion.2), channel_id=1, source_target_pairs={{0,1},{1,2},{2,3},{3,4},{4,5},{5,6},{6,7},{8,9},{9,10},{10,11},{11... | collective-permute-start | bytes 393224 | tf_op jit(solution)/shard_map/ppermute | solution.py:416
  23.6 6.7 %collective-permute-start.7 = (bf16[128,512]{1,0:T(8,128)(2,1)S(1)}, bf16[128,512]{1,0:T(8,128)(2,1)S(1)}, u32[]{:S(2)}, u32[]{:S(2)}) collective-permute-start(bf16[128,512]{1,0:T(8,128)(2,1)S(1)} %pad_maximum_fusion.3), channel_id=1, source_target_pairs={{1,0},{2,1},{3,2},{4,3},{5,4},{6,5},{7,6},{9,8},{10,9},{11,10},{12... | collective-permute-start | bytes 393224 | tf_op jit(solution)/shard_map/ppermute | solution.py:417
  38.8 18.4 %copy-start.18 = (bf16[864,512]{1,0:T(8,128)(2,1)}, bf16[864,512]{1,0:T(8,128)(2,1)S(1)}, u32[]{:S(2)}) copy-start(bf16[864,512]{1,0:T(8,128)(2,1)S(1)} %collective-permute-done.3.refs_3_) | copy-start | bytes 2654212
  39.4 0.7 copy-start.4
  40.1 17.1 %collective-permute-start.10 = (bf16[384,256]{1,0:T(8,128)(2,1)S(1)}, bf16[384,256]{1,0:T(8,128)(2,1)S(1)}, u32[]{:S(2)}, u32[]{:S(2)}) collective-permute-start(bf16[384,256]{1,0:T(8,128)(2,1)S(1)} %get-tuple-element.48), channel_id=1, source_target_pairs={{0,1},{1,0},{2,3},{3,2},{4,5},{5,4},{6,7},{7,6},{8,9},{9,8},{10,11... | collective-permute-start | bytes 589832 | tf_op jit(solution)/shard_map/ppermute | solution.py:438
  40.5 31.8 %collective-permute-start.8 = (bf16[864,512]{1,0:T(8,128)(2,1)S(1)}, bf16[864,512]{1,0:T(8,128)(2,1)S(1)}, u32[]{:S(2)}, u32[]{:S(2)}) collective-permute-start(bf16[864,512]{1,0:T(8,128)(2,1)S(1)} %collective-permute-done.3.refs_3_), channel_id=1, source_target_pairs={{0,4},{1,5},{4,8},{5,9},{8,12},{9,13},{12,14},{13,15},{14,10},{15,... | collective-permute-start | bytes 2654216 | tf_op jit(solution)/shard_map/ppermute | solution.py:403
  42.7 29.6 %collective-permute-start.9 = (bf16[864,512]{1,0:T(8,128)(2,1)}, bf16[864,512]{1,0:T(8,128)(2,1)}, u32[]{:S(2)}, u32[]{:S(2)}) collective-permute-start(bf16[864,512]{1,0:T(8,128)(2,1)} %collective-permute-done.4.refs_4_), channel_id=1, source_target_pairs={{0,2},{1,3},{4,0},{5,1},{8,4},{9,5},{12,8},{13,9},{14,12},{15,13},... | collective-permute-start | bytes 2654216 | tf_op jit(solution)/shard_map/ppermute | solution.py:404
  57.2 0.7 copy-start.20
  72.3 2.8 %copy-start.19 = (bf16[864,512]{1,0:T(8,128)(2,1)}, bf16[864,512]{1,0:T(8,128)(2,1)S(1)}, u32[]{:S(2)}) copy-start(bf16[864,512]{1,0:T(8,128)(2,1)S(1)} %collective-permute-done.8.refs_5_) | copy-start | bytes 2654212
  72.3 21.0 %collective-permute-start.11 = (bf16[864,512]{1,0:T(8,128)(2,1)S(1)}, bf16[864,512]{1,0:T(8,128)(2,1)S(1)}, u32[]{:S(2)}, u32[]{:S(2)}) collective-permute-start(bf16[864,512]{1,0:T(8,128)(2,1)S(1)} %collective-permute-done.8.refs_5_), channel_id=1, source_target_pairs={{0,4},{1,5},{4,8},{5,9},{8,12},{9,13},{12,14},{13,15},{14,10},{15,... | collective-permute-start | bytes 2654216 | tf_op jit(solution)/shard_map/ppermute | solution.py:403
  73.8 20.5 %collective-permute-start.12 = (bf16[864,512]{1,0:T(8,128)(2,1)}, bf16[864,512]{1,0:T(8,128)(2,1)S(1)}, u32[]{:S(2)}, u32[]{:S(2)}) collective-permute-start(bf16[864,512]{1,0:T(8,128)(2,1)} %collective-permute-done.9.refs_6_), channel_id=1, source_target_pairs={{0,2},{1,3},{4,0},{5,1},{8,4},{9,5},{12,8},{13,9},{14,12},{15,13},... | collective-permute-start | bytes 2654216 | tf_op jit(solution)/shard_map/ppermute | solution.py:404
  93.3 4.0 %copy-start.5 = (bf16[864,512]{1,0:T(8,128)(2,1)}, bf16[864,512]{1,0:T(8,128)(2,1)S(1)}, u32[]{:S(2)}) copy-start(bf16[864,512]{1,0:T(8,128)(2,1)S(1)} %collective-permute-done.11.refs_2_) | copy-start | bytes 2654212
  94.3 3.0 %copy-start.6 = (bf16[864,512]{1,0:T(8,128)(2,1)}, bf16[864,512]{1,0:T(8,128)(2,1)S(1)}, u32[]{:S(2)}) copy-start(bf16[864,512]{1,0:T(8,128)(2,1)S(1)} %collective-permute-done.12.refs_3_) | copy-start | bytes 2654212
  94.4 9.9 %collective-permute-start.13 = (bf16[432,512]{1,0:T(8,128)(2,1)S(1)}, bf16[432,512]{1,0:T(8,128)(2,1)S(1)}, u32[]{:S(2)}, u32[]{:S(2)}) collective-permute-start(bf16[432,512]{1,0:T(8,128)(2,1)S(1)} %slice.74), channel_id=1, source_target_pairs={{0,4},{1,5},{4,8},{5,9},{8,12},{9,13},{12,14},{13,15},{14,10},{15,... | collective-permute-start | bytes 1327112 | tf_op jit(solution)/shard_map/ppermute | solution.py:403
  94.8 10.2 %collective-permute-start.14 = (bf16[432,512]{1,0:T(8,128)(2,1)S(1)}, bf16[432,512]{1,0:T(8,128)(2,1)S(1)}, u32[]{:S(2)}, u32[]{:S(2)}) collective-permute-start(bf16[432,512]{1,0:T(8,128)(2,1)S(1)} %slice.75), channel_id=1, source_target_pairs={{0,2},{1,3},{4,0},{5,1},{8,4},{9,5},{12,8},{13,9},{14,12},{15,13},... | collective-permute-start | bytes 1327112 | tf_op jit(solution)/shard_map/ppermute | solution.py:404
  104.3 0.8 copy-start.7
  105.0 0.8 copy-start.8
  105.8 7.2 %copy-start.15 = (s32[512]{0:T(512)S(1)}, s32[512]{0:T(512)}, u32[]{:S(2)}) copy-start(s32[512]{0:T(512)} %param.27) | copy-start | bytes 6148
  110.2 7.6 %collective-permute-start.15 = (f32[512,512]{1,0:T(8,128)}, f32[512,512]{1,0:T(8,128)S(1)}, u32[]{:S(2)}, u32[]{:S(2)}) collective-permute-start(f32[512,512]{1,0:T(8,128)} %shard_map.152), channel_id=1, source_target_pairs={{0,1},{1,0},{2,3},{3,2},{4,5},{5,4},{6,7},{7,6},{8,9},{9,8},{10,11... | collective-permute-start | bytes 3145736 | tf_op jit(solution)/shard_map/ppermute | solution.py:465
  113.3 4.6 %copy-start.1 = (bf16[512,512]{1,0:T(8,128)(2,1)S(1)}, bf16[512,512]{1,0:T(8,128)(2,1)}, u32[]{:S(2)}) copy-start(bf16[512,512]{1,0:T(8,128)(2,1)} %features_ref.3) | copy-start | bytes 1572868
  113.3 4.6 %copy-start.2 = (bf16[512,512]{1,0:T(8,128)(2,1)S(1)}, bf16[512,512]{1,0:T(8,128)(2,1)}, u32[]{:S(2)}) copy-start(bf16[512,512]{1,0:T(8,128)(2,1)} %weight_ref.1) | copy-start | bytes 1572868
  113.3 4.6 %copy-start.3 = (f32[512]{0:T(512)S(1)}, f32[512]{0:T(512)}, u32[]{:S(2)}) copy-start(f32[512]{0:T(512)} %param.18) | copy-start | bytes 6148
  117.9 1.2 copy-start
  121.5 5.2 %copy-start.9 = (bf16[512,1536]{1,0:T(8,128)(2,1)S(1)}, bf16[512,1536]{1,0:T(8,128)(2,1)}, u32[]{:S(2)}) copy-start(bf16[512,1536]{1,0:T(8,128)(2,1)} %param.20) | copy-start | bytes 4718596
  121.5 30.2 %all-to-all-start = ((bf16[16,64,512]{2,1,0:T(8,128)(2,1)}), bf16[16,64,512]{2,1,0:T(8,128)(2,1)}, u32[]{:S(2)}, u32[]{:S(2)}) async-start(bf16[16,64,512]{2,1,0:T(8,128)(2,1)} %bitcast.10), calls=%async_computation | async-start | bytes 2097152 | tf_op jit(solution)/shard_map/all_to_all | solution.py:481
  126.7 1.3 copy-start.17
  128.3 23.3 %copy-start.16 = (s32[512]{0:T(512)}, s32[512]{0:T(512)S(1)}, u32[]{:S(2)}) copy-start(s32[512]{0:T(512)S(1)} %multiply_add_fusion) | copy-start | bytes 6148
  175.9 29.8 %all-to-all-start.1 = ((bf16[16,64,512]{2,1,0:T(8,128)(2,1)}), bf16[16,64,512]{2,1,0:T(8,128)(2,1)S(1)}, u32[]{:S(2)}, u32[]{:S(2)}) async-start(bf16[16,64,512]{2,1,0:T(8,128)(2,1)} %bitcast.29), calls=%async_computation.1 | async-start | bytes 2097152 | tf_op jit(solution)/shard_map/all_to_all | solution.py:512

commit v10 on v9

--- a/solution.py
+++ b/solution.py
@@ -83,27 +83,24 @@
 
 def gather_kernel(taps, start_ref, rows_ref, own_ref, got_ref, out_ref):
     half = own_ref.shape[1]
-    part = lax.rem(lax.broadcasted_iota(jnp.int32, (rows_ref.shape[1], 128), 0), 128)
-    lane = lax.broadcasted_iota(jnp.int32, (1, 128), 1)
+    lane = lax.broadcasted_iota(jnp.int32, rows_ref.shape, 1)
+    parts = []
+    for table, start in ((own_ref, 0), (got_ref, start_ref[0])):
+        ids = lax.broadcasted_iota(jnp.int32, (1, table.shape[0]), 1) + start
+        parts.append((table, ids.astype(F32)))
     for at in range(taps):
-        chosen = one_hot(part == taps * pl.program_id(0) + at)
-        index = dot(rows_ref[...], chosen)
-        taken = None
-        for table, start in ((own_ref, 0), (got_ref, start_ref[0])):
-            hits = [
-                one_hot(index == (lane + (start + first)).astype(F32))
-                for first in range(0, table.shape[0], 128)
-            ]
-            product = dot(jnp.concatenate(hits, axis=1), table[...])
-            taken = product if taken is None else taken + product
-        out_ref[:, at * half : (at + 1) * half] = taken.astype(BF16)
+        chosen = lane == taps * pl.program_id(0) + at
+        column = jnp.sum(jnp.where(chosen, rows_ref[...], 0.0), axis=1, keepdims=True)
+        hits = [one_hot(column == ids) for _, ids in parts]
+        products = [dot(hit, table[...]) for hit, (table, _) in zip(hits, parts)]
+        out_ref[:, at * half : (at + 1) * half] = (products[0] + products[1]).astype(BF16)
 
 
 def gather_block(start, rows, own, got):
     points, lanes = rows.shape
     half = own.shape[1]
     height = own.shape[0] + got.shape[0]
-    taps = 3
+    taps = 9
     whole = lambda step: (0, 0)
     return call(
         functools.partial(gather_kernel, taps),
@@ -193,8 +190,26 @@
     )(places.reshape(-1), *stacked, *flat, *(before or ()))
 
 
-def mix_kernel(own_ref, got_ref, features_ref, weight_ref, gain_ref, slot_ref, out_ref):
-    convolved = (own_ref[...] + got_ref[...]).astype(BF16)
+def mix_kernel(
+    count,
+    places_ref,
+    own_ref,
+    got_ref,
+    features_ref,
+    weight_ref,
+    gain_ref,
+    slot_ref,
+    *refs,
+):
+    out_ref, own_held = refs[-5], refs[-4]
+    if count:
+        conv_kernel(
+            [count], 1, False, places_ref, *refs[: 1 + count], own_ref, own_held, *refs[-3:]
+        )
+        own = own_held[...]
+    else:
+        own = own_ref[...]
+    convolved = (own + got_ref[...]).astype(BF16)
     linear = dot(convolved, weight_ref[...])
     mixed = (features_ref[...].astype(F32) + layer_norm(linear, gain_ref[...])).astype(BF16)
     slots = lax.broadcasted_iota(jnp.int32, (out_ref.shape[0], mixed.shape[0]), 0)
@@ -329,8 +344,7 @@
     rest = jnp.zeros((points, 128 - TAPS), jnp.int32)
     middle = TAPS // 2
     rows = jnp.concatenate([neighbours[:, :middle], own, neighbours[:, middle:], rest], axis=1)
-    fine = rows % 32
-    return jnp.concatenate([rows - fine, fine], axis=1).astype(BF16)
+    return rows.astype(F32)
 
 
 def body(
@@ -447,12 +461,15 @@
         sums = conv_part(stacked, places[5:7], [[back[3]], [on[3]]], sums, length)
         last = [[back[4], on[4]]]
         (for_partner,) = conv_part(stacked[:1], places[7:], last, sums[:1], length)
-        (own_part,) = conv_part(stacked[1:], places[7:], last, sums[1:], length)
+        own_part = sums[1]
+        rest = [stacked[1], *last[0]]
+        places = places[7]
     else:
         groups = [list(range(first, devices, 2)) for first in range(2)]
         weight = lax.all_gather(mine, "blocks", axis=0, tiled=True, axis_index_groups=groups)
         nowhere = jnp.zeros((1, 2), jnp.int32)
         for_partner, own_part = conv_part(stacked, nowhere, [[weight]], None, length)
+        places, rest = nowhere[0], []
 
     positions = jnp.arange(points, dtype=jnp.int32)
     target = serial_rank // points
@@ -465,18 +482,29 @@
     from_partner = lax.ppermute(for_partner, "blocks", partner)
 
     outgoing = call(
-        mix_kernel,
+        functools.partial(mix_kernel, len(rest) - 1 if rest else 0),
         jax.ShapeDtypeStruct((slots, width), BF16),
-        32,
-        2 * points * width * (width + slots),
+        48,
+        2 * points * width * (width + slots + length),
         8 * points * width,
+        in_specs=[pl.BlockSpec(memory_space=pltpu.SMEM)]
+        + [pl.BlockSpec()] * 6
+        + [pl.BlockSpec(memory_space=pl.ANY)] * len(rest),
+        scratch_shapes=[
+            pltpu.VMEM((points, width), F32),
+            pltpu.VMEM((1, 1, points, length if rest else 128), BF16),
+            pltpu.VMEM((1, length if rest else 128, width), BF16),
+            pltpu.SemaphoreType.DMA((1, 4)),
+        ],
     )(
+        places,
         own_part,
         from_partner,
         features,
         cpe_weight,
         cpe_gain.reshape(1, width),
         out_slot.reshape(1, points),
+        *rest,
     )
     arrived = lax.all_to_all(
         outgoing.reshape(devices, capacity, width), "blocks", split_axis=0, concat_axis=0, tiled=True

time: 208 us -> 201 us (0.966)
  Pallas kernels: 85.3 us -> 75.7 us
    pallas_call x2, Pallas kernels: 28.9 us -> 21.2 us  [gather_block(): call(functools.partial(gather_kernel, taps), jax.ShapeDtypeStruct((points...]
    pallas_call x4 -> x3, Pallas kernels: 25.3 us -> 21 us  [conv_part(): call(functools.partial(conv_kernel, slots, blocks, before is None), [jax....]
    pallas_call x1, Pallas kernels: 2.33 us -> 4.77 us  [body(): call(functools.partial(mix_kernel, len(rest) - 1 if rest else 0), jax.Sha...]
    ppermute x1, waiting for transfers between devices: 0.01 us -> 2.12 us  [body(): from_partner = lax.ppermute(for_partner, 'blocks', partner)]
    unnamed x45 -> x53, local copies, waits for them, and re-layouts: 3.97 us -> 4.79 us
  transfers between devices with their start and end apart: 18 -> 18, of which waited for: 9 -> 10; matrix products, arithmetic and copies ran while one was open for 5% -> 5% of each run, Pallas kernels for 25% -> 20%
where the time goes in v10:
time: 201 us
  waiting for transfers between devices  78.4 us (39%)
  Pallas kernels  75.7 us (38%)
  starting transfers between devices  29.9 us (15%)
  local copies, waits for them, and re-layouts  12.4 us (6%)
  other arithmetic  3.78 us (2%)
    all_to_all x1, waiting for transfers between devices, body(): lax.all_to_all(back.reshape(devices, capacity, width), 'blocks', split_ax...  24.7 us
    pallas_call x1, Pallas kernels, body(): call(block_kernel, jax.ShapeDtypeStruct((slots, width), BF16), 60, 20 * p...  24.2 us
    all_to_all x1, waiting for transfers between devices, body(): lax.all_to_all(outgoing.reshape(devices, capacity, width), 'blocks', spli...  21.4 us
    pallas_call x2, Pallas kernels, gather_block(): call(functools.partial(gather_kernel, taps), jax.ShapeDtypeStruct((points...  21.2 us
    pallas_call x3, Pallas kernels, conv_part(): call(functools.partial(conv_kernel, slots, blocks, before is None), [jax....  21 us
    ppermute x4, waiting for transfers between devices, pass_on(): back.append(lax.ppermute(first, 'blocks', back_pairs))  17.4 us
    ppermute x1, waiting for transfers between devices, body(): lists = lax.ppermute(lists, 'blocks', side)  7.19 us
    all_to_all x1, starting transfers between devices, body(): lax.all_to_all(outgoing.reshape(devices, capacity, width), 'blocks', spli...  5.61 us
  transfers between devices with their start and end apart: 18, of which 10 were waited for; matrix products, arithmetic and copies ran while one was open for 5% of the time, Pallas kernels for 20%

profile of v10, /device:TPU:9, one launch (start us, length us, event | category | flops | bytes accessed | tf_op | source)
XLA Modules:
  0.0 200.6 jit_solution(3214318639035727240)
XLA Ops:
  0.0 1.1 slice.64
  1.1 0.7 collective-permute-start
  1.9 0.7 slice_bitcast_fusion
  2.6 0.8 select_bitcast_fusion
  3.3 0.8 reshape.89.rows_ref
  4.2 2.5 %shard_map.145 = (bf16[512,256]{1,0:T(8,128)(2,1)}, bf16[512,256]{1,0:T(8,128)(2,1)}, bf16[192,512]{1,0:T(8,128)(2,1)}, bf16[64,512]{1,0:T(8,128)(2,1)}, bf16[64,512]{1,0:T(8,128)(2,1)}) custom-call(s32[1]{0:T(128)} %bitcast.3.core_ref, bf16[512,512]{1,0:T(8,128)(2,1)} %features_ref.3, s32[320,1]{1,0:T(8,128)} %reshape.89.rows_ref), custom_call_target="tpu_custom_call" | custom-call | flops 536870912 | bytes 2097152 | tf_op jit(solution)/shard_map/pallas_call | solution.py:392
  6.6 0.1 copy.33
  6.8 0.6 collective-permute-start.2
  7.4 0.1 copy.34
  7.6 0.1 copy.35
  7.7 0.1 pad.11.clone
  7.8 0.1 pad_add_fusion.1.flags_ref
  7.9 0.1 maximum_select_fusion
  8.0 0.5 collective-permute-done.2
  8.5 2.3 %collective-permute-start.5 = (bf16[192,512]{1,0:T(8,128)(2,1)S(1)}, bf16[192,512]{1,0:T(8,128)(2,1)S(1)}, u32[]{:S(2)}, u32[]{:S(2)}) collective-permute-start(bf16[192,512]{1,0:T(8,128)(2,1)S(1)} %copy-done.23), channel_id=1, source_target_pairs={{0,8},{1,9},{2,10},{3,11},{4,12},{5,13},{6,14},{7,15},{8,0},{9,1},... | collective-permute-start | bytes 589832 | tf_op jit(solution)/shard_map/ppermute | solution.py:425
  10.8 1.5 collective-permute-start.4
  12.3 0.1 fusion.6
  12.4 7.2 %collective-permute-done.5.side_ref = bf16[192,512]{1,0:T(8,128)(2,1)S(1)} collective-permute-done((bf16[192,512]{1,0:T(8,128)(2,1)S(1)}, bf16[192,512]{1,0:T(8,128)(2,1)S(1)}, u32[]{:S(2)}, u32[]{:S(2)}) %collective-permute-start.5) | collective-permute-done | bytes 196640 | tf_op jit(solution)/shard_map/ppermute | solution.py:425
  19.7 3.6 %collective-permute-start.6 = (bf16[128,512]{1,0:T(8,128)(2,1)S(1)}, bf16[128,512]{1,0:T(8,128)(2,1)S(1)}, u32[]{:S(2)}, u32[]{:S(2)}) collective-permute-start(bf16[128,512]{1,0:T(8,128)(2,1)S(1)} %pad_maximum_fusion), channel_id=1, source_target_pairs={{0,1},{1,2},{2,3},{3,4},{4,5},{5,6},{6,7},{8,9},{9,10},{10,11},{11... | collective-permute-start | bytes 393224 | tf_op jit(solution)/shard_map/ppermute | solution.py:430
  23.3 1.9 collective-permute-start.7
  25.2 1.1 add_convert_fusion.1
  26.3 3.7 %collective-permute-done.7.ahead_ref = bf16[128,512]{1,0:T(8,128)(2,1)S(1)} collective-permute-done((bf16[128,512]{1,0:T(8,128)(2,1)S(1)}, bf16[128,512]{1,0:T(8,128)(2,1)S(1)}, u32[]{:S(2)}, u32[]{:S(2)}) %collective-permute-start.7) | collective-permute-done | bytes 131104 | tf_op jit(solution)/shard_map/ppermute | solution.py:431
  30.0 8.6 %collective-permute-done.3.refs_3_ = bf16[864,512]{1,0:T(8,128)(2,1)} collective-permute-done((bf16[864,512]{1,0:T(8,128)(2,1)S(1)}, bf16[864,512]{1,0:T(8,128)(2,1)}, u32[]{:S(2)}, u32[]{:S(2)}) %collective-permute-start.3) | collective-permute-done | bytes 884768 | tf_op jit(solution)/shard_map/ppermute | solution.py:417
  38.6 0.6 shard_map.146
  39.2 0.7 copy-done.9
  39.9 0.5 collective-permute-start.10
  40.4 2.3 %collective-permute-start.8 = (bf16[864,512]{1,0:T(8,128)(2,1)}, bf16[864,512]{1,0:T(8,128)(2,1)S(1)}, u32[]{:S(2)}, u32[]{:S(2)}) collective-permute-start(bf16[864,512]{1,0:T(8,128)(2,1)} %collective-permute-done.3.refs_3_), channel_id=1, source_target_pairs={{0,4},{1,5},{4,8},{5,9},{8,12},{9,13},{12,14},{13,15},{14,10},{15,... | collective-permute-start | bytes 2654216 | tf_op jit(solution)/shard_map/ppermute | solution.py:417
  42.7 10.6 %shard_map.148.refs_1_.refs_0_ = bf16[512,6912]{1,0:T(8,128)(2,1)} custom-call(s32[1]{0:T(128)} %bitcast.6.start_ref, f32[512,128]{1,0:T(8,128)} %get-tuple-element.66.rows_ref, bf16[512,256]{1,0:T(8,128)(2,1)} %get-tuple-element.49.own_ref, bf16[384,256]{1,0:T(8,128)(2,1)} %copy-done.9), custom_call_target="tpu_custom_call" | custom-call | flops 6341787648 | bytes 7077888 | tf_op jit(solution)/shard_map/pallas_call | solution.py:105
  53.3 0.7 copy-done.24
  54.0 10.6 %shard_map.147.refs_0_ = bf16[512,6912]{1,0:T(8,128)(2,1)} custom-call(s32[1]{0:T(128)} %bitcast.6.start_ref, f32[512,128]{1,0:T(8,128)} %get-tuple-element.67.rows_ref, bf16[512,256]{1,0:T(8,128)(2,1)} %collective-permute-done.1.own_ref, bf16[384,256]{1,0:T(8,128)(2,1)} %copy-done.24), custom_call_target="tpu_custom_call" | custom-call | flops 6341787648 | bytes 7077888 | tf_op jit(solution)/shard_map/pallas_call | solution.py:105
  64.6 1.5 collective-permute-start.11
  66.1 0.7 constant_dynamic-slice_fusion
  66.8 0.6 reshape.76.places_ref
  67.4 9.4 %shard_map.149 = (f32[512,512]{1,0:T(8,128)}, f32[512,512]{1,0:T(8,128)}) custom-call(s32[10]{0:T(128)} %reshape.76.places_ref, bf16[512,6912]{1,0:T(8,128)(2,1)} %shard_map.147.refs_0_, bf16[512,6912]{1,0:T(8,128)(2,1)} %shard_map.148.refs_1_.refs_0_, bf16[864,512]{1,0:T(8,128)(2,1)} %bitcast.34, bf16[864,512]{1,0:T(8,128)(2,1)} %collective-permute-done.3.refs_3_, ...), custom_call_target="tpu_custom_call" | custom-call | flops 5368709120 | bytes 15728640 | tf_op jit(solution)/shard_map/pallas_call | solution.py:173
  76.8 8.7 %collective-permute-done.11.refs_2_ = bf16[864,512]{1,0:T(8,128)(2,1)S(1)} collective-permute-done((bf16[864,512]{1,0:T(8,128)(2,1)S(1)}, bf16[864,512]{1,0:T(8,128)(2,1)S(1)}, u32[]{:S(2)}, u32[]{:S(2)}) %collective-permute-start.11) | collective-permute-done | bytes 884768 | tf_op jit(solution)/shard_map/ppermute | solution.py:417
  85.6 0.8 collective-permute-done.12.refs_3_
  86.4 0.4 collective-permute-start.13
  86.9 1.3 collective-permute-start.14
  88.2 0.6 reshape.71.places_ref
  88.8 0.6 slice_bitcast_fusion.1.places_ref
  89.4 6.9 %shard_map.150 = (f32[512,512]{1,0:T(8,128)}, f32[512,512]{1,0:T(8,128)}) custom-call(s32[4]{0:T(128)} %reshape.71.places_ref, bf16[512,6912]{1,0:T(8,128)(2,1)} %shard_map.147.refs_0_, bf16[512,6912]{1,0:T(8,128)(2,1)} %shard_map.148.refs_1_.refs_0_, bf16[864,512]{1,0:T(8,128)(2,1)} %copy-done.10, ...), custom_call_target="tpu_custom_call", output_to_operand_aliasing={{0}: (5, {}), {1}: (6, {})} | custom-call | flops 2147483648 | bytes 6291456 | tf_op jit(solution)/shard_map/pallas_call | solution.py:173
  96.4 0.7 collective-permute-done.14.refs_2_
  97.1 0.1 copy-done.1
  97.1 0.7 copy-done.3
  97.9 4.6 %shard_map.151 = f32[512,512]{1,0:T(8,128)} custom-call(s32[2]{0:T(128)} %slice_bitcast_fusion.1.places_ref, bf16[512,6912]{1,0:T(8,128)(2,1)} %shard_map.147.refs_0_, bf16[432,512]{1,0:T(8,128)(2,1)} %copy-done.1, bf16[432,512]{1,0:T(8,128)(2,1)} %copy-done.3, f32[512,512]{1,0:T(8,128)} %get-tuple-element.62.refs_3_), custom_call_target="tpu_custom_call", output_to_operand_aliasing={{}: (4, {})} | custom-call | flops 536870912 | bytes 2097152 | tf_op jit(solution)/shard_map/pallas_call | solution.py:173
  102.4 2.7 %collective-permute-start.15 = (f32[512,512]{1,0:T(8,128)}, f32[512,512]{1,0:T(8,128)S(1)}, u32[]{:S(2)}, u32[]{:S(2)}) collective-permute-start(f32[512,512]{1,0:T(8,128)} %shard_map.151), channel_id=1, source_target_pairs={{0,1},{1,0},{2,3},{3,2},{4,5},{5,4},{6,7},{7,6},{8,9},{9,8},{10,11... | collective-permute-start | bytes 3145736 | tf_op jit(solution)/shard_map/ppermute | solution.py:482
  105.2 0.3 convert_reduce_fusion.1
  105.5 2.1 %collective-permute-done.15.got_ref = f32[512,512]{1,0:T(8,128)S(1)} collective-permute-done((f32[512,512]{1,0:T(8,128)}, f32[512,512]{1,0:T(8,128)S(1)}, u32[]{:S(2)}, u32[]{:S(2)}) %collective-permute-start.15) | collective-permute-done | bytes 1048608 | tf_op jit(solution)/shard_map/ppermute | solution.py:482
  107.7 1.0 copy-done.2
  108.7 1.0 copy-done.4
  109.7 4.8 %shard_map.152 = bf16[1024,512]{1,0:T(8,128)(2,1)} custom-call(s32[2]{0:T(128)S(1)} %copy-done.7, f32[512,512]{1,0:T(8,128)S(1)} %copy-done, f32[512,512]{1,0:T(8,128)S(1)} %collective-permute-done.15.got_ref, bf16[512,512]{1,0:T(8,128)(2,1)S(1)} %copy-done.5, bf16[512,512]{1,0:T(8,128)(2,1)S(1)} %copy-done.6, f32[1,512]{1,0:T(1,128)S(1)} %bitcast.28, ...), custom_call_target="tpu_custom_call" | custom-call | flops 1342177280 | bytes 2097152 | tf_op jit(solution)/shard_map/pallas_call | solution.py:484
  114.5 5.6 %all-to-all-start = ((bf16[16,64,512]{2,1,0:T(8,128)(2,1)}), bf16[16,64,512]{2,1,0:T(8,128)(2,1)}, u32[]{:S(2)}, u32[]{:S(2)}) async-start(bf16[16,64,512]{2,1,0:T(8,128)(2,1)} %bitcast.10), calls=%async_computation | async-start | bytes 2097152 | tf_op jit(solution)/shard_map/all_to_all | solution.py:509
  120.1 0.9 fusion.5
  121.0 0.2 copy.40
  121.2 0.2 copy.41
  121.5 0.2 convert_reduce_fusion
  121.8 0.9 copy.38.slot_col_ref
  122.6 1.1 maximum_bitcast_fusion.qv_hbm
  123.7 21.4 %all-to-all-done = bf16[16,64,512]{2,1,0:T(8,128)(2,1)} async-done(((bf16[16,64,512]{2,1,0:T(8,128)(2,1)}), bf16[16,64,512]{2,1,0:T(8,128)(2,1)}, u32[]{:S(2)}, u32[]{:S(2)}) %all-to-all-start) | async-done | bytes 1048608 | tf_op jit(solution)/shard_map/all_to_all | solution.py:509
  145.1 24.2 %shard_map.153 = bf16[1024,512]{1,0:T(8,128)(2,1)} custom-call(bf16[1024,512]{1,0:T(8,128)(2,1)} %bitcast.11.arrived_ref, s32[512,1]{1,0:T(8,128)} %copy.38.slot_col_ref, s32[1,512]{1,0:T(1,128)} %bitcast.37, f32[1,512]{1,0:T(1,128)} %bitcast.38, f32[1,512]{1,0:T(1,128)} %bitcast.39, bf16[1024,512]{1,0:T(8,128)(2,1)} %maximum_bitcast_fusion.qv_hbm, ...), custom_call_target="tpu_custom_call" | custom-call | flops 2684354560 | bytes 4194304 | tf_op jit(solution)/shard_map/pallas_call | solution.py:516
  169.3 5.0 %all-to-all-start.1 = ((bf16[16,64,512]{2,1,0:T(8,128)(2,1)}), bf16[16,64,512]{2,1,0:T(8,128)(2,1)S(1)}, u32[]{:S(2)}, u32[]{:S(2)}) async-start(bf16[16,64,512]{2,1,0:T(8,128)(2,1)} %bitcast.29), calls=%async_computation.1 | async-start | bytes 2097152 | tf_op jit(solution)/shard_map/all_to_all | solution.py:540
  174.2 0.1 copy.39.slot_ref
  174.4 24.7 %all-to-all-done.1 = bf16[16,64,512]{2,1,0:T(8,128)(2,1)S(1)} async-done(((bf16[16,64,512]{2,1,0:T(8,128)(2,1)}), bf16[16,64,512]{2,1,0:T(8,128)(2,1)S(1)}, u32[]{:S(2)}, u32[]{:S(2)}) %all-to-all-start.1) | async-done | bytes 1048608 | tf_op jit(solution)/shard_map/all_to_all | solution.py:540
  199.1 1.5 shard_map.154
  (71 shorter events, 0.4 us)
Async XLA Ops:
  0.0 7.3 %copy-start.13 = (bf16[864,512]{1,0:T(8,128)(2,1)S(1)}, bf16[864,512]{1,0:T(8,128)(2,1)}, u32[]{:S(2)}) copy-start(bf16[864,512]{1,0:T(8,128)(2,1)} %param.16) | copy-start | bytes 2654212
  0.0 6.6 %copy-start.15 = (s32[512,26]{0,1:T(8,128)S(1)}, s32[512,26]{0,1:T(8,128)}, u32[]{:S(2)}) copy-start(s32[512,26]{0,1:T(8,128)} %param.26) | copy-start | bytes 159748
  1.1 6.7 %collective-permute-start = (bf16[13,32,512]{2,1,0:T(8,128)(2,1)S(1)}, bf16[13,32,512]{2,1,0:T(8,128)(2,1)S(1)}, u32[]{:S(2)}, u32[]{:S(2)}) collective-permute-start(bf16[13,32,512]{2,1,0:T(8,128)(2,1)S(1)} %slice.64), channel_id=1, source_target_pairs={{0,1},{1,0},{2,3},{3,2},{4,5},{5,4},{6,7},{7,6},{8,9},{9,8},{10,11... | collective-permute-start | bytes 1277960 | tf_op jit(solution)/shard_map/ppermute | solution.py:378
  6.6 1.9 collective-permute-start.1
  6.8 1.7 collective-permute-start.2
  7.3 12.3 %copy-start.17 = (bf16[64,512]{1,0:T(8,128)(2,1)S(1)}, bf16[64,512]{1,0:T(8,128)(2,1)}, u32[]{:S(2)}) copy-start(bf16[64,512]{1,0:T(8,128)(2,1)} %get-tuple-element.39) | copy-start | bytes 196612
  7.4 1.1 copy-start.23
  7.4 15.8 %copy-start.16 = (bf16[64,512]{1,0:T(8,128)(2,1)S(1)}, bf16[64,512]{1,0:T(8,128)(2,1)}, u32[]{:S(2)}) copy-start(bf16[64,512]{1,0:T(8,128)(2,1)} %get-tuple-element.40) | copy-start | bytes 196612
  8.0 31.2 %copy-start.14 = (bf16[27,32,512]{2,1,0:T(8,128)(2,1)}, bf16[27,32,512]{2,1,0:T(8,128)(2,1)S(1)}, u32[]{:S(2)}) copy-start(bf16[27,32,512]{2,1,0:T(8,128)(2,1)S(1)} %maximum_select_fusion) | copy-start | bytes 2654212
  8.5 11.1 %collective-permute-start.5 = (bf16[192,512]{1,0:T(8,128)(2,1)S(1)}, bf16[192,512]{1,0:T(8,128)(2,1)S(1)}, u32[]{:S(2)}, u32[]{:S(2)}) collective-permute-start(bf16[192,512]{1,0:T(8,128)(2,1)S(1)} %copy-done.23), channel_id=1, source_target_pairs={{0,8},{1,9},{2,10},{3,11},{4,12},{5,13},{6,14},{7,15},{8,0},{9,1},... | collective-permute-start | bytes 589832 | tf_op jit(solution)/shard_map/ppermute | solution.py:425
  10.8 27.8 %collective-permute-start.3 = (bf16[864,512]{1,0:T(8,128)(2,1)S(1)}, bf16[864,512]{1,0:T(8,128)(2,1)}, u32[]{:S(2)}, u32[]{:S(2)}) collective-permute-start(bf16[864,512]{1,0:T(8,128)(2,1)S(1)} %bitcast.32), channel_id=1, source_target_pairs={{0,4},{1,5},{4,8},{5,9},{8,12},{9,13},{12,14},{13,15},{14,10},{15,... | collective-permute-start | bytes 2654216 | tf_op jit(solution)/shard_map/ppermute | solution.py:417
  10.8 27.8 %collective-permute-start.4 = (bf16[864,512]{1,0:T(8,128)(2,1)S(1)}, bf16[864,512]{1,0:T(8,128)(2,1)}, u32[]{:S(2)}, u32[]{:S(2)}) collective-permute-start(bf16[864,512]{1,0:T(8,128)(2,1)S(1)} %bitcast.33), channel_id=1, source_target_pairs={{0,2},{1,3},{4,0},{5,1},{8,4},{9,5},{12,8},{13,9},{14,12},{15,13},... | collective-permute-start | bytes 2654216 | tf_op jit(solution)/shard_map/ppermute | solution.py:418
  19.7 6.6 %collective-permute-start.6 = (bf16[128,512]{1,0:T(8,128)(2,1)S(1)}, bf16[128,512]{1,0:T(8,128)(2,1)S(1)}, u32[]{:S(2)}, u32[]{:S(2)}) collective-permute-start(bf16[128,512]{1,0:T(8,128)(2,1)S(1)} %pad_maximum_fusion), channel_id=1, source_target_pairs={{0,1},{1,2},{2,3},{3,4},{4,5},{5,6},{6,7},{8,9},{9,10},{10,11},{11... | collective-permute-start | bytes 393224 | tf_op jit(solution)/shard_map/ppermute | solution.py:430
  23.3 6.7 %collective-permute-start.7 = (bf16[128,512]{1,0:T(8,128)(2,1)S(1)}, bf16[128,512]{1,0:T(8,128)(2,1)S(1)}, u32[]{:S(2)}, u32[]{:S(2)}) collective-permute-start(bf16[128,512]{1,0:T(8,128)(2,1)S(1)} %pad_maximum_fusion.1), channel_id=1, source_target_pairs={{1,0},{2,1},{3,2},{4,3},{5,4},{6,5},{7,6},{9,8},{10,9},{11,10},{12... | collective-permute-start | bytes 393224 | tf_op jit(solution)/shard_map/ppermute | solution.py:431
  39.2 0.7 copy-start.9
  39.9 13.4 %collective-permute-start.10 = (bf16[384,256]{1,0:T(8,128)(2,1)S(1)}, bf16[384,256]{1,0:T(8,128)(2,1)S(1)}, u32[]{:S(2)}, u32[]{:S(2)}) collective-permute-start(bf16[384,256]{1,0:T(8,128)(2,1)S(1)} %get-tuple-element.48), channel_id=1, source_target_pairs={{0,1},{1,0},{2,3},{3,2},{4,5},{5,4},{6,7},{7,6},{8,9},{9,8},{10,11... | collective-permute-start | bytes 589832 | tf_op jit(solution)/shard_map/ppermute | solution.py:452
  40.4 24.2 %collective-permute-start.8 = (bf16[864,512]{1,0:T(8,128)(2,1)}, bf16[864,512]{1,0:T(8,128)(2,1)S(1)}, u32[]{:S(2)}, u32[]{:S(2)}) collective-permute-start(bf16[864,512]{1,0:T(8,128)(2,1)} %collective-permute-done.3.refs_3_), channel_id=1, source_target_pairs={{0,4},{1,5},{4,8},{5,9},{8,12},{9,13},{12,14},{13,15},{14,10},{15,... | collective-permute-start | bytes 2654216 | tf_op jit(solution)/shard_map/ppermute | solution.py:417
  42.7 21.9 %collective-permute-start.9 = (bf16[864,512]{1,0:T(8,128)(2,1)}, bf16[864,512]{1,0:T(8,128)(2,1)S(1)}, u32[]{:S(2)}, u32[]{:S(2)}) collective-permute-start(bf16[864,512]{1,0:T(8,128)(2,1)} %collective-permute-done.4.refs_4_), channel_id=1, source_target_pairs={{0,2},{1,3},{4,0},{5,1},{8,4},{9,5},{12,8},{13,9},{14,12},{15,13},... | collective-permute-start | bytes 2654216 | tf_op jit(solution)/shard_map/ppermute | solution.py:418
  53.3 0.7 copy-start.24
  64.6 2.8 %copy-start.21 = (bf16[864,512]{1,0:T(8,128)(2,1)}, bf16[864,512]{1,0:T(8,128)(2,1)S(1)}, u32[]{:S(2)}) copy-start(bf16[864,512]{1,0:T(8,128)(2,1)S(1)} %collective-permute-done.8.refs_5_) | copy-start | bytes 2654212
  64.6 2.8 %copy-start.22 = (bf16[864,512]{1,0:T(8,128)(2,1)}, bf16[864,512]{1,0:T(8,128)(2,1)S(1)}, u32[]{:S(2)}) copy-start(bf16[864,512]{1,0:T(8,128)(2,1)S(1)} %collective-permute-done.9.refs_6_) | copy-start | bytes 2654212
  64.6 21.0 %collective-permute-start.11 = (bf16[864,512]{1,0:T(8,128)(2,1)S(1)}, bf16[864,512]{1,0:T(8,128)(2,1)S(1)}, u32[]{:S(2)}, u32[]{:S(2)}) collective-permute-start(bf16[864,512]{1,0:T(8,128)(2,1)S(1)} %collective-permute-done.8.refs_5_), channel_id=1, source_target_pairs={{0,4},{1,5},{4,8},{5,9},{8,12},{9,13},{12,14},{13,15},{14,10},{15,... | collective-permute-start | bytes 2654216 | tf_op jit(solution)/shard_map/ppermute | solution.py:417
  66.1 20.3 %collective-permute-start.12 = (bf16[864,512]{1,0:T(8,128)(2,1)S(1)}, bf16[864,512]{1,0:T(8,128)(2,1)S(1)}, u32[]{:S(2)}, u32[]{:S(2)}) collective-permute-start(bf16[864,512]{1,0:T(8,128)(2,1)S(1)} %collective-permute-done.9.refs_6_), channel_id=1, source_target_pairs={{0,2},{1,3},{4,0},{5,1},{8,4},{9,5},{12,8},{13,9},{14,12},{15,13},... | collective-permute-start | bytes 2654216 | tf_op jit(solution)/shard_map/ppermute | solution.py:418
  85.6 3.8 %copy-start.10 = (bf16[864,512]{1,0:T(8,128)(2,1)}, bf16[864,512]{1,0:T(8,128)(2,1)S(1)}, u32[]{:S(2)}) copy-start(bf16[864,512]{1,0:T(8,128)(2,1)S(1)} %collective-permute-done.11.refs_2_) | copy-start | bytes 2654212
  86.4 3.0 %copy-start.11 = (bf16[864,512]{1,0:T(8,128)(2,1)}, bf16[864,512]{1,0:T(8,128)(2,1)S(1)}, u32[]{:S(2)}) copy-start(bf16[864,512]{1,0:T(8,128)(2,1)S(1)} %collective-permute-done.12.refs_3_) | copy-start | bytes 2654212
  86.4 9.9 %collective-permute-start.13 = (bf16[432,512]{1,0:T(8,128)(2,1)S(1)}, bf16[432,512]{1,0:T(8,128)(2,1)S(1)}, u32[]{:S(2)}, u32[]{:S(2)}) collective-permute-start(bf16[432,512]{1,0:T(8,128)(2,1)S(1)} %slice.75), channel_id=1, source_target_pairs={{0,4},{1,5},{4,8},{5,9},{8,12},{9,13},{12,14},{13,15},{14,10},{15,... | collective-permute-start | bytes 1327112 | tf_op jit(solution)/shard_map/ppermute | solution.py:417
  86.9 10.2 %collective-permute-start.14 = (bf16[432,512]{1,0:T(8,128)(2,1)S(1)}, bf16[432,512]{1,0:T(8,128)(2,1)S(1)}, u32[]{:S(2)}, u32[]{:S(2)}) collective-permute-start(bf16[432,512]{1,0:T(8,128)(2,1)S(1)} %slice.76), channel_id=1, source_target_pairs={{0,2},{1,3},{4,0},{5,1},{8,4},{9,5},{12,8},{13,9},{14,12},{15,13},... | collective-permute-start | bytes 1327112 | tf_op jit(solution)/shard_map/ppermute | solution.py:418
  96.4 0.8 copy-start.1
  97.1 0.8 copy-start.3
  97.8 7.3 %copy-start.18 = (s32[512]{0:T(512)S(1)}, s32[512]{0:T(512)}, u32[]{:S(2)}) copy-start(s32[512]{0:T(512)} %param.27) | copy-start | bytes 6148
  97.8 9.8 %copy-start = (f32[512,512]{1,0:T(8,128)S(1)}, f32[512,512]{1,0:T(8,128)}, u32[]{:S(2)}) copy-start(f32[512,512]{1,0:T(8,128)} %get-tuple-element.61.own_ref) | copy-start | bytes 3145732
  97.8 9.8 %copy-start.5 = (bf16[512,512]{1,0:T(8,128)(2,1)S(1)}, bf16[512,512]{1,0:T(8,128)(2,1)}, u32[]{:S(2)}) copy-start(bf16[512,512]{1,0:T(8,128)(2,1)} %features_ref.3) | copy-start | bytes 1572868
  97.8 9.8 %copy-start.6 = (bf16[512,512]{1,0:T(8,128)(2,1)S(1)}, bf16[512,512]{1,0:T(8,128)(2,1)}, u32[]{:S(2)}) copy-start(bf16[512,512]{1,0:T(8,128)(2,1)} %weight_ref.1) | copy-start | bytes 1572868
  97.8 9.8 %copy-start.7 = (s32[2]{0:T(128)S(1)}, s32[2]{0:T(128)}, u32[]{:S(2)}) copy-start(s32[2]{0:T(128)} %slice_bitcast_fusion.1.places_ref) | copy-start | bytes 28
  97.8 9.8 %copy-start.8 = (f32[512]{0:T(512)S(1)}, f32[512]{0:T(512)}, u32[]{:S(2)}) copy-start(f32[512]{0:T(512)} %param.18) | copy-start | bytes 6148
  102.4 5.2 %collective-permute-start.15 = (f32[512,512]{1,0:T(8,128)}, f32[512,512]{1,0:T(8,128)S(1)}, u32[]{:S(2)}, u32[]{:S(2)}) collective-permute-start(f32[512,512]{1,0:T(8,128)} %shard_map.151), channel_id=1, source_target_pairs={{0,1},{1,0},{2,3},{3,2},{4,5},{5,4},{6,7},{7,6},{8,9},{9,8},{10,11... | collective-permute-start | bytes 3145736 | tf_op jit(solution)/shard_map/ppermute | solution.py:482
  107.7 1.0 copy-start.2
  108.7 1.0 copy-start.4
  114.5 5.6 %copy-start.12 = (bf16[512,1536]{1,0:T(8,128)(2,1)S(1)}, bf16[512,1536]{1,0:T(8,128)(2,1)}, u32[]{:S(2)}) copy-start(bf16[512,1536]{1,0:T(8,128)(2,1)} %param.20) | copy-start | bytes 4718596
  114.5 30.6 %all-to-all-start = ((bf16[16,64,512]{2,1,0:T(8,128)(2,1)}), bf16[16,64,512]{2,1,0:T(8,128)(2,1)}, u32[]{:S(2)}, u32[]{:S(2)}) async-start(bf16[16,64,512]{2,1,0:T(8,128)(2,1)} %bitcast.10), calls=%async_computation | async-start | bytes 2097152 | tf_op jit(solution)/shard_map/all_to_all | solution.py:509
  120.1 1.3 copy-start.20
  121.8 23.3 %copy-start.19 = (s32[512]{0:T(512)}, s32[512]{0:T(512)S(1)}, u32[]{:S(2)}) copy-start(s32[512]{0:T(512)S(1)} %multiply_add_fusion) | copy-start | bytes 6148
  169.3 29.8 %all-to-all-start.1 = ((bf16[16,64,512]{2,1,0:T(8,128)(2,1)}), bf16[16,64,512]{2,1,0:T(8,128)(2,1)S(1)}, u32[]{:S(2)}, u32[]{:S(2)}) async-start(bf16[16,64,512]{2,1,0:T(8,128)(2,1)} %bitcast.29), calls=%async_computation.1 | async-start | bytes 2097152 | tf_op jit(solution)/shard_map/all_to_all | solution.py:540

commit v11 on v10

--- a/solution.py
+++ b/solution.py
@@ -160,10 +160,10 @@
             elif first:
                 ref[...] = product
             else:
-                ref[...] = before[block][...] + product
-
-
-def conv_part(stacked, places, pieces, before, length):
+                ref[...] = (before[block][...] + product).astype(ref.dtype)
+
+
+def conv_part(stacked, places, pieces, before, length, dtype=F32):
     points, depth = stacked[0].shape
     width = pieces[0][0].shape[1]
     slots = [len(parts) for parts in pieces]
@@ -172,7 +172,7 @@
     held = 1 + blocks + len(flat)
     return call(
         functools.partial(conv_kernel, slots, blocks, before is None),
-        [jax.ShapeDtypeStruct((points, width), F32)] * blocks,
+        [jax.ShapeDtypeStruct((points, width), dtype)] * blocks,
         60,
         2 * blocks * points * length * width * len(slots),
         2 * length * (blocks * points + width) * len(slots),
@@ -180,7 +180,9 @@
         + [pl.BlockSpec(memory_space=pl.ANY)] * (held - 1)
         + ([] if before is None else [pl.BlockSpec()] * blocks),
         input_output_aliases=(
-            {} if before is None else {held + block: block for block in range(blocks)}
+            {}
+            if before is None or dtype != F32
+            else {held + block: block for block in range(blocks)}
         ),
         scratch_shapes=[
             pltpu.VMEM((len(slots), blocks, points, length), BF16),
@@ -191,25 +193,26 @@
 
 
 def mix_kernel(
-    count,
-    places_ref,
-    own_ref,
-    got_ref,
-    features_ref,
-    weight_ref,
-    gain_ref,
-    slot_ref,
-    *refs,
+    count, places_ref, got_ref, gain_ref, slot_ref, own_hbm, features_hbm, weight_hbm, *refs
 ):
-    out_ref, own_held = refs[-5], refs[-4]
+    out_ref, own_ref, features_ref, weight_ref, own_held, load_sems = refs[-9:-3]
+    loads = [
+        pltpu.make_async_copy(source, target, load_sems.at[at])
+        for at, (source, target) in enumerate(
+            ((own_hbm, own_ref), (features_hbm, features_ref), (weight_hbm, weight_ref))
+        )
+    ]
+    for load in loads:
+        load.start()
     if count:
         conv_kernel(
-            [count], 1, False, places_ref, *refs[: 1 + count], own_ref, own_held, *refs[-3:]
+            [count], 1, True, places_ref, *refs[: 1 + count], own_held, *refs[-3:]
         )
-        own = own_held[...]
     else:
-        own = own_ref[...]
-    convolved = (own + got_ref[...]).astype(BF16)
+        own_held[...] = jnp.zeros_like(own_held)
+    for load in loads:
+        load.wait()
+    convolved = (own_ref[...] + own_held[...] + got_ref[...].astype(F32)).astype(BF16)
     linear = dot(convolved, weight_ref[...])
     mixed = (features_ref[...].astype(F32) + layer_norm(linear, gain_ref[...])).astype(BF16)
     slots = lax.broadcasted_iota(jnp.int32, (out_ref.shape[0], mixed.shape[0]), 0)
@@ -239,6 +242,8 @@
     keys_ref,
     heads_ref,
     total_ref,
+    scores_ref,
+    weights_ref,
 ):
     sources = (key_hbm, qv_hbm, proj_hbm, up_hbm, down_hbm)
     targets = (key_ref, qv_ref, proj_ref, up_ref, down_ref)
@@ -269,21 +274,40 @@
     per_group = 128 // HD
     head_of_row = lax.broadcasted_iota(jnp.int32, (128, points), 0) // HD
 
-    for group in range(HEADS // per_group):
-        base = group * 128
-
-        def attend(head, carry):
-            group_queries = qv_cols_ref[base : base + 128]
-            queries = jnp.where(head_of_row == head, group_queries.astype(F32), 0.0).astype(BF16)
-            scores = dot(keys_ref[:, base : base + 128], queries)
-            weights = jnp.exp2(scores - jnp.max(scores, axis=0, keepdims=True)).astype(BF16)
-            at = pl.multiple_of(base + head * HD, HD)
-            values = qv_cols_ref[pl.ds(width + at, HD)]
-            sums = dot(jnp.concatenate([values, ones], axis=0), weights)
-            heads_ref[pl.ds(at, HD)] = (sums[:HD] / sums[HD : HD + 1]).astype(BF16)
-            return carry
-
-        lax.fori_loop(0, per_group, attend, 0, unroll=4)
+    def score(head, slot):
+        base = pl.multiple_of(head // per_group * 128, 128)
+        group_queries = qv_cols_ref[pl.ds(base, 128)].astype(F32)
+        chosen = head_of_row == lax.rem(head, per_group)
+        queries = jnp.where(chosen, group_queries, 0.0).astype(BF16)
+        scores_ref[slot] = dot(keys_ref[:, pl.ds(base, 128)], queries)
+
+    def weigh(slot):
+        scores = scores_ref[slot]
+        weights_ref[slot] = jnp.exp2(scores - jnp.max(scores, axis=0, keepdims=True)).astype(BF16)
+
+    def gather(head, slot):
+        at = pl.multiple_of(head * HD, HD)
+        values = jnp.concatenate([qv_cols_ref[pl.ds(width + at, HD)], ones], axis=0)
+        sums = dot(values, weights_ref[slot])
+        heads_ref[pl.ds(at, HD)] = (sums[:HD] / sums[HD : HD + 1]).astype(BF16)
+
+    score(0, 0)
+    score(1, 1)
+    weigh(0)
+
+    def two_heads(pair, carry):
+        head = 2 * pair + 1
+        for slot in (1, 0):
+            score(head + 1, 1 - slot)
+            weigh(slot)
+            gather(head - 1, 1 - slot)
+            head += 1
+        return carry
+
+    lax.fori_loop(0, HEADS // 2 - 1, two_heads, 0)
+    weigh(1)
+    gather(HEADS - 2, 0)
+    gather(HEADS - 1, 1)
 
     for copy in copies[2:]:
         copy.wait()
@@ -460,7 +484,7 @@
         sums = pass_on(*sums)
         sums = conv_part(stacked, places[5:7], [[back[3]], [on[3]]], sums, length)
         last = [[back[4], on[4]]]
-        (for_partner,) = conv_part(stacked[:1], places[7:], last, sums[:1], length)
+        (for_partner,) = conv_part(stacked[:1], places[7:], last, sums[:1], length, BF16)
         own_part = sums[1]
         rest = [stacked[1], *last[0]]
         places = places[7]
@@ -484,26 +508,30 @@
     outgoing = call(
         functools.partial(mix_kernel, len(rest) - 1 if rest else 0),
         jax.ShapeDtypeStruct((slots, width), BF16),
-        48,
+        60,
         2 * points * width * (width + slots + length),
         8 * points * width,
         in_specs=[pl.BlockSpec(memory_space=pltpu.SMEM)]
-        + [pl.BlockSpec()] * 6
-        + [pl.BlockSpec(memory_space=pl.ANY)] * len(rest),
+        + [pl.BlockSpec()] * 3
+        + [pl.BlockSpec(memory_space=pl.ANY)] * (3 + len(rest)),
         scratch_shapes=[
             pltpu.VMEM((points, width), F32),
+            pltpu.VMEM((points, width), BF16),
+            pltpu.VMEM((width, width), BF16),
+            pltpu.VMEM((points, width), F32),
+            pltpu.SemaphoreType.DMA((3,)),
             pltpu.VMEM((1, 1, points, length if rest else 128), BF16),
             pltpu.VMEM((1, length if rest else 128, width), BF16),
             pltpu.SemaphoreType.DMA((1, 4)),
         ],
     )(
         places,
+        from_partner,
+        cpe_gain.reshape(1, width),
+        out_slot.reshape(1, points),
         own_part,
-        from_partner,
         features,
         cpe_weight,
-        cpe_gain.reshape(1, width),
-        out_slot.reshape(1, points),
         *rest,
     )
     arrived = lax.all_to_all(
@@ -528,6 +556,8 @@
             pltpu.VMEM((points, width), BF16),
             pltpu.VMEM((width, points), BF16),
             pltpu.VMEM((points, width), F32),
+            pltpu.VMEM((2, points, points), F32),
+            pltpu.VMEM((2, points, points), BF16),
         ],
     )(
         arrived,

time: 201 us -> 198 us (0.985)
    pallas_call x1, Pallas kernels: 24.2 us -> 21.6 us  [body(): call(block_kernel, jax.ShapeDtypeStruct((slots, width), BF16), 60, 20 * p...]
    unnamed x53 -> x45, local copies, waits for them, and re-layouts: 4.79 us -> 3.52 us
  transfers between devices with their start and end apart: 18 -> 18, of which waited for: 10 -> 11; matrix products, arithmetic and copies ran while one was open for 5% -> 6% of each run, Pallas kernels for 20% -> 20%
where the time goes in v11:
time: 198 us; the launch traced here: 197 us
  waiting for transfers between devices  77.3 us (39%)
  Pallas kernels  74.4 us (38%)
  starting transfers between devices  29.8 us (15%)
  local copies, waits for them, and re-layouts  11.2 us (6%)
  other arithmetic  4.35 us (2%)
    all_to_all x1, waiting for transfers between devices, body(): lax.all_to_all(back.reshape(devices, capacity, width), 'blocks', split_ax...  24.7 us
    pallas_call x1, Pallas kernels, body(): call(block_kernel, jax.ShapeDtypeStruct((slots, width), BF16), 60, 20 * p...  21.6 us
    all_to_all x1, waiting for transfers between devices, body(): lax.all_to_all(outgoing.reshape(devices, capacity, width), 'blocks', spli...  21.3 us
    pallas_call x2, Pallas kernels, gather_block(): call(functools.partial(gather_kernel, taps), jax.ShapeDtypeStruct((points...  21.2 us
    pallas_call x3, Pallas kernels, conv_part(): call(functools.partial(conv_kernel, slots, blocks, before is None), [jax....  20.6 us
    ppermute x4, waiting for transfers between devices, pass_on(): back.append(lax.ppermute(first, 'blocks', back_pairs))  17.3 us
    ppermute x1, waiting for transfers between devices, body(): lists = lax.ppermute(lists, 'blocks', side)  7.19 us
    pallas_call x1, Pallas kernels, body(): call(functools.partial(mix_kernel, len(rest) - 1 if rest else 0), jax.Sha...  6.36 us
  transfers between devices with their start and end apart: 18, of which 11 were waited for; matrix products, arithmetic and copies ran while one was open for 6% of the time, Pallas kernels for 20%

profile of v11, /device:TPU:9, one launch (start us, length us, event | category | flops | bytes accessed | tf_op | source)
XLA Modules:
  0.0 197.4 jit_solution(4870986050515918572)
XLA Ops:
  0.0 1.1 slice.63
  1.1 0.7 collective-permute-start
  1.9 0.7 slice_bitcast_fusion
  2.6 0.8 select_bitcast_fusion
  3.3 0.8 reshape.89.rows_ref
  4.2 2.5 %shard_map.145 = (bf16[512,256]{1,0:T(8,128)(2,1)}, bf16[512,256]{1,0:T(8,128)(2,1)}, bf16[192,512]{1,0:T(8,128)(2,1)}, bf16[64,512]{1,0:T(8,128)(2,1)}, bf16[64,512]{1,0:T(8,128)(2,1)}) custom-call(s32[1]{0:T(128)} %bitcast.3.core_ref, bf16[512,512]{1,0:T(8,128)(2,1)} %features_hbm.1, s32[320,1]{1,0:T(8,128)} %reshape.89.rows_ref), custom_call_target="tpu_custom_call" | custom-call | flops 536870912 | bytes 2097152 | tf_op jit(solution)/shard_map/pallas_call | solution.py:416
  6.6 0.1 copy.32
  6.8 0.6 collective-permute-start.2
  7.4 0.1 copy.33
  7.6 0.1 copy.34
  7.7 0.1 pad.11.clone
  7.8 0.1 pad_add_fusion.1.flags_ref
  7.9 0.1 maximum_select_fusion
  8.0 0.5 collective-permute-done.2
  8.5 2.4 %collective-permute-start.5 = (bf16[192,512]{1,0:T(8,128)(2,1)S(1)}, bf16[192,512]{1,0:T(8,128)(2,1)S(1)}, u32[]{:S(2)}, u32[]{:S(2)}) collective-permute-start(bf16[192,512]{1,0:T(8,128)(2,1)S(1)} %copy-done.19), channel_id=1, source_target_pairs={{0,8},{1,9},{2,10},{3,11},{4,12},{5,13},{6,14},{7,15},{8,0},{9,1},... | collective-permute-start | bytes 589832 | tf_op jit(solution)/shard_map/ppermute | solution.py:449
  10.9 1.5 collective-permute-start.4
  12.4 0.1 fusion.6
  12.5 7.2 %collective-permute-done.5.side_ref = bf16[192,512]{1,0:T(8,128)(2,1)S(1)} collective-permute-done((bf16[192,512]{1,0:T(8,128)(2,1)S(1)}, bf16[192,512]{1,0:T(8,128)(2,1)S(1)}, u32[]{:S(2)}, u32[]{:S(2)}) %collective-permute-start.5) | collective-permute-done | bytes 196640 | tf_op jit(solution)/shard_map/ppermute | solution.py:449
  19.7 3.6 %collective-permute-start.6 = (bf16[128,512]{1,0:T(8,128)(2,1)S(1)}, bf16[128,512]{1,0:T(8,128)(2,1)S(1)}, u32[]{:S(2)}, u32[]{:S(2)}) collective-permute-start(bf16[128,512]{1,0:T(8,128)(2,1)S(1)} %pad_maximum_fusion), channel_id=1, source_target_pairs={{0,1},{1,2},{2,3},{3,4},{4,5},{5,6},{6,7},{8,9},{9,10},{10,11},{11... | collective-permute-start | bytes 393224 | tf_op jit(solution)/shard_map/ppermute | solution.py:454
  23.4 1.9 collective-permute-start.7
  25.3 1.1 add_convert_fusion.1
  26.4 3.7 %collective-permute-done.7.ahead_ref = bf16[128,512]{1,0:T(8,128)(2,1)S(1)} collective-permute-done((bf16[128,512]{1,0:T(8,128)(2,1)S(1)}, bf16[128,512]{1,0:T(8,128)(2,1)S(1)}, u32[]{:S(2)}, u32[]{:S(2)}) %collective-permute-start.7) | collective-permute-done | bytes 131104 | tf_op jit(solution)/shard_map/ppermute | solution.py:455
  30.1 8.6 %collective-permute-done.3.refs_3_ = bf16[864,512]{1,0:T(8,128)(2,1)S(1)} collective-permute-done((bf16[864,512]{1,0:T(8,128)(2,1)S(1)}, bf16[864,512]{1,0:T(8,128)(2,1)S(1)}, u32[]{:S(2)}, u32[]{:S(2)}) %collective-permute-start.3) | collective-permute-done | bytes 884768 | tf_op jit(solution)/shard_map/ppermute | solution.py:441
  38.7 0.6 shard_map.146
  39.3 0.7 copy-done
  40.0 0.5 collective-permute-start.10
  40.4 2.2 %collective-permute-start.8 = (bf16[864,512]{1,0:T(8,128)(2,1)S(1)}, bf16[864,512]{1,0:T(8,128)(2,1)S(1)}, u32[]{:S(2)}, u32[]{:S(2)}) collective-permute-start(bf16[864,512]{1,0:T(8,128)(2,1)S(1)} %collective-permute-done.3.refs_3_), channel_id=1, source_target_pairs={{0,4},{1,5},{4,8},{5,9},{8,12},{9,13},{12,14},{13,15},{14,10},{15,... | collective-permute-start | bytes 2654216 | tf_op jit(solution)/shard_map/ppermute | solution.py:441
  42.6 10.6 %shard_map.148.refs_1_.refs_0_ = bf16[512,6912]{1,0:T(8,128)(2,1)} custom-call(s32[1]{0:T(128)} %bitcast.6.start_ref, f32[512,128]{1,0:T(8,128)} %get-tuple-element.66.rows_ref, bf16[512,256]{1,0:T(8,128)(2,1)} %get-tuple-element.49.own_ref, bf16[384,256]{1,0:T(8,128)(2,1)} %copy-done), custom_call_target="tpu_custom_call" | custom-call | flops 6341787648 | bytes 7077888 | tf_op jit(solution)/shard_map/pallas_call | solution.py:105
  53.3 0.7 copy-done.20
  53.9 10.6 %shard_map.147.refs_0_ = bf16[512,6912]{1,0:T(8,128)(2,1)} custom-call(s32[1]{0:T(128)} %bitcast.6.start_ref, f32[512,128]{1,0:T(8,128)} %get-tuple-element.67.rows_ref, bf16[512,256]{1,0:T(8,128)(2,1)} %copy-done.18, bf16[384,256]{1,0:T(8,128)(2,1)} %copy-done.20), custom_call_target="tpu_custom_call" | custom-call | flops 6341787648 | bytes 7077888 | tf_op jit(solution)/shard_map/pallas_call | solution.py:105
  64.5 1.5 collective-permute-start.11
  66.1 0.7 constant_dynamic-slice_fusion
  66.8 0.6 reshape.75.places_ref
  67.3 9.4 %shard_map.149 = (f32[512,512]{1,0:T(8,128)}, f32[512,512]{1,0:T(8,128)}) custom-call(s32[10]{0:T(128)} %reshape.75.places_ref, bf16[512,6912]{1,0:T(8,128)(2,1)} %shard_map.147.refs_0_, bf16[512,6912]{1,0:T(8,128)(2,1)} %shard_map.148.refs_1_.refs_0_, bf16[864,512]{1,0:T(8,128)(2,1)} %bitcast.32, bf16[864,512]{1,0:T(8,128)(2,1)} %copy-done.16, ...), custom_call_target="tpu_custom_call" | custom-call | flops 5368709120 | bytes 15728640 | tf_op jit(solution)/shard_map/pallas_call | solution.py:173
  76.8 8.6 %collective-permute-done.11.refs_2_ = bf16[864,512]{1,0:T(8,128)(2,1)S(1)} collective-permute-done((bf16[864,512]{1,0:T(8,128)(2,1)S(1)}, bf16[864,512]{1,0:T(8,128)(2,1)S(1)}, u32[]{:S(2)}, u32[]{:S(2)}) %collective-permute-start.11) | collective-permute-done | bytes 884768 | tf_op jit(solution)/shard_map/ppermute | solution.py:441
  85.4 1.1 collective-permute-done.12.refs_3_
  86.6 0.4 collective-permute-start.13
  87.1 1.3 collective-permute-start.14
  88.4 0.6 reshape.76.places_ref
  89.0 0.5 slice_bitcast_fusion.1.places_ref
  89.5 6.9 %shard_map.150 = (f32[512,512]{1,0:T(8,128)}, f32[512,512]{1,0:T(8,128)}) custom-call(s32[4]{0:T(128)} %reshape.76.places_ref, bf16[512,6912]{1,0:T(8,128)(2,1)} %shard_map.147.refs_0_, bf16[512,6912]{1,0:T(8,128)(2,1)} %shard_map.148.refs_1_.refs_0_, bf16[864,512]{1,0:T(8,128)(2,1)} %copy-done.1, ...), custom_call_target="tpu_custom_call", output_to_operand_aliasing={{0}: (5, {}), {1}: (6, {})} | custom-call | flops 2147483648 | bytes 6291456 | tf_op jit(solution)/shard_map/pallas_call | solution.py:173
  96.5 0.7 collective-permute-done.14.refs_2_
  97.2 0.1 copy-done.3
  97.3 0.7 copy-done.4
  98.0 4.2 %shard_map.151 = bf16[512,512]{1,0:T(8,128)(2,1)} custom-call(s32[2]{0:T(128)} %slice_bitcast_fusion.1.places_ref, bf16[512,6912]{1,0:T(8,128)(2,1)} %shard_map.147.refs_0_, bf16[432,512]{1,0:T(8,128)(2,1)} %copy-done.3, bf16[432,512]{1,0:T(8,128)(2,1)} %copy-done.4, f32[512,512]{1,0:T(8,128)} %get-tuple-element.61.refs_3_), custom_call_target="tpu_custom_call" | custom-call | flops 536870912 | bytes 2097152 | tf_op jit(solution)/shard_map/pallas_call | solution.py:173
  102.2 2.7 %collective-permute-start.15 = (bf16[512,512]{1,0:T(8,128)(2,1)}, bf16[512,512]{1,0:T(8,128)(2,1)S(1)}, u32[]{:S(2)}, u32[]{:S(2)}) collective-permute-start(bf16[512,512]{1,0:T(8,128)(2,1)} %shard_map.151), channel_id=1, source_target_pairs={{0,1},{1,0},{2,3},{3,2},{4,5},{5,4},{6,7},{7,6},{8,9},{9,8},{10,11... | collective-permute-start | bytes 1572872 | tf_op jit(solution)/shard_map/ppermute | solution.py:506
  105.0 0.3 convert_reduce_fusion.1
  105.3 0.6 multiply_add_fusion.1
  105.9 0.8 collective-permute-done.15.got_ref
  106.7 0.8 copy-done.8
  107.5 6.4 %shard_map.152 = bf16[1024,512]{1,0:T(8,128)(2,1)} custom-call(s32[2]{0:T(128)} %slice_bitcast_fusion.1.places_ref, bf16[512,512]{1,0:T(8,128)(2,1)} %copy-done.8, f32[1,512]{1,0:T(1,128)} %bitcast.38, s32[1,512]{1,0:T(1,128)} %bitcast.34, f32[512,512]{1,0:T(8,128)} %get-tuple-element.62.own_hbm, bf16[512,512]{1,0:T(8,128)(2,1)} %features_hbm.1, ...), custom_call_target="tpu_custom_call" | custom-call | flops 1342177280 | bytes 2097152 | tf_op jit(solution)/shard_map/pallas_call | solution.py:508
  113.9 5.6 %all-to-all-start = ((bf16[16,64,512]{2,1,0:T(8,128)(2,1)}), bf16[16,64,512]{2,1,0:T(8,128)(2,1)}, u32[]{:S(2)}, u32[]{:S(2)}) async-start(bf16[16,64,512]{2,1,0:T(8,128)(2,1)} %bitcast.26), calls=%async_computation | async-start | bytes 2097152 | tf_op jit(solution)/shard_map/all_to_all | solution.py:537
  119.5 1.0 fusion.5
  120.5 0.2 copy.39
  120.7 0.2 copy.40
  120.9 0.2 convert_reduce_fusion
  121.2 0.9 copy.37.slot_col_ref
  122.1 1.1 maximum_bitcast_fusion.qv_hbm
  123.1 21.3 %all-to-all-done = bf16[16,64,512]{2,1,0:T(8,128)(2,1)} async-done(((bf16[16,64,512]{2,1,0:T(8,128)(2,1)}), bf16[16,64,512]{2,1,0:T(8,128)(2,1)}, u32[]{:S(2)}, u32[]{:S(2)}) %all-to-all-start) | async-done | bytes 1048608 | tf_op jit(solution)/shard_map/all_to_all | solution.py:537
  144.5 21.6 %shard_map.153 = bf16[1024,512]{1,0:T(8,128)(2,1)} custom-call(bf16[1024,512]{1,0:T(8,128)(2,1)} %bitcast.11.arrived_ref, s32[512,1]{1,0:T(8,128)} %copy.37.slot_col_ref, s32[1,512]{1,0:T(1,128)} %bitcast.37, f32[1,512]{1,0:T(1,128)} %bitcast.39, f32[1,512]{1,0:T(1,128)} %bitcast.40, bf16[1024,512]{1,0:T(8,128)(2,1)} %maximum_bitcast_fusion.qv_hbm, ...), custom_call_target="tpu_custom_call" | custom-call | flops 2684354560 | bytes 4194304 | tf_op jit(solution)/shard_map/pallas_call | solution.py:544
  166.1 4.9 %all-to-all-start.1 = ((bf16[16,64,512]{2,1,0:T(8,128)(2,1)}), bf16[16,64,512]{2,1,0:T(8,128)(2,1)S(1)}, u32[]{:S(2)}, u32[]{:S(2)}) async-start(bf16[16,64,512]{2,1,0:T(8,128)(2,1)} %bitcast.27), calls=%async_computation.1 | async-start | bytes 2097152 | tf_op jit(solution)/shard_map/all_to_all | solution.py:570
  171.0 0.1 copy.38.slot_ref
  171.2 24.7 %all-to-all-done.1 = bf16[16,64,512]{2,1,0:T(8,128)(2,1)S(1)} async-done(((bf16[16,64,512]{2,1,0:T(8,128)(2,1)}), bf16[16,64,512]{2,1,0:T(8,128)(2,1)S(1)}, u32[]{:S(2)}, u32[]{:S(2)}) %all-to-all-start.1) | async-done | bytes 1048608 | tf_op jit(solution)/shard_map/all_to_all | solution.py:570
  195.9 1.5 shard_map.154
  (63 shorter events, 0.4 us)
Async XLA Ops:
  0.0 7.4 %copy-start.6 = (bf16[864,512]{1,0:T(8,128)(2,1)S(1)}, bf16[864,512]{1,0:T(8,128)(2,1)}, u32[]{:S(2)}) copy-start(bf16[864,512]{1,0:T(8,128)(2,1)} %param.16) | copy-start | bytes 2654212
  0.0 6.6 %copy-start.9 = (s32[512,26]{0,1:T(8,128)S(1)}, s32[512,26]{0,1:T(8,128)}, u32[]{:S(2)}) copy-start(s32[512,26]{0,1:T(8,128)} %param.26) | copy-start | bytes 159748
  1.1 6.7 %collective-permute-start = (bf16[13,32,512]{2,1,0:T(8,128)(2,1)S(1)}, bf16[13,32,512]{2,1,0:T(8,128)(2,1)S(1)}, u32[]{:S(2)}, u32[]{:S(2)}) collective-permute-start(bf16[13,32,512]{2,1,0:T(8,128)(2,1)S(1)} %slice.63), channel_id=1, source_target_pairs={{0,1},{1,0},{2,3},{3,2},{4,5},{5,4},{6,7},{7,6},{8,9},{9,8},{10,11... | collective-permute-start | bytes 1277960 | tf_op jit(solution)/shard_map/ppermute | solution.py:402
  6.6 1.9 copy-start.19
  6.6 1.9 collective-permute-start.1
  6.8 1.8 collective-permute-start.2
  7.4 12.4 %copy-start.11 = (bf16[64,512]{1,0:T(8,128)(2,1)S(1)}, bf16[64,512]{1,0:T(8,128)(2,1)}, u32[]{:S(2)}) copy-start(bf16[64,512]{1,0:T(8,128)(2,1)} %get-tuple-element.39) | copy-start | bytes 196612
  7.4 15.9 %copy-start.10 = (bf16[64,512]{1,0:T(8,128)(2,1)S(1)}, bf16[64,512]{1,0:T(8,128)(2,1)}, u32[]{:S(2)}) copy-start(bf16[64,512]{1,0:T(8,128)(2,1)} %get-tuple-element.40) | copy-start | bytes 196612
  8.0 31.2 %copy-start.7 = (bf16[27,32,512]{2,1,0:T(8,128)(2,1)}, bf16[27,32,512]{2,1,0:T(8,128)(2,1)S(1)}, u32[]{:S(2)}) copy-start(bf16[27,32,512]{2,1,0:T(8,128)(2,1)S(1)} %maximum_select_fusion) | copy-start | bytes 2654212
  8.5 30.7 %copy-start.18 = (bf16[512,256]{1,0:T(8,128)(2,1)}, bf16[512,256]{1,0:T(8,128)(2,1)S(1)}, u32[]{:S(2)}) copy-start(bf16[512,256]{1,0:T(8,128)(2,1)S(1)} %collective-permute-done.1.own_ref) | copy-start | bytes 786436
  8.5 11.2 %collective-permute-start.5 = (bf16[192,512]{1,0:T(8,128)(2,1)S(1)}, bf16[192,512]{1,0:T(8,128)(2,1)S(1)}, u32[]{:S(2)}, u32[]{:S(2)}) collective-permute-start(bf16[192,512]{1,0:T(8,128)(2,1)S(1)} %copy-done.19), channel_id=1, source_target_pairs={{0,8},{1,9},{2,10},{3,11},{4,12},{5,13},{6,14},{7,15},{8,0},{9,1},... | collective-permute-start | bytes 589832 | tf_op jit(solution)/shard_map/ppermute | solution.py:449
  10.9 27.8 %collective-permute-start.3 = (bf16[864,512]{1,0:T(8,128)(2,1)S(1)}, bf16[864,512]{1,0:T(8,128)(2,1)S(1)}, u32[]{:S(2)}, u32[]{:S(2)}) collective-permute-start(bf16[864,512]{1,0:T(8,128)(2,1)S(1)} %bitcast.30), channel_id=1, source_target_pairs={{0,4},{1,5},{4,8},{5,9},{8,12},{9,13},{12,14},{13,15},{14,10},{15,... | collective-permute-start | bytes 2654216 | tf_op jit(solution)/shard_map/ppermute | solution.py:441
  10.9 27.8 %collective-permute-start.4 = (bf16[864,512]{1,0:T(8,128)(2,1)S(1)}, bf16[864,512]{1,0:T(8,128)(2,1)}, u32[]{:S(2)}, u32[]{:S(2)}) collective-permute-start(bf16[864,512]{1,0:T(8,128)(2,1)S(1)} %bitcast.31), channel_id=1, source_target_pairs={{0,2},{1,3},{4,0},{5,1},{8,4},{9,5},{12,8},{13,9},{14,12},{15,13},... | collective-permute-start | bytes 2654216 | tf_op jit(solution)/shard_map/ppermute | solution.py:442
  19.7 6.6 %collective-permute-start.6 = (bf16[128,512]{1,0:T(8,128)(2,1)S(1)}, bf16[128,512]{1,0:T(8,128)(2,1)S(1)}, u32[]{:S(2)}, u32[]{:S(2)}) collective-permute-start(bf16[128,512]{1,0:T(8,128)(2,1)S(1)} %pad_maximum_fusion), channel_id=1, source_target_pairs={{0,1},{1,2},{2,3},{3,4},{4,5},{5,6},{6,7},{8,9},{9,10},{10,11},{11... | collective-permute-start | bytes 393224 | tf_op jit(solution)/shard_map/ppermute | solution.py:454
  23.4 6.7 %collective-permute-start.7 = (bf16[128,512]{1,0:T(8,128)(2,1)S(1)}, bf16[128,512]{1,0:T(8,128)(2,1)S(1)}, u32[]{:S(2)}, u32[]{:S(2)}) collective-permute-start(bf16[128,512]{1,0:T(8,128)(2,1)S(1)} %pad_maximum_fusion.1), channel_id=1, source_target_pairs={{1,0},{2,1},{3,2},{4,3},{5,4},{6,5},{7,6},{9,8},{10,9},{11,10},{12... | collective-permute-start | bytes 393224 | tf_op jit(solution)/shard_map/ppermute | solution.py:455
  38.7 14.6 %copy-start.16 = (bf16[864,512]{1,0:T(8,128)(2,1)}, bf16[864,512]{1,0:T(8,128)(2,1)S(1)}, u32[]{:S(2)}) copy-start(bf16[864,512]{1,0:T(8,128)(2,1)S(1)} %collective-permute-done.3.refs_3_) | copy-start | bytes 2654212
  39.3 0.7 copy-start
  40.0 13.3 %collective-permute-start.10 = (bf16[384,256]{1,0:T(8,128)(2,1)S(1)}, bf16[384,256]{1,0:T(8,128)(2,1)S(1)}, u32[]{:S(2)}, u32[]{:S(2)}) collective-permute-start(bf16[384,256]{1,0:T(8,128)(2,1)S(1)} %get-tuple-element.48), channel_id=1, source_target_pairs={{0,1},{1,0},{2,3},{3,2},{4,5},{5,4},{6,7},{7,6},{8,9},{9,8},{10,11... | collective-permute-start | bytes 589832 | tf_op jit(solution)/shard_map/ppermute | solution.py:476
  40.4 24.1 %collective-permute-start.8 = (bf16[864,512]{1,0:T(8,128)(2,1)S(1)}, bf16[864,512]{1,0:T(8,128)(2,1)S(1)}, u32[]{:S(2)}, u32[]{:S(2)}) collective-permute-start(bf16[864,512]{1,0:T(8,128)(2,1)S(1)} %collective-permute-done.3.refs_3_), channel_id=1, source_target_pairs={{0,4},{1,5},{4,8},{5,9},{8,12},{9,13},{12,14},{13,15},{14,10},{15,... | collective-permute-start | bytes 2654216 | tf_op jit(solution)/shard_map/ppermute | solution.py:441
  42.6 21.9 %collective-permute-start.9 = (bf16[864,512]{1,0:T(8,128)(2,1)}, bf16[864,512]{1,0:T(8,128)(2,1)}, u32[]{:S(2)}, u32[]{:S(2)}) collective-permute-start(bf16[864,512]{1,0:T(8,128)(2,1)} %collective-permute-done.4.refs_4_), channel_id=1, source_target_pairs={{0,2},{1,3},{4,0},{5,1},{8,4},{9,5},{12,8},{13,9},{14,12},{15,13},... | collective-permute-start | bytes 2654216 | tf_op jit(solution)/shard_map/ppermute | solution.py:442
  53.3 0.7 copy-start.20
  64.5 2.8 %copy-start.17 = (bf16[864,512]{1,0:T(8,128)(2,1)}, bf16[864,512]{1,0:T(8,128)(2,1)S(1)}, u32[]{:S(2)}) copy-start(bf16[864,512]{1,0:T(8,128)(2,1)S(1)} %collective-permute-done.8.refs_5_) | copy-start | bytes 2654212
  64.5 20.9 %collective-permute-start.11 = (bf16[864,512]{1,0:T(8,128)(2,1)S(1)}, bf16[864,512]{1,0:T(8,128)(2,1)S(1)}, u32[]{:S(2)}, u32[]{:S(2)}) collective-permute-start(bf16[864,512]{1,0:T(8,128)(2,1)S(1)} %collective-permute-done.8.refs_5_), channel_id=1, source_target_pairs={{0,4},{1,5},{4,8},{5,9},{8,12},{9,13},{12,14},{13,15},{14,10},{15,... | collective-permute-start | bytes 2654216 | tf_op jit(solution)/shard_map/ppermute | solution.py:441
  66.1 20.5 %collective-permute-start.12 = (bf16[864,512]{1,0:T(8,128)(2,1)}, bf16[864,512]{1,0:T(8,128)(2,1)S(1)}, u32[]{:S(2)}, u32[]{:S(2)}) collective-permute-start(bf16[864,512]{1,0:T(8,128)(2,1)} %collective-permute-done.9.refs_6_), channel_id=1, source_target_pairs={{0,2},{1,3},{4,0},{5,1},{8,4},{9,5},{12,8},{13,9},{14,12},{15,13},... | collective-permute-start | bytes 2654216 | tf_op jit(solution)/shard_map/ppermute | solution.py:442
  85.4 4.1 %copy-start.1 = (bf16[864,512]{1,0:T(8,128)(2,1)}, bf16[864,512]{1,0:T(8,128)(2,1)S(1)}, u32[]{:S(2)}) copy-start(bf16[864,512]{1,0:T(8,128)(2,1)S(1)} %collective-permute-done.11.refs_2_) | copy-start | bytes 2654212
  86.6 3.0 %copy-start.2 = (bf16[864,512]{1,0:T(8,128)(2,1)}, bf16[864,512]{1,0:T(8,128)(2,1)S(1)}, u32[]{:S(2)}) copy-start(bf16[864,512]{1,0:T(8,128)(2,1)S(1)} %collective-permute-done.12.refs_3_) | copy-start | bytes 2654212
  86.6 9.9 %collective-permute-start.13 = (bf16[432,512]{1,0:T(8,128)(2,1)S(1)}, bf16[432,512]{1,0:T(8,128)(2,1)S(1)}, u32[]{:S(2)}, u32[]{:S(2)}) collective-permute-start(bf16[432,512]{1,0:T(8,128)(2,1)S(1)} %slice.74), channel_id=1, source_target_pairs={{0,4},{1,5},{4,8},{5,9},{8,12},{9,13},{12,14},{13,15},{14,10},{15,... | collective-permute-start | bytes 1327112 | tf_op jit(solution)/shard_map/ppermute | solution.py:441
  87.1 10.2 %collective-permute-start.14 = (bf16[432,512]{1,0:T(8,128)(2,1)S(1)}, bf16[432,512]{1,0:T(8,128)(2,1)S(1)}, u32[]{:S(2)}, u32[]{:S(2)}) collective-permute-start(bf16[432,512]{1,0:T(8,128)(2,1)S(1)} %slice.75), channel_id=1, source_target_pairs={{0,2},{1,3},{4,0},{5,1},{8,4},{9,5},{12,8},{13,9},{14,12},{15,13},... | collective-permute-start | bytes 1327112 | tf_op jit(solution)/shard_map/ppermute | solution.py:442
  96.5 0.8 copy-start.3
  97.2 0.8 copy-start.4
  98.0 7.0 %copy-start.12 = (s32[512]{0:T(512)S(1)}, s32[512]{0:T(512)}, u32[]{:S(2)}) copy-start(s32[512]{0:T(512)} %param.27) | copy-start | bytes 6148
  102.2 4.5 %collective-permute-start.15 = (bf16[512,512]{1,0:T(8,128)(2,1)}, bf16[512,512]{1,0:T(8,128)(2,1)S(1)}, u32[]{:S(2)}, u32[]{:S(2)}) collective-permute-start(bf16[512,512]{1,0:T(8,128)(2,1)} %shard_map.151), channel_id=1, source_target_pairs={{0,1},{1,0},{2,3},{3,2},{4,5},{5,4},{6,7},{7,6},{8,9},{9,8},{10,11... | collective-permute-start | bytes 1572872 | tf_op jit(solution)/shard_map/ppermute | solution.py:506
  106.7 0.8 copy-start.8
  113.9 5.6 %copy-start.5 = (bf16[512,1536]{1,0:T(8,128)(2,1)S(1)}, bf16[512,1536]{1,0:T(8,128)(2,1)}, u32[]{:S(2)}) copy-start(bf16[512,1536]{1,0:T(8,128)(2,1)} %param.20) | copy-start | bytes 4718596
  113.9 30.6 %all-to-all-start = ((bf16[16,64,512]{2,1,0:T(8,128)(2,1)}), bf16[16,64,512]{2,1,0:T(8,128)(2,1)}, u32[]{:S(2)}, u32[]{:S(2)}) async-start(bf16[16,64,512]{2,1,0:T(8,128)(2,1)} %bitcast.26), calls=%async_computation | async-start | bytes 2097152 | tf_op jit(solution)/shard_map/all_to_all | solution.py:537
  119.5 1.4 copy-start.15
  121.2 23.3 %copy-start.14 = (s32[512]{0:T(512)}, s32[512]{0:T(512)S(1)}, u32[]{:S(2)}) copy-start(s32[512]{0:T(512)S(1)} %multiply_add_fusion) | copy-start | bytes 6148
  166.1 4.9 %copy-start.13 = (s32[512]{0:T(512)S(1)}, s32[512]{0:T(512)}, u32[]{:S(2)}) copy-start(s32[512]{0:T(512)} %multiply_add_fusion.1) | copy-start | bytes 6148
  166.1 29.8 %all-to-all-start.1 = ((bf16[16,64,512]{2,1,0:T(8,128)(2,1)}), bf16[16,64,512]{2,1,0:T(8,128)(2,1)S(1)}, u32[]{:S(2)}, u32[]{:S(2)}) async-start(bf16[16,64,512]{2,1,0:T(8,128)(2,1)} %bitcast.27), calls=%async_computation.1 | async-start | bytes 2097152 | tf_op jit(solution)/shard_map/all_to_all | solution.py:570

commit v12 on v11

--- a/solution.py
+++ b/solution.py
@@ -18,6 +18,7 @@
 F32 = jnp.float32
 BF16 = jnp.bfloat16
 MIB = 1 << 20
+CONV_LIMITS = (24, 40)
 
 
 def dot(left, right):
@@ -170,20 +171,20 @@
     flat = [piece for parts in pieces for piece in parts]
     blocks = len(stacked)
     held = 1 + blocks + len(flat)
+    kept = [] if before is None else [block for block in range(blocks) if block or dtype == F32]
     return call(
         functools.partial(conv_kernel, slots, blocks, before is None),
-        [jax.ShapeDtypeStruct((points, width), dtype)] * blocks,
-        60,
+        [
+            jax.ShapeDtypeStruct((points, width), dtype if block == 0 else F32)
+            for block in range(blocks)
+        ],
+        CONV_LIMITS[len(slots) > 2],
         2 * blocks * points * length * width * len(slots),
         2 * length * (blocks * points + width) * len(slots),
         in_specs=[pl.BlockSpec(memory_space=pltpu.SMEM)]
         + [pl.BlockSpec(memory_space=pl.ANY)] * (held - 1)
         + ([] if before is None else [pl.BlockSpec()] * blocks),
-        input_output_aliases=(
-            {}
-            if before is None or dtype != F32
-            else {held + block: block for block in range(blocks)}
-        ),
+        input_output_aliases={held + block: block for block in kept},
         scratch_shapes=[
             pltpu.VMEM((len(slots), blocks, points, length), BF16),
             pltpu.VMEM((len(slots), length, width), BF16),
@@ -192,27 +193,8 @@
     )(places.reshape(-1), *stacked, *flat, *(before or ()))
 
 
-def mix_kernel(
-    count, places_ref, got_ref, gain_ref, slot_ref, own_hbm, features_hbm, weight_hbm, *refs
-):
-    out_ref, own_ref, features_ref, weight_ref, own_held, load_sems = refs[-9:-3]
-    loads = [
-        pltpu.make_async_copy(source, target, load_sems.at[at])
-        for at, (source, target) in enumerate(
-            ((own_hbm, own_ref), (features_hbm, features_ref), (weight_hbm, weight_ref))
-        )
-    ]
-    for load in loads:
-        load.start()
-    if count:
-        conv_kernel(
-            [count], 1, True, places_ref, *refs[: 1 + count], own_held, *refs[-3:]
-        )
-    else:
-        own_held[...] = jnp.zeros_like(own_held)
-    for load in loads:
-        load.wait()
-    convolved = (own_ref[...] + own_held[...] + got_ref[...].astype(F32)).astype(BF16)
+def mix_kernel(own_ref, got_ref, features_ref, weight_ref, gain_ref, slot_ref, out_ref):
+    convolved = (own_ref[...] + got_ref[...].astype(F32)).astype(BF16)
     linear = dot(convolved, weight_ref[...])
     mixed = (features_ref[...].astype(F32) + layer_norm(linear, gain_ref[...])).astype(BF16)
     slots = lax.broadcasted_iota(jnp.int32, (out_ref.shape[0], mixed.shape[0]), 0)
@@ -484,16 +466,12 @@
         sums = pass_on(*sums)
         sums = conv_part(stacked, places[5:7], [[back[3]], [on[3]]], sums, length)
         last = [[back[4], on[4]]]
-        (for_partner,) = conv_part(stacked[:1], places[7:], last, sums[:1], length, BF16)
-        own_part = sums[1]
-        rest = [stacked[1], *last[0]]
-        places = places[7]
+        for_partner, own_part = conv_part(stacked, places[7:], last, sums, length, BF16)
     else:
         groups = [list(range(first, devices, 2)) for first in range(2)]
         weight = lax.all_gather(mine, "blocks", axis=0, tiled=True, axis_index_groups=groups)
         nowhere = jnp.zeros((1, 2), jnp.int32)
         for_partner, own_part = conv_part(stacked, nowhere, [[weight]], None, length)
-        places, rest = nowhere[0], []
 
     positions = jnp.arange(points, dtype=jnp.int32)
     target = serial_rank // points
@@ -506,33 +484,18 @@
     from_partner = lax.ppermute(for_partner, "blocks", partner)
 
     outgoing = call(
-        functools.partial(mix_kernel, len(rest) - 1 if rest else 0),
+        mix_kernel,
         jax.ShapeDtypeStruct((slots, width), BF16),
-        60,
-        2 * points * width * (width + slots + length),
+        32,
+        2 * points * width * (width + slots),
         8 * points * width,
-        in_specs=[pl.BlockSpec(memory_space=pltpu.SMEM)]
-        + [pl.BlockSpec()] * 3
-        + [pl.BlockSpec(memory_space=pl.ANY)] * (3 + len(rest)),
-        scratch_shapes=[
-            pltpu.VMEM((points, width), F32),
-            pltpu.VMEM((points, width), BF16),
-            pltpu.VMEM((width, width), BF16),
-            pltpu.VMEM((points, width), F32),
-            pltpu.SemaphoreType.DMA((3,)),
-            pltpu.VMEM((1, 1, points, length if rest else 128), BF16),
-            pltpu.VMEM((1, length if rest else 128, width), BF16),
-            pltpu.SemaphoreType.DMA((1, 4)),
-        ],
     )(
-        places,
+        own_part,
         from_partner,
+        features,
+        cpe_weight,
         cpe_gain.reshape(1, width),
         out_slot.reshape(1, points),
-        own_part,
-        features,
-        cpe_weight,
-        *rest,
     )
     arrived = lax.all_to_all(
         outgoing.reshape(devices, capacity, width), "blocks", split_axis=0, concat_axis=0, tiled=True

time: 198 us -> 195 us (0.985)
  local copies, waits for them, and re-layouts: 11.2 us -> 24 us
  Pallas kernels: 74.4 us -> 65.1 us
  waiting for transfers between devices: 77.3 us -> 71.7 us
    unnamed x45 -> x51, local copies, waits for them, and re-layouts: 3.52 us -> 15.5 us
    pallas_call x3, Pallas kernels: 20.6 us -> 15.4 us  [conv_part(): call(functools.partial(conv_kernel, slots, blocks, before is None), [jax....]
    pallas_call x1, Pallas kernels: 6.36 us -> 2.31 us  [body(): call(mix_kernel, jax.ShapeDtypeStruct((slots, width), BF16), 32, 2 * poin...]
    ppermute x4, waiting for transfers between devices: 17.3 us -> 13.3 us  [pass_on(): back.append(lax.ppermute(first, 'blocks', back_pairs))]
    slice x2, local copies, waits for them, and re-layouts: 0.06 us -> 2.59 us  [pass_on(): first, second = (first[:rows // 2], second[rows // 2:])]
  transfers between devices with their start and end apart: 18 -> 18, of which waited for: 11 -> 9; matrix products, arithmetic and copies ran while one was open for 6% -> 6% of each run, Pallas kernels for 20% -> 18%
where the time goes in v12:
time: 195 us; the launch traced here: 194 us
  waiting for transfers between devices  71.7 us (37%)
  Pallas kernels  65.1 us (33%)
  starting transfers between devices  28.9 us (15%)
  local copies, waits for them, and re-layouts  24 us (12%)
  other arithmetic  3.78 us (2%)
    all_to_all x1, waiting for transfers between devices, body(): lax.all_to_all(back.reshape(devices, capacity, width), 'blocks', split_ax...  24.7 us
    pallas_call x1, Pallas kernels, body(): call(block_kernel, jax.ShapeDtypeStruct((slots, width), BF16), 60, 20 * p...  21.6 us
    all_to_all x1, waiting for transfers between devices, body(): lax.all_to_all(outgoing.reshape(devices, capacity, width), 'blocks', spli...  21.4 us
    pallas_call x2, Pallas kernels, gather_block(): call(functools.partial(gather_kernel, taps), jax.ShapeDtypeStruct((points...  21.2 us
    unnamed x51, local copies, waits for them, and re-layouts  15.5 us
    pallas_call x3, Pallas kernels, conv_part(): call(functools.partial(conv_kernel, slots, blocks, before is None), [jax....  15.4 us
    ppermute x4, waiting for transfers between devices, pass_on(): back.append(lax.ppermute(first, 'blocks', back_pairs))  13.3 us
    ppermute x1, waiting for transfers between devices, body(): lists = lax.ppermute(lists, 'blocks', side)  6.25 us
  transfers between devices with their start and end apart: 18, of which 9 were waited for; matrix products, arithmetic and copies ran while one was open for 6% of the time, Pallas kernels for 18%

profile of v12, /device:TPU:9, one launch (start us, length us, event | category | flops | bytes accessed | tf_op | source)
XLA Modules:
  0.0 193.8 jit_solution(3773729326199641785)
XLA Ops:
  0.0 1.1 slice.62
  1.1 0.7 collective-permute-start
  1.9 0.7 slice_bitcast_fusion
  2.6 0.8 select_bitcast_fusion
  3.3 0.8 reshape.92.rows_ref
  4.2 2.4 %shard_map.145 = (bf16[512,256]{1,0:T(8,128)(2,1)}, bf16[512,256]{1,0:T(8,128)(2,1)}, bf16[192,512]{1,0:T(8,128)(2,1)}, bf16[64,512]{1,0:T(8,128)(2,1)}, bf16[64,512]{1,0:T(8,128)(2,1)}) custom-call(s32[1]{0:T(128)} %bitcast.3.core_ref, bf16[512,512]{1,0:T(8,128)(2,1)} %features_ref.3, s32[320,1]{1,0:T(8,128)} %reshape.92.rows_ref), custom_call_target="tpu_custom_call" | custom-call | flops 536870912 | bytes 2097152 | tf_op jit(solution)/shard_map/pallas_call | solution.py:398
  6.6 0.1 copy.33
  6.8 0.6 collective-permute-start.2
  7.4 0.1 copy.34
  7.5 0.1 copy.35
  7.9 0.1 maximum_select_fusion
  8.0 0.5 collective-permute-done.2
  8.5 2.4 %collective-permute-start.5 = (bf16[192,512]{1,0:T(8,128)(2,1)S(1)}, bf16[192,512]{1,0:T(8,128)(2,1)S(1)}, u32[]{:S(2)}, u32[]{:S(2)}) collective-permute-start(bf16[192,512]{1,0:T(8,128)(2,1)S(1)} %copy-done.22), channel_id=1, source_target_pairs={{0,8},{1,9},{2,10},{3,11},{4,12},{5,13},{6,14},{7,15},{8,0},{9,1},... | collective-permute-start | bytes 589832 | tf_op jit(solution)/shard_map/ppermute | solution.py:431
  10.9 1.5 collective-permute-start.4
  12.4 0.9 copy-done.3
  13.3 0.1 fusion.6
  13.4 6.2 %collective-permute-done.5.side_ref = bf16[192,512]{1,0:T(8,128)(2,1)S(1)} collective-permute-done((bf16[192,512]{1,0:T(8,128)(2,1)S(1)}, bf16[192,512]{1,0:T(8,128)(2,1)S(1)}, u32[]{:S(2)}, u32[]{:S(2)}) %collective-permute-start.5) | collective-permute-done | bytes 196640 | tf_op jit(solution)/shard_map/ppermute | solution.py:431
  19.7 3.6 %collective-permute-start.6 = (bf16[128,512]{1,0:T(8,128)(2,1)S(1)}, bf16[128,512]{1,0:T(8,128)(2,1)S(1)}, u32[]{:S(2)}, u32[]{:S(2)}) collective-permute-start(bf16[128,512]{1,0:T(8,128)(2,1)S(1)} %pad_maximum_fusion), channel_id=1, source_target_pairs={{0,1},{1,2},{2,3},{3,4},{4,5},{5,6},{6,7},{8,9},{9,10},{10,11},{11... | collective-permute-start | bytes 393224 | tf_op jit(solution)/shard_map/ppermute | solution.py:436
  23.3 1.9 collective-permute-start.7
  25.3 1.1 add_convert_fusion.1
  26.4 3.6 %collective-permute-done.7.ahead_ref = bf16[128,512]{1,0:T(8,128)(2,1)S(1)} collective-permute-done((bf16[128,512]{1,0:T(8,128)(2,1)S(1)}, bf16[128,512]{1,0:T(8,128)(2,1)S(1)}, u32[]{:S(2)}, u32[]{:S(2)}) %collective-permute-start.7) | collective-permute-done | bytes 131104 | tf_op jit(solution)/shard_map/ppermute | solution.py:437
  29.9 8.7 %collective-permute-done.3.refs_3_ = bf16[864,512]{1,0:T(8,128)(2,1)S(1)} collective-permute-done((bf16[864,512]{1,0:T(8,128)(2,1)S(1)}, bf16[864,512]{1,0:T(8,128)(2,1)S(1)}, u32[]{:S(2)}, u32[]{:S(2)}) %collective-permute-start.3) | collective-permute-done | bytes 884768 | tf_op jit(solution)/shard_map/ppermute | solution.py:423
  38.7 0.6 shard_map.146
  39.3 0.7 copy-done.12
  39.9 0.5 collective-permute-start.10
  40.4 2.2 %collective-permute-start.8 = (bf16[864,512]{1,0:T(8,128)(2,1)S(1)}, bf16[864,512]{1,0:T(8,128)(2,1)}, u32[]{:S(2)}, u32[]{:S(2)}) collective-permute-start(bf16[864,512]{1,0:T(8,128)(2,1)S(1)} %collective-permute-done.3.refs_3_), channel_id=1, source_target_pairs={{0,4},{1,5},{4,8},{5,9},{8,12},{9,13},{12,14},{13,15},{14,10},{15,... | collective-permute-start | bytes 2654216 | tf_op jit(solution)/shard_map/ppermute | solution.py:423
  42.6 10.6 %shard_map.148.refs_1_ = bf16[512,6912]{1,0:T(8,128)(2,1)} custom-call(s32[1]{0:T(128)} %bitcast.6.start_ref, f32[512,128]{1,0:T(8,128)} %get-tuple-element.70.rows_ref, bf16[512,256]{1,0:T(8,128)(2,1)} %get-tuple-element.51.own_ref, bf16[384,256]{1,0:T(8,128)(2,1)} %copy-done.12), custom_call_target="tpu_custom_call" | custom-call | flops 6341787648 | bytes 7077888 | tf_op jit(solution)/shard_map/pallas_call | solution.py:106
  53.2 0.7 copy-done.23
  53.9 10.6 %shard_map.147.refs_0_ = bf16[512,6912]{1,0:T(8,128)(2,1)} custom-call(s32[1]{0:T(128)} %bitcast.6.start_ref, f32[512,128]{1,0:T(8,128)} %get-tuple-element.71.rows_ref, bf16[512,256]{1,0:T(8,128)(2,1)} %copy-done.21, bf16[384,256]{1,0:T(8,128)(2,1)} %copy-done.23), custom_call_target="tpu_custom_call" | custom-call | flops 6341787648 | bytes 7077888 | tf_op jit(solution)/shard_map/pallas_call | solution.py:106
  64.5 1.5 collective-permute-start.11
  66.1 0.7 constant_dynamic-slice_fusion
  66.8 3.0 %copy-done.1 = bf16[512,6912]{1,0:T(8,128)(2,1)S(1)} copy-done((bf16[512,6912]{1,0:T(8,128)(2,1)S(1)}, bf16[512,6912]{1,0:T(8,128)(2,1)}, u32[]{:S(2)}) %copy-start.1) | copy-done | bytes 7077912
  69.8 1.2 copy-done.4
  71.0 1.2 copy-done.9
  72.2 1.2 copy-done.11
  73.3 7.9 %shard_map.149 = (f32[512,512]{1,0:T(8,128)S(1)}, f32[512,512]{1,0:T(8,128)S(1)}) custom-call(s32[10]{0:T(128)S(1)} %reshape.78.places_ref, bf16[512,6912]{1,0:T(8,128)(2,1)S(1)} %copy-done.1, bf16[512,6912]{1,0:T(8,128)(2,1)} %shard_map.148.refs_1_, bf16[864,512]{1,0:T(8,128)(2,1)S(1)} %bitcast.28, bf16[864,512]{1,0:T(8,128)(2,1)S(1)} %copy-done.9, ...), custom_call_target="tpu_custom_call" | custom-call | flops 5368709120 | bytes 15728640 | tf_op jit(solution)/shard_map/pallas_call | solution.py:175
  81.2 4.6 %collective-permute-done.11.refs_2_ = bf16[864,512]{1,0:T(8,128)(2,1)S(1)} collective-permute-done((bf16[864,512]{1,0:T(8,128)(2,1)}, bf16[864,512]{1,0:T(8,128)(2,1)S(1)}, u32[]{:S(2)}, u32[]{:S(2)}) %collective-permute-start.11) | collective-permute-done | bytes 884768 | tf_op jit(solution)/shard_map/ppermute | solution.py:423
  85.8 0.8 collective-permute-done.12.refs_3_
  86.6 0.8 slice.73
  87.4 0.4 collective-permute-start.13
  87.8 1.8 slice.74
  89.6 1.1 collective-permute-start.14
  90.7 0.1 reshape.79.places_ref
  90.8 3.0 %copy-done = bf16[512,6912]{1,0:T(8,128)(2,1)S(1)} copy-done((bf16[512,6912]{1,0:T(8,128)(2,1)S(1)}, bf16[512,6912]{1,0:T(8,128)(2,1)}, u32[]{:S(2)}) %copy-start) | copy-done | bytes 7077912
  93.8 3.0 %copy-done.2 = bf16[512,6912]{1,0:T(8,128)(2,1)S(1)} copy-done((bf16[512,6912]{1,0:T(8,128)(2,1)S(1)}, bf16[512,6912]{1,0:T(8,128)(2,1)}, u32[]{:S(2)}) %copy-start.2) | copy-done | bytes 7077912
  96.8 4.0 %shard_map.150 = (f32[512,512]{1,0:T(8,128)S(1)}, f32[512,512]{1,0:T(8,128)S(1)}) custom-call(s32[4]{0:T(128)S(1)} %reshape.79.places_ref, bf16[512,6912]{1,0:T(8,128)(2,1)S(1)} %copy-done.2, bf16[512,6912]{1,0:T(8,128)(2,1)S(1)} %copy-done, bf16[864,512]{1,0:T(8,128)(2,1)S(1)} %collective-permute-done.11.refs_2_, ...), custom_call_target="tpu_custom_call", output_to_operand_aliasing={{0}: (5, {}), {1}: (6, {})} | custom-call | flops 2147483648 | bytes 6291456 | tf_op jit(solution)/shard_map/pallas_call | solution.py:175
  100.9 3.4 %shard_map.151 = (bf16[512,512]{1,0:T(8,128)(2,1)S(1)}, f32[512,512]{1,0:T(8,128)S(1)}) custom-call(s32[2]{0:T(128)S(1)} %slice_bitcast_fusion.1.places_ref, bf16[512,6912]{1,0:T(8,128)(2,1)S(1)} %copy-done.2, bf16[512,6912]{1,0:T(8,128)(2,1)S(1)} %copy-done, bf16[432,512]{1,0:T(8,128)(2,1)S(1)} %collective-permute-done.13.refs_2_, ...), custom_call_target="tpu_custom_call", output_to_operand_aliasing={{1}: (6, {})} | custom-call | flops 1073741824 | bytes 3145728 | tf_op jit(solution)/shard_map/pallas_call | solution.py:175
  104.4 2.4 %collective-permute-start.15 = (bf16[512,512]{1,0:T(8,128)(2,1)S(1)}, bf16[512,512]{1,0:T(8,128)(2,1)S(1)}, u32[]{:S(2)}, u32[]{:S(2)}) collective-permute-start(bf16[512,512]{1,0:T(8,128)(2,1)S(1)} %get-tuple-element.66), channel_id=1, source_target_pairs={{0,1},{1,0},{2,3},{3,2},{4,5},{5,4},{6,7},{7,6},{8,9},{9,8},{10,11... | collective-permute-start | bytes 1572872 | tf_op jit(solution)/shard_map/ppermute | solution.py:484
  106.8 0.3 convert_reduce_fusion.1
  107.2 1.2 collective-permute-done.15.got_ref
  108.3 2.3 %shard_map.152 = bf16[1024,512]{1,0:T(8,128)(2,1)} custom-call(f32[512,512]{1,0:T(8,128)S(1)} %get-tuple-element.65.own_ref, bf16[512,512]{1,0:T(8,128)(2,1)S(1)} %collective-permute-done.15.got_ref, bf16[512,512]{1,0:T(8,128)(2,1)S(1)} %copy-done.5, bf16[512,512]{1,0:T(8,128)(2,1)S(1)} %copy-done.6, f32[1,512]{1,0:T(1,128)S(1)} %bitcast.31, ...), custom_call_target="tpu_custom_call" | custom-call | flops 805306368 | bytes 2097152 | tf_op jit(solution)/shard_map/pallas_call | solution.py:486
  110.6 5.2 %all-to-all-start = ((bf16[16,64,512]{2,1,0:T(8,128)(2,1)}), bf16[16,64,512]{2,1,0:T(8,128)(2,1)}, u32[]{:S(2)}, u32[]{:S(2)}) async-start(bf16[16,64,512]{2,1,0:T(8,128)(2,1)} %bitcast.10), calls=%async_computation | async-start | bytes 2097152 | tf_op jit(solution)/shard_map/all_to_all | solution.py:500
  115.8 0.9 fusion.5
  116.7 0.2 copy.40
  117.0 0.2 copy.41
  117.2 0.2 convert_reduce_fusion
  117.5 0.9 copy.38.slot_col_ref
  118.3 1.1 maximum_bitcast_fusion.qv_hbm
  119.4 21.4 %all-to-all-done = bf16[16,64,512]{2,1,0:T(8,128)(2,1)} async-done(((bf16[16,64,512]{2,1,0:T(8,128)(2,1)}), bf16[16,64,512]{2,1,0:T(8,128)(2,1)}, u32[]{:S(2)}, u32[]{:S(2)}) %all-to-all-start) | async-done | bytes 1048608 | tf_op jit(solution)/shard_map/all_to_all | solution.py:500
  140.8 21.6 %shard_map.153 = bf16[1024,512]{1,0:T(8,128)(2,1)} custom-call(bf16[1024,512]{1,0:T(8,128)(2,1)} %bitcast.11.arrived_ref, s32[512,1]{1,0:T(8,128)} %copy.38.slot_col_ref, s32[1,512]{1,0:T(1,128)} %bitcast.37, f32[1,512]{1,0:T(1,128)} %bitcast.38, f32[1,512]{1,0:T(1,128)} %bitcast.39, bf16[1024,512]{1,0:T(8,128)(2,1)} %maximum_bitcast_fusion.qv_hbm, ...), custom_call_target="tpu_custom_call" | custom-call | flops 2684354560 | bytes 4194304 | tf_op jit(solution)/shard_map/pallas_call | solution.py:507
  162.4 5.0 %all-to-all-start.1 = ((bf16[16,64,512]{2,1,0:T(8,128)(2,1)}), bf16[16,64,512]{2,1,0:T(8,128)(2,1)S(1)}, u32[]{:S(2)}, u32[]{:S(2)}) async-start(bf16[16,64,512]{2,1,0:T(8,128)(2,1)} %bitcast.32), calls=%async_computation.1 | async-start | bytes 2097152 | tf_op jit(solution)/shard_map/all_to_all | solution.py:533
  167.4 0.1 copy.39.slot_ref
  167.5 24.7 %all-to-all-done.1 = bf16[16,64,512]{2,1,0:T(8,128)(2,1)S(1)} async-done(((bf16[16,64,512]{2,1,0:T(8,128)(2,1)}), bf16[16,64,512]{2,1,0:T(8,128)(2,1)S(1)}, u32[]{:S(2)}, u32[]{:S(2)}) %all-to-all-start.1) | async-done | bytes 1048608 | tf_op jit(solution)/shard_map/all_to_all | solution.py:533
  192.2 1.5 shard_map.154
  (69 shorter events, 0.5 us)
Async XLA Ops:
  0.0 7.3 %copy-start.14 = (bf16[864,512]{1,0:T(8,128)(2,1)S(1)}, bf16[864,512]{1,0:T(8,128)(2,1)}, u32[]{:S(2)}) copy-start(bf16[864,512]{1,0:T(8,128)(2,1)} %param.16) | copy-start | bytes 2654212
  0.0 6.6 %copy-start.15 = (s32[512,26]{0,1:T(8,128)S(1)}, s32[512,26]{0,1:T(8,128)}, u32[]{:S(2)}) copy-start(s32[512,26]{0,1:T(8,128)} %param.26) | copy-start | bytes 159748
  1.1 6.7 %collective-permute-start = (bf16[13,32,512]{2,1,0:T(8,128)(2,1)S(1)}, bf16[13,32,512]{2,1,0:T(8,128)(2,1)S(1)}, u32[]{:S(2)}, u32[]{:S(2)}) collective-permute-start(bf16[13,32,512]{2,1,0:T(8,128)(2,1)S(1)} %slice.62), channel_id=1, source_target_pairs={{0,1},{1,0},{2,3},{3,2},{4,5},{5,4},{6,7},{7,6},{8,9},{9,8},{10,11... | collective-permute-start | bytes 1277960 | tf_op jit(solution)/shard_map/ppermute | solution.py:384
  6.6 1.9 copy-start.22
  6.6 1.9 collective-permute-start.1
  6.8 1.7 collective-permute-start.2
  7.3 12.4 %copy-start.17 = (bf16[64,512]{1,0:T(8,128)(2,1)S(1)}, bf16[64,512]{1,0:T(8,128)(2,1)}, u32[]{:S(2)}) copy-start(bf16[64,512]{1,0:T(8,128)(2,1)} %get-tuple-element.41) | copy-start | bytes 196612
  7.4 15.9 %copy-start.16 = (bf16[64,512]{1,0:T(8,128)(2,1)S(1)}, bf16[64,512]{1,0:T(8,128)(2,1)}, u32[]{:S(2)}) copy-start(bf16[64,512]{1,0:T(8,128)(2,1)} %get-tuple-element.42) | copy-start | bytes 196612
  8.5 44.7 %copy-start.21 = (bf16[512,256]{1,0:T(8,128)(2,1)}, bf16[512,256]{1,0:T(8,128)(2,1)S(1)}, u32[]{:S(2)}) copy-start(bf16[512,256]{1,0:T(8,128)(2,1)S(1)} %collective-permute-done.1.own_ref) | copy-start | bytes 786436
  8.5 11.2 %collective-permute-start.5 = (bf16[192,512]{1,0:T(8,128)(2,1)S(1)}, bf16[192,512]{1,0:T(8,128)(2,1)S(1)}, u32[]{:S(2)}, u32[]{:S(2)}) collective-permute-start(bf16[192,512]{1,0:T(8,128)(2,1)S(1)} %copy-done.22), channel_id=1, source_target_pairs={{0,8},{1,9},{2,10},{3,11},{4,12},{5,13},{6,14},{7,15},{8,0},{9,1},... | collective-permute-start | bytes 589832 | tf_op jit(solution)/shard_map/ppermute | solution.py:431
  10.9 27.8 %collective-permute-start.3 = (bf16[864,512]{1,0:T(8,128)(2,1)S(1)}, bf16[864,512]{1,0:T(8,128)(2,1)S(1)}, u32[]{:S(2)}, u32[]{:S(2)}) collective-permute-start(bf16[864,512]{1,0:T(8,128)(2,1)S(1)} %bitcast.26), channel_id=1, source_target_pairs={{0,4},{1,5},{4,8},{5,9},{8,12},{9,13},{12,14},{13,15},{14,10},{15,... | collective-permute-start | bytes 2654216 | tf_op jit(solution)/shard_map/ppermute | solution.py:423
  10.9 27.8 %collective-permute-start.4 = (bf16[864,512]{1,0:T(8,128)(2,1)S(1)}, bf16[864,512]{1,0:T(8,128)(2,1)S(1)}, u32[]{:S(2)}, u32[]{:S(2)}) collective-permute-start(bf16[864,512]{1,0:T(8,128)(2,1)S(1)} %bitcast.27), channel_id=1, source_target_pairs={{0,2},{1,3},{4,0},{5,1},{8,4},{9,5},{12,8},{13,9},{14,12},{15,13},... | collective-permute-start | bytes 2654216 | tf_op jit(solution)/shard_map/ppermute | solution.py:424
  12.4 0.9 copy-start.3
  19.7 6.6 %collective-permute-start.6 = (bf16[128,512]{1,0:T(8,128)(2,1)S(1)}, bf16[128,512]{1,0:T(8,128)(2,1)S(1)}, u32[]{:S(2)}, u32[]{:S(2)}) collective-permute-start(bf16[128,512]{1,0:T(8,128)(2,1)S(1)} %pad_maximum_fusion), channel_id=1, source_target_pairs={{0,1},{1,2},{2,3},{3,4},{4,5},{5,6},{6,7},{8,9},{9,10},{10,11},{11... | collective-permute-start | bytes 393224 | tf_op jit(solution)/shard_map/ppermute | solution.py:436
  23.3 6.6 %collective-permute-start.7 = (bf16[128,512]{1,0:T(8,128)(2,1)S(1)}, bf16[128,512]{1,0:T(8,128)(2,1)S(1)}, u32[]{:S(2)}, u32[]{:S(2)}) collective-permute-start(bf16[128,512]{1,0:T(8,128)(2,1)S(1)} %pad_maximum_fusion.1), channel_id=1, source_target_pairs={{1,0},{2,1},{3,2},{4,3},{5,4},{6,5},{7,6},{9,8},{10,9},{11,10},{12... | collective-permute-start | bytes 393224 | tf_op jit(solution)/shard_map/ppermute | solution.py:437
  38.6 14.6 %copy-start.8 = (bf16[864,512]{1,0:T(8,128)(2,1)}, bf16[864,512]{1,0:T(8,128)(2,1)S(1)}, u32[]{:S(2)}) copy-start(bf16[864,512]{1,0:T(8,128)(2,1)S(1)} %collective-permute-done.3.refs_3_) | copy-start | bytes 2654212
  38.7 14.6 %copy-start.10 = (bf16[864,512]{1,0:T(8,128)(2,1)}, bf16[864,512]{1,0:T(8,128)(2,1)S(1)}, u32[]{:S(2)}) copy-start(bf16[864,512]{1,0:T(8,128)(2,1)S(1)} %collective-permute-done.4.refs_4_) | copy-start | bytes 2654212
  39.2 0.7 copy-start.12
  39.9 13.3 %collective-permute-start.10 = (bf16[384,256]{1,0:T(8,128)(2,1)S(1)}, bf16[384,256]{1,0:T(8,128)(2,1)S(1)}, u32[]{:S(2)}, u32[]{:S(2)}) collective-permute-start(bf16[384,256]{1,0:T(8,128)(2,1)S(1)} %get-tuple-element.50), channel_id=1, source_target_pairs={{0,1},{1,0},{2,3},{3,2},{4,5},{5,4},{6,7},{7,6},{8,9},{9,8},{10,11... | collective-permute-start | bytes 589832 | tf_op jit(solution)/shard_map/ppermute | solution.py:458
  40.4 24.1 %collective-permute-start.8 = (bf16[864,512]{1,0:T(8,128)(2,1)S(1)}, bf16[864,512]{1,0:T(8,128)(2,1)}, u32[]{:S(2)}, u32[]{:S(2)}) collective-permute-start(bf16[864,512]{1,0:T(8,128)(2,1)S(1)} %collective-permute-done.3.refs_3_), channel_id=1, source_target_pairs={{0,4},{1,5},{4,8},{5,9},{8,12},{9,13},{12,14},{13,15},{14,10},{15,... | collective-permute-start | bytes 2654216 | tf_op jit(solution)/shard_map/ppermute | solution.py:423
  42.6 21.9 %collective-permute-start.9 = (bf16[864,512]{1,0:T(8,128)(2,1)S(1)}, bf16[864,512]{1,0:T(8,128)(2,1)}, u32[]{:S(2)}, u32[]{:S(2)}) collective-permute-start(bf16[864,512]{1,0:T(8,128)(2,1)S(1)} %collective-permute-done.4.refs_4_), channel_id=1, source_target_pairs={{0,2},{1,3},{4,0},{5,1},{8,4},{9,5},{12,8},{13,9},{14,12},{15,13},... | collective-permute-start | bytes 2654216 | tf_op jit(solution)/shard_map/ppermute | solution.py:424
  53.2 0.7 copy-start.23
  64.5 21.3 %collective-permute-start.11 = (bf16[864,512]{1,0:T(8,128)(2,1)}, bf16[864,512]{1,0:T(8,128)(2,1)S(1)}, u32[]{:S(2)}, u32[]{:S(2)}) collective-permute-start(bf16[864,512]{1,0:T(8,128)(2,1)} %collective-permute-done.8.refs_5_), channel_id=1, source_target_pairs={{0,4},{1,5},{4,8},{5,9},{8,12},{9,13},{12,14},{13,15},{14,10},{15,... | collective-permute-start | bytes 2654216 | tf_op jit(solution)/shard_map/ppermute | solution.py:423
  66.0 20.6 %collective-permute-start.12 = (bf16[864,512]{1,0:T(8,128)(2,1)}, bf16[864,512]{1,0:T(8,128)(2,1)}, u32[]{:S(2)}, u32[]{:S(2)}) collective-permute-start(bf16[864,512]{1,0:T(8,128)(2,1)} %collective-permute-done.9.refs_6_), channel_id=1, source_target_pairs={{0,2},{1,3},{4,0},{5,1},{8,4},{9,5},{12,8},{13,9},{14,12},{15,13},... | collective-permute-start | bytes 2654216 | tf_op jit(solution)/shard_map/ppermute | solution.py:424
  66.8 3.0 %copy-start.1 = (bf16[512,6912]{1,0:T(8,128)(2,1)S(1)}, bf16[512,6912]{1,0:T(8,128)(2,1)}, u32[]{:S(2)}) copy-start(bf16[512,6912]{1,0:T(8,128)(2,1)} %shard_map.147.refs_0_) | copy-start | bytes 21233668
  69.8 1.2 copy-start.4
  71.0 1.2 copy-start.9
  72.2 1.2 copy-start.11
  87.4 13.4 %collective-permute-start.13 = (bf16[432,512]{1,0:T(8,128)(2,1)}, bf16[432,512]{1,0:T(8,128)(2,1)S(1)}, u32[]{:S(2)}, u32[]{:S(2)}) collective-permute-start(bf16[432,512]{1,0:T(8,128)(2,1)} %slice.73), channel_id=1, source_target_pairs={{0,4},{1,5},{4,8},{5,9},{8,12},{9,13},{12,14},{13,15},{14,10},{15,... | collective-permute-start | bytes 1327112 | tf_op jit(solution)/shard_map/ppermute | solution.py:423
  89.6 11.3 %collective-permute-start.14 = (bf16[432,512]{1,0:T(8,128)(2,1)}, bf16[432,512]{1,0:T(8,128)(2,1)}, u32[]{:S(2)}, u32[]{:S(2)}) collective-permute-start(bf16[432,512]{1,0:T(8,128)(2,1)} %slice.74), channel_id=1, source_target_pairs={{0,2},{1,3},{4,0},{5,1},{8,4},{9,5},{12,8},{13,9},{14,12},{15,13},... | collective-permute-start | bytes 1327112 | tf_op jit(solution)/shard_map/ppermute | solution.py:424
  90.8 3.0 %copy-start = (bf16[512,6912]{1,0:T(8,128)(2,1)S(1)}, bf16[512,6912]{1,0:T(8,128)(2,1)}, u32[]{:S(2)}) copy-start(bf16[512,6912]{1,0:T(8,128)(2,1)} %shard_map.148.refs_1_) | copy-start | bytes 21233668
  93.8 3.0 %copy-start.2 = (bf16[512,6912]{1,0:T(8,128)(2,1)S(1)}, bf16[512,6912]{1,0:T(8,128)(2,1)}, u32[]{:S(2)}) copy-start(bf16[512,6912]{1,0:T(8,128)(2,1)} %shard_map.147.refs_0_) | copy-start | bytes 21233668
  100.9 5.9 %copy-start.18 = (s32[512]{0:T(512)S(1)}, s32[512]{0:T(512)}, u32[]{:S(2)}) copy-start(s32[512]{0:T(512)} %param.27) | copy-start | bytes 6148
  100.9 7.4 %copy-start.5 = (bf16[512,512]{1,0:T(8,128)(2,1)S(1)}, bf16[512,512]{1,0:T(8,128)(2,1)}, u32[]{:S(2)}) copy-start(bf16[512,512]{1,0:T(8,128)(2,1)} %features_ref.3) | copy-start | bytes 1572868
  100.9 7.4 %copy-start.6 = (bf16[512,512]{1,0:T(8,128)(2,1)S(1)}, bf16[512,512]{1,0:T(8,128)(2,1)}, u32[]{:S(2)}) copy-start(bf16[512,512]{1,0:T(8,128)(2,1)} %weight_ref.1) | copy-start | bytes 1572868
  100.9 7.4 %copy-start.7 = (f32[512]{0:T(512)S(1)}, f32[512]{0:T(512)}, u32[]{:S(2)}) copy-start(f32[512]{0:T(512)} %param.18) | copy-start | bytes 6148
  104.4 3.9 %collective-permute-start.15 = (bf16[512,512]{1,0:T(8,128)(2,1)S(1)}, bf16[512,512]{1,0:T(8,128)(2,1)S(1)}, u32[]{:S(2)}, u32[]{:S(2)}) collective-permute-start(bf16[512,512]{1,0:T(8,128)(2,1)S(1)} %get-tuple-element.66), channel_id=1, source_target_pairs={{0,1},{1,0},{2,3},{3,2},{4,5},{5,4},{6,7},{7,6},{8,9},{9,8},{10,11... | collective-permute-start | bytes 1572872 | tf_op jit(solution)/shard_map/ppermute | solution.py:484
  108.3 7.5 %copy-start.13 = (bf16[512,1536]{1,0:T(8,128)(2,1)S(1)}, bf16[512,1536]{1,0:T(8,128)(2,1)}, u32[]{:S(2)}) copy-start(bf16[512,1536]{1,0:T(8,128)(2,1)} %param.20) | copy-start | bytes 4718596
  110.6 30.1 %all-to-all-start = ((bf16[16,64,512]{2,1,0:T(8,128)(2,1)}), bf16[16,64,512]{2,1,0:T(8,128)(2,1)}, u32[]{:S(2)}, u32[]{:S(2)}) async-start(bf16[16,64,512]{2,1,0:T(8,128)(2,1)} %bitcast.10), calls=%async_computation | async-start | bytes 2097152 | tf_op jit(solution)/shard_map/all_to_all | solution.py:500
  115.8 1.3 copy-start.20
  117.5 23.3 %copy-start.19 = (s32[512]{0:T(512)}, s32[512]{0:T(512)S(1)}, u32[]{:S(2)}) copy-start(s32[512]{0:T(512)S(1)} %multiply_add_fusion) | copy-start | bytes 6148
  162.4 29.8 %all-to-all-start.1 = ((bf16[16,64,512]{2,1,0:T(8,128)(2,1)}), bf16[16,64,512]{2,1,0:T(8,128)(2,1)S(1)}, u32[]{:S(2)}, u32[]{:S(2)}) async-start(bf16[16,64,512]{2,1,0:T(8,128)(2,1)} %bitcast.32), calls=%async_computation.1 | async-start | bytes 2097152 | tf_op jit(solution)/shard_map/all_to_all | solution.py:533

commit v13 on v12

--- a/solution.py
+++ b/solution.py
@@ -18,7 +18,6 @@
 F32 = jnp.float32
 BF16 = jnp.bfloat16
 MIB = 1 << 20
-CONV_LIMITS = (24, 40)
 
 
 def dot(left, right):
@@ -120,23 +119,39 @@
     )(start, rows, own, got)
 
 
-def conv_kernel(slots, blocks, first, places_ref, *refs):
-    stacked, refs = refs[:blocks], refs[blocks:]
-    pieces, refs = refs[: sum(slots)], refs[sum(slots) :]
-    before = [] if first else refs[:blocks]
-    outs, (lhs, held, sems) = refs[-3 - blocks : -3], refs[-3:]
+def conv_kernel(slots, later, ready, first, places_ref, *refs):
+    refs = list(refs)
+
+    def take(count):
+        taken = refs[:count]
+        del refs[:count]
+        return taken
+
+    sources = take(1 if ready else 2)
+    pieces = take(sum(slots))
+    before = [] if first else take(2)
+    outs = take(2)
+    kept = take(len(later))
+    (lhs,) = sources if ready else take(1)
+    held, sems = take(2)
     length = held.shape[1]
+
+    def stretch(slot, target, sem):
+        column = pl.multiple_of(places_ref[2 * slot], 128)
+        copies = [
+            pltpu.make_async_copy(
+                stacked.at[:, pl.ds(column, length)], target.at[block], sem.at[block]
+            )
+            for block, stacked in enumerate(sources)
+        ]
+        for copy in copies:
+            copy.start()
+        return copies
+
     copies, taken = [], 0
     for at, count in enumerate(slots):
-        column = pl.multiple_of(places_ref[2 * at], 128)
         row = pl.multiple_of(places_ref[2 * at + 1], 16)
-        copies.append([])
-        for block in range(blocks):
-            copy = pltpu.make_async_copy(
-                stacked[block].at[:, pl.ds(column, length)], lhs.at[at, block], sems.at[at, block]
-            )
-            copy.start()
-            copies[-1].append(copy)
+        copies.append([] if ready else stretch(at, lhs.at[at], sems.at[at]))
         short = count * pieces[taken].shape[0]
         edge = length - short
         if edge:
@@ -151,6 +166,11 @@
             copy.start()
             copies[-1].append(copy)
             taken += 1
+    extra, slot = [], len(slots)
+    for group, count in enumerate(later):
+        for place in range(count):
+            extra += stretch(slot, kept[group].at[place], sems.at[slot])
+            slot += 1
     for at in range(len(slots)):
         for copy in copies[at]:
             copy.wait()
@@ -162,35 +182,40 @@
                 ref[...] = product
             else:
                 ref[...] = (before[block][...] + product).astype(ref.dtype)
-
-
-def conv_part(stacked, places, pieces, before, length, dtype=F32):
-    points, depth = stacked[0].shape
+    for copy in extra:
+        copy.wait()
+
+
+def conv_part(sources, places, pieces, before, length, later=(), dtype=F32):
+    ready = len(sources) == 1
+    points = sources[0].shape[2] if ready else sources[0].shape[0]
     width = pieces[0][0].shape[1]
     slots = [len(parts) for parts in pieces]
     flat = [piece for parts in pieces for piece in parts]
-    blocks = len(stacked)
-    held = 1 + blocks + len(flat)
-    kept = [] if before is None else [block for block in range(blocks) if block or dtype == F32]
+    held = 1 + len(sources) + len(flat)
+    kept = [] if before is None else [block for block in range(2) if block or dtype == F32]
+    spec = pl.BlockSpec(memory_space=pl.ANY)
     return call(
-        functools.partial(conv_kernel, slots, blocks, before is None),
+        functools.partial(conv_kernel, slots, later, ready, before is None),
         [
-            jax.ShapeDtypeStruct((points, width), dtype if block == 0 else F32)
-            for block in range(blocks)
+            jax.ShapeDtypeStruct((points, width), dtype),
+            jax.ShapeDtypeStruct((points, width), F32),
+        ]
+        + [jax.ShapeDtypeStruct((count, 2, points, length), BF16) for count in later],
+        24 if ready else 36,
+        4 * points * length * width * len(slots),
+        2 * length * (2 * points + width) * len(slots),
+        in_specs=[pl.BlockSpec(memory_space=pltpu.SMEM)]
+        + [pl.BlockSpec() if ready else spec] * len(sources)
+        + [spec] * len(flat)
+        + ([] if before is None else [pl.BlockSpec()] * 2),
+        input_output_aliases={held + block: block for block in kept},
+        scratch_shapes=([] if ready else [pltpu.VMEM((len(slots), 2, points, length), BF16)])
+        + [
+            pltpu.VMEM((len(slots), length, width), BF16),
+            pltpu.SemaphoreType.DMA((len(slots) + sum(later), 4)),
         ],
-        CONV_LIMITS[len(slots) > 2],
-        2 * blocks * points * length * width * len(slots),
-        2 * length * (blocks * points + width) * len(slots),
-        in_specs=[pl.BlockSpec(memory_space=pltpu.SMEM)]
-        + [pl.BlockSpec(memory_space=pl.ANY)] * (held - 1)
-        + ([] if before is None else [pl.BlockSpec()] * blocks),
-        input_output_aliases={held + block: block for block in kept},
-        scratch_shapes=[
-            pltpu.VMEM((len(slots), blocks, points, length), BF16),
-            pltpu.VMEM((len(slots), length, width), BF16),
-            pltpu.SemaphoreType.DMA((len(slots), 4)),
-        ],
-    )(places.reshape(-1), *stacked, *flat, *(before or ()))
+    )(places.reshape(-1), *sources, *flat, *(before or ()))
 
 
 def mix_kernel(own_ref, got_ref, features_ref, weight_ref, gain_ref, slot_ref, out_ref):
@@ -462,11 +487,14 @@
     if round_trip:
         places = jnp.array(places, jnp.int32)[index]
         early = [[mine], [back[1]], [on[1]], [back[2]], [on[2]]]
-        sums = conv_part(stacked, places[:5], early, None, length)
+        *sums, next_lhs, last_lhs = conv_part(stacked, places, early, None, length, (2, 1))
         sums = pass_on(*sums)
-        sums = conv_part(stacked, places[5:7], [[back[3]], [on[3]]], sums, length)
+        late = [[back[3]], [on[3]]]
+        sums = conv_part([next_lhs], places[5:7], late, sums, length)
         last = [[back[4], on[4]]]
-        for_partner, own_part = conv_part(stacked, places[7:], last, sums, length, BF16)
+        for_partner, own_part = conv_part(
+            [last_lhs], places[7:], last, sums, length, dtype=BF16
+        )
     else:
         groups = [list(range(first, devices, 2)) for first in range(2)]
         weight = lax.all_gather(mine, "blocks", axis=0, tiled=True, axis_index_groups=groups)

time: 195 us -> 194 us (level)
  local copies, waits for them, and re-layouts: 24 us -> 20.4 us
  waiting for transfers between devices: 71.7 us -> 74.5 us
    unnamed x51 -> x53, local copies, waits for them, and re-layouts: 15.5 us -> 11.9 us
    ppermute x4, waiting for transfers between devices: 0.82 us -> 3.06 us  [pass_on(): on.append(lax.ppermute(second, 'blocks', on_pairs))]
  transfers between devices with their start and end apart: 18 -> 18, of which waited for: 9 -> 11; matrix products, arithmetic and copies ran while one was open for 6% -> 6% of each run, Pallas kernels for 18% -> 18%
where the time goes in v13:
time: 194 us; the launch traced here: 193 us
  waiting for transfers between devices  74.5 us (38%)
  Pallas kernels  64.5 us (33%)
  starting transfers between devices  29.4 us (15%)
  local copies, waits for them, and re-layouts  20.4 us (11%)
  other arithmetic  3.79 us (2%)
    all_to_all x1, waiting for transfers between devices, body(): lax.all_to_all(back.reshape(devices, capacity, width), 'blocks', split_ax...  24.7 us
    pallas_call x1, Pallas kernels, body(): call(block_kernel, jax.ShapeDtypeStruct((slots, width), BF16), 60, 20 * p...  21.6 us
    all_to_all x1, waiting for transfers between devices, body(): lax.all_to_all(outgoing.reshape(devices, capacity, width), 'blocks', spli...  21.4 us
    pallas_call x2, Pallas kernels, gather_block(): call(functools.partial(gather_kernel, taps), jax.ShapeDtypeStruct((points...  21.2 us
    pallas_call x3, Pallas kernels, conv_part(): call(functools.partial(conv_kernel, slots, later, ready, before is None),...  14.8 us
    ppermute x4, waiting for transfers between devices, pass_on(): back.append(lax.ppermute(first, 'blocks', back_pairs))  13.9 us
    unnamed x53, local copies, waits for them, and re-layouts  11.9 us
    ppermute x1, waiting for transfers between devices, body(): lists = lax.ppermute(lists, 'blocks', side)  6.25 us
  transfers between devices with their start and end apart: 18, of which 11 were waited for; matrix products, arithmetic and copies ran while one was open for 6% of the time, Pallas kernels for 18%

profile of v13, /device:TPU:9, one launch (start us, length us, event | category | flops | bytes accessed | tf_op | source)
XLA Modules:
  0.0 193.0 jit_solution(15419119371368630658)
XLA Ops:
  0.0 1.1 slice.58
  1.1 0.7 collective-permute-start
  1.9 0.7 slice_bitcast_fusion
  2.6 0.8 select_bitcast_fusion
  3.3 0.8 reshape.86.rows_ref
  4.2 2.4 %shard_map.145 = (bf16[512,256]{1,0:T(8,128)(2,1)}, bf16[512,256]{1,0:T(8,128)(2,1)}, bf16[192,512]{1,0:T(8,128)(2,1)}, bf16[64,512]{1,0:T(8,128)(2,1)}, bf16[64,512]{1,0:T(8,128)(2,1)}) custom-call(s32[1]{0:T(128)} %bitcast.3.core_ref, bf16[512,512]{1,0:T(8,128)(2,1)} %features_ref.3, s32[320,1]{1,0:T(8,128)} %reshape.86.rows_ref), custom_call_target="tpu_custom_call" | custom-call | flops 536870912 | bytes 2097152 | tf_op jit(solution)/shard_map/pallas_call | solution.py:423
  6.6 0.1 copy.33
  6.8 0.6 collective-permute-start.2
  7.4 0.1 copy.34
  7.5 0.1 copy.35
  7.8 0.1 maximum_select_fusion
  8.0 0.5 collective-permute-done.2
  8.5 2.4 %collective-permute-start.5 = (bf16[192,512]{1,0:T(8,128)(2,1)S(1)}, bf16[192,512]{1,0:T(8,128)(2,1)S(1)}, u32[]{:S(2)}, u32[]{:S(2)}) collective-permute-start(bf16[192,512]{1,0:T(8,128)(2,1)S(1)} %copy-done.23), channel_id=1, source_target_pairs={{0,8},{1,9},{2,10},{3,11},{4,12},{5,13},{6,14},{7,15},{8,0},{9,1},... | collective-permute-start | bytes 589832 | tf_op jit(solution)/shard_map/ppermute | solution.py:456
  10.9 1.5 collective-permute-start.4
  12.4 0.9 copy-done.4
  13.4 6.2 %collective-permute-done.5.side_ref = bf16[192,512]{1,0:T(8,128)(2,1)S(1)} collective-permute-done((bf16[192,512]{1,0:T(8,128)(2,1)S(1)}, bf16[192,512]{1,0:T(8,128)(2,1)S(1)}, u32[]{:S(2)}, u32[]{:S(2)}) %collective-permute-start.5) | collective-permute-done | bytes 196640 | tf_op jit(solution)/shard_map/ppermute | solution.py:456
  19.7 3.6 %collective-permute-start.6 = (bf16[128,512]{1,0:T(8,128)(2,1)S(1)}, bf16[128,512]{1,0:T(8,128)(2,1)S(1)}, u32[]{:S(2)}, u32[]{:S(2)}) collective-permute-start(bf16[128,512]{1,0:T(8,128)(2,1)S(1)} %pad_maximum_fusion), channel_id=1, source_target_pairs={{0,1},{1,2},{2,3},{3,4},{4,5},{5,6},{6,7},{8,9},{9,10},{10,11},{11... | collective-permute-start | bytes 393224 | tf_op jit(solution)/shard_map/ppermute | solution.py:461
  23.3 1.9 collective-permute-start.7
  25.3 1.1 add_convert_fusion.1
  26.4 3.5 %collective-permute-done.7.ahead_ref = bf16[128,512]{1,0:T(8,128)(2,1)S(1)} collective-permute-done((bf16[128,512]{1,0:T(8,128)(2,1)S(1)}, bf16[128,512]{1,0:T(8,128)(2,1)S(1)}, u32[]{:S(2)}, u32[]{:S(2)}) %collective-permute-start.7) | collective-permute-done | bytes 131104 | tf_op jit(solution)/shard_map/ppermute | solution.py:462
  29.9 8.7 %collective-permute-done.3.refs_3_ = bf16[864,512]{1,0:T(8,128)(2,1)S(1)} collective-permute-done((bf16[864,512]{1,0:T(8,128)(2,1)S(1)}, bf16[864,512]{1,0:T(8,128)(2,1)S(1)}, u32[]{:S(2)}, u32[]{:S(2)}) %collective-permute-start.3) | collective-permute-done | bytes 884768 | tf_op jit(solution)/shard_map/ppermute | solution.py:448
  38.6 0.6 shard_map.146
  39.2 0.7 copy-done.13
  39.9 0.5 collective-permute-start.10
  40.4 2.2 %collective-permute-start.8 = (bf16[864,512]{1,0:T(8,128)(2,1)S(1)}, bf16[864,512]{1,0:T(8,128)(2,1)}, u32[]{:S(2)}, u32[]{:S(2)}) collective-permute-start(bf16[864,512]{1,0:T(8,128)(2,1)S(1)} %collective-permute-done.3.refs_3_), channel_id=1, source_target_pairs={{0,4},{1,5},{4,8},{5,9},{8,12},{9,13},{12,14},{13,15},{14,10},{15,... | collective-permute-start | bytes 2654216 | tf_op jit(solution)/shard_map/ppermute | solution.py:448
  42.6 10.6 %shard_map.148.refs_1_ = bf16[512,6912]{1,0:T(8,128)(2,1)} custom-call(s32[1]{0:T(128)} %bitcast.6.start_ref, f32[512,128]{1,0:T(8,128)} %get-tuple-element.74.rows_ref, bf16[512,256]{1,0:T(8,128)(2,1)} %get-tuple-element.53.own_ref, bf16[384,256]{1,0:T(8,128)(2,1)} %copy-done.13), custom_call_target="tpu_custom_call" | custom-call | flops 6341787648 | bytes 7077888 | tf_op jit(solution)/shard_map/pallas_call | solution.py:105
  53.3 0.7 copy-done.24
  53.9 10.6 %shard_map.147.refs_0_ = bf16[512,6912]{1,0:T(8,128)(2,1)} custom-call(s32[1]{0:T(128)} %bitcast.6.start_ref, f32[512,128]{1,0:T(8,128)} %get-tuple-element.75.rows_ref, bf16[512,256]{1,0:T(8,128)(2,1)} %copy-done.22, bf16[384,256]{1,0:T(8,128)(2,1)} %copy-done.24), custom_call_target="tpu_custom_call" | custom-call | flops 6341787648 | bytes 7077888 | tf_op jit(solution)/shard_map/pallas_call | solution.py:105
  64.5 1.5 collective-permute-start.11
  66.0 0.7 constant_dynamic-slice_fusion
  66.8 1.2 copy-done.5
  68.0 1.2 copy-done.10
  69.2 1.2 copy-done.12
  70.3 8.2 %shard_map.149 = (f32[512,512]{1,0:T(8,128)S(1)}, f32[512,512]{1,0:T(8,128)S(1)}, bf16[2,2,512,1024]{3,2,1,0:T(8,128)(2,1)S(1)}, bf16[1,2,512,1024]{3,2,1,0:T(8,128)(2,1)S(1)}) custom-call(s32[16]{0:T(128)S(1)} %reshape_squeeze.3.places_ref, bf16[512,6912]{1,0:T(8,128)(2,1)} %shard_map.147.refs_0_, bf16[512,6912]{1,0:T(8,128)(2,1)} %shard_map.148.refs_1_, ...), custom_call_target="tpu_custom_call" | custom-call | flops 5368709120 | bytes 15728640 | tf_op jit(solution)/shard_map/pallas_call | solution.py:198
  78.5 1.9 %copy-done = bf16[2,2,512,1024]{3,2,1,0:T(8,128)(2,1)} copy-done((bf16[2,2,512,1024]{3,2,1,0:T(8,128)(2,1)}, bf16[2,2,512,1024]{3,2,1,0:T(8,128)(2,1)S(1)}, u32[]{:S(2)}) %copy-start) | copy-done | bytes 4194328
  80.5 1.4 copy-done.2
  81.8 4.0 %collective-permute-done.11.refs_1_ = bf16[864,512]{1,0:T(8,128)(2,1)S(1)} collective-permute-done((bf16[864,512]{1,0:T(8,128)(2,1)}, bf16[864,512]{1,0:T(8,128)(2,1)S(1)}, u32[]{:S(2)}, u32[]{:S(2)}) %collective-permute-start.11) | collective-permute-done | bytes 884768 | tf_op jit(solution)/shard_map/ppermute | solution.py:448
  85.8 0.8 collective-permute-done.12.refs_2_
  86.6 0.8 slice.68
  87.4 0.4 collective-permute-start.13
  87.8 1.8 slice.69
  89.6 1.1 collective-permute-start.14
  90.8 2.2 %copy-done.1 = bf16[2,2,512,1024]{3,2,1,0:T(8,128)(2,1)S(1)} copy-done((bf16[2,2,512,1024]{3,2,1,0:T(8,128)(2,1)S(1)}, bf16[2,2,512,1024]{3,2,1,0:T(8,128)(2,1)}, u32[]{:S(2)}) %copy-start.1) | copy-done | bytes 4194328
  93.0 3.5 %shard_map.150 = (f32[512,512]{1,0:T(8,128)S(1)}, f32[512,512]{1,0:T(8,128)S(1)}) custom-call(s32[4]{0:T(128)S(1)} %reshape.73.places_ref, bf16[2,2,512,1024]{3,2,1,0:T(8,128)(2,1)S(1)} %copy-done.1, bf16[864,512]{1,0:T(8,128)(2,1)S(1)} %collective-permute-done.11.refs_1_, ...), custom_call_target="tpu_custom_call", output_to_operand_aliasing={{0}: (4, {}), {1}: (5, {})} | custom-call | flops 2147483648 | bytes 6291456 | tf_op jit(solution)/shard_map/pallas_call | solution.py:198
  96.4 1.2 collective-permute-done.13.refs_1_
  97.6 2.2 %collective-permute-done.14.refs_2_ = bf16[432,512]{1,0:T(8,128)(2,1)} collective-permute-done((bf16[432,512]{1,0:T(8,128)(2,1)}, bf16[432,512]{1,0:T(8,128)(2,1)}, u32[]{:S(2)}, u32[]{:S(2)}) %collective-permute-start.14) | collective-permute-done | bytes 442400 | tf_op jit(solution)/shard_map/ppermute | solution.py:449
  99.9 3.1 %shard_map.151 = (bf16[512,512]{1,0:T(8,128)(2,1)S(1)}, f32[512,512]{1,0:T(8,128)S(1)}) custom-call(s32[2]{0:T(128)S(1)} %slice_bitcast_fusion.1.places_ref, bf16[1,2,512,1024]{3,2,1,0:T(8,128)(2,1)S(1)} %copy-done.3, bf16[432,512]{1,0:T(8,128)(2,1)S(1)} %collective-permute-done.13.refs_1_, ...), custom_call_target="tpu_custom_call", output_to_operand_aliasing={{1}: (5, {})} | custom-call | flops 1073741824 | bytes 3145728 | tf_op jit(solution)/shard_map/pallas_call | solution.py:198
  103.0 2.7 %collective-permute-start.15 = (bf16[512,512]{1,0:T(8,128)(2,1)S(1)}, bf16[512,512]{1,0:T(8,128)(2,1)S(1)}, u32[]{:S(2)}, u32[]{:S(2)}) collective-permute-start(bf16[512,512]{1,0:T(8,128)(2,1)S(1)} %get-tuple-element.70), channel_id=1, source_target_pairs={{0,1},{1,0},{2,3},{3,2},{4,5},{5,4},{6,7},{7,6},{8,9},{9,8},{10,11... | collective-permute-start | bytes 1572872 | tf_op jit(solution)/shard_map/ppermute | solution.py:512
  105.8 0.3 convert_reduce_fusion.1
  106.1 1.2 collective-permute-done.15.got_ref
  107.3 2.3 %shard_map.152 = bf16[1024,512]{1,0:T(8,128)(2,1)} custom-call(f32[512,512]{1,0:T(8,128)S(1)} %get-tuple-element.69.own_ref, bf16[512,512]{1,0:T(8,128)(2,1)S(1)} %collective-permute-done.15.got_ref, bf16[512,512]{1,0:T(8,128)(2,1)S(1)} %copy-done.6, bf16[512,512]{1,0:T(8,128)(2,1)S(1)} %copy-done.7, f32[1,512]{1,0:T(1,128)S(1)} %bitcast.30, ...), custom_call_target="tpu_custom_call" | custom-call | flops 805306368 | bytes 2097152 | tf_op jit(solution)/shard_map/pallas_call | solution.py:514
  109.6 5.5 %all-to-all-start = ((bf16[16,64,512]{2,1,0:T(8,128)(2,1)}), bf16[16,64,512]{2,1,0:T(8,128)(2,1)}, u32[]{:S(2)}, u32[]{:S(2)}) async-start(bf16[16,64,512]{2,1,0:T(8,128)(2,1)} %bitcast.10), calls=%async_computation | async-start | bytes 2097152 | tf_op jit(solution)/shard_map/all_to_all | solution.py:528
  115.1 0.9 fusion.5
  116.0 0.2 copy.40
  116.2 0.2 copy.41
  116.4 0.2 convert_reduce_fusion
  116.7 0.9 copy.38.slot_col_ref
  117.6 1.1 maximum_bitcast_fusion.qv_hbm
  118.6 21.4 %all-to-all-done = bf16[16,64,512]{2,1,0:T(8,128)(2,1)} async-done(((bf16[16,64,512]{2,1,0:T(8,128)(2,1)}), bf16[16,64,512]{2,1,0:T(8,128)(2,1)}, u32[]{:S(2)}, u32[]{:S(2)}) %all-to-all-start) | async-done | bytes 1048608 | tf_op jit(solution)/shard_map/all_to_all | solution.py:528
  140.1 21.6 %shard_map.153 = bf16[1024,512]{1,0:T(8,128)(2,1)} custom-call(bf16[1024,512]{1,0:T(8,128)(2,1)} %bitcast.11.arrived_ref, s32[512,1]{1,0:T(8,128)} %copy.38.slot_col_ref, s32[1,512]{1,0:T(1,128)} %bitcast.35, f32[1,512]{1,0:T(1,128)} %bitcast.36, f32[1,512]{1,0:T(1,128)} %bitcast.37, bf16[1024,512]{1,0:T(8,128)(2,1)} %maximum_bitcast_fusion.qv_hbm, ...), custom_call_target="tpu_custom_call" | custom-call | flops 2684354560 | bytes 4194304 | tf_op jit(solution)/shard_map/pallas_call | solution.py:535
  161.7 4.9 %all-to-all-start.1 = ((bf16[16,64,512]{2,1,0:T(8,128)(2,1)}), bf16[16,64,512]{2,1,0:T(8,128)(2,1)S(1)}, u32[]{:S(2)}, u32[]{:S(2)}) async-start(bf16[16,64,512]{2,1,0:T(8,128)(2,1)} %bitcast.31), calls=%async_computation.1 | async-start | bytes 2097152 | tf_op jit(solution)/shard_map/all_to_all | solution.py:561
  166.6 0.1 copy.39.slot_ref
  166.8 24.7 %all-to-all-done.1 = bf16[16,64,512]{2,1,0:T(8,128)(2,1)S(1)} async-done(((bf16[16,64,512]{2,1,0:T(8,128)(2,1)}), bf16[16,64,512]{2,1,0:T(8,128)(2,1)S(1)}, u32[]{:S(2)}, u32[]{:S(2)}) %all-to-all-start.1) | async-done | bytes 1048608 | tf_op jit(solution)/shard_map/all_to_all | solution.py:561
  191.4 1.5 shard_map.154
  (71 shorter events, 0.7 us)
Async XLA Ops:
  0.0 7.3 %copy-start.15 = (bf16[864,512]{1,0:T(8,128)(2,1)S(1)}, bf16[864,512]{1,0:T(8,128)(2,1)}, u32[]{:S(2)}) copy-start(bf16[864,512]{1,0:T(8,128)(2,1)} %param.16) | copy-start | bytes 2654212
  0.0 6.6 %copy-start.16 = (s32[512,26]{0,1:T(8,128)S(1)}, s32[512,26]{0,1:T(8,128)}, u32[]{:S(2)}) copy-start(s32[512,26]{0,1:T(8,128)} %param.26) | copy-start | bytes 159748
  1.1 6.7 %collective-permute-start = (bf16[13,32,512]{2,1,0:T(8,128)(2,1)S(1)}, bf16[13,32,512]{2,1,0:T(8,128)(2,1)S(1)}, u32[]{:S(2)}, u32[]{:S(2)}) collective-permute-start(bf16[13,32,512]{2,1,0:T(8,128)(2,1)S(1)} %slice.58), channel_id=1, source_target_pairs={{0,1},{1,0},{2,3},{3,2},{4,5},{5,4},{6,7},{7,6},{8,9},{9,8},{10,11... | collective-permute-start | bytes 1277960 | tf_op jit(solution)/shard_map/ppermute | solution.py:409
  6.6 1.9 copy-start.23
  6.6 1.9 collective-permute-start.1
  6.8 1.7 collective-permute-start.2
  7.3 12.4 %copy-start.18 = (bf16[64,512]{1,0:T(8,128)(2,1)S(1)}, bf16[64,512]{1,0:T(8,128)(2,1)}, u32[]{:S(2)}) copy-start(bf16[64,512]{1,0:T(8,128)(2,1)} %get-tuple-element.43) | copy-start | bytes 196612
  7.4 15.9 %copy-start.17 = (bf16[64,512]{1,0:T(8,128)(2,1)S(1)}, bf16[64,512]{1,0:T(8,128)(2,1)}, u32[]{:S(2)}) copy-start(bf16[64,512]{1,0:T(8,128)(2,1)} %get-tuple-element.44) | copy-start | bytes 196612
  8.5 44.7 %copy-start.22 = (bf16[512,256]{1,0:T(8,128)(2,1)}, bf16[512,256]{1,0:T(8,128)(2,1)S(1)}, u32[]{:S(2)}) copy-start(bf16[512,256]{1,0:T(8,128)(2,1)S(1)} %collective-permute-done.1.own_ref) | copy-start | bytes 786436
  8.5 11.2 %collective-permute-start.5 = (bf16[192,512]{1,0:T(8,128)(2,1)S(1)}, bf16[192,512]{1,0:T(8,128)(2,1)S(1)}, u32[]{:S(2)}, u32[]{:S(2)}) collective-permute-start(bf16[192,512]{1,0:T(8,128)(2,1)S(1)} %copy-done.23), channel_id=1, source_target_pairs={{0,8},{1,9},{2,10},{3,11},{4,12},{5,13},{6,14},{7,15},{8,0},{9,1},... | collective-permute-start | bytes 589832 | tf_op jit(solution)/shard_map/ppermute | solution.py:456
  10.9 27.7 %collective-permute-start.3 = (bf16[864,512]{1,0:T(8,128)(2,1)S(1)}, bf16[864,512]{1,0:T(8,128)(2,1)S(1)}, u32[]{:S(2)}, u32[]{:S(2)}) collective-permute-start(bf16[864,512]{1,0:T(8,128)(2,1)S(1)} %bitcast.25), channel_id=1, source_target_pairs={{0,4},{1,5},{4,8},{5,9},{8,12},{9,13},{12,14},{13,15},{14,10},{15,... | collective-permute-start | bytes 2654216 | tf_op jit(solution)/shard_map/ppermute | solution.py:448
  10.9 27.7 %collective-permute-start.4 = (bf16[864,512]{1,0:T(8,128)(2,1)S(1)}, bf16[864,512]{1,0:T(8,128)(2,1)S(1)}, u32[]{:S(2)}, u32[]{:S(2)}) collective-permute-start(bf16[864,512]{1,0:T(8,128)(2,1)S(1)} %bitcast.26), channel_id=1, source_target_pairs={{0,2},{1,3},{4,0},{5,1},{8,4},{9,5},{12,8},{13,9},{14,12},{15,13},... | collective-permute-start | bytes 2654216 | tf_op jit(solution)/shard_map/ppermute | solution.py:449
  12.4 0.9 copy-start.4
  19.7 6.7 %collective-permute-start.6 = (bf16[128,512]{1,0:T(8,128)(2,1)S(1)}, bf16[128,512]{1,0:T(8,128)(2,1)S(1)}, u32[]{:S(2)}, u32[]{:S(2)}) collective-permute-start(bf16[128,512]{1,0:T(8,128)(2,1)S(1)} %pad_maximum_fusion), channel_id=1, source_target_pairs={{0,1},{1,2},{2,3},{3,4},{4,5},{5,6},{6,7},{8,9},{9,10},{10,11},{11... | collective-permute-start | bytes 393224 | tf_op jit(solution)/shard_map/ppermute | solution.py:461
  23.3 6.6 %collective-permute-start.7 = (bf16[128,512]{1,0:T(8,128)(2,1)S(1)}, bf16[128,512]{1,0:T(8,128)(2,1)S(1)}, u32[]{:S(2)}, u32[]{:S(2)}) collective-permute-start(bf16[128,512]{1,0:T(8,128)(2,1)S(1)} %pad_maximum_fusion.1), channel_id=1, source_target_pairs={{1,0},{2,1},{3,2},{4,3},{5,4},{6,5},{7,6},{9,8},{10,9},{11,10},{12... | collective-permute-start | bytes 393224 | tf_op jit(solution)/shard_map/ppermute | solution.py:462
  38.6 14.6 %copy-start.9 = (bf16[864,512]{1,0:T(8,128)(2,1)}, bf16[864,512]{1,0:T(8,128)(2,1)S(1)}, u32[]{:S(2)}) copy-start(bf16[864,512]{1,0:T(8,128)(2,1)S(1)} %collective-permute-done.3.refs_3_) | copy-start | bytes 2654212
  38.6 14.6 %copy-start.11 = (bf16[864,512]{1,0:T(8,128)(2,1)}, bf16[864,512]{1,0:T(8,128)(2,1)S(1)}, u32[]{:S(2)}) copy-start(bf16[864,512]{1,0:T(8,128)(2,1)S(1)} %collective-permute-done.4.refs_4_) | copy-start | bytes 2654212
  39.2 0.7 copy-start.13
  39.9 13.3 %collective-permute-start.10 = (bf16[384,256]{1,0:T(8,128)(2,1)S(1)}, bf16[384,256]{1,0:T(8,128)(2,1)S(1)}, u32[]{:S(2)}, u32[]{:S(2)}) collective-permute-start(bf16[384,256]{1,0:T(8,128)(2,1)S(1)} %get-tuple-element.52), channel_id=1, source_target_pairs={{0,1},{1,0},{2,3},{3,2},{4,5},{5,4},{6,7},{7,6},{8,9},{9,8},{10,11... | collective-permute-start | bytes 589832 | tf_op jit(solution)/shard_map/ppermute | solution.py:483
  40.4 24.1 %collective-permute-start.8 = (bf16[864,512]{1,0:T(8,128)(2,1)S(1)}, bf16[864,512]{1,0:T(8,128)(2,1)}, u32[]{:S(2)}, u32[]{:S(2)}) collective-permute-start(bf16[864,512]{1,0:T(8,128)(2,1)S(1)} %collective-permute-done.3.refs_3_), channel_id=1, source_target_pairs={{0,4},{1,5},{4,8},{5,9},{8,12},{9,13},{12,14},{13,15},{14,10},{15,... | collective-permute-start | bytes 2654216 | tf_op jit(solution)/shard_map/ppermute | solution.py:448
  42.6 21.9 %collective-permute-start.9 = (bf16[864,512]{1,0:T(8,128)(2,1)S(1)}, bf16[864,512]{1,0:T(8,128)(2,1)}, u32[]{:S(2)}, u32[]{:S(2)}) collective-permute-start(bf16[864,512]{1,0:T(8,128)(2,1)S(1)} %collective-permute-done.4.refs_4_), channel_id=1, source_target_pairs={{0,2},{1,3},{4,0},{5,1},{8,4},{9,5},{12,8},{13,9},{14,12},{15,13},... | collective-permute-start | bytes 2654216 | tf_op jit(solution)/shard_map/ppermute | solution.py:449
  53.2 0.7 copy-start.24
  64.5 21.3 %collective-permute-start.11 = (bf16[864,512]{1,0:T(8,128)(2,1)}, bf16[864,512]{1,0:T(8,128)(2,1)S(1)}, u32[]{:S(2)}, u32[]{:S(2)}) collective-permute-start(bf16[864,512]{1,0:T(8,128)(2,1)} %collective-permute-done.8.refs_5_), channel_id=1, source_target_pairs={{0,4},{1,5},{4,8},{5,9},{8,12},{9,13},{12,14},{13,15},{14,10},{15,... | collective-permute-start | bytes 2654216 | tf_op jit(solution)/shard_map/ppermute | solution.py:448
  66.0 20.6 %collective-permute-start.12 = (bf16[864,512]{1,0:T(8,128)(2,1)}, bf16[864,512]{1,0:T(8,128)(2,1)}, u32[]{:S(2)}, u32[]{:S(2)}) collective-permute-start(bf16[864,512]{1,0:T(8,128)(2,1)} %collective-permute-done.9.refs_6_), channel_id=1, source_target_pairs={{0,2},{1,3},{4,0},{5,1},{8,4},{9,5},{12,8},{13,9},{14,12},{15,13},... | collective-permute-start | bytes 2654216 | tf_op jit(solution)/shard_map/ppermute | solution.py:449
  66.8 1.2 copy-start.5
  68.0 1.2 copy-start.10
  69.2 1.2 copy-start.12
  78.5 2.0 %copy-start = (bf16[2,2,512,1024]{3,2,1,0:T(8,128)(2,1)}, bf16[2,2,512,1024]{3,2,1,0:T(8,128)(2,1)S(1)}, u32[]{:S(2)}) copy-start(bf16[2,2,512,1024]{3,2,1,0:T(8,128)(2,1)S(1)} %get-tuple-element.64.refs_0_) | copy-start | bytes 12582916
  80.5 1.4 copy-start.2
  87.4 10.2 %collective-permute-start.13 = (bf16[432,512]{1,0:T(8,128)(2,1)}, bf16[432,512]{1,0:T(8,128)(2,1)S(1)}, u32[]{:S(2)}, u32[]{:S(2)}) collective-permute-start(bf16[432,512]{1,0:T(8,128)(2,1)} %slice.68), channel_id=1, source_target_pairs={{0,4},{1,5},{4,8},{5,9},{8,12},{9,13},{12,14},{13,15},{14,10},{15,... | collective-permute-start | bytes 1327112 | tf_op jit(solution)/shard_map/ppermute | solution.py:448
  89.6 10.2 %collective-permute-start.14 = (bf16[432,512]{1,0:T(8,128)(2,1)}, bf16[432,512]{1,0:T(8,128)(2,1)}, u32[]{:S(2)}, u32[]{:S(2)}) collective-permute-start(bf16[432,512]{1,0:T(8,128)(2,1)} %slice.69), channel_id=1, source_target_pairs={{0,2},{1,3},{4,0},{5,1},{8,4},{9,5},{12,8},{13,9},{14,12},{15,13},... | collective-permute-start | bytes 1327112 | tf_op jit(solution)/shard_map/ppermute | solution.py:449
  90.8 2.2 %copy-start.1 = (bf16[2,2,512,1024]{3,2,1,0:T(8,128)(2,1)S(1)}, bf16[2,2,512,1024]{3,2,1,0:T(8,128)(2,1)}, u32[]{:S(2)}) copy-start(bf16[2,2,512,1024]{3,2,1,0:T(8,128)(2,1)} %copy-done) | copy-start | bytes 12582916
  93.0 6.9 %copy-start.3 = (bf16[1,2,512,1024]{3,2,1,0:T(8,128)(2,1)S(1)}, bf16[1,2,512,1024]{3,2,1,0:T(8,128)(2,1)}, u32[]{:S(2)}) copy-start(bf16[1,2,512,1024]{3,2,1,0:T(8,128)(2,1)} %copy-done.2) | copy-start | bytes 6291460
  99.9 5.9 %copy-start.19 = (s32[512]{0:T(512)S(1)}, s32[512]{0:T(512)}, u32[]{:S(2)}) copy-start(s32[512]{0:T(512)} %param.27) | copy-start | bytes 6148
  99.9 7.4 %copy-start.6 = (bf16[512,512]{1,0:T(8,128)(2,1)S(1)}, bf16[512,512]{1,0:T(8,128)(2,1)}, u32[]{:S(2)}) copy-start(bf16[512,512]{1,0:T(8,128)(2,1)} %features_ref.3) | copy-start | bytes 1572868
  99.9 7.4 %copy-start.7 = (bf16[512,512]{1,0:T(8,128)(2,1)S(1)}, bf16[512,512]{1,0:T(8,128)(2,1)}, u32[]{:S(2)}) copy-start(bf16[512,512]{1,0:T(8,128)(2,1)} %weight_ref.1) | copy-start | bytes 1572868
  99.9 7.4 %copy-start.8 = (f32[512]{0:T(512)S(1)}, f32[512]{0:T(512)}, u32[]{:S(2)}) copy-start(f32[512]{0:T(512)} %param.18) | copy-start | bytes 6148
  103.0 4.3 %collective-permute-start.15 = (bf16[512,512]{1,0:T(8,128)(2,1)S(1)}, bf16[512,512]{1,0:T(8,128)(2,1)S(1)}, u32[]{:S(2)}, u32[]{:S(2)}) collective-permute-start(bf16[512,512]{1,0:T(8,128)(2,1)S(1)} %get-tuple-element.70), channel_id=1, source_target_pairs={{0,1},{1,0},{2,3},{3,2},{4,5},{5,4},{6,7},{7,6},{8,9},{9,8},{10,11... | collective-permute-start | bytes 1572872 | tf_op jit(solution)/shard_map/ppermute | solution.py:512
  107.3 7.8 %copy-start.14 = (bf16[512,1536]{1,0:T(8,128)(2,1)S(1)}, bf16[512,1536]{1,0:T(8,128)(2,1)}, u32[]{:S(2)}) copy-start(bf16[512,1536]{1,0:T(8,128)(2,1)} %param.20) | copy-start | bytes 4718596
  109.6 30.4 %all-to-all-start = ((bf16[16,64,512]{2,1,0:T(8,128)(2,1)}), bf16[16,64,512]{2,1,0:T(8,128)(2,1)}, u32[]{:S(2)}, u32[]{:S(2)}) async-start(bf16[16,64,512]{2,1,0:T(8,128)(2,1)} %bitcast.10), calls=%async_computation | async-start | bytes 2097152 | tf_op jit(solution)/shard_map/all_to_all | solution.py:528
  115.1 1.3 copy-start.21
  116.7 23.3 %copy-start.20 = (s32[512]{0:T(512)}, s32[512]{0:T(512)S(1)}, u32[]{:S(2)}) copy-start(s32[512]{0:T(512)S(1)} %multiply_add_fusion) | copy-start | bytes 6148
  161.7 29.8 %all-to-all-start.1 = ((bf16[16,64,512]{2,1,0:T(8,128)(2,1)}), bf16[16,64,512]{2,1,0:T(8,128)(2,1)S(1)}, u32[]{:S(2)}, u32[]{:S(2)}) async-start(bf16[16,64,512]{2,1,0:T(8,128)(2,1)} %bitcast.31), calls=%async_computation.1 | async-start | bytes 2097152 | tf_op jit(solution)/shard_map/all_to_all | solution.py:561

commit v14 on v13

--- a/solution.py
+++ b/solution.py
@@ -119,7 +119,7 @@
     )(start, rows, own, got)
 
 
-def conv_kernel(slots, later, ready, first, places_ref, *refs):
+def conv_kernel(slots, later, ready, first, places_ref, shifts_ref, *refs):
     refs = list(refs)
 
     def take(count):
@@ -128,7 +128,7 @@
         return taken
 
     sources = take(1 if ready else 2)
-    pieces = take(sum(slots))
+    pieces = take(sum(len(parts) for parts in slots))
     before = [] if first else take(2)
     outs = take(2)
     kept = take(len(later))
@@ -148,24 +148,23 @@
             copy.start()
         return copies
 
-    copies, taken = [], 0
-    for at, count in enumerate(slots):
+    copies = []
+    for at, parts in enumerate(slots):
         row = pl.multiple_of(places_ref[2 * at + 1], 16)
         copies.append([] if ready else stretch(at, lhs.at[at], sems.at[at]))
-        short = count * pieces[taken].shape[0]
-        edge = length - short
+        edge = length - sum(size for _, size, _ in parts)
         if edge:
             held[at, :edge] = jnp.zeros((edge, held.shape[2]), BF16)
             held[at, length - edge :] = jnp.zeros((edge, held.shape[2]), BF16)
-        for part in range(count):
-            piece = pieces[taken]
-            size = piece.shape[0]
+        for part, (start, size, kind) in enumerate(parts):
+            place = row if kind is None else pl.multiple_of(row + shifts_ref[kind], 16)
+            (piece,) = pieces[:1]
+            del pieces[:1]
             copy = pltpu.make_async_copy(
-                piece, held.at[at, pl.ds(row + part * size, size)], sems.at[at, 2 + part]
+                piece.at[pl.ds(start, size)], held.at[at, pl.ds(place, size)], sems.at[at, 2 + part]
             )
             copy.start()
             copies[-1].append(copy)
-            taken += 1
     extra, slot = [], len(slots)
     for group, count in enumerate(later):
         for place in range(count):
@@ -186,13 +185,13 @@
         copy.wait()
 
 
-def conv_part(sources, places, pieces, before, length, later=(), dtype=F32):
+def conv_part(sources, places, shifts, pieces, before, length, later=(), dtype=F32):
     ready = len(sources) == 1
     points = sources[0].shape[2] if ready else sources[0].shape[0]
-    width = pieces[0][0].shape[1]
-    slots = [len(parts) for parts in pieces]
-    flat = [piece for parts in pieces for piece in parts]
-    held = 1 + len(sources) + len(flat)
+    width = pieces[0][0][0].shape[1]
+    slots = [[part[1:] for part in parts] for parts in pieces]
+    flat = [part[0] for parts in pieces for part in parts]
+    held = 2 + len(sources) + len(flat)
     kept = [] if before is None else [block for block in range(2) if block or dtype == F32]
     spec = pl.BlockSpec(memory_space=pl.ANY)
     return call(
@@ -205,7 +204,7 @@
         24 if ready else 36,
         4 * points * length * width * len(slots),
         2 * length * (2 * points + width) * len(slots),
-        in_specs=[pl.BlockSpec(memory_space=pltpu.SMEM)]
+        in_specs=[pl.BlockSpec(memory_space=pltpu.SMEM)] * 2
         + [pl.BlockSpec() if ready else spec] * len(sources)
         + [spec] * len(flat)
         + ([] if before is None else [pl.BlockSpec()] * 2),
@@ -215,7 +214,7 @@
             pltpu.VMEM((len(slots), length, width), BF16),
             pltpu.SemaphoreType.DMA((len(slots) + sum(later), 4)),
         ],
-    )(places.reshape(-1), *sources, *flat, *(before or ()))
+    )(places.reshape(-1), shifts, *sources, *flat, *(before or ()))
 
 
 def mix_kernel(own_ref, got_ref, features_ref, weight_ref, gain_ref, slot_ref, out_ref):
@@ -350,23 +349,23 @@
 def way_round(devices, rows, length):
     chips = devices // 2
     cycle = list(range(0, chips, 2)) + list(range(chips - 1, 0, -2))
-    back, on = [], []
+    chains = [], []
     places = [None] * devices
     for place, chip in enumerate(cycle):
-        for core in range(2):
+        for core, way in ((0, 1), (1, -1)):
             me = 2 * chip + core
-            back.append((me, 2 * cycle[(place + 1) % chips] + core))
-            on.append((me, 2 * cycle[place - 1] + core))
+            for chain, step in zip(chains, (way, -way)):
+                chain.append((me, 2 * cycle[(place + step) % chips] + core))
             order = [0]
             for step in range(1, chips // 2):
-                order += [-step, step]
+                order += [-step * way, step * way]
             order.append(chips // 2)
             places[me] = []
             for offset in order:
                 start = cycle[(place + offset) % chips] * rows
                 column = min(start // 128 * 128, chips * rows - length)
                 places[me].append((column, start - column))
-    return back, on, places
+    return *chains, places
 
 
 def padded_taps(neighbours):
@@ -424,7 +423,7 @@
         functools.partial(faces_kernel, unit),
         [jax.ShapeDtypeStruct((points, half), BF16)] * 2
         + [jax.ShapeDtypeStruct((count * size, width), BF16) for count in counts],
-        60,
+        32,
         4 * points * width * width,
         8 * points * width,
         in_specs=[pl.BlockSpec(memory_space=pltpu.SMEM)] + [pl.BlockSpec()] * 2,
@@ -434,26 +433,41 @@
 
     rows = mine.shape[0]
     length = -(-(rows + 127) // 128) * 128 if round_trip else rows * (devices // 2)
-    back_pairs, on_pairs, places = way_round(devices, rows, length)
-    back, on = [mine], [mine]
+    first_pairs, second_pairs, places = way_round(devices, rows, length)
+    side = lax.axis_index("groups")
+    missing = -(-rows // 64) * 16
+    passed = rows - missing
+    shifts = jnp.stack([side * missing, (1 - side) * passed]).astype(jnp.int32)
+    begun = lax.dynamic_slice(mine, (side * missing, 0), (passed, width))
+    first, second = [begun], [begun]
 
     def pass_on(*beside):
         if not round_trip:
             return beside
-        tied = lax.optimization_barrier((back[-1], on[-1], *beside))
-        first, second = tied[:2]
-        back[-1], on[-1] = first, second
-        if len(back) == devices // 4:
-            first, second = first[: rows // 2], second[rows // 2 :]
-        back.append(lax.ppermute(first, "blocks", back_pairs))
-        on.append(lax.ppermute(second, "blocks", on_pairs))
+        tied = lax.optimization_barrier((first[-1], second[-1], *beside))
+        first[-1], second[-1] = tied[:2]
+        last = len(first) == devices // 4
+        first.append(lax.ppermute(first[-1], "blocks", first_pairs))
+        if not last:
+            second.append(lax.ppermute(second[-1], "blocks", second_pairs))
         return tied[2:]
+
+    def complete(*arrived):
+        lent = [
+            lax.dynamic_slice(piece, (side * (passed - missing), 0), (missing, width))
+            for piece in arrived
+        ]
+        got = lax.ppermute(jnp.concatenate(lent), "groups", [(0, 1), (1, 0)])
+        return [
+            [(piece, 0, passed, 0), (got, at * missing, missing, 1)]
+            for at, piece in enumerate(arrived)
+        ]
 
     if round_trip:
         lists, back_list, on_list = faces
-        side = face_pairs(devices, 1, 0) + face_pairs(devices, -1, 0)
+        across = face_pairs(devices, 1, 0) + face_pairs(devices, -1, 0)
         lists, other_local, other_neighbours = pass_on(lists, other_local, other_neighbours)
-        lists = lax.ppermute(lists, "blocks", side)
+        lists = lax.ppermute(lists, "blocks", across)
     own_rows, other_rows = padded_taps(neighbours), padded_taps(other_neighbours)
     if round_trip:
         to_on = jnp.concatenate([on_list, lists[2 * size :]])
@@ -461,6 +475,7 @@
         behind = lax.ppermute(to_on, "blocks", face_pairs(devices, 0, 1))
         ahead = lax.ppermute(to_back, "blocks", face_pairs(devices, 0, -1))
         lists, behind, ahead = pass_on(lists, behind, ahead)
+        near = complete(first[1], second[1])
         own_remote, other_half = call(
             received_kernel,
             [jax.ShapeDtypeStruct((6 * size, half), BF16)] * 2,
@@ -482,24 +497,33 @@
         start = jnp.full((1,), points, jnp.int32)
     other_remote = lax.ppermute(other_half, "blocks", partner)
     own_stacked = gather_block(start, own_rows, own_local, own_remote)
+    own_stacked, other_rows, other_remote = pass_on(own_stacked, other_rows, other_remote)
+    if round_trip:
+        middle = complete(first[2], second[2])
     other_stacked = gather_block(start, other_rows, other_local, other_remote)
-    stacked = pass_on(other_stacked, own_stacked)
     if round_trip:
+        other_stacked, own_stacked, middle_got = pass_on(other_stacked, own_stacked, middle[0][1][0])
+        middle = [[parts[0], (middle_got, *parts[1][1:])] for parts in middle]
+    stacked = other_stacked, own_stacked
+    if round_trip:
+        far = complete(first[3], second[3])
+        opposite = complete(first[4])
         places = jnp.array(places, jnp.int32)[index]
-        early = [[mine], [back[1]], [on[1]], [back[2]], [on[2]]]
-        *sums, next_lhs, last_lhs = conv_part(stacked, places, early, None, length, (2, 1))
-        sums = pass_on(*sums)
-        late = [[back[3]], [on[3]]]
-        sums = conv_part([next_lhs], places[5:7], late, sums, length)
-        last = [[back[4], on[4]]]
+        early = [[(mine, 0, rows, None)]] + near
+        *sums, middle_lhs, far_lhs, last_lhs = conv_part(
+            stacked, places, shifts, early, None, length, (2, 2, 1)
+        )
+        sums = conv_part([middle_lhs], places[3:5], shifts, middle, sums, length)
+        sums = conv_part([far_lhs], places[5:7], shifts, far, sums, length)
         for_partner, own_part = conv_part(
-            [last_lhs], places[7:], last, sums, length, dtype=BF16
+            [last_lhs], places[7:], shifts, opposite, sums, length, dtype=BF16
         )
     else:
-        groups = [list(range(first, devices, 2)) for first in range(2)]
+        groups = [list(range(core, devices, 2)) for core in range(2)]
         weight = lax.all_gather(mine, "blocks", axis=0, tiled=True, axis_index_groups=groups)
         nowhere = jnp.zeros((1, 2), jnp.int32)
-        for_partner, own_part = conv_part(stacked, nowhere, [[weight]], None, length)
+        whole = [[(weight, 0, weight.shape[0], None)]]
+        for_partner, own_part = conv_part(stacked, nowhere, shifts, whole, None, length)
 
     positions = jnp.arange(points, dtype=jnp.int32)
     target = serial_rank // points

time: 194 us -> 184 us (0.948)
  waiting for transfers between devices: 74.5 us -> 65.6 us
  local copies, waits for them, and re-layouts: 20.4 us -> 13.1 us
  other arithmetic: 3.79 us -> 6.61 us
  starting transfers between devices: 29.4 us -> 31.4 us
    ppermute x9 -> x12, waiting for transfers between devices: 23.2 us -> 14.8 us  [the longest x1 7.22 us: body(): lists = lax.ppermute(lists, 'blocks', across)]
    unnamed x53 -> x27, local copies, waits for them, and re-layouts: 11.9 us -> 3.71 us
    dynamic_slice x0 -> x6, local copies, waits for them, and re-layouts: none -> 3.02 us  [the longest x5 2.97 us: complete(): lax.dynamic_slice(piece, (side * (passed - missing), 0), (missing, width))]
    pallas_call x3 -> x4, Pallas kernels: 14.8 us -> 17.7 us  [conv_part(): call(functools.partial(conv_kernel, slots, later, ready, before is None),...]
    slice x3 -> x1, local copies, waits for them, and re-layouts: 2.59 us -> 0.01 us  [body(): sums = conv_part([middle_lhs], places[3:5], shifts, middle, sums, length)]
    ppermute x9 -> x12, starting transfers between devices: 9.01 us -> 11.2 us  [the longest x3 5.29 us: pass_on(): second.append(lax.ppermute(second[-1], 'blocks', second_pairs))]
  transfers between devices with their start and end apart: 18 -> 21, of which waited for: 11 -> 10; matrix products, arithmetic and copies ran while one was open for 6% -> 9% of each run, Pallas kernels for 18% -> 21%
where the time goes in v14:
time: 184 us; the launch traced here: 183 us
  Pallas kernels  65.7 us (36%)
  waiting for transfers between devices  65.6 us (36%)
  starting transfers between devices  31.4 us (17%)
  local copies, waits for them, and re-layouts  13.1 us (7%)
  other arithmetic  6.61 us (4%)
    all_to_all x1, waiting for transfers between devices, body(): lax.all_to_all(back.reshape(devices, capacity, width), 'blocks', split_ax...  24.7 us
    pallas_call x1, Pallas kernels, body(): call(block_kernel, jax.ShapeDtypeStruct((slots, width), BF16), 60, 20 * p...  21.6 us
    all_to_all x1, waiting for transfers between devices, body(): lax.all_to_all(outgoing.reshape(devices, capacity, width), 'blocks', spli...  21.4 us
    pallas_call x2, Pallas kernels, gather_block(): call(functools.partial(gather_kernel, taps), jax.ShapeDtypeStruct((points...  21.2 us
    pallas_call x4, Pallas kernels, conv_part(): call(functools.partial(conv_kernel, slots, later, ready, before is None),...  17.7 us
    ppermute x1, waiting for transfers between devices, body(): lists = lax.ppermute(lists, 'blocks', across)  7.22 us
    all_to_all x1, starting transfers between devices, body(): lax.all_to_all(outgoing.reshape(devices, capacity, width), 'blocks', spli...  5.33 us
    ppermute x3, starting transfers between devices, pass_on(): second.append(lax.ppermute(second[-1], 'blocks', second_pairs))  5.29 us
  transfers between devices with their start and end apart: 21, of which 10 were waited for; matrix products, arithmetic and copies ran while one was open for 9% of the time, Pallas kernels for 21%

profile of v14, /device:TPU:9, one launch (start us, length us, event | category | flops | bytes accessed | tf_op | source)
XLA Modules:
  0.0 182.8 jit_solution(11147961564721084982)
XLA Ops:
  0.0 1.1 slice.56
  1.1 0.7 collective-permute-start
  1.8 0.7 slice_bitcast_fusion
  2.5 0.8 select_bitcast_fusion
  3.3 0.2 reshape.92.rows_ref
  3.5 1.0 copy-done
  4.5 0.7 shard_map.145
  5.2 0.7 copy-done.5
  5.9 0.8 copy.35
  6.8 0.5 collective-permute-start.2
  7.3 1.1 slice.55
  8.3 0.7 constant_dynamic-slice_fusion.8
  9.3 0.1 copy.37
  9.8 1.3 maximum_select_fusion
  11.2 2.4 %collective-permute-start.5 = (bf16[192,512]{1,0:T(8,128)(2,1)S(1)}, bf16[192,512]{1,0:T(8,128)(2,1)S(1)}, u32[]{:S(2)}, u32[]{:S(2)}) collective-permute-start(bf16[192,512]{1,0:T(8,128)(2,1)S(1)} %get-tuple-element.47), channel_id=1, source_target_pairs={{0,8},{1,9},{2,10},{3,11},{4,12},{5,13},{6,14},{7,15},{8,0},{9,1},... | collective-permute-start | bytes 589832 | tf_op jit(solution)/shard_map/ppermute | solution.py:470
  13.6 0.2 collective-permute-start.3
  13.7 1.3 collective-permute-start.4
  15.2 7.2 %collective-permute-done.5.side_ref = bf16[192,512]{1,0:T(8,128)(2,1)S(1)} collective-permute-done((bf16[192,512]{1,0:T(8,128)(2,1)S(1)}, bf16[192,512]{1,0:T(8,128)(2,1)S(1)}, u32[]{:S(2)}, u32[]{:S(2)}) %collective-permute-start.5) | collective-permute-done | bytes 196640 | tf_op jit(solution)/shard_map/ppermute | solution.py:470
  22.4 3.5 %collective-permute-start.6 = (bf16[128,512]{1,0:T(8,128)(2,1)S(1)}, bf16[128,512]{1,0:T(8,128)(2,1)S(1)}, u32[]{:S(2)}, u32[]{:S(2)}) collective-permute-start(bf16[128,512]{1,0:T(8,128)(2,1)S(1)} %pad_maximum_fusion.3), channel_id=1, source_target_pairs={{0,1},{1,2},{2,3},{3,4},{4,5},{5,6},{6,7},{8,9},{9,10},{10,11},{11... | collective-permute-start | bytes 393224 | tf_op jit(solution)/shard_map/ppermute | solution.py:475
  26.0 1.9 %collective-permute-start.7 = (bf16[128,512]{1,0:T(8,128)(2,1)S(1)}, bf16[128,512]{1,0:T(8,128)(2,1)S(1)}, u32[]{:S(2)}, u32[]{:S(2)}) collective-permute-start(bf16[128,512]{1,0:T(8,128)(2,1)S(1)} %pad_maximum_fusion.4), channel_id=1, source_target_pairs={{1,0},{2,1},{3,2},{4,3},{5,4},{6,5},{7,6},{9,8},{10,9},{11,10},{12... | collective-permute-start | bytes 393224 | tf_op jit(solution)/shard_map/ppermute | solution.py:476
  27.9 1.1 add_convert_fusion.1
  29.0 3.5 %collective-permute-done.7.ahead_ref = bf16[128,512]{1,0:T(8,128)(2,1)S(1)} collective-permute-done((bf16[128,512]{1,0:T(8,128)(2,1)S(1)}, bf16[128,512]{1,0:T(8,128)(2,1)S(1)}, u32[]{:S(2)}, u32[]{:S(2)}) %collective-permute-start.7) | collective-permute-done | bytes 131104 | tf_op jit(solution)/shard_map/ppermute | solution.py:476
  32.5 3.6 %collective-permute-done.3.refs_3_ = bf16[640,512]{1,0:T(8,128)(2,1)S(1)} collective-permute-done((bf16[640,512]{1,0:T(8,128)(2,1)S(1)}, bf16[640,512]{1,0:T(8,128)(2,1)S(1)}, u32[]{:S(2)}, u32[]{:S(2)}) %collective-permute-start.3) | collective-permute-done | bytes 655392 | tf_op jit(solution)/shard_map/ppermute | solution.py:450
  36.1 0.3 collective-permute-done.4.refs_5_
  36.4 2.2 %collective-permute-start.9 = (bf16[640,512]{1,0:T(8,128)(2,1)S(1)}, bf16[640,512]{1,0:T(8,128)(2,1)}, u32[]{:S(2)}, u32[]{:S(2)}) collective-permute-start(bf16[640,512]{1,0:T(8,128)(2,1)S(1)} %collective-permute-done.4.refs_5_), channel_id=1, source_target_pairs={{0,2},{1,5},{4,0},{5,9},{8,4},{9,13},{12,8},{13,15},{14,12},{15,11... | collective-permute-start | bytes 1966088 | tf_op jit(solution)/shard_map/ppermute | solution.py:452
  38.7 0.8 pad_maximum_fusion.1
  39.5 1.2 collective-permute-start.14
  40.7 0.6 shard_map.146
  41.3 0.7 copy-done.4
  41.9 1.0 collective-permute-start.10
  42.9 10.6 %shard_map.147.refs_1_ = bf16[512,6912]{1,0:T(8,128)(2,1)} custom-call(s32[1]{0:T(128)} %bitcast.8.start_ref, f32[512,128]{1,0:T(8,128)} %get-tuple-element.85.rows_ref, bf16[512,256]{1,0:T(8,128)(2,1)} %copy-done.5, bf16[384,256]{1,0:T(8,128)(2,1)} %copy-done.4), custom_call_target="tpu_custom_call" | custom-call | flops 6341787648 | bytes 7077888 | tf_op jit(solution)/shard_map/pallas_call | solution.py:105
  53.6 1.0 constant_dynamic-slice_fusion.5
  54.6 1.8 collective-permute-start.12
  56.4 0.8 pad_maximum_fusion
  57.2 0.4 collective-permute-start.13
  57.7 10.6 %shard_map.148.refs_0_ = bf16[512,6912]{1,0:T(8,128)(2,1)} custom-call(s32[1]{0:T(128)} %bitcast.8.start_ref, f32[512,128]{1,0:T(8,128)} %get-tuple-element.61.rows_ref, bf16[512,256]{1,0:T(8,128)(2,1)} %collective-permute-done.1.own_ref, bf16[384,256]{1,0:T(8,128)(2,1)} %copy-done.11), custom_call_target="tpu_custom_call" | custom-call | flops 6341787648 | bytes 7077888 | tf_op jit(solution)/shard_map/pallas_call | solution.py:105
  68.3 0.2 collective-permute-done.13.refs_2_.refs_4_
  68.5 3.2 %collective-permute-done.12.refs_3_ = bf16[640,512]{1,0:T(8,128)(2,1)} collective-permute-done((bf16[640,512]{1,0:T(8,128)(2,1)}, bf16[640,512]{1,0:T(8,128)(2,1)}, u32[]{:S(2)}, u32[]{:S(2)}) %collective-permute-start.12) | collective-permute-done | bytes 655392 | tf_op jit(solution)/shard_map/ppermute | solution.py:452
  71.7 1.0 constant_dynamic-slice_fusion.1
  72.7 1.0 constant_dynamic-slice_fusion
  73.7 0.8 collective-permute-start.17
  74.6 6.9 %shard_map.149 = (f32[512,512]{1,0:T(8,128)S(1)}, f32[512,512]{1,0:T(8,128)S(1)}, bf16[2,2,512,1024]{3,2,1,0:T(8,128)(2,1)S(1)}, bf16[2,2,512,1024]{3,2,1,0:T(8,128)(2,1)S(1)}, bf16[1,2,512,1024]{3,2,1,0:T(8,128)(2,1)S(1)}) custom-call(s32[16]{0:T(128)S(1)} %reshape_squeeze.3.places_ref, s32[2]{0:T(128)S(1)} %pad_add_fusion.1.shifts_ref, ...), custom_call_target="tpu_custom_call" | custom-call | flops 3221225472 | bytes 9437184 | tf_op jit(solution)/shard_map/pallas_call | solution.py:197
  81.5 0.2 collective-permute-done.15.refs_1_
  81.7 0.8 collective-permute-start.16
  82.5 4.1 %shard_map.150 = (f32[512,512]{1,0:T(8,128)S(1)}, f32[512,512]{1,0:T(8,128)S(1)}) custom-call(s32[4]{0:T(128)S(1)} %reshape.79.places_ref, s32[2]{0:T(128)S(1)} %pad_add_fusion.1.shifts_ref, bf16[2,2,512,1024]{3,2,1,0:T(8,128)(2,1)S(1)} %get-tuple-element.71.refs_0_, ...), custom_call_target="tpu_custom_call", output_to_operand_aliasing={{0}: (7, {}), {1}: (8, {})} | custom-call | flops 2147483648 | bytes 6291456 | tf_op jit(solution)/shard_map/pallas_call | solution.py:197
  86.6 4.4 %shard_map.151 = (f32[512,512]{1,0:T(8,128)S(1)}, f32[512,512]{1,0:T(8,128)S(1)}) custom-call(s32[4]{0:T(128)S(1)} %reshape.78.places_ref, s32[2]{0:T(128)S(1)} %pad_add_fusion.1.shifts_ref, bf16[2,2,512,1024]{3,2,1,0:T(8,128)(2,1)S(1)} %get-tuple-element.69.refs_0_, ...), custom_call_target="tpu_custom_call", output_to_operand_aliasing={{0}: (7, {}), {1}: (8, {})} | custom-call | flops 2147483648 | bytes 6291456 | tf_op jit(solution)/shard_map/pallas_call | solution.py:197
  91.1 2.4 %shard_map.152 = (bf16[512,512]{1,0:T(8,128)(2,1)S(1)}, f32[512,512]{1,0:T(8,128)S(1)}) custom-call(s32[2]{0:T(128)S(1)} %slice_bitcast_fusion.1.places_ref, s32[2]{0:T(128)S(1)} %pad_add_fusion.1.shifts_ref, bf16[1,2,512,1024]{3,2,1,0:T(8,128)(2,1)S(1)} %get-tuple-element.67.refs_0_, ...), custom_call_target="tpu_custom_call", output_to_operand_aliasing={{1}: (6, {})} | custom-call | flops 1073741824 | bytes 3145728 | tf_op jit(solution)/shard_map/pallas_call | solution.py:197
  93.4 2.2 %collective-permute-start.18 = (bf16[512,512]{1,0:T(8,128)(2,1)S(1)}, bf16[512,512]{1,0:T(8,128)(2,1)S(1)}, u32[]{:S(2)}, u32[]{:S(2)}) collective-permute-start(bf16[512,512]{1,0:T(8,128)(2,1)S(1)} %get-tuple-element.80), channel_id=1, source_target_pairs={{0,1},{1,0},{2,3},{3,2},{4,5},{5,4},{6,7},{7,6},{8,9},{9,8},{10,11... | collective-permute-start | bytes 1572872 | tf_op jit(solution)/shard_map/ppermute | solution.py:536
  95.7 0.3 convert_reduce_fusion.1
  96.0 1.2 collective-permute-done.18.got_ref
  97.2 2.3 %shard_map.153 = bf16[1024,512]{1,0:T(8,128)(2,1)} custom-call(f32[512,512]{1,0:T(8,128)S(1)} %get-tuple-element.79.own_ref, bf16[512,512]{1,0:T(8,128)(2,1)S(1)} %collective-permute-done.18.got_ref, bf16[512,512]{1,0:T(8,128)(2,1)S(1)} %copy-done.1, bf16[512,512]{1,0:T(8,128)(2,1)S(1)} %copy-done.2, f32[1,512]{1,0:T(1,128)S(1)} %bitcast.31, ...), custom_call_target="tpu_custom_call" | custom-call | flops 805306368 | bytes 2097152 | tf_op jit(solution)/shard_map/pallas_call | solution.py:538
  99.5 5.3 %all-to-all-start = ((bf16[16,64,512]{2,1,0:T(8,128)(2,1)}), bf16[16,64,512]{2,1,0:T(8,128)(2,1)}, u32[]{:S(2)}, u32[]{:S(2)}) async-start(bf16[16,64,512]{2,1,0:T(8,128)(2,1)} %bitcast.12), calls=%async_computation | async-start | bytes 2097152 | tf_op jit(solution)/shard_map/all_to_all | solution.py:552
  104.9 0.2 convert_reduce_fusion
  105.1 0.9 copy.40.slot_col_ref
  106.0 0.9 fusion.5
  106.9 0.2 copy.42
  107.1 0.2 copy.43
  107.4 1.1 maximum_bitcast_fusion.qv_hbm
  108.4 21.4 %all-to-all-done = bf16[16,64,512]{2,1,0:T(8,128)(2,1)} async-done(((bf16[16,64,512]{2,1,0:T(8,128)(2,1)}), bf16[16,64,512]{2,1,0:T(8,128)(2,1)}, u32[]{:S(2)}, u32[]{:S(2)}) %all-to-all-start) | async-done | bytes 1048608 | tf_op jit(solution)/shard_map/all_to_all | solution.py:552
  129.8 21.6 %shard_map.154 = bf16[1024,512]{1,0:T(8,128)(2,1)} custom-call(bf16[1024,512]{1,0:T(8,128)(2,1)} %bitcast.13.arrived_ref, s32[512,1]{1,0:T(8,128)} %copy.40.slot_col_ref, s32[1,512]{1,0:T(1,128)} %bitcast.36, f32[1,512]{1,0:T(1,128)} %bitcast.37, f32[1,512]{1,0:T(1,128)} %bitcast.38, bf16[1024,512]{1,0:T(8,128)(2,1)} %maximum_bitcast_fusion.qv_hbm, ...), custom_call_target="tpu_custom_call" | custom-call | flops 2684354560 | bytes 4194304 | tf_op jit(solution)/shard_map/pallas_call | solution.py:559
  151.4 5.0 %all-to-all-start.1 = ((bf16[16,64,512]{2,1,0:T(8,128)(2,1)}), bf16[16,64,512]{2,1,0:T(8,128)(2,1)S(1)}, u32[]{:S(2)}, u32[]{:S(2)}) async-start(bf16[16,64,512]{2,1,0:T(8,128)(2,1)} %bitcast.32), calls=%async_computation.1 | async-start | bytes 2097152 | tf_op jit(solution)/shard_map/all_to_all | solution.py:585
  156.4 0.1 copy.41.slot_ref
  156.5 24.7 %all-to-all-done.1 = bf16[16,64,512]{2,1,0:T(8,128)(2,1)S(1)} async-done(((bf16[16,64,512]{2,1,0:T(8,128)(2,1)}), bf16[16,64,512]{2,1,0:T(8,128)(2,1)S(1)}, u32[]{:S(2)}, u32[]{:S(2)}) %all-to-all-start.1) | async-done | bytes 1048608 | tf_op jit(solution)/shard_map/all_to_all | solution.py:585
  181.2 1.5 shard_map.155
  (60 shorter events, 1.1 us)
Async XLA Ops:
  0.0 5.9 %copy-start.7 = (s32[512,26]{0,1:T(8,128)S(1)}, s32[512,26]{0,1:T(8,128)}, u32[]{:S(2)}) copy-start(s32[512,26]{0,1:T(8,128)} %param.26) | copy-start | bytes 159748
  1.1 8.7 %collective-permute-start = (bf16[13,32,512]{2,1,0:T(8,128)(2,1)S(1)}, bf16[13,32,512]{2,1,0:T(8,128)(2,1)}, u32[]{:S(2)}, u32[]{:S(2)}) collective-permute-start(bf16[13,32,512]{2,1,0:T(8,128)(2,1)S(1)} %slice.56), channel_id=1, source_target_pairs={{0,1},{1,0},{2,3},{3,2},{4,5},{5,4},{6,7},{7,6},{8,9},{9,8},{10,11... | collective-permute-start | bytes 1277960 | tf_op jit(solution)/shard_map/ppermute | solution.py:408
  3.4 1.0 copy-start
  5.2 0.7 copy-start.5
  5.9 5.3 %collective-permute-start.1 = (bf16[512,256]{1,0:T(8,128)(2,1)S(1)}, bf16[512,256]{1,0:T(8,128)(2,1)}, u32[]{:S(2)}, u32[]{:S(2)}) collective-permute-start(bf16[512,256]{1,0:T(8,128)(2,1)S(1)} %get-tuple-element.44), channel_id=1, source_target_pairs={{0,1},{1,0},{2,3},{3,2},{4,5},{5,4},{6,7},{7,6},{8,9},{9,8},{10,11... | collective-permute-start | bytes 786440 | tf_op jit(solution)/shard_map/ppermute | solution.py:431
  6.8 4.4 %collective-permute-start.2 = (s32[512,26]{1,0:T(8,128)}, s32[512,26]{1,0:T(8,128)S(1)}, u32[]{:S(2)}, u32[]{:S(2)}) collective-permute-start(s32[512,26]{1,0:T(8,128)} %copy.35), channel_id=1, source_target_pairs={{0,1},{1,0},{2,3},{3,2},{4,5},{5,4},{6,7},{7,6},{8,9},{9,8},{10,11... | collective-permute-start | bytes 159752 | tf_op jit(solution)/shard_map/ppermute | solution.py:432
  11.2 11.2 %collective-permute-start.5 = (bf16[192,512]{1,0:T(8,128)(2,1)S(1)}, bf16[192,512]{1,0:T(8,128)(2,1)S(1)}, u32[]{:S(2)}, u32[]{:S(2)}) collective-permute-start(bf16[192,512]{1,0:T(8,128)(2,1)S(1)} %get-tuple-element.47), channel_id=1, source_target_pairs={{0,8},{1,9},{2,10},{3,11},{4,12},{5,13},{6,14},{7,15},{8,0},{9,1},... | collective-permute-start | bytes 589832 | tf_op jit(solution)/shard_map/ppermute | solution.py:470
  13.6 22.5 %collective-permute-start.3 = (bf16[640,512]{1,0:T(8,128)(2,1)S(1)}, bf16[640,512]{1,0:T(8,128)(2,1)S(1)}, u32[]{:S(2)}, u32[]{:S(2)}) collective-permute-start(bf16[640,512]{1,0:T(8,128)(2,1)S(1)} %constant_dynamic-slice_fusion.7), channel_id=1, source_target_pairs={{0,4},{1,3},{4,8},{5,1},{8,12},{9,5},{12,14},{13,9},{14,10},{15,13... | collective-permute-start | bytes 1966088 | tf_op jit(solution)/shard_map/ppermute | solution.py:450
  13.7 22.7 %collective-permute-start.4 = (bf16[640,512]{1,0:T(8,128)(2,1)S(1)}, bf16[640,512]{1,0:T(8,128)(2,1)S(1)}, u32[]{:S(2)}, u32[]{:S(2)}) collective-permute-start(bf16[640,512]{1,0:T(8,128)(2,1)S(1)} %constant_dynamic-slice_fusion.7), channel_id=1, source_target_pairs={{0,2},{1,5},{4,0},{5,9},{8,4},{9,13},{12,8},{13,15},{14,12},{15,11... | collective-permute-start | bytes 1966088 | tf_op jit(solution)/shard_map/ppermute | solution.py:452
  22.4 6.6 %collective-permute-start.6 = (bf16[128,512]{1,0:T(8,128)(2,1)S(1)}, bf16[128,512]{1,0:T(8,128)(2,1)S(1)}, u32[]{:S(2)}, u32[]{:S(2)}) collective-permute-start(bf16[128,512]{1,0:T(8,128)(2,1)S(1)} %pad_maximum_fusion.3), channel_id=1, source_target_pairs={{0,1},{1,2},{2,3},{3,4},{4,5},{5,6},{6,7},{8,9},{9,10},{10,11},{11... | collective-permute-start | bytes 393224 | tf_op jit(solution)/shard_map/ppermute | solution.py:475
  26.0 6.6 %collective-permute-start.7 = (bf16[128,512]{1,0:T(8,128)(2,1)S(1)}, bf16[128,512]{1,0:T(8,128)(2,1)S(1)}, u32[]{:S(2)}, u32[]{:S(2)}) collective-permute-start(bf16[128,512]{1,0:T(8,128)(2,1)S(1)} %pad_maximum_fusion.4), channel_id=1, source_target_pairs={{1,0},{2,1},{3,2},{4,3},{5,4},{6,5},{7,6},{9,8},{10,9},{11,10},{12... | collective-permute-start | bytes 393224 | tf_op jit(solution)/shard_map/ppermute | solution.py:476
  36.4 17.1 %collective-permute-start.8 = (bf16[640,512]{1,0:T(8,128)(2,1)S(1)}, bf16[640,512]{1,0:T(8,128)(2,1)S(1)}, u32[]{:S(2)}, u32[]{:S(2)}) collective-permute-start(bf16[640,512]{1,0:T(8,128)(2,1)S(1)} %collective-permute-done.3.refs_3_), channel_id=1, source_target_pairs={{0,4},{1,3},{4,8},{5,1},{8,12},{9,5},{12,14},{13,9},{14,10},{15,13... | collective-permute-start | bytes 1966088 | tf_op jit(solution)/shard_map/ppermute | solution.py:450
  36.4 17.1 %collective-permute-start.9 = (bf16[640,512]{1,0:T(8,128)(2,1)S(1)}, bf16[640,512]{1,0:T(8,128)(2,1)}, u32[]{:S(2)}, u32[]{:S(2)}) collective-permute-start(bf16[640,512]{1,0:T(8,128)(2,1)S(1)} %collective-permute-done.4.refs_5_), channel_id=1, source_target_pairs={{0,2},{1,5},{4,0},{5,9},{8,4},{9,13},{12,8},{13,15},{14,12},{15,11... | collective-permute-start | bytes 1966088 | tf_op jit(solution)/shard_map/ppermute | solution.py:452
  39.5 35.1 %collective-permute-start.14 = (bf16[448,512]{1,0:T(8,128)(2,1)}, bf16[448,512]{1,0:T(8,128)(2,1)S(1)}, u32[]{:S(2)}, u32[]{:S(2)}) collective-permute-start(bf16[448,512]{1,0:T(8,128)(2,1)} %pad_maximum_fusion.1), channel_id=1, source_target_pairs={{0,16},{16,0},{1,17},{17,1},{2,18},{18,2},{3,19},{19,3},{4,20},{20... | collective-permute-start | bytes 1376264 | tf_op jit(solution)/shard_map/ppermute | solution.py:460
  41.3 0.7 copy-start.4
  41.9 11.6 %collective-permute-start.10 = (bf16[384,256]{1,0:T(8,128)(2,1)S(1)}, bf16[384,256]{1,0:T(8,128)(2,1)S(1)}, u32[]{:S(2)}, u32[]{:S(2)}) collective-permute-start(bf16[384,256]{1,0:T(8,128)(2,1)S(1)} %get-tuple-element.58), channel_id=1, source_target_pairs={{0,1},{1,0},{2,3},{3,2},{4,5},{5,4},{6,7},{7,6},{8,9},{9,8},{10,11... | collective-permute-start | bytes 589832 | tf_op jit(solution)/shard_map/ppermute | solution.py:498
  53.6 2.9 %copy-start.11 = (bf16[384,256]{1,0:T(8,128)(2,1)}, bf16[384,256]{1,0:T(8,128)(2,1)S(1)}, u32[]{:S(2)}) copy-start(bf16[384,256]{1,0:T(8,128)(2,1)S(1)} %collective-permute-done.10.got_ref) | copy-start | bytes 589828
  53.6 14.9 %collective-permute-start.11 = (bf16[640,512]{1,0:T(8,128)(2,1)S(1)}, bf16[640,512]{1,0:T(8,128)(2,1)}, u32[]{:S(2)}, u32[]{:S(2)}) collective-permute-start(bf16[640,512]{1,0:T(8,128)(2,1)S(1)} %collective-permute-done.8.refs_1_), channel_id=1, source_target_pairs={{0,4},{1,3},{4,8},{5,1},{8,12},{9,5},{12,14},{13,9},{14,10},{15,13... | collective-permute-start | bytes 1966088 | tf_op jit(solution)/shard_map/ppermute | solution.py:450
  54.6 17.1 %collective-permute-start.12 = (bf16[640,512]{1,0:T(8,128)(2,1)}, bf16[640,512]{1,0:T(8,128)(2,1)}, u32[]{:S(2)}, u32[]{:S(2)}) collective-permute-start(bf16[640,512]{1,0:T(8,128)(2,1)} %collective-permute-done.9.refs_3_), channel_id=1, source_target_pairs={{0,2},{1,5},{4,0},{5,9},{8,4},{9,13},{12,8},{13,15},{14,12},{15,11... | collective-permute-start | bytes 1966088 | tf_op jit(solution)/shard_map/ppermute | solution.py:452
  57.2 11.3 %collective-permute-start.13 = (bf16[448,512]{1,0:T(8,128)(2,1)}, bf16[448,512]{1,0:T(8,128)(2,1)S(1)}, u32[]{:S(2)}, u32[]{:S(2)}) collective-permute-start(bf16[448,512]{1,0:T(8,128)(2,1)} %pad_maximum_fusion), channel_id=1, source_target_pairs={{0,16},{16,0},{1,17},{17,1},{2,18},{18,2},{3,19},{19,3},{4,20},{20... | collective-permute-start | bytes 1376264 | tf_op jit(solution)/shard_map/ppermute | solution.py:460
  71.7 9.9 %collective-permute-start.15 = (bf16[640,512]{1,0:T(8,128)(2,1)}, bf16[640,512]{1,0:T(8,128)(2,1)S(1)}, u32[]{:S(2)}, u32[]{:S(2)}) collective-permute-start(bf16[640,512]{1,0:T(8,128)(2,1)} %collective-permute-done.11.refs_1_), channel_id=1, source_target_pairs={{0,4},{1,3},{4,8},{5,1},{8,12},{9,5},{12,14},{13,9},{14,10},{15,13... | collective-permute-start | bytes 1966088 | tf_op jit(solution)/shard_map/ppermute | solution.py:450
  73.7 12.9 %collective-permute-start.17 = (bf16[448,512]{1,0:T(8,128)(2,1)S(1)}, bf16[448,512]{1,0:T(8,128)(2,1)S(1)}, u32[]{:S(2)}, u32[]{:S(2)}) collective-permute-start(bf16[448,512]{1,0:T(8,128)(2,1)S(1)} %pad_maximum_fusion.2), channel_id=1, source_target_pairs={{0,16},{16,0},{1,17},{17,1},{2,18},{18,2},{3,19},{19,3},{4,20},{20... | collective-permute-start | bytes 1376264 | tf_op jit(solution)/shard_map/ppermute | solution.py:460
  81.7 9.3 %collective-permute-start.16 = (bf16[224,512]{1,0:T(8,128)(2,1)S(1)}, bf16[224,512]{1,0:T(8,128)(2,1)S(1)}, u32[]{:S(2)}, u32[]{:S(2)}) collective-permute-start(bf16[224,512]{1,0:T(8,128)(2,1)S(1)} %constant_dynamic-slice_fusion.2), channel_id=1, source_target_pairs={{0,16},{16,0},{1,17},{17,1},{2,18},{18,2},{3,19},{19,3},{4,20},{20... | collective-permute-start | bytes 688136 | tf_op jit(solution)/shard_map/ppermute | solution.py:460
  91.0 4.7 %copy-start.8 = (s32[512]{0:T(512)S(1)}, s32[512]{0:T(512)}, u32[]{:S(2)}) copy-start(s32[512]{0:T(512)} %param.27) | copy-start | bytes 6148
  91.0 4.7 %copy-start.10 = (s32[512]{0:T(512)S(1)}, s32[512]{0:T(512)}, u32[]{:S(2)}) copy-start(s32[512]{0:T(512)} %param.28) | copy-start | bytes 6148
  91.0 6.2 %copy-start.1 = (bf16[512,512]{1,0:T(8,128)(2,1)S(1)}, bf16[512,512]{1,0:T(8,128)(2,1)}, u32[]{:S(2)}) copy-start(bf16[512,512]{1,0:T(8,128)(2,1)} %features_ref.3) | copy-start | bytes 1572868
  91.0 6.2 %copy-start.2 = (bf16[512,512]{1,0:T(8,128)(2,1)S(1)}, bf16[512,512]{1,0:T(8,128)(2,1)}, u32[]{:S(2)}) copy-start(bf16[512,512]{1,0:T(8,128)(2,1)} %weight_ref.1) | copy-start | bytes 1572868
  91.1 6.2 %copy-start.3 = (f32[512]{0:T(512)S(1)}, f32[512]{0:T(512)}, u32[]{:S(2)}) copy-start(f32[512]{0:T(512)} %param.18) | copy-start | bytes 6148
  93.4 3.8 %collective-permute-start.18 = (bf16[512,512]{1,0:T(8,128)(2,1)S(1)}, bf16[512,512]{1,0:T(8,128)(2,1)S(1)}, u32[]{:S(2)}, u32[]{:S(2)}) collective-permute-start(bf16[512,512]{1,0:T(8,128)(2,1)S(1)} %get-tuple-element.80), channel_id=1, source_target_pairs={{0,1},{1,0},{2,3},{3,2},{4,5},{5,4},{6,7},{7,6},{8,9},{9,8},{10,11... | collective-permute-start | bytes 1572872 | tf_op jit(solution)/shard_map/ppermute | solution.py:536
  99.5 6.5 %copy-start.6 = (bf16[512,1536]{1,0:T(8,128)(2,1)S(1)}, bf16[512,1536]{1,0:T(8,128)(2,1)}, u32[]{:S(2)}) copy-start(bf16[512,1536]{1,0:T(8,128)(2,1)} %param.20) | copy-start | bytes 4718596
  99.5 30.3 %all-to-all-start = ((bf16[16,64,512]{2,1,0:T(8,128)(2,1)}), bf16[16,64,512]{2,1,0:T(8,128)(2,1)}, u32[]{:S(2)}, u32[]{:S(2)}) async-start(bf16[16,64,512]{2,1,0:T(8,128)(2,1)} %bitcast.12), calls=%async_computation | async-start | bytes 2097152 | tf_op jit(solution)/shard_map/all_to_all | solution.py:552
  105.1 2.0 %copy-start.9 = (s32[512]{0:T(512)}, s32[512]{0:T(512)S(1)}, u32[]{:S(2)}) copy-start(s32[512]{0:T(512)S(1)} %multiply_add_fusion) | copy-start | bytes 6148
  151.4 29.8 %all-to-all-start.1 = ((bf16[16,64,512]{2,1,0:T(8,128)(2,1)}), bf16[16,64,512]{2,1,0:T(8,128)(2,1)S(1)}, u32[]{:S(2)}, u32[]{:S(2)}) async-start(bf16[16,64,512]{2,1,0:T(8,128)(2,1)} %bitcast.32), calls=%async_computation.1 | async-start | bytes 2097152 | tf_op jit(solution)/shard_map/all_to_all | solution.py:585

commit v15 on v14

--- a/solution.py
+++ b/solution.py
@@ -43,6 +43,22 @@
         cost_estimate=pl.CostEstimate(flops=flops, bytes_accessed=moved, transcendentals=0),
         **extra,
     )
+
+
+def rows_kernel(flags_ref, units_ref, got_ref, mine_ref, begun_ref):
+    count, unit, _ = units_ref.shape
+    missing = mine_ref.shape[0] - begun_ref.shape[0]
+    kept = [units_ref.at[at] for at in range(0, count, 2)]
+    got = [got_ref.at[at] for at in range(count // 2)]
+    for core, order in enumerate((kept + got, got + kept)):
+
+        @pl.when(flags_ref[0] == core)
+        def _():
+            for at, source in enumerate(order):
+                mine_ref[at * unit : (at + 1) * unit] = source[...]
+
+    start = pl.multiple_of(flags_ref[1] * missing, 16)
+    begun_ref[...] = mine_ref[pl.ds(start, begun_ref.shape[0])]
 
 
 def faces_kernel(unit, core_ref, features_ref, rows_ref, own_ref, other_ref, *face_refs):
@@ -65,41 +81,54 @@
         taken += ref.shape[0]
 
 
-def received_kernel(flags_ref, side_ref, behind_ref, ahead_ref, own_ref, other_ref):
+def table_kernel(
+    flags_ref, own_rows, other_rows, side_ref, behind_ref, ahead_ref, own_ref, other_ref
+):
     size = behind_ref.shape[0] // 2
-    half = own_ref.shape[1]
+    points, half = own_rows.shape
     lower, even = flags_ref[0] == 1, flags_ref[1] == 0
+    own_ref[:points] = own_rows[...]
+    other_ref[:points] = other_rows[...]
     across = [ahead_ref[size:], side_ref[size : 2 * size], behind_ref[size:]]
     along = [ahead_ref[:size], behind_ref[:size]]
     for at, (low, high) in enumerate(zip(across + along, along + across)):
         rows = jnp.where(lower, low, high)
         first, second = rows[:, :half], rows[:, half:]
-        own_ref[at * size : (at + 1) * size] = jnp.where(even, first, second)
-        other_ref[at * size : (at + 1) * size] = jnp.where(even, second, first)
+        start = points + at * size
+        own_ref[start : start + size] = jnp.where(even, first, second)
+        other_ref[start : start + size] = jnp.where(even, second, first)
     rest = jnp.zeros((size, half), BF16)
-    own_ref[5 * size :] = rest
-    other_ref[5 * size :] = rest
-
-
-def gather_kernel(taps, start_ref, rows_ref, own_ref, got_ref, out_ref):
-    half = own_ref.shape[1]
-    lane = lax.broadcasted_iota(jnp.int32, rows_ref.shape, 1)
-    parts = []
-    for table, start in ((own_ref, 0), (got_ref, start_ref[0])):
-        ids = lax.broadcasted_iota(jnp.int32, (1, table.shape[0]), 1) + start
-        parts.append((table, ids.astype(F32)))
+    own_ref[points + 5 * size :] = rest
+    other_ref[points + 5 * size :] = rest
+
+
+def gather_kernel(taps, start_ref, rows_ref, table_ref, out_ref):
+    points, lanes = rows_ref.shape
+    height, half = table_ref.shape
+    lane = lax.broadcasted_iota(jnp.int32, (points, lanes), 1)
+    segments = []
+    for first in range(0, height, 256):
+        start = first if first < points else first - points + start_ref[0]
+        segments.append(
+            (first, min(height, first + 256), jnp.asarray(start, jnp.int32).astype(F32))
+        )
+    places = lax.broadcasted_iota(jnp.int32, (1, 256), 1).astype(F32).astype(BF16)
+    one, zero = jnp.ones((), BF16), jnp.zeros((), BF16)
     for at in range(taps):
         chosen = lane == taps * pl.program_id(0) + at
         column = jnp.sum(jnp.where(chosen, rows_ref[...], 0.0), axis=1, keepdims=True)
-        hits = [one_hot(column == ids) for _, ids in parts]
-        products = [dot(hit, table[...]) for hit, (table, _) in zip(hits, parts)]
-        out_ref[:, at * half : (at + 1) * half] = (products[0] + products[1]).astype(BF16)
-
-
-def gather_block(start, rows, own, got):
+        taken = None
+        for first, end, start in segments:
+            place = jnp.clip(column - start, -1.0, 256.0).astype(BF16)
+            hits = jnp.where(place == places[:, : end - first], one, zero)
+            product = dot(hits, table_ref[first:end])
+            taken = product if taken is None else taken + product
+        out_ref[:, at * half : (at + 1) * half] = taken.astype(BF16)
+
+
+def gather_block(start, rows, table):
     points, lanes = rows.shape
-    half = own.shape[1]
-    height = own.shape[0] + got.shape[0]
+    height, half = table.shape
     taps = 9
     whole = lambda step: (0, 0)
     return call(
@@ -112,11 +141,10 @@
         in_specs=[
             pl.BlockSpec(memory_space=pltpu.SMEM),
             pl.BlockSpec((points, lanes), whole),
-            pl.BlockSpec(own.shape, whole),
-            pl.BlockSpec(got.shape, whole),
+            pl.BlockSpec((height, half), whole),
         ],
         out_specs=pl.BlockSpec((points, taps * half), lambda step: (0, step)),
-    )(start, rows, own, got)
+    )(start, rows, table)
 
 
 def conv_kernel(slots, later, ready, first, places_ref, shifts_ref, *refs):
@@ -404,11 +432,29 @@
 
     unit = conv_weight.shape[0] // TAPS
     units = conv_weight.reshape(TAPS, unit, width)
-    kept, sent = units[0::2], units[1::2]
-    got = lax.ppermute(sent, "blocks", partner)
-    mine = jnp.where(
-        core == 0, jnp.concatenate([kept, got]), jnp.concatenate([got, kept])
-    ).reshape(TAPS * unit, width)
+    got = lax.ppermute(units[1::2], "blocks", partner)
+    rows = TAPS * unit
+    side = lax.axis_index("groups")
+    missing = -(-rows // 64) * 16
+    passed = rows - missing
+    if devices == 2 * GY:
+        mine, begun = call(
+            rows_kernel,
+            [
+                jax.ShapeDtypeStruct((rows, width), BF16),
+                jax.ShapeDtypeStruct((passed, width), BF16),
+            ],
+            24,
+            0,
+            8 * rows * width,
+            in_specs=[pl.BlockSpec(memory_space=pltpu.SMEM)] + [pl.BlockSpec()] * 2,
+        )(jnp.stack([core, side]).astype(jnp.int32), units, got)
+    else:
+        kept = units[0::2]
+        mine = begun = jnp.where(
+            core == 0, jnp.concatenate([kept, got]), jnp.concatenate([got, kept])
+        ).reshape(rows, width)
+
     round_trip = devices == 2 * GY
     lower = index < GY
     if round_trip:
@@ -419,7 +465,7 @@
         face_list = face_rows.reshape(-1, 1)
         counts = (1,) * 8
     size = face_rows.shape[2]
-    own_local, other_half, *faces = call(
+    own_local, other_local, *faces = call(
         functools.partial(faces_kernel, unit),
         [jax.ShapeDtypeStruct((points, half), BF16)] * 2
         + [jax.ShapeDtypeStruct((count * size, width), BF16) for count in counts],
@@ -428,17 +474,9 @@
         8 * points * width,
         in_specs=[pl.BlockSpec(memory_space=pltpu.SMEM)] + [pl.BlockSpec()] * 2,
     )(core.reshape(1), features, face_list)
-    other_local = lax.ppermute(other_half, "blocks", partner)
-    other_neighbours = lax.ppermute(neighbours, "blocks", partner)
-
-    rows = mine.shape[0]
     length = -(-(rows + 127) // 128) * 128 if round_trip else rows * (devices // 2)
     first_pairs, second_pairs, places = way_round(devices, rows, length)
-    side = lax.axis_index("groups")
-    missing = -(-rows // 64) * 16
-    passed = rows - missing
     shifts = jnp.stack([side * missing, (1 - side) * passed]).astype(jnp.int32)
-    begun = lax.dynamic_slice(mine, (side * missing, 0), (passed, width))
     first, second = [begun], [begun]
 
     def pass_on(*beside):
@@ -452,12 +490,16 @@
             second.append(lax.ppermute(second[-1], "blocks", second_pairs))
         return tied[2:]
 
-    def complete(*arrived):
-        lent = [
-            lax.dynamic_slice(piece, (side * (passed - missing), 0), (missing, width))
-            for piece in arrived
-        ]
-        got = lax.ppermute(jnp.concatenate(lent), "groups", [(0, 1), (1, 0)])
+    def lend(*arrived):
+        return jnp.concatenate(
+            [
+                lax.dynamic_slice(piece, (side * (passed - missing), 0), (missing, width))
+                for piece in arrived
+            ]
+        )
+
+    def complete(lent, *arrived):
+        got = lax.ppermute(lent, "groups", [(0, 1), (1, 0)])
         return [
             [(piece, 0, passed, 0), (got, at * missing, missing, 1)]
             for at, piece in enumerate(arrived)
@@ -466,53 +508,65 @@
     if round_trip:
         lists, back_list, on_list = faces
         across = face_pairs(devices, 1, 0) + face_pairs(devices, -1, 0)
-        lists, other_local, other_neighbours = pass_on(lists, other_local, other_neighbours)
+        (lists,) = pass_on(lists)
         lists = lax.ppermute(lists, "blocks", across)
-    own_rows, other_rows = padded_taps(neighbours), padded_taps(other_neighbours)
-    if round_trip:
         to_on = jnp.concatenate([on_list, lists[2 * size :]])
         to_back = jnp.concatenate([back_list, lists[:size]])
         behind = lax.ppermute(to_on, "blocks", face_pairs(devices, 0, 1))
         ahead = lax.ppermute(to_back, "blocks", face_pairs(devices, 0, -1))
-        lists, behind, ahead = pass_on(lists, behind, ahead)
-        near = complete(first[1], second[1])
-        own_remote, other_half = call(
-            received_kernel,
-            [jax.ShapeDtypeStruct((6 * size, half), BF16)] * 2,
+        sent_neighbours, lists, behind, ahead = pass_on(neighbours, lists, behind, ahead)
+        near = complete(lend(first[1], second[1]), first[1], second[1])
+        own_table, other_half = call(
+            table_kernel,
+            [jax.ShapeDtypeStruct((points + 6 * size, half), BF16)] * 2,
             32,
             0,
             20 * size * width,
-            in_specs=[pl.BlockSpec(memory_space=pltpu.SMEM)] + [pl.BlockSpec()] * 3,
-        )(jnp.stack([lower.astype(jnp.int32), core]), lists, behind, ahead)
+            in_specs=[pl.BlockSpec(memory_space=pltpu.SMEM)] + [pl.BlockSpec()] * 5,
+        )(
+            jnp.stack([lower.astype(jnp.int32), core]),
+            own_local,
+            other_local,
+            lists,
+            behind,
+            ahead,
+        )
         start = jnp.where(lower, points, points + 3 * size).reshape(1)
     else:
+        sent_neighbours = neighbours
         received = jnp.concatenate(
             [
                 lax.ppermute(faces[k], "blocks", face_pairs(devices, STEPS_X[k], STEPS_Y[k]))
                 for k in range(8)
             ]
         )
-        own_remote = lax.dynamic_slice(received, (0, core * half), (8 * size, half))
-        other_half = lax.dynamic_slice(received, (0, (1 - core) * half), (8 * size, half))
+        shape = (received.shape[0], half)
+        own_table = jnp.concatenate(
+            [own_local, lax.dynamic_slice(received, (0, core * half), shape)]
+        )
+        other_half = jnp.concatenate(
+            [other_local, lax.dynamic_slice(received, (0, (1 - core) * half), shape)]
+        )
         start = jnp.full((1,), points, jnp.int32)
-    other_remote = lax.ppermute(other_half, "blocks", partner)
-    own_stacked = gather_block(start, own_rows, own_local, own_remote)
-    own_stacked, other_rows, other_remote = pass_on(own_stacked, other_rows, other_remote)
+    other_table = lax.ppermute(other_half, "blocks", partner)
+    other_neighbours = lax.ppermute(sent_neighbours, "blocks", partner)
+    own_stacked = gather_block(start, padded_taps(neighbours), own_table)
+    other_rows = padded_taps(other_neighbours)
+    own_stacked, other_rows, other_table = pass_on(own_stacked, other_rows, other_table)
     if round_trip:
-        middle = complete(first[2], second[2])
-    other_stacked = gather_block(start, other_rows, other_local, other_remote)
-    if round_trip:
-        other_stacked, own_stacked, middle_got = pass_on(other_stacked, own_stacked, middle[0][1][0])
-        middle = [[parts[0], (middle_got, *parts[1][1:])] for parts in middle]
+        middle = complete(lend(first[2], second[2]), first[2], second[2])
+    other_stacked = gather_block(start, other_rows, other_table)
     stacked = other_stacked, own_stacked
     if round_trip:
-        far = complete(first[3], second[3])
-        opposite = complete(first[4])
         places = jnp.array(places, jnp.int32)[index]
         early = [[(mine, 0, rows, None)]] + near
         *sums, middle_lhs, far_lhs, last_lhs = conv_part(
             stacked, places, shifts, early, None, length, (2, 2, 1)
         )
+        *sums, middle_got, lent = pass_on(*sums, middle[0][1][0], lend(first[3], second[3]))
+        middle = [[parts[0], (middle_got, *parts[1][1:])] for parts in middle]
+        far = complete(lent, first[3], second[3])
+        opposite = complete(lend(first[4]), first[4])
         sums = conv_part([middle_lhs], places[3:5], shifts, middle, sums, length)
         sums = conv_part([far_lhs], places[5:7], shifts, far, sums, length)
         for_partner, own_part = conv_part(

time: 184 us -> 199 us (1.082)
  local copies, waits for them, and re-layouts: 13.1 us -> 22.1 us
  waiting for transfers between devices: 65.6 us -> 70.7 us
  Pallas kernels: 65.7 us -> 67.8 us
    ppermute x4, waiting for transfers between devices: 3.78 us -> 12.4 us  [pass_on(): first.append(lax.ppermute(first[-1], 'blocks', first_pairs))]
    unnamed x27 -> x46, local copies, waits for them, and re-layouts: 3.71 us -> 12.2 us
    ppermute x3, waiting for transfers between devices: 3.57 us -> 0.43 us  [pass_on(): second.append(lax.ppermute(second[-1], 'blocks', second_pairs))]
    ppermute x8 -> x7, starting transfers between devices: 5.55 us -> 5.29 us  [the longest x4 3.75 us: complete(): got = lax.ppermute(lent, 'groups', [(0, 1), (1, 0)])]
  transfers between devices with their start and end apart: 21 -> 20, of which waited for: 10 -> 8; matrix products, arithmetic and copies ran while one was open for 9% -> 7% of each run, Pallas kernels for 21% -> 19%
where the time goes in v15:
time: 199 us; the launch traced here: 198 us
  waiting for transfers between devices  70.7 us (36%)
  Pallas kernels  67.8 us (34%)
  starting transfers between devices  31.8 us (16%)
  local copies, waits for them, and re-layouts  22.1 us (11%)
  other arithmetic  5.44 us (3%)
    all_to_all x1, waiting for transfers between devices, body(): lax.all_to_all(back.reshape(devices, capacity, width), 'blocks', split_ax...  24.7 us
    pallas_call x1, Pallas kernels, body(): call(block_kernel, jax.ShapeDtypeStruct((slots, width), BF16), 60, 20 * p...  21.6 us
    all_to_all x1, waiting for transfers between devices, body(): lax.all_to_all(outgoing.reshape(devices, capacity, width), 'blocks', spli...  21.4 us
    pallas_call x2, Pallas kernels, gather_block(): call(functools.partial(gather_kernel, taps), jax.ShapeDtypeStruct((points...  21.2 us
    pallas_call x4, Pallas kernels, conv_part(): call(functools.partial(conv_kernel, slots, later, ready, before is None),...  18.4 us
    ppermute x4, waiting for transfers between devices, pass_on(): first.append(lax.ppermute(first[-1], 'blocks', first_pairs))  12.4 us
    unnamed x46, local copies, waits for them, and re-layouts  12.2 us
    ppermute x1, waiting for transfers between devices, body(): lists = lax.ppermute(lists, 'blocks', across)  7.3 us
  transfers between devices with their start and end apart: 20, of which 8 were waited for; matrix products, arithmetic and copies ran while one was open for 7% of the time, Pallas kernels for 19%

profile of v15, /device:TPU:9, one launch (start us, length us, event | category | flops | bytes accessed | tf_op | source)
XLA Modules:
  0.0 198.3 jit_solution(18183116932958792239)
XLA Ops:
  0.0 1.1 slice.52
  1.1 0.7 collective-permute-start
  1.9 0.8 select_bitcast_fusion
  2.6 0.7 slice_bitcast_fusion
  3.3 0.2 reshape.84.rows_ref
  3.5 1.0 copy-done.11
  4.5 0.7 shard_map.146
  5.3 0.7 constant_dynamic-slice_fusion.7
  6.0 1.5 shard_map.145
  7.5 0.9 copy-done.9
  8.5 2.3 %collective-permute-start.3 = (bf16[192,512]{1,0:T(8,128)(2,1)S(1)}, bf16[192,512]{1,0:T(8,128)(2,1)S(1)}, u32[]{:S(2)}, u32[]{:S(2)}) collective-permute-start(bf16[192,512]{1,0:T(8,128)(2,1)S(1)} %get-tuple-element.49), channel_id=1, source_target_pairs={{0,8},{1,9},{2,10},{3,11},{4,12},{5,13},{6,14},{7,15},{8,0},{9,1},... | collective-permute-start | bytes 589832 | tf_op jit(solution)/shard_map/ppermute | solution.py:512
  10.8 0.2 collective-permute-start.1
  11.0 1.3 collective-permute-start.2
  12.3 7.3 %collective-permute-done.3.side_ref = bf16[192,512]{1,0:T(8,128)(2,1)S(1)} collective-permute-done((bf16[192,512]{1,0:T(8,128)(2,1)S(1)}, bf16[192,512]{1,0:T(8,128)(2,1)S(1)}, u32[]{:S(2)}, u32[]{:S(2)}) %collective-permute-start.3) | collective-permute-done | bytes 196640 | tf_op jit(solution)/shard_map/ppermute | solution.py:512
  19.6 3.5 %collective-permute-start.4 = (bf16[128,512]{1,0:T(8,128)(2,1)S(1)}, bf16[128,512]{1,0:T(8,128)(2,1)S(1)}, u32[]{:S(2)}, u32[]{:S(2)}) collective-permute-start(bf16[128,512]{1,0:T(8,128)(2,1)S(1)} %pad_maximum_fusion.3), channel_id=1, source_target_pairs={{0,1},{1,2},{2,3},{3,4},{4,5},{5,6},{6,7},{8,9},{9,10},{10,11},{11... | collective-permute-start | bytes 393224 | tf_op jit(solution)/shard_map/ppermute | solution.py:515
  23.2 1.9 collective-permute-start.5
  25.5 0.9 copy.35
  26.4 3.3 %collective-permute-done.5.ahead_ref = bf16[128,512]{1,0:T(8,128)(2,1)S(1)} collective-permute-done((bf16[128,512]{1,0:T(8,128)(2,1)S(1)}, bf16[128,512]{1,0:T(8,128)(2,1)S(1)}, u32[]{:S(2)}, u32[]{:S(2)}) %collective-permute-start.5) | collective-permute-done | bytes 131104 | tf_op jit(solution)/shard_map/ppermute | solution.py:516
  29.7 3.6 %collective-permute-done.1.refs_3_ = bf16[640,512]{1,0:T(8,128)(2,1)S(1)} collective-permute-done((bf16[640,512]{1,0:T(8,128)(2,1)}, bf16[640,512]{1,0:T(8,128)(2,1)S(1)}, u32[]{:S(2)}, u32[]{:S(2)}) %collective-permute-start.1) | collective-permute-done | bytes 655392 | tf_op jit(solution)/shard_map/ppermute | solution.py:488
  33.3 0.4 collective-permute-done.2.refs_5_
  33.7 2.1 %collective-permute-start.7 = (bf16[640,512]{1,0:T(8,128)(2,1)S(1)}, bf16[640,512]{1,0:T(8,128)(2,1)}, u32[]{:S(2)}, u32[]{:S(2)}) collective-permute-start(bf16[640,512]{1,0:T(8,128)(2,1)S(1)} %collective-permute-done.2.refs_5_), channel_id=1, source_target_pairs={{0,2},{1,5},{4,0},{5,9},{8,4},{9,13},{12,8},{13,15},{14,12},{15,11... | collective-permute-start | bytes 1966088 | tf_op jit(solution)/shard_map/ppermute | solution.py:490
  35.8 0.8 copy.37
  36.7 0.7 collective-permute-start.8
  37.4 0.6 shard_map.147
  38.2 1.3 collective-permute-start.10
  39.7 1.1 add_convert_fusion.1
  40.8 10.6 %shard_map.148.refs_1_ = bf16[512,6912]{1,0:T(8,128)(2,1)} custom-call(s32[1]{0:T(128)} %bitcast.3.start_ref, f32[512,128]{1,0:T(8,128)} %get-tuple-element.89.rows_ref, bf16[896,256]{1,0:T(8,128)(2,1)} %copy-done.15), custom_call_target="tpu_custom_call" | custom-call | flops 6341787648 | bytes 7077888 | tf_op jit(solution)/shard_map/pallas_call | solution.py:134
  51.4 1.8 collective-permute-start.12
  53.2 1.1 constant_dynamic-slice_fusion.3
  54.3 0.8 pad_maximum_fusion.1
  55.1 0.5 collective-permute-start.13
  55.6 10.6 %shard_map.149.refs_0_ = bf16[512,6912]{1,0:T(8,128)(2,1)} custom-call(s32[1]{0:T(128)} %bitcast.3.start_ref, f32[512,128]{1,0:T(8,128)} %get-tuple-element.62.rows_ref, bf16[896,256]{1,0:T(8,128)(2,1)} %collective-permute-done.9.table_ref), custom_call_target="tpu_custom_call" | custom-call | flops 6341787648 | bytes 7077888 | tf_op jit(solution)/shard_map/pallas_call | solution.py:134
  66.2 1.1 copy-done.8
  67.3 1.2 copy-done.10
  68.5 6.9 %shard_map.150 = (f32[512,512]{1,0:T(8,128)S(1)}, f32[512,512]{1,0:T(8,128)S(1)}, bf16[2,2,512,1024]{3,2,1,0:T(8,128)(2,1)S(1)}, bf16[2,2,512,1024]{3,2,1,0:T(8,128)(2,1)S(1)}, bf16[1,2,512,1024]{3,2,1,0:T(8,128)(2,1)S(1)}) custom-call(s32[16]{0:T(128)S(1)} %reshape_squeeze.3.places_ref, s32[2]{0:T(128)S(1)} %pad_add_fusion.1.shifts_ref, ...), custom_call_target="tpu_custom_call" | custom-call | flops 3221225472 | bytes 9437184 | tf_op jit(solution)/shard_map/pallas_call | solution.py:225
  75.4 2.0 copy-done
  77.4 2.0 %copy-done.2 = bf16[2,2,512,1024]{3,2,1,0:T(8,128)(2,1)} copy-done((bf16[2,2,512,1024]{3,2,1,0:T(8,128)(2,1)}, bf16[2,2,512,1024]{3,2,1,0:T(8,128)(2,1)S(1)}, u32[]{:S(2)}) %copy-start.2) | copy-done | bytes 4194328
  79.4 1.3 copy-done.4
  80.7 1.0 constant_dynamic-slice_fusion.1
  81.7 1.0 constant_dynamic-slice_fusion.2
  82.6 0.8 pad_maximum_fusion.2
  83.6 1.0 collective-permute-start.16
  84.6 8.8 %collective-permute-done.14.refs_1_ = bf16[640,512]{1,0:T(8,128)(2,1)S(1)} collective-permute-done((bf16[640,512]{1,0:T(8,128)(2,1)}, bf16[640,512]{1,0:T(8,128)(2,1)S(1)}, u32[]{:S(2)}, u32[]{:S(2)}) %collective-permute-start.14) | collective-permute-done | bytes 655392 | tf_op jit(solution)/shard_map/ppermute | solution.py:488
  93.4 1.0 collective-permute-start.15
  94.4 2.2 %copy-done.3 = bf16[2,2,512,1024]{3,2,1,0:T(8,128)(2,1)S(1)} copy-done((bf16[2,2,512,1024]{3,2,1,0:T(8,128)(2,1)S(1)}, bf16[2,2,512,1024]{3,2,1,0:T(8,128)(2,1)}, u32[]{:S(2)}) %copy-start.3) | copy-done | bytes 4194328
  96.6 4.7 %shard_map.151 = (f32[512,512]{1,0:T(8,128)S(1)}, f32[512,512]{1,0:T(8,128)S(1)}) custom-call(s32[4]{0:T(128)S(1)} %reshape.71.places_ref, s32[2]{0:T(128)S(1)} %pad_add_fusion.1.shifts_ref, bf16[2,2,512,1024]{3,2,1,0:T(8,128)(2,1)S(1)} %copy-done.3, bf16[640,512]{1,0:T(8,128)(2,1)} %collective-permute-done.6.refs_1_, ...), custom_call_target="tpu_custom_call", output_to_operand_aliasing={{0}: (7, {}), {1}: (8, {})} | custom-call | flops 2147483648 | bytes 6291456 | tf_op jit(solution)/shard_map/pallas_call | solution.py:225
  101.3 4.4 %shard_map.152 = (f32[512,512]{1,0:T(8,128)S(1)}, f32[512,512]{1,0:T(8,128)S(1)}) custom-call(s32[4]{0:T(128)S(1)} %reshape.70.places_ref, s32[2]{0:T(128)S(1)} %pad_add_fusion.1.shifts_ref, bf16[2,2,512,1024]{3,2,1,0:T(8,128)(2,1)S(1)} %copy-done.1, bf16[640,512]{1,0:T(8,128)(2,1)} %collective-permute-done.11.refs_1_, ...), custom_call_target="tpu_custom_call", output_to_operand_aliasing={{0}: (7, {}), {1}: (8, {})} | custom-call | flops 2147483648 | bytes 6291456 | tf_op jit(solution)/shard_map/pallas_call | solution.py:225
  105.8 2.4 %shard_map.153 = (bf16[512,512]{1,0:T(8,128)(2,1)S(1)}, f32[512,512]{1,0:T(8,128)S(1)}) custom-call(s32[2]{0:T(128)S(1)} %slice_bitcast_fusion.1.places_ref, s32[2]{0:T(128)S(1)} %pad_add_fusion.1.shifts_ref, bf16[1,2,512,1024]{3,2,1,0:T(8,128)(2,1)S(1)} %copy-done.5, ...), custom_call_target="tpu_custom_call", output_to_operand_aliasing={{1}: (6, {})} | custom-call | flops 1073741824 | bytes 3145728 | tf_op jit(solution)/shard_map/pallas_call | solution.py:225
  108.2 2.4 %collective-permute-start.17 = (bf16[512,512]{1,0:T(8,128)(2,1)S(1)}, bf16[512,512]{1,0:T(8,128)(2,1)S(1)}, u32[]{:S(2)}, u32[]{:S(2)}) collective-permute-start(bf16[512,512]{1,0:T(8,128)(2,1)S(1)} %get-tuple-element.84), channel_id=1, source_target_pairs={{0,1},{1,0},{2,3},{3,2},{4,5},{5,4},{6,7},{7,6},{8,9},{9,8},{10,11... | collective-permute-start | bytes 1572872 | tf_op jit(solution)/shard_map/ppermute | solution.py:590
  110.7 0.3 convert_reduce_fusion.1
  111.0 1.2 collective-permute-done.17.got_ref
  112.2 2.3 %shard_map.154 = bf16[1024,512]{1,0:T(8,128)(2,1)} custom-call(f32[512,512]{1,0:T(8,128)S(1)} %get-tuple-element.83.own_ref, bf16[512,512]{1,0:T(8,128)(2,1)S(1)} %collective-permute-done.17.got_ref, bf16[512,512]{1,0:T(8,128)(2,1)S(1)} %copy-done.12, bf16[512,512]{1,0:T(8,128)(2,1)S(1)} %copy-done.13, f32[1,512]{1,0:T(1,128)S(1)} %bitcast.31, ...), custom_call_target="tpu_custom_call" | custom-call | flops 805306368 | bytes 2097152 | tf_op jit(solution)/shard_map/pallas_call | solution.py:592
  114.5 5.9 %all-to-all-start = ((bf16[16,64,512]{2,1,0:T(8,128)(2,1)}), bf16[16,64,512]{2,1,0:T(8,128)(2,1)}, u32[]{:S(2)}, u32[]{:S(2)}) async-start(bf16[16,64,512]{2,1,0:T(8,128)(2,1)} %bitcast.12), calls=%async_computation | async-start | bytes 2097152 | tf_op jit(solution)/shard_map/all_to_all | solution.py:606
  120.4 0.2 convert_reduce_fusion
  120.6 0.8 copy.40.slot_col_ref
  121.5 0.9 fusion.5
  122.4 0.2 copy.43
  122.6 0.2 copy.42
  122.9 1.0 maximum_bitcast_fusion.qv_hbm
  123.9 21.4 %all-to-all-done = bf16[16,64,512]{2,1,0:T(8,128)(2,1)} async-done(((bf16[16,64,512]{2,1,0:T(8,128)(2,1)}), bf16[16,64,512]{2,1,0:T(8,128)(2,1)}, u32[]{:S(2)}, u32[]{:S(2)}) %all-to-all-start) | async-done | bytes 1048608 | tf_op jit(solution)/shard_map/all_to_all | solution.py:606
  145.3 21.6 %shard_map.155 = bf16[1024,512]{1,0:T(8,128)(2,1)} custom-call(bf16[1024,512]{1,0:T(8,128)(2,1)} %bitcast.13.arrived_ref, s32[512,1]{1,0:T(8,128)} %copy.40.slot_col_ref, s32[1,512]{1,0:T(1,128)} %bitcast.34, f32[1,512]{1,0:T(1,128)} %bitcast.35, f32[1,512]{1,0:T(1,128)} %bitcast.36, bf16[1024,512]{1,0:T(8,128)(2,1)} %maximum_bitcast_fusion.qv_hbm, ...), custom_call_target="tpu_custom_call" | custom-call | flops 2684354560 | bytes 4194304 | tf_op jit(solution)/shard_map/pallas_call | solution.py:613
  166.9 5.0 %all-to-all-start.1 = ((bf16[16,64,512]{2,1,0:T(8,128)(2,1)}), bf16[16,64,512]{2,1,0:T(8,128)(2,1)S(1)}, u32[]{:S(2)}, u32[]{:S(2)}) async-start(bf16[16,64,512]{2,1,0:T(8,128)(2,1)} %bitcast.32), calls=%async_computation.1 | async-start | bytes 2097152 | tf_op jit(solution)/shard_map/all_to_all | solution.py:639
  172.1 24.7 %all-to-all-done.1 = bf16[16,64,512]{2,1,0:T(8,128)(2,1)S(1)} async-done(((bf16[16,64,512]{2,1,0:T(8,128)(2,1)}), bf16[16,64,512]{2,1,0:T(8,128)(2,1)S(1)}, u32[]{:S(2)}, u32[]{:S(2)}) %all-to-all-start.1) | async-done | bytes 1048608 | tf_op jit(solution)/shard_map/all_to_all | solution.py:639
  196.8 1.5 shard_map.156
  (77 shorter events, 1.4 us)
Async XLA Ops:
  0.0 6.0 %copy-start.6 = (bf16[864,512]{1,0:T(8,128)(2,1)S(1)}, bf16[864,512]{1,0:T(8,128)(2,1)}, u32[]{:S(2)}) copy-start(bf16[864,512]{1,0:T(8,128)(2,1)} %param.16) | copy-start | bytes 2654212
  0.0 10.8 %copy-start.18 = (s32[512,26]{0,1:T(8,128)S(1)}, s32[512,26]{0,1:T(8,128)}, u32[]{:S(2)}) copy-start(s32[512,26]{0,1:T(8,128)} %param.26) | copy-start | bytes 159748
  1.1 4.9 %collective-permute-start = (bf16[13,32,512]{2,1,0:T(8,128)(2,1)S(1)}, bf16[13,32,512]{2,1,0:T(8,128)(2,1)S(1)}, u32[]{:S(2)}, u32[]{:S(2)}) collective-permute-start(bf16[13,32,512]{2,1,0:T(8,128)(2,1)S(1)} %slice.52), channel_id=1, source_target_pairs={{0,1},{1,0},{2,3},{3,2},{4,5},{5,4},{6,7},{7,6},{8,9},{9,8},{10,11... | collective-permute-start | bytes 1277960 | tf_op jit(solution)/shard_map/ppermute | solution.py:435
  3.5 1.0 copy-start.11
  7.5 0.9 copy-start.9
  8.5 11.1 %collective-permute-start.3 = (bf16[192,512]{1,0:T(8,128)(2,1)S(1)}, bf16[192,512]{1,0:T(8,128)(2,1)S(1)}, u32[]{:S(2)}, u32[]{:S(2)}) collective-permute-start(bf16[192,512]{1,0:T(8,128)(2,1)S(1)} %get-tuple-element.49), channel_id=1, source_target_pairs={{0,8},{1,9},{2,10},{3,11},{4,12},{5,13},{6,14},{7,15},{8,0},{9,1},... | collective-permute-start | bytes 589832 | tf_op jit(solution)/shard_map/ppermute | solution.py:512
  10.8 22.5 %collective-permute-start.1 = (bf16[640,512]{1,0:T(8,128)(2,1)}, bf16[640,512]{1,0:T(8,128)(2,1)S(1)}, u32[]{:S(2)}, u32[]{:S(2)}) collective-permute-start(bf16[640,512]{1,0:T(8,128)(2,1)} %get-tuple-element.48), channel_id=1, source_target_pairs={{0,4},{1,3},{4,8},{5,1},{8,12},{9,5},{12,14},{13,9},{14,10},{15,13... | collective-permute-start | bytes 1966088 | tf_op jit(solution)/shard_map/ppermute | solution.py:488
  11.0 22.7 %collective-permute-start.2 = (bf16[640,512]{1,0:T(8,128)(2,1)}, bf16[640,512]{1,0:T(8,128)(2,1)S(1)}, u32[]{:S(2)}, u32[]{:S(2)}) collective-permute-start(bf16[640,512]{1,0:T(8,128)(2,1)} %get-tuple-element.48), channel_id=1, source_target_pairs={{0,2},{1,5},{4,0},{5,9},{8,4},{9,13},{12,8},{13,15},{14,12},{15,11... | collective-permute-start | bytes 1966088 | tf_op jit(solution)/shard_map/ppermute | solution.py:490
  19.6 6.8 %collective-permute-start.4 = (bf16[128,512]{1,0:T(8,128)(2,1)S(1)}, bf16[128,512]{1,0:T(8,128)(2,1)S(1)}, u32[]{:S(2)}, u32[]{:S(2)}) collective-permute-start(bf16[128,512]{1,0:T(8,128)(2,1)S(1)} %pad_maximum_fusion.3), channel_id=1, source_target_pairs={{0,1},{1,2},{2,3},{3,4},{4,5},{5,6},{6,7},{8,9},{9,10},{10,11},{11... | collective-permute-start | bytes 393224 | tf_op jit(solution)/shard_map/ppermute | solution.py:515
  23.2 6.6 %collective-permute-start.5 = (bf16[128,512]{1,0:T(8,128)(2,1)S(1)}, bf16[128,512]{1,0:T(8,128)(2,1)S(1)}, u32[]{:S(2)}, u32[]{:S(2)}) collective-permute-start(bf16[128,512]{1,0:T(8,128)(2,1)S(1)} %pad_maximum_fusion.4), channel_id=1, source_target_pairs={{1,0},{2,1},{3,2},{4,3},{5,4},{6,5},{7,6},{9,8},{10,9},{11,10},{12... | collective-permute-start | bytes 393224 | tf_op jit(solution)/shard_map/ppermute | solution.py:516
  33.7 5.9 %copy-start.7 = (bf16[640,512]{1,0:T(8,128)(2,1)}, bf16[640,512]{1,0:T(8,128)(2,1)S(1)}, u32[]{:S(2)}) copy-start(bf16[640,512]{1,0:T(8,128)(2,1)S(1)} %collective-permute-done.2.refs_5_) | copy-start | bytes 1966084
  33.7 17.6 %collective-permute-start.6 = (bf16[640,512]{1,0:T(8,128)(2,1)S(1)}, bf16[640,512]{1,0:T(8,128)(2,1)}, u32[]{:S(2)}, u32[]{:S(2)}) collective-permute-start(bf16[640,512]{1,0:T(8,128)(2,1)S(1)} %collective-permute-done.1.refs_3_), channel_id=1, source_target_pairs={{0,4},{1,3},{4,8},{5,1},{8,12},{9,5},{12,14},{13,9},{14,10},{15,13... | collective-permute-start | bytes 1966088 | tf_op jit(solution)/shard_map/ppermute | solution.py:488
  33.7 17.6 %collective-permute-start.7 = (bf16[640,512]{1,0:T(8,128)(2,1)S(1)}, bf16[640,512]{1,0:T(8,128)(2,1)}, u32[]{:S(2)}, u32[]{:S(2)}) collective-permute-start(bf16[640,512]{1,0:T(8,128)(2,1)S(1)} %collective-permute-done.2.refs_5_), channel_id=1, source_target_pairs={{0,2},{1,5},{4,0},{5,9},{8,4},{9,13},{12,8},{13,15},{14,12},{15,11... | collective-permute-start | bytes 1966088 | tf_op jit(solution)/shard_map/ppermute | solution.py:490
  36.7 3.0 %copy-start.17 = (s32[512,13]{1,0:T(8,128)S(1)}, s32[512,13]{1,0:T(8,128)}, u32[]{:S(2)}) copy-start(s32[512,13]{1,0:T(8,128)} %copy.35) | copy-start | bytes 79876
  36.7 2.8 %collective-permute-start.8 = (s32[512,26]{1,0:T(8,128)}, s32[512,26]{1,0:T(8,128)S(1)}, u32[]{:S(2)}, u32[]{:S(2)}) collective-permute-start(s32[512,26]{1,0:T(8,128)} %copy.37), channel_id=1, source_target_pairs={{0,1},{1,0},{2,3},{3,2},{4,5},{5,4},{6,7},{7,6},{8,9},{9,8},{10,11... | collective-permute-start | bytes 159752 | tf_op jit(solution)/shard_map/ppermute | solution.py:552
  38.0 2.7 %copy-start.15 = (bf16[896,256]{1,0:T(8,128)(2,1)}, bf16[896,256]{1,0:T(8,128)(2,1)S(1)}, u32[]{:S(2)}) copy-start(bf16[896,256]{1,0:T(8,128)(2,1)S(1)} %get-tuple-element.59.table_ref) | copy-start | bytes 1376260
  38.0 13.3 %collective-permute-start.9 = (bf16[896,256]{1,0:T(8,128)(2,1)S(1)}, bf16[896,256]{1,0:T(8,128)(2,1)}, u32[]{:S(2)}, u32[]{:S(2)}) collective-permute-start(bf16[896,256]{1,0:T(8,128)(2,1)S(1)} %get-tuple-element.61), channel_id=1, source_target_pairs={{0,1},{1,0},{2,3},{3,2},{4,5},{5,4},{6,7},{7,6},{8,9},{9,8},{10,11... | collective-permute-start | bytes 1376264 | tf_op jit(solution)/shard_map/ppermute | solution.py:551
  38.2 28.0 %collective-permute-start.10 = (bf16[448,512]{1,0:T(8,128)(2,1)S(1)}, bf16[448,512]{1,0:T(8,128)(2,1)S(1)}, u32[]{:S(2)}, u32[]{:S(2)}) collective-permute-start(bf16[448,512]{1,0:T(8,128)(2,1)S(1)} %pad_maximum_fusion), channel_id=1, source_target_pairs={{0,16},{16,0},{1,17},{17,1},{2,18},{18,2},{3,19},{19,3},{4,20},{20... | collective-permute-start | bytes 1376264 | tf_op jit(solution)/shard_map/ppermute | solution.py:502
  51.4 30.3 %collective-permute-start.11 = (bf16[640,512]{1,0:T(8,128)(2,1)}, bf16[640,512]{1,0:T(8,128)(2,1)}, u32[]{:S(2)}, u32[]{:S(2)}) collective-permute-start(bf16[640,512]{1,0:T(8,128)(2,1)} %collective-permute-done.6.refs_1_), channel_id=1, source_target_pairs={{0,4},{1,3},{4,8},{5,1},{8,12},{9,5},{12,14},{13,9},{14,10},{15,13... | collective-permute-start | bytes 1966088 | tf_op jit(solution)/shard_map/ppermute | solution.py:488
  51.4 29.3 %collective-permute-start.12 = (bf16[640,512]{1,0:T(8,128)(2,1)}, bf16[640,512]{1,0:T(8,128)(2,1)}, u32[]{:S(2)}, u32[]{:S(2)}) collective-permute-start(bf16[640,512]{1,0:T(8,128)(2,1)} %collective-permute-done.7.refs_3_), channel_id=1, source_target_pairs={{0,2},{1,5},{4,0},{5,9},{8,4},{9,13},{12,8},{13,15},{14,12},{15,11... | collective-permute-start | bytes 1966088 | tf_op jit(solution)/shard_map/ppermute | solution.py:490
  55.1 28.3 %collective-permute-start.13 = (bf16[448,512]{1,0:T(8,128)(2,1)}, bf16[448,512]{1,0:T(8,128)(2,1)S(1)}, u32[]{:S(2)}, u32[]{:S(2)}) collective-permute-start(bf16[448,512]{1,0:T(8,128)(2,1)} %pad_maximum_fusion.1), channel_id=1, source_target_pairs={{0,16},{16,0},{1,17},{17,1},{2,18},{18,2},{3,19},{19,3},{4,20},{20... | collective-permute-start | bytes 1376264 | tf_op jit(solution)/shard_map/ppermute | solution.py:502
  66.2 1.1 copy-start.8
  67.3 1.2 copy-start.10
  75.4 2.0 %copy-start = (bf16[2,2,512,1024]{3,2,1,0:T(8,128)(2,1)}, bf16[2,2,512,1024]{3,2,1,0:T(8,128)(2,1)S(1)}, u32[]{:S(2)}) copy-start(bf16[2,2,512,1024]{3,2,1,0:T(8,128)(2,1)S(1)} %get-tuple-element.72.refs_0_) | copy-start | bytes 12582916
  77.4 2.0 %copy-start.2 = (bf16[2,2,512,1024]{3,2,1,0:T(8,128)(2,1)}, bf16[2,2,512,1024]{3,2,1,0:T(8,128)(2,1)S(1)}, u32[]{:S(2)}) copy-start(bf16[2,2,512,1024]{3,2,1,0:T(8,128)(2,1)S(1)} %get-tuple-element.75.refs_0_) | copy-start | bytes 12582916
  79.4 1.3 copy-start.4
  83.4 9.9 %collective-permute-start.14 = (bf16[640,512]{1,0:T(8,128)(2,1)}, bf16[640,512]{1,0:T(8,128)(2,1)S(1)}, u32[]{:S(2)}, u32[]{:S(2)}) collective-permute-start(bf16[640,512]{1,0:T(8,128)(2,1)} %collective-permute-done.11.refs_1_), channel_id=1, source_target_pairs={{0,4},{1,3},{4,8},{5,1},{8,12},{9,5},{12,14},{13,9},{14,10},{15,13... | collective-permute-start | bytes 1966088 | tf_op jit(solution)/shard_map/ppermute | solution.py:488
  83.6 17.7 %collective-permute-start.16 = (bf16[448,512]{1,0:T(8,128)(2,1)}, bf16[448,512]{1,0:T(8,128)(2,1)S(1)}, u32[]{:S(2)}, u32[]{:S(2)}) collective-permute-start(bf16[448,512]{1,0:T(8,128)(2,1)} %pad_maximum_fusion.2), channel_id=1, source_target_pairs={{0,16},{16,0},{1,17},{17,1},{2,18},{18,2},{3,19},{19,3},{4,20},{20... | collective-permute-start | bytes 1376264 | tf_op jit(solution)/shard_map/ppermute | solution.py:502
  93.4 12.3 %collective-permute-start.15 = (bf16[224,512]{1,0:T(8,128)(2,1)S(1)}, bf16[224,512]{1,0:T(8,128)(2,1)S(1)}, u32[]{:S(2)}, u32[]{:S(2)}) collective-permute-start(bf16[224,512]{1,0:T(8,128)(2,1)S(1)} %constant_dynamic-slice_fusion), channel_id=1, source_target_pairs={{0,16},{16,0},{1,17},{17,1},{2,18},{18,2},{3,19},{19,3},{4,20},{20... | collective-permute-start | bytes 688136 | tf_op jit(solution)/shard_map/ppermute | solution.py:502
  94.4 2.2 %copy-start.3 = (bf16[2,2,512,1024]{3,2,1,0:T(8,128)(2,1)S(1)}, bf16[2,2,512,1024]{3,2,1,0:T(8,128)(2,1)}, u32[]{:S(2)}) copy-start(bf16[2,2,512,1024]{3,2,1,0:T(8,128)(2,1)} %copy-done.2) | copy-start | bytes 12582916
  96.6 4.7 %copy-start.1 = (bf16[2,2,512,1024]{3,2,1,0:T(8,128)(2,1)S(1)}, bf16[2,2,512,1024]{3,2,1,0:T(8,128)(2,1)}, u32[]{:S(2)}) copy-start(bf16[2,2,512,1024]{3,2,1,0:T(8,128)(2,1)} %copy-done) | copy-start | bytes 12582916
  101.3 4.4 %copy-start.5 = (bf16[1,2,512,1024]{3,2,1,0:T(8,128)(2,1)S(1)}, bf16[1,2,512,1024]{3,2,1,0:T(8,128)(2,1)}, u32[]{:S(2)}) copy-start(bf16[1,2,512,1024]{3,2,1,0:T(8,128)(2,1)} %copy-done.4) | copy-start | bytes 6291460
  105.8 4.9 %copy-start.19 = (s32[512]{0:T(512)S(1)}, s32[512]{0:T(512)}, u32[]{:S(2)}) copy-start(s32[512]{0:T(512)} %param.27) | copy-start | bytes 6148
  105.8 4.9 %copy-start.21 = (s32[512]{0:T(512)S(1)}, s32[512]{0:T(512)}, u32[]{:S(2)}) copy-start(s32[512]{0:T(512)} %param.28) | copy-start | bytes 6148
  105.8 6.4 %copy-start.12 = (bf16[512,512]{1,0:T(8,128)(2,1)S(1)}, bf16[512,512]{1,0:T(8,128)(2,1)}, u32[]{:S(2)}) copy-start(bf16[512,512]{1,0:T(8,128)(2,1)} %features_ref.3) | copy-start | bytes 1572868
  105.8 6.4 %copy-start.13 = (bf16[512,512]{1,0:T(8,128)(2,1)S(1)}, bf16[512,512]{1,0:T(8,128)(2,1)}, u32[]{:S(2)}) copy-start(bf16[512,512]{1,0:T(8,128)(2,1)} %weight_ref.1) | copy-start | bytes 1572868
  105.8 6.4 %copy-start.14 = (f32[512]{0:T(512)S(1)}, f32[512]{0:T(512)}, u32[]{:S(2)}) copy-start(f32[512]{0:T(512)} %param.18) | copy-start | bytes 6148
  108.2 4.0 %collective-permute-start.17 = (bf16[512,512]{1,0:T(8,128)(2,1)S(1)}, bf16[512,512]{1,0:T(8,128)(2,1)S(1)}, u32[]{:S(2)}, u32[]{:S(2)}) collective-permute-start(bf16[512,512]{1,0:T(8,128)(2,1)S(1)} %get-tuple-element.84), channel_id=1, source_target_pairs={{0,1},{1,0},{2,3},{3,2},{4,5},{5,4},{6,7},{7,6},{8,9},{9,8},{10,11... | collective-permute-start | bytes 1572872 | tf_op jit(solution)/shard_map/ppermute | solution.py:590
  114.5 7.0 %copy-start.16 = (bf16[512,1536]{1,0:T(8,128)(2,1)S(1)}, bf16[512,1536]{1,0:T(8,128)(2,1)}, u32[]{:S(2)}) copy-start(bf16[512,1536]{1,0:T(8,128)(2,1)} %param.20) | copy-start | bytes 4718596
  114.5 30.8 %all-to-all-start = ((bf16[16,64,512]{2,1,0:T(8,128)(2,1)}), bf16[16,64,512]{2,1,0:T(8,128)(2,1)}, u32[]{:S(2)}, u32[]{:S(2)}) async-start(bf16[16,64,512]{2,1,0:T(8,128)(2,1)} %bitcast.12), calls=%async_computation | async-start | bytes 2097152 | tf_op jit(solution)/shard_map/all_to_all | solution.py:606
  120.6 2.0 %copy-start.20 = (s32[512]{0:T(512)}, s32[512]{0:T(512)S(1)}, u32[]{:S(2)}) copy-start(s32[512]{0:T(512)S(1)} %multiply_add_fusion) | copy-start | bytes 6148
  166.9 29.8 %all-to-all-start.1 = ((bf16[16,64,512]{2,1,0:T(8,128)(2,1)}), bf16[16,64,512]{2,1,0:T(8,128)(2,1)S(1)}, u32[]{:S(2)}, u32[]{:S(2)}) async-start(bf16[16,64,512]{2,1,0:T(8,128)(2,1)} %bitcast.32), calls=%async_computation.1 | async-start | bytes 2097152 | tf_op jit(solution)/shard_map/all_to_all | solution.py:639

commit v16 on v15

--- a/solution.py
+++ b/solution.py
@@ -558,13 +558,15 @@
     other_stacked = gather_block(start, other_rows, other_table)
     stacked = other_stacked, own_stacked
     if round_trip:
+        *stacked, middle_got, lent = pass_on(
+            *stacked, middle[0][1][0], lend(first[3], second[3])
+        )
+        middle = [[parts[0], (middle_got, *parts[1][1:])] for parts in middle]
         places = jnp.array(places, jnp.int32)[index]
         early = [[(mine, 0, rows, None)]] + near
         *sums, middle_lhs, far_lhs, last_lhs = conv_part(
             stacked, places, shifts, early, None, length, (2, 2, 1)
         )
-        *sums, middle_got, lent = pass_on(*sums, middle[0][1][0], lend(first[3], second[3]))
-        middle = [[parts[0], (middle_got, *parts[1][1:])] for parts in middle]
         far = complete(lent, first[3], second[3])
         opposite = complete(lend(first[4]), first[4])
         sums = conv_part([middle_lhs], places[3:5], shifts, middle, sums, length)

time: 199 us -> 186 us (0.935)
  local copies, waits for them, and re-layouts: 22.1 us -> 14.7 us
  waiting for transfers between devices: 70.7 us -> 64.4 us
    unnamed x46 -> x30, local copies, waits for them, and re-layouts: 12.2 us -> 3.61 us
    ppermute x4, waiting for transfers between devices: 12.4 us -> 5.76 us  [pass_on(): first.append(lax.ppermute(first[-1], 'blocks', first_pairs))]
  transfers between devices with their start and end apart: 20 -> 20, of which waited for: 8 -> 9; matrix products, arithmetic and copies ran while one was open for 7% -> 8% of each run, Pallas kernels for 19% -> 21%
where the time goes in v16:
time: 186 us; the launch traced here: 185 us
  Pallas kernels  67.2 us (36%)
  waiting for transfers between devices  64.4 us (35%)
  starting transfers between devices  32.6 us (18%)
  local copies, waits for them, and re-layouts  14.7 us (8%)
  other arithmetic  6.06 us (3%)
    all_to_all x1, waiting for transfers between devices, body(): lax.all_to_all(back.reshape(devices, capacity, width), 'blocks', split_ax...  24.7 us
    pallas_call x1, Pallas kernels, body(): call(block_kernel, jax.ShapeDtypeStruct((slots, width), BF16), 60, 20 * p...  21.6 us
    all_to_all x1, waiting for transfers between devices, body(): lax.all_to_all(outgoing.reshape(devices, capacity, width), 'blocks', spli...  21.4 us
    pallas_call x2, Pallas kernels, gather_block(): call(functools.partial(gather_kernel, taps), jax.ShapeDtypeStruct((points...  21.3 us
    pallas_call x4, Pallas kernels, conv_part(): call(functools.partial(conv_kernel, slots, later, ready, before is None),...  18.5 us
    ppermute x1, waiting for transfers between devices, body(): lists = lax.ppermute(lists, 'blocks', across)  7.29 us
    ppermute x4, waiting for transfers between devices, pass_on(): first.append(lax.ppermute(first[-1], 'blocks', first_pairs))  5.76 us
    ppermute x3, starting transfers between devices, pass_on(): second.append(lax.ppermute(second[-1], 'blocks', second_pairs))  5.54 us
  transfers between devices with their start and end apart: 20, of which 9 were waited for; matrix products, arithmetic and copies ran while one was open for 8% of the time, Pallas kernels for 21%

profile of v16, /device:TPU:9, one launch (start us, length us, event | category | flops | bytes accessed | tf_op | source)
XLA Modules:
  0.0 185.3 jit_solution(13620479183559513028)
XLA Ops:
  0.0 1.1 slice.52
  1.1 0.7 collective-permute-start
  1.9 0.8 select_bitcast_fusion
  2.6 0.7 slice_bitcast_fusion
  3.3 0.2 reshape.84.rows_ref
  3.5 1.0 copy-done.3
  4.5 0.7 shard_map.146
  5.3 0.7 shard_map.145
  6.0 0.9 copy-done.1
  6.9 2.3 %collective-permute-start.3 = (bf16[192,512]{1,0:T(8,128)(2,1)S(1)}, bf16[192,512]{1,0:T(8,128)(2,1)S(1)}, u32[]{:S(2)}, u32[]{:S(2)}) collective-permute-start(bf16[192,512]{1,0:T(8,128)(2,1)S(1)} %get-tuple-element.49), channel_id=1, source_target_pairs={{0,8},{1,9},{2,10},{3,11},{4,12},{5,13},{6,14},{7,15},{8,0},{9,1},... | collective-permute-start | bytes 589832 | tf_op jit(solution)/shard_map/ppermute | solution.py:512
  9.3 0.2 collective-permute-start.1
  9.5 1.3 collective-permute-start.2
  10.8 7.3 %collective-permute-done.3.side_ref = bf16[192,512]{1,0:T(8,128)(2,1)S(1)} collective-permute-done((bf16[192,512]{1,0:T(8,128)(2,1)S(1)}, bf16[192,512]{1,0:T(8,128)(2,1)S(1)}, u32[]{:S(2)}, u32[]{:S(2)}) %collective-permute-start.3) | collective-permute-done | bytes 196640 | tf_op jit(solution)/shard_map/ppermute | solution.py:512
  18.1 3.5 %collective-permute-start.4 = (bf16[128,512]{1,0:T(8,128)(2,1)S(1)}, bf16[128,512]{1,0:T(8,128)(2,1)S(1)}, u32[]{:S(2)}, u32[]{:S(2)}) collective-permute-start(bf16[128,512]{1,0:T(8,128)(2,1)S(1)} %pad_maximum_fusion.3), channel_id=1, source_target_pairs={{0,1},{1,2},{2,3},{3,4},{4,5},{5,6},{6,7},{8,9},{9,10},{10,11},{11... | collective-permute-start | bytes 393224 | tf_op jit(solution)/shard_map/ppermute | solution.py:515
  21.6 0.7 pad_maximum_fusion.4
  22.3 1.9 %collective-permute-start.5 = (bf16[128,512]{1,0:T(8,128)(2,1)}, bf16[128,512]{1,0:T(8,128)(2,1)S(1)}, u32[]{:S(2)}, u32[]{:S(2)}) collective-permute-start(bf16[128,512]{1,0:T(8,128)(2,1)} %pad_maximum_fusion.4), channel_id=1, source_target_pairs={{1,0},{2,1},{3,2},{4,3},{5,4},{6,5},{7,6},{9,8},{10,9},{11,10},{12... | collective-permute-start | bytes 393224 | tf_op jit(solution)/shard_map/ppermute | solution.py:516
  24.4 0.9 copy.36
  25.4 0.7 constant_dynamic-slice_fusion.7
  26.1 3.0 %collective-permute-done.5.ahead_ref = bf16[128,512]{1,0:T(8,128)(2,1)S(1)} collective-permute-done((bf16[128,512]{1,0:T(8,128)(2,1)}, bf16[128,512]{1,0:T(8,128)(2,1)S(1)}, u32[]{:S(2)}, u32[]{:S(2)}) %collective-permute-start.5) | collective-permute-done | bytes 131104 | tf_op jit(solution)/shard_map/ppermute | solution.py:516
  29.1 2.7 %collective-permute-done.1.refs_3_ = bf16[640,512]{1,0:T(8,128)(2,1)S(1)} collective-permute-done((bf16[640,512]{1,0:T(8,128)(2,1)S(1)}, bf16[640,512]{1,0:T(8,128)(2,1)S(1)}, u32[]{:S(2)}, u32[]{:S(2)}) %collective-permute-start.1) | collective-permute-done | bytes 655392 | tf_op jit(solution)/shard_map/ppermute | solution.py:488
  31.8 0.3 collective-permute-done.2.refs_5_
  32.1 0.9 copy.37
  33.0 0.5 collective-permute-start.8
  33.4 0.6 shard_map.147
  34.2 2.2 %collective-permute-start.7 = (bf16[640,512]{1,0:T(8,128)(2,1)S(1)}, bf16[640,512]{1,0:T(8,128)(2,1)S(1)}, u32[]{:S(2)}, u32[]{:S(2)}) collective-permute-start(bf16[640,512]{1,0:T(8,128)(2,1)S(1)} %collective-permute-done.2.refs_5_), channel_id=1, source_target_pairs={{0,2},{1,5},{4,0},{5,9},{8,4},{9,13},{12,8},{13,15},{14,12},{15,11... | collective-permute-start | bytes 1966088 | tf_op jit(solution)/shard_map/ppermute | solution.py:490
  36.5 0.8 pad_maximum_fusion.2
  37.3 1.2 collective-permute-start.13
  38.7 1.1 add_convert_fusion.1
  39.7 10.6 %shard_map.148.refs_1_ = bf16[512,6912]{1,0:T(8,128)(2,1)} custom-call(s32[1]{0:T(128)} %bitcast.8.start_ref, f32[512,128]{1,0:T(8,128)} %get-tuple-element.89.rows_ref, bf16[896,256]{1,0:T(8,128)(2,1)} %copy-done.7), custom_call_target="tpu_custom_call" | custom-call | flops 6341787648 | bytes 7077888 | tf_op jit(solution)/shard_map/pallas_call | solution.py:134
  50.4 2.0 %collective-permute-start.11 = (bf16[640,512]{1,0:T(8,128)(2,1)S(1)}, bf16[640,512]{1,0:T(8,128)(2,1)}, u32[]{:S(2)}, u32[]{:S(2)}) collective-permute-start(bf16[640,512]{1,0:T(8,128)(2,1)S(1)} %collective-permute-done.7.refs_3_), channel_id=1, source_target_pairs={{0,2},{1,5},{4,0},{5,9},{8,4},{9,13},{12,8},{13,15},{14,12},{15,11... | collective-permute-start | bytes 1966088 | tf_op jit(solution)/shard_map/ppermute | solution.py:490
  52.5 1.3 collective-permute-start.12
  53.7 10.7 %shard_map.149.refs_0_ = bf16[512,6912]{1,0:T(8,128)(2,1)} custom-call(s32[1]{0:T(128)} %bitcast.8.start_ref, f32[512,128]{1,0:T(8,128)} %get-tuple-element.64.rows_ref, bf16[896,256]{1,0:T(8,128)(2,1)} %collective-permute-done.9.table_ref), custom_call_target="tpu_custom_call" | custom-call | flops 6341787648 | bytes 7077888 | tf_op jit(solution)/shard_map/pallas_call | solution.py:134
  64.4 0.7 collective-permute-done.11.refs_3_
  65.1 1.0 constant_dynamic-slice_fusion.3
  66.1 3.0 %collective-permute-done.10.refs_1_ = bf16[640,512]{1,0:T(8,128)(2,1)} collective-permute-done((bf16[640,512]{1,0:T(8,128)(2,1)S(1)}, bf16[640,512]{1,0:T(8,128)(2,1)}, u32[]{:S(2)}, u32[]{:S(2)}) %collective-permute-start.10) | collective-permute-done | bytes 655392 | tf_op jit(solution)/shard_map/ppermute | solution.py:488
  69.1 1.0 constant_dynamic-slice_fusion.4
  70.1 0.8 pad_maximum_fusion.1
  70.9 0.6 fusion.9
  71.6 0.7 reshape.70.places_ref
  72.4 1.2 collective-permute-start.16
  73.6 1.2 copy-done.2
  74.8 6.9 %shard_map.150 = (f32[512,512]{1,0:T(8,128)S(1)}, f32[512,512]{1,0:T(8,128)S(1)}, bf16[2,2,512,1024]{3,2,1,0:T(8,128)(2,1)S(1)}, bf16[2,2,512,1024]{3,2,1,0:T(8,128)(2,1)S(1)}, bf16[1,2,512,1024]{3,2,1,0:T(8,128)(2,1)S(1)}) custom-call(s32[16]{0:T(128)S(1)} %reshape_squeeze.3.places_ref, s32[2]{0:T(128)S(1)} %pad_add_fusion.1.shifts_ref, ...), custom_call_target="tpu_custom_call" | custom-call | flops 3221225472 | bytes 9437184 | tf_op jit(solution)/shard_map/pallas_call | solution.py:225
  81.7 1.0 constant_dynamic-slice_fusion
  82.7 0.5 collective-permute-start.15
  83.1 4.3 %shard_map.151 = (f32[512,512]{1,0:T(8,128)S(1)}, f32[512,512]{1,0:T(8,128)S(1)}) custom-call(s32[4]{0:T(128)S(1)} %reshape.71.places_ref, s32[2]{0:T(128)S(1)} %pad_add_fusion.1.shifts_ref, bf16[2,2,512,1024]{3,2,1,0:T(8,128)(2,1)S(1)} %get-tuple-element.75.refs_0_, ...), custom_call_target="tpu_custom_call", output_to_operand_aliasing={{0}: (7, {}), {1}: (8, {})} | custom-call | flops 2147483648 | bytes 6291456 | tf_op jit(solution)/shard_map/pallas_call | solution.py:225
  87.4 4.4 %shard_map.152 = (f32[512,512]{1,0:T(8,128)S(1)}, f32[512,512]{1,0:T(8,128)S(1)}) custom-call(s32[4]{0:T(128)S(1)} %reshape.70.places_ref, s32[2]{0:T(128)S(1)} %pad_add_fusion.1.shifts_ref, bf16[2,2,512,1024]{3,2,1,0:T(8,128)(2,1)S(1)} %get-tuple-element.72.refs_0_, ...), custom_call_target="tpu_custom_call", output_to_operand_aliasing={{0}: (7, {}), {1}: (8, {})} | custom-call | flops 2147483648 | bytes 6291456 | tf_op jit(solution)/shard_map/pallas_call | solution.py:225
  91.9 2.9 %shard_map.153 = (bf16[512,512]{1,0:T(8,128)(2,1)S(1)}, f32[512,512]{1,0:T(8,128)S(1)}) custom-call(s32[2]{0:T(128)S(1)} %slice_bitcast_fusion.1.places_ref, s32[2]{0:T(128)S(1)} %pad_add_fusion.1.shifts_ref, bf16[1,2,512,1024]{3,2,1,0:T(8,128)(2,1)S(1)} %get-tuple-element.70.refs_0_, ...), custom_call_target="tpu_custom_call", output_to_operand_aliasing={{1}: (6, {})} | custom-call | flops 1073741824 | bytes 3145728 | tf_op jit(solution)/shard_map/pallas_call | solution.py:225
  94.8 3.3 %collective-permute-start.17 = (bf16[512,512]{1,0:T(8,128)(2,1)S(1)}, bf16[512,512]{1,0:T(8,128)(2,1)S(1)}, u32[]{:S(2)}, u32[]{:S(2)}) collective-permute-start(bf16[512,512]{1,0:T(8,128)(2,1)S(1)} %get-tuple-element.84), channel_id=1, source_target_pairs={{0,1},{1,0},{2,3},{3,2},{4,5},{5,4},{6,7},{7,6},{8,9},{9,8},{10,11... | collective-permute-start | bytes 1572872 | tf_op jit(solution)/shard_map/ppermute | solution.py:592
  98.2 0.3 convert_reduce_fusion.1
  98.6 1.2 collective-permute-done.17.got_ref
  99.7 2.3 %shard_map.154 = bf16[1024,512]{1,0:T(8,128)(2,1)} custom-call(f32[512,512]{1,0:T(8,128)S(1)} %get-tuple-element.83.own_ref, bf16[512,512]{1,0:T(8,128)(2,1)S(1)} %collective-permute-done.17.got_ref, bf16[512,512]{1,0:T(8,128)(2,1)S(1)} %copy-done.4, bf16[512,512]{1,0:T(8,128)(2,1)S(1)} %copy-done.5, f32[1,512]{1,0:T(1,128)S(1)} %bitcast.31, ...), custom_call_target="tpu_custom_call" | custom-call | flops 805306368 | bytes 2097152 | tf_op jit(solution)/shard_map/pallas_call | solution.py:594
  102.0 5.3 %all-to-all-start = ((bf16[16,64,512]{2,1,0:T(8,128)(2,1)}), bf16[16,64,512]{2,1,0:T(8,128)(2,1)}, u32[]{:S(2)}, u32[]{:S(2)}) async-start(bf16[16,64,512]{2,1,0:T(8,128)(2,1)} %bitcast.12), calls=%async_computation | async-start | bytes 2097152 | tf_op jit(solution)/shard_map/all_to_all | solution.py:608
  107.4 0.2 convert_reduce_fusion
  107.6 0.9 copy.40.slot_col_ref
  108.5 0.9 fusion.5
  109.4 0.2 copy.42
  109.6 0.2 copy.43
  109.8 1.0 maximum_bitcast_fusion.qv_hbm
  110.9 21.4 %all-to-all-done = bf16[16,64,512]{2,1,0:T(8,128)(2,1)} async-done(((bf16[16,64,512]{2,1,0:T(8,128)(2,1)}), bf16[16,64,512]{2,1,0:T(8,128)(2,1)}, u32[]{:S(2)}, u32[]{:S(2)}) %all-to-all-start) | async-done | bytes 1048608 | tf_op jit(solution)/shard_map/all_to_all | solution.py:608
  132.3 21.6 %shard_map.155 = bf16[1024,512]{1,0:T(8,128)(2,1)} custom-call(bf16[1024,512]{1,0:T(8,128)(2,1)} %bitcast.13.arrived_ref, s32[512,1]{1,0:T(8,128)} %copy.40.slot_col_ref, s32[1,512]{1,0:T(1,128)} %bitcast.34, f32[1,512]{1,0:T(1,128)} %bitcast.35, f32[1,512]{1,0:T(1,128)} %bitcast.36, bf16[1024,512]{1,0:T(8,128)(2,1)} %maximum_bitcast_fusion.qv_hbm, ...), custom_call_target="tpu_custom_call" | custom-call | flops 2684354560 | bytes 4194304 | tf_op jit(solution)/shard_map/pallas_call | solution.py:615
  153.9 5.0 %all-to-all-start.1 = ((bf16[16,64,512]{2,1,0:T(8,128)(2,1)}), bf16[16,64,512]{2,1,0:T(8,128)(2,1)S(1)}, u32[]{:S(2)}, u32[]{:S(2)}) async-start(bf16[16,64,512]{2,1,0:T(8,128)(2,1)} %bitcast.32), calls=%async_computation.1 | async-start | bytes 2097152 | tf_op jit(solution)/shard_map/all_to_all | solution.py:641
  158.9 0.1 copy.41.slot_ref
  159.1 24.7 %all-to-all-done.1 = bf16[16,64,512]{2,1,0:T(8,128)(2,1)S(1)} async-done(((bf16[16,64,512]{2,1,0:T(8,128)(2,1)}), bf16[16,64,512]{2,1,0:T(8,128)(2,1)S(1)}, u32[]{:S(2)}, u32[]{:S(2)}) %all-to-all-start.1) | async-done | bytes 1048608 | tf_op jit(solution)/shard_map/all_to_all | solution.py:641
  183.7 1.5 shard_map.156
  (61 shorter events, 1.1 us)
Async XLA Ops:
  0.0 5.3 %copy-start = (bf16[864,512]{1,0:T(8,128)(2,1)S(1)}, bf16[864,512]{1,0:T(8,128)(2,1)}, u32[]{:S(2)}) copy-start(bf16[864,512]{1,0:T(8,128)(2,1)} %param.16) | copy-start | bytes 2654212
  0.0 9.2 %copy-start.10 = (s32[512,26]{0,1:T(8,128)S(1)}, s32[512,26]{0,1:T(8,128)}, u32[]{:S(2)}) copy-start(s32[512,26]{0,1:T(8,128)} %param.26) | copy-start | bytes 159748
  1.1 4.2 %collective-permute-start = (bf16[13,32,512]{2,1,0:T(8,128)(2,1)S(1)}, bf16[13,32,512]{2,1,0:T(8,128)(2,1)S(1)}, u32[]{:S(2)}, u32[]{:S(2)}) collective-permute-start(bf16[13,32,512]{2,1,0:T(8,128)(2,1)S(1)} %slice.52), channel_id=1, source_target_pairs={{0,1},{1,0},{2,3},{3,2},{4,5},{5,4},{6,7},{7,6},{8,9},{9,8},{10,11... | collective-permute-start | bytes 1277960 | tf_op jit(solution)/shard_map/ppermute | solution.py:435
  3.5 1.0 copy-start.3
  6.0 0.9 copy-start.1
  6.9 11.1 %collective-permute-start.3 = (bf16[192,512]{1,0:T(8,128)(2,1)S(1)}, bf16[192,512]{1,0:T(8,128)(2,1)S(1)}, u32[]{:S(2)}, u32[]{:S(2)}) collective-permute-start(bf16[192,512]{1,0:T(8,128)(2,1)S(1)} %get-tuple-element.49), channel_id=1, source_target_pairs={{0,8},{1,9},{2,10},{3,11},{4,12},{5,13},{6,14},{7,15},{8,0},{9,1},... | collective-permute-start | bytes 589832 | tf_op jit(solution)/shard_map/ppermute | solution.py:512
  9.3 22.5 %collective-permute-start.1 = (bf16[640,512]{1,0:T(8,128)(2,1)S(1)}, bf16[640,512]{1,0:T(8,128)(2,1)S(1)}, u32[]{:S(2)}, u32[]{:S(2)}) collective-permute-start(bf16[640,512]{1,0:T(8,128)(2,1)S(1)} %get-tuple-element.48), channel_id=1, source_target_pairs={{0,4},{1,3},{4,8},{5,1},{8,12},{9,5},{12,14},{13,9},{14,10},{15,13... | collective-permute-start | bytes 1966088 | tf_op jit(solution)/shard_map/ppermute | solution.py:488
  9.5 22.6 %collective-permute-start.2 = (bf16[640,512]{1,0:T(8,128)(2,1)S(1)}, bf16[640,512]{1,0:T(8,128)(2,1)S(1)}, u32[]{:S(2)}, u32[]{:S(2)}) collective-permute-start(bf16[640,512]{1,0:T(8,128)(2,1)S(1)} %get-tuple-element.48), channel_id=1, source_target_pairs={{0,2},{1,5},{4,0},{5,9},{8,4},{9,13},{12,8},{13,15},{14,12},{15,11... | collective-permute-start | bytes 1966088 | tf_op jit(solution)/shard_map/ppermute | solution.py:490
  18.1 8.0 %collective-permute-start.4 = (bf16[128,512]{1,0:T(8,128)(2,1)S(1)}, bf16[128,512]{1,0:T(8,128)(2,1)S(1)}, u32[]{:S(2)}, u32[]{:S(2)}) collective-permute-start(bf16[128,512]{1,0:T(8,128)(2,1)S(1)} %pad_maximum_fusion.3), channel_id=1, source_target_pairs={{0,1},{1,2},{2,3},{3,4},{4,5},{5,6},{6,7},{8,9},{9,10},{10,11},{11... | collective-permute-start | bytes 393224 | tf_op jit(solution)/shard_map/ppermute | solution.py:515
  22.3 6.8 %collective-permute-start.5 = (bf16[128,512]{1,0:T(8,128)(2,1)}, bf16[128,512]{1,0:T(8,128)(2,1)S(1)}, u32[]{:S(2)}, u32[]{:S(2)}) collective-permute-start(bf16[128,512]{1,0:T(8,128)(2,1)} %pad_maximum_fusion.4), channel_id=1, source_target_pairs={{1,0},{2,1},{3,2},{4,3},{5,4},{6,5},{7,6},{9,8},{10,9},{11,10},{12... | collective-permute-start | bytes 393224 | tf_op jit(solution)/shard_map/ppermute | solution.py:516
  33.0 5.7 %copy-start.9 = (s32[512,13]{1,0:T(8,128)S(1)}, s32[512,13]{1,0:T(8,128)}, u32[]{:S(2)}) copy-start(s32[512,13]{1,0:T(8,128)} %copy.36) | copy-start | bytes 79876
  33.0 5.5 %collective-permute-start.8 = (s32[512,26]{1,0:T(8,128)}, s32[512,26]{1,0:T(8,128)S(1)}, u32[]{:S(2)}, u32[]{:S(2)}) collective-permute-start(s32[512,26]{1,0:T(8,128)} %copy.37), channel_id=1, source_target_pairs={{0,1},{1,0},{2,3},{3,2},{4,5},{5,4},{6,7},{7,6},{8,9},{9,8},{10,11... | collective-permute-start | bytes 159752 | tf_op jit(solution)/shard_map/ppermute | solution.py:552
  34.0 5.7 %copy-start.7 = (bf16[896,256]{1,0:T(8,128)(2,1)}, bf16[896,256]{1,0:T(8,128)(2,1)S(1)}, u32[]{:S(2)}) copy-start(bf16[896,256]{1,0:T(8,128)(2,1)S(1)} %get-tuple-element.59.table_ref) | copy-start | bytes 1376260
  34.1 16.3 %collective-permute-start.9 = (bf16[896,256]{1,0:T(8,128)(2,1)S(1)}, bf16[896,256]{1,0:T(8,128)(2,1)}, u32[]{:S(2)}, u32[]{:S(2)}) collective-permute-start(bf16[896,256]{1,0:T(8,128)(2,1)S(1)} %get-tuple-element.61), channel_id=1, source_target_pairs={{0,1},{1,0},{2,3},{3,2},{4,5},{5,4},{6,7},{7,6},{8,9},{9,8},{10,11... | collective-permute-start | bytes 1376264 | tf_op jit(solution)/shard_map/ppermute | solution.py:551
  34.2 16.2 %collective-permute-start.6 = (bf16[640,512]{1,0:T(8,128)(2,1)S(1)}, bf16[640,512]{1,0:T(8,128)(2,1)S(1)}, u32[]{:S(2)}, u32[]{:S(2)}) collective-permute-start(bf16[640,512]{1,0:T(8,128)(2,1)S(1)} %collective-permute-done.1.refs_3_), channel_id=1, source_target_pairs={{0,4},{1,3},{4,8},{5,1},{8,12},{9,5},{12,14},{13,9},{14,10},{15,13... | collective-permute-start | bytes 1966088 | tf_op jit(solution)/shard_map/ppermute | solution.py:488
  34.2 16.2 %collective-permute-start.7 = (bf16[640,512]{1,0:T(8,128)(2,1)S(1)}, bf16[640,512]{1,0:T(8,128)(2,1)S(1)}, u32[]{:S(2)}, u32[]{:S(2)}) collective-permute-start(bf16[640,512]{1,0:T(8,128)(2,1)S(1)} %collective-permute-done.2.refs_5_), channel_id=1, source_target_pairs={{0,2},{1,5},{4,0},{5,9},{8,4},{9,13},{12,8},{13,15},{14,12},{15,11... | collective-permute-start | bytes 1966088 | tf_op jit(solution)/shard_map/ppermute | solution.py:490
  37.3 36.3 %collective-permute-start.13 = (bf16[448,512]{1,0:T(8,128)(2,1)}, bf16[448,512]{1,0:T(8,128)(2,1)S(1)}, u32[]{:S(2)}, u32[]{:S(2)}) collective-permute-start(bf16[448,512]{1,0:T(8,128)(2,1)} %pad_maximum_fusion.2), channel_id=1, source_target_pairs={{0,16},{16,0},{1,17},{17,1},{2,18},{18,2},{3,19},{19,3},{4,20},{20... | collective-permute-start | bytes 1376264 | tf_op jit(solution)/shard_map/ppermute | solution.py:502
  50.4 14.7 %collective-permute-start.11 = (bf16[640,512]{1,0:T(8,128)(2,1)S(1)}, bf16[640,512]{1,0:T(8,128)(2,1)}, u32[]{:S(2)}, u32[]{:S(2)}) collective-permute-start(bf16[640,512]{1,0:T(8,128)(2,1)S(1)} %collective-permute-done.7.refs_3_), channel_id=1, source_target_pairs={{0,2},{1,5},{4,0},{5,9},{8,4},{9,13},{12,8},{13,15},{14,12},{15,11... | collective-permute-start | bytes 1966088 | tf_op jit(solution)/shard_map/ppermute | solution.py:490
  52.4 16.7 %collective-permute-start.10 = (bf16[640,512]{1,0:T(8,128)(2,1)S(1)}, bf16[640,512]{1,0:T(8,128)(2,1)}, u32[]{:S(2)}, u32[]{:S(2)}) collective-permute-start(bf16[640,512]{1,0:T(8,128)(2,1)S(1)} %collective-permute-done.6.refs_1_), channel_id=1, source_target_pairs={{0,4},{1,3},{4,8},{5,1},{8,12},{9,5},{12,14},{13,9},{14,10},{15,13... | collective-permute-start | bytes 1966088 | tf_op jit(solution)/shard_map/ppermute | solution.py:488
  52.5 18.4 %collective-permute-start.12 = (bf16[448,512]{1,0:T(8,128)(2,1)S(1)}, bf16[448,512]{1,0:T(8,128)(2,1)S(1)}, u32[]{:S(2)}, u32[]{:S(2)}) collective-permute-start(bf16[448,512]{1,0:T(8,128)(2,1)S(1)} %pad_maximum_fusion), channel_id=1, source_target_pairs={{0,16},{16,0},{1,17},{17,1},{2,18},{18,2},{3,19},{19,3},{4,20},{20... | collective-permute-start | bytes 1376264 | tf_op jit(solution)/shard_map/ppermute | solution.py:502
  70.9 10.8 %collective-permute-start.14 = (bf16[640,512]{1,0:T(8,128)(2,1)}, bf16[640,512]{1,0:T(8,128)(2,1)}, u32[]{:S(2)}, u32[]{:S(2)}) collective-permute-start(bf16[640,512]{1,0:T(8,128)(2,1)} %collective-permute-done.10.refs_1_), channel_id=1, source_target_pairs={{0,4},{1,3},{4,8},{5,1},{8,12},{9,5},{12,14},{13,9},{14,10},{15,13... | collective-permute-start | bytes 1966088 | tf_op jit(solution)/shard_map/ppermute | solution.py:488
  72.4 15.0 %collective-permute-start.16 = (bf16[448,512]{1,0:T(8,128)(2,1)}, bf16[448,512]{1,0:T(8,128)(2,1)S(1)}, u32[]{:S(2)}, u32[]{:S(2)}) collective-permute-start(bf16[448,512]{1,0:T(8,128)(2,1)} %pad_maximum_fusion.1), channel_id=1, source_target_pairs={{0,16},{16,0},{1,17},{17,1},{2,18},{18,2},{3,19},{19,3},{4,20},{20... | collective-permute-start | bytes 1376264 | tf_op jit(solution)/shard_map/ppermute | solution.py:502
  73.6 1.2 copy-start.2
  82.7 9.1 %collective-permute-start.15 = (bf16[224,512]{1,0:T(8,128)(2,1)S(1)}, bf16[224,512]{1,0:T(8,128)(2,1)S(1)}, u32[]{:S(2)}, u32[]{:S(2)}) collective-permute-start(bf16[224,512]{1,0:T(8,128)(2,1)S(1)} %constant_dynamic-slice_fusion), channel_id=1, source_target_pairs={{0,16},{16,0},{1,17},{17,1},{2,18},{18,2},{3,19},{19,3},{4,20},{20... | collective-permute-start | bytes 688136 | tf_op jit(solution)/shard_map/ppermute | solution.py:502
  91.8 6.4 %copy-start.11 = (s32[512]{0:T(512)S(1)}, s32[512]{0:T(512)}, u32[]{:S(2)}) copy-start(s32[512]{0:T(512)} %param.27) | copy-start | bytes 6148
  91.8 6.4 %copy-start.13 = (s32[512]{0:T(512)S(1)}, s32[512]{0:T(512)}, u32[]{:S(2)}) copy-start(s32[512]{0:T(512)} %param.28) | copy-start | bytes 6148
  91.8 7.9 %copy-start.4 = (bf16[512,512]{1,0:T(8,128)(2,1)S(1)}, bf16[512,512]{1,0:T(8,128)(2,1)}, u32[]{:S(2)}) copy-start(bf16[512,512]{1,0:T(8,128)(2,1)} %features_ref.3) | copy-start | bytes 1572868
  91.8 7.9 %copy-start.5 = (bf16[512,512]{1,0:T(8,128)(2,1)S(1)}, bf16[512,512]{1,0:T(8,128)(2,1)}, u32[]{:S(2)}) copy-start(bf16[512,512]{1,0:T(8,128)(2,1)} %weight_ref.1) | copy-start | bytes 1572868
  91.9 7.9 %copy-start.6 = (f32[512]{0:T(512)S(1)}, f32[512]{0:T(512)}, u32[]{:S(2)}) copy-start(f32[512]{0:T(512)} %param.18) | copy-start | bytes 6148
  94.8 4.9 %collective-permute-start.17 = (bf16[512,512]{1,0:T(8,128)(2,1)S(1)}, bf16[512,512]{1,0:T(8,128)(2,1)S(1)}, u32[]{:S(2)}, u32[]{:S(2)}) collective-permute-start(bf16[512,512]{1,0:T(8,128)(2,1)S(1)} %get-tuple-element.84), channel_id=1, source_target_pairs={{0,1},{1,0},{2,3},{3,2},{4,5},{5,4},{6,7},{7,6},{8,9},{9,8},{10,11... | collective-permute-start | bytes 1572872 | tf_op jit(solution)/shard_map/ppermute | solution.py:592
  102.0 6.4 %copy-start.8 = (bf16[512,1536]{1,0:T(8,128)(2,1)S(1)}, bf16[512,1536]{1,0:T(8,128)(2,1)}, u32[]{:S(2)}) copy-start(bf16[512,1536]{1,0:T(8,128)(2,1)} %param.20) | copy-start | bytes 4718596
  102.0 30.3 %all-to-all-start = ((bf16[16,64,512]{2,1,0:T(8,128)(2,1)}), bf16[16,64,512]{2,1,0:T(8,128)(2,1)}, u32[]{:S(2)}, u32[]{:S(2)}) async-start(bf16[16,64,512]{2,1,0:T(8,128)(2,1)} %bitcast.12), calls=%async_computation | async-start | bytes 2097152 | tf_op jit(solution)/shard_map/all_to_all | solution.py:608
  107.6 2.0 %copy-start.12 = (s32[512]{0:T(512)}, s32[512]{0:T(512)S(1)}, u32[]{:S(2)}) copy-start(s32[512]{0:T(512)S(1)} %multiply_add_fusion) | copy-start | bytes 6148
  153.9 29.8 %all-to-all-start.1 = ((bf16[16,64,512]{2,1,0:T(8,128)(2,1)}), bf16[16,64,512]{2,1,0:T(8,128)(2,1)S(1)}, u32[]{:S(2)}, u32[]{:S(2)}) async-start(bf16[16,64,512]{2,1,0:T(8,128)(2,1)} %bitcast.32), calls=%async_computation.1 | async-start | bytes 2097152 | tf_op jit(solution)/shard_map/all_to_all | solution.py:641

commit v17 on v15

--- a/solution.py
+++ b/solution.py
@@ -57,8 +57,10 @@
             for at, source in enumerate(order):
                 mine_ref[at * unit : (at + 1) * unit] = source[...]
 
-    start = pl.multiple_of(flags_ref[1] * missing, 16)
-    begun_ref[...] = mine_ref[pl.ds(start, begun_ref.shape[0])]
+    passed = begun_ref.shape[0]
+    lent = pl.multiple_of(flags_ref[1] * passed, 16)
+    begun_ref[:missing] = mine_ref[pl.ds(lent, missing)]
+    begun_ref[missing:] = mine_ref[missing:passed]
 
 
 def faces_kernel(unit, core_ref, features_ref, rows_ref, own_ref, other_ref, *face_refs):
@@ -180,12 +182,13 @@
     for at, parts in enumerate(slots):
         row = pl.multiple_of(places_ref[2 * at + 1], 16)
         copies.append([] if ready else stretch(at, lhs.at[at], sems.at[at]))
-        edge = length - sum(size for _, size, _ in parts)
+        edge = length - sum(size for _, size, _, _ in parts)
         if edge:
             held[at, :edge] = jnp.zeros((edge, held.shape[2]), BF16)
             held[at, length - edge :] = jnp.zeros((edge, held.shape[2]), BF16)
-        for part, (start, size, kind) in enumerate(parts):
-            place = row if kind is None else pl.multiple_of(row + shifts_ref[kind], 16)
+        for part, (start, size, offset, kind) in enumerate(parts):
+            moved = row + offset if kind is None else row + shifts_ref[kind]
+            place = pl.multiple_of(moved, 16)
             (piece,) = pieces[:1]
             del pieces[:1]
             copy = pltpu.make_async_copy(
@@ -240,9 +243,9 @@
         scratch_shapes=([] if ready else [pltpu.VMEM((len(slots), 2, points, length), BF16)])
         + [
             pltpu.VMEM((len(slots), length, width), BF16),
-            pltpu.SemaphoreType.DMA((len(slots) + sum(later), 4)),
+            pltpu.SemaphoreType.DMA((len(slots) + sum(later), 5)),
         ],
-    )(places.reshape(-1), shifts, *sources, *flat, *(before or ()))
+    )(places, shifts, *sources, *flat, *(before or ()))
 
 
 def mix_kernel(own_ref, got_ref, features_ref, weight_ref, gain_ref, slot_ref, out_ref):
@@ -476,7 +479,7 @@
     )(core.reshape(1), features, face_list)
     length = -(-(rows + 127) // 128) * 128 if round_trip else rows * (devices // 2)
     first_pairs, second_pairs, places = way_round(devices, rows, length)
-    shifts = jnp.stack([side * missing, (1 - side) * passed]).astype(jnp.int32)
+    shifts = jnp.stack([side * passed, (1 - side) * passed]).astype(jnp.int32)
     first, second = [begun], [begun]
 
     def pass_on(*beside):
@@ -490,18 +493,16 @@
             second.append(lax.ppermute(second[-1], "blocks", second_pairs))
         return tied[2:]
 
-    def lend(*arrived):
-        return jnp.concatenate(
-            [
-                lax.dynamic_slice(piece, (side * (passed - missing), 0), (missing, width))
-                for piece in arrived
-            ]
-        )
-
-    def complete(lent, *arrived):
+    def complete(*arrived):
+        lent = [piece[:missing] for piece in arrived]
+        lent = jnp.concatenate(lent) if len(lent) > 1 else lent[0]
         got = lax.ppermute(lent, "groups", [(0, 1), (1, 0)])
         return [
-            [(piece, 0, passed, 0), (got, at * missing, missing, 1)]
+            [
+                (piece, 0, missing, 0, 0),
+                (piece, missing, passed - missing, missing, None),
+                (got, at * missing, missing, 0, 1),
+            ]
             for at, piece in enumerate(arrived)
         ]
 
@@ -510,12 +511,15 @@
         across = face_pairs(devices, 1, 0) + face_pairs(devices, -1, 0)
         (lists,) = pass_on(lists)
         lists = lax.ppermute(lists, "blocks", across)
+        places = jnp.array(places, jnp.int32)[index].reshape(-1)
+        lists, sent_neighbours, places = lax.optimization_barrier((lists, neighbours, places))
+        other_neighbours = lax.ppermute(sent_neighbours, "blocks", partner)
         to_on = jnp.concatenate([on_list, lists[2 * size :]])
         to_back = jnp.concatenate([back_list, lists[:size]])
         behind = lax.ppermute(to_on, "blocks", face_pairs(devices, 0, 1))
         ahead = lax.ppermute(to_back, "blocks", face_pairs(devices, 0, -1))
-        sent_neighbours, lists, behind, ahead = pass_on(neighbours, lists, behind, ahead)
-        near = complete(lend(first[1], second[1]), first[1], second[1])
+        lists, behind, ahead = pass_on(lists, behind, ahead)
+        near = complete(first[1], second[1])
         own_table, other_half = call(
             table_kernel,
             [jax.ShapeDtypeStruct((points + 6 * size, half), BF16)] * 2,
@@ -533,7 +537,7 @@
         )
         start = jnp.where(lower, points, points + 3 * size).reshape(1)
     else:
-        sent_neighbours = neighbours
+        other_neighbours = lax.ppermute(neighbours, "blocks", partner)
         received = jnp.concatenate(
             [
                 lax.ppermute(faces[k], "blocks", face_pairs(devices, STEPS_X[k], STEPS_Y[k]))
@@ -549,34 +553,32 @@
         )
         start = jnp.full((1,), points, jnp.int32)
     other_table = lax.ppermute(other_half, "blocks", partner)
-    other_neighbours = lax.ppermute(sent_neighbours, "blocks", partner)
     own_stacked = gather_block(start, padded_taps(neighbours), own_table)
     other_rows = padded_taps(other_neighbours)
     own_stacked, other_rows, other_table = pass_on(own_stacked, other_rows, other_table)
     if round_trip:
-        middle = complete(lend(first[2], second[2]), first[2], second[2])
+        middle = complete(first[2], second[2])
     other_stacked = gather_block(start, other_rows, other_table)
     stacked = other_stacked, own_stacked
     if round_trip:
-        places = jnp.array(places, jnp.int32)[index]
-        early = [[(mine, 0, rows, None)]] + near
+        *stacked, middle_got = pass_on(*stacked, middle[0][2][0])
+        middle = [[*parts[:2], (middle_got, *parts[2][1:])] for parts in middle]
+        early = [[(mine, 0, rows, 0, None)]] + near
         *sums, middle_lhs, far_lhs, last_lhs = conv_part(
             stacked, places, shifts, early, None, length, (2, 2, 1)
         )
-        *sums, middle_got, lent = pass_on(*sums, middle[0][1][0], lend(first[3], second[3]))
-        middle = [[parts[0], (middle_got, *parts[1][1:])] for parts in middle]
-        far = complete(lent, first[3], second[3])
-        opposite = complete(lend(first[4]), first[4])
-        sums = conv_part([middle_lhs], places[3:5], shifts, middle, sums, length)
-        sums = conv_part([far_lhs], places[5:7], shifts, far, sums, length)
+        far = complete(first[3], second[3])
+        opposite = complete(first[4])
+        sums = conv_part([middle_lhs], places[6:10], shifts, middle, sums, length)
+        sums = conv_part([far_lhs], places[10:14], shifts, far, sums, length)
         for_partner, own_part = conv_part(
-            [last_lhs], places[7:], shifts, opposite, sums, length, dtype=BF16
+            [last_lhs], places[14:], shifts, opposite, sums, length, dtype=BF16
         )
     else:
         groups = [list(range(core, devices, 2)) for core in range(2)]
         weight = lax.all_gather(mine, "blocks", axis=0, tiled=True, axis_index_groups=groups)
-        nowhere = jnp.zeros((1, 2), jnp.int32)
-        whole = [[(weight, 0, weight.shape[0], None)]]
+        nowhere = jnp.zeros((2,), jnp.int32)
+        whole = [[(weight, 0, weight.shape[0], 0, None)]]
         for_partner, own_part = conv_part(stacked, nowhere, shifts, whole, None, length)
 
     positions = jnp.arange(points, dtype=jnp.int32)

time: 199 us -> 180 us (0.905)
  waiting for transfers between devices: 70.7 us -> 59.9 us
  local copies, waits for them, and re-layouts: 22.1 us -> 12.6 us
    ppermute x4, waiting for transfers between devices: 12.4 us -> 2.34 us  [pass_on(): first.append(lax.ppermute(first[-1], 'blocks', first_pairs))]
    unnamed x46 -> x30, local copies, waits for them, and re-layouts: 12.2 us -> 3.95 us
    dynamic_slice x6 -> x1, local copies, waits for them, and re-layouts: 3.74 us -> 0.69 us  [body(): places = jnp.array(places, jnp.int32)[index].reshape(-1)]
    ppermute x1, waiting for transfers between devices: 7.3 us -> 4.72 us  [body(): lists = lax.ppermute(lists, 'blocks', across)]
  transfers between devices with their start and end apart: 20 -> 20, of which waited for: 8 -> 11; matrix products, arithmetic and copies ran while one was open for 7% -> 8% of each run, Pallas kernels for 19% -> 22%
where the time goes in v17:
time: 180 us
  Pallas kernels  68.3 us (38%)
  waiting for transfers between devices  59.9 us (33%)
  starting transfers between devices  31.3 us (17%)
  local copies, waits for them, and re-layouts  12.6 us (7%)
  other arithmetic  7.1 us (4%)
    all_to_all x1, waiting for transfers between devices, body(): lax.all_to_all(back.reshape(devices, capacity, width), 'blocks', split_ax...  24.7 us
    pallas_call x1, Pallas kernels, body(): call(block_kernel, jax.ShapeDtypeStruct((slots, width), BF16), 60, 20 * p...  21.6 us
    all_to_all x1, waiting for transfers between devices, body(): lax.all_to_all(outgoing.reshape(devices, capacity, width), 'blocks', spli...  21.4 us
    pallas_call x2, Pallas kernels, gather_block(): call(functools.partial(gather_kernel, taps), jax.ShapeDtypeStruct((points...  21.2 us
    pallas_call x4, Pallas kernels, conv_part(): call(functools.partial(conv_kernel, slots, later, ready, before is None),...  18.8 us
    ppermute x3, starting transfers between devices, pass_on(): second.append(lax.ppermute(second[-1], 'blocks', second_pairs))  5.33 us
    all_to_all x1, starting transfers between devices, body(): lax.all_to_all(outgoing.reshape(devices, capacity, width), 'blocks', spli...  5.31 us
    all_to_all x1, starting transfers between devices, body(): lax.all_to_all(back.reshape(devices, capacity, width), 'blocks', split_ax...  5.01 us
  transfers between devices with their start and end apart: 20, of which 11 were waited for; matrix products, arithmetic and copies ran while one was open for 8% of the time, Pallas kernels for 22%

profile of v17, /device:TPU:9, one launch (start us, length us, event | category | flops | bytes accessed | tf_op | source)
XLA Modules:
  0.0 179.6 jit_solution(15314455264052878046)
XLA Ops:
  0.0 1.1 slice.69
  1.1 0.7 collective-permute-start
  1.9 0.7 slice_bitcast_fusion
  2.6 0.8 select_bitcast_fusion
  3.3 0.1 reshape.66.rows_ref
  3.5 1.0 copy-done.3
  4.5 0.7 shard_map.146
  5.4 0.7 shard_map.145
  6.0 0.9 copy-done.1
  7.0 2.3 %collective-permute-start.1 = (bf16[192,512]{1,0:T(8,128)(2,1)S(1)}, bf16[192,512]{1,0:T(8,128)(2,1)S(1)}, u32[]{:S(2)}, u32[]{:S(2)}) collective-permute-start(bf16[192,512]{1,0:T(8,128)(2,1)S(1)} %get-tuple-element.48), channel_id=1, source_target_pairs={{0,8},{1,9},{2,10},{3,11},{4,12},{5,13},{6,14},{7,15},{8,0},{9,1},... | collective-permute-start | bytes 589832 | tf_op jit(solution)/shard_map/ppermute | solution.py:513
  9.3 0.7 constant_dynamic-slice_fusion
  10.0 0.9 copy.35
  10.9 0.9 copy.36
  11.9 0.2 collective-permute-start.2
  12.1 1.3 collective-permute-start.3
  13.4 4.7 %collective-permute-done.1.side_ref = bf16[192,512]{1,0:T(8,128)(2,1)S(1)} collective-permute-done((bf16[192,512]{1,0:T(8,128)(2,1)S(1)}, bf16[192,512]{1,0:T(8,128)(2,1)S(1)}, u32[]{:S(2)}, u32[]{:S(2)}) %collective-permute-start.1) | collective-permute-done | bytes 196640 | tf_op jit(solution)/shard_map/ppermute | solution.py:513
  18.1 0.6 pad_maximum_fusion.3
  18.8 3.5 %collective-permute-start.4 = (bf16[128,512]{1,0:T(8,128)(2,1)}, bf16[128,512]{1,0:T(8,128)(2,1)S(1)}, u32[]{:S(2)}, u32[]{:S(2)}) collective-permute-start(bf16[128,512]{1,0:T(8,128)(2,1)} %pad_maximum_fusion.3), channel_id=1, source_target_pairs={{0,1},{1,2},{2,3},{3,4},{4,5},{5,6},{6,7},{8,9},{9,10},{10,11},{11... | collective-permute-start | bytes 393224 | tf_op jit(solution)/shard_map/ppermute | solution.py:519
  22.3 0.8 copy.37
  23.1 2.4 %collective-permute-start.5 = (bf16[128,512]{1,0:T(8,128)(2,1)S(1)}, bf16[128,512]{1,0:T(8,128)(2,1)S(1)}, u32[]{:S(2)}, u32[]{:S(2)}) collective-permute-start(bf16[128,512]{1,0:T(8,128)(2,1)S(1)} %pad_maximum_fusion.4), channel_id=1, source_target_pairs={{1,0},{2,1},{3,2},{4,3},{5,4},{6,5},{7,6},{9,8},{10,9},{11,10},{12... | collective-permute-start | bytes 393224 | tf_op jit(solution)/shard_map/ppermute | solution.py:520
  25.7 2.1 %add_convert_fusion.1 = (f32[512,128]{1,0:T(8,128)}, f32[512,128]{1,0:T(8,128)}) fusion(s32[512,13]{1,0:T(8,128)S(1)} %get-tuple-element.93, s32[512,13]{1,0:T(8,128)S(1)} %get-tuple-element.92, s32[512,1]{1,0:T(8,128)S(1)} %iota.13, s32[128]{0:T(128)S(1)} %pad.17.clone, s32[512,13]{1,0:T(8,128)} %copy.36, s32[512,13]{1,0:T(8,128)} %copy.35), kind=kLoop, calls=%fused_computation.9 | loop fusion | flops 524288 | bytes 633344 | tf_op jit(solution)/shard_map/convert_element_type | solution.py:408
  27.9 2.5 %collective-permute-done.5.ahead_ref = bf16[128,512]{1,0:T(8,128)(2,1)S(1)} collective-permute-done((bf16[128,512]{1,0:T(8,128)(2,1)S(1)}, bf16[128,512]{1,0:T(8,128)(2,1)S(1)}, u32[]{:S(2)}, u32[]{:S(2)}) %collective-permute-start.5) | collective-permute-done | bytes 131104 | tf_op jit(solution)/shard_map/ppermute | solution.py:520
  30.4 1.4 collective-permute-done.2.refs_3_.refs_4_
  31.8 0.3 collective-permute-done.3.refs_6_.refs_7_
  32.2 2.3 %collective-permute-start.7 = (bf16[640,512]{1,0:T(8,128)(2,1)S(1)}, bf16[640,512]{1,0:T(8,128)(2,1)S(1)}, u32[]{:S(2)}, u32[]{:S(2)}) collective-permute-start(bf16[640,512]{1,0:T(8,128)(2,1)S(1)} %collective-permute-done.3.refs_6_.refs_7_), channel_id=1, source_target_pairs={{0,2},{1,5},{4,0},{5,9},{8,4},{9,13},{12,8},{13,15},{14,12},{15,11... | collective-permute-start | bytes 1966088 | tf_op jit(solution)/shard_map/ppermute | solution.py:493
  34.4 1.4 shard_map.147
  35.8 0.8 copy-done.7
  36.6 0.7 collective-permute-start.9
  37.3 0.8 pad_maximum_fusion.1
  38.1 1.2 collective-permute-start.13
  39.3 10.6 %shard_map.148.refs_1_ = bf16[512,6912]{1,0:T(8,128)(2,1)} custom-call(s32[1]{0:T(128)} %bitcast.7.start_ref, f32[512,128]{1,0:T(8,128)} %get-tuple-element.91.rows_ref, bf16[896,256]{1,0:T(8,128)(2,1)} %copy-done.7), custom_call_target="tpu_custom_call" | custom-call | flops 6341787648 | bytes 7077888 | tf_op jit(solution)/shard_map/pallas_call | solution.py:136
  49.9 0.7 copy-done.13
  50.8 1.8 collective-permute-start.11
  52.6 0.8 pad_maximum_fusion
  53.4 0.3 collective-permute-start.12
  53.6 10.7 %shard_map.149.refs_0_ = bf16[512,6912]{1,0:T(8,128)(2,1)} custom-call(s32[1]{0:T(128)} %bitcast.7.start_ref, f32[512,128]{1,0:T(8,128)} %get-tuple-element.67.rows_ref, bf16[896,256]{1,0:T(8,128)(2,1)} %copy-done.13), custom_call_target="tpu_custom_call" | custom-call | flops 6341787648 | bytes 7077888 | tf_op jit(solution)/shard_map/pallas_call | solution.py:136
  64.3 0.9 collective-permute-done.12.refs_3_.refs_6_
  65.2 1.8 %collective-permute-done.11.refs_4_.refs_5_ = bf16[640,512]{1,0:T(8,128)(2,1)} collective-permute-done((bf16[640,512]{1,0:T(8,128)(2,1)S(1)}, bf16[640,512]{1,0:T(8,128)(2,1)}, u32[]{:S(2)}, u32[]{:S(2)}) %collective-permute-start.11) | collective-permute-done | bytes 655392 | tf_op jit(solution)/shard_map/ppermute | solution.py:493
  67.1 0.7 collective-permute-start.14
  68.0 1.0 slice.87
  69.0 0.3 collective-permute-start.16
  69.3 6.9 %shard_map.150 = (f32[512,512]{1,0:T(8,128)S(1)}, f32[512,512]{1,0:T(8,128)S(1)}, bf16[2,2,512,1024]{3,2,1,0:T(8,128)(2,1)S(1)}, bf16[2,2,512,1024]{3,2,1,0:T(8,128)(2,1)S(1)}, bf16[1,2,512,1024]{3,2,1,0:T(8,128)(2,1)S(1)}) custom-call(s32[16]{0:T(128)S(1)} %reshape_squeeze.3.places_ref, s32[2]{0:T(128)S(1)} %pad_add_fusion.2.shifts_ref, ...), custom_call_target="tpu_custom_call" | custom-call | flops 3221225472 | bytes 9437184 | tf_op jit(solution)/shard_map/pallas_call | solution.py:228
  76.2 0.9 collective-permute-done.14.refs_1_.refs_2_
  77.1 0.5 collective-permute-start.15
  77.6 4.7 %shard_map.151 = (f32[512,512]{1,0:T(8,128)S(1)}, f32[512,512]{1,0:T(8,128)S(1)}) custom-call(s32[4]{0:T(128)S(1)} %get-tuple-element.98.places_ref, s32[2]{0:T(128)S(1)} %pad_add_fusion.2.shifts_ref, bf16[2,2,512,1024]{3,2,1,0:T(8,128)(2,1)S(1)} %get-tuple-element.77.refs_0_, ...), custom_call_target="tpu_custom_call", output_to_operand_aliasing={{0}: (9, {}), {1}: (10, {})} | custom-call | flops 2147483648 | bytes 6291456 | tf_op jit(solution)/shard_map/pallas_call | solution.py:228
  82.3 4.4 %shard_map.152 = (f32[512,512]{1,0:T(8,128)S(1)}, f32[512,512]{1,0:T(8,128)S(1)}) custom-call(s32[4]{0:T(128)S(1)} %get-tuple-element.99.places_ref, s32[2]{0:T(128)S(1)} %pad_add_fusion.2.shifts_ref, bf16[2,2,512,1024]{3,2,1,0:T(8,128)(2,1)S(1)} %get-tuple-element.75.refs_0_, ...), custom_call_target="tpu_custom_call", output_to_operand_aliasing={{0}: (9, {}), {1}: (10, {})} | custom-call | flops 2147483648 | bytes 6291456 | tf_op jit(solution)/shard_map/pallas_call | solution.py:228
  86.8 2.7 %shard_map.153 = (bf16[512,512]{1,0:T(8,128)(2,1)S(1)}, f32[512,512]{1,0:T(8,128)S(1)}) custom-call(s32[2]{0:T(128)S(1)} %slice.73.places_ref, s32[2]{0:T(128)S(1)} %pad_add_fusion.2.shifts_ref, bf16[1,2,512,1024]{3,2,1,0:T(8,128)(2,1)S(1)} %get-tuple-element.73.refs_0_, ...), custom_call_target="tpu_custom_call", output_to_operand_aliasing={{1}: (7, {})} | custom-call | flops 1073741824 | bytes 3145728 | tf_op jit(solution)/shard_map/pallas_call | solution.py:228
  89.5 2.9 %collective-permute-start.17 = (bf16[512,512]{1,0:T(8,128)(2,1)S(1)}, bf16[512,512]{1,0:T(8,128)(2,1)S(1)}, u32[]{:S(2)}, u32[]{:S(2)}) collective-permute-start(bf16[512,512]{1,0:T(8,128)(2,1)S(1)} %get-tuple-element.86), channel_id=1, source_target_pairs={{0,1},{1,0},{2,3},{3,2},{4,5},{5,4},{6,7},{7,6},{8,9},{9,8},{10,11... | collective-permute-start | bytes 1572872 | tf_op jit(solution)/shard_map/ppermute | solution.py:592
  92.4 0.3 convert_reduce_fusion.1
  92.8 1.2 collective-permute-done.17.got_ref
  94.0 2.3 %shard_map.154 = bf16[1024,512]{1,0:T(8,128)(2,1)} custom-call(f32[512,512]{1,0:T(8,128)S(1)} %get-tuple-element.85.own_ref, bf16[512,512]{1,0:T(8,128)(2,1)S(1)} %collective-permute-done.17.got_ref, bf16[512,512]{1,0:T(8,128)(2,1)S(1)} %copy-done.4, bf16[512,512]{1,0:T(8,128)(2,1)S(1)} %copy-done.5, f32[1,512]{1,0:T(1,128)S(1)} %bitcast.29, ...), custom_call_target="tpu_custom_call" | custom-call | flops 805306368 | bytes 2097152 | tf_op jit(solution)/shard_map/pallas_call | solution.py:594
  96.3 5.3 %all-to-all-start = ((bf16[16,64,512]{2,1,0:T(8,128)(2,1)}), bf16[16,64,512]{2,1,0:T(8,128)(2,1)}, u32[]{:S(2)}, u32[]{:S(2)}) async-start(bf16[16,64,512]{2,1,0:T(8,128)(2,1)} %bitcast.11), calls=%async_computation | async-start | bytes 2097152 | tf_op jit(solution)/shard_map/all_to_all | solution.py:608
  101.6 0.9 fusion.5
  102.5 0.2 copy.42
  102.8 0.2 copy.43
  103.0 0.2 convert_reduce_fusion
  103.3 0.9 copy.40.slot_col_ref
  104.1 1.0 maximum_bitcast_fusion.qv_hbm
  105.2 21.4 %all-to-all-done = bf16[16,64,512]{2,1,0:T(8,128)(2,1)} async-done(((bf16[16,64,512]{2,1,0:T(8,128)(2,1)}), bf16[16,64,512]{2,1,0:T(8,128)(2,1)}, u32[]{:S(2)}, u32[]{:S(2)}) %all-to-all-start) | async-done | bytes 1048608 | tf_op jit(solution)/shard_map/all_to_all | solution.py:608
  126.6 21.6 %shard_map.155 = bf16[1024,512]{1,0:T(8,128)(2,1)} custom-call(bf16[1024,512]{1,0:T(8,128)(2,1)} %bitcast.12.arrived_ref, s32[512,1]{1,0:T(8,128)} %copy.40.slot_col_ref, s32[1,512]{1,0:T(1,128)} %bitcast.32, f32[1,512]{1,0:T(1,128)} %bitcast.33, f32[1,512]{1,0:T(1,128)} %bitcast.34, bf16[1024,512]{1,0:T(8,128)(2,1)} %maximum_bitcast_fusion.qv_hbm, ...), custom_call_target="tpu_custom_call" | custom-call | flops 2684354560 | bytes 4194304 | tf_op jit(solution)/shard_map/pallas_call | solution.py:615
  148.2 5.0 %all-to-all-start.1 = ((bf16[16,64,512]{2,1,0:T(8,128)(2,1)}), bf16[16,64,512]{2,1,0:T(8,128)(2,1)S(1)}, u32[]{:S(2)}, u32[]{:S(2)}) async-start(bf16[16,64,512]{2,1,0:T(8,128)(2,1)} %bitcast.30), calls=%async_computation.1 | async-start | bytes 2097152 | tf_op jit(solution)/shard_map/all_to_all | solution.py:641
  153.2 0.1 copy.41.slot_ref
  153.4 24.7 %all-to-all-done.1 = bf16[16,64,512]{2,1,0:T(8,128)(2,1)S(1)} async-done(((bf16[16,64,512]{2,1,0:T(8,128)(2,1)}), bf16[16,64,512]{2,1,0:T(8,128)(2,1)S(1)}, u32[]{:S(2)}, u32[]{:S(2)}) %all-to-all-start.1) | async-done | bytes 1048608 | tf_op jit(solution)/shard_map/all_to_all | solution.py:641
  178.0 1.5 shard_map.156
  (62 shorter events, 1.1 us)
Async XLA Ops:
  0.0 5.3 %copy-start = (bf16[864,512]{1,0:T(8,128)(2,1)S(1)}, bf16[864,512]{1,0:T(8,128)(2,1)}, u32[]{:S(2)}) copy-start(bf16[864,512]{1,0:T(8,128)(2,1)} %param.16) | copy-start | bytes 2654212
  0.0 5.3 %copy-start.9 = (s32[512,26]{0,1:T(8,128)S(1)}, s32[512,26]{0,1:T(8,128)}, u32[]{:S(2)}) copy-start(s32[512,26]{0,1:T(8,128)} %param.26) | copy-start | bytes 159748
  1.1 4.2 %collective-permute-start = (bf16[13,32,512]{2,1,0:T(8,128)(2,1)S(1)}, bf16[13,32,512]{2,1,0:T(8,128)(2,1)S(1)}, u32[]{:S(2)}, u32[]{:S(2)}) collective-permute-start(bf16[13,32,512]{2,1,0:T(8,128)(2,1)S(1)} %slice.69), channel_id=1, source_target_pairs={{0,1},{1,0},{2,3},{3,2},{4,5},{5,4},{6,7},{7,6},{8,9},{9,8},{10,11... | collective-permute-start | bytes 1277960 | tf_op jit(solution)/shard_map/ppermute | solution.py:438
  3.5 1.0 copy-start.3
  6.0 0.9 copy-start.1
  7.0 11.1 %collective-permute-start.1 = (bf16[192,512]{1,0:T(8,128)(2,1)S(1)}, bf16[192,512]{1,0:T(8,128)(2,1)S(1)}, u32[]{:S(2)}, u32[]{:S(2)}) collective-permute-start(bf16[192,512]{1,0:T(8,128)(2,1)S(1)} %get-tuple-element.48), channel_id=1, source_target_pairs={{0,8},{1,9},{2,10},{3,11},{4,12},{5,13},{6,14},{7,15},{8,0},{9,1},... | collective-permute-start | bytes 589832 | tf_op jit(solution)/shard_map/ppermute | solution.py:513
  11.9 19.9 %collective-permute-start.2 = (bf16[640,512]{1,0:T(8,128)(2,1)S(1)}, bf16[640,512]{1,0:T(8,128)(2,1)S(1)}, u32[]{:S(2)}, u32[]{:S(2)}) collective-permute-start(bf16[640,512]{1,0:T(8,128)(2,1)S(1)} %get-tuple-element.51), channel_id=1, source_target_pairs={{0,4},{1,3},{4,8},{5,1},{8,12},{9,5},{12,14},{13,9},{14,10},{15,13... | collective-permute-start | bytes 1966088 | tf_op jit(solution)/shard_map/ppermute | solution.py:491
  12.1 20.1 %collective-permute-start.3 = (bf16[640,512]{1,0:T(8,128)(2,1)S(1)}, bf16[640,512]{1,0:T(8,128)(2,1)S(1)}, u32[]{:S(2)}, u32[]{:S(2)}) collective-permute-start(bf16[640,512]{1,0:T(8,128)(2,1)S(1)} %get-tuple-element.51), channel_id=1, source_target_pairs={{0,2},{1,5},{4,0},{5,9},{8,4},{9,13},{12,8},{13,15},{14,12},{15,11... | collective-permute-start | bytes 1966088 | tf_op jit(solution)/shard_map/ppermute | solution.py:493
  18.8 9.1 %collective-permute-start.4 = (bf16[128,512]{1,0:T(8,128)(2,1)}, bf16[128,512]{1,0:T(8,128)(2,1)S(1)}, u32[]{:S(2)}, u32[]{:S(2)}) collective-permute-start(bf16[128,512]{1,0:T(8,128)(2,1)} %pad_maximum_fusion.3), channel_id=1, source_target_pairs={{0,1},{1,2},{2,3},{3,4},{4,5},{5,6},{6,7},{8,9},{9,10},{10,11},{11... | collective-permute-start | bytes 393224 | tf_op jit(solution)/shard_map/ppermute | solution.py:519
  23.1 2.4 %collective-permute-start.8 = (s32[512,26]{1,0:T(8,128)}, s32[512,26]{1,0:T(8,128)S(1)}, u32[]{:S(2)}, u32[]{:S(2)}) collective-permute-start(s32[512,26]{1,0:T(8,128)} %copy.37), channel_id=1, source_target_pairs={{0,1},{1,0},{2,3},{3,2},{4,5},{5,4},{6,7},{7,6},{8,9},{9,8},{10,11... | collective-permute-start | bytes 159752 | tf_op jit(solution)/shard_map/ppermute | solution.py:516
  23.1 7.3 %collective-permute-start.5 = (bf16[128,512]{1,0:T(8,128)(2,1)S(1)}, bf16[128,512]{1,0:T(8,128)(2,1)S(1)}, u32[]{:S(2)}, u32[]{:S(2)}) collective-permute-start(bf16[128,512]{1,0:T(8,128)(2,1)S(1)} %pad_maximum_fusion.4), channel_id=1, source_target_pairs={{1,0},{2,1},{3,2},{4,3},{5,4},{6,5},{7,6},{9,8},{10,9},{11,10},{12... | collective-permute-start | bytes 393224 | tf_op jit(solution)/shard_map/ppermute | solution.py:520
  32.1 17.8 %collective-permute-start.6 = (bf16[640,512]{1,0:T(8,128)(2,1)S(1)}, bf16[640,512]{1,0:T(8,128)(2,1)S(1)}, u32[]{:S(2)}, u32[]{:S(2)}) collective-permute-start(bf16[640,512]{1,0:T(8,128)(2,1)S(1)} %collective-permute-done.2.refs_3_.refs_4_), channel_id=1, source_target_pairs={{0,4},{1,3},{4,8},{5,1},{8,12},{9,5},{12,14},{13,9},{14,10},{15,13... | collective-permute-start | bytes 1966088 | tf_op jit(solution)/shard_map/ppermute | solution.py:491
  32.2 17.8 %collective-permute-start.7 = (bf16[640,512]{1,0:T(8,128)(2,1)S(1)}, bf16[640,512]{1,0:T(8,128)(2,1)S(1)}, u32[]{:S(2)}, u32[]{:S(2)}) collective-permute-start(bf16[640,512]{1,0:T(8,128)(2,1)S(1)} %collective-permute-done.3.refs_6_.refs_7_), channel_id=1, source_target_pairs={{0,2},{1,5},{4,0},{5,9},{8,4},{9,13},{12,8},{13,15},{14,12},{15,11... | collective-permute-start | bytes 1966088 | tf_op jit(solution)/shard_map/ppermute | solution.py:493
  35.8 0.8 copy-start.7
  36.6 13.3 %collective-permute-start.9 = (bf16[896,256]{1,0:T(8,128)(2,1)}, bf16[896,256]{1,0:T(8,128)(2,1)S(1)}, u32[]{:S(2)}, u32[]{:S(2)}) collective-permute-start(bf16[896,256]{1,0:T(8,128)(2,1)} %get-tuple-element.64), channel_id=1, source_target_pairs={{0,1},{1,0},{2,3},{3,2},{4,5},{5,4},{6,7},{7,6},{8,9},{9,8},{10,11... | collective-permute-start | bytes 1376264 | tf_op jit(solution)/shard_map/ppermute | solution.py:555
  38.1 31.1 %collective-permute-start.13 = (bf16[448,512]{1,0:T(8,128)(2,1)}, bf16[448,512]{1,0:T(8,128)(2,1)S(1)}, u32[]{:S(2)}, u32[]{:S(2)}) collective-permute-start(bf16[448,512]{1,0:T(8,128)(2,1)} %pad_maximum_fusion.1), channel_id=1, source_target_pairs={{0,16},{16,0},{1,17},{17,1},{2,18},{18,2},{3,19},{19,3},{4,20},{20... | collective-permute-start | bytes 1376264 | tf_op jit(solution)/shard_map/ppermute | solution.py:499
  49.9 0.8 copy-start.13
  50.7 14.5 %collective-permute-start.10 = (bf16[640,512]{1,0:T(8,128)(2,1)S(1)}, bf16[640,512]{1,0:T(8,128)(2,1)S(1)}, u32[]{:S(2)}, u32[]{:S(2)}) collective-permute-start(bf16[640,512]{1,0:T(8,128)(2,1)S(1)} %collective-permute-done.6.refs_1_.refs_2_), channel_id=1, source_target_pairs={{0,4},{1,3},{4,8},{5,1},{8,12},{9,5},{12,14},{13,9},{14,10},{15,13... | collective-permute-start | bytes 1966088 | tf_op jit(solution)/shard_map/ppermute | solution.py:491
  50.8 16.3 %collective-permute-start.11 = (bf16[640,512]{1,0:T(8,128)(2,1)S(1)}, bf16[640,512]{1,0:T(8,128)(2,1)}, u32[]{:S(2)}, u32[]{:S(2)}) collective-permute-start(bf16[640,512]{1,0:T(8,128)(2,1)S(1)} %collective-permute-done.7.refs_4_.refs_5_), channel_id=1, source_target_pairs={{0,2},{1,5},{4,0},{5,9},{8,4},{9,13},{12,8},{13,15},{14,12},{15,11... | collective-permute-start | bytes 1966088 | tf_op jit(solution)/shard_map/ppermute | solution.py:493
  53.4 11.8 %collective-permute-start.12 = (bf16[448,512]{1,0:T(8,128)(2,1)}, bf16[448,512]{1,0:T(8,128)(2,1)}, u32[]{:S(2)}, u32[]{:S(2)}) collective-permute-start(bf16[448,512]{1,0:T(8,128)(2,1)} %pad_maximum_fusion), channel_id=1, source_target_pairs={{0,16},{16,0},{1,17},{17,1},{2,18},{18,2},{3,19},{19,3},{4,20},{20... | collective-permute-start | bytes 1376264 | tf_op jit(solution)/shard_map/ppermute | solution.py:499
  64.3 5.0 %copy-start.2 = (bf16[864,512]{1,0:T(8,128)(2,1)S(1)}, bf16[864,512]{1,0:T(8,128)(2,1)}, u32[]{:S(2)}) copy-start(bf16[864,512]{1,0:T(8,128)(2,1)} %copy-done.1) | copy-start | bytes 2654212
  67.1 10.0 %collective-permute-start.14 = (bf16[640,512]{1,0:T(8,128)(2,1)S(1)}, bf16[640,512]{1,0:T(8,128)(2,1)S(1)}, u32[]{:S(2)}, u32[]{:S(2)}) collective-permute-start(bf16[640,512]{1,0:T(8,128)(2,1)S(1)} %collective-permute-done.10.refs_1_.refs_2_), channel_id=1, source_target_pairs={{0,4},{1,3},{4,8},{5,1},{8,12},{9,5},{12,14},{13,9},{14,10},{15,13... | collective-permute-start | bytes 1966088 | tf_op jit(solution)/shard_map/ppermute | solution.py:491
  69.0 13.4 %collective-permute-start.16 = (bf16[448,512]{1,0:T(8,128)(2,1)S(1)}, bf16[448,512]{1,0:T(8,128)(2,1)S(1)}, u32[]{:S(2)}, u32[]{:S(2)}) collective-permute-start(bf16[448,512]{1,0:T(8,128)(2,1)S(1)} %pad_maximum_fusion.2), channel_id=1, source_target_pairs={{0,16},{16,0},{1,17},{17,1},{2,18},{18,2},{3,19},{19,3},{4,20},{20... | collective-permute-start | bytes 1376264 | tf_op jit(solution)/shard_map/ppermute | solution.py:499
  77.1 9.7 %collective-permute-start.15 = (bf16[224,512]{1,0:T(8,128)(2,1)S(1)}, bf16[224,512]{1,0:T(8,128)(2,1)S(1)}, u32[]{:S(2)}, u32[]{:S(2)}) collective-permute-start(bf16[224,512]{1,0:T(8,128)(2,1)S(1)} %slice.94), channel_id=1, source_target_pairs={{0,16},{16,0},{1,17},{17,1},{2,18},{18,2},{3,19},{19,3},{4,20},{20... | collective-permute-start | bytes 688136 | tf_op jit(solution)/shard_map/ppermute | solution.py:499
  86.8 5.7 %copy-start.10 = (s32[512]{0:T(512)S(1)}, s32[512]{0:T(512)}, u32[]{:S(2)}) copy-start(s32[512]{0:T(512)} %param.27) | copy-start | bytes 6148
  86.8 7.2 %copy-start.4 = (bf16[512,512]{1,0:T(8,128)(2,1)S(1)}, bf16[512,512]{1,0:T(8,128)(2,1)}, u32[]{:S(2)}) copy-start(bf16[512,512]{1,0:T(8,128)(2,1)} %features_ref.3) | copy-start | bytes 1572868
  86.8 7.2 %copy-start.5 = (bf16[512,512]{1,0:T(8,128)(2,1)S(1)}, bf16[512,512]{1,0:T(8,128)(2,1)}, u32[]{:S(2)}) copy-start(bf16[512,512]{1,0:T(8,128)(2,1)} %weight_ref.1) | copy-start | bytes 1572868
  86.8 7.2 %copy-start.6 = (f32[512]{0:T(512)S(1)}, f32[512]{0:T(512)}, u32[]{:S(2)}) copy-start(f32[512]{0:T(512)} %param.18) | copy-start | bytes 6148
  89.5 4.4 %collective-permute-start.17 = (bf16[512,512]{1,0:T(8,128)(2,1)S(1)}, bf16[512,512]{1,0:T(8,128)(2,1)S(1)}, u32[]{:S(2)}, u32[]{:S(2)}) collective-permute-start(bf16[512,512]{1,0:T(8,128)(2,1)S(1)} %get-tuple-element.86), channel_id=1, source_target_pairs={{0,1},{1,0},{2,3},{3,2},{4,5},{5,4},{6,7},{7,6},{8,9},{9,8},{10,11... | collective-permute-start | bytes 1572872 | tf_op jit(solution)/shard_map/ppermute | solution.py:592
  94.0 7.7 %copy-start.8 = (bf16[512,1536]{1,0:T(8,128)(2,1)S(1)}, bf16[512,1536]{1,0:T(8,128)(2,1)}, u32[]{:S(2)}) copy-start(bf16[512,1536]{1,0:T(8,128)(2,1)} %param.20) | copy-start | bytes 4718596
  96.3 30.3 %all-to-all-start = ((bf16[16,64,512]{2,1,0:T(8,128)(2,1)}), bf16[16,64,512]{2,1,0:T(8,128)(2,1)}, u32[]{:S(2)}, u32[]{:S(2)}) async-start(bf16[16,64,512]{2,1,0:T(8,128)(2,1)} %bitcast.11), calls=%async_computation | async-start | bytes 2097152 | tf_op jit(solution)/shard_map/all_to_all | solution.py:608
  101.6 1.3 copy-start.12
  103.3 23.3 %copy-start.11 = (s32[512]{0:T(512)}, s32[512]{0:T(512)S(1)}, u32[]{:S(2)}) copy-start(s32[512]{0:T(512)S(1)} %multiply_add_fusion) | copy-start | bytes 6148
  148.2 29.8 %all-to-all-start.1 = ((bf16[16,64,512]{2,1,0:T(8,128)(2,1)}), bf16[16,64,512]{2,1,0:T(8,128)(2,1)S(1)}, u32[]{:S(2)}, u32[]{:S(2)}) async-start(bf16[16,64,512]{2,1,0:T(8,128)(2,1)} %bitcast.30), calls=%async_computation.1 | async-start | bytes 2097152 | tf_op jit(solution)/shard_map/all_to_all | solution.py:641

commit v18 on v17

--- a/solution.py
+++ b/solution.py
@@ -116,16 +116,23 @@
         )
     places = lax.broadcasted_iota(jnp.int32, (1, 256), 1).astype(F32).astype(BF16)
     one, zero = jnp.ones((), BF16), jnp.zeros((), BF16)
-    for at in range(taps):
-        chosen = lane == taps * pl.program_id(0) + at
-        column = jnp.sum(jnp.where(chosen, rows_ref[...], 0.0), axis=1, keepdims=True)
+    together = 3
+    for base in range(0, taps, together):
+        columns = []
+        for at in range(base, base + together):
+            chosen = lane == taps * pl.program_id(0) + at
+            columns.append(jnp.sum(jnp.where(chosen, rows_ref[...], 0.0), axis=1, keepdims=True))
+        column = jnp.concatenate(columns, axis=0)
         taken = None
         for first, end, start in segments:
             place = jnp.clip(column - start, -1.0, 256.0).astype(BF16)
             hits = jnp.where(place == places[:, : end - first], one, zero)
             product = dot(hits, table_ref[first:end])
             taken = product if taken is None else taken + product
-        out_ref[:, at * half : (at + 1) * half] = taken.astype(BF16)
+        taken = taken.astype(BF16)
+        for at in range(together):
+            column_block = slice((base + at) * half, (base + at + 1) * half)
+            out_ref[:, column_block] = taken[at * points : (at + 1) * points]
 
 
 def gather_block(start, rows, table):
@@ -204,8 +211,10 @@
     for at in range(len(slots)):
         for copy in copies[at]:
             copy.wait()
+        points = lhs.shape[2]
+        products = dot(lhs[at].reshape(2 * points, length), held[at])
         for block, ref in enumerate(outs):
-            product = dot(lhs[at, block], held[at])
+            product = products[block * points : (block + 1) * points]
             if at > 0:
                 ref[...] += product
             elif first:

time: 180 us -> 182 us (1.011)
  Pallas kernels: 68.3 us -> 71.2 us
    pallas_call x2, Pallas kernels: 21.2 us -> 24.1 us  [gather_block(): call(functools.partial(gather_kernel, taps), jax.ShapeDtypeStruct((points...]
  transfers between devices with their start and end apart: 20 -> 20, of which waited for: 11 -> 9; matrix products, arithmetic and copies ran while one was open for 8% -> 8% of each run, Pallas kernels for 22% -> 23%
where the time goes in v18:
time: 182 us; the launch traced here: 181 us
  Pallas kernels  71.2 us (39%)
  waiting for transfers between devices  58.5 us (32%)
  starting transfers between devices  31.3 us (17%)
  local copies, waits for them, and re-layouts  12.6 us (7%)
  other arithmetic  7.1 us (4%)
    all_to_all x1, waiting for transfers between devices, body(): lax.all_to_all(back.reshape(devices, capacity, width), 'blocks', split_ax...  24.7 us
    pallas_call x2, Pallas kernels, gather_block(): call(functools.partial(gather_kernel, taps), jax.ShapeDtypeStruct((points...  24.1 us
    pallas_call x1, Pallas kernels, body(): call(block_kernel, jax.ShapeDtypeStruct((slots, width), BF16), 60, 20 * p...  21.6 us
    all_to_all x1, waiting for transfers between devices, body(): lax.all_to_all(outgoing.reshape(devices, capacity, width), 'blocks', spli...  21.4 us
    pallas_call x4, Pallas kernels, conv_part(): call(functools.partial(conv_kernel, slots, later, ready, before is None),...  18.8 us
    ppermute x3, starting transfers between devices, pass_on(): second.append(lax.ppermute(second[-1], 'blocks', second_pairs))  5.33 us
    all_to_all x1, starting transfers between devices, body(): lax.all_to_all(outgoing.reshape(devices, capacity, width), 'blocks', spli...  5.3 us
    all_to_all x1, starting transfers between devices, body(): lax.all_to_all(back.reshape(devices, capacity, width), 'blocks', split_ax...  5 us
  transfers between devices with their start and end apart: 20, of which 9 were waited for; matrix products, arithmetic and copies ran while one was open for 8% of the time, Pallas kernels for 23%

profile of v18, /device:TPU:9, one launch (start us, length us, event | category | flops | bytes accessed | tf_op | source)
XLA Modules:
  0.0 181.0 jit_solution(17414496500276337703)
XLA Ops:
  0.0 1.1 slice.69
  1.1 0.7 collective-permute-start
  1.9 0.7 slice_bitcast_fusion
  2.6 0.8 select_bitcast_fusion
  3.3 0.1 reshape.66.rows_ref
  3.5 1.0 copy-done.3
  4.5 0.7 shard_map.146
  5.4 0.7 shard_map.145
  6.0 0.9 copy-done.1
  7.0 2.3 %collective-permute-start.1 = (bf16[192,512]{1,0:T(8,128)(2,1)S(1)}, bf16[192,512]{1,0:T(8,128)(2,1)S(1)}, u32[]{:S(2)}, u32[]{:S(2)}) collective-permute-start(bf16[192,512]{1,0:T(8,128)(2,1)S(1)} %get-tuple-element.48), channel_id=1, source_target_pairs={{0,8},{1,9},{2,10},{3,11},{4,12},{5,13},{6,14},{7,15},{8,0},{9,1},... | collective-permute-start | bytes 589832 | tf_op jit(solution)/shard_map/ppermute | solution.py:522
  9.3 0.7 constant_dynamic-slice_fusion
  10.0 0.9 copy.35
  10.9 0.9 copy.36
  11.9 0.2 collective-permute-start.2
  12.1 1.3 collective-permute-start.3
  13.4 4.7 %collective-permute-done.1.side_ref = bf16[192,512]{1,0:T(8,128)(2,1)S(1)} collective-permute-done((bf16[192,512]{1,0:T(8,128)(2,1)S(1)}, bf16[192,512]{1,0:T(8,128)(2,1)S(1)}, u32[]{:S(2)}, u32[]{:S(2)}) %collective-permute-start.1) | collective-permute-done | bytes 196640 | tf_op jit(solution)/shard_map/ppermute | solution.py:522
  18.1 0.6 pad_maximum_fusion.3
  18.8 3.5 %collective-permute-start.4 = (bf16[128,512]{1,0:T(8,128)(2,1)}, bf16[128,512]{1,0:T(8,128)(2,1)S(1)}, u32[]{:S(2)}, u32[]{:S(2)}) collective-permute-start(bf16[128,512]{1,0:T(8,128)(2,1)} %pad_maximum_fusion.3), channel_id=1, source_target_pairs={{0,1},{1,2},{2,3},{3,4},{4,5},{5,6},{6,7},{8,9},{9,10},{10,11},{11... | collective-permute-start | bytes 393224 | tf_op jit(solution)/shard_map/ppermute | solution.py:528
  22.3 0.8 copy.37
  23.1 2.4 %collective-permute-start.5 = (bf16[128,512]{1,0:T(8,128)(2,1)S(1)}, bf16[128,512]{1,0:T(8,128)(2,1)S(1)}, u32[]{:S(2)}, u32[]{:S(2)}) collective-permute-start(bf16[128,512]{1,0:T(8,128)(2,1)S(1)} %pad_maximum_fusion.4), channel_id=1, source_target_pairs={{1,0},{2,1},{3,2},{4,3},{5,4},{6,5},{7,6},{9,8},{10,9},{11,10},{12... | collective-permute-start | bytes 393224 | tf_op jit(solution)/shard_map/ppermute | solution.py:529
  25.6 0.1 fusion.6
  25.7 2.1 %add_convert_fusion.1 = (f32[512,128]{1,0:T(8,128)}, f32[512,128]{1,0:T(8,128)}) fusion(s32[512,13]{1,0:T(8,128)S(1)} %get-tuple-element.93, s32[512,13]{1,0:T(8,128)S(1)} %get-tuple-element.92, s32[512,1]{1,0:T(8,128)S(1)} %iota.13, s32[128]{0:T(128)S(1)} %pad.17.clone, s32[512,13]{1,0:T(8,128)} %copy.36, s32[512,13]{1,0:T(8,128)} %copy.35), kind=kLoop, calls=%fused_computation.9 | loop fusion | flops 524288 | bytes 633344 | tf_op jit(solution)/shard_map/convert_element_type | solution.py:417
  27.9 2.5 %collective-permute-done.5.ahead_ref = bf16[128,512]{1,0:T(8,128)(2,1)S(1)} collective-permute-done((bf16[128,512]{1,0:T(8,128)(2,1)S(1)}, bf16[128,512]{1,0:T(8,128)(2,1)S(1)}, u32[]{:S(2)}, u32[]{:S(2)}) %collective-permute-start.5) | collective-permute-done | bytes 131104 | tf_op jit(solution)/shard_map/ppermute | solution.py:529
  30.4 1.4 collective-permute-done.2.refs_3_.refs_4_
  31.8 0.3 collective-permute-done.3.refs_6_.refs_7_
  32.2 2.3 %collective-permute-start.7 = (bf16[640,512]{1,0:T(8,128)(2,1)S(1)}, bf16[640,512]{1,0:T(8,128)(2,1)S(1)}, u32[]{:S(2)}, u32[]{:S(2)}) collective-permute-start(bf16[640,512]{1,0:T(8,128)(2,1)S(1)} %collective-permute-done.3.refs_6_.refs_7_), channel_id=1, source_target_pairs={{0,2},{1,5},{4,0},{5,9},{8,4},{9,13},{12,8},{13,15},{14,12},{15,11... | collective-permute-start | bytes 1966088 | tf_op jit(solution)/shard_map/ppermute | solution.py:502
  34.4 1.4 shard_map.147
  35.8 0.8 copy-done.7
  36.6 0.7 collective-permute-start.9
  37.3 0.8 pad_maximum_fusion.1
  38.1 1.2 collective-permute-start.13
  39.3 12.0 %shard_map.148.refs_1_ = bf16[512,6912]{1,0:T(8,128)(2,1)} custom-call(s32[1]{0:T(128)} %bitcast.7.start_ref, f32[512,128]{1,0:T(8,128)} %get-tuple-element.91.rows_ref, bf16[896,256]{1,0:T(8,128)(2,1)} %copy-done.7), custom_call_target="tpu_custom_call" | custom-call | flops 6341787648 | bytes 7077888 | tf_op jit(solution)/shard_map/pallas_call | solution.py:143
  51.4 0.7 copy-done.13
  52.2 1.8 collective-permute-start.11
  54.0 0.8 pad_maximum_fusion
  54.8 0.3 collective-permute-start.12
  55.1 12.1 %shard_map.149.refs_0_ = bf16[512,6912]{1,0:T(8,128)(2,1)} custom-call(s32[1]{0:T(128)} %bitcast.7.start_ref, f32[512,128]{1,0:T(8,128)} %get-tuple-element.67.rows_ref, bf16[896,256]{1,0:T(8,128)(2,1)} %copy-done.13), custom_call_target="tpu_custom_call" | custom-call | flops 6341787648 | bytes 7077888 | tf_op jit(solution)/shard_map/pallas_call | solution.py:143
  67.2 1.3 collective-permute-done.11.refs_4_.refs_5_
  68.5 0.6 collective-permute-start.14
  69.4 1.0 slice.87
  70.4 0.3 collective-permute-start.16
  70.7 6.9 %shard_map.150 = (f32[512,512]{1,0:T(8,128)S(1)}, f32[512,512]{1,0:T(8,128)S(1)}, bf16[2,2,512,1024]{3,2,1,0:T(8,128)(2,1)S(1)}, bf16[2,2,512,1024]{3,2,1,0:T(8,128)(2,1)S(1)}, bf16[1,2,512,1024]{3,2,1,0:T(8,128)(2,1)S(1)}) custom-call(s32[16]{0:T(128)S(1)} %reshape_squeeze.3.places_ref, s32[2]{0:T(128)S(1)} %pad_add_fusion.2.shifts_ref, ...), custom_call_target="tpu_custom_call" | custom-call | flops 3221225472 | bytes 9437184 | tf_op jit(solution)/shard_map/pallas_call | solution.py:237
  77.7 0.9 collective-permute-done.14.refs_1_.refs_2_
  78.6 0.4 collective-permute-start.15
  79.0 4.7 %shard_map.151 = (f32[512,512]{1,0:T(8,128)S(1)}, f32[512,512]{1,0:T(8,128)S(1)}) custom-call(s32[4]{0:T(128)S(1)} %get-tuple-element.98.places_ref, s32[2]{0:T(128)S(1)} %pad_add_fusion.2.shifts_ref, bf16[2,2,512,1024]{3,2,1,0:T(8,128)(2,1)S(1)} %get-tuple-element.77.refs_0_, ...), custom_call_target="tpu_custom_call", output_to_operand_aliasing={{0}: (9, {}), {1}: (10, {})} | custom-call | flops 2147483648 | bytes 6291456 | tf_op jit(solution)/shard_map/pallas_call | solution.py:237
  83.8 4.4 %shard_map.152 = (f32[512,512]{1,0:T(8,128)S(1)}, f32[512,512]{1,0:T(8,128)S(1)}) custom-call(s32[4]{0:T(128)S(1)} %get-tuple-element.99.places_ref, s32[2]{0:T(128)S(1)} %pad_add_fusion.2.shifts_ref, bf16[2,2,512,1024]{3,2,1,0:T(8,128)(2,1)S(1)} %get-tuple-element.75.refs_0_, ...), custom_call_target="tpu_custom_call", output_to_operand_aliasing={{0}: (9, {}), {1}: (10, {})} | custom-call | flops 2147483648 | bytes 6291456 | tf_op jit(solution)/shard_map/pallas_call | solution.py:237
  88.3 2.7 %shard_map.153 = (bf16[512,512]{1,0:T(8,128)(2,1)S(1)}, f32[512,512]{1,0:T(8,128)S(1)}) custom-call(s32[2]{0:T(128)S(1)} %slice.73.places_ref, s32[2]{0:T(128)S(1)} %pad_add_fusion.2.shifts_ref, bf16[1,2,512,1024]{3,2,1,0:T(8,128)(2,1)S(1)} %get-tuple-element.73.refs_0_, ...), custom_call_target="tpu_custom_call", output_to_operand_aliasing={{1}: (7, {})} | custom-call | flops 1073741824 | bytes 3145728 | tf_op jit(solution)/shard_map/pallas_call | solution.py:237
  91.0 2.9 %collective-permute-start.17 = (bf16[512,512]{1,0:T(8,128)(2,1)S(1)}, bf16[512,512]{1,0:T(8,128)(2,1)S(1)}, u32[]{:S(2)}, u32[]{:S(2)}) collective-permute-start(bf16[512,512]{1,0:T(8,128)(2,1)S(1)} %get-tuple-element.86), channel_id=1, source_target_pairs={{0,1},{1,0},{2,3},{3,2},{4,5},{5,4},{6,7},{7,6},{8,9},{9,8},{10,11... | collective-permute-start | bytes 1572872 | tf_op jit(solution)/shard_map/ppermute | solution.py:601
  93.9 0.3 convert_reduce_fusion.1
  94.3 1.2 collective-permute-done.17.got_ref
  95.4 2.3 %shard_map.154 = bf16[1024,512]{1,0:T(8,128)(2,1)} custom-call(f32[512,512]{1,0:T(8,128)S(1)} %get-tuple-element.85.own_ref, bf16[512,512]{1,0:T(8,128)(2,1)S(1)} %collective-permute-done.17.got_ref, bf16[512,512]{1,0:T(8,128)(2,1)S(1)} %copy-done.4, bf16[512,512]{1,0:T(8,128)(2,1)S(1)} %copy-done.5, f32[1,512]{1,0:T(1,128)S(1)} %bitcast.29, ...), custom_call_target="tpu_custom_call" | custom-call | flops 805306368 | bytes 2097152 | tf_op jit(solution)/shard_map/pallas_call | solution.py:603
  97.8 5.3 %all-to-all-start = ((bf16[16,64,512]{2,1,0:T(8,128)(2,1)}), bf16[16,64,512]{2,1,0:T(8,128)(2,1)}, u32[]{:S(2)}, u32[]{:S(2)}) async-start(bf16[16,64,512]{2,1,0:T(8,128)(2,1)} %bitcast.11), calls=%async_computation | async-start | bytes 2097152 | tf_op jit(solution)/shard_map/all_to_all | solution.py:617
  103.1 0.9 fusion.5
  104.0 0.2 copy.42
  104.2 0.2 copy.43
  104.4 0.2 convert_reduce_fusion
  104.7 0.9 copy.40.slot_col_ref
  105.6 1.0 maximum_bitcast_fusion.qv_hbm
  106.6 21.4 %all-to-all-done = bf16[16,64,512]{2,1,0:T(8,128)(2,1)} async-done(((bf16[16,64,512]{2,1,0:T(8,128)(2,1)}), bf16[16,64,512]{2,1,0:T(8,128)(2,1)}, u32[]{:S(2)}, u32[]{:S(2)}) %all-to-all-start) | async-done | bytes 1048608 | tf_op jit(solution)/shard_map/all_to_all | solution.py:617
  128.0 21.6 %shard_map.155 = bf16[1024,512]{1,0:T(8,128)(2,1)} custom-call(bf16[1024,512]{1,0:T(8,128)(2,1)} %bitcast.12.arrived_ref, s32[512,1]{1,0:T(8,128)} %copy.40.slot_col_ref, s32[1,512]{1,0:T(1,128)} %bitcast.32, f32[1,512]{1,0:T(1,128)} %bitcast.33, f32[1,512]{1,0:T(1,128)} %bitcast.34, bf16[1024,512]{1,0:T(8,128)(2,1)} %maximum_bitcast_fusion.qv_hbm, ...), custom_call_target="tpu_custom_call" | custom-call | flops 2684354560 | bytes 4194304 | tf_op jit(solution)/shard_map/pallas_call | solution.py:624
  149.6 5.0 %all-to-all-start.1 = ((bf16[16,64,512]{2,1,0:T(8,128)(2,1)}), bf16[16,64,512]{2,1,0:T(8,128)(2,1)S(1)}, u32[]{:S(2)}, u32[]{:S(2)}) async-start(bf16[16,64,512]{2,1,0:T(8,128)(2,1)} %bitcast.30), calls=%async_computation.1 | async-start | bytes 2097152 | tf_op jit(solution)/shard_map/all_to_all | solution.py:650
  154.6 0.1 copy.41.slot_ref
  154.8 24.7 %all-to-all-done.1 = bf16[16,64,512]{2,1,0:T(8,128)(2,1)S(1)} async-done(((bf16[16,64,512]{2,1,0:T(8,128)(2,1)}), bf16[16,64,512]{2,1,0:T(8,128)(2,1)S(1)}, u32[]{:S(2)}, u32[]{:S(2)}) %all-to-all-start.1) | async-done | bytes 1048608 | tf_op jit(solution)/shard_map/all_to_all | solution.py:650
  179.5 1.5 shard_map.156
  (62 shorter events, 0.9 us)
Async XLA Ops:
  0.0 5.3 %copy-start = (bf16[864,512]{1,0:T(8,128)(2,1)S(1)}, bf16[864,512]{1,0:T(8,128)(2,1)}, u32[]{:S(2)}) copy-start(bf16[864,512]{1,0:T(8,128)(2,1)} %param.16) | copy-start | bytes 2654212
  0.0 5.3 %copy-start.9 = (s32[512,26]{0,1:T(8,128)S(1)}, s32[512,26]{0,1:T(8,128)}, u32[]{:S(2)}) copy-start(s32[512,26]{0,1:T(8,128)} %param.26) | copy-start | bytes 159748
  1.1 4.2 %collective-permute-start = (bf16[13,32,512]{2,1,0:T(8,128)(2,1)S(1)}, bf16[13,32,512]{2,1,0:T(8,128)(2,1)S(1)}, u32[]{:S(2)}, u32[]{:S(2)}) collective-permute-start(bf16[13,32,512]{2,1,0:T(8,128)(2,1)S(1)} %slice.69), channel_id=1, source_target_pairs={{0,1},{1,0},{2,3},{3,2},{4,5},{5,4},{6,7},{7,6},{8,9},{9,8},{10,11... | collective-permute-start | bytes 1277960 | tf_op jit(solution)/shard_map/ppermute | solution.py:447
  3.5 1.0 copy-start.3
  6.0 0.9 copy-start.1
  7.0 11.1 %collective-permute-start.1 = (bf16[192,512]{1,0:T(8,128)(2,1)S(1)}, bf16[192,512]{1,0:T(8,128)(2,1)S(1)}, u32[]{:S(2)}, u32[]{:S(2)}) collective-permute-start(bf16[192,512]{1,0:T(8,128)(2,1)S(1)} %get-tuple-element.48), channel_id=1, source_target_pairs={{0,8},{1,9},{2,10},{3,11},{4,12},{5,13},{6,14},{7,15},{8,0},{9,1},... | collective-permute-start | bytes 589832 | tf_op jit(solution)/shard_map/ppermute | solution.py:522
  11.9 19.9 %collective-permute-start.2 = (bf16[640,512]{1,0:T(8,128)(2,1)S(1)}, bf16[640,512]{1,0:T(8,128)(2,1)S(1)}, u32[]{:S(2)}, u32[]{:S(2)}) collective-permute-start(bf16[640,512]{1,0:T(8,128)(2,1)S(1)} %get-tuple-element.51), channel_id=1, source_target_pairs={{0,4},{1,3},{4,8},{5,1},{8,12},{9,5},{12,14},{13,9},{14,10},{15,13... | collective-permute-start | bytes 1966088 | tf_op jit(solution)/shard_map/ppermute | solution.py:500
  12.1 20.1 %collective-permute-start.3 = (bf16[640,512]{1,0:T(8,128)(2,1)S(1)}, bf16[640,512]{1,0:T(8,128)(2,1)S(1)}, u32[]{:S(2)}, u32[]{:S(2)}) collective-permute-start(bf16[640,512]{1,0:T(8,128)(2,1)S(1)} %get-tuple-element.51), channel_id=1, source_target_pairs={{0,2},{1,5},{4,0},{5,9},{8,4},{9,13},{12,8},{13,15},{14,12},{15,11... | collective-permute-start | bytes 1966088 | tf_op jit(solution)/shard_map/ppermute | solution.py:502
  18.8 9.1 %collective-permute-start.4 = (bf16[128,512]{1,0:T(8,128)(2,1)}, bf16[128,512]{1,0:T(8,128)(2,1)S(1)}, u32[]{:S(2)}, u32[]{:S(2)}) collective-permute-start(bf16[128,512]{1,0:T(8,128)(2,1)} %pad_maximum_fusion.3), channel_id=1, source_target_pairs={{0,1},{1,2},{2,3},{3,4},{4,5},{5,6},{6,7},{8,9},{9,10},{10,11},{11... | collective-permute-start | bytes 393224 | tf_op jit(solution)/shard_map/ppermute | solution.py:528
  23.1 2.4 %collective-permute-start.8 = (s32[512,26]{1,0:T(8,128)}, s32[512,26]{1,0:T(8,128)S(1)}, u32[]{:S(2)}, u32[]{:S(2)}) collective-permute-start(s32[512,26]{1,0:T(8,128)} %copy.37), channel_id=1, source_target_pairs={{0,1},{1,0},{2,3},{3,2},{4,5},{5,4},{6,7},{7,6},{8,9},{9,8},{10,11... | collective-permute-start | bytes 159752 | tf_op jit(solution)/shard_map/ppermute | solution.py:525
  23.1 7.3 %collective-permute-start.5 = (bf16[128,512]{1,0:T(8,128)(2,1)S(1)}, bf16[128,512]{1,0:T(8,128)(2,1)S(1)}, u32[]{:S(2)}, u32[]{:S(2)}) collective-permute-start(bf16[128,512]{1,0:T(8,128)(2,1)S(1)} %pad_maximum_fusion.4), channel_id=1, source_target_pairs={{1,0},{2,1},{3,2},{4,3},{5,4},{6,5},{7,6},{9,8},{10,9},{11,10},{12... | collective-permute-start | bytes 393224 | tf_op jit(solution)/shard_map/ppermute | solution.py:529
  32.1 19.2 %collective-permute-start.6 = (bf16[640,512]{1,0:T(8,128)(2,1)S(1)}, bf16[640,512]{1,0:T(8,128)(2,1)S(1)}, u32[]{:S(2)}, u32[]{:S(2)}) collective-permute-start(bf16[640,512]{1,0:T(8,128)(2,1)S(1)} %collective-permute-done.2.refs_3_.refs_4_), channel_id=1, source_target_pairs={{0,4},{1,3},{4,8},{5,1},{8,12},{9,5},{12,14},{13,9},{14,10},{15,13... | collective-permute-start | bytes 1966088 | tf_op jit(solution)/shard_map/ppermute | solution.py:500
  32.2 19.2 %collective-permute-start.7 = (bf16[640,512]{1,0:T(8,128)(2,1)S(1)}, bf16[640,512]{1,0:T(8,128)(2,1)S(1)}, u32[]{:S(2)}, u32[]{:S(2)}) collective-permute-start(bf16[640,512]{1,0:T(8,128)(2,1)S(1)} %collective-permute-done.3.refs_6_.refs_7_), channel_id=1, source_target_pairs={{0,2},{1,5},{4,0},{5,9},{8,4},{9,13},{12,8},{13,15},{14,12},{15,11... | collective-permute-start | bytes 1966088 | tf_op jit(solution)/shard_map/ppermute | solution.py:502
  35.8 0.8 copy-start.7
  36.6 14.8 %collective-permute-start.9 = (bf16[896,256]{1,0:T(8,128)(2,1)}, bf16[896,256]{1,0:T(8,128)(2,1)S(1)}, u32[]{:S(2)}, u32[]{:S(2)}) collective-permute-start(bf16[896,256]{1,0:T(8,128)(2,1)} %get-tuple-element.64), channel_id=1, source_target_pairs={{0,1},{1,0},{2,3},{3,2},{4,5},{5,4},{6,7},{7,6},{8,9},{9,8},{10,11... | collective-permute-start | bytes 1376264 | tf_op jit(solution)/shard_map/ppermute | solution.py:564
  38.1 32.6 %collective-permute-start.13 = (bf16[448,512]{1,0:T(8,128)(2,1)}, bf16[448,512]{1,0:T(8,128)(2,1)S(1)}, u32[]{:S(2)}, u32[]{:S(2)}) collective-permute-start(bf16[448,512]{1,0:T(8,128)(2,1)} %pad_maximum_fusion.1), channel_id=1, source_target_pairs={{0,16},{16,0},{1,17},{17,1},{2,18},{18,2},{3,19},{19,3},{4,20},{20... | collective-permute-start | bytes 1376264 | tf_op jit(solution)/shard_map/ppermute | solution.py:508
  51.4 0.8 copy-start.13
  52.1 15.0 %collective-permute-start.10 = (bf16[640,512]{1,0:T(8,128)(2,1)S(1)}, bf16[640,512]{1,0:T(8,128)(2,1)S(1)}, u32[]{:S(2)}, u32[]{:S(2)}) collective-permute-start(bf16[640,512]{1,0:T(8,128)(2,1)S(1)} %collective-permute-done.6.refs_1_.refs_2_), channel_id=1, source_target_pairs={{0,4},{1,3},{4,8},{5,1},{8,12},{9,5},{12,14},{13,9},{14,10},{15,13... | collective-permute-start | bytes 1966088 | tf_op jit(solution)/shard_map/ppermute | solution.py:500
  52.2 16.3 %collective-permute-start.11 = (bf16[640,512]{1,0:T(8,128)(2,1)S(1)}, bf16[640,512]{1,0:T(8,128)(2,1)}, u32[]{:S(2)}, u32[]{:S(2)}) collective-permute-start(bf16[640,512]{1,0:T(8,128)(2,1)S(1)} %collective-permute-done.7.refs_4_.refs_5_), channel_id=1, source_target_pairs={{0,2},{1,5},{4,0},{5,9},{8,4},{9,13},{12,8},{13,15},{14,12},{15,11... | collective-permute-start | bytes 1966088 | tf_op jit(solution)/shard_map/ppermute | solution.py:502
  54.8 12.4 %collective-permute-start.12 = (bf16[448,512]{1,0:T(8,128)(2,1)}, bf16[448,512]{1,0:T(8,128)(2,1)}, u32[]{:S(2)}, u32[]{:S(2)}) collective-permute-start(bf16[448,512]{1,0:T(8,128)(2,1)} %pad_maximum_fusion), channel_id=1, source_target_pairs={{0,16},{16,0},{1,17},{17,1},{2,18},{18,2},{3,19},{19,3},{4,20},{20... | collective-permute-start | bytes 1376264 | tf_op jit(solution)/shard_map/ppermute | solution.py:508
  67.2 3.5 %copy-start.2 = (bf16[864,512]{1,0:T(8,128)(2,1)S(1)}, bf16[864,512]{1,0:T(8,128)(2,1)}, u32[]{:S(2)}) copy-start(bf16[864,512]{1,0:T(8,128)(2,1)} %copy-done.1) | copy-start | bytes 2654212
  68.5 10.0 %collective-permute-start.14 = (bf16[640,512]{1,0:T(8,128)(2,1)S(1)}, bf16[640,512]{1,0:T(8,128)(2,1)S(1)}, u32[]{:S(2)}, u32[]{:S(2)}) collective-permute-start(bf16[640,512]{1,0:T(8,128)(2,1)S(1)} %collective-permute-done.10.refs_1_.refs_2_), channel_id=1, source_target_pairs={{0,4},{1,3},{4,8},{5,1},{8,12},{9,5},{12,14},{13,9},{14,10},{15,13... | collective-permute-start | bytes 1966088 | tf_op jit(solution)/shard_map/ppermute | solution.py:500
  70.4 13.3 %collective-permute-start.16 = (bf16[448,512]{1,0:T(8,128)(2,1)S(1)}, bf16[448,512]{1,0:T(8,128)(2,1)S(1)}, u32[]{:S(2)}, u32[]{:S(2)}) collective-permute-start(bf16[448,512]{1,0:T(8,128)(2,1)S(1)} %pad_maximum_fusion.2), channel_id=1, source_target_pairs={{0,16},{16,0},{1,17},{17,1},{2,18},{18,2},{3,19},{19,3},{4,20},{20... | collective-permute-start | bytes 1376264 | tf_op jit(solution)/shard_map/ppermute | solution.py:508
  78.6 9.6 %collective-permute-start.15 = (bf16[224,512]{1,0:T(8,128)(2,1)S(1)}, bf16[224,512]{1,0:T(8,128)(2,1)S(1)}, u32[]{:S(2)}, u32[]{:S(2)}) collective-permute-start(bf16[224,512]{1,0:T(8,128)(2,1)S(1)} %slice.94), channel_id=1, source_target_pairs={{0,16},{16,0},{1,17},{17,1},{2,18},{18,2},{3,19},{19,3},{4,20},{20... | collective-permute-start | bytes 688136 | tf_op jit(solution)/shard_map/ppermute | solution.py:508
  88.2 5.7 %copy-start.10 = (s32[512]{0:T(512)S(1)}, s32[512]{0:T(512)}, u32[]{:S(2)}) copy-start(s32[512]{0:T(512)} %param.27) | copy-start | bytes 6148
  88.2 7.2 %copy-start.4 = (bf16[512,512]{1,0:T(8,128)(2,1)S(1)}, bf16[512,512]{1,0:T(8,128)(2,1)}, u32[]{:S(2)}) copy-start(bf16[512,512]{1,0:T(8,128)(2,1)} %features_ref.3) | copy-start | bytes 1572868
  88.2 7.2 %copy-start.5 = (bf16[512,512]{1,0:T(8,128)(2,1)S(1)}, bf16[512,512]{1,0:T(8,128)(2,1)}, u32[]{:S(2)}) copy-start(bf16[512,512]{1,0:T(8,128)(2,1)} %weight_ref.1) | copy-start | bytes 1572868
  88.2 7.2 %copy-start.6 = (f32[512]{0:T(512)S(1)}, f32[512]{0:T(512)}, u32[]{:S(2)}) copy-start(f32[512]{0:T(512)} %param.18) | copy-start | bytes 6148
  91.0 4.5 %collective-permute-start.17 = (bf16[512,512]{1,0:T(8,128)(2,1)S(1)}, bf16[512,512]{1,0:T(8,128)(2,1)S(1)}, u32[]{:S(2)}, u32[]{:S(2)}) collective-permute-start(bf16[512,512]{1,0:T(8,128)(2,1)S(1)} %get-tuple-element.86), channel_id=1, source_target_pairs={{0,1},{1,0},{2,3},{3,2},{4,5},{5,4},{6,7},{7,6},{8,9},{9,8},{10,11... | collective-permute-start | bytes 1572872 | tf_op jit(solution)/shard_map/ppermute | solution.py:601
  95.4 7.6 %copy-start.8 = (bf16[512,1536]{1,0:T(8,128)(2,1)S(1)}, bf16[512,1536]{1,0:T(8,128)(2,1)}, u32[]{:S(2)}) copy-start(bf16[512,1536]{1,0:T(8,128)(2,1)} %param.20) | copy-start | bytes 4718596
  97.8 30.2 %all-to-all-start = ((bf16[16,64,512]{2,1,0:T(8,128)(2,1)}), bf16[16,64,512]{2,1,0:T(8,128)(2,1)}, u32[]{:S(2)}, u32[]{:S(2)}) async-start(bf16[16,64,512]{2,1,0:T(8,128)(2,1)} %bitcast.11), calls=%async_computation | async-start | bytes 2097152 | tf_op jit(solution)/shard_map/all_to_all | solution.py:617
  103.1 1.3 copy-start.12
  104.7 23.3 %copy-start.11 = (s32[512]{0:T(512)}, s32[512]{0:T(512)S(1)}, u32[]{:S(2)}) copy-start(s32[512]{0:T(512)S(1)} %multiply_add_fusion) | copy-start | bytes 6148
  149.6 29.8 %all-to-all-start.1 = ((bf16[16,64,512]{2,1,0:T(8,128)(2,1)}), bf16[16,64,512]{2,1,0:T(8,128)(2,1)S(1)}, u32[]{:S(2)}, u32[]{:S(2)}) async-start(bf16[16,64,512]{2,1,0:T(8,128)(2,1)} %bitcast.30), calls=%async_computation.1 | async-start | bytes 2097152 | tf_op jit(solution)/shard_map/all_to_all | solution.py:650

commit v19 on v17

--- a/solution.py
+++ b/solution.py
@@ -18,6 +18,7 @@
 F32 = jnp.float32
 BF16 = jnp.bfloat16
 MIB = 1 << 20
+GATHER_LIMIT, CONV_LIMIT = 24, 24
 
 
 def dot(left, right):
@@ -136,7 +137,7 @@
     return call(
         functools.partial(gather_kernel, taps),
         jax.ShapeDtypeStruct((points, TAPS * half), BF16),
-        60,
+        GATHER_LIMIT,
         2 * TAPS * points * height * half,
         2 * TAPS * points * half,
         grid=(TAPS // taps,),
@@ -149,7 +150,7 @@
     )(start, rows, table)
 
 
-def conv_kernel(slots, later, ready, first, places_ref, shifts_ref, *refs):
+def conv_kernel(slots, first, places_ref, shifts_ref, *refs):
     refs = list(refs)
 
     def take(count):
@@ -157,31 +158,16 @@
         del refs[:count]
         return taken
 
-    sources = take(1 if ready else 2)
+    stacked = take(2)
     pieces = take(sum(len(parts) for parts in slots))
     before = [] if first else take(2)
     outs = take(2)
-    kept = take(len(later))
-    (lhs,) = sources if ready else take(1)
-    held, sems = take(2)
+    held, sems = refs
     length = held.shape[1]
-
-    def stretch(slot, target, sem):
-        column = pl.multiple_of(places_ref[2 * slot], 128)
-        copies = [
-            pltpu.make_async_copy(
-                stacked.at[:, pl.ds(column, length)], target.at[block], sem.at[block]
-            )
-            for block, stacked in enumerate(sources)
-        ]
-        for copy in copies:
-            copy.start()
-        return copies
-
     copies = []
     for at, parts in enumerate(slots):
         row = pl.multiple_of(places_ref[2 * at + 1], 16)
-        copies.append([] if ready else stretch(at, lhs.at[at], sems.at[at]))
+        copies.append([])
         edge = length - sum(size for _, size, _, _ in parts)
         if edge:
             held[at, :edge] = jnp.zeros((edge, held.shape[2]), BF16)
@@ -192,60 +178,50 @@
             (piece,) = pieces[:1]
             del pieces[:1]
             copy = pltpu.make_async_copy(
-                piece.at[pl.ds(start, size)], held.at[at, pl.ds(place, size)], sems.at[at, 2 + part]
+                piece.at[pl.ds(start, size)], held.at[at, pl.ds(place, size)], sems.at[at, part]
             )
             copy.start()
             copies[-1].append(copy)
-    extra, slot = [], len(slots)
-    for group, count in enumerate(later):
-        for place in range(count):
-            extra += stretch(slot, kept[group].at[place], sems.at[slot])
-            slot += 1
     for at in range(len(slots)):
         for copy in copies[at]:
             copy.wait()
+        column = pl.multiple_of(places_ref[2 * at], 128)
         for block, ref in enumerate(outs):
-            product = dot(lhs[at, block], held[at])
+            product = dot(stacked[block][:, pl.ds(column, length)], held[at])
             if at > 0:
                 ref[...] += product
             elif first:
                 ref[...] = product
             else:
                 ref[...] = (before[block][...] + product).astype(ref.dtype)
-    for copy in extra:
-        copy.wait()
-
-
-def conv_part(sources, places, shifts, pieces, before, length, later=(), dtype=F32):
-    ready = len(sources) == 1
-    points = sources[0].shape[2] if ready else sources[0].shape[0]
+
+
+def conv_part(stacked, places, shifts, pieces, before, length, limit, dtype=F32):
+    points = stacked[0].shape[0]
     width = pieces[0][0][0].shape[1]
     slots = [[part[1:] for part in parts] for parts in pieces]
     flat = [part[0] for parts in pieces for part in parts]
-    held = 2 + len(sources) + len(flat)
+    held = 4 + len(flat)
     kept = [] if before is None else [block for block in range(2) if block or dtype == F32]
-    spec = pl.BlockSpec(memory_space=pl.ANY)
     return call(
-        functools.partial(conv_kernel, slots, later, ready, before is None),
+        functools.partial(conv_kernel, slots, before is None),
         [
             jax.ShapeDtypeStruct((points, width), dtype),
             jax.ShapeDtypeStruct((points, width), F32),
-        ]
-        + [jax.ShapeDtypeStruct((count, 2, points, length), BF16) for count in later],
-        24 if ready else 36,
+        ],
+        limit,
         4 * points * length * width * len(slots),
         2 * length * (2 * points + width) * len(slots),
         in_specs=[pl.BlockSpec(memory_space=pltpu.SMEM)] * 2
-        + [pl.BlockSpec() if ready else spec] * len(sources)
-        + [spec] * len(flat)
+        + [pl.BlockSpec()] * 2
+        + [pl.BlockSpec(memory_space=pl.ANY)] * len(flat)
         + ([] if before is None else [pl.BlockSpec()] * 2),
         input_output_aliases={held + block: block for block in kept},
-        scratch_shapes=([] if ready else [pltpu.VMEM((len(slots), 2, points, length), BF16)])
-        + [
+        scratch_shapes=[
             pltpu.VMEM((len(slots), length, width), BF16),
-            pltpu.SemaphoreType.DMA((len(slots) + sum(later), 5)),
+            pltpu.SemaphoreType.DMA((len(slots), 3)),
         ],
-    )(places, shifts, *sources, *flat, *(before or ()))
+    )(places, shifts, *stacked, *flat, *(before or ()))
 
 
 def mix_kernel(own_ref, got_ref, features_ref, weight_ref, gain_ref, slot_ref, out_ref):
@@ -564,22 +540,20 @@
         *stacked, middle_got = pass_on(*stacked, middle[0][2][0])
         middle = [[*parts[:2], (middle_got, *parts[2][1:])] for parts in middle]
         early = [[(mine, 0, rows, 0, None)]] + near
-        *sums, middle_lhs, far_lhs, last_lhs = conv_part(
-            stacked, places, shifts, early, None, length, (2, 2, 1)
-        )
+        sums = conv_part(stacked, places[:6], shifts, early, None, length, CONV_LIMIT)
         far = complete(first[3], second[3])
         opposite = complete(first[4])
-        sums = conv_part([middle_lhs], places[6:10], shifts, middle, sums, length)
-        sums = conv_part([far_lhs], places[10:14], shifts, far, sums, length)
+        sums = conv_part(stacked, places[6:10], shifts, middle, sums, length, CONV_LIMIT)
+        sums = conv_part(stacked, places[10:14], shifts, far, sums, length, CONV_LIMIT)
         for_partner, own_part = conv_part(
-            [last_lhs], places[14:], shifts, opposite, sums, length, dtype=BF16
+            stacked, places[14:], shifts, opposite, sums, length, CONV_LIMIT, BF16
         )
     else:
         groups = [list(range(core, devices, 2)) for core in range(2)]
         weight = lax.all_gather(mine, "blocks", axis=0, tiled=True, axis_index_groups=groups)
         nowhere = jnp.zeros((2,), jnp.int32)
         whole = [[(weight, 0, weight.shape[0], 0, None)]]
-        for_partner, own_part = conv_part(stacked, nowhere, shifts, whole, None, length)
+        for_partner, own_part = conv_part(stacked, nowhere, shifts, whole, None, length, 48)
 
     positions = jnp.arange(points, dtype=jnp.int32)
     target = serial_rank // points

time: 180 us -> 181 us (level)
  waiting for transfers between devices: 59.9 us -> 66.2 us
  Pallas kernels: 68.3 us -> 62.9 us
  starting transfers between devices: 31.3 us -> 35.1 us
  other arithmetic: 7.1 us -> 4.67 us
    pallas_call x2, Pallas kernels: 21.2 us -> 16.9 us  [gather_block(): call(functools.partial(gather_kernel, taps), jax.ShapeDtypeStruct((points...]
    ppermute x4, starting transfers between devices: 2.21 us -> 5.46 us  [complete(): got = lax.ppermute(lent, 'groups', [(0, 1), (1, 0)])]
    ppermute x3, waiting for transfers between devices: 2.16 us -> 5.29 us  [pass_on(): second.append(lax.ppermute(second[-1], 'blocks', second_pairs))]
    unnamed x30 -> x24, local copies, waits for them, and re-layouts: 3.95 us -> 2.36 us
  transfers between devices with their start and end apart: 20 -> 20, of which waited for: 11 -> 13; matrix products, arithmetic and copies ran while one was open for 8% -> 7% of each run, Pallas kernels for 22% -> 19%
where the time goes in v19:
time: 181 us
  waiting for transfers between devices  66.2 us (37%)
  Pallas kernels  62.9 us (35%)
  starting transfers between devices  35.1 us (19%)
  local copies, waits for them, and re-layouts  11.5 us (6%)
  other arithmetic  4.67 us (3%)
    all_to_all x1, waiting for transfers between devices, body(): lax.all_to_all(back.reshape(devices, capacity, width), 'blocks', split_ax...  24.7 us
    pallas_call x1, Pallas kernels, body(): call(block_kernel, jax.ShapeDtypeStruct((slots, width), BF16), 60, 20 * p...  21.6 us
    all_to_all x1, waiting for transfers between devices, body(): lax.all_to_all(outgoing.reshape(devices, capacity, width), 'blocks', spli...  21.4 us
    pallas_call x4, Pallas kernels, conv_part(): call(functools.partial(conv_kernel, slots, before is None), [jax.ShapeDty...  18.6 us
    pallas_call x2, Pallas kernels, gather_block(): call(functools.partial(gather_kernel, taps), jax.ShapeDtypeStruct((points...  16.9 us
    all_to_all x1, starting transfers between devices, body(): lax.all_to_all(outgoing.reshape(devices, capacity, width), 'blocks', spli...  6.51 us
    ppermute x4, starting transfers between devices, complete(): got = lax.ppermute(lent, 'groups', [(0, 1), (1, 0)])  5.46 us
    ppermute x3, waiting for transfers between devices, pass_on(): second.append(lax.ppermute(second[-1], 'blocks', second_pairs))  5.29 us
  transfers between devices with their start and end apart: 20, of which 13 were waited for; matrix products, arithmetic and copies ran while one was open for 7% of the time, Pallas kernels for 19%

profile of v19, /device:TPU:9, one launch (start us, length us, event | category | flops | bytes accessed | tf_op | source)
XLA Modules:
  0.0 180.8 jit_solution(4082489427257534781)
XLA Ops:
  0.0 1.1 slice.72
  1.1 0.7 collective-permute-start
  1.9 0.7 slice_bitcast_fusion
  2.6 0.8 select_bitcast_fusion
  3.3 0.1 reshape.66.rows_ref
  3.5 1.0 copy-done.1
  4.5 0.7 shard_map.146
  5.3 0.6 fusion.8
  6.0 0.7 shard_map.145
  6.6 0.8 copy-done.5
  7.5 2.3 %collective-permute-start.1 = (bf16[192,512]{1,0:T(8,128)(2,1)S(1)}, bf16[192,512]{1,0:T(8,128)(2,1)S(1)}, u32[]{:S(2)}, u32[]{:S(2)}) collective-permute-start(bf16[192,512]{1,0:T(8,128)(2,1)S(1)} %get-tuple-element.45), channel_id=1, source_target_pairs={{0,8},{1,9},{2,10},{3,11},{4,12},{5,13},{6,14},{7,15},{8,0},{9,1},... | collective-permute-start | bytes 589832 | tf_op jit(solution)/shard_map/ppermute | solution.py:489
  9.8 0.7 constant_dynamic-slice_fusion
  10.5 0.1 reshape_squeeze.3
  10.5 0.9 copy.35
  11.4 0.9 copy.36
  12.5 0.2 collective-permute-start.2
  12.7 1.3 collective-permute-start.3
  13.9 4.7 %collective-permute-done.1.side_ref = bf16[192,512]{1,0:T(8,128)(2,1)S(1)} collective-permute-done((bf16[192,512]{1,0:T(8,128)(2,1)S(1)}, bf16[192,512]{1,0:T(8,128)(2,1)S(1)}, u32[]{:S(2)}, u32[]{:S(2)}) %collective-permute-start.1) | collective-permute-done | bytes 196640 | tf_op jit(solution)/shard_map/ppermute | solution.py:489
  18.6 0.7 pad_maximum_fusion.3
  19.3 3.5 %collective-permute-start.4 = (bf16[128,512]{1,0:T(8,128)(2,1)}, bf16[128,512]{1,0:T(8,128)(2,1)S(1)}, u32[]{:S(2)}, u32[]{:S(2)}) collective-permute-start(bf16[128,512]{1,0:T(8,128)(2,1)} %pad_maximum_fusion.3), channel_id=1, source_target_pairs={{0,1},{1,2},{2,3},{3,4},{4,5},{5,6},{6,7},{8,9},{9,10},{10,11},{11... | collective-permute-start | bytes 393224 | tf_op jit(solution)/shard_map/ppermute | solution.py:495
  22.8 1.7 copy.37
  24.5 2.4 %collective-permute-start.5 = (bf16[128,512]{1,0:T(8,128)(2,1)S(1)}, bf16[128,512]{1,0:T(8,128)(2,1)S(1)}, u32[]{:S(2)}, u32[]{:S(2)}) collective-permute-start(bf16[128,512]{1,0:T(8,128)(2,1)S(1)} %pad_maximum_fusion.4), channel_id=1, source_target_pairs={{1,0},{2,1},{3,2},{4,3},{5,4},{6,5},{7,6},{9,8},{10,9},{11,10},{12... | collective-permute-start | bytes 393224 | tf_op jit(solution)/shard_map/ppermute | solution.py:496
  26.9 0.1 fusion.6
  27.1 1.2 add_convert_fusion.1
  28.3 3.9 %collective-permute-done.5.ahead_ref = bf16[128,512]{1,0:T(8,128)(2,1)S(1)} collective-permute-done((bf16[128,512]{1,0:T(8,128)(2,1)S(1)}, bf16[128,512]{1,0:T(8,128)(2,1)S(1)}, u32[]{:S(2)}, u32[]{:S(2)}) %collective-permute-start.5) | collective-permute-done | bytes 131104 | tf_op jit(solution)/shard_map/ppermute | solution.py:496
  32.3 0.4 collective-permute-done.3.refs_6_.refs_7_
  32.8 2.1 %collective-permute-start.7 = (bf16[640,512]{1,0:T(8,128)(2,1)S(1)}, bf16[640,512]{1,0:T(8,128)(2,1)S(1)}, u32[]{:S(2)}, u32[]{:S(2)}) collective-permute-start(bf16[640,512]{1,0:T(8,128)(2,1)S(1)} %collective-permute-done.3.refs_6_.refs_7_), channel_id=1, source_target_pairs={{0,2},{1,5},{4,0},{5,9},{8,4},{9,13},{12,8},{13,15},{14,12},{15,11... | collective-permute-start | bytes 1966088 | tf_op jit(solution)/shard_map/ppermute | solution.py:469
  34.9 0.6 shard_map.147
  35.6 0.8 collective-permute-start.9
  36.4 1.3 collective-permute-start.16
  37.7 8.5 %shard_map.148.refs_1_ = bf16[512,6912]{1,0:T(8,128)(2,1)S(1)} custom-call(s32[1]{0:T(128)} %bitcast.7.start_ref, f32[512,128]{1,0:T(8,128)S(1)} %get-tuple-element.85.rows_ref, bf16[896,256]{1,0:T(8,128)(2,1)S(1)} %get-tuple-element.59.table_ref), custom_call_target="tpu_custom_call" | custom-call | flops 6341787648 | bytes 7077888 | tf_op jit(solution)/shard_map/pallas_call | solution.py:137
  46.1 1.2 collective-permute-done.6.refs_2_.refs_3_
  47.3 2.9 %collective-permute-done.7.refs_5_.refs_6_ = bf16[640,512]{1,0:T(8,128)(2,1)S(1)} collective-permute-done((bf16[640,512]{1,0:T(8,128)(2,1)S(1)}, bf16[640,512]{1,0:T(8,128)(2,1)S(1)}, u32[]{:S(2)}, u32[]{:S(2)}) %collective-permute-start.7) | collective-permute-done | bytes 655392 | tf_op jit(solution)/shard_map/ppermute | solution.py:469
  50.4 1.5 collective-permute-start.11
  51.9 1.4 collective-permute-start.12
  53.3 8.4 %shard_map.149.refs_0_ = bf16[512,6912]{1,0:T(8,128)(2,1)S(1)} custom-call(s32[1]{0:T(128)} %bitcast.7.start_ref, f32[512,128]{1,0:T(8,128)S(1)} %get-tuple-element.64.rows_ref, bf16[896,256]{1,0:T(8,128)(2,1)S(1)} %collective-permute-done.9.table_ref), custom_call_target="tpu_custom_call" | custom-call | flops 6341787648 | bytes 7077888 | tf_op jit(solution)/shard_map/pallas_call | solution.py:137
  61.7 1.2 collective-permute-done.12.refs_4_.refs_7_
  62.9 1.4 collective-permute-done.10.refs_2_.refs_3_
  64.4 2.0 %collective-permute-done.11.refs_5_.refs_6_ = bf16[640,512]{1,0:T(8,128)(2,1)S(1)} collective-permute-done((bf16[640,512]{1,0:T(8,128)(2,1)S(1)}, bf16[640,512]{1,0:T(8,128)(2,1)S(1)}, u32[]{:S(2)}, u32[]{:S(2)}) %collective-permute-start.11) | collective-permute-done | bytes 655392 | tf_op jit(solution)/shard_map/ppermute | solution.py:469
  66.3 1.0 collective-permute-start.13
  67.7 1.3 collective-permute-start.15
  69.0 6.0 %shard_map.150 = (f32[512,512]{1,0:T(8,128)S(1)}, f32[512,512]{1,0:T(8,128)S(1)}) custom-call(s32[6]{0:T(128)S(1)} %bitcast.30, s32[2]{0:T(128)S(1)} %pad_add_fusion.2.shifts_ref, bf16[512,6912]{1,0:T(8,128)(2,1)S(1)} %shard_map.149.refs_0_, bf16[512,6912]{1,0:T(8,128)(2,1)S(1)} %shard_map.148.refs_1_, bf16[864,512]{1,0:T(8,128)(2,1)S(1)} %get-tuple-element.72.refs_2_, ...), custom_call_target="tpu_custom_call" | custom-call | flops 3221225472 | bytes 9437184 | tf_op jit(solution)/shard_map/pallas_call | solution.py:206
  75.0 1.1 collective-permute-done.13.refs_2_.refs_3_
  76.2 1.5 collective-permute-start.14
  77.7 4.9 %shard_map.151 = (f32[512,512]{1,0:T(8,128)S(1)}, f32[512,512]{1,0:T(8,128)S(1)}) custom-call(s32[4]{0:T(128)S(1)} %get-tuple-element.92.places_ref, s32[2]{0:T(128)S(1)} %pad_add_fusion.2.shifts_ref, bf16[512,6912]{1,0:T(8,128)(2,1)S(1)} %shard_map.149.refs_0_, ...), custom_call_target="tpu_custom_call", output_to_operand_aliasing={{0}: (10, {}), {1}: (11, {})} | custom-call | flops 2147483648 | bytes 6291456 | tf_op jit(solution)/shard_map/pallas_call | solution.py:206
  82.6 4.9 %shard_map.152 = (f32[512,512]{1,0:T(8,128)S(1)}, f32[512,512]{1,0:T(8,128)S(1)}) custom-call(s32[4]{0:T(128)S(1)} %get-tuple-element.93.places_ref, s32[2]{0:T(128)S(1)} %pad_add_fusion.2.shifts_ref, bf16[512,6912]{1,0:T(8,128)(2,1)S(1)} %shard_map.149.refs_0_, ...), custom_call_target="tpu_custom_call", output_to_operand_aliasing={{0}: (10, {}), {1}: (11, {})} | custom-call | flops 2147483648 | bytes 6291456 | tf_op jit(solution)/shard_map/pallas_call | solution.py:206
  87.6 2.7 %shard_map.153 = (bf16[512,512]{1,0:T(8,128)(2,1)S(1)}, f32[512,512]{1,0:T(8,128)S(1)}) custom-call(s32[2]{0:T(128)S(1)} %slice.76.places_ref, s32[2]{0:T(128)S(1)} %pad_add_fusion.2.shifts_ref, bf16[512,6912]{1,0:T(8,128)(2,1)S(1)} %shard_map.149.refs_0_, bf16[512,6912]{1,0:T(8,128)(2,1)S(1)} %shard_map.148.refs_1_, ...), custom_call_target="tpu_custom_call", output_to_operand_aliasing={{1}: (8, {})} | custom-call | flops 1073741824 | bytes 3145728 | tf_op jit(solution)/shard_map/pallas_call | solution.py:206
  90.3 2.2 %collective-permute-start.17 = (bf16[512,512]{1,0:T(8,128)(2,1)S(1)}, bf16[512,512]{1,0:T(8,128)(2,1)S(1)}, u32[]{:S(2)}, u32[]{:S(2)}) collective-permute-start(bf16[512,512]{1,0:T(8,128)(2,1)S(1)} %get-tuple-element.80), channel_id=1, source_target_pairs={{0,1},{1,0},{2,3},{3,2},{4,5},{5,4},{6,7},{7,6},{8,9},{9,8},{10,11... | collective-permute-start | bytes 1572872 | tf_op jit(solution)/shard_map/ppermute | solution.py:566
  92.5 0.3 convert_reduce_fusion.1
  92.9 1.2 collective-permute-done.17.got_ref
  94.1 2.3 %shard_map.154 = bf16[1024,512]{1,0:T(8,128)(2,1)} custom-call(f32[512,512]{1,0:T(8,128)S(1)} %get-tuple-element.79.own_ref, bf16[512,512]{1,0:T(8,128)(2,1)S(1)} %collective-permute-done.17.got_ref, bf16[512,512]{1,0:T(8,128)(2,1)S(1)} %copy-done.2, bf16[512,512]{1,0:T(8,128)(2,1)S(1)} %copy-done.3, f32[1,512]{1,0:T(1,128)S(1)} %bitcast.31, ...), custom_call_target="tpu_custom_call" | custom-call | flops 805306368 | bytes 2097152 | tf_op jit(solution)/shard_map/pallas_call | solution.py:568
  96.4 6.5 %all-to-all-start = ((bf16[16,64,512]{2,1,0:T(8,128)(2,1)}), bf16[16,64,512]{2,1,0:T(8,128)(2,1)}, u32[]{:S(2)}, u32[]{:S(2)}) async-start(bf16[16,64,512]{2,1,0:T(8,128)(2,1)} %bitcast.11), calls=%async_computation | async-start | bytes 2097152 | tf_op jit(solution)/shard_map/all_to_all | solution.py:582
  102.9 0.9 fusion.5
  103.8 0.2 copy.42
  104.0 0.2 copy.43
  104.3 0.2 convert_reduce_fusion
  104.5 0.8 copy.40.slot_col_ref
  105.4 1.0 maximum_bitcast_fusion.qv_hbm
  106.4 21.4 %all-to-all-done = bf16[16,64,512]{2,1,0:T(8,128)(2,1)} async-done(((bf16[16,64,512]{2,1,0:T(8,128)(2,1)}), bf16[16,64,512]{2,1,0:T(8,128)(2,1)}, u32[]{:S(2)}, u32[]{:S(2)}) %all-to-all-start) | async-done | bytes 1048608 | tf_op jit(solution)/shard_map/all_to_all | solution.py:582
  127.8 21.6 %shard_map.155 = bf16[1024,512]{1,0:T(8,128)(2,1)} custom-call(bf16[1024,512]{1,0:T(8,128)(2,1)} %bitcast.12.arrived_ref, s32[512,1]{1,0:T(8,128)} %copy.40.slot_col_ref, s32[1,512]{1,0:T(1,128)} %bitcast.34, f32[1,512]{1,0:T(1,128)} %bitcast.35, f32[1,512]{1,0:T(1,128)} %bitcast.36, bf16[1024,512]{1,0:T(8,128)(2,1)} %maximum_bitcast_fusion.qv_hbm, ...), custom_call_target="tpu_custom_call" | custom-call | flops 2684354560 | bytes 4194304 | tf_op jit(solution)/shard_map/pallas_call | solution.py:589
  149.5 5.0 %all-to-all-start.1 = ((bf16[16,64,512]{2,1,0:T(8,128)(2,1)}), bf16[16,64,512]{2,1,0:T(8,128)(2,1)S(1)}, u32[]{:S(2)}, u32[]{:S(2)}) async-start(bf16[16,64,512]{2,1,0:T(8,128)(2,1)} %bitcast.32), calls=%async_computation.1 | async-start | bytes 2097152 | tf_op jit(solution)/shard_map/all_to_all | solution.py:615
  154.4 0.1 copy.41.slot_ref
  154.6 24.7 %all-to-all-done.1 = bf16[16,64,512]{2,1,0:T(8,128)(2,1)S(1)} async-done(((bf16[16,64,512]{2,1,0:T(8,128)(2,1)}), bf16[16,64,512]{2,1,0:T(8,128)(2,1)S(1)}, u32[]{:S(2)}, u32[]{:S(2)}) %all-to-all-start.1) | async-done | bytes 1048608 | tf_op jit(solution)/shard_map/all_to_all | solution.py:615
  179.3 1.5 shard_map.156
  (56 shorter events, 0.9 us)
Async XLA Ops:
  0.0 6.0 %copy-start = (bf16[864,512]{1,0:T(8,128)(2,1)S(1)}, bf16[864,512]{1,0:T(8,128)(2,1)}, u32[]{:S(2)}) copy-start(bf16[864,512]{1,0:T(8,128)(2,1)} %param.16) | copy-start | bytes 2654212
  0.0 5.3 %copy-start.7 = (s32[512,26]{0,1:T(8,128)S(1)}, s32[512,26]{0,1:T(8,128)}, u32[]{:S(2)}) copy-start(s32[512,26]{0,1:T(8,128)} %param.26) | copy-start | bytes 159748
  1.1 4.8 %collective-permute-start = (bf16[13,32,512]{2,1,0:T(8,128)(2,1)S(1)}, bf16[13,32,512]{2,1,0:T(8,128)(2,1)S(1)}, u32[]{:S(2)}, u32[]{:S(2)}) collective-permute-start(bf16[13,32,512]{2,1,0:T(8,128)(2,1)S(1)} %slice.72), channel_id=1, source_target_pairs={{0,1},{1,0},{2,3},{3,2},{4,5},{5,4},{6,7},{7,6},{8,9},{9,8},{10,11... | collective-permute-start | bytes 1277960 | tf_op jit(solution)/shard_map/ppermute | solution.py:414
  3.5 1.0 copy-start.1
  6.6 0.9 copy-start.5
  7.5 11.1 %collective-permute-start.1 = (bf16[192,512]{1,0:T(8,128)(2,1)S(1)}, bf16[192,512]{1,0:T(8,128)(2,1)S(1)}, u32[]{:S(2)}, u32[]{:S(2)}) collective-permute-start(bf16[192,512]{1,0:T(8,128)(2,1)S(1)} %get-tuple-element.45), channel_id=1, source_target_pairs={{0,8},{1,9},{2,10},{3,11},{4,12},{5,13},{6,14},{7,15},{8,0},{9,1},... | collective-permute-start | bytes 589832 | tf_op jit(solution)/shard_map/ppermute | solution.py:489
  12.5 19.8 %collective-permute-start.2 = (bf16[640,512]{1,0:T(8,128)(2,1)}, bf16[640,512]{1,0:T(8,128)(2,1)S(1)}, u32[]{:S(2)}, u32[]{:S(2)}) collective-permute-start(bf16[640,512]{1,0:T(8,128)(2,1)} %copy-done.5), channel_id=1, source_target_pairs={{0,4},{1,3},{4,8},{5,1},{8,12},{9,5},{12,14},{13,9},{14,10},{15,13... | collective-permute-start | bytes 1966088 | tf_op jit(solution)/shard_map/ppermute | solution.py:467
  12.7 20.1 %collective-permute-start.3 = (bf16[640,512]{1,0:T(8,128)(2,1)}, bf16[640,512]{1,0:T(8,128)(2,1)S(1)}, u32[]{:S(2)}, u32[]{:S(2)}) collective-permute-start(bf16[640,512]{1,0:T(8,128)(2,1)} %copy-done.5), channel_id=1, source_target_pairs={{0,2},{1,5},{4,0},{5,9},{8,4},{9,13},{12,8},{13,15},{14,12},{15,11... | collective-permute-start | bytes 1966088 | tf_op jit(solution)/shard_map/ppermute | solution.py:469
  19.3 9.0 %collective-permute-start.4 = (bf16[128,512]{1,0:T(8,128)(2,1)}, bf16[128,512]{1,0:T(8,128)(2,1)S(1)}, u32[]{:S(2)}, u32[]{:S(2)}) collective-permute-start(bf16[128,512]{1,0:T(8,128)(2,1)} %pad_maximum_fusion.3), channel_id=1, source_target_pairs={{0,1},{1,2},{2,3},{3,4},{4,5},{5,6},{6,7},{8,9},{9,10},{10,11},{11... | collective-permute-start | bytes 393224 | tf_op jit(solution)/shard_map/ppermute | solution.py:495
  24.5 2.4 %collective-permute-start.8 = (s32[512,26]{1,0:T(8,128)}, s32[512,26]{1,0:T(8,128)S(1)}, u32[]{:S(2)}, u32[]{:S(2)}) collective-permute-start(s32[512,26]{1,0:T(8,128)} %copy.37), channel_id=1, source_target_pairs={{0,1},{1,0},{2,3},{3,2},{4,5},{5,4},{6,7},{7,6},{8,9},{9,8},{10,11... | collective-permute-start | bytes 159752 | tf_op jit(solution)/shard_map/ppermute | solution.py:492
  24.5 7.8 %collective-permute-start.5 = (bf16[128,512]{1,0:T(8,128)(2,1)S(1)}, bf16[128,512]{1,0:T(8,128)(2,1)S(1)}, u32[]{:S(2)}, u32[]{:S(2)}) collective-permute-start(bf16[128,512]{1,0:T(8,128)(2,1)S(1)} %pad_maximum_fusion.4), channel_id=1, source_target_pairs={{1,0},{2,1},{3,2},{4,3},{5,4},{6,5},{7,6},{9,8},{10,9},{11,10},{12... | collective-permute-start | bytes 393224 | tf_op jit(solution)/shard_map/ppermute | solution.py:496
  32.8 14.6 %collective-permute-start.6 = (bf16[640,512]{1,0:T(8,128)(2,1)S(1)}, bf16[640,512]{1,0:T(8,128)(2,1)S(1)}, u32[]{:S(2)}, u32[]{:S(2)}) collective-permute-start(bf16[640,512]{1,0:T(8,128)(2,1)S(1)} %collective-permute-done.2.refs_3_.refs_4_), channel_id=1, source_target_pairs={{0,4},{1,3},{4,8},{5,1},{8,12},{9,5},{12,14},{13,9},{14,10},{15,13... | collective-permute-start | bytes 1966088 | tf_op jit(solution)/shard_map/ppermute | solution.py:467
  32.8 17.5 %collective-permute-start.7 = (bf16[640,512]{1,0:T(8,128)(2,1)S(1)}, bf16[640,512]{1,0:T(8,128)(2,1)S(1)}, u32[]{:S(2)}, u32[]{:S(2)}) collective-permute-start(bf16[640,512]{1,0:T(8,128)(2,1)S(1)} %collective-permute-done.3.refs_6_.refs_7_), channel_id=1, source_target_pairs={{0,2},{1,5},{4,0},{5,9},{8,4},{9,13},{12,8},{13,15},{14,12},{15,11... | collective-permute-start | bytes 1966088 | tf_op jit(solution)/shard_map/ppermute | solution.py:469
  35.6 10.6 %collective-permute-start.9 = (bf16[896,256]{1,0:T(8,128)(2,1)S(1)}, bf16[896,256]{1,0:T(8,128)(2,1)S(1)}, u32[]{:S(2)}, u32[]{:S(2)}) collective-permute-start(bf16[896,256]{1,0:T(8,128)(2,1)S(1)} %get-tuple-element.61), channel_id=1, source_target_pairs={{0,1},{1,0},{2,3},{3,2},{4,5},{5,4},{6,7},{7,6},{8,9},{9,8},{10,11... | collective-permute-start | bytes 1376264 | tf_op jit(solution)/shard_map/ppermute | solution.py:531
  36.4 32.6 %collective-permute-start.16 = (bf16[448,512]{1,0:T(8,128)(2,1)S(1)}, bf16[448,512]{1,0:T(8,128)(2,1)S(1)}, u32[]{:S(2)}, u32[]{:S(2)}) collective-permute-start(bf16[448,512]{1,0:T(8,128)(2,1)S(1)} %pad_maximum_fusion.2), channel_id=1, source_target_pairs={{0,16},{16,0},{1,17},{17,1},{2,18},{18,2},{3,19},{19,3},{4,20},{20... | collective-permute-start | bytes 1376264 | tf_op jit(solution)/shard_map/ppermute | solution.py:475
  50.3 14.1 %collective-permute-start.10 = (bf16[640,512]{1,0:T(8,128)(2,1)S(1)}, bf16[640,512]{1,0:T(8,128)(2,1)S(1)}, u32[]{:S(2)}, u32[]{:S(2)}) collective-permute-start(bf16[640,512]{1,0:T(8,128)(2,1)S(1)} %collective-permute-done.6.refs_2_.refs_3_), channel_id=1, source_target_pairs={{0,4},{1,3},{4,8},{5,1},{8,12},{9,5},{12,14},{13,9},{14,10},{15,13... | collective-permute-start | bytes 1966088 | tf_op jit(solution)/shard_map/ppermute | solution.py:467
  50.4 16.0 %collective-permute-start.11 = (bf16[640,512]{1,0:T(8,128)(2,1)S(1)}, bf16[640,512]{1,0:T(8,128)(2,1)S(1)}, u32[]{:S(2)}, u32[]{:S(2)}) collective-permute-start(bf16[640,512]{1,0:T(8,128)(2,1)S(1)} %collective-permute-done.7.refs_5_.refs_6_), channel_id=1, source_target_pairs={{0,2},{1,5},{4,0},{5,9},{8,4},{9,13},{12,8},{13,15},{14,12},{15,11... | collective-permute-start | bytes 1966088 | tf_op jit(solution)/shard_map/ppermute | solution.py:469
  51.9 11.0 %collective-permute-start.12 = (bf16[448,512]{1,0:T(8,128)(2,1)S(1)}, bf16[448,512]{1,0:T(8,128)(2,1)S(1)}, u32[]{:S(2)}, u32[]{:S(2)}) collective-permute-start(bf16[448,512]{1,0:T(8,128)(2,1)S(1)} %pad_maximum_fusion), channel_id=1, source_target_pairs={{0,16},{16,0},{1,17},{17,1},{2,18},{18,2},{3,19},{19,3},{4,20},{20... | collective-permute-start | bytes 1376264 | tf_op jit(solution)/shard_map/ppermute | solution.py:475
  66.3 9.8 %collective-permute-start.13 = (bf16[640,512]{1,0:T(8,128)(2,1)S(1)}, bf16[640,512]{1,0:T(8,128)(2,1)S(1)}, u32[]{:S(2)}, u32[]{:S(2)}) collective-permute-start(bf16[640,512]{1,0:T(8,128)(2,1)S(1)} %collective-permute-done.10.refs_2_.refs_3_), channel_id=1, source_target_pairs={{0,4},{1,3},{4,8},{5,1},{8,12},{9,5},{12,14},{13,9},{14,10},{15,13... | collective-permute-start | bytes 1966088 | tf_op jit(solution)/shard_map/ppermute | solution.py:467
  67.7 14.9 %collective-permute-start.15 = (bf16[448,512]{1,0:T(8,128)(2,1)S(1)}, bf16[448,512]{1,0:T(8,128)(2,1)S(1)}, u32[]{:S(2)}, u32[]{:S(2)}) collective-permute-start(bf16[448,512]{1,0:T(8,128)(2,1)S(1)} %pad_maximum_fusion.1), channel_id=1, source_target_pairs={{0,16},{16,0},{1,17},{17,1},{2,18},{18,2},{3,19},{19,3},{4,20},{20... | collective-permute-start | bytes 1376264 | tf_op jit(solution)/shard_map/ppermute | solution.py:475
  76.2 11.4 %collective-permute-start.14 = (bf16[224,512]{1,0:T(8,128)(2,1)S(1)}, bf16[224,512]{1,0:T(8,128)(2,1)S(1)}, u32[]{:S(2)}, u32[]{:S(2)}) collective-permute-start(bf16[224,512]{1,0:T(8,128)(2,1)S(1)} %slice.98), channel_id=1, source_target_pairs={{0,16},{16,0},{1,17},{17,1},{2,18},{18,2},{3,19},{19,3},{4,20},{20... | collective-permute-start | bytes 688136 | tf_op jit(solution)/shard_map/ppermute | solution.py:475
  87.6 5.0 %copy-start.8 = (s32[512]{0:T(512)S(1)}, s32[512]{0:T(512)}, u32[]{:S(2)}) copy-start(s32[512]{0:T(512)} %param.27) | copy-start | bytes 6148
  87.6 6.5 %copy-start.2 = (bf16[512,512]{1,0:T(8,128)(2,1)S(1)}, bf16[512,512]{1,0:T(8,128)(2,1)}, u32[]{:S(2)}) copy-start(bf16[512,512]{1,0:T(8,128)(2,1)} %features_ref.3) | copy-start | bytes 1572868
  87.6 6.5 %copy-start.3 = (bf16[512,512]{1,0:T(8,128)(2,1)S(1)}, bf16[512,512]{1,0:T(8,128)(2,1)}, u32[]{:S(2)}) copy-start(bf16[512,512]{1,0:T(8,128)(2,1)} %weight_ref.1) | copy-start | bytes 1572868
  87.6 6.5 %copy-start.4 = (f32[512]{0:T(512)S(1)}, f32[512]{0:T(512)}, u32[]{:S(2)}) copy-start(f32[512]{0:T(512)} %param.18) | copy-start | bytes 6148
  90.3 3.8 %collective-permute-start.17 = (bf16[512,512]{1,0:T(8,128)(2,1)S(1)}, bf16[512,512]{1,0:T(8,128)(2,1)S(1)}, u32[]{:S(2)}, u32[]{:S(2)}) collective-permute-start(bf16[512,512]{1,0:T(8,128)(2,1)S(1)} %get-tuple-element.80), channel_id=1, source_target_pairs={{0,1},{1,0},{2,3},{3,2},{4,5},{5,4},{6,7},{7,6},{8,9},{9,8},{10,11... | collective-permute-start | bytes 1572872 | tf_op jit(solution)/shard_map/ppermute | solution.py:566
  94.1 8.8 %copy-start.6 = (bf16[512,1536]{1,0:T(8,128)(2,1)S(1)}, bf16[512,1536]{1,0:T(8,128)(2,1)}, u32[]{:S(2)}) copy-start(bf16[512,1536]{1,0:T(8,128)(2,1)} %param.20) | copy-start | bytes 4718596
  96.4 31.5 %all-to-all-start = ((bf16[16,64,512]{2,1,0:T(8,128)(2,1)}), bf16[16,64,512]{2,1,0:T(8,128)(2,1)}, u32[]{:S(2)}, u32[]{:S(2)}) async-start(bf16[16,64,512]{2,1,0:T(8,128)(2,1)} %bitcast.11), calls=%async_computation | async-start | bytes 2097152 | tf_op jit(solution)/shard_map/all_to_all | solution.py:582
  102.9 1.3 copy-start.10
  104.5 23.3 %copy-start.9 = (s32[512]{0:T(512)}, s32[512]{0:T(512)S(1)}, u32[]{:S(2)}) copy-start(s32[512]{0:T(512)S(1)} %multiply_add_fusion) | copy-start | bytes 6148
  149.5 29.8 %all-to-all-start.1 = ((bf16[16,64,512]{2,1,0:T(8,128)(2,1)}), bf16[16,64,512]{2,1,0:T(8,128)(2,1)S(1)}, u32[]{:S(2)}, u32[]{:S(2)}) async-start(bf16[16,64,512]{2,1,0:T(8,128)(2,1)} %bitcast.32), calls=%async_computation.1 | async-start | bytes 2097152 | tf_op jit(solution)/shard_map/all_to_all | solution.py:615

commit v20 on v19

--- a/solution.py
+++ b/solution.py
@@ -487,14 +487,15 @@
         across = face_pairs(devices, 1, 0) + face_pairs(devices, -1, 0)
         (lists,) = pass_on(lists)
         lists = lax.ppermute(lists, "blocks", across)
-        places = jnp.array(places, jnp.int32)[index].reshape(-1)
-        lists, sent_neighbours, places = lax.optimization_barrier((lists, neighbours, places))
-        other_neighbours = lax.ppermute(sent_neighbours, "blocks", partner)
         to_on = jnp.concatenate([on_list, lists[2 * size :]])
         to_back = jnp.concatenate([back_list, lists[:size]])
         behind = lax.ppermute(to_on, "blocks", face_pairs(devices, 0, 1))
         ahead = lax.ppermute(to_back, "blocks", face_pairs(devices, 0, -1))
-        lists, behind, ahead = pass_on(lists, behind, ahead)
+        places = jnp.array(places, jnp.int32)[index].reshape(-1)
+        sent_neighbours, places, lists, behind, ahead = pass_on(
+            neighbours, places, lists, behind, ahead
+        )
+        other_neighbours = lax.ppermute(sent_neighbours, "blocks", partner)
         near = complete(first[1], second[1])
         own_table, other_half = call(
             table_kernel,
@@ -537,10 +538,10 @@
     other_stacked = gather_block(start, other_rows, other_table)
     stacked = other_stacked, own_stacked
     if round_trip:
-        *stacked, middle_got = pass_on(*stacked, middle[0][2][0])
-        middle = [[*parts[:2], (middle_got, *parts[2][1:])] for parts in middle]
         early = [[(mine, 0, rows, 0, None)]] + near
         sums = conv_part(stacked, places[:6], shifts, early, None, length, CONV_LIMIT)
+        *sums, middle_got = pass_on(*sums, middle[0][2][0])
+        middle = [[*parts[:2], (middle_got, *parts[2][1:])] for parts in middle]
         far = complete(first[3], second[3])
         opposite = complete(first[4])
         sums = conv_part(stacked, places[6:10], shifts, middle, sums, length, CONV_LIMIT)

time: 181 us -> 186 us (1.028)
  local copies, waits for them, and re-layouts: 11.5 us -> 17.4 us
  starting transfers between devices: 35.1 us -> 32.5 us
    ppermute x4, waiting for transfers between devices: 3.81 us -> 10.3 us  [pass_on(): first.append(lax.ppermute(first[-1], 'blocks', first_pairs))]
    unnamed x24 -> x46, local copies, waits for them, and re-layouts: 2.36 us -> 7.44 us
    ppermute x3, waiting for transfers between devices: 5.29 us -> 0.32 us  [pass_on(): second.append(lax.ppermute(second[-1], 'blocks', second_pairs))]
    ppermute x1, waiting for transfers between devices: 4.65 us -> 7.29 us  [body(): lists = lax.ppermute(lists, 'blocks', across)]
  transfers between devices with their start and end apart: 20 -> 20, of which waited for: 13 -> 8; matrix products, arithmetic and copies ran while one was open for 7% -> 8% of each run, Pallas kernels for 19% -> 18%
where the time goes in v20:
time: 186 us; the launch traced here: 185 us
  waiting for transfers between devices  67.4 us (36%)
  Pallas kernels  62.9 us (34%)
  starting transfers between devices  32.5 us (17%)
  local copies, waits for them, and re-layouts  17.4 us (9%)
  other arithmetic  4.79 us (3%)
    all_to_all x1, waiting for transfers between devices, body(): lax.all_to_all(back.reshape(devices, capacity, width), 'blocks', split_ax...  24.7 us
    pallas_call x1, Pallas kernels, body(): call(block_kernel, jax.ShapeDtypeStruct((slots, width), BF16), 60, 20 * p...  21.6 us
    all_to_all x1, waiting for transfers between devices, body(): lax.all_to_all(outgoing.reshape(devices, capacity, width), 'blocks', spli...  21.4 us
    pallas_call x4, Pallas kernels, conv_part(): call(functools.partial(conv_kernel, slots, before is None), [jax.ShapeDty...  18.6 us
    pallas_call x2, Pallas kernels, gather_block(): call(functools.partial(gather_kernel, taps), jax.ShapeDtypeStruct((points...  17 us
    ppermute x4, waiting for transfers between devices, pass_on(): first.append(lax.ppermute(first[-1], 'blocks', first_pairs))  10.3 us
    unnamed x46, local copies, waits for them, and re-layouts  7.44 us
    ppermute x1, waiting for transfers between devices, body(): lists = lax.ppermute(lists, 'blocks', across)  7.29 us
  transfers between devices with their start and end apart: 20, of which 8 were waited for; matrix products, arithmetic and copies ran while one was open for 8% of the time, Pallas kernels for 18%

profile of v20, /device:TPU:9, one launch (start us, length us, event | category | flops | bytes accessed | tf_op | source)
XLA Modules:
  0.0 185.4 jit_solution(1190911392872770953)
XLA Ops:
  0.0 1.1 slice.72
  1.1 0.7 collective-permute-start
  1.9 0.8 select_bitcast_fusion
  2.6 0.7 slice_bitcast_fusion
  3.5 1.0 copy-done.3
  4.5 0.7 shard_map.146
  5.3 0.7 constant_dynamic-slice_fusion
  6.1 0.7 shard_map.145
  6.7 2.4 %collective-permute-start.3 = (bf16[192,512]{1,0:T(8,128)(2,1)S(1)}, bf16[192,512]{1,0:T(8,128)(2,1)S(1)}, u32[]{:S(2)}, u32[]{:S(2)}) collective-permute-start(bf16[192,512]{1,0:T(8,128)(2,1)S(1)} %get-tuple-element.46), channel_id=1, source_target_pairs={{0,8},{1,9},{2,10},{3,11},{4,12},{5,13},{6,14},{7,15},{8,0},{9,1},... | collective-permute-start | bytes 589832 | tf_op jit(solution)/shard_map/ppermute | solution.py:489
  9.1 0.2 collective-permute-start.1
  9.4 1.3 collective-permute-start.2
  10.6 7.3 %collective-permute-done.3.side_ref = bf16[192,512]{1,0:T(8,128)(2,1)S(1)} collective-permute-done((bf16[192,512]{1,0:T(8,128)(2,1)S(1)}, bf16[192,512]{1,0:T(8,128)(2,1)S(1)}, u32[]{:S(2)}, u32[]{:S(2)}) %collective-permute-start.3) | collective-permute-done | bytes 196640 | tf_op jit(solution)/shard_map/ppermute | solution.py:489
  18.0 3.5 %collective-permute-start.4 = (bf16[128,512]{1,0:T(8,128)(2,1)S(1)}, bf16[128,512]{1,0:T(8,128)(2,1)S(1)}, u32[]{:S(2)}, u32[]{:S(2)}) collective-permute-start(bf16[128,512]{1,0:T(8,128)(2,1)S(1)} %pad_maximum_fusion.3), channel_id=1, source_target_pairs={{0,1},{1,2},{2,3},{3,4},{4,5},{5,6},{6,7},{8,9},{9,10},{10,11},{11... | collective-permute-start | bytes 393224 | tf_op jit(solution)/shard_map/ppermute | solution.py:492
  21.5 0.7 pad_maximum_fusion.4
  22.2 1.9 %collective-permute-start.5 = (bf16[128,512]{1,0:T(8,128)(2,1)}, bf16[128,512]{1,0:T(8,128)(2,1)S(1)}, u32[]{:S(2)}, u32[]{:S(2)}) collective-permute-start(bf16[128,512]{1,0:T(8,128)(2,1)} %pad_maximum_fusion.4), channel_id=1, source_target_pairs={{1,0},{2,1},{3,2},{4,3},{5,4},{6,5},{7,6},{9,8},{10,9},{11,10},{12... | collective-permute-start | bytes 393224 | tf_op jit(solution)/shard_map/ppermute | solution.py:493
  24.2 0.9 copy.35
  25.1 0.8 copy.36
  26.1 0.6 copy-done.10
  26.7 2.2 %collective-permute-done.5.ahead_ref = bf16[128,512]{1,0:T(8,128)(2,1)S(1)} collective-permute-done((bf16[128,512]{1,0:T(8,128)(2,1)}, bf16[128,512]{1,0:T(8,128)(2,1)S(1)}, u32[]{:S(2)}, u32[]{:S(2)}) %collective-permute-start.5) | collective-permute-done | bytes 131104 | tf_op jit(solution)/shard_map/ppermute | solution.py:493
  29.0 0.6 copy-done.12
  29.6 2.1 %collective-permute-done.1.refs_3_.refs_4_ = bf16[640,512]{1,0:T(8,128)(2,1)S(1)} collective-permute-done((bf16[640,512]{1,0:T(8,128)(2,1)S(1)}, bf16[640,512]{1,0:T(8,128)(2,1)S(1)}, u32[]{:S(2)}, u32[]{:S(2)}) %collective-permute-start.1) | collective-permute-done | bytes 655392 | tf_op jit(solution)/shard_map/ppermute | solution.py:467
  31.7 0.3 collective-permute-done.2.refs_6_.refs_7_
  32.0 0.7 slice.84
  32.7 2.2 %collective-permute-start.7 = (bf16[640,512]{1,0:T(8,128)(2,1)S(1)}, bf16[640,512]{1,0:T(8,128)(2,1)S(1)}, u32[]{:S(2)}, u32[]{:S(2)}) collective-permute-start(bf16[640,512]{1,0:T(8,128)(2,1)S(1)} %collective-permute-done.2.refs_6_.refs_7_), channel_id=1, source_target_pairs={{0,2},{1,5},{4,0},{5,9},{8,4},{9,13},{12,8},{13,15},{14,12},{15,11... | collective-permute-start | bytes 1966088 | tf_op jit(solution)/shard_map/ppermute | solution.py:469
  34.9 0.7 slice.85
  35.6 1.7 copy.37
  37.3 0.8 collective-permute-start.8
  38.1 0.9 copy-done.2
  39.0 0.9 copy-done.7
  40.0 0.9 copy-done.9
  40.9 0.9 copy-done.11
  41.8 0.9 copy-done.13
  42.7 0.6 shard_map.147
  43.4 1.1 pad_maximum_fusion
  44.5 1.3 collective-permute-start.12
  46.0 0.3 add_convert_fusion.1
  46.2 8.5 %shard_map.148.refs_1_ = bf16[512,6912]{1,0:T(8,128)(2,1)S(1)} custom-call(s32[1]{0:T(128)} %bitcast.7.start_ref, f32[512,128]{1,0:T(8,128)S(1)} %get-tuple-element.83.rows_ref, bf16[896,256]{1,0:T(8,128)(2,1)S(1)} %get-tuple-element.57.table_ref), custom_call_target="tpu_custom_call" | custom-call | flops 6341787648 | bytes 7077888 | tf_op jit(solution)/shard_map/pallas_call | solution.py:137
  54.9 1.7 collective-permute-start.11
  56.6 0.3 collective-permute-start.13
  57.0 8.5 %shard_map.149.refs_0_ = bf16[512,6912]{1,0:T(8,128)(2,1)S(1)} custom-call(s32[1]{0:T(128)} %bitcast.7.start_ref, f32[512,128]{1,0:T(8,128)S(1)} %get-tuple-element.60.rows_ref, bf16[896,256]{1,0:T(8,128)(2,1)S(1)} %collective-permute-done.9.table_ref), custom_call_target="tpu_custom_call" | custom-call | flops 6341787648 | bytes 7077888 | tf_op jit(solution)/shard_map/pallas_call | solution.py:137
  65.5 6.0 %shard_map.150 = (f32[512,512]{1,0:T(8,128)S(1)}, f32[512,512]{1,0:T(8,128)S(1)}) custom-call(s32[6]{0:T(128)S(1)} %bitcast.30, s32[2]{0:T(128)S(1)} %pad_add_fusion.2.shifts_ref, bf16[512,6912]{1,0:T(8,128)(2,1)S(1)} %shard_map.149.refs_0_, bf16[512,6912]{1,0:T(8,128)(2,1)S(1)} %shard_map.148.refs_1_, bf16[864,512]{1,0:T(8,128)(2,1)S(1)} %get-tuple-element.65.refs_2_, ...), custom_call_target="tpu_custom_call" | custom-call | flops 3221225472 | bytes 9437184 | tf_op jit(solution)/shard_map/pallas_call | solution.py:206
  71.5 0.7 collective-permute-start.14
  72.3 0.8 collective-permute-start.16
  73.3 8.2 %collective-permute-done.14.refs_2_.refs_3_ = bf16[640,512]{1,0:T(8,128)(2,1)S(1)} collective-permute-done((bf16[640,512]{1,0:T(8,128)(2,1)S(1)}, bf16[640,512]{1,0:T(8,128)(2,1)S(1)}, u32[]{:S(2)}, u32[]{:S(2)}) %collective-permute-start.14) | collective-permute-done | bytes 655392 | tf_op jit(solution)/shard_map/ppermute | solution.py:467
  81.5 1.3 collective-permute-start.15
  82.8 4.9 %shard_map.151 = (f32[512,512]{1,0:T(8,128)S(1)}, f32[512,512]{1,0:T(8,128)S(1)}) custom-call(s32[4]{0:T(128)S(1)} %get-tuple-element.90.places_ref, s32[2]{0:T(128)S(1)} %pad_add_fusion.2.shifts_ref, bf16[512,6912]{1,0:T(8,128)(2,1)S(1)} %shard_map.149.refs_0_, ...), custom_call_target="tpu_custom_call", output_to_operand_aliasing={{0}: (10, {}), {1}: (11, {})} | custom-call | flops 2147483648 | bytes 6291456 | tf_op jit(solution)/shard_map/pallas_call | solution.py:206
  87.7 4.9 %shard_map.152 = (f32[512,512]{1,0:T(8,128)S(1)}, f32[512,512]{1,0:T(8,128)S(1)}) custom-call(s32[4]{0:T(128)S(1)} %get-tuple-element.91.places_ref, s32[2]{0:T(128)S(1)} %pad_add_fusion.2.shifts_ref, bf16[512,6912]{1,0:T(8,128)(2,1)S(1)} %shard_map.149.refs_0_, ...), custom_call_target="tpu_custom_call", output_to_operand_aliasing={{0}: (10, {}), {1}: (11, {})} | custom-call | flops 2147483648 | bytes 6291456 | tf_op jit(solution)/shard_map/pallas_call | solution.py:206
  92.7 2.7 %shard_map.153 = (bf16[512,512]{1,0:T(8,128)(2,1)S(1)}, f32[512,512]{1,0:T(8,128)S(1)}) custom-call(s32[2]{0:T(128)S(1)} %slice.78.places_ref, s32[2]{0:T(128)S(1)} %pad_add_fusion.2.shifts_ref, bf16[512,6912]{1,0:T(8,128)(2,1)S(1)} %shard_map.149.refs_0_, bf16[512,6912]{1,0:T(8,128)(2,1)S(1)} %shard_map.148.refs_1_, ...), custom_call_target="tpu_custom_call", output_to_operand_aliasing={{1}: (8, {})} | custom-call | flops 1073741824 | bytes 3145728 | tf_op jit(solution)/shard_map/pallas_call | solution.py:206
  95.4 2.6 %collective-permute-start.17 = (bf16[512,512]{1,0:T(8,128)(2,1)S(1)}, bf16[512,512]{1,0:T(8,128)(2,1)S(1)}, u32[]{:S(2)}, u32[]{:S(2)}) collective-permute-start(bf16[512,512]{1,0:T(8,128)(2,1)S(1)} %get-tuple-element.78), channel_id=1, source_target_pairs={{0,1},{1,0},{2,3},{3,2},{4,5},{5,4},{6,7},{7,6},{8,9},{9,8},{10,11... | collective-permute-start | bytes 1572872 | tf_op jit(solution)/shard_map/ppermute | solution.py:567
  98.0 0.3 convert_reduce_fusion.1
  98.4 1.2 collective-permute-done.17.got_ref
  99.6 2.3 %shard_map.154 = bf16[1024,512]{1,0:T(8,128)(2,1)} custom-call(f32[512,512]{1,0:T(8,128)S(1)} %get-tuple-element.77.own_ref, bf16[512,512]{1,0:T(8,128)(2,1)S(1)} %collective-permute-done.17.got_ref, bf16[512,512]{1,0:T(8,128)(2,1)S(1)} %copy-done.4, bf16[512,512]{1,0:T(8,128)(2,1)S(1)} %copy-done.5, f32[1,512]{1,0:T(1,128)S(1)} %bitcast.31, ...), custom_call_target="tpu_custom_call" | custom-call | flops 805306368 | bytes 2097152 | tf_op jit(solution)/shard_map/pallas_call | solution.py:569
  101.8 5.7 %all-to-all-start = ((bf16[16,64,512]{2,1,0:T(8,128)(2,1)}), bf16[16,64,512]{2,1,0:T(8,128)(2,1)}, u32[]{:S(2)}, u32[]{:S(2)}) async-start(bf16[16,64,512]{2,1,0:T(8,128)(2,1)} %bitcast.11), calls=%async_computation | async-start | bytes 2097152 | tf_op jit(solution)/shard_map/all_to_all | solution.py:583
  107.5 0.9 fusion.5
  108.4 0.2 copy.42
  108.7 0.2 copy.43
  108.9 0.2 convert_reduce_fusion
  109.2 0.9 copy.40.slot_col_ref
  110.0 1.1 maximum_bitcast_fusion.qv_hbm
  111.1 21.4 %all-to-all-done = bf16[16,64,512]{2,1,0:T(8,128)(2,1)} async-done(((bf16[16,64,512]{2,1,0:T(8,128)(2,1)}), bf16[16,64,512]{2,1,0:T(8,128)(2,1)}, u32[]{:S(2)}, u32[]{:S(2)}) %all-to-all-start) | async-done | bytes 1048608 | tf_op jit(solution)/shard_map/all_to_all | solution.py:583
  132.5 21.6 %shard_map.155 = bf16[1024,512]{1,0:T(8,128)(2,1)} custom-call(bf16[1024,512]{1,0:T(8,128)(2,1)} %bitcast.12.arrived_ref, s32[512,1]{1,0:T(8,128)} %copy.40.slot_col_ref, s32[1,512]{1,0:T(1,128)} %bitcast.34, f32[1,512]{1,0:T(1,128)} %bitcast.35, f32[1,512]{1,0:T(1,128)} %bitcast.36, bf16[1024,512]{1,0:T(8,128)(2,1)} %maximum_bitcast_fusion.qv_hbm, ...), custom_call_target="tpu_custom_call" | custom-call | flops 2684354560 | bytes 4194304 | tf_op jit(solution)/shard_map/pallas_call | solution.py:590
  154.1 5.0 %all-to-all-start.1 = ((bf16[16,64,512]{2,1,0:T(8,128)(2,1)}), bf16[16,64,512]{2,1,0:T(8,128)(2,1)S(1)}, u32[]{:S(2)}, u32[]{:S(2)}) async-start(bf16[16,64,512]{2,1,0:T(8,128)(2,1)} %bitcast.32), calls=%async_computation.1 | async-start | bytes 2097152 | tf_op jit(solution)/shard_map/all_to_all | solution.py:616
  159.2 24.7 %all-to-all-done.1 = bf16[16,64,512]{2,1,0:T(8,128)(2,1)S(1)} async-done(((bf16[16,64,512]{2,1,0:T(8,128)(2,1)}), bf16[16,64,512]{2,1,0:T(8,128)(2,1)S(1)}, u32[]{:S(2)}, u32[]{:S(2)}) %all-to-all-start.1) | async-done | bytes 1048608 | tf_op jit(solution)/shard_map/all_to_all | solution.py:616
  183.9 1.5 shard_map.156
  (78 shorter events, 1.4 us)
Async XLA Ops:
  0.0 6.1 %copy-start = (bf16[864,512]{1,0:T(8,128)(2,1)S(1)}, bf16[864,512]{1,0:T(8,128)(2,1)}, u32[]{:S(2)}) copy-start(bf16[864,512]{1,0:T(8,128)(2,1)} %param.16) | copy-start | bytes 2654212
  0.0 9.1 %copy-start.18 = (s32[512,26]{0,1:T(8,128)S(1)}, s32[512,26]{0,1:T(8,128)}, u32[]{:S(2)}) copy-start(s32[512,26]{0,1:T(8,128)} %param.26) | copy-start | bytes 159748
  1.1 4.9 %collective-permute-start = (bf16[13,32,512]{2,1,0:T(8,128)(2,1)S(1)}, bf16[13,32,512]{2,1,0:T(8,128)(2,1)S(1)}, u32[]{:S(2)}, u32[]{:S(2)}) collective-permute-start(bf16[13,32,512]{2,1,0:T(8,128)(2,1)S(1)} %slice.72), channel_id=1, source_target_pairs={{0,1},{1,0},{2,3},{3,2},{4,5},{5,4},{6,7},{7,6},{8,9},{9,8},{10,11... | collective-permute-start | bytes 1277960 | tf_op jit(solution)/shard_map/ppermute | solution.py:414
  3.5 1.0 copy-start.3
  5.3 12.7 %copy-start.6 = (bf16[512,256]{1,0:T(8,128)(2,1)}, bf16[512,256]{1,0:T(8,128)(2,1)S(1)}, u32[]{:S(2)}) copy-start(bf16[512,256]{1,0:T(8,128)(2,1)S(1)} %get-tuple-element.52.own_rows) | copy-start | bytes 786436
  5.3 12.7 %copy-start.8 = (bf16[512,256]{1,0:T(8,128)(2,1)}, bf16[512,256]{1,0:T(8,128)(2,1)S(1)}, u32[]{:S(2)}) copy-start(bf16[512,256]{1,0:T(8,128)(2,1)S(1)} %get-tuple-element.53.other_rows) | copy-start | bytes 786436
  6.7 11.2 %collective-permute-start.3 = (bf16[192,512]{1,0:T(8,128)(2,1)S(1)}, bf16[192,512]{1,0:T(8,128)(2,1)S(1)}, u32[]{:S(2)}, u32[]{:S(2)}) collective-permute-start(bf16[192,512]{1,0:T(8,128)(2,1)S(1)} %get-tuple-element.46), channel_id=1, source_target_pairs={{0,8},{1,9},{2,10},{3,11},{4,12},{5,13},{6,14},{7,15},{8,0},{9,1},... | collective-permute-start | bytes 589832 | tf_op jit(solution)/shard_map/ppermute | solution.py:489
  9.1 22.5 %collective-permute-start.1 = (bf16[640,512]{1,0:T(8,128)(2,1)S(1)}, bf16[640,512]{1,0:T(8,128)(2,1)S(1)}, u32[]{:S(2)}, u32[]{:S(2)}) collective-permute-start(bf16[640,512]{1,0:T(8,128)(2,1)S(1)} %get-tuple-element.45), channel_id=1, source_target_pairs={{0,4},{1,3},{4,8},{5,1},{8,12},{9,5},{12,14},{13,9},{14,10},{15,13... | collective-permute-start | bytes 1966088 | tf_op jit(solution)/shard_map/ppermute | solution.py:467
  9.4 22.6 %collective-permute-start.2 = (bf16[640,512]{1,0:T(8,128)(2,1)S(1)}, bf16[640,512]{1,0:T(8,128)(2,1)S(1)}, u32[]{:S(2)}, u32[]{:S(2)}) collective-permute-start(bf16[640,512]{1,0:T(8,128)(2,1)S(1)} %get-tuple-element.45), channel_id=1, source_target_pairs={{0,2},{1,5},{4,0},{5,9},{8,4},{9,13},{12,8},{13,15},{14,12},{15,11... | collective-permute-start | bytes 1966088 | tf_op jit(solution)/shard_map/ppermute | solution.py:469
  17.9 13.7 %copy-start.1 = (bf16[192,512]{1,0:T(8,128)(2,1)}, bf16[192,512]{1,0:T(8,128)(2,1)S(1)}, u32[]{:S(2)}) copy-start(bf16[192,512]{1,0:T(8,128)(2,1)S(1)} %collective-permute-done.3.side_ref) | copy-start | bytes 589828
  18.0 8.1 %collective-permute-start.4 = (bf16[128,512]{1,0:T(8,128)(2,1)S(1)}, bf16[128,512]{1,0:T(8,128)(2,1)S(1)}, u32[]{:S(2)}, u32[]{:S(2)}) collective-permute-start(bf16[128,512]{1,0:T(8,128)(2,1)S(1)} %pad_maximum_fusion.3), channel_id=1, source_target_pairs={{0,1},{1,2},{2,3},{3,4},{4,5},{5,6},{6,7},{8,9},{9,10},{10,11},{11... | collective-permute-start | bytes 393224 | tf_op jit(solution)/shard_map/ppermute | solution.py:492
  22.2 6.8 %collective-permute-start.5 = (bf16[128,512]{1,0:T(8,128)(2,1)}, bf16[128,512]{1,0:T(8,128)(2,1)S(1)}, u32[]{:S(2)}, u32[]{:S(2)}) collective-permute-start(bf16[128,512]{1,0:T(8,128)(2,1)} %pad_maximum_fusion.4), channel_id=1, source_target_pairs={{1,0},{2,1},{3,2},{4,3},{5,4},{6,5},{7,6},{9,8},{10,9},{11,10},{12... | collective-permute-start | bytes 393224 | tf_op jit(solution)/shard_map/ppermute | solution.py:493
  26.1 0.6 copy-start.10
  28.9 0.6 copy-start.12
  32.0 22.8 %collective-permute-start.6 = (bf16[640,512]{1,0:T(8,128)(2,1)S(1)}, bf16[640,512]{1,0:T(8,128)(2,1)S(1)}, u32[]{:S(2)}, u32[]{:S(2)}) collective-permute-start(bf16[640,512]{1,0:T(8,128)(2,1)S(1)} %collective-permute-done.1.refs_3_.refs_4_), channel_id=1, source_target_pairs={{0,4},{1,3},{4,8},{5,1},{8,12},{9,5},{12,14},{13,9},{14,10},{15,13... | collective-permute-start | bytes 1966088 | tf_op jit(solution)/shard_map/ppermute | solution.py:467
  32.7 22.1 %collective-permute-start.7 = (bf16[640,512]{1,0:T(8,128)(2,1)S(1)}, bf16[640,512]{1,0:T(8,128)(2,1)S(1)}, u32[]{:S(2)}, u32[]{:S(2)}) collective-permute-start(bf16[640,512]{1,0:T(8,128)(2,1)S(1)} %collective-permute-done.2.refs_6_.refs_7_), channel_id=1, source_target_pairs={{0,2},{1,5},{4,0},{5,9},{8,4},{9,13},{12,8},{13,15},{14,12},{15,11... | collective-permute-start | bytes 1966088 | tf_op jit(solution)/shard_map/ppermute | solution.py:469
  37.3 8.5 %collective-permute-start.8 = (s32[512,26]{1,0:T(8,128)}, s32[512,26]{1,0:T(8,128)S(1)}, u32[]{:S(2)}, u32[]{:S(2)}) collective-permute-start(s32[512,26]{1,0:T(8,128)} %copy.37), channel_id=1, source_target_pairs={{0,1},{1,0},{2,3},{3,2},{4,5},{5,4},{6,7},{7,6},{8,9},{9,8},{10,11... | collective-permute-start | bytes 159752 | tf_op jit(solution)/shard_map/ppermute | solution.py:498
  38.1 0.9 copy-start.2
  39.0 0.9 copy-start.7
  39.9 0.9 copy-start.9
  40.9 0.9 copy-start.11
  41.8 0.9 copy-start.13
  42.7 3.2 %copy-start.16 = (s32[512,13]{1,0:T(8,128)S(1)}, s32[512,13]{1,0:T(8,128)}, u32[]{:S(2)}) copy-start(s32[512,13]{1,0:T(8,128)} %copy.35) | copy-start | bytes 79876
  42.7 3.2 %copy-start.17 = (s32[512,13]{1,0:T(8,128)S(1)}, s32[512,13]{1,0:T(8,128)}, u32[]{:S(2)}) copy-start(s32[512,13]{1,0:T(8,128)} %copy.36) | copy-start | bytes 79876
  43.3 11.4 %collective-permute-start.9 = (bf16[896,256]{1,0:T(8,128)(2,1)S(1)}, bf16[896,256]{1,0:T(8,128)(2,1)S(1)}, u32[]{:S(2)}, u32[]{:S(2)}) collective-permute-start(bf16[896,256]{1,0:T(8,128)(2,1)S(1)} %get-tuple-element.59), channel_id=1, source_target_pairs={{0,1},{1,0},{2,3},{3,2},{4,5},{5,4},{6,7},{7,6},{8,9},{9,8},{10,11... | collective-permute-start | bytes 1376264 | tf_op jit(solution)/shard_map/ppermute | solution.py:532
  44.5 21.0 %collective-permute-start.12 = (bf16[448,512]{1,0:T(8,128)(2,1)S(1)}, bf16[448,512]{1,0:T(8,128)(2,1)S(1)}, u32[]{:S(2)}, u32[]{:S(2)}) collective-permute-start(bf16[448,512]{1,0:T(8,128)(2,1)S(1)} %pad_maximum_fusion), channel_id=1, source_target_pairs={{0,16},{16,0},{1,17},{17,1},{2,18},{18,2},{3,19},{19,3},{4,20},{20... | collective-permute-start | bytes 1376264 | tf_op jit(solution)/shard_map/ppermute | solution.py:475
  54.8 16.7 %collective-permute-start.10 = (bf16[640,512]{1,0:T(8,128)(2,1)S(1)}, bf16[640,512]{1,0:T(8,128)(2,1)S(1)}, u32[]{:S(2)}, u32[]{:S(2)}) collective-permute-start(bf16[640,512]{1,0:T(8,128)(2,1)S(1)} %collective-permute-done.6.refs_2_.refs_3_), channel_id=1, source_target_pairs={{0,4},{1,3},{4,8},{5,1},{8,12},{9,5},{12,14},{13,9},{14,10},{15,13... | collective-permute-start | bytes 1966088 | tf_op jit(solution)/shard_map/ppermute | solution.py:467
  54.9 16.6 %collective-permute-start.11 = (bf16[640,512]{1,0:T(8,128)(2,1)S(1)}, bf16[640,512]{1,0:T(8,128)(2,1)S(1)}, u32[]{:S(2)}, u32[]{:S(2)}) collective-permute-start(bf16[640,512]{1,0:T(8,128)(2,1)S(1)} %collective-permute-done.7.refs_5_.refs_6_), channel_id=1, source_target_pairs={{0,2},{1,5},{4,0},{5,9},{8,4},{9,13},{12,8},{13,15},{14,12},{15,11... | collective-permute-start | bytes 1966088 | tf_op jit(solution)/shard_map/ppermute | solution.py:469
  56.6 14.9 %collective-permute-start.13 = (bf16[448,512]{1,0:T(8,128)(2,1)S(1)}, bf16[448,512]{1,0:T(8,128)(2,1)S(1)}, u32[]{:S(2)}, u32[]{:S(2)}) collective-permute-start(bf16[448,512]{1,0:T(8,128)(2,1)S(1)} %pad_maximum_fusion.1), channel_id=1, source_target_pairs={{0,16},{16,0},{1,17},{17,1},{2,18},{18,2},{3,19},{19,3},{4,20},{20... | collective-permute-start | bytes 1376264 | tf_op jit(solution)/shard_map/ppermute | solution.py:475
  71.5 10.0 %collective-permute-start.14 = (bf16[640,512]{1,0:T(8,128)(2,1)S(1)}, bf16[640,512]{1,0:T(8,128)(2,1)S(1)}, u32[]{:S(2)}, u32[]{:S(2)}) collective-permute-start(bf16[640,512]{1,0:T(8,128)(2,1)S(1)} %collective-permute-done.10.refs_2_.refs_3_), channel_id=1, source_target_pairs={{0,4},{1,3},{4,8},{5,1},{8,12},{9,5},{12,14},{13,9},{14,10},{15,13... | collective-permute-start | bytes 1966088 | tf_op jit(solution)/shard_map/ppermute | solution.py:467
  72.3 15.4 %collective-permute-start.16 = (bf16[448,512]{1,0:T(8,128)(2,1)S(1)}, bf16[448,512]{1,0:T(8,128)(2,1)S(1)}, u32[]{:S(2)}, u32[]{:S(2)}) collective-permute-start(bf16[448,512]{1,0:T(8,128)(2,1)S(1)} %pad_maximum_fusion.2), channel_id=1, source_target_pairs={{0,16},{16,0},{1,17},{17,1},{2,18},{18,2},{3,19},{19,3},{4,20},{20... | collective-permute-start | bytes 1376264 | tf_op jit(solution)/shard_map/ppermute | solution.py:475
  81.5 11.1 %collective-permute-start.15 = (bf16[224,512]{1,0:T(8,128)(2,1)S(1)}, bf16[224,512]{1,0:T(8,128)(2,1)S(1)}, u32[]{:S(2)}, u32[]{:S(2)}) collective-permute-start(bf16[224,512]{1,0:T(8,128)(2,1)S(1)} %slice.100), channel_id=1, source_target_pairs={{0,16},{16,0},{1,17},{17,1},{2,18},{18,2},{3,19},{19,3},{4,20},{20... | collective-permute-start | bytes 688136 | tf_op jit(solution)/shard_map/ppermute | solution.py:475
  92.7 5.3 %copy-start.19 = (s32[512]{0:T(512)S(1)}, s32[512]{0:T(512)}, u32[]{:S(2)}) copy-start(s32[512]{0:T(512)} %param.27) | copy-start | bytes 6148
  92.7 6.9 %copy-start.4 = (bf16[512,512]{1,0:T(8,128)(2,1)S(1)}, bf16[512,512]{1,0:T(8,128)(2,1)}, u32[]{:S(2)}) copy-start(bf16[512,512]{1,0:T(8,128)(2,1)} %features_ref.3) | copy-start | bytes 1572868
  92.7 6.9 %copy-start.5 = (bf16[512,512]{1,0:T(8,128)(2,1)S(1)}, bf16[512,512]{1,0:T(8,128)(2,1)}, u32[]{:S(2)}) copy-start(bf16[512,512]{1,0:T(8,128)(2,1)} %weight_ref.1) | copy-start | bytes 1572868
  92.7 6.9 %copy-start.14 = (f32[512]{0:T(512)S(1)}, f32[512]{0:T(512)}, u32[]{:S(2)}) copy-start(f32[512]{0:T(512)} %param.18) | copy-start | bytes 6148
  95.4 4.1 %collective-permute-start.17 = (bf16[512,512]{1,0:T(8,128)(2,1)S(1)}, bf16[512,512]{1,0:T(8,128)(2,1)S(1)}, u32[]{:S(2)}, u32[]{:S(2)}) collective-permute-start(bf16[512,512]{1,0:T(8,128)(2,1)S(1)} %get-tuple-element.78), channel_id=1, source_target_pairs={{0,1},{1,0},{2,3},{3,2},{4,5},{5,4},{6,7},{7,6},{8,9},{9,8},{10,11... | collective-permute-start | bytes 1572872 | tf_op jit(solution)/shard_map/ppermute | solution.py:567
  99.5 8.0 %copy-start.15 = (bf16[512,1536]{1,0:T(8,128)(2,1)S(1)}, bf16[512,1536]{1,0:T(8,128)(2,1)}, u32[]{:S(2)}) copy-start(bf16[512,1536]{1,0:T(8,128)(2,1)} %param.20) | copy-start | bytes 4718596
  101.8 30.6 %all-to-all-start = ((bf16[16,64,512]{2,1,0:T(8,128)(2,1)}), bf16[16,64,512]{2,1,0:T(8,128)(2,1)}, u32[]{:S(2)}, u32[]{:S(2)}) async-start(bf16[16,64,512]{2,1,0:T(8,128)(2,1)} %bitcast.11), calls=%async_computation | async-start | bytes 2097152 | tf_op jit(solution)/shard_map/all_to_all | solution.py:583
  107.5 1.3 copy-start.21
  109.2 23.3 %copy-start.20 = (s32[512]{0:T(512)}, s32[512]{0:T(512)S(1)}, u32[]{:S(2)}) copy-start(s32[512]{0:T(512)S(1)} %multiply_add_fusion) | copy-start | bytes 6148
  154.1 29.8 %all-to-all-start.1 = ((bf16[16,64,512]{2,1,0:T(8,128)(2,1)}), bf16[16,64,512]{2,1,0:T(8,128)(2,1)S(1)}, u32[]{:S(2)}, u32[]{:S(2)}) async-start(bf16[16,64,512]{2,1,0:T(8,128)(2,1)} %bitcast.32), calls=%async_computation.1 | async-start | bytes 2097152 | tf_op jit(solution)/shard_map/all_to_all | solution.py:616

commit v21 on v20

--- a/solution.py
+++ b/solution.py
@@ -18,7 +18,7 @@
 F32 = jnp.float32
 BF16 = jnp.bfloat16
 MIB = 1 << 20
-GATHER_LIMIT, CONV_LIMIT = 24, 24
+GATHER_LIMIT, CONV_LIMIT = 20, 20
 
 
 def dot(left, right):
@@ -538,10 +538,10 @@
     other_stacked = gather_block(start, other_rows, other_table)
     stacked = other_stacked, own_stacked
     if round_trip:
+        *stacked, middle_got = pass_on(*stacked, middle[0][2][0])
+        middle = [[*parts[:2], (middle_got, *parts[2][1:])] for parts in middle]
         early = [[(mine, 0, rows, 0, None)]] + near
         sums = conv_part(stacked, places[:6], shifts, early, None, length, CONV_LIMIT)
-        *sums, middle_got = pass_on(*sums, middle[0][2][0])
-        middle = [[*parts[:2], (middle_got, *parts[2][1:])] for parts in middle]
         far = complete(first[3], second[3])
         opposite = complete(first[4])
         sums = conv_part(stacked, places[6:10], shifts, middle, sums, length, CONV_LIMIT)

time: 186 us -> 183 us (0.984)
  waiting for transfers between devices: 67.4 us -> 65.1 us
    ppermute x4, waiting for transfers between devices: 10.3 us -> 4.68 us  [pass_on(): first.append(lax.ppermute(first[-1], 'blocks', first_pairs))]
    ppermute x4, waiting for transfers between devices: 0.01 us -> 2.19 us  [complete(): got = lax.ppermute(lent, 'groups', [(0, 1), (1, 0)])]
  transfers between devices with their start and end apart: 20 -> 20, of which waited for: 8 -> 11; matrix products, arithmetic and copies ran while one was open for 8% -> 8% of each run, Pallas kernels for 18% -> 19%
where the time goes in v21:
time: 183 us
  waiting for transfers between devices  65.1 us (36%)
  Pallas kernels  62.9 us (34%)
  starting transfers between devices  32.1 us (18%)
  local copies, waits for them, and re-layouts  17.4 us (10%)
  other arithmetic  4.79 us (3%)
    all_to_all x1, waiting for transfers between devices, body(): lax.all_to_all(back.reshape(devices, capacity, width), 'blocks', split_ax...  24.7 us
    pallas_call x1, Pallas kernels, body(): call(block_kernel, jax.ShapeDtypeStruct((slots, width), BF16), 60, 20 * p...  21.6 us
    all_to_all x1, waiting for transfers between devices, body(): lax.all_to_all(outgoing.reshape(devices, capacity, width), 'blocks', spli...  21.4 us
    pallas_call x4, Pallas kernels, conv_part(): call(functools.partial(conv_kernel, slots, before is None), [jax.ShapeDty...  18.6 us
    pallas_call x2, Pallas kernels, gather_block(): call(functools.partial(gather_kernel, taps), jax.ShapeDtypeStruct((points...  16.9 us
    unnamed x46, local copies, waits for them, and re-layouts  7.44 us
    ppermute x1, waiting for transfers between devices, body(): lists = lax.ppermute(lists, 'blocks', across)  7.29 us
    all_to_all x1, starting transfers between devices, body(): lax.all_to_all(outgoing.reshape(devices, capacity, width), 'blocks', spli...  5.53 us
  transfers between devices with their start and end apart: 20, of which 11 were waited for; matrix products, arithmetic and copies ran while one was open for 8% of the time, Pallas kernels for 19%

profile of v21, /device:TPU:9, one launch (start us, length us, event | category | flops | bytes accessed | tf_op | source)
XLA Modules:
  0.0 182.7 jit_solution(16216878249353453234)
XLA Ops:
  0.0 1.1 slice.72
  1.1 0.7 collective-permute-start
  1.9 0.8 select_bitcast_fusion
  2.6 0.7 slice_bitcast_fusion
  3.5 1.0 copy-done.3
  4.5 0.7 shard_map.146
  5.4 0.7 shard_map.145
  6.0 2.4 %collective-permute-start.3 = (bf16[192,512]{1,0:T(8,128)(2,1)S(1)}, bf16[192,512]{1,0:T(8,128)(2,1)S(1)}, u32[]{:S(2)}, u32[]{:S(2)}) collective-permute-start(bf16[192,512]{1,0:T(8,128)(2,1)S(1)} %get-tuple-element.46), channel_id=1, source_target_pairs={{0,8},{1,9},{2,10},{3,11},{4,12},{5,13},{6,14},{7,15},{8,0},{9,1},... | collective-permute-start | bytes 589832 | tf_op jit(solution)/shard_map/ppermute | solution.py:489
  8.6 1.3 collective-permute-start.2
  9.9 7.3 %collective-permute-done.3.side_ref = bf16[192,512]{1,0:T(8,128)(2,1)S(1)} collective-permute-done((bf16[192,512]{1,0:T(8,128)(2,1)S(1)}, bf16[192,512]{1,0:T(8,128)(2,1)S(1)}, u32[]{:S(2)}, u32[]{:S(2)}) %collective-permute-start.3) | collective-permute-done | bytes 196640 | tf_op jit(solution)/shard_map/ppermute | solution.py:489
  17.3 3.5 %collective-permute-start.4 = (bf16[128,512]{1,0:T(8,128)(2,1)S(1)}, bf16[128,512]{1,0:T(8,128)(2,1)S(1)}, u32[]{:S(2)}, u32[]{:S(2)}) collective-permute-start(bf16[128,512]{1,0:T(8,128)(2,1)S(1)} %pad_maximum_fusion.3), channel_id=1, source_target_pairs={{0,1},{1,2},{2,3},{3,4},{4,5},{5,6},{6,7},{8,9},{9,10},{10,11},{11... | collective-permute-start | bytes 393224 | tf_op jit(solution)/shard_map/ppermute | solution.py:492
  20.8 0.7 pad_maximum_fusion.4
  21.4 1.9 %collective-permute-start.5 = (bf16[128,512]{1,0:T(8,128)(2,1)}, bf16[128,512]{1,0:T(8,128)(2,1)S(1)}, u32[]{:S(2)}, u32[]{:S(2)}) collective-permute-start(bf16[128,512]{1,0:T(8,128)(2,1)} %pad_maximum_fusion.4), channel_id=1, source_target_pairs={{1,0},{2,1},{3,2},{4,3},{5,4},{6,5},{7,6},{9,8},{10,9},{11,10},{12... | collective-permute-start | bytes 393224 | tf_op jit(solution)/shard_map/ppermute | solution.py:493
  23.4 0.7 constant_dynamic-slice_fusion
  24.1 0.9 copy.35
  25.0 0.8 copy.36
  26.0 0.6 copy-done.10
  26.6 1.6 collective-permute-done.5.ahead_ref
  28.2 0.6 copy-done.12
  28.9 2.1 %collective-permute-done.1.refs_3_.refs_4_ = bf16[640,512]{1,0:T(8,128)(2,1)S(1)} collective-permute-done((bf16[640,512]{1,0:T(8,128)(2,1)S(1)}, bf16[640,512]{1,0:T(8,128)(2,1)S(1)}, u32[]{:S(2)}, u32[]{:S(2)}) %collective-permute-start.1) | collective-permute-done | bytes 655392 | tf_op jit(solution)/shard_map/ppermute | solution.py:467
  30.9 0.3 collective-permute-done.2.refs_6_.refs_7_
  31.3 0.7 slice.91
  32.0 2.2 %collective-permute-start.7 = (bf16[640,512]{1,0:T(8,128)(2,1)S(1)}, bf16[640,512]{1,0:T(8,128)(2,1)S(1)}, u32[]{:S(2)}, u32[]{:S(2)}) collective-permute-start(bf16[640,512]{1,0:T(8,128)(2,1)S(1)} %collective-permute-done.2.refs_6_.refs_7_), channel_id=1, source_target_pairs={{0,2},{1,5},{4,0},{5,9},{8,4},{9,13},{12,8},{13,15},{14,12},{15,11... | collective-permute-start | bytes 1966088 | tf_op jit(solution)/shard_map/ppermute | solution.py:469
  34.2 0.7 slice.92
  34.9 1.7 copy.37
  36.6 0.8 collective-permute-start.8
  37.3 0.9 copy-done.2
  38.3 0.9 copy-done.7
  39.2 0.9 copy-done.9
  40.2 0.9 copy-done.11
  41.1 0.9 copy-done.13
  42.0 0.6 shard_map.147
  42.7 1.1 pad_maximum_fusion.2
  43.8 1.3 collective-permute-start.16
  45.2 0.3 add_convert_fusion.1
  45.5 8.5 %shard_map.148.refs_1_ = bf16[512,6912]{1,0:T(8,128)(2,1)S(1)} custom-call(s32[1]{0:T(128)} %bitcast.7.start_ref, f32[512,128]{1,0:T(8,128)S(1)} %get-tuple-element.83.rows_ref, bf16[896,256]{1,0:T(8,128)(2,1)S(1)} %get-tuple-element.57.table_ref), custom_call_target="tpu_custom_call" | custom-call | flops 6341787648 | bytes 7077888 | tf_op jit(solution)/shard_map/pallas_call | solution.py:137
  54.2 1.7 collective-permute-start.11
  55.9 0.3 collective-permute-start.12
  56.3 8.5 %shard_map.149.refs_0_ = bf16[512,6912]{1,0:T(8,128)(2,1)S(1)} custom-call(s32[1]{0:T(128)} %bitcast.7.start_ref, f32[512,128]{1,0:T(8,128)S(1)} %get-tuple-element.62.rows_ref, bf16[896,256]{1,0:T(8,128)(2,1)S(1)} %collective-permute-done.9.table_ref), custom_call_target="tpu_custom_call" | custom-call | flops 6341787648 | bytes 7077888 | tf_op jit(solution)/shard_map/pallas_call | solution.py:137
  64.7 2.2 %collective-permute-done.12.refs_4_.refs_7_ = bf16[448,512]{1,0:T(8,128)(2,1)S(1)} collective-permute-done((bf16[448,512]{1,0:T(8,128)(2,1)S(1)}, bf16[448,512]{1,0:T(8,128)(2,1)S(1)}, u32[]{:S(2)}, u32[]{:S(2)}) %collective-permute-start.12) | collective-permute-done | bytes 458784 | tf_op jit(solution)/shard_map/ppermute | solution.py:475
  66.9 1.1 collective-permute-done.10.refs_2_.refs_3_
  68.0 1.8 collective-permute-done.11.refs_5_.refs_6_
  69.8 1.7 collective-permute-start.13
  71.8 0.3 collective-permute-start.15
  72.2 6.0 %shard_map.150 = (f32[512,512]{1,0:T(8,128)S(1)}, f32[512,512]{1,0:T(8,128)S(1)}) custom-call(s32[6]{0:T(128)S(1)} %bitcast.30, s32[2]{0:T(128)S(1)} %pad_add_fusion.2.shifts_ref, bf16[512,6912]{1,0:T(8,128)(2,1)S(1)} %shard_map.149.refs_0_, bf16[512,6912]{1,0:T(8,128)(2,1)S(1)} %shard_map.148.refs_1_, bf16[864,512]{1,0:T(8,128)(2,1)S(1)} %get-tuple-element.70.refs_2_, ...), custom_call_target="tpu_custom_call" | custom-call | flops 3221225472 | bytes 9437184 | tf_op jit(solution)/shard_map/pallas_call | solution.py:206
  78.2 1.5 collective-permute-done.13.refs_2_.refs_3_
  79.8 0.3 collective-permute-start.14
  80.1 4.9 %shard_map.151 = (f32[512,512]{1,0:T(8,128)S(1)}, f32[512,512]{1,0:T(8,128)S(1)}) custom-call(s32[4]{0:T(128)S(1)} %get-tuple-element.90.places_ref, s32[2]{0:T(128)S(1)} %pad_add_fusion.2.shifts_ref, bf16[512,6912]{1,0:T(8,128)(2,1)S(1)} %shard_map.149.refs_0_, ...), custom_call_target="tpu_custom_call", output_to_operand_aliasing={{0}: (10, {}), {1}: (11, {})} | custom-call | flops 2147483648 | bytes 6291456 | tf_op jit(solution)/shard_map/pallas_call | solution.py:206
  85.0 4.9 %shard_map.152 = (f32[512,512]{1,0:T(8,128)S(1)}, f32[512,512]{1,0:T(8,128)S(1)}) custom-call(s32[4]{0:T(128)S(1)} %get-tuple-element.91.places_ref, s32[2]{0:T(128)S(1)} %pad_add_fusion.2.shifts_ref, bf16[512,6912]{1,0:T(8,128)(2,1)S(1)} %shard_map.149.refs_0_, ...), custom_call_target="tpu_custom_call", output_to_operand_aliasing={{0}: (10, {}), {1}: (11, {})} | custom-call | flops 2147483648 | bytes 6291456 | tf_op jit(solution)/shard_map/pallas_call | solution.py:206
  90.0 2.7 %shard_map.153 = (bf16[512,512]{1,0:T(8,128)(2,1)S(1)}, f32[512,512]{1,0:T(8,128)S(1)}) custom-call(s32[2]{0:T(128)S(1)} %slice.78.places_ref, s32[2]{0:T(128)S(1)} %pad_add_fusion.2.shifts_ref, bf16[512,6912]{1,0:T(8,128)(2,1)S(1)} %shard_map.149.refs_0_, bf16[512,6912]{1,0:T(8,128)(2,1)S(1)} %shard_map.148.refs_1_, ...), custom_call_target="tpu_custom_call", output_to_operand_aliasing={{1}: (8, {})} | custom-call | flops 1073741824 | bytes 3145728 | tf_op jit(solution)/shard_map/pallas_call | solution.py:206
  92.7 2.7 %collective-permute-start.17 = (bf16[512,512]{1,0:T(8,128)(2,1)S(1)}, bf16[512,512]{1,0:T(8,128)(2,1)S(1)}, u32[]{:S(2)}, u32[]{:S(2)}) collective-permute-start(bf16[512,512]{1,0:T(8,128)(2,1)S(1)} %get-tuple-element.78), channel_id=1, source_target_pairs={{0,1},{1,0},{2,3},{3,2},{4,5},{5,4},{6,7},{7,6},{8,9},{9,8},{10,11... | collective-permute-start | bytes 1572872 | tf_op jit(solution)/shard_map/ppermute | solution.py:567
  95.4 0.3 convert_reduce_fusion.1
  95.8 1.2 collective-permute-done.17.got_ref
  97.0 2.3 %shard_map.154 = bf16[1024,512]{1,0:T(8,128)(2,1)} custom-call(f32[512,512]{1,0:T(8,128)S(1)} %get-tuple-element.77.own_ref, bf16[512,512]{1,0:T(8,128)(2,1)S(1)} %collective-permute-done.17.got_ref, bf16[512,512]{1,0:T(8,128)(2,1)S(1)} %copy-done.4, bf16[512,512]{1,0:T(8,128)(2,1)S(1)} %copy-done.5, f32[1,512]{1,0:T(1,128)S(1)} %bitcast.31, ...), custom_call_target="tpu_custom_call" | custom-call | flops 805306368 | bytes 2097152 | tf_op jit(solution)/shard_map/pallas_call | solution.py:569
  99.3 5.5 %all-to-all-start = ((bf16[16,64,512]{2,1,0:T(8,128)(2,1)}), bf16[16,64,512]{2,1,0:T(8,128)(2,1)}, u32[]{:S(2)}, u32[]{:S(2)}) async-start(bf16[16,64,512]{2,1,0:T(8,128)(2,1)} %bitcast.11), calls=%async_computation | async-start | bytes 2097152 | tf_op jit(solution)/shard_map/all_to_all | solution.py:583
  104.8 0.9 fusion.5
  106.2 0.2 convert_reduce_fusion
  106.5 0.9 copy.40.slot_col_ref
  107.3 1.1 maximum_bitcast_fusion.qv_hbm
  108.4 21.4 %all-to-all-done = bf16[16,64,512]{2,1,0:T(8,128)(2,1)} async-done(((bf16[16,64,512]{2,1,0:T(8,128)(2,1)}), bf16[16,64,512]{2,1,0:T(8,128)(2,1)}, u32[]{:S(2)}, u32[]{:S(2)}) %all-to-all-start) | async-done | bytes 1048608 | tf_op jit(solution)/shard_map/all_to_all | solution.py:583
  129.8 21.6 %shard_map.155 = bf16[1024,512]{1,0:T(8,128)(2,1)} custom-call(bf16[1024,512]{1,0:T(8,128)(2,1)} %bitcast.12.arrived_ref, s32[512,1]{1,0:T(8,128)} %copy.40.slot_col_ref, s32[1,512]{1,0:T(1,128)} %bitcast.34, f32[1,512]{1,0:T(1,128)} %bitcast.35, f32[1,512]{1,0:T(1,128)} %bitcast.36, bf16[1024,512]{1,0:T(8,128)(2,1)} %maximum_bitcast_fusion.qv_hbm, ...), custom_call_target="tpu_custom_call" | custom-call | flops 2684354560 | bytes 4194304 | tf_op jit(solution)/shard_map/pallas_call | solution.py:590
  151.4 5.0 %all-to-all-start.1 = ((bf16[16,64,512]{2,1,0:T(8,128)(2,1)}), bf16[16,64,512]{2,1,0:T(8,128)(2,1)S(1)}, u32[]{:S(2)}, u32[]{:S(2)}) async-start(bf16[16,64,512]{2,1,0:T(8,128)(2,1)} %bitcast.32), calls=%async_computation.1 | async-start | bytes 2097152 | tf_op jit(solution)/shard_map/all_to_all | solution.py:616
  156.5 24.7 %all-to-all-done.1 = bf16[16,64,512]{2,1,0:T(8,128)(2,1)S(1)} async-done(((bf16[16,64,512]{2,1,0:T(8,128)(2,1)}), bf16[16,64,512]{2,1,0:T(8,128)(2,1)S(1)}, u32[]{:S(2)}, u32[]{:S(2)}) %all-to-all-start.1) | async-done | bytes 1048608 | tf_op jit(solution)/shard_map/all_to_all | solution.py:616
  181.2 1.5 shard_map.156
  (78 shorter events, 2.1 us)
Async XLA Ops:
  0.0 5.4 %copy-start = (bf16[864,512]{1,0:T(8,128)(2,1)S(1)}, bf16[864,512]{1,0:T(8,128)(2,1)}, u32[]{:S(2)}) copy-start(bf16[864,512]{1,0:T(8,128)(2,1)} %param.16) | copy-start | bytes 2654212
  0.0 8.4 %copy-start.18 = (s32[512,26]{0,1:T(8,128)S(1)}, s32[512,26]{0,1:T(8,128)}, u32[]{:S(2)}) copy-start(s32[512,26]{0,1:T(8,128)} %param.26) | copy-start | bytes 159748
  1.1 4.2 %collective-permute-start = (bf16[13,32,512]{2,1,0:T(8,128)(2,1)S(1)}, bf16[13,32,512]{2,1,0:T(8,128)(2,1)S(1)}, u32[]{:S(2)}, u32[]{:S(2)}) collective-permute-start(bf16[13,32,512]{2,1,0:T(8,128)(2,1)S(1)} %slice.72), channel_id=1, source_target_pairs={{0,1},{1,0},{2,3},{3,2},{4,5},{5,4},{6,7},{7,6},{8,9},{9,8},{10,11... | collective-permute-start | bytes 1277960 | tf_op jit(solution)/shard_map/ppermute | solution.py:414
  3.5 1.0 copy-start.3
  5.3 12.0 %copy-start.6 = (bf16[512,256]{1,0:T(8,128)(2,1)}, bf16[512,256]{1,0:T(8,128)(2,1)S(1)}, u32[]{:S(2)}) copy-start(bf16[512,256]{1,0:T(8,128)(2,1)S(1)} %get-tuple-element.52.own_rows) | copy-start | bytes 786436
  5.3 12.0 %copy-start.8 = (bf16[512,256]{1,0:T(8,128)(2,1)}, bf16[512,256]{1,0:T(8,128)(2,1)S(1)}, u32[]{:S(2)}) copy-start(bf16[512,256]{1,0:T(8,128)(2,1)S(1)} %get-tuple-element.53.other_rows) | copy-start | bytes 786436
  6.0 11.2 %collective-permute-start.3 = (bf16[192,512]{1,0:T(8,128)(2,1)S(1)}, bf16[192,512]{1,0:T(8,128)(2,1)S(1)}, u32[]{:S(2)}, u32[]{:S(2)}) collective-permute-start(bf16[192,512]{1,0:T(8,128)(2,1)S(1)} %get-tuple-element.46), channel_id=1, source_target_pairs={{0,8},{1,9},{2,10},{3,11},{4,12},{5,13},{6,14},{7,15},{8,0},{9,1},... | collective-permute-start | bytes 589832 | tf_op jit(solution)/shard_map/ppermute | solution.py:489
  8.4 22.5 %collective-permute-start.1 = (bf16[640,512]{1,0:T(8,128)(2,1)S(1)}, bf16[640,512]{1,0:T(8,128)(2,1)S(1)}, u32[]{:S(2)}, u32[]{:S(2)}) collective-permute-start(bf16[640,512]{1,0:T(8,128)(2,1)S(1)} %get-tuple-element.45), channel_id=1, source_target_pairs={{0,4},{1,3},{4,8},{5,1},{8,12},{9,5},{12,14},{13,9},{14,10},{15,13... | collective-permute-start | bytes 1966088 | tf_op jit(solution)/shard_map/ppermute | solution.py:467
  8.6 22.6 %collective-permute-start.2 = (bf16[640,512]{1,0:T(8,128)(2,1)S(1)}, bf16[640,512]{1,0:T(8,128)(2,1)S(1)}, u32[]{:S(2)}, u32[]{:S(2)}) collective-permute-start(bf16[640,512]{1,0:T(8,128)(2,1)S(1)} %get-tuple-element.45), channel_id=1, source_target_pairs={{0,2},{1,5},{4,0},{5,9},{8,4},{9,13},{12,8},{13,15},{14,12},{15,11... | collective-permute-start | bytes 1966088 | tf_op jit(solution)/shard_map/ppermute | solution.py:469
  17.2 13.7 %copy-start.1 = (bf16[192,512]{1,0:T(8,128)(2,1)}, bf16[192,512]{1,0:T(8,128)(2,1)S(1)}, u32[]{:S(2)}) copy-start(bf16[192,512]{1,0:T(8,128)(2,1)S(1)} %collective-permute-done.3.side_ref) | copy-start | bytes 589828
  17.3 8.7 %collective-permute-start.4 = (bf16[128,512]{1,0:T(8,128)(2,1)S(1)}, bf16[128,512]{1,0:T(8,128)(2,1)S(1)}, u32[]{:S(2)}, u32[]{:S(2)}) collective-permute-start(bf16[128,512]{1,0:T(8,128)(2,1)S(1)} %pad_maximum_fusion.3), channel_id=1, source_target_pairs={{0,1},{1,2},{2,3},{3,4},{4,5},{5,6},{6,7},{8,9},{9,10},{10,11},{11... | collective-permute-start | bytes 393224 | tf_op jit(solution)/shard_map/ppermute | solution.py:492
  21.4 6.8 %collective-permute-start.5 = (bf16[128,512]{1,0:T(8,128)(2,1)}, bf16[128,512]{1,0:T(8,128)(2,1)S(1)}, u32[]{:S(2)}, u32[]{:S(2)}) collective-permute-start(bf16[128,512]{1,0:T(8,128)(2,1)} %pad_maximum_fusion.4), channel_id=1, source_target_pairs={{1,0},{2,1},{3,2},{4,3},{5,4},{6,5},{7,6},{9,8},{10,9},{11,10},{12... | collective-permute-start | bytes 393224 | tf_op jit(solution)/shard_map/ppermute | solution.py:493
  26.0 0.6 copy-start.10
  28.2 0.6 copy-start.12
  31.3 22.8 %collective-permute-start.6 = (bf16[640,512]{1,0:T(8,128)(2,1)S(1)}, bf16[640,512]{1,0:T(8,128)(2,1)S(1)}, u32[]{:S(2)}, u32[]{:S(2)}) collective-permute-start(bf16[640,512]{1,0:T(8,128)(2,1)S(1)} %collective-permute-done.1.refs_3_.refs_4_), channel_id=1, source_target_pairs={{0,4},{1,3},{4,8},{5,1},{8,12},{9,5},{12,14},{13,9},{14,10},{15,13... | collective-permute-start | bytes 1966088 | tf_op jit(solution)/shard_map/ppermute | solution.py:467
  32.0 22.0 %collective-permute-start.7 = (bf16[640,512]{1,0:T(8,128)(2,1)S(1)}, bf16[640,512]{1,0:T(8,128)(2,1)S(1)}, u32[]{:S(2)}, u32[]{:S(2)}) collective-permute-start(bf16[640,512]{1,0:T(8,128)(2,1)S(1)} %collective-permute-done.2.refs_6_.refs_7_), channel_id=1, source_target_pairs={{0,2},{1,5},{4,0},{5,9},{8,4},{9,13},{12,8},{13,15},{14,12},{15,11... | collective-permute-start | bytes 1966088 | tf_op jit(solution)/shard_map/ppermute | solution.py:469
  36.6 8.5 %collective-permute-start.8 = (s32[512,26]{1,0:T(8,128)}, s32[512,26]{1,0:T(8,128)S(1)}, u32[]{:S(2)}, u32[]{:S(2)}) collective-permute-start(s32[512,26]{1,0:T(8,128)} %copy.37), channel_id=1, source_target_pairs={{0,1},{1,0},{2,3},{3,2},{4,5},{5,4},{6,7},{7,6},{8,9},{9,8},{10,11... | collective-permute-start | bytes 159752 | tf_op jit(solution)/shard_map/ppermute | solution.py:498
  37.3 0.9 copy-start.2
  38.3 0.9 copy-start.7
  39.2 0.9 copy-start.9
  40.2 0.9 copy-start.11
  41.1 0.9 copy-start.13
  42.0 3.2 %copy-start.16 = (s32[512,13]{1,0:T(8,128)S(1)}, s32[512,13]{1,0:T(8,128)}, u32[]{:S(2)}) copy-start(s32[512,13]{1,0:T(8,128)} %copy.35) | copy-start | bytes 79876
  42.0 3.2 %copy-start.17 = (s32[512,13]{1,0:T(8,128)S(1)}, s32[512,13]{1,0:T(8,128)}, u32[]{:S(2)}) copy-start(s32[512,13]{1,0:T(8,128)} %copy.36) | copy-start | bytes 79876
  42.6 11.4 %collective-permute-start.9 = (bf16[896,256]{1,0:T(8,128)(2,1)S(1)}, bf16[896,256]{1,0:T(8,128)(2,1)S(1)}, u32[]{:S(2)}, u32[]{:S(2)}) collective-permute-start(bf16[896,256]{1,0:T(8,128)(2,1)S(1)} %get-tuple-element.59), channel_id=1, source_target_pairs={{0,1},{1,0},{2,3},{3,2},{4,5},{5,4},{6,7},{7,6},{8,9},{9,8},{10,11... | collective-permute-start | bytes 1376264 | tf_op jit(solution)/shard_map/ppermute | solution.py:532
  43.8 28.4 %collective-permute-start.16 = (bf16[448,512]{1,0:T(8,128)(2,1)S(1)}, bf16[448,512]{1,0:T(8,128)(2,1)S(1)}, u32[]{:S(2)}, u32[]{:S(2)}) collective-permute-start(bf16[448,512]{1,0:T(8,128)(2,1)S(1)} %pad_maximum_fusion.2), channel_id=1, source_target_pairs={{0,16},{16,0},{1,17},{17,1},{2,18},{18,2},{3,19},{19,3},{4,20},{20... | collective-permute-start | bytes 1376264 | tf_op jit(solution)/shard_map/ppermute | solution.py:475
  54.1 13.9 %collective-permute-start.10 = (bf16[640,512]{1,0:T(8,128)(2,1)S(1)}, bf16[640,512]{1,0:T(8,128)(2,1)S(1)}, u32[]{:S(2)}, u32[]{:S(2)}) collective-permute-start(bf16[640,512]{1,0:T(8,128)(2,1)S(1)} %collective-permute-done.6.refs_2_.refs_3_), channel_id=1, source_target_pairs={{0,4},{1,3},{4,8},{5,1},{8,12},{9,5},{12,14},{13,9},{14,10},{15,13... | collective-permute-start | bytes 1966088 | tf_op jit(solution)/shard_map/ppermute | solution.py:467
  54.2 15.6 %collective-permute-start.11 = (bf16[640,512]{1,0:T(8,128)(2,1)S(1)}, bf16[640,512]{1,0:T(8,128)(2,1)S(1)}, u32[]{:S(2)}, u32[]{:S(2)}) collective-permute-start(bf16[640,512]{1,0:T(8,128)(2,1)S(1)} %collective-permute-done.7.refs_5_.refs_6_), channel_id=1, source_target_pairs={{0,2},{1,5},{4,0},{5,9},{8,4},{9,13},{12,8},{13,15},{14,12},{15,11... | collective-permute-start | bytes 1966088 | tf_op jit(solution)/shard_map/ppermute | solution.py:469
  55.9 11.0 %collective-permute-start.12 = (bf16[448,512]{1,0:T(8,128)(2,1)S(1)}, bf16[448,512]{1,0:T(8,128)(2,1)S(1)}, u32[]{:S(2)}, u32[]{:S(2)}) collective-permute-start(bf16[448,512]{1,0:T(8,128)(2,1)S(1)} %pad_maximum_fusion), channel_id=1, source_target_pairs={{0,16},{16,0},{1,17},{17,1},{2,18},{18,2},{3,19},{19,3},{4,20},{20... | collective-permute-start | bytes 1376264 | tf_op jit(solution)/shard_map/ppermute | solution.py:475
  69.8 10.0 %collective-permute-start.13 = (bf16[640,512]{1,0:T(8,128)(2,1)S(1)}, bf16[640,512]{1,0:T(8,128)(2,1)S(1)}, u32[]{:S(2)}, u32[]{:S(2)}) collective-permute-start(bf16[640,512]{1,0:T(8,128)(2,1)S(1)} %collective-permute-done.10.refs_2_.refs_3_), channel_id=1, source_target_pairs={{0,4},{1,3},{4,8},{5,1},{8,12},{9,5},{12,14},{13,9},{14,10},{15,13... | collective-permute-start | bytes 1966088 | tf_op jit(solution)/shard_map/ppermute | solution.py:467
  71.8 13.2 %collective-permute-start.15 = (bf16[448,512]{1,0:T(8,128)(2,1)S(1)}, bf16[448,512]{1,0:T(8,128)(2,1)S(1)}, u32[]{:S(2)}, u32[]{:S(2)}) collective-permute-start(bf16[448,512]{1,0:T(8,128)(2,1)S(1)} %pad_maximum_fusion.1), channel_id=1, source_target_pairs={{0,16},{16,0},{1,17},{17,1},{2,18},{18,2},{3,19},{19,3},{4,20},{20... | collective-permute-start | bytes 1376264 | tf_op jit(solution)/shard_map/ppermute | solution.py:475
  79.8 10.2 %collective-permute-start.14 = (bf16[224,512]{1,0:T(8,128)(2,1)S(1)}, bf16[224,512]{1,0:T(8,128)(2,1)S(1)}, u32[]{:S(2)}, u32[]{:S(2)}) collective-permute-start(bf16[224,512]{1,0:T(8,128)(2,1)S(1)} %slice.100), channel_id=1, source_target_pairs={{0,16},{16,0},{1,17},{17,1},{2,18},{18,2},{3,19},{19,3},{4,20},{20... | collective-permute-start | bytes 688136 | tf_op jit(solution)/shard_map/ppermute | solution.py:475
  90.0 5.4 %copy-start.19 = (s32[512]{0:T(512)S(1)}, s32[512]{0:T(512)}, u32[]{:S(2)}) copy-start(s32[512]{0:T(512)} %param.27) | copy-start | bytes 6148
  90.0 7.0 %copy-start.4 = (bf16[512,512]{1,0:T(8,128)(2,1)S(1)}, bf16[512,512]{1,0:T(8,128)(2,1)}, u32[]{:S(2)}) copy-start(bf16[512,512]{1,0:T(8,128)(2,1)} %features_ref.3) | copy-start | bytes 1572868
  90.0 6.9 %copy-start.5 = (bf16[512,512]{1,0:T(8,128)(2,1)S(1)}, bf16[512,512]{1,0:T(8,128)(2,1)}, u32[]{:S(2)}) copy-start(bf16[512,512]{1,0:T(8,128)(2,1)} %weight_ref.1) | copy-start | bytes 1572868
  90.0 6.9 %copy-start.14 = (f32[512]{0:T(512)S(1)}, f32[512]{0:T(512)}, u32[]{:S(2)}) copy-start(f32[512]{0:T(512)} %param.18) | copy-start | bytes 6148
  92.7 4.2 %collective-permute-start.17 = (bf16[512,512]{1,0:T(8,128)(2,1)S(1)}, bf16[512,512]{1,0:T(8,128)(2,1)S(1)}, u32[]{:S(2)}, u32[]{:S(2)}) collective-permute-start(bf16[512,512]{1,0:T(8,128)(2,1)S(1)} %get-tuple-element.78), channel_id=1, source_target_pairs={{0,1},{1,0},{2,3},{3,2},{4,5},{5,4},{6,7},{7,6},{8,9},{9,8},{10,11... | collective-permute-start | bytes 1572872 | tf_op jit(solution)/shard_map/ppermute | solution.py:567
  97.0 7.8 %copy-start.15 = (bf16[512,1536]{1,0:T(8,128)(2,1)S(1)}, bf16[512,1536]{1,0:T(8,128)(2,1)}, u32[]{:S(2)}) copy-start(bf16[512,1536]{1,0:T(8,128)(2,1)} %param.20) | copy-start | bytes 4718596
  99.3 30.5 %all-to-all-start = ((bf16[16,64,512]{2,1,0:T(8,128)(2,1)}), bf16[16,64,512]{2,1,0:T(8,128)(2,1)}, u32[]{:S(2)}, u32[]{:S(2)}) async-start(bf16[16,64,512]{2,1,0:T(8,128)(2,1)} %bitcast.11), calls=%async_computation | async-start | bytes 2097152 | tf_op jit(solution)/shard_map/all_to_all | solution.py:583
  104.8 1.3 copy-start.21
  106.5 23.3 %copy-start.20 = (s32[512]{0:T(512)}, s32[512]{0:T(512)S(1)}, u32[]{:S(2)}) copy-start(s32[512]{0:T(512)S(1)} %multiply_add_fusion) | copy-start | bytes 6148
  151.4 29.8 %all-to-all-start.1 = ((bf16[16,64,512]{2,1,0:T(8,128)(2,1)}), bf16[16,64,512]{2,1,0:T(8,128)(2,1)S(1)}, u32[]{:S(2)}, u32[]{:S(2)}) async-start(bf16[16,64,512]{2,1,0:T(8,128)(2,1)} %bitcast.32), calls=%async_computation.1 | async-start | bytes 2097152 | tf_op jit(solution)/shard_map/all_to_all | solution.py:616

commit v22 on v17

--- a/solution.py
+++ b/solution.py
@@ -615,7 +615,7 @@
     back = call(
         block_kernel,
         jax.ShapeDtypeStruct((slots, width), BF16),
-        60,
+        50,
         20 * points * width * width,
         16 * width * width,
         in_specs=[pl.BlockSpec()] * 5 + [pl.BlockSpec(memory_space=pl.ANY)] * len(weights),

time: 180 us -> 179 us (level)
    all_to_all x1, waiting for transfers between devices: 21.4 us -> 19.6 us  [body(): lax.all_to_all(outgoing.reshape(devices, capacity, width), 'blocks', spli...]
    unnamed x30 -> x32, local copies, waits for them, and re-layouts: 3.95 us -> 5.02 us
  transfers between devices with their start and end apart: 20 -> 20, of which waited for: 11 -> 10; matrix products, arithmetic and copies ran while one was open for 8% -> 9% of each run, Pallas kernels for 22% -> 22%
where the time goes in v22:
time: 179 us; the launch traced here: 178 us
  Pallas kernels  67 us (37%)
  waiting for transfers between devices  58.2 us (33%)
  starting transfers between devices  31.3 us (17%)
  local copies, waits for them, and re-layouts  14.3 us (8%)
  other arithmetic  7.17 us (4%)
    all_to_all x1, waiting for transfers between devices, body(): lax.all_to_all(back.reshape(devices, capacity, width), 'blocks', split_ax...  24.7 us
    pallas_call x2, Pallas kernels, gather_block(): call(functools.partial(gather_kernel, taps), jax.ShapeDtypeStruct((points...  21.2 us
    pallas_call x1, Pallas kernels, body(): call(block_kernel, jax.ShapeDtypeStruct((slots, width), BF16), 50, 20 * p...  20.4 us
    all_to_all x1, waiting for transfers between devices, body(): lax.all_to_all(outgoing.reshape(devices, capacity, width), 'blocks', spli...  19.6 us
    pallas_call x4, Pallas kernels, conv_part(): call(functools.partial(conv_kernel, slots, later, ready, before is None),...  18.8 us
    ppermute x3, starting transfers between devices, pass_on(): second.append(lax.ppermute(second[-1], 'blocks', second_pairs))  5.33 us
    all_to_all x1, starting transfers between devices, body(): lax.all_to_all(outgoing.reshape(devices, capacity, width), 'blocks', spli...  5.3 us
    unnamed x32, local copies, waits for them, and re-layouts  5.02 us
  transfers between devices with their start and end apart: 20, of which 10 were waited for; matrix products, arithmetic and copies ran while one was open for 9% of the time, Pallas kernels for 22%

profile of v22, /device:TPU:9, one launch (start us, length us, event | category | flops | bytes accessed | tf_op | source)
XLA Modules:
  0.0 178.3 jit_solution(2393305887462022648)
XLA Ops:
  0.0 1.1 slice.69
  1.1 0.7 collective-permute-start
  1.9 0.7 slice_bitcast_fusion
  2.6 0.8 select_bitcast_fusion
  3.3 0.1 reshape.66.rows_ref
  3.5 1.0 copy-done.3
  4.5 0.7 shard_map.146
  5.4 0.7 shard_map.145
  6.0 0.9 copy-done.1
  7.0 2.3 %collective-permute-start.1 = (bf16[192,512]{1,0:T(8,128)(2,1)S(1)}, bf16[192,512]{1,0:T(8,128)(2,1)S(1)}, u32[]{:S(2)}, u32[]{:S(2)}) collective-permute-start(bf16[192,512]{1,0:T(8,128)(2,1)S(1)} %get-tuple-element.48), channel_id=1, source_target_pairs={{0,8},{1,9},{2,10},{3,11},{4,12},{5,13},{6,14},{7,15},{8,0},{9,1},... | collective-permute-start | bytes 589832 | tf_op jit(solution)/shard_map/ppermute | solution.py:513
  9.3 0.7 constant_dynamic-slice_fusion
  10.1 0.9 copy.35
  10.9 0.9 copy.36
  11.9 0.2 collective-permute-start.2
  12.1 1.3 collective-permute-start.3
  13.4 4.7 %collective-permute-done.1.side_ref = bf16[192,512]{1,0:T(8,128)(2,1)S(1)} collective-permute-done((bf16[192,512]{1,0:T(8,128)(2,1)S(1)}, bf16[192,512]{1,0:T(8,128)(2,1)S(1)}, u32[]{:S(2)}, u32[]{:S(2)}) %collective-permute-start.1) | collective-permute-done | bytes 196640 | tf_op jit(solution)/shard_map/ppermute | solution.py:513
  18.1 0.7 pad_maximum_fusion.3
  18.8 3.5 %collective-permute-start.4 = (bf16[128,512]{1,0:T(8,128)(2,1)}, bf16[128,512]{1,0:T(8,128)(2,1)S(1)}, u32[]{:S(2)}, u32[]{:S(2)}) collective-permute-start(bf16[128,512]{1,0:T(8,128)(2,1)} %pad_maximum_fusion.3), channel_id=1, source_target_pairs={{0,1},{1,2},{2,3},{3,4},{4,5},{5,6},{6,7},{8,9},{9,10},{10,11},{11... | collective-permute-start | bytes 393224 | tf_op jit(solution)/shard_map/ppermute | solution.py:519
  22.3 0.8 copy.37
  23.2 2.4 %collective-permute-start.5 = (bf16[128,512]{1,0:T(8,128)(2,1)S(1)}, bf16[128,512]{1,0:T(8,128)(2,1)S(1)}, u32[]{:S(2)}, u32[]{:S(2)}) collective-permute-start(bf16[128,512]{1,0:T(8,128)(2,1)S(1)} %pad_maximum_fusion.4), channel_id=1, source_target_pairs={{1,0},{2,1},{3,2},{4,3},{5,4},{6,5},{7,6},{9,8},{10,9},{11,10},{12... | collective-permute-start | bytes 393224 | tf_op jit(solution)/shard_map/ppermute | solution.py:520
  25.8 2.1 %add_convert_fusion.1 = (f32[512,128]{1,0:T(8,128)}, f32[512,128]{1,0:T(8,128)}) fusion(s32[512,13]{1,0:T(8,128)S(1)} %get-tuple-element.93, s32[512,13]{1,0:T(8,128)S(1)} %get-tuple-element.92, s32[512,1]{1,0:T(8,128)S(1)} %iota.13, s32[128]{0:T(128)S(1)} %pad.17.clone, s32[512,13]{1,0:T(8,128)} %copy.36, s32[512,13]{1,0:T(8,128)} %copy.35), kind=kLoop, calls=%fused_computation.9 | loop fusion | flops 524288 | bytes 633344 | tf_op jit(solution)/shard_map/convert_element_type | solution.py:408
  27.9 2.5 %collective-permute-done.5.ahead_ref = bf16[128,512]{1,0:T(8,128)(2,1)S(1)} collective-permute-done((bf16[128,512]{1,0:T(8,128)(2,1)S(1)}, bf16[128,512]{1,0:T(8,128)(2,1)S(1)}, u32[]{:S(2)}, u32[]{:S(2)}) %collective-permute-start.5) | collective-permute-done | bytes 131104 | tf_op jit(solution)/shard_map/ppermute | solution.py:520
  30.4 1.4 collective-permute-done.2.refs_3_.refs_4_
  31.8 0.3 collective-permute-done.3.refs_6_.refs_7_
  32.2 2.3 %collective-permute-start.7 = (bf16[640,512]{1,0:T(8,128)(2,1)S(1)}, bf16[640,512]{1,0:T(8,128)(2,1)S(1)}, u32[]{:S(2)}, u32[]{:S(2)}) collective-permute-start(bf16[640,512]{1,0:T(8,128)(2,1)S(1)} %collective-permute-done.3.refs_6_.refs_7_), channel_id=1, source_target_pairs={{0,2},{1,5},{4,0},{5,9},{8,4},{9,13},{12,8},{13,15},{14,12},{15,11... | collective-permute-start | bytes 1966088 | tf_op jit(solution)/shard_map/ppermute | solution.py:493
  34.4 1.4 shard_map.147
  35.8 0.8 copy-done.8
  36.6 0.7 collective-permute-start.9
  37.3 0.8 pad_maximum_fusion.1
  38.2 1.2 collective-permute-start.13
  39.4 10.6 %shard_map.148.refs_1_ = bf16[512,6912]{1,0:T(8,128)(2,1)} custom-call(s32[1]{0:T(128)} %bitcast.7.start_ref, f32[512,128]{1,0:T(8,128)} %get-tuple-element.91.rows_ref, bf16[896,256]{1,0:T(8,128)(2,1)} %copy-done.8), custom_call_target="tpu_custom_call" | custom-call | flops 6341787648 | bytes 7077888 | tf_op jit(solution)/shard_map/pallas_call | solution.py:136
  50.0 0.7 copy-done.14
  50.9 1.8 collective-permute-start.11
  52.6 0.8 pad_maximum_fusion
  53.5 0.3 collective-permute-start.12
  53.7 10.6 %shard_map.149.refs_0_ = bf16[512,6912]{1,0:T(8,128)(2,1)} custom-call(s32[1]{0:T(128)} %bitcast.7.start_ref, f32[512,128]{1,0:T(8,128)} %get-tuple-element.67.rows_ref, bf16[896,256]{1,0:T(8,128)(2,1)} %copy-done.14), custom_call_target="tpu_custom_call" | custom-call | flops 6341787648 | bytes 7077888 | tf_op jit(solution)/shard_map/pallas_call | solution.py:136
  64.3 1.0 collective-permute-done.12.refs_3_.refs_6_
  65.3 1.8 %collective-permute-done.11.refs_4_.refs_5_ = bf16[640,512]{1,0:T(8,128)(2,1)} collective-permute-done((bf16[640,512]{1,0:T(8,128)(2,1)S(1)}, bf16[640,512]{1,0:T(8,128)(2,1)}, u32[]{:S(2)}, u32[]{:S(2)}) %collective-permute-start.11) | collective-permute-done | bytes 655392 | tf_op jit(solution)/shard_map/ppermute | solution.py:493
  67.2 0.6 collective-permute-start.14
  68.0 1.0 slice.87
  69.0 0.3 collective-permute-start.16
  69.3 6.9 %shard_map.150 = (f32[512,512]{1,0:T(8,128)S(1)}, f32[512,512]{1,0:T(8,128)S(1)}, bf16[2,2,512,1024]{3,2,1,0:T(8,128)(2,1)S(1)}, bf16[2,2,512,1024]{3,2,1,0:T(8,128)(2,1)S(1)}, bf16[1,2,512,1024]{3,2,1,0:T(8,128)(2,1)S(1)}) custom-call(s32[16]{0:T(128)S(1)} %reshape_squeeze.3.places_ref, s32[2]{0:T(128)S(1)} %pad_add_fusion.2.shifts_ref, ...), custom_call_target="tpu_custom_call" | custom-call | flops 3221225472 | bytes 9437184 | tf_op jit(solution)/shard_map/pallas_call | solution.py:228
  76.3 0.9 collective-permute-done.14.refs_1_.refs_2_
  77.2 0.5 collective-permute-start.15
  77.6 4.7 %shard_map.151 = (f32[512,512]{1,0:T(8,128)S(1)}, f32[512,512]{1,0:T(8,128)S(1)}) custom-call(s32[4]{0:T(128)S(1)} %get-tuple-element.98.places_ref, s32[2]{0:T(128)S(1)} %pad_add_fusion.2.shifts_ref, bf16[2,2,512,1024]{3,2,1,0:T(8,128)(2,1)S(1)} %get-tuple-element.77.refs_0_, ...), custom_call_target="tpu_custom_call", output_to_operand_aliasing={{0}: (9, {}), {1}: (10, {})} | custom-call | flops 2147483648 | bytes 6291456 | tf_op jit(solution)/shard_map/pallas_call | solution.py:228
  82.4 4.4 %shard_map.152 = (f32[512,512]{1,0:T(8,128)S(1)}, f32[512,512]{1,0:T(8,128)S(1)}) custom-call(s32[4]{0:T(128)S(1)} %get-tuple-element.99.places_ref, s32[2]{0:T(128)S(1)} %pad_add_fusion.2.shifts_ref, bf16[2,2,512,1024]{3,2,1,0:T(8,128)(2,1)S(1)} %get-tuple-element.75.refs_0_, ...), custom_call_target="tpu_custom_call", output_to_operand_aliasing={{0}: (9, {}), {1}: (10, {})} | custom-call | flops 2147483648 | bytes 6291456 | tf_op jit(solution)/shard_map/pallas_call | solution.py:228
  86.9 2.7 %shard_map.153 = (bf16[512,512]{1,0:T(8,128)(2,1)S(1)}, f32[512,512]{1,0:T(8,128)S(1)}) custom-call(s32[2]{0:T(128)S(1)} %slice.73.places_ref, s32[2]{0:T(128)S(1)} %pad_add_fusion.2.shifts_ref, bf16[1,2,512,1024]{3,2,1,0:T(8,128)(2,1)S(1)} %get-tuple-element.73.refs_0_, ...), custom_call_target="tpu_custom_call", output_to_operand_aliasing={{1}: (7, {})} | custom-call | flops 1073741824 | bytes 3145728 | tf_op jit(solution)/shard_map/pallas_call | solution.py:228
  89.6 2.9 %collective-permute-start.17 = (bf16[512,512]{1,0:T(8,128)(2,1)S(1)}, bf16[512,512]{1,0:T(8,128)(2,1)S(1)}, u32[]{:S(2)}, u32[]{:S(2)}) collective-permute-start(bf16[512,512]{1,0:T(8,128)(2,1)S(1)} %get-tuple-element.86), channel_id=1, source_target_pairs={{0,1},{1,0},{2,3},{3,2},{4,5},{5,4},{6,7},{7,6},{8,9},{9,8},{10,11... | collective-permute-start | bytes 1572872 | tf_op jit(solution)/shard_map/ppermute | solution.py:592
  92.5 0.3 convert_reduce_fusion.1
  92.9 1.2 collective-permute-done.17.got_ref
  94.1 2.3 %shard_map.154 = bf16[1024,512]{1,0:T(8,128)(2,1)} custom-call(f32[512,512]{1,0:T(8,128)S(1)} %get-tuple-element.85.own_ref, bf16[512,512]{1,0:T(8,128)(2,1)S(1)} %collective-permute-done.17.got_ref, bf16[512,512]{1,0:T(8,128)(2,1)S(1)} %copy-done.4, bf16[512,512]{1,0:T(8,128)(2,1)S(1)} %copy-done.5, f32[1,512]{1,0:T(1,128)S(1)} %bitcast.32, ...), custom_call_target="tpu_custom_call" | custom-call | flops 805306368 | bytes 2097152 | tf_op jit(solution)/shard_map/pallas_call | solution.py:594
  96.4 5.3 %all-to-all-start = ((bf16[16,64,512]{2,1,0:T(8,128)(2,1)}), bf16[16,64,512]{2,1,0:T(8,128)(2,1)S(1)}, u32[]{:S(2)}, u32[]{:S(2)}) async-start(bf16[16,64,512]{2,1,0:T(8,128)(2,1)} %bitcast.11), calls=%async_computation | async-start | bytes 2097152 | tf_op jit(solution)/shard_map/all_to_all | solution.py:608
  101.7 2.3 %fusion.5 = (bf16[512,512]{1,0:T(8,128)(2,1)S(1)}, bf16[512,512]{1,0:T(8,128)(2,1)S(1)}, bf16[512,512]{1,0:T(8,128)(2,1)}) fusion(bf16[512,1536]{1,0:T(8,128)(2,1)} %param.20), kind=kLoop, calls=%fused_computation.35 | loop fusion | bytes 3145728 | tf_op jit(solution)/shard_map/slice | solution.py:612
  104.0 0.2 copy.42
  104.2 1.3 copy.43
  105.5 0.2 convert_reduce_fusion
  105.7 0.1 copy.40.slot_col_ref
  105.9 1.1 maximum_bitcast_fusion.qv_hbm
  106.9 19.6 %all-to-all-done = bf16[16,64,512]{2,1,0:T(8,128)(2,1)S(1)} async-done(((bf16[16,64,512]{2,1,0:T(8,128)(2,1)}), bf16[16,64,512]{2,1,0:T(8,128)(2,1)S(1)}, u32[]{:S(2)}, u32[]{:S(2)}) %all-to-all-start) | async-done | bytes 1048608 | tf_op jit(solution)/shard_map/all_to_all | solution.py:608
  126.5 20.4 %shard_map.155 = bf16[1024,512]{1,0:T(8,128)(2,1)} custom-call(bf16[1024,512]{1,0:T(8,128)(2,1)S(1)} %bitcast.26, s32[512,1]{1,0:T(8,128)S(1)} %copy.40.slot_col_ref, s32[1,512]{1,0:T(1,128)S(1)} %bitcast.31, f32[1,512]{1,0:T(1,128)S(1)} %bitcast.33, f32[1,512]{1,0:T(1,128)S(1)} %bitcast.34, bf16[1024,512]{1,0:T(8,128)(2,1)} %maximum_bitcast_fusion.qv_hbm, ...), custom_call_target="tpu_custom_call" | custom-call | flops 2684354560 | bytes 4194304 | tf_op jit(solution)/shard_map/pallas_call | solution.py:615
  146.9 5.0 %all-to-all-start.1 = ((bf16[16,64,512]{2,1,0:T(8,128)(2,1)}), bf16[16,64,512]{2,1,0:T(8,128)(2,1)S(1)}, u32[]{:S(2)}, u32[]{:S(2)}) async-start(bf16[16,64,512]{2,1,0:T(8,128)(2,1)} %bitcast.18), calls=%async_computation.1 | async-start | bytes 2097152 | tf_op jit(solution)/shard_map/all_to_all | solution.py:641
  151.9 0.1 copy.41.slot_ref
  152.0 24.7 %all-to-all-done.1 = bf16[16,64,512]{2,1,0:T(8,128)(2,1)S(1)} async-done(((bf16[16,64,512]{2,1,0:T(8,128)(2,1)}), bf16[16,64,512]{2,1,0:T(8,128)(2,1)S(1)}, u32[]{:S(2)}, u32[]{:S(2)}) %all-to-all-start.1) | async-done | bytes 1048608 | tf_op jit(solution)/shard_map/all_to_all | solution.py:641
  176.7 1.5 shard_map.156
  (64 shorter events, 1.1 us)
Async XLA Ops:
  0.0 5.3 %copy-start = (bf16[864,512]{1,0:T(8,128)(2,1)S(1)}, bf16[864,512]{1,0:T(8,128)(2,1)}, u32[]{:S(2)}) copy-start(bf16[864,512]{1,0:T(8,128)(2,1)} %param.16) | copy-start | bytes 2654212
  0.0 5.3 %copy-start.11 = (s32[512,26]{0,1:T(8,128)S(1)}, s32[512,26]{0,1:T(8,128)}, u32[]{:S(2)}) copy-start(s32[512,26]{0,1:T(8,128)} %param.26) | copy-start | bytes 159748
  1.1 4.2 %collective-permute-start = (bf16[13,32,512]{2,1,0:T(8,128)(2,1)S(1)}, bf16[13,32,512]{2,1,0:T(8,128)(2,1)S(1)}, u32[]{:S(2)}, u32[]{:S(2)}) collective-permute-start(bf16[13,32,512]{2,1,0:T(8,128)(2,1)S(1)} %slice.69), channel_id=1, source_target_pairs={{0,1},{1,0},{2,3},{3,2},{4,5},{5,4},{6,7},{7,6},{8,9},{9,8},{10,11... | collective-permute-start | bytes 1277960 | tf_op jit(solution)/shard_map/ppermute | solution.py:438
  3.5 1.0 copy-start.3
  6.0 1.0 copy-start.1
  7.0 11.1 %collective-permute-start.1 = (bf16[192,512]{1,0:T(8,128)(2,1)S(1)}, bf16[192,512]{1,0:T(8,128)(2,1)S(1)}, u32[]{:S(2)}, u32[]{:S(2)}) collective-permute-start(bf16[192,512]{1,0:T(8,128)(2,1)S(1)} %get-tuple-element.48), channel_id=1, source_target_pairs={{0,8},{1,9},{2,10},{3,11},{4,12},{5,13},{6,14},{7,15},{8,0},{9,1},... | collective-permute-start | bytes 589832 | tf_op jit(solution)/shard_map/ppermute | solution.py:513
  11.9 19.9 %collective-permute-start.2 = (bf16[640,512]{1,0:T(8,128)(2,1)S(1)}, bf16[640,512]{1,0:T(8,128)(2,1)S(1)}, u32[]{:S(2)}, u32[]{:S(2)}) collective-permute-start(bf16[640,512]{1,0:T(8,128)(2,1)S(1)} %get-tuple-element.51), channel_id=1, source_target_pairs={{0,4},{1,3},{4,8},{5,1},{8,12},{9,5},{12,14},{13,9},{14,10},{15,13... | collective-permute-start | bytes 1966088 | tf_op jit(solution)/shard_map/ppermute | solution.py:491
  12.1 20.1 %collective-permute-start.3 = (bf16[640,512]{1,0:T(8,128)(2,1)S(1)}, bf16[640,512]{1,0:T(8,128)(2,1)S(1)}, u32[]{:S(2)}, u32[]{:S(2)}) collective-permute-start(bf16[640,512]{1,0:T(8,128)(2,1)S(1)} %get-tuple-element.51), channel_id=1, source_target_pairs={{0,2},{1,5},{4,0},{5,9},{8,4},{9,13},{12,8},{13,15},{14,12},{15,11... | collective-permute-start | bytes 1966088 | tf_op jit(solution)/shard_map/ppermute | solution.py:493
  18.8 9.1 %collective-permute-start.4 = (bf16[128,512]{1,0:T(8,128)(2,1)}, bf16[128,512]{1,0:T(8,128)(2,1)S(1)}, u32[]{:S(2)}, u32[]{:S(2)}) collective-permute-start(bf16[128,512]{1,0:T(8,128)(2,1)} %pad_maximum_fusion.3), channel_id=1, source_target_pairs={{0,1},{1,2},{2,3},{3,4},{4,5},{5,6},{6,7},{8,9},{9,10},{10,11},{11... | collective-permute-start | bytes 393224 | tf_op jit(solution)/shard_map/ppermute | solution.py:519
  23.1 2.4 %collective-permute-start.8 = (s32[512,26]{1,0:T(8,128)}, s32[512,26]{1,0:T(8,128)S(1)}, u32[]{:S(2)}, u32[]{:S(2)}) collective-permute-start(s32[512,26]{1,0:T(8,128)} %copy.37), channel_id=1, source_target_pairs={{0,1},{1,0},{2,3},{3,2},{4,5},{5,4},{6,7},{7,6},{8,9},{9,8},{10,11... | collective-permute-start | bytes 159752 | tf_op jit(solution)/shard_map/ppermute | solution.py:516
  23.2 7.3 %collective-permute-start.5 = (bf16[128,512]{1,0:T(8,128)(2,1)S(1)}, bf16[128,512]{1,0:T(8,128)(2,1)S(1)}, u32[]{:S(2)}, u32[]{:S(2)}) collective-permute-start(bf16[128,512]{1,0:T(8,128)(2,1)S(1)} %pad_maximum_fusion.4), channel_id=1, source_target_pairs={{1,0},{2,1},{3,2},{4,3},{5,4},{6,5},{7,6},{9,8},{10,9},{11,10},{12... | collective-permute-start | bytes 393224 | tf_op jit(solution)/shard_map/ppermute | solution.py:520
  32.2 17.8 %collective-permute-start.6 = (bf16[640,512]{1,0:T(8,128)(2,1)S(1)}, bf16[640,512]{1,0:T(8,128)(2,1)S(1)}, u32[]{:S(2)}, u32[]{:S(2)}) collective-permute-start(bf16[640,512]{1,0:T(8,128)(2,1)S(1)} %collective-permute-done.2.refs_3_.refs_4_), channel_id=1, source_target_pairs={{0,4},{1,3},{4,8},{5,1},{8,12},{9,5},{12,14},{13,9},{14,10},{15,13... | collective-permute-start | bytes 1966088 | tf_op jit(solution)/shard_map/ppermute | solution.py:491
  32.2 17.8 %collective-permute-start.7 = (bf16[640,512]{1,0:T(8,128)(2,1)S(1)}, bf16[640,512]{1,0:T(8,128)(2,1)S(1)}, u32[]{:S(2)}, u32[]{:S(2)}) collective-permute-start(bf16[640,512]{1,0:T(8,128)(2,1)S(1)} %collective-permute-done.3.refs_6_.refs_7_), channel_id=1, source_target_pairs={{0,2},{1,5},{4,0},{5,9},{8,4},{9,13},{12,8},{13,15},{14,12},{15,11... | collective-permute-start | bytes 1966088 | tf_op jit(solution)/shard_map/ppermute | solution.py:493
  35.8 0.8 copy-start.8
  36.6 13.4 %collective-permute-start.9 = (bf16[896,256]{1,0:T(8,128)(2,1)}, bf16[896,256]{1,0:T(8,128)(2,1)S(1)}, u32[]{:S(2)}, u32[]{:S(2)}) collective-permute-start(bf16[896,256]{1,0:T(8,128)(2,1)} %get-tuple-element.64), channel_id=1, source_target_pairs={{0,1},{1,0},{2,3},{3,2},{4,5},{5,4},{6,7},{7,6},{8,9},{9,8},{10,11... | collective-permute-start | bytes 1376264 | tf_op jit(solution)/shard_map/ppermute | solution.py:555
  38.2 31.2 %collective-permute-start.13 = (bf16[448,512]{1,0:T(8,128)(2,1)}, bf16[448,512]{1,0:T(8,128)(2,1)S(1)}, u32[]{:S(2)}, u32[]{:S(2)}) collective-permute-start(bf16[448,512]{1,0:T(8,128)(2,1)} %pad_maximum_fusion.1), channel_id=1, source_target_pairs={{0,16},{16,0},{1,17},{17,1},{2,18},{18,2},{3,19},{19,3},{4,20},{20... | collective-permute-start | bytes 1376264 | tf_op jit(solution)/shard_map/ppermute | solution.py:499
  50.0 0.8 copy-start.14
  50.8 14.6 %collective-permute-start.10 = (bf16[640,512]{1,0:T(8,128)(2,1)S(1)}, bf16[640,512]{1,0:T(8,128)(2,1)S(1)}, u32[]{:S(2)}, u32[]{:S(2)}) collective-permute-start(bf16[640,512]{1,0:T(8,128)(2,1)S(1)} %collective-permute-done.6.refs_1_.refs_2_), channel_id=1, source_target_pairs={{0,4},{1,3},{4,8},{5,1},{8,12},{9,5},{12,14},{13,9},{14,10},{15,13... | collective-permute-start | bytes 1966088 | tf_op jit(solution)/shard_map/ppermute | solution.py:491
  50.9 16.3 %collective-permute-start.11 = (bf16[640,512]{1,0:T(8,128)(2,1)S(1)}, bf16[640,512]{1,0:T(8,128)(2,1)}, u32[]{:S(2)}, u32[]{:S(2)}) collective-permute-start(bf16[640,512]{1,0:T(8,128)(2,1)S(1)} %collective-permute-done.7.refs_4_.refs_5_), channel_id=1, source_target_pairs={{0,2},{1,5},{4,0},{5,9},{8,4},{9,13},{12,8},{13,15},{14,12},{15,11... | collective-permute-start | bytes 1966088 | tf_op jit(solution)/shard_map/ppermute | solution.py:493
  53.5 11.8 %collective-permute-start.12 = (bf16[448,512]{1,0:T(8,128)(2,1)}, bf16[448,512]{1,0:T(8,128)(2,1)}, u32[]{:S(2)}, u32[]{:S(2)}) collective-permute-start(bf16[448,512]{1,0:T(8,128)(2,1)} %pad_maximum_fusion), channel_id=1, source_target_pairs={{0,16},{16,0},{1,17},{17,1},{2,18},{18,2},{3,19},{19,3},{4,20},{20... | collective-permute-start | bytes 1376264 | tf_op jit(solution)/shard_map/ppermute | solution.py:499
  64.3 5.0 %copy-start.2 = (bf16[864,512]{1,0:T(8,128)(2,1)S(1)}, bf16[864,512]{1,0:T(8,128)(2,1)}, u32[]{:S(2)}) copy-start(bf16[864,512]{1,0:T(8,128)(2,1)} %copy-done.1) | copy-start | bytes 2654212
  67.2 10.0 %collective-permute-start.14 = (bf16[640,512]{1,0:T(8,128)(2,1)S(1)}, bf16[640,512]{1,0:T(8,128)(2,1)S(1)}, u32[]{:S(2)}, u32[]{:S(2)}) collective-permute-start(bf16[640,512]{1,0:T(8,128)(2,1)S(1)} %collective-permute-done.10.refs_1_.refs_2_), channel_id=1, source_target_pairs={{0,4},{1,3},{4,8},{5,1},{8,12},{9,5},{12,14},{13,9},{14,10},{15,13... | collective-permute-start | bytes 1966088 | tf_op jit(solution)/shard_map/ppermute | solution.py:491
  69.0 13.3 %collective-permute-start.16 = (bf16[448,512]{1,0:T(8,128)(2,1)S(1)}, bf16[448,512]{1,0:T(8,128)(2,1)S(1)}, u32[]{:S(2)}, u32[]{:S(2)}) collective-permute-start(bf16[448,512]{1,0:T(8,128)(2,1)S(1)} %pad_maximum_fusion.2), channel_id=1, source_target_pairs={{0,16},{16,0},{1,17},{17,1},{2,18},{18,2},{3,19},{19,3},{4,20},{20... | collective-permute-start | bytes 1376264 | tf_op jit(solution)/shard_map/ppermute | solution.py:499
  77.2 9.7 %collective-permute-start.15 = (bf16[224,512]{1,0:T(8,128)(2,1)S(1)}, bf16[224,512]{1,0:T(8,128)(2,1)S(1)}, u32[]{:S(2)}, u32[]{:S(2)}) collective-permute-start(bf16[224,512]{1,0:T(8,128)(2,1)S(1)} %slice.94), channel_id=1, source_target_pairs={{0,16},{16,0},{1,17},{17,1},{2,18},{18,2},{3,19},{19,3},{4,20},{20... | collective-permute-start | bytes 688136 | tf_op jit(solution)/shard_map/ppermute | solution.py:499
  86.9 5.7 %copy-start.12 = (s32[512]{0:T(512)S(1)}, s32[512]{0:T(512)}, u32[]{:S(2)}) copy-start(s32[512]{0:T(512)} %param.27) | copy-start | bytes 6148
  86.9 7.2 %copy-start.4 = (bf16[512,512]{1,0:T(8,128)(2,1)S(1)}, bf16[512,512]{1,0:T(8,128)(2,1)}, u32[]{:S(2)}) copy-start(bf16[512,512]{1,0:T(8,128)(2,1)} %features_ref.3) | copy-start | bytes 1572868
  86.9 7.2 %copy-start.5 = (bf16[512,512]{1,0:T(8,128)(2,1)S(1)}, bf16[512,512]{1,0:T(8,128)(2,1)}, u32[]{:S(2)}) copy-start(bf16[512,512]{1,0:T(8,128)(2,1)} %weight_ref.1) | copy-start | bytes 1572868
  86.9 7.2 %copy-start.6 = (f32[512]{0:T(512)S(1)}, f32[512]{0:T(512)}, u32[]{:S(2)}) copy-start(f32[512]{0:T(512)} %param.18) | copy-start | bytes 6148
  89.6 4.4 %collective-permute-start.17 = (bf16[512,512]{1,0:T(8,128)(2,1)S(1)}, bf16[512,512]{1,0:T(8,128)(2,1)S(1)}, u32[]{:S(2)}, u32[]{:S(2)}) collective-permute-start(bf16[512,512]{1,0:T(8,128)(2,1)S(1)} %get-tuple-element.86), channel_id=1, source_target_pairs={{0,1},{1,0},{2,3},{3,2},{4,5},{5,4},{6,7},{7,6},{8,9},{9,8},{10,11... | collective-permute-start | bytes 1572872 | tf_op jit(solution)/shard_map/ppermute | solution.py:592
  96.4 30.1 %all-to-all-start = ((bf16[16,64,512]{2,1,0:T(8,128)(2,1)}), bf16[16,64,512]{2,1,0:T(8,128)(2,1)S(1)}, u32[]{:S(2)}, u32[]{:S(2)}) async-start(bf16[16,64,512]{2,1,0:T(8,128)(2,1)} %bitcast.11), calls=%async_computation | async-start | bytes 2097152 | tf_op jit(solution)/shard_map/all_to_all | solution.py:608
  101.7 3.8 %copy-start.13 = (s32[512]{0:T(512)S(1)}, s32[512]{0:T(512)}, u32[]{:S(2)}) copy-start(s32[512]{0:T(512)} %param.28) | copy-start | bytes 6148
  103.9 22.6 %copy-start.7 = (bf16[512,512]{1,0:T(8,128)(2,1)S(1)}, bf16[512,512]{1,0:T(8,128)(2,1)}, u32[]{:S(2)}) copy-start(bf16[512,512]{1,0:T(8,128)(2,1)} %proj_hbm.1) | copy-start | bytes 1572868
  104.0 22.6 %copy-start.9 = (f32[512]{0:T(512)S(1)}, f32[512]{0:T(512)}, u32[]{:S(2)}) copy-start(f32[512]{0:T(512)} %param.19) | copy-start | bytes 6148
  104.0 22.6 %copy-start.10 = (f32[512]{0:T(512)S(1)}, f32[512]{0:T(512)}, u32[]{:S(2)}) copy-start(f32[512]{0:T(512)} %param.22) | copy-start | bytes 6148
  146.9 29.8 %all-to-all-start.1 = ((bf16[16,64,512]{2,1,0:T(8,128)(2,1)}), bf16[16,64,512]{2,1,0:T(8,128)(2,1)S(1)}, u32[]{:S(2)}, u32[]{:S(2)}) async-start(bf16[16,64,512]{2,1,0:T(8,128)(2,1)} %bitcast.18), calls=%async_computation.1 | async-start | bytes 2097152 | tf_op jit(solution)/shard_map/all_to_all | solution.py:641

commit v23 on v19

--- a/solution.py
+++ b/solution.py
@@ -589,7 +589,7 @@
     back = call(
         block_kernel,
         jax.ShapeDtypeStruct((slots, width), BF16),
-        60,
+        50,
         20 * points * width * width,
         16 * width * width,
         in_specs=[pl.BlockSpec()] * 5 + [pl.BlockSpec(memory_space=pl.ANY)] * len(weights),

time: 181 us -> 180 us (level)
  waiting for transfers between devices: 66.2 us -> 64.3 us
    all_to_all x1, waiting for transfers between devices: 21.4 us -> 19.6 us  [body(): lax.all_to_all(outgoing.reshape(devices, capacity, width), 'blocks', spli...]
  transfers between devices with their start and end apart: 20 -> 20, of which waited for: 13 -> 13; matrix products, arithmetic and copies ran while one was open for 7% -> 8% of each run, Pallas kernels for 19% -> 19%
where the time goes in v23:
time: 180 us; the launch traced here: 179 us
  waiting for transfers between devices  64.3 us (36%)
  Pallas kernels  61.7 us (34%)
  starting transfers between devices  35.2 us (20%)
  local copies, waits for them, and re-layouts  13.2 us (7%)
  other arithmetic  4.69 us (3%)
    all_to_all x1, waiting for transfers between devices, body(): lax.all_to_all(back.reshape(devices, capacity, width), 'blocks', split_ax...  24.7 us
    pallas_call x1, Pallas kernels, body(): call(block_kernel, jax.ShapeDtypeStruct((slots, width), BF16), 50, 20 * p...  20.4 us
    all_to_all x1, waiting for transfers between devices, body(): lax.all_to_all(outgoing.reshape(devices, capacity, width), 'blocks', spli...  19.6 us
    pallas_call x4, Pallas kernels, conv_part(): call(functools.partial(conv_kernel, slots, before is None), [jax.ShapeDty...  18.6 us
    pallas_call x2, Pallas kernels, gather_block(): call(functools.partial(gather_kernel, taps), jax.ShapeDtypeStruct((points...  16.9 us
    all_to_all x1, starting transfers between devices, body(): lax.all_to_all(outgoing.reshape(devices, capacity, width), 'blocks', spli...  6.54 us
    ppermute x4, starting transfers between devices, complete(): got = lax.ppermute(lent, 'groups', [(0, 1), (1, 0)])  5.46 us
    ppermute x3, waiting for transfers between devices, pass_on(): second.append(lax.ppermute(second[-1], 'blocks', second_pairs))  5.29 us
  transfers between devices with their start and end apart: 20, of which 13 were waited for; matrix products, arithmetic and copies ran while one was open for 8% of the time, Pallas kernels for 19%

profile of v23, /device:TPU:9, one launch (start us, length us, event | category | flops | bytes accessed | tf_op | source)
XLA Modules:
  0.0 179.5 jit_solution(16541649409417611213)
XLA Ops:
  0.0 1.1 slice.72
  1.1 0.7 collective-permute-start
  1.9 0.7 slice_bitcast_fusion
  2.6 0.8 select_bitcast_fusion
  3.3 0.1 reshape.66.rows_ref
  3.5 1.0 copy-done.1
  4.5 0.7 shard_map.146
  5.3 0.6 fusion.8
  6.0 0.7 shard_map.145
  6.6 0.8 copy-done.5
  7.5 2.3 %collective-permute-start.1 = (bf16[192,512]{1,0:T(8,128)(2,1)S(1)}, bf16[192,512]{1,0:T(8,128)(2,1)S(1)}, u32[]{:S(2)}, u32[]{:S(2)}) collective-permute-start(bf16[192,512]{1,0:T(8,128)(2,1)S(1)} %get-tuple-element.45), channel_id=1, source_target_pairs={{0,8},{1,9},{2,10},{3,11},{4,12},{5,13},{6,14},{7,15},{8,0},{9,1},... | collective-permute-start | bytes 589832 | tf_op jit(solution)/shard_map/ppermute | solution.py:489
  9.8 0.7 constant_dynamic-slice_fusion
  10.5 0.1 reshape_squeeze.3
  10.5 0.9 copy.35
  11.4 0.9 copy.36
  12.5 0.2 collective-permute-start.2
  12.6 1.3 collective-permute-start.3
  13.9 4.7 %collective-permute-done.1.side_ref = bf16[192,512]{1,0:T(8,128)(2,1)S(1)} collective-permute-done((bf16[192,512]{1,0:T(8,128)(2,1)S(1)}, bf16[192,512]{1,0:T(8,128)(2,1)S(1)}, u32[]{:S(2)}, u32[]{:S(2)}) %collective-permute-start.1) | collective-permute-done | bytes 196640 | tf_op jit(solution)/shard_map/ppermute | solution.py:489
  18.6 0.7 pad_maximum_fusion.3
  19.3 3.5 %collective-permute-start.4 = (bf16[128,512]{1,0:T(8,128)(2,1)}, bf16[128,512]{1,0:T(8,128)(2,1)S(1)}, u32[]{:S(2)}, u32[]{:S(2)}) collective-permute-start(bf16[128,512]{1,0:T(8,128)(2,1)} %pad_maximum_fusion.3), channel_id=1, source_target_pairs={{0,1},{1,2},{2,3},{3,4},{4,5},{5,6},{6,7},{8,9},{9,10},{10,11},{11... | collective-permute-start | bytes 393224 | tf_op jit(solution)/shard_map/ppermute | solution.py:495
  22.8 1.7 copy.37
  24.5 2.4 %collective-permute-start.5 = (bf16[128,512]{1,0:T(8,128)(2,1)S(1)}, bf16[128,512]{1,0:T(8,128)(2,1)S(1)}, u32[]{:S(2)}, u32[]{:S(2)}) collective-permute-start(bf16[128,512]{1,0:T(8,128)(2,1)S(1)} %pad_maximum_fusion.4), channel_id=1, source_target_pairs={{1,0},{2,1},{3,2},{4,3},{5,4},{6,5},{7,6},{9,8},{10,9},{11,10},{12... | collective-permute-start | bytes 393224 | tf_op jit(solution)/shard_map/ppermute | solution.py:496
  26.9 0.1 fusion.6
  27.1 1.2 add_convert_fusion.1
  28.3 3.9 %collective-permute-done.5.ahead_ref = bf16[128,512]{1,0:T(8,128)(2,1)S(1)} collective-permute-done((bf16[128,512]{1,0:T(8,128)(2,1)S(1)}, bf16[128,512]{1,0:T(8,128)(2,1)S(1)}, u32[]{:S(2)}, u32[]{:S(2)}) %collective-permute-start.5) | collective-permute-done | bytes 131104 | tf_op jit(solution)/shard_map/ppermute | solution.py:496
  32.3 0.4 collective-permute-done.3.refs_6_.refs_7_
  32.8 2.1 %collective-permute-start.7 = (bf16[640,512]{1,0:T(8,128)(2,1)S(1)}, bf16[640,512]{1,0:T(8,128)(2,1)S(1)}, u32[]{:S(2)}, u32[]{:S(2)}) collective-permute-start(bf16[640,512]{1,0:T(8,128)(2,1)S(1)} %collective-permute-done.3.refs_6_.refs_7_), channel_id=1, source_target_pairs={{0,2},{1,5},{4,0},{5,9},{8,4},{9,13},{12,8},{13,15},{14,12},{15,11... | collective-permute-start | bytes 1966088 | tf_op jit(solution)/shard_map/ppermute | solution.py:469
  34.9 0.6 shard_map.147
  35.6 0.8 collective-permute-start.9
  36.4 1.3 collective-permute-start.16
  37.7 8.5 %shard_map.148.refs_1_ = bf16[512,6912]{1,0:T(8,128)(2,1)S(1)} custom-call(s32[1]{0:T(128)} %bitcast.7.start_ref, f32[512,128]{1,0:T(8,128)S(1)} %get-tuple-element.85.rows_ref, bf16[896,256]{1,0:T(8,128)(2,1)S(1)} %get-tuple-element.59.table_ref), custom_call_target="tpu_custom_call" | custom-call | flops 6341787648 | bytes 7077888 | tf_op jit(solution)/shard_map/pallas_call | solution.py:137
  46.1 1.2 collective-permute-done.6.refs_2_.refs_3_
  47.4 2.9 %collective-permute-done.7.refs_5_.refs_6_ = bf16[640,512]{1,0:T(8,128)(2,1)S(1)} collective-permute-done((bf16[640,512]{1,0:T(8,128)(2,1)S(1)}, bf16[640,512]{1,0:T(8,128)(2,1)S(1)}, u32[]{:S(2)}, u32[]{:S(2)}) %collective-permute-start.7) | collective-permute-done | bytes 655392 | tf_op jit(solution)/shard_map/ppermute | solution.py:469
  50.3 1.5 collective-permute-start.11
  51.9 1.4 collective-permute-start.12
  53.2 8.5 %shard_map.149.refs_0_ = bf16[512,6912]{1,0:T(8,128)(2,1)S(1)} custom-call(s32[1]{0:T(128)} %bitcast.7.start_ref, f32[512,128]{1,0:T(8,128)S(1)} %get-tuple-element.64.rows_ref, bf16[896,256]{1,0:T(8,128)(2,1)S(1)} %collective-permute-done.9.table_ref), custom_call_target="tpu_custom_call" | custom-call | flops 6341787648 | bytes 7077888 | tf_op jit(solution)/shard_map/pallas_call | solution.py:137
  61.7 1.2 collective-permute-done.12.refs_4_.refs_7_
  62.9 1.4 collective-permute-done.10.refs_2_.refs_3_
  64.3 2.0 %collective-permute-done.11.refs_5_.refs_6_ = bf16[640,512]{1,0:T(8,128)(2,1)S(1)} collective-permute-done((bf16[640,512]{1,0:T(8,128)(2,1)S(1)}, bf16[640,512]{1,0:T(8,128)(2,1)S(1)}, u32[]{:S(2)}, u32[]{:S(2)}) %collective-permute-start.11) | collective-permute-done | bytes 655392 | tf_op jit(solution)/shard_map/ppermute | solution.py:469
  66.3 1.0 collective-permute-start.13
  67.7 1.3 collective-permute-start.15
  69.0 6.0 %shard_map.150 = (f32[512,512]{1,0:T(8,128)S(1)}, f32[512,512]{1,0:T(8,128)S(1)}) custom-call(s32[6]{0:T(128)S(1)} %bitcast.31, s32[2]{0:T(128)S(1)} %pad_add_fusion.2.shifts_ref, bf16[512,6912]{1,0:T(8,128)(2,1)S(1)} %shard_map.149.refs_0_, bf16[512,6912]{1,0:T(8,128)(2,1)S(1)} %shard_map.148.refs_1_, bf16[864,512]{1,0:T(8,128)(2,1)S(1)} %get-tuple-element.72.refs_2_, ...), custom_call_target="tpu_custom_call" | custom-call | flops 3221225472 | bytes 9437184 | tf_op jit(solution)/shard_map/pallas_call | solution.py:206
  75.0 1.1 collective-permute-done.13.refs_2_.refs_3_
  76.1 1.5 collective-permute-start.14
  77.6 4.9 %shard_map.151 = (f32[512,512]{1,0:T(8,128)S(1)}, f32[512,512]{1,0:T(8,128)S(1)}) custom-call(s32[4]{0:T(128)S(1)} %get-tuple-element.92.places_ref, s32[2]{0:T(128)S(1)} %pad_add_fusion.2.shifts_ref, bf16[512,6912]{1,0:T(8,128)(2,1)S(1)} %shard_map.149.refs_0_, ...), custom_call_target="tpu_custom_call", output_to_operand_aliasing={{0}: (10, {}), {1}: (11, {})} | custom-call | flops 2147483648 | bytes 6291456 | tf_op jit(solution)/shard_map/pallas_call | solution.py:206
  82.6 4.9 %shard_map.152 = (f32[512,512]{1,0:T(8,128)S(1)}, f32[512,512]{1,0:T(8,128)S(1)}) custom-call(s32[4]{0:T(128)S(1)} %get-tuple-element.93.places_ref, s32[2]{0:T(128)S(1)} %pad_add_fusion.2.shifts_ref, bf16[512,6912]{1,0:T(8,128)(2,1)S(1)} %shard_map.149.refs_0_, ...), custom_call_target="tpu_custom_call", output_to_operand_aliasing={{0}: (10, {}), {1}: (11, {})} | custom-call | flops 2147483648 | bytes 6291456 | tf_op jit(solution)/shard_map/pallas_call | solution.py:206
  87.6 2.7 %shard_map.153 = (bf16[512,512]{1,0:T(8,128)(2,1)S(1)}, f32[512,512]{1,0:T(8,128)S(1)}) custom-call(s32[2]{0:T(128)S(1)} %slice.76.places_ref, s32[2]{0:T(128)S(1)} %pad_add_fusion.2.shifts_ref, bf16[512,6912]{1,0:T(8,128)(2,1)S(1)} %shard_map.149.refs_0_, bf16[512,6912]{1,0:T(8,128)(2,1)S(1)} %shard_map.148.refs_1_, ...), custom_call_target="tpu_custom_call", output_to_operand_aliasing={{1}: (8, {})} | custom-call | flops 1073741824 | bytes 3145728 | tf_op jit(solution)/shard_map/pallas_call | solution.py:206
  90.3 2.3 %collective-permute-start.17 = (bf16[512,512]{1,0:T(8,128)(2,1)S(1)}, bf16[512,512]{1,0:T(8,128)(2,1)S(1)}, u32[]{:S(2)}, u32[]{:S(2)}) collective-permute-start(bf16[512,512]{1,0:T(8,128)(2,1)S(1)} %get-tuple-element.80), channel_id=1, source_target_pairs={{0,1},{1,0},{2,3},{3,2},{4,5},{5,4},{6,7},{7,6},{8,9},{9,8},{10,11... | collective-permute-start | bytes 1572872 | tf_op jit(solution)/shard_map/ppermute | solution.py:566
  92.5 0.3 convert_reduce_fusion.1
  92.9 1.2 collective-permute-done.17.got_ref
  94.1 2.3 %shard_map.154 = bf16[1024,512]{1,0:T(8,128)(2,1)} custom-call(f32[512,512]{1,0:T(8,128)S(1)} %get-tuple-element.79.own_ref, bf16[512,512]{1,0:T(8,128)(2,1)S(1)} %collective-permute-done.17.got_ref, bf16[512,512]{1,0:T(8,128)(2,1)S(1)} %copy-done.2, bf16[512,512]{1,0:T(8,128)(2,1)S(1)} %copy-done.3, f32[1,512]{1,0:T(1,128)S(1)} %bitcast.34, ...), custom_call_target="tpu_custom_call" | custom-call | flops 805306368 | bytes 2097152 | tf_op jit(solution)/shard_map/pallas_call | solution.py:568
  96.4 6.5 %all-to-all-start = ((bf16[16,64,512]{2,1,0:T(8,128)(2,1)}), bf16[16,64,512]{2,1,0:T(8,128)(2,1)S(1)}, u32[]{:S(2)}, u32[]{:S(2)}) async-start(bf16[16,64,512]{2,1,0:T(8,128)(2,1)} %bitcast.11), calls=%async_computation | async-start | bytes 2097152 | tf_op jit(solution)/shard_map/all_to_all | solution.py:582
  102.9 2.3 %fusion.5 = (bf16[512,512]{1,0:T(8,128)(2,1)S(1)}, bf16[512,512]{1,0:T(8,128)(2,1)S(1)}, bf16[512,512]{1,0:T(8,128)(2,1)}) fusion(bf16[512,1536]{1,0:T(8,128)(2,1)} %param.20), kind=kLoop, calls=%fused_computation.35 | loop fusion | bytes 3145728 | tf_op jit(solution)/shard_map/slice | solution.py:586
  105.2 0.2 copy.42
  105.4 1.3 copy.43
  106.7 0.2 convert_reduce_fusion
  106.9 0.1 copy.40.slot_col_ref
  107.1 1.1 maximum_bitcast_fusion.qv_hbm
  108.2 19.6 %all-to-all-done = bf16[16,64,512]{2,1,0:T(8,128)(2,1)S(1)} async-done(((bf16[16,64,512]{2,1,0:T(8,128)(2,1)}), bf16[16,64,512]{2,1,0:T(8,128)(2,1)S(1)}, u32[]{:S(2)}, u32[]{:S(2)}) %all-to-all-start) | async-done | bytes 1048608 | tf_op jit(solution)/shard_map/all_to_all | solution.py:582
  127.7 20.4 %shard_map.155 = bf16[1024,512]{1,0:T(8,128)(2,1)} custom-call(bf16[1024,512]{1,0:T(8,128)(2,1)S(1)} %bitcast.27, s32[512,1]{1,0:T(8,128)S(1)} %copy.40.slot_col_ref, s32[1,512]{1,0:T(1,128)S(1)} %bitcast.33, f32[1,512]{1,0:T(1,128)S(1)} %bitcast.35, f32[1,512]{1,0:T(1,128)S(1)} %bitcast.36, bf16[1024,512]{1,0:T(8,128)(2,1)} %maximum_bitcast_fusion.qv_hbm, ...), custom_call_target="tpu_custom_call" | custom-call | flops 2684354560 | bytes 4194304 | tf_op jit(solution)/shard_map/pallas_call | solution.py:589
  148.1 5.0 %all-to-all-start.1 = ((bf16[16,64,512]{2,1,0:T(8,128)(2,1)}), bf16[16,64,512]{2,1,0:T(8,128)(2,1)S(1)}, u32[]{:S(2)}, u32[]{:S(2)}) async-start(bf16[16,64,512]{2,1,0:T(8,128)(2,1)} %bitcast.18), calls=%async_computation.1 | async-start | bytes 2097152 | tf_op jit(solution)/shard_map/all_to_all | solution.py:615
  153.1 0.1 copy.41.slot_ref
  153.2 24.7 %all-to-all-done.1 = bf16[16,64,512]{2,1,0:T(8,128)(2,1)S(1)} async-done(((bf16[16,64,512]{2,1,0:T(8,128)(2,1)}), bf16[16,64,512]{2,1,0:T(8,128)(2,1)S(1)}, u32[]{:S(2)}, u32[]{:S(2)}) %all-to-all-start.1) | async-done | bytes 1048608 | tf_op jit(solution)/shard_map/all_to_all | solution.py:615
  177.9 1.5 shard_map.156
  (58 shorter events, 0.9 us)
Async XLA Ops:
  0.0 6.0 %copy-start = (bf16[864,512]{1,0:T(8,128)(2,1)S(1)}, bf16[864,512]{1,0:T(8,128)(2,1)}, u32[]{:S(2)}) copy-start(bf16[864,512]{1,0:T(8,128)(2,1)} %param.16) | copy-start | bytes 2654212
  0.0 5.3 %copy-start.9 = (s32[512,26]{0,1:T(8,128)S(1)}, s32[512,26]{0,1:T(8,128)}, u32[]{:S(2)}) copy-start(s32[512,26]{0,1:T(8,128)} %param.26) | copy-start | bytes 159748
  1.1 4.8 %collective-permute-start = (bf16[13,32,512]{2,1,0:T(8,128)(2,1)S(1)}, bf16[13,32,512]{2,1,0:T(8,128)(2,1)S(1)}, u32[]{:S(2)}, u32[]{:S(2)}) collective-permute-start(bf16[13,32,512]{2,1,0:T(8,128)(2,1)S(1)} %slice.72), channel_id=1, source_target_pairs={{0,1},{1,0},{2,3},{3,2},{4,5},{5,4},{6,7},{7,6},{8,9},{9,8},{10,11... | collective-permute-start | bytes 1277960 | tf_op jit(solution)/shard_map/ppermute | solution.py:414
  3.5 1.0 copy-start.1
  6.6 0.9 copy-start.5
  7.5 11.1 %collective-permute-start.1 = (bf16[192,512]{1,0:T(8,128)(2,1)S(1)}, bf16[192,512]{1,0:T(8,128)(2,1)S(1)}, u32[]{:S(2)}, u32[]{:S(2)}) collective-permute-start(bf16[192,512]{1,0:T(8,128)(2,1)S(1)} %get-tuple-element.45), channel_id=1, source_target_pairs={{0,8},{1,9},{2,10},{3,11},{4,12},{5,13},{6,14},{7,15},{8,0},{9,1},... | collective-permute-start | bytes 589832 | tf_op jit(solution)/shard_map/ppermute | solution.py:489
  12.5 19.9 %collective-permute-start.2 = (bf16[640,512]{1,0:T(8,128)(2,1)}, bf16[640,512]{1,0:T(8,128)(2,1)S(1)}, u32[]{:S(2)}, u32[]{:S(2)}) collective-permute-start(bf16[640,512]{1,0:T(8,128)(2,1)} %copy-done.5), channel_id=1, source_target_pairs={{0,4},{1,3},{4,8},{5,1},{8,12},{9,5},{12,14},{13,9},{14,10},{15,13... | collective-permute-start | bytes 1966088 | tf_op jit(solution)/shard_map/ppermute | solution.py:467
  12.6 20.1 %collective-permute-start.3 = (bf16[640,512]{1,0:T(8,128)(2,1)}, bf16[640,512]{1,0:T(8,128)(2,1)S(1)}, u32[]{:S(2)}, u32[]{:S(2)}) collective-permute-start(bf16[640,512]{1,0:T(8,128)(2,1)} %copy-done.5), channel_id=1, source_target_pairs={{0,2},{1,5},{4,0},{5,9},{8,4},{9,13},{12,8},{13,15},{14,12},{15,11... | collective-permute-start | bytes 1966088 | tf_op jit(solution)/shard_map/ppermute | solution.py:469
  19.3 9.0 %collective-permute-start.4 = (bf16[128,512]{1,0:T(8,128)(2,1)}, bf16[128,512]{1,0:T(8,128)(2,1)S(1)}, u32[]{:S(2)}, u32[]{:S(2)}) collective-permute-start(bf16[128,512]{1,0:T(8,128)(2,1)} %pad_maximum_fusion.3), channel_id=1, source_target_pairs={{0,1},{1,2},{2,3},{3,4},{4,5},{5,6},{6,7},{8,9},{9,10},{10,11},{11... | collective-permute-start | bytes 393224 | tf_op jit(solution)/shard_map/ppermute | solution.py:495
  24.5 2.4 %collective-permute-start.8 = (s32[512,26]{1,0:T(8,128)}, s32[512,26]{1,0:T(8,128)S(1)}, u32[]{:S(2)}, u32[]{:S(2)}) collective-permute-start(s32[512,26]{1,0:T(8,128)} %copy.37), channel_id=1, source_target_pairs={{0,1},{1,0},{2,3},{3,2},{4,5},{5,4},{6,7},{7,6},{8,9},{9,8},{10,11... | collective-permute-start | bytes 159752 | tf_op jit(solution)/shard_map/ppermute | solution.py:492
  24.5 7.8 %collective-permute-start.5 = (bf16[128,512]{1,0:T(8,128)(2,1)S(1)}, bf16[128,512]{1,0:T(8,128)(2,1)S(1)}, u32[]{:S(2)}, u32[]{:S(2)}) collective-permute-start(bf16[128,512]{1,0:T(8,128)(2,1)S(1)} %pad_maximum_fusion.4), channel_id=1, source_target_pairs={{1,0},{2,1},{3,2},{4,3},{5,4},{6,5},{7,6},{9,8},{10,9},{11,10},{12... | collective-permute-start | bytes 393224 | tf_op jit(solution)/shard_map/ppermute | solution.py:496
  32.8 14.6 %collective-permute-start.6 = (bf16[640,512]{1,0:T(8,128)(2,1)S(1)}, bf16[640,512]{1,0:T(8,128)(2,1)S(1)}, u32[]{:S(2)}, u32[]{:S(2)}) collective-permute-start(bf16[640,512]{1,0:T(8,128)(2,1)S(1)} %collective-permute-done.2.refs_3_.refs_4_), channel_id=1, source_target_pairs={{0,4},{1,3},{4,8},{5,1},{8,12},{9,5},{12,14},{13,9},{14,10},{15,13... | collective-permute-start | bytes 1966088 | tf_op jit(solution)/shard_map/ppermute | solution.py:467
  32.8 17.4 %collective-permute-start.7 = (bf16[640,512]{1,0:T(8,128)(2,1)S(1)}, bf16[640,512]{1,0:T(8,128)(2,1)S(1)}, u32[]{:S(2)}, u32[]{:S(2)}) collective-permute-start(bf16[640,512]{1,0:T(8,128)(2,1)S(1)} %collective-permute-done.3.refs_6_.refs_7_), channel_id=1, source_target_pairs={{0,2},{1,5},{4,0},{5,9},{8,4},{9,13},{12,8},{13,15},{14,12},{15,11... | collective-permute-start | bytes 1966088 | tf_op jit(solution)/shard_map/ppermute | solution.py:469
  35.6 10.6 %collective-permute-start.9 = (bf16[896,256]{1,0:T(8,128)(2,1)S(1)}, bf16[896,256]{1,0:T(8,128)(2,1)S(1)}, u32[]{:S(2)}, u32[]{:S(2)}) collective-permute-start(bf16[896,256]{1,0:T(8,128)(2,1)S(1)} %get-tuple-element.61), channel_id=1, source_target_pairs={{0,1},{1,0},{2,3},{3,2},{4,5},{5,4},{6,7},{7,6},{8,9},{9,8},{10,11... | collective-permute-start | bytes 1376264 | tf_op jit(solution)/shard_map/ppermute | solution.py:531
  36.4 32.6 %collective-permute-start.16 = (bf16[448,512]{1,0:T(8,128)(2,1)S(1)}, bf16[448,512]{1,0:T(8,128)(2,1)S(1)}, u32[]{:S(2)}, u32[]{:S(2)}) collective-permute-start(bf16[448,512]{1,0:T(8,128)(2,1)S(1)} %pad_maximum_fusion.2), channel_id=1, source_target_pairs={{0,16},{16,0},{1,17},{17,1},{2,18},{18,2},{3,19},{19,3},{4,20},{20... | collective-permute-start | bytes 1376264 | tf_op jit(solution)/shard_map/ppermute | solution.py:475
  50.2 14.1 %collective-permute-start.10 = (bf16[640,512]{1,0:T(8,128)(2,1)S(1)}, bf16[640,512]{1,0:T(8,128)(2,1)S(1)}, u32[]{:S(2)}, u32[]{:S(2)}) collective-permute-start(bf16[640,512]{1,0:T(8,128)(2,1)S(1)} %collective-permute-done.6.refs_2_.refs_3_), channel_id=1, source_target_pairs={{0,4},{1,3},{4,8},{5,1},{8,12},{9,5},{12,14},{13,9},{14,10},{15,13... | collective-permute-start | bytes 1966088 | tf_op jit(solution)/shard_map/ppermute | solution.py:467
  50.3 16.0 %collective-permute-start.11 = (bf16[640,512]{1,0:T(8,128)(2,1)S(1)}, bf16[640,512]{1,0:T(8,128)(2,1)S(1)}, u32[]{:S(2)}, u32[]{:S(2)}) collective-permute-start(bf16[640,512]{1,0:T(8,128)(2,1)S(1)} %collective-permute-done.7.refs_5_.refs_6_), channel_id=1, source_target_pairs={{0,2},{1,5},{4,0},{5,9},{8,4},{9,13},{12,8},{13,15},{14,12},{15,11... | collective-permute-start | bytes 1966088 | tf_op jit(solution)/shard_map/ppermute | solution.py:469
  51.9 11.0 %collective-permute-start.12 = (bf16[448,512]{1,0:T(8,128)(2,1)S(1)}, bf16[448,512]{1,0:T(8,128)(2,1)S(1)}, u32[]{:S(2)}, u32[]{:S(2)}) collective-permute-start(bf16[448,512]{1,0:T(8,128)(2,1)S(1)} %pad_maximum_fusion), channel_id=1, source_target_pairs={{0,16},{16,0},{1,17},{17,1},{2,18},{18,2},{3,19},{19,3},{4,20},{20... | collective-permute-start | bytes 1376264 | tf_op jit(solution)/shard_map/ppermute | solution.py:475
  66.3 9.8 %collective-permute-start.13 = (bf16[640,512]{1,0:T(8,128)(2,1)S(1)}, bf16[640,512]{1,0:T(8,128)(2,1)S(1)}, u32[]{:S(2)}, u32[]{:S(2)}) collective-permute-start(bf16[640,512]{1,0:T(8,128)(2,1)S(1)} %collective-permute-done.10.refs_2_.refs_3_), channel_id=1, source_target_pairs={{0,4},{1,3},{4,8},{5,1},{8,12},{9,5},{12,14},{13,9},{14,10},{15,13... | collective-permute-start | bytes 1966088 | tf_op jit(solution)/shard_map/ppermute | solution.py:467
  67.7 14.9 %collective-permute-start.15 = (bf16[448,512]{1,0:T(8,128)(2,1)S(1)}, bf16[448,512]{1,0:T(8,128)(2,1)S(1)}, u32[]{:S(2)}, u32[]{:S(2)}) collective-permute-start(bf16[448,512]{1,0:T(8,128)(2,1)S(1)} %pad_maximum_fusion.1), channel_id=1, source_target_pairs={{0,16},{16,0},{1,17},{17,1},{2,18},{18,2},{3,19},{19,3},{4,20},{20... | collective-permute-start | bytes 1376264 | tf_op jit(solution)/shard_map/ppermute | solution.py:475
  76.1 11.4 %collective-permute-start.14 = (bf16[224,512]{1,0:T(8,128)(2,1)S(1)}, bf16[224,512]{1,0:T(8,128)(2,1)S(1)}, u32[]{:S(2)}, u32[]{:S(2)}) collective-permute-start(bf16[224,512]{1,0:T(8,128)(2,1)S(1)} %slice.98), channel_id=1, source_target_pairs={{0,16},{16,0},{1,17},{17,1},{2,18},{18,2},{3,19},{19,3},{4,20},{20... | collective-permute-start | bytes 688136 | tf_op jit(solution)/shard_map/ppermute | solution.py:475
  87.5 5.0 %copy-start.10 = (s32[512]{0:T(512)S(1)}, s32[512]{0:T(512)}, u32[]{:S(2)}) copy-start(s32[512]{0:T(512)} %param.27) | copy-start | bytes 6148
  87.5 6.5 %copy-start.2 = (bf16[512,512]{1,0:T(8,128)(2,1)S(1)}, bf16[512,512]{1,0:T(8,128)(2,1)}, u32[]{:S(2)}) copy-start(bf16[512,512]{1,0:T(8,128)(2,1)} %features_ref.3) | copy-start | bytes 1572868
  87.5 6.5 %copy-start.3 = (bf16[512,512]{1,0:T(8,128)(2,1)S(1)}, bf16[512,512]{1,0:T(8,128)(2,1)}, u32[]{:S(2)}) copy-start(bf16[512,512]{1,0:T(8,128)(2,1)} %weight_ref.1) | copy-start | bytes 1572868
  87.5 6.5 %copy-start.4 = (f32[512]{0:T(512)S(1)}, f32[512]{0:T(512)}, u32[]{:S(2)}) copy-start(f32[512]{0:T(512)} %param.18) | copy-start | bytes 6148
  90.3 3.8 %collective-permute-start.17 = (bf16[512,512]{1,0:T(8,128)(2,1)S(1)}, bf16[512,512]{1,0:T(8,128)(2,1)S(1)}, u32[]{:S(2)}, u32[]{:S(2)}) collective-permute-start(bf16[512,512]{1,0:T(8,128)(2,1)S(1)} %get-tuple-element.80), channel_id=1, source_target_pairs={{0,1},{1,0},{2,3},{3,2},{4,5},{5,4},{6,7},{7,6},{8,9},{9,8},{10,11... | collective-permute-start | bytes 1572872 | tf_op jit(solution)/shard_map/ppermute | solution.py:566
  96.4 31.4 %all-to-all-start = ((bf16[16,64,512]{2,1,0:T(8,128)(2,1)}), bf16[16,64,512]{2,1,0:T(8,128)(2,1)S(1)}, u32[]{:S(2)}, u32[]{:S(2)}) async-start(bf16[16,64,512]{2,1,0:T(8,128)(2,1)} %bitcast.11), calls=%async_computation | async-start | bytes 2097152 | tf_op jit(solution)/shard_map/all_to_all | solution.py:582
  102.9 3.8 %copy-start.11 = (s32[512]{0:T(512)S(1)}, s32[512]{0:T(512)}, u32[]{:S(2)}) copy-start(s32[512]{0:T(512)} %param.28) | copy-start | bytes 6148
  105.2 22.6 %copy-start.6 = (bf16[512,512]{1,0:T(8,128)(2,1)S(1)}, bf16[512,512]{1,0:T(8,128)(2,1)}, u32[]{:S(2)}) copy-start(bf16[512,512]{1,0:T(8,128)(2,1)} %proj_hbm.1) | copy-start | bytes 1572868
  105.2 22.6 %copy-start.7 = (f32[512]{0:T(512)S(1)}, f32[512]{0:T(512)}, u32[]{:S(2)}) copy-start(f32[512]{0:T(512)} %param.19) | copy-start | bytes 6148
  105.2 22.6 %copy-start.8 = (f32[512]{0:T(512)S(1)}, f32[512]{0:T(512)}, u32[]{:S(2)}) copy-start(f32[512]{0:T(512)} %param.22) | copy-start | bytes 6148
  148.1 29.8 %all-to-all-start.1 = ((bf16[16,64,512]{2,1,0:T(8,128)(2,1)}), bf16[16,64,512]{2,1,0:T(8,128)(2,1)S(1)}, u32[]{:S(2)}, u32[]{:S(2)}) async-start(bf16[16,64,512]{2,1,0:T(8,128)(2,1)} %bitcast.18), calls=%async_computation.1 | async-start | bytes 2097152 | tf_op jit(solution)/shard_map/all_to_all | solution.py:615
